TPU v7x, 32 devices: a whole 2x2x4 slice. The times are simulated.
32 devices in a mesh: groups: 2 (over y), latent: 4 (over z), token: 2 (over x), layer: 2 (over core).
Axes of the slice: x: 2, y: 2, z: 4, core: 2. Of those that a mesh axis runs over, the one named last changes fastest.
Arguments:
- inputs: bfloat16 [2, 1536, 4096], P('layer', ('groups', 'token')), parts along dimension 1, may hold values from -1800 to 1800
- targets: bfloat16 [2, 1536, 4096], P('layer', ('groups', 'token'), 'latent'), parts along dimension 1, may hold values from -90 to 90
- enc_weight: bfloat16 [2, 4096, 16384], P('layer', None, ('latent', 'token')), may hold values from -0.09375 to 0.09375
- encoder_layer_bias: bfloat16 [2, 16384], P('layer', 'latent'), may hold values from -3 to 3
- dec_self: bfloat16 [2, 16384, 4096], P('layer', ('latent', 'token')), may hold values from -3 to 3
- dec_cross: bfloat16 [16384, 4096], P(('latent', 'token')), may hold values from -3 to 3
- dec_bias: bfloat16 [2, 4096], P('layer', 'latent'), may hold values from -3 to 3
Outputs:
- recon: bfloat16 [2, 1536, 4096], P('layer', ('groups', 'token'), 'latent'), parts along dimension 1
- loss: float32 [2], P('groups'), parts along dimension 0
There are 2 independent parts, one for each index of `groups`. A program takes and returns all parts, laid end to end along the dimension named above; an argument that names none is the same for every part. Nothing has to cross between parts.
All inputs are finite; a program needn't handle non-finite values.
Results may differ from a plain program's by a relative error of at most 0.0054.
Values may be sent and summed in bfloat16 or wider, within the bound.
No kernel may reach another device: no remote copies, remote signals or barrier semaphores. Data moves between devices by JAX's collectives and lax.ppermute only.
A program may use at most 320 MiB of HBM per device.

v0:
```python
import jax
import jax.numpy as jnp
from jax import lax
from jax.sharding import PartitionSpec as P


def passed_along(block, axis, distance):
    devices = range(lax.axis_size(axis))
    route = [(i - distance, i) for i in devices if i - distance in devices]
    return lax.ppermute(block, axis, route)


def local(inputs, targets, enc_weight, encoder_layer_bias, dec_self, dec_cross, dec_bias):
    layer_idx = lax.axis_index("layer")
    slots = (jnp.arange(lax.axis_size("layer")) == layer_idx).astype(jnp.float32)
    target = targets[0].astype(jnp.float32)
    target_sq = jnp.sum(target * target)
    norm_vec = lax.psum(slots * target_sq, ("latent", "token", "layer"))
    x_local = inputs[0]
    rows = x_local.shape[0]
    lat_dev = enc_weight.shape[2]
    n_tok = lax.axis_size("token")
    col_width = dec_bias.shape[1]
    bias_block = encoder_layer_bias[0]
    whole = lax.all_gather(x_local, "token", axis=0, tiled=True).astype(jnp.float32)
    scale = jnp.sqrt(jnp.mean(whole * whole) + 1e-06)
    normed = (whole / scale).astype(jnp.bfloat16)
    bias_piece = lax.dynamic_slice_in_dim(
        bias_block, lax.axis_index("token") * lat_dev, lat_dev
    ).astype(jnp.float32)
    codes = jnp.maximum(
        jnp.dot(normed, enc_weight[0], preferred_element_type=jnp.float32) + bias_piece, 0.0
    ).astype(jnp.bfloat16)
    earlier = passed_along(codes, "layer", 1)
    diagonal_full = dec_self[0]
    span = rows * n_tok
    blocks = rows * lax.axis_size(("latent", "token")) // span
    diagonal_cols = diagonal_full.reshape(lat_dev, blocks, col_width)
    cross_cols = dec_cross.reshape(lat_dev, blocks, col_width)
    result = jnp.einsum("tm,mkp->ktp", codes, diagonal_cols, preferred_element_type=jnp.float32)
    result = result + jnp.einsum(
        "tm,mkp->ktp", earlier, cross_cols, preferred_element_type=jnp.float32
    )
    total = lax.psum_scatter(
        result.reshape(rows * lax.axis_size(("latent", "token")), col_width),
        ("latent", "token"),
        scatter_dimension=0,
        tiled=True,
    )
    total = total + dec_bias[0].astype(jnp.float32)[None, :]
    recon = total.astype(jnp.bfloat16)[None]
    diff = total - target
    err_local = jnp.sum(diff * diff)
    err_vec = lax.psum(slots * err_local, ("latent", "token", "layer"))
    loss = jnp.mean(err_vec / norm_vec).reshape(1)
    return (recon, loss)


def solution(mesh):
    return jax.shard_map(
        local,
        mesh=mesh,
        in_specs=(
            P("layer", ("groups", "token"), None),
            P("layer", ("groups", "token"), "latent"),
            P("layer", None, ("latent", "token")),
            P("layer", "latent"),
            P("layer", ("latent", "token"), None),
            P(("latent", "token"), None),
            P("layer", "latent"),
        ),
        out_specs=(P("layer", ("groups", "token"), "latent"), P("groups")),
        check_vma=False,
    )
```

profile of v0, /device:TPU:0, one launch (start us, length us, event | category | flops | bytes accessed | tf_op | source)
XLA Modules:
  0.0 416.0 jit_solution(18058362100144846557)
XLA Ops:
  7.2 0.0 all-gather.3.cloned.1.call-start
  7.2 0.7 all-gather.3.cloned.1.call-update
  7.9 0.0 reduce-scatter.2.cloned.1.call-start
  8.0 0.0 copy-start.1
  8.0 28.3 %reshape_squeeze.3 = bf16[2048,4,1024]{2,1,0:T(4,128)(2,1)} reshape(bf16[1,2048,4096]{2,1,0:T(8,128)(2,1)} %param.11) | data formatting | bytes 33554432 | tf_op jit(solution)/shard_map/reshape;squeeze | solution.py:38
  36.3 0.0 copy-done.1
  36.3 56.4 %all-gather.3.cloned.1.call-done = bf16[1,768,4096]{2,1,0:T(8,128)(2,1)} async-done(((bf16[1,384,4096]{2,1,0:T(8,128)(2,1)}), bf16[1,768,4096]{2,1,0:T(8,128)(2,1)}) %all-gather.3.cloned.1.call-update) | async-done | bytes 6291472 | tf_op jit(solution)/shard_map/all_gather | solution.py:25
  92.7 6.6 %fusion.8 = f32[]{:T(128)} fusion(bf16[1,768,4096]{2,1,0:T(8,128)(2,1)} %all-gather.3.cloned.1.call-done), kind=kLoop, calls=%fused_computation.10 | loop fusion | flops 9437183 | bytes 6291460 | tf_op jit(solution)/shard_map/reduce_sum | solution.py:26
  100.0 18.5 %maximum_convert_fusion = bf16[768,2048]{1,0:T(8,128)(2,1)S(1)} fusion(bf16[1,4096,2048]{2,1,0:T(8,128)(2,1)} %param.9, bf16[1,768,4096]{2,1,0:T(8,128)(2,1)} %all-gather.3.cloned.1.call-done, f32[]{:T(128)S(6)} %sqrt.3, f32[2048]{0:T(1024)S(1)} %bitcast.36), kind=kOutput, calls=%fused_computation.13 | convolution fusion | flops 12899057664 | bytes 26222596 | tf_op jit(solution)/shard_map/dot_general | solution.py:32
  118.5 2.1 collective-permute-start
  120.6 21.2 %fusion.5 = f32[768,4,1024]{2,0,1:T(8,128)} fusion(bf16[2048,4,1024]{2,1,0:T(4,128)(2,1)} %reshape_squeeze.3, bf16[768,2048]{1,0:T(8,128)(2,1)S(1)} %maximum_convert_fusion), kind=kOutput, calls=%fused_computation.5 | convolution fusion | flops 12884901888 | bytes 32505856 | tf_op jit(solution)/shard_map/tm,mkp->ktp/dot_general | solution.py:40
  141.8 0.0 collective-permute-done
  141.8 21.3 %fusion.12 = f32[768,4,1024]{2,0,1:T(8,128)} fusion(f32[768,4,1024]{2,0,1:T(8,128)} %fusion.5, bf16[256,4,8,1024]{3,2,1,0:T(8,128)(2,1)} %bitcast.37, bf16[768,2048]{1,0:T(8,128)(2,1)S(1)} %collective-permute-done), kind=kOutput, calls=%fused_computation.14 | convolution fusion | flops 12888047616 | bytes 45088768 | tf_op jit(solution)/shard_map/tm,mkp->ktp/dot_general | solution.py:41
  163.2 0.0 copy-start.2
  163.2 0.0 copy-start
  163.2 0.0 reduce-scatter.2.cloned.1.call-update
  163.2 0.7 copy-done.2
  163.9 206.9 %reduce-scatter.2.cloned.1.call-done = f32[384,1024]{1,0:T(8,128)} async-done(((f32[3072,1024]{1,0:T(8,128)}), f32[384,1024]{1,0:T(8,128)}) %reduce-scatter.2.cloned.1.call-update) | async-done | bytes 1572880 | tf_op jit(solution)/shard_map/reduce_scatter | solution.py:44
  370.7 0.0 copy-done
  370.7 3.3 fusion.23
  374.0 1.3 compare_select_fusion
  375.3 31.5 %all-reduce = (f32[2]{0:T(128)S(1)}, f32[2]{0:T(128)S(1)}) all-reduce(f32[2]{0:T(128)S(1)} %get-tuple-element.8, f32[2]{0:T(128)S(1)} %get-tuple-element.7), channel_id=1, replica_groups=mesh['groups'=2,'latent'=4,'token'=2,'layer'=2] {'latent','token','layer'}, use_global_device_ids=true, to_apply=%region_3.0 | all-reduce | flops 4 | bytes 32 | tf_op jit(solution)/shard_map/psum | solution.py:54
  406.8 0.6 divide_reduce_fusion
  (2 shorter events, 0.0 us)
Async XLA Ops:
  7.2 85.5 %all-gather.3.cloned.1.call-start = ((), (), s32[]{:S(2)}) async-start(), calls=%async_computation.2 | async-start | bytes 9437184 | tf_op jit(solution)/shard_map/all_gather | solution.py:25
  7.9 362.8 %reduce-scatter.2.cloned.1.call-start = ((), (), s32[]{:S(2)}) async-start(), calls=%async_computation.1 | async-start | bytes 14155776 | tf_op jit(solution)/shard_map/reduce_scatter | solution.py:44
  8.0 28.3 %copy-start.1 = (bf16[1,4096]{1,0:T(2,128)(2,1)S(1)}, bf16[1,4096]{1,0:T(2,128)(2,1)}, u32[]{:S(2)}) copy-start(bf16[1,4096]{1,0:T(2,128)(2,1)} %param.10) | copy-start | bytes 24580
  118.5 23.4 %collective-permute-start = (bf16[768,2048]{1,0:T(8,128)(2,1)S(1)}, bf16[768,2048]{1,0:T(8,128)(2,1)S(1)}, u32[]{:S(2)}, u32[]{:S(2)}) collective-permute-start(bf16[768,2048]{1,0:T(8,128)(2,1)S(1)} %maximum_convert_fusion), channel_id=1, source_target_pairs={{0,1},{2,3},{4,5},{6,7},{8,9},{10,11},{12,13},{14,15},{16,17},{18,... | collective-permute-start | bytes 9437192 | tf_op jit(solution)/shard_map/ppermute | solution.py:10
  163.2 0.7 copy-start.2
  163.2 207.5 %copy-start = (bf16[1,384,1024]{2,1,0:T(8,128)(2,1)S(1)}, bf16[1,384,1024]{2,1,0:T(8,128)(2,1)}, u32[]{:S(2)}) copy-start(bf16[1,384,1024]{2,1,0:T(8,128)(2,1)} %param.8) | copy-start | bytes 2359300
Sparse Core Ops, SparseCore 0:
  9.5 83.0 all-gather.2
  163.3 207.3 reduce-scatter.1
where the time goes:
time: 417 us; the launch traced here: 416 us
  waiting for transfers between devices  264 us (63%)
  matrix products  61.1 us (15%)
  blocking collectives  31.5 us (8%)
  local copies, waits for them, and re-layouts  29 us (7%)
  between operations  16.6 us (4%)
  other arithmetic  11.8 us (3%)
    reduce_scatter x1, waiting for transfers between devices, local(): lax.psum_scatter(result.reshape(rows * lax.axis_size(('latent', 'token'))...  207 us
    all_gather x1, waiting for transfers between devices, local(): lax.all_gather(x_local, 'token', axis=0, tiled=True).astype(jnp.float32)  56.4 us
    psum x1, blocking collectives, local(): err_vec = lax.psum(slots * err_local, ('latent', 'token', 'layer'))  31.5 us
    another operation x1, local copies, waits for them, and re-layouts, local(): diagonal_cols = diagonal_full.reshape(lat_dev, blocks, col_width)  28.3 us
    dot_general x1, matrix products, local(): jnp.einsum('tm,mkp->ktp', earlier, cross_cols, preferred_element_type=jnp...  21.3 us
    dot_general x1, matrix products, local(): jnp.einsum('tm,mkp->ktp', codes, diagonal_cols, preferred_element_type=jn...  21.2 us
    dot_general x1, matrix products, local(): jnp.dot(normed, enc_weight[0], preferred_element_type=jnp.float32)  18.5 us
  transfers between devices with their start and end apart: 3, of which 2 were waited for; matrix products, arithmetic and copies ran while one was open for 12% of the time, Pallas kernels for 0%

commit v1 on v0

v1 whole, which is shorter than its diff:
```python
import functools

import jax
import jax.numpy as jnp
from jax import lax
from jax.experimental import pallas as pl
from jax.experimental.pallas import tpu as pltpu
from jax.sharding import PartitionSpec as P

VMEM_LIMIT = 48 * 1024 * 1024
CHUNKS = 2


def tile_of(size, most):
    tile = min(size, most)
    while size % tile:
        tile //= 2
    return tile


def encode_body(inv_ref, x_ref, w_ref, b_ref, o_ref):
    pre = jnp.dot(x_ref[...], w_ref[...], preferred_element_type=jnp.float32)
    pre = pre * inv_ref[0] + b_ref[...].astype(jnp.float32)
    o_ref[...] = jnp.maximum(pre, 0.0).astype(o_ref.dtype)


def encode(x, inv, weight, bias):
    rows, width = x.shape
    latents = weight.shape[1]
    tile = tile_of(latents, 256)
    return pl.pallas_call(
        encode_body,
        grid=(latents // tile,),
        in_specs=[
            pl.BlockSpec(memory_space=pltpu.SMEM),
            pl.BlockSpec((rows, width), lambda j: (0, 0)),
            pl.BlockSpec((width, tile), lambda j: (0, j)),
            pl.BlockSpec((1, tile), lambda j: (0, j)),
        ],
        out_specs=pl.BlockSpec((rows, tile), lambda j: (0, j)),
        out_shape=jax.ShapeDtypeStruct((rows, latents), jnp.bfloat16),
        compiler_params=pltpu.CompilerParams(vmem_limit_bytes=VMEM_LIMIT),
        cost_estimate=pl.CostEstimate(
            flops=2 * rows * width * latents,
            bytes_accessed=2 * (rows * width + width * latents + rows * latents),
            transcendentals=0,
        ),
        name="encode",
    )(inv.reshape(1), x, weight, bias)


def decode_body(info_ref, c_ref, e_ref, s_ref, x_ref, o_ref):
    own = jnp.dot(c_ref[...], s_ref[...], preferred_element_type=jnp.float32)
    layer = info_ref[0]

    @pl.when(layer == 0)
    def _():
        o_ref[0] = own.astype(o_ref.dtype)

    @pl.when(layer != 0)
    def _():
        cross = jnp.dot(e_ref[...], x_ref[...], preferred_element_type=jnp.float32)
        o_ref[0] = (own + cross).astype(o_ref.dtype)


def decode(codes, earlier, own_w, cross_w, info, blocks, width, dtype):
    rows, latents = codes.shape
    tile = tile_of(width, 512)
    per = width // tile

    def column(b, j, info_ref):
        return (0, info_ref[1 + b] * per + j)

    def cross_column(b, j, info_ref):
        return (0, jnp.where(info_ref[0] == 0, 0, info_ref[1 + b] * per + j))

    return pl.pallas_call(
        decode_body,
        grid_spec=pltpu.PrefetchScalarGridSpec(
            num_scalar_prefetch=1,
            grid=(blocks, per),
            in_specs=[
                pl.BlockSpec((rows, latents), lambda b, j, r: (0, 0)),
                pl.BlockSpec((rows, latents), lambda b, j, r: (0, 0)),
                pl.BlockSpec((latents, tile), column),
                pl.BlockSpec((latents, tile), cross_column),
            ],
            out_specs=pl.BlockSpec((1, rows, tile), lambda b, j, r: (b, 0, j)),
        ),
        out_shape=jax.ShapeDtypeStruct((blocks, rows, width), dtype),
        compiler_params=pltpu.CompilerParams(vmem_limit_bytes=VMEM_LIMIT),
        cost_estimate=pl.CostEstimate(
            flops=4 * rows * latents * blocks * width,
            bytes_accessed=4 * (rows * latents + latents * blocks * width) + 4 * rows * blocks * width,
            transcendentals=0,
        ),
        name="decode",
    )(info, codes, earlier, own_w, cross_w)


def shifted(value, axis, distance):
    n = lax.axis_size(axis)
    return lax.ppermute(value, axis, [(i, (i + distance) % n) for i in range(n)])


def swapped(value, axis, bit):
    n = lax.axis_size(axis)
    return lax.ppermute(value, axis, [(i, i ^ bit) for i in range(n)])


def sum_over(value, axis):
    total = value
    for distance in range(1, lax.axis_size(axis)):
        total = total + shifted(value, axis, distance)
    return total


def local(inputs, targets, enc_weight, encoder_layer_bias, dec_self, dec_cross, dec_bias):
    layer = lax.axis_index("layer")
    lat = lax.axis_index("latent")
    n_lat = lax.axis_size("latent")
    n_tok = lax.axis_size("token")
    x_own = inputs[0]
    rows, model = x_own.shape
    enc_w = enc_weight[0]
    own_w = dec_self[0]
    lat_dev = enc_w.shape[1]
    width = dec_bias.shape[1]
    chunk = rows // CHUNKS

    foreign = []
    for distance in range(1, n_tok):
        for c in range(CHUNKS):
            piece = x_own[c * chunk:(c + 1) * chunk]
            foreign.append((distance, shifted(piece, "token", distance)))

    field = x_own.astype(jnp.float32)
    square = sum_over(jnp.sum(field * field).reshape(1, 1), "token")
    scale = jnp.sqrt(square[0, 0] / (rows * n_tok * model) + 1e-06)
    inv = 1.0 / scale
    bias = lax.dynamic_slice_in_dim(
        encoder_layer_bias, lax.axis_index("token") * lat_dev, lat_dev, axis=1
    )

    half = n_lat // 2
    kept = [2 * i + lat % 2 for i in range(half)]
    sent = [2 * i + 1 - lat % 2 for i in range(half)]
    info_kept = jnp.stack([layer] + kept).astype(jnp.int32)
    info_sent = jnp.stack([layer] + sent).astype(jnp.int32)

    def work(x):
        codes = encode(x, inv, enc_w, bias)
        earlier = lax.ppermute(codes, "layer", [(0, 1)])
        away = decode(codes, earlier, own_w, dec_cross, info_sent, half, width, jnp.bfloat16)
        arrived = swapped(away, "latent", 1)
        total = decode(codes, earlier, own_w, dec_cross, info_kept, half, width, jnp.float32)
        total = total + arrived.astype(jnp.float32)
        bit = 2
        while bit < n_lat:
            mine = (lat // bit) % 2
            pairs = total.reshape(total.shape[0] // 2, 2, x.shape[0], width)
            away = lax.dynamic_index_in_dim(pairs, 1 - mine, 1, keepdims=False).astype(jnp.bfloat16)
            arrived = swapped(away, "latent", bit)
            total = lax.dynamic_index_in_dim(pairs, mine, 1, keepdims=False) + arrived.astype(jnp.float32)
            bit *= 2
        return total[0]

    total = work(x_own)
    returned = []
    for distance, x in foreign:
        part = work(x).astype(jnp.bfloat16)
        returned.append(shifted(part, "token", n_tok - distance))
    for d in range(n_tok - 1):
        total = total + jnp.concatenate(returned[d * CHUNKS:(d + 1) * CHUNKS]).astype(jnp.float32)
    total = total + dec_bias.astype(jnp.float32)
    recon = total.astype(jnp.bfloat16)[None]

    target = targets[0].astype(jnp.float32)
    diff = total - target
    sums = jnp.stack([jnp.sum(diff * diff), jnp.sum(target * target)]).reshape(1, 2)
    sums = sum_over(sum_over(sums, "latent"), "token")
    ratio = sums[:, 0] / sums[:, 1]
    loss = sum_over(ratio, "layer") / 2.0
    return (recon, loss)


def solution(mesh):
    return jax.shard_map(
        local,
        mesh=mesh,
        in_specs=(
            P("layer", ("groups", "token"), None),
            P("layer", ("groups", "token"), "latent"),
            P("layer", None, ("latent", "token")),
            P("layer", "latent"),
            P("layer", ("latent", "token"), None),
            P(("latent", "token"), None),
            P("layer", "latent"),
        ),
        out_specs=(P("layer", ("groups", "token"), "latent"), P("groups")),
        check_vma=False,
    )
```

time: 417 us -> 254 us (0.61)
  waiting for transfers between devices: 264 us -> 132 us
  Pallas kernels: 0 us -> 77.3 us
  matrix products: 61.1 us -> 0 us
  blocking collectives: 31.5 us -> 0 us
  local copies, waits for them, and re-layouts: 29 us -> 2.88 us
  starting transfers between devices: 2.2 us -> 24.1 us
  between operations: 16.6 us -> 5.4 us
    reduce_scatter x1 -> x0, waiting for transfers between devices: 207 us -> none  [local(): lax.psum_scatter(result.reshape(rows * lax.axis_size(('latent', 'token'))...]
    ppermute x1 -> x19, waiting for transfers between devices: 0.01 us -> 132 us  [the longest x6 75.6 us: swapped(): return lax.ppermute(value, axis, [(i, i ^ bit) for i in range(n)])]
    pallas_call x0 -> x9, Pallas kernels: none -> 77.3 us  [the longest x6 43.9 us: decode(): pl.pallas_call(decode_body, grid_spec=pltpu.PrefetchScalarGridSpec(num_sc...]
    dot_general x3 -> x0, matrix products: 61.1 us -> none  [the longest x1 21.3 us: local(): jnp.einsum('tm,mkp->ktp', earlier, cross_cols, preferred_element_type=jnp...]
    all_gather x1 -> x0, waiting for transfers between devices: 56.4 us -> none  [local(): lax.all_gather(x_local, 'token', axis=0, tiled=True).astype(jnp.float32)]
    psum x1 -> x0, blocking collectives: 31.5 us -> none  [local(): err_vec = lax.psum(slots * err_local, ('latent', 'token', 'layer'))]
    another operation x1 -> x0, local copies, waits for them, and re-layouts: 28.3 us -> none  [local(): diagonal_cols = diagonal_full.reshape(lat_dev, blocks, col_width)]
    ppermute x1 -> x19, starting transfers between devices: 2.12 us -> 24.1 us  [the longest x10 10.4 us: shifted(): lax.ppermute(value, axis, [(i, (i + distance) % n) for i in range(n)])]
  transfers between devices with their start and end apart: 3 -> 19, of which waited for: 2 -> 11; matrix products, arithmetic and copies ran while one was open for 12% -> 2% of each run, Pallas kernels for 0% -> 30%
where the time goes in v1:
time: 254 us
  waiting for transfers between devices  132 us (52%)
  Pallas kernels  77.3 us (30%)
  starting transfers between devices  24.1 us (9%)
  other arithmetic  11.8 us (5%)
  between operations  5.4 us (2%)
  local copies, waits for them, and re-layouts  2.88 us (1%)
    ppermute x6, waiting for transfers between devices, swapped(): return lax.ppermute(value, axis, [(i, i ^ bit) for i in range(n)])  75.6 us
    ppermute x10, waiting for transfers between devices, shifted(): lax.ppermute(value, axis, [(i, (i + distance) % n) for i in range(n)])  56.4 us
    pallas_call x6, Pallas kernels, decode(): pl.pallas_call(decode_body, grid_spec=pltpu.PrefetchScalarGridSpec(num_sc...  43.9 us
    pallas_call x3, Pallas kernels, encode(): pl.pallas_call(encode_body, grid=(latents // tile,), in_specs=[pl.BlockSp...  33.4 us
    ppermute x10, starting transfers between devices, shifted(): lax.ppermute(value, axis, [(i, (i + distance) % n) for i in range(n)])  10.4 us
    ppermute x6, starting transfers between devices, swapped(): return lax.ppermute(value, axis, [(i, i ^ bit) for i in range(n)])  9.51 us
  transfers between devices with their start and end apart: 19, of which 11 were waited for; matrix products, arithmetic and copies ran while one was open for 2% of the time, Pallas kernels for 30%

profile of v1, /device:TPU:0, one launch (start us, length us, event | category | flops | bytes accessed | tf_op | source)
XLA Modules:
  0.0 253.5 jit_solution(1605430621733730171)
XLA Ops:
  0.7 4.3 %multiply_reduce_fusion = f32[]{:T(128)} fusion(bf16[1,384,4096]{2,1,0:T(8,128)(2,1)} %param.7), kind=kLoop, calls=%fused_computation | loop fusion | flops 4718591 | bytes 3145732 | tf_op jit(solution)/shard_map/reduce_sum | solution.py:138
  4.9 2.9 %collective-permute-start = (f32[1,1]{1,0:T(1,128)}, f32[1,1]{1,0:T(1,128)}, u32[]{:S(2)}, u32[]{:S(2)}) collective-permute-start(f32[1,1]{1,0:T(1,128)} %bitcast.4), channel_id=1, source_target_pairs={{0,2},{2,0},{1,3},{3,1},{4,6},{6,4},{5,7},{7,5},{8,10},{10,8},{9,1... | collective-permute-start | bytes 20 | tf_op jit(solution)/shard_map/ppermute | solution.py:103
  7.9 2.0 slice_bitcast_fusion.1
  9.9 2.0 collective-permute-start.9
  13.2 12.7 %encode.3.c_ref = bf16[384,2048]{1,0:T(8,128)(2,1)} custom-call(f32[1]{0:T(128)} %bitcast.5.inv_ref, bf16[384,4096]{1,0:T(8,128)(2,1)S(1)} %bitcast.39, bf16[4096,2048]{1,0:T(8,128)(2,1)} %bitcast.46, bf16[1,2048]{1,0:T(2,128)(2,1)S(1)} %constant_dynamic-slice_fusion.b_ref), custom_call_target="tpu_custom_call" | custom-call | flops 6442450944 | bytes 21495808 | tf_op jit(solution)/shard_map/encode/pallas_call | solution.py:31
  25.8 1.4 collective-permute-start.1
  27.4 20.1 %collective-permute-done.4.x_ref = bf16[192,4096]{1,0:T(8,128)(2,1)} collective-permute-done((bf16[192,4096]{1,0:T(8,128)(2,1)}, bf16[192,4096]{1,0:T(8,128)(2,1)}, u32[]{:S(2)}, u32[]{:S(2)}) %collective-permute-start.4) | collective-permute-done | bytes 1572896 | tf_op jit(solution)/shard_map/ppermute | solution.py:103
  47.5 10.4 %encode.4.c_ref = bf16[192,2048]{1,0:T(8,128)(2,1)S(1)} custom-call(f32[1]{0:T(128)} %bitcast.5.inv_ref, bf16[192,4096]{1,0:T(8,128)(2,1)} %collective-permute-done.4.x_ref, bf16[4096,2048]{1,0:T(8,128)(2,1)} %bitcast.47, bf16[1,2048]{1,0:T(2,128)(2,1)S(1)} %constant_dynamic-slice_fusion.b_ref), custom_call_target="tpu_custom_call" | custom-call | flops 3221225472 | bytes 19136512 | tf_op jit(solution)/shard_map/encode/pallas_call | solution.py:31
  57.9 1.3 collective-permute-start.5
  59.2 20.5 %collective-permute-done.9.x_ref = bf16[192,4096]{1,0:T(8,128)(2,1)} collective-permute-done((bf16[192,4096]{1,0:T(8,128)(2,1)}, bf16[192,4096]{1,0:T(8,128)(2,1)}, u32[]{:S(2)}, u32[]{:S(2)}) %collective-permute-start.9) | collective-permute-done | bytes 1572896 | tf_op jit(solution)/shard_map/ppermute | solution.py:103
  79.7 10.4 %encode.5.c_ref = bf16[192,2048]{1,0:T(8,128)(2,1)S(1)} custom-call(f32[1]{0:T(128)} %bitcast.5.inv_ref, bf16[192,4096]{1,0:T(8,128)(2,1)} %collective-permute-done.9.x_ref, bf16[4096,2048]{1,0:T(8,128)(2,1)} %bitcast.48, bf16[1,2048]{1,0:T(2,128)(2,1)S(1)} %constant_dynamic-slice_fusion.b_ref), custom_call_target="tpu_custom_call" | custom-call | flops 3221225472 | bytes 19136512 | tf_op jit(solution)/shard_map/encode/pallas_call | solution.py:31
  90.1 1.5 collective-permute-start.10
  91.6 8.2 %decode.7 = bf16[2,384,1024]{2,1,0:T(8,128)(2,1)S(1)} custom-call(s32[3]{0:T(128)S(1)} %pad_add_fusion.1.info_ref, bf16[384,2048]{1,0:T(8,128)(2,1)} %encode.3.c_ref, bf16[384,2048]{1,0:T(8,128)(2,1)S(1)} %collective-permute-done.1.e_ref, bf16[2048,4096]{1,0:T(8,128)(2,1)} %bitcast.40, bf16[2048,4096]{1,0:T(8,128)(2,1)} %x_ref.11), custom_call_target="tpu_custom_call" | custom-call | flops 6442450944 | bytes 23068672 | tf_op jit(solution)/shard_map/decode/pallas_call | solution.py:77
  99.9 1.6 collective-permute-start.2
  101.5 9.4 %decode.6 = f32[2,384,1024]{2,1,0:T(8,128)} custom-call(s32[3]{0:T(128)S(1)} %pad_add_fusion.info_ref, bf16[384,2048]{1,0:T(8,128)(2,1)} %encode.3.c_ref, bf16[384,2048]{1,0:T(8,128)(2,1)S(1)} %collective-permute-done.1.e_ref, bf16[2048,4096]{1,0:T(8,128)(2,1)} %bitcast.41, bf16[2048,4096]{1,0:T(8,128)(2,1)} %x_ref.11), custom_call_target="tpu_custom_call" | custom-call | flops 6442450944 | bytes 23068672 | tf_op jit(solution)/shard_map/decode/pallas_call | solution.py:77
  110.9 6.6 %decode.9 = bf16[2,192,1024]{2,1,0:T(8,128)(2,1)S(1)} custom-call(s32[3]{0:T(128)S(1)} %pad_add_fusion.1.info_ref, bf16[192,2048]{1,0:T(8,128)(2,1)S(1)} %encode.4.c_ref, bf16[192,2048]{1,0:T(8,128)(2,1)S(1)} %collective-permute-done.5.e_ref, bf16[2048,4096]{1,0:T(8,128)(2,1)} %bitcast.42, bf16[2048,4096]{1,0:T(8,128)(2,1)} %x_ref.11), custom_call_target="tpu_custom_call" | custom-call | flops 3221225472 | bytes 19922944 | tf_op jit(solution)/shard_map/decode/pallas_call | solution.py:77
  117.5 0.5 collective-permute-start.6
  118.0 6.6 %decode.11 = bf16[2,192,1024]{2,1,0:T(8,128)(2,1)S(1)} custom-call(s32[3]{0:T(128)S(1)} %pad_add_fusion.1.info_ref, bf16[192,2048]{1,0:T(8,128)(2,1)S(1)} %encode.5.c_ref, bf16[192,2048]{1,0:T(8,128)(2,1)S(1)} %collective-permute-done.10.e_ref, bf16[2048,4096]{1,0:T(8,128)(2,1)} %bitcast.43, bf16[2048,4096]{1,0:T(8,128)(2,1)} %x_ref.11), custom_call_target="tpu_custom_call" | custom-call | flops 3221225472 | bytes 19922944 | tf_op jit(solution)/shard_map/decode/pallas_call | solution.py:77
  124.6 1.6 collective-permute-start.11
  126.2 6.6 %decode.8 = f32[2,192,1024]{2,1,0:T(8,128)S(1)} custom-call(s32[3]{0:T(128)S(1)} %pad_add_fusion.info_ref, bf16[192,2048]{1,0:T(8,128)(2,1)S(1)} %encode.4.c_ref, bf16[192,2048]{1,0:T(8,128)(2,1)S(1)} %collective-permute-done.5.e_ref, bf16[2048,4096]{1,0:T(8,128)(2,1)} %bitcast.44, bf16[2048,4096]{1,0:T(8,128)(2,1)} %x_ref.11), custom_call_target="tpu_custom_call" | custom-call | flops 3221225472 | bytes 19922944 | tf_op jit(solution)/shard_map/decode/pallas_call | solution.py:77
  132.8 6.6 %decode.10 = f32[2,192,1024]{2,1,0:T(8,128)S(1)} custom-call(s32[3]{0:T(128)S(1)} %pad_add_fusion.info_ref, bf16[192,2048]{1,0:T(8,128)(2,1)S(1)} %encode.5.c_ref, bf16[192,2048]{1,0:T(8,128)(2,1)S(1)} %collective-permute-done.10.e_ref, bf16[2048,4096]{1,0:T(8,128)(2,1)} %bitcast.45, bf16[2048,4096]{1,0:T(8,128)(2,1)} %x_ref.11), custom_call_target="tpu_custom_call" | custom-call | flops 3221225472 | bytes 19922944 | tf_op jit(solution)/shard_map/decode/pallas_call | solution.py:77
  139.4 13.6 %collective-permute-done.6 = bf16[2,192,1024]{2,1,0:T(8,128)(2,1)S(1)} collective-permute-done((bf16[2,192,1024]{2,1,0:T(8,128)(2,1)S(1)}, bf16[2,192,1024]{2,1,0:T(8,128)(2,1)S(1)}, u32[]{:S(2)}, u32[]{:S(2)}) %collective-permute-start.6) | collective-permute-done | bytes 786464 | tf_op jit(solution)/shard_map/ppermute | solution.py:108
  153.1 0.3 convert_add_fusion.2
  153.5 2.7 %collective-permute-start.7 = (bf16[1,192,1024]{2,1,0:T(8,128)(2,1)S(1)}, bf16[1,192,1024]{2,1,0:T(8,128)(2,1)S(1)}, u32[]{:S(2)}, u32[]{:S(2)}) collective-permute-start(bf16[1,192,1024]{2,1,0:T(8,128)(2,1)S(1)} %dynamic-slice_convert_fusion.2), channel_id=1, source_target_pairs={{0,8},{4,12},{8,0},{12,4},{1,9},{5,13},{9,1},{13,5},{2,10},{6,14},... | collective-permute-start | bytes 1179656 | tf_op jit(solution)/shard_map/ppermute | solution.py:108
  156.1 22.2 %collective-permute-done.11 = bf16[2,192,1024]{2,1,0:T(8,128)(2,1)S(1)} collective-permute-done((bf16[2,192,1024]{2,1,0:T(8,128)(2,1)S(1)}, bf16[2,192,1024]{2,1,0:T(8,128)(2,1)S(1)}, u32[]{:S(2)}, u32[]{:S(2)}) %collective-permute-start.11) | collective-permute-done | bytes 786464 | tf_op jit(solution)/shard_map/ppermute | solution.py:108
  178.3 0.3 convert_add_fusion.1
  178.7 1.7 collective-permute-start.12
  180.5 0.7 convert_add_fusion
  181.2 0.1 dynamic-slice_convert_fusion
  181.4 1.3 collective-permute-start.3
  182.7 0.1 fusion.4
  182.9 34.1 %collective-permute-done.12 = bf16[1,192,1024]{2,1,0:T(8,128)(2,1)S(1)} collective-permute-done((bf16[1,192,1024]{2,1,0:T(8,128)(2,1)S(1)}, bf16[1,192,1024]{2,1,0:T(8,128)(2,1)S(1)}, u32[]{:S(2)}, u32[]{:S(2)}) %collective-permute-start.12) | collective-permute-done | bytes 393248 | tf_op jit(solution)/shard_map/ppermute | solution.py:108
  217.0 0.1 fusion.5
  217.2 10.8 %collective-permute-done.13 = bf16[192,1024]{1,0:T(8,128)(2,1)S(1)} collective-permute-done((bf16[192,1024]{1,0:T(8,128)(2,1)S(1)}, bf16[192,1024]{1,0:T(8,128)(2,1)S(1)}, u32[]{:S(2)}, u32[]{:S(2)}) %collective-permute-start.13) | collective-permute-done | bytes 393248 | tf_op jit(solution)/shard_map/ppermute | solution.py:103
  228.0 5.7 %collective-permute-done.3 = bf16[1,384,1024]{2,1,0:T(8,128)(2,1)S(1)} collective-permute-done((bf16[1,384,1024]{2,1,0:T(8,128)(2,1)S(1)}, bf16[1,384,1024]{2,1,0:T(8,128)(2,1)S(1)}, u32[]{:S(2)}, u32[]{:S(2)}) %collective-permute-start.3) | collective-permute-done | bytes 786464 | tf_op jit(solution)/shard_map/ppermute | solution.py:108
  233.7 1.7 fusion.1
  235.4 1.4 maximum_bitcast_fusion
  236.8 3.3 %collective-permute-start.15 = (f32[1,2]{1,0:T(1,128)S(1)}, f32[1,2]{1,0:T(1,128)S(1)}, u32[]{:S(2)}, u32[]{:S(2)}) collective-permute-start(f32[1,2]{1,0:T(1,128)S(1)} %maximum_bitcast_fusion), channel_id=1, source_target_pairs={{0,8},{4,12},{8,0},{12,4},{1,9},{5,13},{9,1},{13,5},{2,10},{6,14},... | collective-permute-start | bytes 32 | tf_op jit(solution)/shard_map/ppermute | solution.py:103
  240.0 0.6 collective-permute-start.16
  240.6 1.3 add_convert_fusion
  241.9 0.2 collective-permute-done.14
  242.1 1.5 collective-permute-done.16
  243.6 1.4 add_add_fusion
  245.0 0.5 collective-permute-start.17
  245.5 3.0 %collective-permute-done.17 = f32[1,2]{1,0:T(1,128)S(1)} collective-permute-done((f32[1,2]{1,0:T(1,128)S(1)}, f32[1,2]{1,0:T(1,128)S(1)}, u32[]{:S(2)}, u32[]{:S(2)}) %collective-permute-start.17) | collective-permute-done | bytes 40 | tf_op jit(solution)/shard_map/ppermute | solution.py:103
  248.5 0.6 fusion.6
  250.5 0.9 collective-permute-start.18
  251.4 0.3 collective-permute-done.18
  (31 shorter events, 0.5 us)
Async XLA Ops:
  0.6 11.3 %copy-start = (bf16[1,4096]{1,0:T(2,128)(2,1)S(1)}, bf16[1,4096]{1,0:T(2,128)(2,1)}, u32[]{:S(2)}) copy-start(bf16[1,4096]{1,0:T(2,128)(2,1)} %param.10) | copy-start | bytes 24580
  0.6 7.2 %copy-start.2 = (bf16[1,384,4096]{2,1,0:T(8,128)(2,1)S(1)}, bf16[1,384,4096]{2,1,0:T(8,128)(2,1)}, u32[]{:S(2)}) copy-start(bf16[1,384,4096]{2,1,0:T(8,128)(2,1)} %param.7) | copy-start | bytes 9437188
  4.9 7.0 %collective-permute-start = (f32[1,1]{1,0:T(1,128)}, f32[1,1]{1,0:T(1,128)}, u32[]{:S(2)}, u32[]{:S(2)}) collective-permute-start(f32[1,1]{1,0:T(1,128)} %bitcast.4), channel_id=1, source_target_pairs={{0,2},{2,0},{1,3},{3,1},{4,6},{6,4},{5,7},{7,5},{8,10},{10,8},{9,1... | collective-permute-start | bytes 20 | tf_op jit(solution)/shard_map/ppermute | solution.py:103
  9.9 37.6 %collective-permute-start.4 = (bf16[192,4096]{1,0:T(8,128)(2,1)}, bf16[192,4096]{1,0:T(8,128)(2,1)}, u32[]{:S(2)}, u32[]{:S(2)}) collective-permute-start(bf16[192,4096]{1,0:T(8,128)(2,1)} %get-tuple-element.4), channel_id=1, source_target_pairs={{0,2},{2,0},{1,3},{3,1},{4,6},{6,4},{5,7},{7,5},{8,10},{10,8},{9,1... | collective-permute-start | bytes 4718600 | tf_op jit(solution)/shard_map/ppermute | solution.py:103
  9.9 69.9 %collective-permute-start.9 = (bf16[192,4096]{1,0:T(8,128)(2,1)}, bf16[192,4096]{1,0:T(8,128)(2,1)}, u32[]{:S(2)}, u32[]{:S(2)}) collective-permute-start(bf16[192,4096]{1,0:T(8,128)(2,1)} %get-tuple-element.5), channel_id=1, source_target_pairs={{0,2},{2,0},{1,3},{3,1},{4,6},{6,4},{5,7},{7,5},{8,10},{10,8},{9,1... | collective-permute-start | bytes 4718600 | tf_op jit(solution)/shard_map/ppermute | solution.py:103
  25.8 65.8 %collective-permute-start.1 = (bf16[384,2048]{1,0:T(8,128)(2,1)}, bf16[384,2048]{1,0:T(8,128)(2,1)S(1)}, u32[]{:S(2)}, u32[]{:S(2)}) collective-permute-start(bf16[384,2048]{1,0:T(8,128)(2,1)} %encode.3.c_ref), channel_id=1, source_target_pairs={{0,1},{2,3},{4,5},{6,7},{8,9},{10,11},{12,13},{14,15},{16,17},{18,... | collective-permute-start | bytes 4718600 | tf_op jit(solution)/shard_map/ppermute | solution.py:153
  57.9 53.1 %collective-permute-start.5 = (bf16[192,2048]{1,0:T(8,128)(2,1)S(1)}, bf16[192,2048]{1,0:T(8,128)(2,1)S(1)}, u32[]{:S(2)}, u32[]{:S(2)}) collective-permute-start(bf16[192,2048]{1,0:T(8,128)(2,1)S(1)} %encode.4.c_ref), channel_id=1, source_target_pairs={{0,1},{2,3},{4,5},{6,7},{8,9},{10,11},{12,13},{14,15},{16,17},{18,... | collective-permute-start | bytes 2359304 | tf_op jit(solution)/shard_map/ppermute | solution.py:153
  90.1 27.9 %collective-permute-start.10 = (bf16[192,2048]{1,0:T(8,128)(2,1)S(1)}, bf16[192,2048]{1,0:T(8,128)(2,1)S(1)}, u32[]{:S(2)}, u32[]{:S(2)}) collective-permute-start(bf16[192,2048]{1,0:T(8,128)(2,1)S(1)} %encode.5.c_ref), channel_id=1, source_target_pairs={{0,1},{2,3},{4,5},{6,7},{8,9},{10,11},{12,13},{14,15},{16,17},{18,... | collective-permute-start | bytes 2359304 | tf_op jit(solution)/shard_map/ppermute | solution.py:153
  99.9 80.6 %collective-permute-start.2 = (bf16[2,384,1024]{2,1,0:T(8,128)(2,1)S(1)}, bf16[2,384,1024]{2,1,0:T(8,128)(2,1)S(1)}, u32[]{:S(2)}, u32[]{:S(2)}) collective-permute-start(bf16[2,384,1024]{2,1,0:T(8,128)(2,1)S(1)} %decode.7), channel_id=1, source_target_pairs={{0,4},{4,0},{8,12},{12,8},{1,5},{5,1},{9,13},{13,9},{2,6},{6,2},{1... | collective-permute-start | bytes 4718600 | tf_op jit(solution)/shard_map/ppermute | solution.py:108
  117.5 35.6 %collective-permute-start.6 = (bf16[2,192,1024]{2,1,0:T(8,128)(2,1)S(1)}, bf16[2,192,1024]{2,1,0:T(8,128)(2,1)S(1)}, u32[]{:S(2)}, u32[]{:S(2)}) collective-permute-start(bf16[2,192,1024]{2,1,0:T(8,128)(2,1)S(1)} %decode.9), channel_id=1, source_target_pairs={{0,4},{4,0},{8,12},{12,8},{1,5},{5,1},{9,13},{13,9},{2,6},{6,2},{1... | collective-permute-start | bytes 2359304 | tf_op jit(solution)/shard_map/ppermute | solution.py:108
  124.6 53.7 %collective-permute-start.11 = (bf16[2,192,1024]{2,1,0:T(8,128)(2,1)S(1)}, bf16[2,192,1024]{2,1,0:T(8,128)(2,1)S(1)}, u32[]{:S(2)}, u32[]{:S(2)}) collective-permute-start(bf16[2,192,1024]{2,1,0:T(8,128)(2,1)S(1)} %decode.11), channel_id=1, source_target_pairs={{0,4},{4,0},{8,12},{12,8},{1,5},{5,1},{9,13},{13,9},{2,6},{6,2},{1... | collective-permute-start | bytes 2359304 | tf_op jit(solution)/shard_map/ppermute | solution.py:108
  153.4 27.0 %copy-start.3 = (f32[2,384,1024]{2,1,0:T(8,128)S(1)}, f32[2,384,1024]{2,1,0:T(8,128)}, u32[]{:S(2)}) copy-start(f32[2,384,1024]{2,1,0:T(8,128)} %decode.6) | copy-start | bytes 9437188
  153.5 29.2 %collective-permute-start.7 = (bf16[1,192,1024]{2,1,0:T(8,128)(2,1)S(1)}, bf16[1,192,1024]{2,1,0:T(8,128)(2,1)S(1)}, u32[]{:S(2)}, u32[]{:S(2)}) collective-permute-start(bf16[1,192,1024]{2,1,0:T(8,128)(2,1)S(1)} %dynamic-slice_convert_fusion.2), channel_id=1, source_target_pairs={{0,8},{4,12},{8,0},{12,4},{1,9},{5,13},{9,1},{13,5},{2,10},{6,14},... | collective-permute-start | bytes 1179656 | tf_op jit(solution)/shard_map/ppermute | solution.py:108
  178.7 38.2 %collective-permute-start.12 = (bf16[1,192,1024]{2,1,0:T(8,128)(2,1)S(1)}, bf16[1,192,1024]{2,1,0:T(8,128)(2,1)S(1)}, u32[]{:S(2)}, u32[]{:S(2)}) collective-permute-start(bf16[1,192,1024]{2,1,0:T(8,128)(2,1)S(1)} %dynamic-slice_convert_fusion.1), channel_id=1, source_target_pairs={{0,8},{4,12},{8,0},{12,4},{1,9},{5,13},{9,1},{13,5},{2,10},{6,14},... | collective-permute-start | bytes 1179656 | tf_op jit(solution)/shard_map/ppermute | solution.py:108
  181.3 35.8 %copy-start.5 = (bf16[1,1024]{1,0:T(2,128)(2,1)S(1)}, bf16[1,1024]{1,0:T(2,128)(2,1)}, u32[]{:S(2)}) copy-start(bf16[1,1024]{1,0:T(2,128)(2,1)} %param.13) | copy-start | bytes 6148
  181.3 52.3 %copy-start.4 = (bf16[1,384,1024]{2,1,0:T(8,128)(2,1)S(1)}, bf16[1,384,1024]{2,1,0:T(8,128)(2,1)}, u32[]{:S(2)}) copy-start(bf16[1,384,1024]{2,1,0:T(8,128)(2,1)} %param.8) | copy-start | bytes 2359300
  181.4 52.3 %collective-permute-start.3 = (bf16[1,384,1024]{2,1,0:T(8,128)(2,1)S(1)}, bf16[1,384,1024]{2,1,0:T(8,128)(2,1)S(1)}, u32[]{:S(2)}, u32[]{:S(2)}) collective-permute-start(bf16[1,384,1024]{2,1,0:T(8,128)(2,1)S(1)} %dynamic-slice_convert_fusion), channel_id=1, source_target_pairs={{0,8},{4,12},{8,0},{12,4},{1,9},{5,13},{9,1},{13,5},{2,10},{6,14},... | collective-permute-start | bytes 2359304 | tf_op jit(solution)/shard_map/ppermute | solution.py:108
  182.8 34.4 %collective-permute-start.8 = (bf16[192,1024]{1,0:T(8,128)(2,1)S(1)}, bf16[192,1024]{1,0:T(8,128)(2,1)S(1)}, u32[]{:S(2)}, u32[]{:S(2)}) collective-permute-start(bf16[192,1024]{1,0:T(8,128)(2,1)S(1)} %fusion.4), channel_id=1, source_target_pairs={{0,2},{2,0},{1,3},{3,1},{4,6},{6,4},{5,7},{7,5},{8,10},{10,8},{9,1... | collective-permute-start | bytes 1179656 | tf_op jit(solution)/shard_map/ppermute | solution.py:103
  217.1 11.0 %collective-permute-start.13 = (bf16[192,1024]{1,0:T(8,128)(2,1)S(1)}, bf16[192,1024]{1,0:T(8,128)(2,1)S(1)}, u32[]{:S(2)}, u32[]{:S(2)}) collective-permute-start(bf16[192,1024]{1,0:T(8,128)(2,1)S(1)} %fusion.5), channel_id=1, source_target_pairs={{0,2},{2,0},{1,3},{3,1},{4,6},{6,4},{5,7},{7,5},{8,10},{10,8},{9,1... | collective-permute-start | bytes 1179656 | tf_op jit(solution)/shard_map/ppermute | solution.py:103
  236.8 5.3 %collective-permute-start.14 = (f32[1,2]{1,0:T(1,128)S(1)}, f32[1,2]{1,0:T(1,128)S(1)}, u32[]{:S(2)}, u32[]{:S(2)}) collective-permute-start(f32[1,2]{1,0:T(1,128)S(1)} %maximum_bitcast_fusion), channel_id=1, source_target_pairs={{0,4},{4,8},{8,12},{12,0},{1,5},{5,9},{9,13},{13,1},{2,6},{6,10},{... | collective-permute-start | bytes 32 | tf_op jit(solution)/shard_map/ppermute | solution.py:103
  236.8 5.3 %collective-permute-start.15 = (f32[1,2]{1,0:T(1,128)S(1)}, f32[1,2]{1,0:T(1,128)S(1)}, u32[]{:S(2)}, u32[]{:S(2)}) collective-permute-start(f32[1,2]{1,0:T(1,128)S(1)} %maximum_bitcast_fusion), channel_id=1, source_target_pairs={{0,8},{4,12},{8,0},{12,4},{1,9},{5,13},{9,1},{13,5},{2,10},{6,14},... | collective-permute-start | bytes 32 | tf_op jit(solution)/shard_map/ppermute | solution.py:103
  240.0 3.5 %collective-permute-start.16 = (f32[1,2]{1,0:T(1,128)S(1)}, f32[1,2]{1,0:T(1,128)S(1)}, u32[]{:S(2)}, u32[]{:S(2)}) collective-permute-start(f32[1,2]{1,0:T(1,128)S(1)} %maximum_bitcast_fusion), channel_id=1, source_target_pairs={{0,12},{4,0},{8,4},{12,8},{1,13},{5,1},{9,5},{13,9},{2,14},{6,2},{... | collective-permute-start | bytes 32 | tf_op jit(solution)/shard_map/ppermute | solution.py:103
  240.6 11.8 %copy-start.1 = (bf16[1,4096]{1,0:T(2,128)(2,1)S(1)}, bf16[1,4096]{1,0:T(2,128)(2,1)}, u32[]{:S(2)}) copy-start(bf16[1,4096]{1,0:T(2,128)(2,1)} %param.10) | copy-start | bytes 24580
  245.0 3.5 %collective-permute-start.17 = (f32[1,2]{1,0:T(1,128)S(1)}, f32[1,2]{1,0:T(1,128)S(1)}, u32[]{:S(2)}, u32[]{:S(2)}) collective-permute-start(f32[1,2]{1,0:T(1,128)S(1)} %add_add_fusion), channel_id=1, source_target_pairs={{0,2},{2,0},{1,3},{3,1},{4,6},{6,4},{5,7},{7,5},{8,10},{10,8},{9,1... | collective-permute-start | bytes 32 | tf_op jit(solution)/shard_map/ppermute | solution.py:103
  250.5 1.2 collective-permute-start.18

commit v2 on v1

v2 whole, which is shorter than its diff:
```python
import jax
import jax.numpy as jnp
from jax import lax
from jax.experimental import pallas as pl
from jax.experimental.pallas import tpu as pltpu
from jax.sharding import PartitionSpec as P

VMEM_LIMIT = 24 * 1024 * 1024
SLOTS = 3


def tile_of(size, most):
    tile = min(size, most)
    while size % tile:
        tile //= 2
    return tile


def square_body(x_ref, o_ref):
    @pl.when(pl.program_id(0) == 0)
    def _():
        o_ref[...] = jnp.zeros_like(o_ref)

    value = x_ref[...].astype(jnp.float32)
    value = value * value
    rows, width = value.shape
    o_ref[...] += jnp.sum(value.reshape(rows // 8, 8, width), axis=0)


def square_sum(x):
    rows, width = x.shape
    tile = tile_of(rows, 96)
    sums = pl.pallas_call(
        square_body,
        grid=(rows // tile,),
        in_specs=[pl.BlockSpec((tile, width), lambda i: (i, 0))],
        out_specs=pl.BlockSpec((8, width), lambda i: (0, 0)),
        out_shape=jax.ShapeDtypeStruct((8, width), jnp.float32),
        cost_estimate=pl.CostEstimate(
            flops=2 * rows * width, bytes_accessed=2 * rows * width, transcendentals=0
        ),
        name="square_sum",
    )(x)
    return jnp.sum(sums)


def ring_loop(count, per, depth, start, wait, lhs, ring, acc, finish):
    slots = ring.shape[0]
    for t in range(slots):
        @pl.when(t < count)
        def _():
            start(t)

    def step(t, carry):
        r = lax.rem(t, per)
        slot = lax.rem(t, slots)
        wait(t, r, slot)
        left = lhs[:, pl.ds(pl.multiple_of(r * depth, depth), depth)]
        part = jnp.dot(left, ring[slot], preferred_element_type=jnp.float32)

        @pl.when(r == 0)
        def _():
            acc[...] = part

        @pl.when(r > 0)
        def _():
            acc[...] += part

        @pl.when(t + slots < count)
        def _():
            start(t + slots)

        @pl.when(r == per - 1)
        def _():
            finish(lax.div(t, per))

        return carry

    lax.fori_loop(0, count, step, 0)


def encode(pieces, places, inv, weight, bias, after):
    sizes = [piece.shape[0] for piece in pieces]
    rows, width = sum(sizes), pieces[0].shape[1]
    latents = weight.shape[1]
    tile = tile_of(latents, 1024)
    depth = tile_of(width, 1024)
    per = width // depth
    count = (latents // tile) * per
    n = len(pieces)

    def body(places_ref, inv_ref, b_ref, *refs):
        x_refs, (w_ref, after_ref, o_ref, lhs, ring, acc, lhs_sem, ring_sem) = refs[:n], refs[n:]

        def lhs_copy(i, r):
            part = pl.ds(r * depth, depth)
            place = pl.ds(pl.multiple_of(places_ref[i], 16), sizes[i])
            return pltpu.make_async_copy(
                x_refs[i].at[:, part], lhs.at[place, part], lhs_sem.at[i, r])

        def tile_copy(t):
            b, r, slot = t // per, t % per, t % SLOTS
            down = pl.ds(pl.multiple_of(r * depth, depth), depth)
            across = pl.ds(pl.multiple_of(b * tile, tile), tile)
            return pltpu.make_async_copy(w_ref.at[down, across], ring.at[slot], ring_sem.at[slot])

        for r in range(per):
            for i in range(n):
                lhs_copy(i, r).start()

        def wait(t, r, slot):
            for s in range(per):
                @pl.when(t == s)
                def _():
                    for i in range(n):
                        lhs_copy(i, s).wait()
            tile_copy(t).wait()

        def finish(b):
            across = pl.ds(pl.multiple_of(b * tile, tile), tile)
            pre = acc[...] * inv_ref[0] + b_ref[:, across].astype(jnp.float32)
            o_ref[:, across] = jnp.maximum(pre, 0.0).astype(o_ref.dtype)

        ring_loop(count, per, depth, lambda t: tile_copy(t).start(), wait, lhs, ring, acc, finish)

    return pl.pallas_call(
        body,
        in_specs=[
            pl.BlockSpec(memory_space=pltpu.SMEM),
            pl.BlockSpec(memory_space=pltpu.SMEM),
            pl.BlockSpec(memory_space=pltpu.VMEM),
        ] + [pl.BlockSpec(memory_space=pl.ANY)] * (n + 2),
        out_specs=pl.BlockSpec(memory_space=pltpu.VMEM),
        out_shape=jax.ShapeDtypeStruct((rows, latents), jnp.bfloat16),
        scratch_shapes=[
            pltpu.VMEM((rows, width), jnp.bfloat16),
            pltpu.VMEM((SLOTS, depth, tile), jnp.bfloat16),
            pltpu.VMEM((rows, tile), jnp.float32),
            pltpu.SemaphoreType.DMA((n, per)),
            pltpu.SemaphoreType.DMA((SLOTS,)),
        ],
        compiler_params=pltpu.CompilerParams(vmem_limit_bytes=VMEM_LIMIT),
        cost_estimate=pl.CostEstimate(
            flops=2 * rows * width * latents,
            bytes_accessed=2 * (rows * width + width * latents + rows * latents),
            transcendentals=0,
        ),
        name="encode",
    )(places, inv.reshape(1), bias, *pieces, weight, after)


def decode(codes, earlier, own_w, cross_w, info, group, width, dtype):
    rows, latents = codes.shape
    depth = tile_of(latents, 1024)
    steps = latents // depth

    def body(info_ref, c_ref, e_ref, s_ref, x_ref, first_ref, second_ref, lhs, ring, acc, lhs_sem, ring_sem):
        later = info_ref[0] != 0
        per = jnp.where(later, 2 * steps, steps)
        count = 2 * group * per

        def lhs_copy(source, i):
            part = pl.ds((i % steps) * depth, depth)
            return pltpu.make_async_copy(
                source.at[:, part], lhs.at[:, pl.ds(i * depth, depth)], lhs_sem.at[i])

        def tile_copy(source, t, k):
            slot = lax.rem(t, SLOTS)
            down = pl.ds(pl.multiple_of(k * depth, depth), depth)
            across = pl.ds(pl.multiple_of(info_ref[1 + lax.div(t, per)] * width, width), width)
            return pltpu.make_async_copy(source.at[down, across], ring.at[slot], ring_sem.at[slot])

        def start(t):
            r = lax.rem(t, per)

            @pl.when(r < steps)
            def _():
                tile_copy(s_ref, t, r).start()

            @pl.when(r >= steps)
            def _():
                tile_copy(x_ref, t, r - steps).start()

        for i in range(steps):
            lhs_copy(c_ref, i).start()

        @pl.when(later)
        def _():
            for i in range(steps, 2 * steps):
                lhs_copy(e_ref, i).start()

        def wait(t, r, slot):
            for i in range(2 * steps):
                @pl.when((t == i) & (t < per))
                def _():
                    lhs_copy(c_ref, i).wait()
            tile_copy(s_ref, t, 0).wait()

        def finish(b):
            @pl.when(b < group)
            def _():
                first_ref[jnp.minimum(b, group - 1)] = acc[...].astype(dtype)

            @pl.when(b >= group)
            def _():
                second_ref[jnp.maximum(b - group, 0)] = acc[...].astype(dtype)

        ring_loop(count, per, depth, start, wait, lhs, ring, acc, finish)

    return pl.pallas_call(
        body,
        in_specs=[pl.BlockSpec(memory_space=pltpu.SMEM)] + [pl.BlockSpec(memory_space=pl.ANY)] * 4,
        out_specs=[pl.BlockSpec(memory_space=pltpu.VMEM)] * 2,
        out_shape=[jax.ShapeDtypeStruct((group, rows, width), dtype)] * 2,
        scratch_shapes=[
            pltpu.VMEM((rows, 2 * latents), jnp.bfloat16),
            pltpu.VMEM((SLOTS, depth, width), jnp.bfloat16),
            pltpu.VMEM((rows, width), jnp.float32),
            pltpu.SemaphoreType.DMA((2 * steps,)),
            pltpu.SemaphoreType.DMA((SLOTS,)),
        ],
        compiler_params=pltpu.CompilerParams(vmem_limit_bytes=VMEM_LIMIT),
        cost_estimate=pl.CostEstimate(
            flops=8 * rows * latents * group * width,
            bytes_accessed=4 * (rows * latents + 2 * latents * group * width) + 8 * rows * group * width,
            transcendentals=0,
        ),
        name="decode",
    )(info, codes, earlier, own_w, cross_w)


def shifted(value, axis, distance):
    n = lax.axis_size(axis)
    return lax.ppermute(value, axis, [(i, (i + distance) % n) for i in range(n)])


def swapped(value, axis, bit):
    n = lax.axis_size(axis)
    return lax.ppermute(value, axis, [(i, i ^ bit) for i in range(n)])


def sum_over(value, axis):
    total = value
    for distance in range(1, lax.axis_size(axis)):
        total = total + shifted(value, axis, distance)
    return total


def wide(value):
    return value.astype(jnp.float32)


def local(inputs, targets, enc_weight, encoder_layer_bias, dec_self, dec_cross, dec_bias):
    layer = lax.axis_index("layer")
    lat = lax.axis_index("latent")
    n_lat = lax.axis_size("latent")
    n_tok = lax.axis_size("token")
    x_own = inputs[0]
    rows, model = x_own.shape
    enc_w = enc_weight[0]
    own_w = dec_self[0]
    lat_dev = enc_w.shape[1]
    width = dec_bias.shape[1]
    quarter = rows // 4
    side = lat % 2

    square = sum_over(square_sum(x_own).reshape(1, 1), "token")
    scale = jnp.sqrt(square[0, 0] / (rows * n_tok * model) + 1e-06)
    inv = 1.0 / scale

    outer = lax.dynamic_slice_in_dim(x_own, side * 3 * quarter, quarter, axis=0)
    middle = x_own[quarter:3 * quarter]
    foreign = []
    for distance in range(1, n_tok):
        mine = shifted(outer, "token", distance)
        centre = shifted(middle, "token", distance)
        theirs = swapped(mine, "latent", 1)
        foreign.append((distance, mine, theirs, centre))

    bias = lax.dynamic_slice_in_dim(
        encoder_layer_bias, lax.axis_index("token") * lat_dev, lat_dev, axis=1
    )

    group = n_lat // 4
    other, mine_bit = 1 - lat % 2, lat % 2
    far, near = 1 - (lat // 2) % 2, (lat // 2) % 2
    info_sent = jnp.stack(
        [layer] + [4 * i + 2 * b + other for b in (far, near) for i in range(group)]
    ).astype(jnp.int32)
    info_kept = jnp.stack(
        [layer] + [4 * i + 2 * b + mine_bit for b in (far, near) for i in range(group)]
    ).astype(jnp.int32)

    def work(pieces, places, after):
        codes = encode(pieces, jnp.stack(places).astype(jnp.int32), inv, enc_w, bias, after)
        height = codes.shape[0]
        earlier = lax.ppermute(codes, "layer", [(0, 1)])
        far_sent, near_sent = decode(
            codes, earlier, own_w, dec_cross, info_sent, group, width, jnp.bfloat16)
        far_in = swapped(far_sent, "latent", 1)
        near_in = swapped(near_sent, "latent", 1)
        far_kept, near_kept = decode(
            codes, earlier, own_w, dec_cross, info_kept, group, width, jnp.float32)
        across = swapped((far_kept + wide(far_in)).astype(jnp.bfloat16), "latent", 2)
        total = near_kept + wide(near_in) + wide(across)
        bit = 4
        while bit < n_lat:
            here = (lat // bit) % 2
            pairs = total.reshape(total.shape[0] // 2, 2, height, width)
            away = lax.dynamic_index_in_dim(pairs, 1 - here, 1, keepdims=False)
            arrived = swapped(away.astype(jnp.bfloat16), "latent", bit)
            total = lax.dynamic_index_in_dim(pairs, here, 1, keepdims=False) + wide(arrived)
            bit *= 2
        return total[0], near_kept

    origin = jnp.int32(0)
    total, after = work([x_own], [origin], x_own)
    for distance, mine, theirs, centre in foreign:
        part, after = work([mine, theirs], [side * quarter, (1 - side) * quarter], after)
        ends = shifted(part.astype(jnp.bfloat16), "token", n_tok - distance)
        part, after = work([centre], [origin], after)
        centre = shifted(part.astype(jnp.bfloat16), "token", n_tok - distance)
        total = total + wide(jnp.concatenate([ends[:quarter], centre, ends[quarter:]]))
    total = total + wide(dec_bias)
    recon = total.astype(jnp.bfloat16)[None]

    target = wide(targets[0])
    diff = total - target
    sums = jnp.stack([jnp.sum(diff * diff), jnp.sum(target * target)]).reshape(1, 2)
    sums = sum_over(sum_over(sums, "latent"), "token")
    ratio = sums[:, 0] / sums[:, 1]
    loss = sum_over(ratio, "layer") / 2.0
    return (recon, loss)


def solution(mesh):
    return jax.shard_map(
        local,
        mesh=mesh,
        in_specs=(
            P("layer", ("groups", "token"), None),
            P("layer", ("groups", "token"), "latent"),
            P("layer", None, ("latent", "token")),
            P("layer", "latent"),
            P("layer", ("latent", "token"), None),
            P(("latent", "token"), None),
            P("layer", "latent"),
        ),
        out_specs=(P("layer", ("groups", "token"), "latent"), P("groups")),
        check_vma=False,
    )
```

time: 254 us -> 267 us (1.051)
  local copies, waits for them, and re-layouts: 2.88 us -> 33.6 us
  waiting for transfers between devices: 132 us -> 117 us
  starting transfers between devices: 24.1 us -> 35 us
  Pallas kernels: 77.3 us -> 67.4 us
  other arithmetic: 11.8 us -> 8.58 us
    ppermute x10, waiting for transfers between devices: 56.4 us -> 23.7 us  [shifted(): lax.ppermute(value, axis, [(i, (i + distance) % n) for i in range(n)])]
    unnamed x12 -> x44, local copies, waits for them, and re-layouts: 0.04 us -> 30.7 us
    ppermute x6 -> x10, waiting for transfers between devices: 75.6 us -> 91.1 us  [swapped(): return lax.ppermute(value, axis, [(i, i ^ bit) for i in range(n)])]
    pallas_call x9 -> x10, Pallas kernels: 77.3 us -> 67.4 us  [the longest x6 32.2 us: decode(): pl.pallas_call(body, in_specs=[pl.BlockSpec(memory_space=pltpu.SMEM)] + [...]
    ppermute x3, starting transfers between devices: 4.24 us -> 10.1 us  [work(): earlier = lax.ppermute(codes, 'layer', [(0, 1)])]
    ppermute x6 -> x10, starting transfers between devices: 9.51 us -> 12.5 us  [swapped(): return lax.ppermute(value, axis, [(i, i ^ bit) for i in range(n)])]
    reduce_sum x1, other arithmetic: 4.26 us -> 1.54 us  [square_sum(): return jnp.sum(sums)]
  transfers between devices with their start and end apart: 19 -> 23, of which waited for: 11 -> 10; matrix products, arithmetic and copies ran while one was open for 2% -> 2% of each run, Pallas kernels for 30% -> 15%
where the time goes in v2:
time: 267 us
  waiting for transfers between devices  117 us (44%)
  Pallas kernels  67.4 us (25%)
  starting transfers between devices  35 us (13%)
  local copies, waits for them, and re-layouts  33.6 us (13%)
  other arithmetic  8.58 us (3%)
  between operations  5.44 us (2%)
    ppermute x10, waiting for transfers between devices, swapped(): return lax.ppermute(value, axis, [(i, i ^ bit) for i in range(n)])  91.1 us
    pallas_call x6, Pallas kernels, decode(): pl.pallas_call(body, in_specs=[pl.BlockSpec(memory_space=pltpu.SMEM)] + [...  32.2 us
    pallas_call x3, Pallas kernels, encode(): pl.pallas_call(body, in_specs=[pl.BlockSpec(memory_space=pltpu.SMEM), pl....  31.7 us
    unnamed x44, local copies, waits for them, and re-layouts  30.7 us
    ppermute x10, waiting for transfers between devices, shifted(): lax.ppermute(value, axis, [(i, (i + distance) % n) for i in range(n)])  23.7 us
    ppermute x10, starting transfers between devices, swapped(): return lax.ppermute(value, axis, [(i, i ^ bit) for i in range(n)])  12.5 us
    ppermute x10, starting transfers between devices, shifted(): lax.ppermute(value, axis, [(i, (i + distance) % n) for i in range(n)])  12.5 us
    ppermute x3, starting transfers between devices, work(): earlier = lax.ppermute(codes, 'layer', [(0, 1)])  10.1 us
  transfers between devices with their start and end apart: 23, of which 10 were waited for; matrix products, arithmetic and copies ran while one was open for 2% of the time, Pallas kernels for 15%

profile of v2, /device:TPU:0, one launch (start us, length us, event | category | flops | bytes accessed | tf_op | source)
XLA Modules:
  0.0 266.7 jit_solution(2274662760450972297)
XLA Ops:
  0.7 3.5 %square_sum.1 = f32[8,4096]{1,0:T(8,128)} custom-call(bf16[384,4096]{1,0:T(8,128)(2,1)} %bitcast.54), custom_call_target="tpu_custom_call" | custom-call | flops 3145728 | bytes 3145728 | tf_op jit(solution)/shard_map/square_sum/pallas_call | solution.py:33
  4.2 1.5 reduce_sum.27
  5.7 2.9 %collective-permute-start = (f32[1,1]{1,0:T(1,128)}, f32[1,1]{1,0:T(1,128)}, u32[]{:S(2)}, u32[]{:S(2)}) collective-permute-start(f32[1,1]{1,0:T(1,128)} %bitcast.4), channel_id=1, source_target_pairs={{0,2},{2,0},{1,3},{3,1},{4,6},{6,4},{5,7},{7,5},{8,10},{10,8},{9,1... | collective-permute-start | bytes 20 | tf_op jit(solution)/shard_map/ppermute | solution.py:234
  8.7 1.7 collective-permute-done
  11.8 5.8 %copy-done.4 = bf16[1,4096,2048]{2,1,0:T(8,128)(2,1)S(1)} copy-done((bf16[1,4096,2048]{2,1,0:T(8,128)(2,1)S(1)}, bf16[1,4096,2048]{2,1,0:T(8,128)(2,1)}, u32[]{:S(2)}) %copy-start.4) | copy-done | bytes 16777240
  17.5 14.2 %encode.3.c_ref = bf16[384,2048]{1,0:T(8,128)(2,1)} custom-call(s32[1]{0:T(128)} %constant.66.clone.1.places_ref, f32[1]{0:T(128)} %bitcast.5.inv_ref, bf16[1,2048]{1,0:T(2,128)(2,1)S(1)} %constant_dynamic-slice_fusion.b_ref, bf16[384,4096]{1,0:T(8,128)(2,1)S(1)} %bitcast.55, bf16[4096,2048]{1,0:T(8,128)(2,1)S(1)} %bitcast.51, bf16[384,4096]{1,0:T(8,128)(2,1)S(1)} %bitcast.56), custom_call_target="tpu_custom_call" | custom-call | flops 6442450944 | bytes 21495808 | tf_op jit(solution)/shard_map/encode/pallas_call | solution.py:126
  31.7 2.5 collective-permute-start.1
  34.2 0.9 dynamic-slice_bitcast_fusion
  35.1 2.0 collective-permute-start.5
  37.1 1.3 slice_bitcast_fusion
  38.5 17.4 %collective-permute-done.5.refs_0_ = bf16[96,4096]{1,0:T(8,128)(2,1)} collective-permute-done((bf16[96,4096]{1,0:T(8,128)(2,1)}, bf16[96,4096]{1,0:T(8,128)(2,1)}, u32[]{:S(2)}, u32[]{:S(2)}) %collective-permute-start.5) | collective-permute-done | bytes 786464 | tf_op jit(solution)/shard_map/ppermute | solution.py:234
  55.9 2.1 collective-permute-start.6
  58.2 5.8 %copy-done.2 = bf16[1,2048,4096]{2,1,0:T(8,128)(2,1)S(1)} copy-done((bf16[1,2048,4096]{2,1,0:T(8,128)(2,1)S(1)}, bf16[1,2048,4096]{2,1,0:T(8,128)(2,1)}, u32[]{:S(2)}) %copy-start.2) | copy-done | bytes 16777240
  63.9 6.7 %decode.6 = (f32[1,384,1024]{2,1,0:T(8,128)S(1)}, f32[1,384,1024]{2,1,0:T(8,128)S(1)}) custom-call(s32[3]{0:T(128)S(1)} %pad_add_fusion.info_ref, bf16[384,2048]{1,0:T(8,128)(2,1)} %encode.3.c_ref, bf16[384,2048]{1,0:T(8,128)(2,1)} %collective-permute-done.1.e_ref, bf16[2048,4096]{1,0:T(8,128)(2,1)S(1)} %bitcast.43, bf16[2048,4096]{1,0:T(8,128)(2,1)} %x_ref.11), custom_call_target="tpu_custom_call" | custom-call | flops 6442450944 | bytes 23068672 | tf_op jit(solution)/shard_map/decode/pallas_call | solution.py:210
  70.7 1.2 copy-done.12
  71.9 5.8 %copy-done.5 = bf16[1,4096,2048]{2,1,0:T(8,128)(2,1)S(1)} copy-done((bf16[1,4096,2048]{2,1,0:T(8,128)(2,1)S(1)}, bf16[1,4096,2048]{2,1,0:T(8,128)(2,1)}, u32[]{:S(2)}) %copy-start.5) | copy-done | bytes 16777240
  77.6 8.6 %encode.4.c_ref = bf16[192,2048]{1,0:T(8,128)(2,1)S(1)} custom-call(s32[2]{0:T(128)S(1)} %pad_add_fusion.2.places_ref, f32[1]{0:T(128)} %bitcast.5.inv_ref, bf16[1,2048]{1,0:T(2,128)(2,1)S(1)} %constant_dynamic-slice_fusion.b_ref, bf16[96,4096]{1,0:T(8,128)(2,1)} %collective-permute-done.5.refs_0_, bf16[96,4096]{1,0:T(8,128)(2,1)S(1)} %collective-permute-done.6.refs_1_, ...), custom_call_target="tpu_custom_call" | custom-call | flops 3221225472 | bytes 19136512 | tf_op jit(solution)/shard_map/encode/pallas_call | solution.py:126
  86.3 1.3 collective-permute-start.7
  87.7 1.8 collective-permute-done.7.e_ref
  89.5 5.8 %copy-done.3 = bf16[1,2048,4096]{2,1,0:T(8,128)(2,1)S(1)} copy-done((bf16[1,2048,4096]{2,1,0:T(8,128)(2,1)S(1)}, bf16[1,2048,4096]{2,1,0:T(8,128)(2,1)}, u32[]{:S(2)}) %copy-start.3) | copy-done | bytes 16777240
  95.3 4.7 %decode.8 = (f32[1,192,1024]{2,1,0:T(8,128)S(1)}, f32[1,192,1024]{2,1,0:T(8,128)S(1)}) custom-call(s32[3]{0:T(128)S(1)} %pad_add_fusion.info_ref, bf16[192,2048]{1,0:T(8,128)(2,1)S(1)} %encode.4.c_ref, bf16[192,2048]{1,0:T(8,128)(2,1)S(1)} %collective-permute-done.7.e_ref, bf16[2048,4096]{1,0:T(8,128)(2,1)S(1)} %bitcast.44, bf16[2048,4096]{1,0:T(8,128)(2,1)} %x_ref.11), custom_call_target="tpu_custom_call" | custom-call | flops 3221225472 | bytes 19922944 | tf_op jit(solution)/shard_map/decode/pallas_call | solution.py:210
  100.0 6.3 %copy-done.6 = bf16[1,4096,2048]{2,1,0:T(8,128)(2,1)S(1)} copy-done((bf16[1,4096,2048]{2,1,0:T(8,128)(2,1)S(1)}, bf16[1,4096,2048]{2,1,0:T(8,128)(2,1)}, u32[]{:S(2)}) %copy-start.6) | copy-done | bytes 16777240
  106.4 8.9 %encode.5.c_ref = bf16[192,2048]{1,0:T(8,128)(2,1)S(1)} custom-call(s32[1]{0:T(128)} %constant.66.clone.1.places_ref, f32[1]{0:T(128)} %bitcast.5.inv_ref, bf16[1,2048]{1,0:T(2,128)(2,1)S(1)} %constant_dynamic-slice_fusion.b_ref, bf16[192,4096]{1,0:T(8,128)(2,1)} %collective-permute-done.12.refs_0_, bf16[4096,2048]{1,0:T(8,128)(2,1)S(1)} %bitcast.53, ...), custom_call_target="tpu_custom_call" | custom-call | flops 3221225472 | bytes 19136512 | tf_op jit(solution)/shard_map/encode/pallas_call | solution.py:126
  115.2 6.3 %collective-permute-start.13 = (bf16[192,2048]{1,0:T(8,128)(2,1)S(1)}, bf16[192,2048]{1,0:T(8,128)(2,1)S(1)}, u32[]{:S(2)}, u32[]{:S(2)}) collective-permute-start(bf16[192,2048]{1,0:T(8,128)(2,1)S(1)} %encode.5.c_ref), channel_id=1, source_target_pairs={{0,1},{2,3},{4,5},{6,7},{8,9},{10,11},{12,13},{14,15},{16,17},{18,... | collective-permute-start | bytes 2359304 | tf_op jit(solution)/shard_map/ppermute | solution.py:297
  121.6 4.6 %decode.9 = (bf16[1,192,1024]{2,1,0:T(8,128)(2,1)S(1)}, bf16[1,192,1024]{2,1,0:T(8,128)(2,1)S(1)}) custom-call(s32[3]{0:T(128)S(1)} %pad_add_fusion.1.info_ref, bf16[192,2048]{1,0:T(8,128)(2,1)S(1)} %encode.4.c_ref, bf16[192,2048]{1,0:T(8,128)(2,1)S(1)} %copy-done.11, bf16[2048,4096]{1,0:T(8,128)(2,1)S(1)} %bitcast.47, bf16[2048,4096]{1,0:T(8,128)(2,1)} %x_ref.11), custom_call_target="tpu_custom_call" | custom-call | flops 3221225472 | bytes 19922944 | tf_op jit(solution)/shard_map/decode/pallas_call | solution.py:210
  126.3 6.7 %decode.7 = (bf16[1,384,1024]{2,1,0:T(8,128)(2,1)S(1)}, bf16[1,384,1024]{2,1,0:T(8,128)(2,1)S(1)}) custom-call(s32[3]{0:T(128)S(1)} %pad_add_fusion.1.info_ref, bf16[384,2048]{1,0:T(8,128)(2,1)} %encode.3.c_ref, bf16[384,2048]{1,0:T(8,128)(2,1)} %collective-permute-done.1.e_ref, bf16[2048,4096]{1,0:T(8,128)(2,1)S(1)} %bitcast.48, bf16[2048,4096]{1,0:T(8,128)(2,1)} %x_ref.11), custom_call_target="tpu_custom_call" | custom-call | flops 6442450944 | bytes 23068672 | tf_op jit(solution)/shard_map/decode/pallas_call | solution.py:210
  133.0 2.1 collective-permute-start.2
  135.1 1.9 collective-permute-start.8
  137.1 4.6 %decode.11 = (bf16[1,192,1024]{2,1,0:T(8,128)(2,1)S(1)}, bf16[1,192,1024]{2,1,0:T(8,128)(2,1)S(1)}) custom-call(s32[3]{0:T(128)S(1)} %pad_add_fusion.1.info_ref, bf16[192,2048]{1,0:T(8,128)(2,1)S(1)} %encode.5.c_ref, bf16[192,2048]{1,0:T(8,128)(2,1)S(1)} %collective-permute-done.13.e_ref, bf16[2048,4096]{1,0:T(8,128)(2,1)S(1)} %bitcast.49, ...), custom_call_target="tpu_custom_call" | custom-call | flops 3221225472 | bytes 19922944 | tf_op jit(solution)/shard_map/decode/pallas_call | solution.py:210
  142.0 3.0 %collective-permute-start.10 = (bf16[1,192,1024]{2,1,0:T(8,128)(2,1)S(1)}, bf16[1,192,1024]{2,1,0:T(8,128)(2,1)S(1)}, u32[]{:S(2)}, u32[]{:S(2)}) collective-permute-start(bf16[1,192,1024]{2,1,0:T(8,128)(2,1)S(1)} %add_convert_fusion.5), channel_id=1, source_target_pairs={{0,8},{4,12},{8,0},{12,4},{1,9},{5,13},{9,1},{13,5},{2,10},{6,14},... | collective-permute-start | bytes 1179656 | tf_op jit(solution)/shard_map/ppermute | solution.py:239
  145.0 4.9 %decode.10 = (f32[1,192,1024]{2,1,0:T(8,128)S(1)}, f32[1,192,1024]{2,1,0:T(8,128)S(1)}) custom-call(s32[3]{0:T(128)S(1)} %pad_add_fusion.info_ref, bf16[192,2048]{1,0:T(8,128)(2,1)S(1)} %encode.5.c_ref, bf16[192,2048]{1,0:T(8,128)(2,1)S(1)} %collective-permute-done.13.e_ref, bf16[2048,4096]{1,0:T(8,128)(2,1)S(1)} %bitcast.50, bf16[2048,4096]{1,0:T(8,128)(2,1)} %x_ref.11), custom_call_target="tpu_custom_call" | custom-call | flops 3221225472 | bytes 19922944 | tf_op jit(solution)/shard_map/decode/pallas_call | solution.py:210
  149.9 42.4 %collective-permute-done.15 = bf16[1,192,1024]{2,1,0:T(8,128)(2,1)S(1)} collective-permute-done((bf16[1,192,1024]{2,1,0:T(8,128)(2,1)S(1)}, bf16[1,192,1024]{2,1,0:T(8,128)(2,1)S(1)}, u32[]{:S(2)}, u32[]{:S(2)}) %collective-permute-start.15) | collective-permute-done | bytes 393248 | tf_op jit(solution)/shard_map/ppermute | solution.py:239
  192.4 1.8 collective-permute-start.16
  194.5 1.2 collective-permute-start.4
  195.9 1.4 collective-permute-start.11
  197.4 8.9 %collective-permute-done.14 = bf16[1,192,1024]{2,1,0:T(8,128)(2,1)S(1)} collective-permute-done((bf16[1,192,1024]{2,1,0:T(8,128)(2,1)S(1)}, bf16[1,192,1024]{2,1,0:T(8,128)(2,1)S(1)}, u32[]{:S(2)}, u32[]{:S(2)}) %collective-permute-start.14) | collective-permute-done | bytes 393248 | tf_op jit(solution)/shard_map/ppermute | solution.py:239
  206.3 5.0 %collective-permute-done.16 = bf16[1,192,1024]{2,1,0:T(8,128)(2,1)S(1)} collective-permute-done((bf16[1,192,1024]{2,1,0:T(8,128)(2,1)S(1)}, bf16[1,192,1024]{2,1,0:T(8,128)(2,1)S(1)}, u32[]{:S(2)}, u32[]{:S(2)}) %collective-permute-start.16) | collective-permute-done | bytes 393248 | tf_op jit(solution)/shard_map/ppermute | solution.py:239
  212.4 34.8 %collective-permute-done.4 = bf16[1,384,1024]{2,1,0:T(8,128)(2,1)S(1)} collective-permute-done((bf16[1,384,1024]{2,1,0:T(8,128)(2,1)S(1)}, bf16[1,384,1024]{2,1,0:T(8,128)(2,1)S(1)}, u32[]{:S(2)}, u32[]{:S(2)}) %collective-permute-start.4) | collective-permute-done | bytes 786464 | tf_op jit(solution)/shard_map/ppermute | solution.py:239
  247.2 1.8 fusion.1
  249.0 1.4 maximum_bitcast_fusion
  250.4 2.0 collective-permute-start.18
  252.4 1.5 add_convert_fusion
  253.9 0.9 collective-permute-done.19
  254.8 1.5 collective-permute-done.18
  256.2 1.4 add_add_fusion
  257.6 1.3 collective-permute-start.21
  258.9 2.2 collective-permute-done.21
  263.1 1.9 collective-permute-start.22
  (73 shorter events, 3.0 us)
Async XLA Ops:
  0.6 8.0 %copy-start = (bf16[1,4096]{1,0:T(2,128)(2,1)S(1)}, bf16[1,4096]{1,0:T(2,128)(2,1)}, u32[]{:S(2)}) copy-start(bf16[1,4096]{1,0:T(2,128)(2,1)} %param.10) | copy-start | bytes 24580
  0.6 11.1 %copy-start.7 = (bf16[1,384,4096]{2,1,0:T(8,128)(2,1)S(1)}, bf16[1,384,4096]{2,1,0:T(8,128)(2,1)}, u32[]{:S(2)}) copy-start(bf16[1,384,4096]{2,1,0:T(8,128)(2,1)} %param.7) | copy-start | bytes 9437188
  5.7 4.7 %collective-permute-start = (f32[1,1]{1,0:T(1,128)}, f32[1,1]{1,0:T(1,128)}, u32[]{:S(2)}, u32[]{:S(2)}) collective-permute-start(f32[1,1]{1,0:T(1,128)} %bitcast.4), channel_id=1, source_target_pairs={{0,2},{2,0},{1,3},{3,1},{4,6},{6,4},{5,7},{7,5},{8,10},{10,8},{9,1... | collective-permute-start | bytes 20 | tf_op jit(solution)/shard_map/ppermute | solution.py:234
  11.8 5.8 %copy-start.4 = (bf16[1,4096,2048]{2,1,0:T(8,128)(2,1)S(1)}, bf16[1,4096,2048]{2,1,0:T(8,128)(2,1)}, u32[]{:S(2)}) copy-start(bf16[1,4096,2048]{2,1,0:T(8,128)(2,1)} %param.9) | copy-start | bytes 50331652
  31.7 26.4 %collective-permute-start.1 = (bf16[384,2048]{1,0:T(8,128)(2,1)}, bf16[384,2048]{1,0:T(8,128)(2,1)}, u32[]{:S(2)}, u32[]{:S(2)}) collective-permute-start(bf16[384,2048]{1,0:T(8,128)(2,1)} %encode.3.c_ref), channel_id=1, source_target_pairs={{0,1},{2,3},{4,5},{6,7},{8,9},{10,11},{12,13},{14,15},{16,17},{18,... | collective-permute-start | bytes 4718600 | tf_op jit(solution)/shard_map/ppermute | solution.py:297
  35.1 20.8 %collective-permute-start.5 = (bf16[96,4096]{1,0:T(8,128)(2,1)}, bf16[96,4096]{1,0:T(8,128)(2,1)}, u32[]{:S(2)}, u32[]{:S(2)}) collective-permute-start(bf16[96,4096]{1,0:T(8,128)(2,1)} %dynamic-slice_bitcast_fusion), channel_id=1, source_target_pairs={{0,2},{2,0},{1,3},{3,1},{4,6},{6,4},{5,7},{7,5},{8,10},{10,8},{9,1... | collective-permute-start | bytes 2359304 | tf_op jit(solution)/shard_map/ppermute | solution.py:234
  38.5 61.5 %collective-permute-start.12 = (bf16[192,4096]{1,0:T(8,128)(2,1)}, bf16[192,4096]{1,0:T(8,128)(2,1)}, u32[]{:S(2)}, u32[]{:S(2)}) collective-permute-start(bf16[192,4096]{1,0:T(8,128)(2,1)} %slice_bitcast_fusion), channel_id=1, source_target_pairs={{0,2},{2,0},{1,3},{3,1},{4,6},{6,4},{5,7},{7,5},{8,10},{10,8},{9,1... | collective-permute-start | bytes 4718600 | tf_op jit(solution)/shard_map/ppermute | solution.py:234
  55.9 16.0 %collective-permute-start.6 = (bf16[96,4096]{1,0:T(8,128)(2,1)}, bf16[96,4096]{1,0:T(8,128)(2,1)S(1)}, u32[]{:S(2)}, u32[]{:S(2)}) collective-permute-start(bf16[96,4096]{1,0:T(8,128)(2,1)} %collective-permute-done.5.refs_0_), channel_id=1, source_target_pairs={{0,4},{4,0},{8,12},{12,8},{1,5},{5,1},{9,13},{13,9},{2,6},{6,2},{1... | collective-permute-start | bytes 2359304 | tf_op jit(solution)/shard_map/ppermute | solution.py:239
  58.2 5.8 %copy-start.2 = (bf16[1,2048,4096]{2,1,0:T(8,128)(2,1)S(1)}, bf16[1,2048,4096]{2,1,0:T(8,128)(2,1)}, u32[]{:S(2)}) copy-start(bf16[1,2048,4096]{2,1,0:T(8,128)(2,1)} %param.11) | copy-start | bytes 50331652
  70.7 1.2 copy-start.12
  71.9 5.8 %copy-start.5 = (bf16[1,4096,2048]{2,1,0:T(8,128)(2,1)S(1)}, bf16[1,4096,2048]{2,1,0:T(8,128)(2,1)}, u32[]{:S(2)}) copy-start(bf16[1,4096,2048]{2,1,0:T(8,128)(2,1)} %param.9) | copy-start | bytes 50331652
  86.3 3.2 %collective-permute-start.7 = (bf16[192,2048]{1,0:T(8,128)(2,1)S(1)}, bf16[192,2048]{1,0:T(8,128)(2,1)S(1)}, u32[]{:S(2)}, u32[]{:S(2)}) collective-permute-start(bf16[192,2048]{1,0:T(8,128)(2,1)S(1)} %encode.4.c_ref), channel_id=1, source_target_pairs={{0,1},{2,3},{4,5},{6,7},{8,9},{10,11},{12,13},{14,15},{16,17},{18,... | collective-permute-start | bytes 2359304 | tf_op jit(solution)/shard_map/ppermute | solution.py:297
  89.5 5.8 %copy-start.3 = (bf16[1,2048,4096]{2,1,0:T(8,128)(2,1)S(1)}, bf16[1,2048,4096]{2,1,0:T(8,128)(2,1)}, u32[]{:S(2)}) copy-start(bf16[1,2048,4096]{2,1,0:T(8,128)(2,1)} %param.11) | copy-start | bytes 50331652
  95.2 4.7 %copy-start.10 = (bf16[192,2048]{1,0:T(8,128)(2,1)}, bf16[192,2048]{1,0:T(8,128)(2,1)S(1)}, u32[]{:S(2)}) copy-start(bf16[192,2048]{1,0:T(8,128)(2,1)S(1)} %collective-permute-done.7.e_ref) | copy-start | bytes 2359300
  95.2 26.3 %slice-start = ((s8[16777216]{0:T(1024)(128)(4,1)}), s8[4194304]{0:T(1024)(128)(4,1)S(1)}, s32[]{:S(2)}) async-start(s8[16777216]{0:T(1024)(128)(4,1)} %bitcast.45), calls=%async_computation | async-start | bytes 8388608
  95.3 26.3 %slice-start.1 = ((s8[16777216]{0:T(1024)(128)(4,1)}), s8[4194304]{0:T(1024)(128)(4,1)S(1)}, s32[]{:S(2)}) async-start(s8[16777216]{0:T(1024)(128)(4,1)} %bitcast.45), calls=%async_computation.1 | async-start | bytes 8388608
  95.3 26.3 %slice-start.2 = ((s8[16777216]{0:T(1024)(128)(4,1)}), s8[4194304]{0:T(1024)(128)(4,1)S(1)}, s32[]{:S(2)}) async-start(s8[16777216]{0:T(1024)(128)(4,1)} %bitcast.45), calls=%async_computation.2 | async-start | bytes 8388608
  100.0 15.2 %copy-start.8 = (f32[1,192,1024]{2,1,0:T(8,128)}, f32[1,192,1024]{2,1,0:T(8,128)S(1)}, u32[]{:S(2)}) copy-start(f32[1,192,1024]{2,1,0:T(8,128)S(1)} %get-tuple-element.18.refs_2_) | copy-start | bytes 2359300
  100.0 15.2 %copy-start.14 = (f32[1,192,1024]{2,1,0:T(8,128)}, f32[1,192,1024]{2,1,0:T(8,128)S(1)}, u32[]{:S(2)}) copy-start(f32[1,192,1024]{2,1,0:T(8,128)S(1)} %get-tuple-element.20) | copy-start | bytes 2359300
  100.0 6.3 %copy-start.6 = (bf16[1,4096,2048]{2,1,0:T(8,128)(2,1)S(1)}, bf16[1,4096,2048]{2,1,0:T(8,128)(2,1)}, u32[]{:S(2)}) copy-start(bf16[1,4096,2048]{2,1,0:T(8,128)(2,1)} %param.9) | copy-start | bytes 50331652
  106.3 15.2 %slice-start.3 = ((s8[16777216]{0:T(1024)(128)(4,1)}), s8[4194304]{0:T(1024)(128)(4,1)S(1)}, s32[]{:S(2)}) async-start(s8[16777216]{0:T(1024)(128)(4,1)} %bitcast.45), calls=%async_computation.3 | async-start | bytes 8388608
  106.3 15.2 %copy-start.11 = (bf16[192,2048]{1,0:T(8,128)(2,1)S(1)}, bf16[192,2048]{1,0:T(8,128)(2,1)}, u32[]{:S(2)}) copy-start(bf16[192,2048]{1,0:T(8,128)(2,1)} %copy-done.10) | copy-start | bytes 2359300
  115.2 21.8 %collective-permute-start.13 = (bf16[192,2048]{1,0:T(8,128)(2,1)S(1)}, bf16[192,2048]{1,0:T(8,128)(2,1)S(1)}, u32[]{:S(2)}, u32[]{:S(2)}) collective-permute-start(bf16[192,2048]{1,0:T(8,128)(2,1)S(1)} %encode.5.c_ref), channel_id=1, source_target_pairs={{0,1},{2,3},{4,5},{6,7},{8,9},{10,11},{12,13},{14,15},{16,17},{18,... | collective-permute-start | bytes 2359304 | tf_op jit(solution)/shard_map/ppermute | solution.py:297
  126.2 15.7 %collective-permute-start.9 = (bf16[1,192,1024]{2,1,0:T(8,128)(2,1)S(1)}, bf16[1,192,1024]{2,1,0:T(8,128)(2,1)S(1)}, u32[]{:S(2)}, u32[]{:S(2)}) collective-permute-start(bf16[1,192,1024]{2,1,0:T(8,128)(2,1)S(1)} %get-tuple-element.21), channel_id=1, source_target_pairs={{0,4},{4,0},{8,12},{12,8},{1,5},{5,1},{9,13},{13,9},{2,6},{6,2},{1... | collective-permute-start | bytes 1179656 | tf_op jit(solution)/shard_map/ppermute | solution.py:239
  133.0 79.4 %collective-permute-start.2 = (bf16[1,384,1024]{2,1,0:T(8,128)(2,1)S(1)}, bf16[1,384,1024]{2,1,0:T(8,128)(2,1)S(1)}, u32[]{:S(2)}, u32[]{:S(2)}) collective-permute-start(bf16[1,384,1024]{2,1,0:T(8,128)(2,1)S(1)} %get-tuple-element.15), channel_id=1, source_target_pairs={{0,4},{4,0},{8,12},{12,8},{1,5},{5,1},{9,13},{13,9},{2,6},{6,2},{1... | collective-permute-start | bytes 2359304 | tf_op jit(solution)/shard_map/ppermute | solution.py:239
  135.0 57.3 %collective-permute-start.3 = (bf16[1,384,1024]{2,1,0:T(8,128)(2,1)S(1)}, bf16[1,384,1024]{2,1,0:T(8,128)(2,1)S(1)}, u32[]{:S(2)}, u32[]{:S(2)}) collective-permute-start(bf16[1,384,1024]{2,1,0:T(8,128)(2,1)S(1)} %get-tuple-element.17), channel_id=1, source_target_pairs={{0,4},{4,0},{8,12},{12,8},{1,5},{5,1},{9,13},{13,9},{2,6},{6,2},{1... | collective-permute-start | bytes 2359304 | tf_op jit(solution)/shard_map/ppermute | solution.py:239
  135.1 6.8 %copy-start.15 = (f32[1,192,1024]{2,1,0:T(8,128)S(1)}, f32[1,192,1024]{2,1,0:T(8,128)}, u32[]{:S(2)}) copy-start(f32[1,192,1024]{2,1,0:T(8,128)} %copy-done.14) | copy-start | bytes 2359300
  135.1 59.4 %collective-permute-start.8 = (bf16[1,192,1024]{2,1,0:T(8,128)(2,1)S(1)}, bf16[1,192,1024]{2,1,0:T(8,128)(2,1)S(1)}, u32[]{:S(2)}, u32[]{:S(2)}) collective-permute-start(bf16[1,192,1024]{2,1,0:T(8,128)(2,1)S(1)} %get-tuple-element.19), channel_id=1, source_target_pairs={{0,4},{4,0},{8,12},{12,8},{1,5},{5,1},{9,13},{13,9},{2,6},{6,2},{1... | collective-permute-start | bytes 1179656 | tf_op jit(solution)/shard_map/ppermute | solution.py:239
  141.7 50.5 %collective-permute-start.15 = (bf16[1,192,1024]{2,1,0:T(8,128)(2,1)S(1)}, bf16[1,192,1024]{2,1,0:T(8,128)(2,1)S(1)}, u32[]{:S(2)}, u32[]{:S(2)}) collective-permute-start(bf16[1,192,1024]{2,1,0:T(8,128)(2,1)S(1)} %get-tuple-element.25), channel_id=1, source_target_pairs={{0,4},{4,0},{8,12},{12,8},{1,5},{5,1},{9,13},{13,9},{2,6},{6,2},{1... | collective-permute-start | bytes 1179656 | tf_op jit(solution)/shard_map/ppermute | solution.py:239
  142.0 53.8 %collective-permute-start.10 = (bf16[1,192,1024]{2,1,0:T(8,128)(2,1)S(1)}, bf16[1,192,1024]{2,1,0:T(8,128)(2,1)S(1)}, u32[]{:S(2)}, u32[]{:S(2)}) collective-permute-start(bf16[1,192,1024]{2,1,0:T(8,128)(2,1)S(1)} %add_convert_fusion.5), channel_id=1, source_target_pairs={{0,8},{4,12},{8,0},{12,4},{1,9},{5,13},{9,1},{13,5},{2,10},{6,14},... | collective-permute-start | bytes 1179656 | tf_op jit(solution)/shard_map/ppermute | solution.py:239
  149.9 44.3 %copy-start.13 = (f32[1,384,1024]{2,1,0:T(8,128)S(1)}, f32[1,384,1024]{2,1,0:T(8,128)}, u32[]{:S(2)}) copy-start(f32[1,384,1024]{2,1,0:T(8,128)} %copy-done.12) | copy-start | bytes 4718596
  192.2 14.0 %collective-permute-start.14 = (bf16[1,192,1024]{2,1,0:T(8,128)(2,1)S(1)}, bf16[1,192,1024]{2,1,0:T(8,128)(2,1)S(1)}, u32[]{:S(2)}, u32[]{:S(2)}) collective-permute-start(bf16[1,192,1024]{2,1,0:T(8,128)(2,1)S(1)} %get-tuple-element.23), channel_id=1, source_target_pairs={{0,4},{4,0},{8,12},{12,8},{1,5},{5,1},{9,13},{13,9},{2,6},{6,2},{1... | collective-permute-start | bytes 1179656 | tf_op jit(solution)/shard_map/ppermute | solution.py:239
  192.4 18.9 %collective-permute-start.16 = (bf16[1,192,1024]{2,1,0:T(8,128)(2,1)S(1)}, bf16[1,192,1024]{2,1,0:T(8,128)(2,1)S(1)}, u32[]{:S(2)}, u32[]{:S(2)}) collective-permute-start(bf16[1,192,1024]{2,1,0:T(8,128)(2,1)S(1)} %add_convert_fusion.3), channel_id=1, source_target_pairs={{0,8},{4,12},{8,0},{12,4},{1,9},{5,13},{9,1},{13,5},{2,10},{6,14},... | collective-permute-start | bytes 1179656 | tf_op jit(solution)/shard_map/ppermute | solution.py:239
  194.2 1.6 copy-start.9
  194.5 17.8 %copy-start.17 = (bf16[1,1024]{1,0:T(2,128)(2,1)S(1)}, bf16[1,1024]{1,0:T(2,128)(2,1)}, u32[]{:S(2)}) copy-start(bf16[1,1024]{1,0:T(2,128)(2,1)} %param.13) | copy-start | bytes 6148
  194.5 52.7 %collective-permute-start.4 = (bf16[1,384,1024]{2,1,0:T(8,128)(2,1)S(1)}, bf16[1,384,1024]{2,1,0:T(8,128)(2,1)S(1)}, u32[]{:S(2)}, u32[]{:S(2)}) collective-permute-start(bf16[1,384,1024]{2,1,0:T(8,128)(2,1)S(1)} %add_convert_fusion.1), channel_id=1, source_target_pairs={{0,8},{4,12},{8,0},{12,4},{1,9},{5,13},{9,1},{13,5},{2,10},{6,14},... | collective-permute-start | bytes 2359304 | tf_op jit(solution)/shard_map/ppermute | solution.py:239
  195.9 16.4 %collective-permute-start.11 = (bf16[192,1024]{1,0:T(8,128)(2,1)S(1)}, bf16[192,1024]{1,0:T(8,128)(2,1)S(1)}, u32[]{:S(2)}, u32[]{:S(2)}) collective-permute-start(bf16[192,1024]{1,0:T(8,128)(2,1)S(1)} %fusion.4), channel_id=1, source_target_pairs={{0,2},{2,0},{1,3},{3,1},{4,6},{6,4},{5,7},{7,5},{8,10},{10,8},{9,1... | collective-permute-start | bytes 1179656 | tf_op jit(solution)/shard_map/ppermute | solution.py:234
  211.3 35.9 %copy-start.16 = (bf16[1,384,1024]{2,1,0:T(8,128)(2,1)S(1)}, bf16[1,384,1024]{2,1,0:T(8,128)(2,1)}, u32[]{:S(2)}) copy-start(bf16[1,384,1024]{2,1,0:T(8,128)(2,1)} %param.8) | copy-start | bytes 2359300
  211.5 35.7 %collective-permute-start.17 = (bf16[192,1024]{1,0:T(8,128)(2,1)S(1)}, bf16[192,1024]{1,0:T(8,128)(2,1)S(1)}, u32[]{:S(2)}, u32[]{:S(2)}) collective-permute-start(bf16[192,1024]{1,0:T(8,128)(2,1)S(1)} %fusion.5), channel_id=1, source_target_pairs={{0,2},{2,0},{1,3},{3,1},{4,6},{6,4},{5,7},{7,5},{8,10},{10,8},{9,1... | collective-permute-start | bytes 1179656 | tf_op jit(solution)/shard_map/ppermute | solution.py:234
  250.3 4.4 %collective-permute-start.19 = (f32[1,2]{1,0:T(1,128)S(1)}, f32[1,2]{1,0:T(1,128)S(1)}, u32[]{:S(2)}, u32[]{:S(2)}) collective-permute-start(f32[1,2]{1,0:T(1,128)S(1)} %maximum_bitcast_fusion), channel_id=1, source_target_pairs={{0,8},{4,12},{8,0},{12,4},{1,9},{5,13},{9,1},{13,5},{2,10},{6,14},... | collective-permute-start | bytes 32 | tf_op jit(solution)/shard_map/ppermute | solution.py:234
  250.3 4.4 %collective-permute-start.20 = (f32[1,2]{1,0:T(1,128)S(1)}, f32[1,2]{1,0:T(1,128)S(1)}, u32[]{:S(2)}, u32[]{:S(2)}) collective-permute-start(f32[1,2]{1,0:T(1,128)S(1)} %maximum_bitcast_fusion), channel_id=1, source_target_pairs={{0,12},{4,0},{8,4},{12,8},{1,13},{5,1},{9,5},{13,9},{2,14},{6,2},{... | collective-permute-start | bytes 32 | tf_op jit(solution)/shard_map/ppermute | solution.py:234
  250.4 5.8 %collective-permute-start.18 = (f32[1,2]{1,0:T(1,128)S(1)}, f32[1,2]{1,0:T(1,128)S(1)}, u32[]{:S(2)}, u32[]{:S(2)}) collective-permute-start(f32[1,2]{1,0:T(1,128)S(1)} %maximum_bitcast_fusion), channel_id=1, source_target_pairs={{0,4},{4,8},{8,12},{12,0},{1,5},{5,9},{9,13},{13,1},{2,6},{6,10},{... | collective-permute-start | bytes 32 | tf_op jit(solution)/shard_map/ppermute | solution.py:234
  252.4 13.2 %copy-start.1 = (bf16[1,4096]{1,0:T(2,128)(2,1)S(1)}, bf16[1,4096]{1,0:T(2,128)(2,1)}, u32[]{:S(2)}) copy-start(bf16[1,4096]{1,0:T(2,128)(2,1)} %param.10) | copy-start | bytes 24580
  257.6 3.5 %collective-permute-start.21 = (f32[1,2]{1,0:T(1,128)S(1)}, f32[1,2]{1,0:T(1,128)S(1)}, u32[]{:S(2)}, u32[]{:S(2)}) collective-permute-start(f32[1,2]{1,0:T(1,128)S(1)} %add_add_fusion), channel_id=1, source_target_pairs={{0,2},{2,0},{1,3},{3,1},{4,6},{6,4},{5,7},{7,5},{8,10},{10,8},{9,1... | collective-permute-start | bytes 32 | tf_op jit(solution)/shard_map/ppermute | solution.py:234
  263.1 1.9 collective-permute-start.22

commit v3 on v0

v3 whole, which is shorter than its diff:
```python
import jax
import jax.numpy as jnp
from jax import lax
from jax.experimental import pallas as pl
from jax.experimental.pallas import tpu as pltpu
from jax.sharding import PartitionSpec as P

VMEM_LIMIT = 48 * 1024 * 1024
SLOTS = 3
TILE = 512
COST = pl.CostEstimate(flops=0, bytes_accessed=0, transcendentals=0)


def tile_of(size, most):
    tile = min(size, most)
    while size % tile:
        tile //= 2
    return tile


def prepare(x, side):
    rows, width = x.shape
    quarter = rows // 4
    lanes = tile_of(width, 1024)

    def body(side_ref, x_ref, outer_ref, inner_ref, o_ref, held, sem, out_sem):
        def load(i):
            place = pl.ds(i * quarter, quarter)
            return pltpu.make_async_copy(x_ref.at[place], held.at[place], sem.at[i])

        first = pl.ds(pl.multiple_of(side_ref[0] * (3 * quarter), 16), quarter)
        cuts = [
            pltpu.make_async_copy(x_ref.at[first], outer_ref, out_sem.at[0]),
            pltpu.make_async_copy(x_ref.at[pl.ds(quarter, 2 * quarter)], inner_ref, out_sem.at[1]),
        ]
        for i in range(4):
            load(i).start()
        for copy in cuts:
            copy.start()
        total = jnp.zeros((8, lanes), jnp.float32)
        for i in range(4):
            load(i).wait()
            for c in range(width // lanes):
                def add(r, acc):
                    here = pl.ds(pl.multiple_of(i * quarter + r * 16, 16), 16)
                    value = held[here, c * lanes:(c + 1) * lanes].astype(jnp.float32)
                    value = value * value
                    return acc + value[:8] + value[8:]

                total = lax.fori_loop(0, quarter // 16, add, total)
        o_ref[0] = jnp.sum(total)
        for copy in cuts:
            copy.wait()

    return pl.pallas_call(
        body,
        in_specs=[pl.BlockSpec(memory_space=pltpu.SMEM), pl.BlockSpec(memory_space=pl.ANY)],
        out_specs=[pl.BlockSpec(memory_space=pl.ANY)] * 2 + [pl.BlockSpec(memory_space=pltpu.SMEM)],
        out_shape=[
            jax.ShapeDtypeStruct((quarter, width), x.dtype),
            jax.ShapeDtypeStruct((2 * quarter, width), x.dtype),
            jax.ShapeDtypeStruct((1,), jnp.float32),
        ],
        scratch_shapes=[
            pltpu.VMEM((rows, width), x.dtype),
            pltpu.SemaphoreType.DMA((4,)),
            pltpu.SemaphoreType.DMA((2,)),
        ],
        compiler_params=pltpu.CompilerParams(vmem_limit_bytes=VMEM_LIMIT),
        cost_estimate=COST,
        name="prepare",
    )(side.reshape(1), x)


def ring_loop(count, start, step):
    for t in range(min(SLOTS, count)):
        start(t, t)

    def turn(t, carry):
        slot = lax.rem(t, SLOTS)
        step(t, slot)

        @pl.when(t + SLOTS < count)
        def _():
            start(t + SLOTS, slot)

        return carry

    lax.fori_loop(0, count, turn, 0)


def encode(pieces, places, inv, weight, bias, parts, after):
    rows, width = sum(piece[2] for piece in pieces), pieces[0][0].shape[1]
    latents = weight.shape[1]
    tile = tile_of(latents // parts, TILE)
    per = latents // parts // tile
    n = len(pieces)

    def body(places_ref, inv_ref, b_ref, *refs):
        x_refs, w_ref, o_refs = refs[:n], refs[n], refs[n + 2:n + 2 + parts]
        lhs, ring, lhs_sem, ring_sem = refs[n + 2 + parts:]

        def lhs_copy(i):
            _, first, count = pieces[i]
            place = pl.ds(pl.multiple_of(places_ref[i], 16), count)
            return pltpu.make_async_copy(
                x_refs[i].at[pl.ds(first, count)], lhs.at[place], lhs_sem.at[i])

        def columns(t):
            return pl.ds(pl.multiple_of(t * tile, tile), tile)

        def tile_copy(t, slot):
            return pltpu.make_async_copy(w_ref.at[:, columns(t)], ring.at[slot], ring_sem.at[slot])

        for i in range(n):
            lhs_copy(i).start()

        def step(t, slot):
            @pl.when(t == 0)
            def _():
                for i in range(n):
                    lhs_copy(i).wait()

            tile_copy(t, slot).wait()
            pre = jnp.dot(lhs[...], ring[slot], preferred_element_type=jnp.float32)
            pre = pre * inv_ref[0] + b_ref[:, columns(t)].astype(jnp.float32)
            value = jnp.maximum(pre, 0.0).astype(jnp.bfloat16)
            for p in range(parts):
                @pl.when(lax.div(t, per) == p)
                def _():
                    o_refs[p][:, columns(lax.rem(t, per))] = value

        ring_loop(latents // tile, lambda t, slot: tile_copy(t, slot).start(), step)

    return pl.pallas_call(
        body,
        in_specs=[
            pl.BlockSpec(memory_space=pltpu.SMEM),
            pl.BlockSpec(memory_space=pltpu.SMEM),
            pl.BlockSpec(memory_space=pltpu.VMEM),
        ] + [pl.BlockSpec(memory_space=pl.ANY)] * (n + 2),
        out_specs=[pl.BlockSpec(memory_space=pltpu.VMEM)] * parts,
        out_shape=[jax.ShapeDtypeStruct((rows, latents // parts), jnp.bfloat16)] * parts,
        scratch_shapes=[
            pltpu.VMEM((rows, width), jnp.bfloat16),
            pltpu.VMEM((SLOTS, width, tile), jnp.bfloat16),
            pltpu.SemaphoreType.DMA((n,)),
            pltpu.SemaphoreType.DMA((SLOTS,)),
        ],
        compiler_params=pltpu.CompilerParams(vmem_limit_bytes=VMEM_LIMIT),
        cost_estimate=COST,
        name="encode",
    )(places, inv.reshape(1), bias, *[piece[0] for piece in pieces], weight, after)


def decode(codes, earlier, own_w, cross_w, info, outs, width, after):
    parts = len(codes)
    rows, part = codes[0].shape
    latents = parts * part
    tile = tile_of(width, TILE)
    per = width // tile
    blocks = info.shape[0] - 1

    def body(info_ref, *refs):
        c_refs, e_refs, s_ref, x_ref = refs[:parts], refs[parts:2 * parts], refs[2 * parts], refs[2 * parts + 1]
        o_refs = refs[2 * parts + 3:2 * parts + 3 + len(outs)]
        lhs, ring, lhs_sem, ring_sem = refs[2 * parts + 3 + len(outs):]
        later = info_ref[0] != 0

        def lhs_copy(i):
            source = c_refs[i] if i < parts else e_refs[i - parts]
            return pltpu.make_async_copy(source, lhs.at[:, pl.ds(i * part, part)], lhs_sem.at[i])

        def tile_copy(source, i, t, slot):
            column = info_ref[1 + lax.div(t, per)] * width + lax.rem(t, per) * tile
            across = pl.ds(pl.multiple_of(column, tile), tile)
            return pltpu.make_async_copy(
                source.at[:, across], ring.at[slot, pl.ds(i * latents, latents)], ring_sem.at[slot, i])

        def start(t, slot):
            t = jnp.int32(t)
            tile_copy(s_ref, 0, t, slot).start()

            @pl.when(later)
            def _():
                tile_copy(x_ref, 1, t, slot).start()

        for i in range(parts):
            lhs_copy(i).start()

        @pl.when(later)
        def _():
            for i in range(parts, 2 * parts):
                lhs_copy(i).start()

        def put(t, value):
            b = lax.div(t, per)
            across = pl.ds(pl.multiple_of(lax.rem(t, per) * tile, tile), tile)
            for (block, count, row, height, dtype), o_ref in zip(outs, o_refs):
                @pl.when((b >= block) & (b < block + count))
                def _():
                    here = jnp.clip(b - block, 0, count - 1)
                    o_ref[here, :, across] = value[row:row + height].astype(dtype)

        def step(t, slot):
            @pl.when(t == 0)
            def _():
                for i in range(parts):
                    lhs_copy(i).wait()

            tile_copy(s_ref, 0, t, slot).wait()

            @pl.when(later)
            def _():
                @pl.when(t == 0)
                def _():
                    for i in range(parts, 2 * parts):
                        lhs_copy(i).wait()

                tile_copy(x_ref, 1, t, slot).wait()
                put(t, jnp.dot(lhs[...], ring[slot], preferred_element_type=jnp.float32))

            @pl.when(jnp.logical_not(later))
            def _():
                put(t, jnp.dot(
                    lhs[:, :latents], ring[slot, :latents], preferred_element_type=jnp.float32))

        ring_loop(blocks * per, start, step)

    return pl.pallas_call(
        body,
        in_specs=[pl.BlockSpec(memory_space=pltpu.SMEM)]
        + [pl.BlockSpec(memory_space=pl.ANY)] * (2 * parts + 3),
        out_specs=[pl.BlockSpec(memory_space=pltpu.VMEM)] * len(outs),
        out_shape=[
            jax.ShapeDtypeStruct((count, height, width), dtype)
            for _, count, _, height, dtype in outs
        ],
        scratch_shapes=[
            pltpu.VMEM((rows, 2 * latents), jnp.bfloat16),
            pltpu.VMEM((SLOTS, 2 * latents, tile), jnp.bfloat16),
            pltpu.SemaphoreType.DMA((2 * parts,)),
            pltpu.SemaphoreType.DMA((SLOTS, 2)),
        ],
        compiler_params=pltpu.CompilerParams(vmem_limit_bytes=VMEM_LIMIT),
        cost_estimate=COST,
        name="decode",
    )(info, *codes, *earlier, own_w, cross_w, after)


def shifted(value, axis, distance):
    n = lax.axis_size(axis)
    return lax.ppermute(value, axis, [(i, (i + distance) % n) for i in range(n)])


def swapped(value, axis, bit):
    n = lax.axis_size(axis)
    return lax.ppermute(value, axis, [(i, i ^ bit) for i in range(n)])


def sum_over(value, axis):
    total = value
    for distance in range(1, lax.axis_size(axis)):
        total = total + shifted(value, axis, distance)
    return total


def wide(value):
    return value.astype(jnp.float32)


def local(inputs, targets, enc_weight, encoder_layer_bias, dec_self, dec_cross, dec_bias):
    layer = lax.axis_index("layer")
    lat = lax.axis_index("latent")
    n_lat = lax.axis_size("latent")
    n_tok = lax.axis_size("token")
    x_own = inputs[0]
    rows, model = x_own.shape
    enc_w = enc_weight[0]
    own_w = dec_self[0]
    lat_dev = enc_w.shape[1]
    width = dec_bias.shape[1]
    quarter = rows // 4
    side = lat % 2

    outer, inner, square = prepare(x_own, side.astype(jnp.int32))
    square = sum_over(square, "token")
    scale = jnp.sqrt(square / (rows * n_tok * model) + 1e-06)
    inv = 1.0 / scale
    foreign = []
    for distance in range(1, n_tok):
        mine = shifted(outer, "token", distance)
        theirs = swapped(mine, "latent", 1)
        foreign.append((n_tok - distance, mine, theirs, shifted(inner, "token", distance)))

    bias = lax.dynamic_slice_in_dim(
        encoder_layer_bias, lax.axis_index("token") * lat_dev, lat_dev, axis=1
    )

    group = n_lat // 4
    other, mine_bit = 1 - lat % 2, lat % 2
    far, near = 1 - (lat // 2) % 2, (lat // 2) % 2
    info_sent = jnp.stack(
        [layer] + [4 * i + 2 * b + other for b in (far, near) for i in range(group)]
    ).astype(jnp.int32)
    info_kept = jnp.stack(
        [layer] + [4 * i + 2 * b + mine_bit for b in (far, near) for i in range(group)]
    ).astype(jnp.int32)

    half = 2 * quarter
    both = 2 * group
    narrow = jnp.bfloat16
    origin = jnp.int32(0)

    def codes_of(pieces, places, parts, after):
        codes = encode(
            pieces, jnp.stack(places).astype(jnp.int32), inv, enc_w, bias, parts, after)
        return codes, [lax.ppermute(part, "layer", [(0, 1)]) for part in codes]

    def products(codes, info, outs, after):
        return decode(*codes, own_w, dec_cross, info, outs, width, after)

    def finish(total):
        bit = 4
        while bit < n_lat:
            here = (lat // bit) % 2
            pairs = total.reshape(total.shape[0] // 2, 2, *total.shape[1:])
            away = lax.dynamic_index_in_dim(pairs, 1 - here, 1, keepdims=False)
            arrived = swapped(away.astype(narrow), "latent", bit)
            total = lax.dynamic_index_in_dim(pairs, here, 1, keepdims=False) + wide(arrived)
            bit *= 2
        return total[0]

    codes = codes_of([(x_own, quarter, half), (x_own, 0, quarter), (x_own, 3 * quarter, quarter)],
                     [origin, origin + half, origin + half + quarter], 2, x_own)
    sent_in, sent_out = products(
        codes, info_sent, [(0, both, 0, half, narrow), (0, both, half, half, jnp.float32)], codes[0][0])
    there_in = swapped(sent_in, "latent", 1)
    kept_in, kept_out = products(
        codes, info_kept, [(0, both, 0, half, jnp.float32), (0, both, half, half, jnp.float32)], sent_in)
    after = kept_in
    across_in = (kept_in[:group] + wide(there_in[:group])).astype(narrow)
    total_in = kept_in[group:] + wide(there_in[group:]) + wide(swapped(across_in, "latent", 2))

    sent_back, kept_back = [], []
    for back, mine, theirs, _ in foreign:
        codes = codes_of([(mine, 0, quarter), (theirs, 0, quarter)],
                         [side * quarter, (1 - side) * quarter], 1, after)
        sent, = products(codes, info_sent, [(0, both, 0, half, narrow)], across_in)
        sent_back.append(shifted(sent, "token", back))
        kept, = products(codes, info_kept, [(0, both, 0, half, narrow)], sent)
        kept_back.append(shifted(kept, "token", back))
        after = kept

    sent_out = (sent_out + sum(wide(part) for part in sent_back)).astype(narrow)
    there_out = swapped(sent_out, "latent", 1)
    returned = []
    for back, _, _, rows_in in foreign:
        codes = codes_of([(rows_in, 0, half)], [origin], 1, after)
        far_sent, near_sent = products(
            codes, info_sent, [(0, group, 0, half, narrow), (group, group, 0, half, narrow)], codes[0][0])
        far_in = swapped(far_sent, "latent", 1)
        near_in = swapped(near_sent, "latent", 1)
        after = far_sent if returned else sent_out
        kept, = products(codes, info_kept, [(0, both, 0, half, jnp.float32)], after)
        across = (kept[:group] + wide(far_in)).astype(narrow)
        part = finish(kept[group:] + wide(near_in) + wide(swapped(across, "latent", 2)))
        returned.append(shifted(part.astype(narrow), "token", back))
        after = kept

    kept_out = kept_out + sum(wide(part) for part in kept_back) + wide(there_out)
    across_out = swapped(kept_out[:group].astype(narrow), "latent", 2)
    total_out = finish(kept_out[group:] + wide(across_out))
    total_in = finish(total_in) + sum(wide(part) for part in returned)
    total = jnp.concatenate([total_out[:quarter], total_in, total_out[quarter:]])
    total = total + wide(dec_bias)
    recon = total.astype(jnp.bfloat16)[None]

    target = wide(targets[0])
    diff = total - target
    sums = jnp.stack([jnp.sum(diff * diff), jnp.sum(target * target)]).reshape(1, 2)
    sums = sum_over(sum_over(sums, "latent"), "token")
    ratio = sums[:, 0] / sums[:, 1]
    loss = sum_over(ratio, "layer") / 2.0
    return (recon, loss)


def solution(mesh):
    return jax.shard_map(
        local,
        mesh=mesh,
        in_specs=(
            P("layer", ("groups", "token"), None),
            P("layer", ("groups", "token"), "latent"),
            P("layer", None, ("latent", "token")),
            P("layer", "latent"),
            P("layer", ("latent", "token"), None),
            P(("latent", "token"), None),
            P("layer", "latent"),
        ),
        out_specs=(P("layer", ("groups", "token"), "latent"), P("groups")),
        check_vma=False,
    )
```

time: 417 us -> 210 us (0.50)
  waiting for transfers between devices: 264 us -> 83 us
  Pallas kernels: 0 us -> 66.8 us
  matrix products: 61.1 us -> 0 us
  starting transfers between devices: 2.2 us -> 42.6 us
  blocking collectives: 31.5 us -> 0 us
  local copies, waits for them, and re-layouts: 29 us -> 3.91 us
  between operations: 16.6 us -> 5.24 us
    reduce_scatter x1 -> x0, waiting for transfers between devices: 207 us -> none  [local(): lax.psum_scatter(result.reshape(rows * lax.axis_size(('latent', 'token'))...]
    ppermute x1 -> x23, waiting for transfers between devices: 0.01 us -> 83 us  [the longest x8 59.8 us: swapped(): return lax.ppermute(value, axis, [(i, i ^ bit) for i in range(n)])]
    pallas_call x0 -> x10, Pallas kernels: none -> 66.8 us  [the longest x6 36.9 us: decode(): pl.pallas_call(body, in_specs=[pl.BlockSpec(memory_space=pltpu.SMEM)] + [...]
    dot_general x3 -> x0, matrix products: 61.1 us -> none  [the longest x1 21.3 us: local(): jnp.einsum('tm,mkp->ktp', earlier, cross_cols, preferred_element_type=jnp...]
    all_gather x1 -> x0, waiting for transfers between devices: 56.4 us -> none  [local(): lax.all_gather(x_local, 'token', axis=0, tiled=True).astype(jnp.float32)]
    ppermute x1 -> x23, starting transfers between devices: 2.12 us -> 42.6 us  [the longest x4 20 us: codes_of(): return (codes, [lax.ppermute(part, 'layer', [(0, 1)]) for part in codes])]
    psum x1 -> x0, blocking collectives: 31.5 us -> none  [local(): err_vec = lax.psum(slots * err_local, ('latent', 'token', 'layer'))]
    another operation x1 -> x0, local copies, waits for them, and re-layouts: 28.3 us -> none  [local(): diagonal_cols = diagonal_full.reshape(lat_dev, blocks, col_width)]
  transfers between devices with their start and end apart: 3 -> 23, of which waited for: 2 -> 12; matrix products, arithmetic and copies ran while one was open for 12% -> 2% of each run, Pallas kernels for 0% -> 31%
where the time goes in v3:
time: 210 us
  waiting for transfers between devices  83 us (40%)
  Pallas kernels  66.8 us (32%)
  starting transfers between devices  42.6 us (20%)
  other arithmetic  8.3 us (4%)
  between operations  5.24 us (2%)
  local copies, waits for them, and re-layouts  3.91 us (2%)
    ppermute x8, waiting for transfers between devices, swapped(): return lax.ppermute(value, axis, [(i, i ^ bit) for i in range(n)])  59.8 us
    pallas_call x6, Pallas kernels, decode(): pl.pallas_call(body, in_specs=[pl.BlockSpec(memory_space=pltpu.SMEM)] + [...  36.9 us
    pallas_call x3, Pallas kernels, encode(): pl.pallas_call(body, in_specs=[pl.BlockSpec(memory_space=pltpu.SMEM), pl....  27.6 us
    ppermute x11, waiting for transfers between devices, shifted(): lax.ppermute(value, axis, [(i, (i + distance) % n) for i in range(n)])  21.9 us
    ppermute x4, starting transfers between devices, codes_of(): return (codes, [lax.ppermute(part, 'layer', [(0, 1)]) for part in codes])  20 us
    ppermute x11, starting transfers between devices, shifted(): lax.ppermute(value, axis, [(i, (i + distance) % n) for i in range(n)])  14.6 us
    ppermute x8, starting transfers between devices, swapped(): return lax.ppermute(value, axis, [(i, i ^ bit) for i in range(n)])  7.96 us
  transfers between devices with their start and end apart: 23, of which 12 were waited for; matrix products, arithmetic and copies ran while one was open for 2% of the time, Pallas kernels for 31%

profile of v3, /device:TPU:0, one launch (start us, length us, event | category | flops | bytes accessed | tf_op | source)
XLA Modules:
  0.0 209.9 jit_solution(7835612863316835663)
XLA Ops:
  0.7 1.9 copy-done.2
  2.6 2.2 %prepare.1 = (bf16[96,4096]{1,0:T(8,128)(2,1)}, bf16[192,4096]{1,0:T(8,128)(2,1)}, f32[1]{0:T(128)}) custom-call(s32[1]{0:T(128)} %bitcast.3.side_ref, bf16[384,4096]{1,0:T(8,128)(2,1)S(1)} %bitcast.32), custom_call_target="tpu_custom_call" | custom-call | tf_op jit(solution)/shard_map/prepare/pallas_call | solution.py:55
  4.8 3.0 %collective-permute-start.3 = (bf16[96,4096]{1,0:T(8,128)(2,1)}, bf16[96,4096]{1,0:T(8,128)(2,1)}, u32[]{:S(2)}, u32[]{:S(2)}) collective-permute-start(bf16[96,4096]{1,0:T(8,128)(2,1)} %get-tuple-element.18), channel_id=1, source_target_pairs={{0,2},{2,0},{1,3},{3,1},{4,6},{6,4},{5,7},{7,5},{8,10},{10,8},{9,1... | collective-permute-start | bytes 2359304 | tf_op jit(solution)/shard_map/ppermute | solution.py:253
  7.9 17.8 %collective-permute-done = f32[1]{0:T(128)} collective-permute-done((f32[1]{0:T(128)}, f32[1]{0:T(128)}, u32[]{:S(2)}, u32[]{:S(2)}) %collective-permute-start) | collective-permute-done | bytes 36 | tf_op jit(solution)/shard_map/ppermute | solution.py:253
  27.0 11.5 %encode.3 = (bf16[384,1024]{1,0:T(8,128)(2,1)}, bf16[384,1024]{1,0:T(8,128)(2,1)}) custom-call(s32[3]{0:T(128)S(1)} %copy-done.6, f32[1]{0:T(128)S(6)} %sqrt.3.inv_ref, bf16[1,2048]{1,0:T(2,128)(2,1)S(1)} %constant_dynamic-slice_fusion.b_ref, bf16[384,4096]{1,0:T(8,128)(2,1)S(1)} %bitcast.33, bf16[384,4096]{1,0:T(8,128)(2,1)S(1)} %bitcast.34, ...), custom_call_target="tpu_custom_call" | custom-call | tf_op jit(solution)/shard_map/encode/pallas_call | solution.py:135
  38.6 1.3 collective-permute-start.1
  39.9 1.3 collective-permute-start.2
  41.3 1.9 collective-permute-start.4
  43.2 1.5 collective-permute-start.12
  44.7 7.7 %decode.6 = (bf16[2,192,1024]{2,1,0:T(8,128)(2,1)}, f32[2,192,1024]{2,1,0:T(8,128)S(1)}) custom-call(s32[3]{0:T(128)S(1)} %pad_add_fusion.1.info_ref, bf16[384,1024]{1,0:T(8,128)(2,1)} %get-tuple-element.14.refs_0_.refs_6_, bf16[384,1024]{1,0:T(8,128)(2,1)} %get-tuple-element.15.refs_1_, bf16[384,1024]{1,0:T(8,128)(2,1)S(1)} %collective-permute-done.1.refs_2_, ...), custom_call_target="tpu_custom_call" | custom-call | tf_op jit(solution)/shard_map/decode/pallas_call | solution.py:230
  52.5 1.1 copy-done.4
  53.6 0.4 collective-permute-start.6
  54.2 8.1 %decode.7 = (f32[2,192,1024]{2,1,0:T(8,128)S(1)}, f32[2,192,1024]{2,1,0:T(8,128)}) custom-call(s32[3]{0:T(128)S(1)} %pad_add_fusion.info_ref, bf16[384,1024]{1,0:T(8,128)(2,1)} %get-tuple-element.14.refs_0_.refs_6_, bf16[384,1024]{1,0:T(8,128)(2,1)} %get-tuple-element.15.refs_1_, bf16[384,1024]{1,0:T(8,128)(2,1)S(1)} %collective-permute-done.1.refs_2_, ...), custom_call_target="tpu_custom_call" | custom-call | tf_op jit(solution)/shard_map/decode/pallas_call | solution.py:230
  62.3 8.7 %encode.4.refs_0_ = bf16[192,2048]{1,0:T(8,128)(2,1)S(1)} custom-call(s32[2]{0:T(128)S(1)} %pad_add_fusion.2.places_ref, f32[1]{0:T(128)S(6)} %sqrt.3.inv_ref, bf16[1,2048]{1,0:T(2,128)(2,1)S(1)} %constant_dynamic-slice_fusion.b_ref, bf16[96,4096]{1,0:T(8,128)(2,1)} %collective-permute-done.3.refs_0_, bf16[96,4096]{1,0:T(8,128)(2,1)} %collective-permute-done.4.refs_1_, ...), custom_call_target="tpu_custom_call" | custom-call | tf_op jit(solution)/shard_map/encode/pallas_call | solution.py:135
  71.0 9.9 %collective-permute-start.5 = (bf16[192,2048]{1,0:T(8,128)(2,1)S(1)}, bf16[192,2048]{1,0:T(8,128)(2,1)S(1)}, u32[]{:S(2)}, u32[]{:S(2)}) collective-permute-start(bf16[192,2048]{1,0:T(8,128)(2,1)S(1)} %encode.4.refs_0_), channel_id=1, source_target_pairs={{0,1},{2,3},{4,5},{6,7},{8,9},{10,11},{12,13},{14,15},{16,17},{18,... | collective-permute-start | bytes 2359304 | tf_op jit(solution)/shard_map/ppermute | solution.py:318
  80.9 1.1 add_convert_fusion.1.refs_4_
  82.0 0.7 collective-permute-done.5.refs_1_
  82.7 5.2 %decode.8.refs_4_ = bf16[2,192,1024]{2,1,0:T(8,128)(2,1)S(1)} custom-call(s32[3]{0:T(128)S(1)} %pad_add_fusion.1.info_ref, bf16[192,2048]{1,0:T(8,128)(2,1)S(1)} %encode.4.refs_0_, bf16[192,2048]{1,0:T(8,128)(2,1)S(1)} %collective-permute-done.5.refs_1_, bf16[2048,4096]{1,0:T(8,128)(2,1)} %bitcast.39, bf16[2048,4096]{1,0:T(8,128)(2,1)} %refs_3_.7, ...), custom_call_target="tpu_custom_call" | custom-call | tf_op jit(solution)/shard_map/decode/pallas_call | solution.py:230
  88.0 1.6 collective-permute-start.8
  89.5 5.2 %decode.9.refs_2_ = bf16[2,192,1024]{2,1,0:T(8,128)(2,1)S(1)} custom-call(s32[3]{0:T(128)S(1)} %pad_add_fusion.info_ref, bf16[192,2048]{1,0:T(8,128)(2,1)S(1)} %encode.4.refs_0_, bf16[192,2048]{1,0:T(8,128)(2,1)S(1)} %collective-permute-done.5.refs_1_, bf16[2048,4096]{1,0:T(8,128)(2,1)} %bitcast.40, bf16[2048,4096]{1,0:T(8,128)(2,1)} %refs_3_.7, ...), custom_call_target="tpu_custom_call" | custom-call | tf_op jit(solution)/shard_map/decode/pallas_call | solution.py:230
  94.8 7.4 %encode.5.refs_0_.refs_4_ = bf16[192,2048]{1,0:T(8,128)(2,1)S(1)} custom-call(s32[1]{0:T(128)} %constant.67.clone.1.places_ref, f32[1]{0:T(128)S(6)} %sqrt.3.inv_ref, bf16[1,2048]{1,0:T(2,128)(2,1)S(1)} %constant_dynamic-slice_fusion.b_ref, bf16[192,4096]{1,0:T(8,128)(2,1)S(1)} %collective-permute-done.12.refs_0_, bf16[4096,2048]{1,0:T(8,128)(2,1)} %bitcast.45, ...), custom_call_target="tpu_custom_call" | custom-call | tf_op jit(solution)/shard_map/encode/pallas_call | solution.py:135
  102.2 7.5 %collective-permute-start.13 = (bf16[192,2048]{1,0:T(8,128)(2,1)S(1)}, bf16[192,2048]{1,0:T(8,128)(2,1)S(1)}, u32[]{:S(2)}, u32[]{:S(2)}) collective-permute-start(bf16[192,2048]{1,0:T(8,128)(2,1)S(1)} %encode.5.refs_0_.refs_4_), channel_id=1, source_target_pairs={{0,1},{2,3},{4,5},{6,7},{8,9},{10,11},{12,13},{14,15},{16,17},{18,... | collective-permute-start | bytes 2359304 | tf_op jit(solution)/shard_map/ppermute | solution.py:318
  109.7 0.6 collective-permute-start.7
  110.9 0.6 collective-permute-done.13.refs_1_
  111.5 5.2 %decode.11 = (bf16[1,192,1024]{2,1,0:T(8,128)(2,1)S(1)}, bf16[1,192,1024]{2,1,0:T(8,128)(2,1)S(1)}) custom-call(s32[3]{0:T(128)S(1)} %pad_add_fusion.1.info_ref, bf16[192,2048]{1,0:T(8,128)(2,1)S(1)} %encode.5.refs_0_.refs_4_, bf16[192,2048]{1,0:T(8,128)(2,1)S(1)} %collective-permute-done.13.refs_1_, bf16[2048,4096]{1,0:T(8,128)(2,1)} %bitcast.41, ...), custom_call_target="tpu_custom_call" | custom-call | tf_op jit(solution)/shard_map/decode/pallas_call | solution.py:230
  116.8 1.2 collective-permute-start.15
  118.0 0.9 collective-permute-start.14
  118.9 5.4 %decode.10 = f32[2,192,1024]{2,1,0:T(8,128)S(1)} custom-call(s32[3]{0:T(128)S(1)} %pad_add_fusion.info_ref, bf16[192,2048]{1,0:T(8,128)(2,1)S(1)} %encode.5.refs_0_.refs_4_, bf16[192,2048]{1,0:T(8,128)(2,1)S(1)} %collective-permute-done.13.refs_1_, bf16[2048,4096]{1,0:T(8,128)(2,1)} %bitcast.42, bf16[2048,4096]{1,0:T(8,128)(2,1)} %refs_3_.7, ...), custom_call_target="tpu_custom_call" | custom-call | tf_op jit(solution)/shard_map/decode/pallas_call | solution.py:230
  124.3 22.0 %collective-permute-done.15 = bf16[1,192,1024]{2,1,0:T(8,128)(2,1)S(1)} collective-permute-done((bf16[1,192,1024]{2,1,0:T(8,128)(2,1)S(1)}, bf16[1,192,1024]{2,1,0:T(8,128)(2,1)S(1)}, u32[]{:S(2)}, u32[]{:S(2)}) %collective-permute-start.15) | collective-permute-done | bytes 393248 | tf_op jit(solution)/shard_map/ppermute | solution.py:258
  147.0 3.0 %collective-permute-start.10 = (bf16[1,192,1024]{2,1,0:T(8,128)(2,1)S(1)}, bf16[1,192,1024]{2,1,0:T(8,128)(2,1)S(1)}, u32[]{:S(2)}, u32[]{:S(2)}) collective-permute-start(bf16[1,192,1024]{2,1,0:T(8,128)(2,1)S(1)} %slice.83), channel_id=1, source_target_pairs={{0,8},{4,12},{8,0},{12,4},{1,9},{5,13},{9,1},{13,5},{2,10},{6,14},... | collective-permute-start | bytes 1179656 | tf_op jit(solution)/shard_map/ppermute | solution.py:258
  150.1 4.6 %collective-permute-done.14 = bf16[1,192,1024]{2,1,0:T(8,128)(2,1)S(1)} collective-permute-done((bf16[1,192,1024]{2,1,0:T(8,128)(2,1)S(1)}, bf16[1,192,1024]{2,1,0:T(8,128)(2,1)S(1)}, u32[]{:S(2)}, u32[]{:S(2)}) %collective-permute-start.14) | collective-permute-done | bytes 393248 | tf_op jit(solution)/shard_map/ppermute | solution.py:258
  154.7 26.8 %collective-permute-done.16 = bf16[1,192,1024]{2,1,0:T(8,128)(2,1)S(1)} collective-permute-done((bf16[1,192,1024]{2,1,0:T(8,128)(2,1)S(1)}, bf16[1,192,1024]{2,1,0:T(8,128)(2,1)S(1)}, u32[]{:S(2)}, u32[]{:S(2)}) %collective-permute-start.16) | collective-permute-done | bytes 393248 | tf_op jit(solution)/shard_map/ppermute | solution.py:258
  181.7 1.6 collective-permute-start.17
  183.3 2.5 %collective-permute-done.10 = bf16[1,192,1024]{2,1,0:T(8,128)(2,1)S(1)} collective-permute-done((bf16[1,192,1024]{2,1,0:T(8,128)(2,1)S(1)}, bf16[1,192,1024]{2,1,0:T(8,128)(2,1)S(1)}, u32[]{:S(2)}, u32[]{:S(2)}) %collective-permute-start.10) | collective-permute-done | bytes 393248 | tf_op jit(solution)/shard_map/ppermute | solution.py:258
  186.0 3.9 %collective-permute-done.11 = bf16[1,192,1024]{2,1,0:T(8,128)(2,1)S(1)} collective-permute-done((bf16[1,192,1024]{2,1,0:T(8,128)(2,1)S(1)}, bf16[1,192,1024]{2,1,0:T(8,128)(2,1)S(1)}, u32[]{:S(2)}, u32[]{:S(2)}) %collective-permute-start.11) | collective-permute-done | bytes 393248 | tf_op jit(solution)/shard_map/ppermute | solution.py:258
  190.0 1.2 bitcast_add_fusion
  191.2 1.1 fusion.1
  192.3 1.3 maximum_bitcast_fusion
  193.6 3.0 %collective-permute-start.19 = (f32[1,2]{1,0:T(1,128)S(1)}, f32[1,2]{1,0:T(1,128)S(1)}, u32[]{:S(2)}, u32[]{:S(2)}) collective-permute-start(f32[1,2]{1,0:T(1,128)S(1)} %maximum_bitcast_fusion), channel_id=1, source_target_pairs={{0,8},{4,12},{8,0},{12,4},{1,9},{5,13},{9,1},{13,5},{2,10},{6,14},... | collective-permute-start | bytes 32 | tf_op jit(solution)/shard_map/ppermute | solution.py:253
  196.7 0.8 collective-permute-start.20
  197.4 1.1 fusion.3
  198.5 0.5 collective-permute-done.18
  199.0 1.2 collective-permute-done.20
  200.2 1.3 add_add_fusion
  201.5 1.5 collective-permute-start.21
  203.0 2.0 collective-permute-done.21
  205.0 0.6 fusion.8
  206.9 1.0 collective-permute-start.22
  (48 shorter events, 2.5 us)
Async XLA Ops:
  0.6 7.2 %copy-start = (bf16[1,4096]{1,0:T(2,128)(2,1)S(1)}, bf16[1,4096]{1,0:T(2,128)(2,1)}, u32[]{:S(2)}) copy-start(bf16[1,4096]{1,0:T(2,128)(2,1)} %param.10) | copy-start | bytes 24580
  0.7 1.9 copy-start.2
  2.6 24.4 %copy-start.3 = (bf16[1,384,4096]{2,1,0:T(8,128)(2,1)S(1)}, bf16[1,384,4096]{2,1,0:T(8,128)(2,1)}, u32[]{:S(2)}) copy-start(bf16[1,384,4096]{2,1,0:T(8,128)(2,1)} %param.7) | copy-start | bytes 9437188
  2.6 24.5 %copy-start.6 = (s32[3]{0:T(128)S(1)}, s32[3]{0:T(128)}, u32[]{:S(2)}) copy-start(s32[3]{0:T(128)} %constant.61.clone.1.places_ref) | copy-start | bytes 40
  4.8 36.5 %collective-permute-start.3 = (bf16[96,4096]{1,0:T(8,128)(2,1)}, bf16[96,4096]{1,0:T(8,128)(2,1)}, u32[]{:S(2)}, u32[]{:S(2)}) collective-permute-start(bf16[96,4096]{1,0:T(8,128)(2,1)} %get-tuple-element.18), channel_id=1, source_target_pairs={{0,2},{2,0},{1,3},{3,1},{4,6},{6,4},{5,7},{7,5},{8,10},{10,8},{9,1... | collective-permute-start | bytes 2359304 | tf_op jit(solution)/shard_map/ppermute | solution.py:253
  7.8 17.9 %collective-permute-start = (f32[1]{0:T(128)}, f32[1]{0:T(128)}, u32[]{:S(2)}, u32[]{:S(2)}) collective-permute-start(f32[1]{0:T(128)} %get-tuple-element.13), channel_id=1, source_target_pairs={{0,2},{2,0},{1,3},{3,1},{4,6},{6,4},{5,7},{7,5},{8,10},{10,8},{9,1... | collective-permute-start | bytes 20 | tf_op jit(solution)/shard_map/ppermute | solution.py:253
  38.6 6.2 %collective-permute-start.1 = (bf16[384,1024]{1,0:T(8,128)(2,1)}, bf16[384,1024]{1,0:T(8,128)(2,1)S(1)}, u32[]{:S(2)}, u32[]{:S(2)}) collective-permute-start(bf16[384,1024]{1,0:T(8,128)(2,1)} %get-tuple-element.14.refs_0_.refs_6_), channel_id=1, source_target_pairs={{0,1},{2,3},{4,5},{6,7},{8,9},{10,11},{12,13},{14,15},{16,17},{18,... | collective-permute-start | bytes 2359304 | tf_op jit(solution)/shard_map/ppermute | solution.py:318
  39.9 4.8 %collective-permute-start.2 = (bf16[384,1024]{1,0:T(8,128)(2,1)}, bf16[384,1024]{1,0:T(8,128)(2,1)S(1)}, u32[]{:S(2)}, u32[]{:S(2)}) collective-permute-start(bf16[384,1024]{1,0:T(8,128)(2,1)} %get-tuple-element.15.refs_1_), channel_id=1, source_target_pairs={{0,1},{2,3},{4,5},{6,7},{8,9},{10,11},{12,13},{14,15},{16,17},{18,... | collective-permute-start | bytes 2359304 | tf_op jit(solution)/shard_map/ppermute | solution.py:318
  41.3 21.0 %collective-permute-start.4 = (bf16[96,4096]{1,0:T(8,128)(2,1)}, bf16[96,4096]{1,0:T(8,128)(2,1)}, u32[]{:S(2)}, u32[]{:S(2)}) collective-permute-start(bf16[96,4096]{1,0:T(8,128)(2,1)} %collective-permute-done.3.refs_0_), channel_id=1, source_target_pairs={{0,4},{4,0},{8,12},{12,8},{1,5},{5,1},{9,13},{13,9},{2,6},{6,2},{1... | collective-permute-start | bytes 2359304 | tf_op jit(solution)/shard_map/ppermute | solution.py:258
  43.2 51.6 %collective-permute-start.12 = (bf16[192,4096]{1,0:T(8,128)(2,1)}, bf16[192,4096]{1,0:T(8,128)(2,1)S(1)}, u32[]{:S(2)}, u32[]{:S(2)}) collective-permute-start(bf16[192,4096]{1,0:T(8,128)(2,1)} %get-tuple-element.21), channel_id=1, source_target_pairs={{0,2},{2,0},{1,3},{3,1},{4,6},{6,4},{5,7},{7,5},{8,10},{10,8},{9,1... | collective-permute-start | bytes 4718600 | tf_op jit(solution)/shard_map/ppermute | solution.py:253
  52.5 1.1 copy-start.4
  53.6 27.3 %collective-permute-start.6 = (bf16[2,192,1024]{2,1,0:T(8,128)(2,1)}, bf16[2,192,1024]{2,1,0:T(8,128)(2,1)}, u32[]{:S(2)}, u32[]{:S(2)}) collective-permute-start(bf16[2,192,1024]{2,1,0:T(8,128)(2,1)} %get-tuple-element.16.refs_6_), channel_id=1, source_target_pairs={{0,4},{4,0},{8,12},{12,8},{1,5},{5,1},{9,13},{13,9},{2,6},{6,2},{1... | collective-permute-start | bytes 2359304 | tf_op jit(solution)/shard_map/ppermute | solution.py:258
  71.0 11.7 %collective-permute-start.5 = (bf16[192,2048]{1,0:T(8,128)(2,1)S(1)}, bf16[192,2048]{1,0:T(8,128)(2,1)S(1)}, u32[]{:S(2)}, u32[]{:S(2)}) collective-permute-start(bf16[192,2048]{1,0:T(8,128)(2,1)S(1)} %encode.4.refs_0_), channel_id=1, source_target_pairs={{0,1},{2,3},{4,5},{6,7},{8,9},{10,11},{12,13},{14,15},{16,17},{18,... | collective-permute-start | bytes 2359304 | tf_op jit(solution)/shard_map/ppermute | solution.py:318
  88.0 22.3 %collective-permute-start.8 = (bf16[2,192,1024]{2,1,0:T(8,128)(2,1)S(1)}, bf16[2,192,1024]{2,1,0:T(8,128)(2,1)S(1)}, u32[]{:S(2)}, u32[]{:S(2)}) collective-permute-start(bf16[2,192,1024]{2,1,0:T(8,128)(2,1)S(1)} %decode.8.refs_4_), channel_id=1, source_target_pairs={{0,2},{2,0},{1,3},{3,1},{4,6},{6,4},{5,7},{7,5},{8,10},{10,8},{9,1... | collective-permute-start | bytes 2359304 | tf_op jit(solution)/shard_map/ppermute | solution.py:253
  94.8 15.5 %copy-start.5 = (f32[2,192,1024]{2,1,0:T(8,128)S(1)}, f32[2,192,1024]{2,1,0:T(8,128)}, u32[]{:S(2)}) copy-start(f32[2,192,1024]{2,1,0:T(8,128)} %copy-done.4) | copy-start | bytes 4718596
  102.2 9.3 %collective-permute-start.13 = (bf16[192,2048]{1,0:T(8,128)(2,1)S(1)}, bf16[192,2048]{1,0:T(8,128)(2,1)S(1)}, u32[]{:S(2)}, u32[]{:S(2)}) collective-permute-start(bf16[192,2048]{1,0:T(8,128)(2,1)S(1)} %encode.5.refs_0_.refs_4_), channel_id=1, source_target_pairs={{0,1},{2,3},{4,5},{6,7},{8,9},{10,11},{12,13},{14,15},{16,17},{18,... | collective-permute-start | bytes 2359304 | tf_op jit(solution)/shard_map/ppermute | solution.py:318
  109.7 36.8 %collective-permute-start.7 = (bf16[2,192,1024]{2,1,0:T(8,128)(2,1)S(1)}, bf16[2,192,1024]{2,1,0:T(8,128)(2,1)S(1)}, u32[]{:S(2)}, u32[]{:S(2)}) collective-permute-start(bf16[2,192,1024]{2,1,0:T(8,128)(2,1)S(1)} %decode.9.refs_2_), channel_id=1, source_target_pairs={{0,2},{2,0},{1,3},{3,1},{4,6},{6,4},{5,7},{7,5},{8,10},{10,8},{9,1... | collective-permute-start | bytes 2359304 | tf_op jit(solution)/shard_map/ppermute | solution.py:253
  110.6 35.9 %collective-permute-start.9 = (bf16[2,192,1024]{2,1,0:T(8,128)(2,1)S(1)}, bf16[2,192,1024]{2,1,0:T(8,128)(2,1)S(1)}, u32[]{:S(2)}, u32[]{:S(2)}) collective-permute-start(bf16[2,192,1024]{2,1,0:T(8,128)(2,1)S(1)} %add_convert_fusion.refs_4_), channel_id=1, source_target_pairs={{0,4},{4,0},{8,12},{12,8},{1,5},{5,1},{9,13},{13,9},{2,6},{6,2},{1... | collective-permute-start | bytes 2359304 | tf_op jit(solution)/shard_map/ppermute | solution.py:258
  116.8 29.6 %collective-permute-start.15 = (bf16[1,192,1024]{2,1,0:T(8,128)(2,1)S(1)}, bf16[1,192,1024]{2,1,0:T(8,128)(2,1)S(1)}, u32[]{:S(2)}, u32[]{:S(2)}) collective-permute-start(bf16[1,192,1024]{2,1,0:T(8,128)(2,1)S(1)} %get-tuple-element.23), channel_id=1, source_target_pairs={{0,4},{4,0},{8,12},{12,8},{1,5},{5,1},{9,13},{13,9},{2,6},{6,2},{1... | collective-permute-start | bytes 1179656 | tf_op jit(solution)/shard_map/ppermute | solution.py:258
  118.0 36.7 %collective-permute-start.14 = (bf16[1,192,1024]{2,1,0:T(8,128)(2,1)S(1)}, bf16[1,192,1024]{2,1,0:T(8,128)(2,1)S(1)}, u32[]{:S(2)}, u32[]{:S(2)}) collective-permute-start(bf16[1,192,1024]{2,1,0:T(8,128)(2,1)S(1)} %get-tuple-element.22), channel_id=1, source_target_pairs={{0,4},{4,0},{8,12},{12,8},{1,5},{5,1},{9,13},{13,9},{2,6},{6,2},{1... | collective-permute-start | bytes 1179656 | tf_op jit(solution)/shard_map/ppermute | solution.py:258
  124.3 22.2 %copy-start.7 = (f32[2,192,1024]{2,1,0:T(8,128)S(1)}, f32[2,192,1024]{2,1,0:T(8,128)}, u32[]{:S(2)}) copy-start(f32[2,192,1024]{2,1,0:T(8,128)} %get-tuple-element.17) | copy-start | bytes 4718596
  146.4 35.1 %collective-permute-start.16 = (bf16[1,192,1024]{2,1,0:T(8,128)(2,1)S(1)}, bf16[1,192,1024]{2,1,0:T(8,128)(2,1)S(1)}, u32[]{:S(2)}, u32[]{:S(2)}) collective-permute-start(bf16[1,192,1024]{2,1,0:T(8,128)(2,1)S(1)} %fusion.4), channel_id=1, source_target_pairs={{0,8},{4,12},{8,0},{12,4},{1,9},{5,13},{9,1},{13,5},{2,10},{6,14},... | collective-permute-start | bytes 1179656 | tf_op jit(solution)/shard_map/ppermute | solution.py:258
  146.5 3.4 %copy-start.9 = (bf16[1,1024]{1,0:T(2,128)(2,1)S(1)}, bf16[1,1024]{1,0:T(2,128)(2,1)}, u32[]{:S(2)}) copy-start(bf16[1,1024]{1,0:T(2,128)(2,1)} %param.13) | copy-start | bytes 6148
  147.0 38.8 %collective-permute-start.10 = (bf16[1,192,1024]{2,1,0:T(8,128)(2,1)S(1)}, bf16[1,192,1024]{2,1,0:T(8,128)(2,1)S(1)}, u32[]{:S(2)}, u32[]{:S(2)}) collective-permute-start(bf16[1,192,1024]{2,1,0:T(8,128)(2,1)S(1)} %slice.83), channel_id=1, source_target_pairs={{0,8},{4,12},{8,0},{12,4},{1,9},{5,13},{9,1},{13,5},{2,10},{6,14},... | collective-permute-start | bytes 1179656 | tf_op jit(solution)/shard_map/ppermute | solution.py:258
  149.9 40.0 %collective-permute-start.11 = (bf16[1,192,1024]{2,1,0:T(8,128)(2,1)S(1)}, bf16[1,192,1024]{2,1,0:T(8,128)(2,1)S(1)}, u32[]{:S(2)}, u32[]{:S(2)}) collective-permute-start(bf16[1,192,1024]{2,1,0:T(8,128)(2,1)S(1)} %add_convert_fusion.1.refs_4_), channel_id=1, source_target_pairs={{0,8},{4,12},{8,0},{12,4},{1,9},{5,13},{9,1},{13,5},{2,10},{6,14},... | collective-permute-start | bytes 1179656 | tf_op jit(solution)/shard_map/ppermute | solution.py:258
  181.7 8.3 %collective-permute-start.17 = (bf16[192,1024]{1,0:T(8,128)(2,1)S(1)}, bf16[192,1024]{1,0:T(8,128)(2,1)S(1)}, u32[]{:S(2)}, u32[]{:S(2)}) collective-permute-start(bf16[192,1024]{1,0:T(8,128)(2,1)S(1)} %fusion.7), channel_id=1, source_target_pairs={{0,2},{2,0},{1,3},{3,1},{4,6},{6,4},{5,7},{7,5},{8,10},{10,8},{9,1... | collective-permute-start | bytes 1179656 | tf_op jit(solution)/shard_map/ppermute | solution.py:253
  186.0 5.2 %copy-start.8 = (bf16[1,384,1024]{2,1,0:T(8,128)(2,1)S(1)}, bf16[1,384,1024]{2,1,0:T(8,128)(2,1)}, u32[]{:S(2)}) copy-start(bf16[1,384,1024]{2,1,0:T(8,128)(2,1)} %param.8) | copy-start | bytes 2359300
  191.2 17.6 %copy-start.1 = (bf16[1,4096]{1,0:T(2,128)(2,1)S(1)}, bf16[1,4096]{1,0:T(2,128)(2,1)}, u32[]{:S(2)}) copy-start(bf16[1,4096]{1,0:T(2,128)(2,1)} %param.10) | copy-start | bytes 24580
  193.6 5.3 %collective-permute-start.18 = (f32[1,2]{1,0:T(1,128)S(1)}, f32[1,2]{1,0:T(1,128)S(1)}, u32[]{:S(2)}, u32[]{:S(2)}) collective-permute-start(f32[1,2]{1,0:T(1,128)S(1)} %maximum_bitcast_fusion), channel_id=1, source_target_pairs={{0,4},{4,8},{8,12},{12,0},{1,5},{5,9},{9,13},{13,1},{2,6},{6,10},{... | collective-permute-start | bytes 32 | tf_op jit(solution)/shard_map/ppermute | solution.py:253
  193.6 5.3 %collective-permute-start.19 = (f32[1,2]{1,0:T(1,128)S(1)}, f32[1,2]{1,0:T(1,128)S(1)}, u32[]{:S(2)}, u32[]{:S(2)}) collective-permute-start(f32[1,2]{1,0:T(1,128)S(1)} %maximum_bitcast_fusion), channel_id=1, source_target_pairs={{0,8},{4,12},{8,0},{12,4},{1,9},{5,13},{9,1},{13,5},{2,10},{6,14},... | collective-permute-start | bytes 32 | tf_op jit(solution)/shard_map/ppermute | solution.py:253
  196.7 3.5 %collective-permute-start.20 = (f32[1,2]{1,0:T(1,128)S(1)}, f32[1,2]{1,0:T(1,128)S(1)}, u32[]{:S(2)}, u32[]{:S(2)}) collective-permute-start(f32[1,2]{1,0:T(1,128)S(1)} %maximum_bitcast_fusion), channel_id=1, source_target_pairs={{0,12},{4,0},{8,4},{12,8},{1,13},{5,1},{9,5},{13,9},{2,14},{6,2},{... | collective-permute-start | bytes 32 | tf_op jit(solution)/shard_map/ppermute | solution.py:253
  201.5 3.5 %collective-permute-start.21 = (f32[1,2]{1,0:T(1,128)S(1)}, f32[1,2]{1,0:T(1,128)S(1)}, u32[]{:S(2)}, u32[]{:S(2)}) collective-permute-start(f32[1,2]{1,0:T(1,128)S(1)} %add_add_fusion), channel_id=1, source_target_pairs={{0,2},{2,0},{1,3},{3,1},{4,6},{6,4},{5,7},{7,5},{8,10},{10,8},{9,1... | collective-permute-start | bytes 32 | tf_op jit(solution)/shard_map/ppermute | solution.py:253
  206.9 1.3 collective-permute-start.22

commit v4 on v0

v4 whole, which is shorter than its diff:
```python
import jax
import jax.numpy as jnp
from jax import lax
from jax.experimental import pallas as pl
from jax.experimental.pallas import tpu as pltpu
from jax.sharding import PartitionSpec as P

VMEM_LIMIT = 24 * 1024 * 1024
SLOTS = 3
TILE = 512
COST = pl.CostEstimate(flops=0, bytes_accessed=0, transcendentals=0)


def tile_of(size, most):
    tile = min(size, most)
    while size % tile:
        tile //= 2
    return tile


def square_sum(x):
    rows, width = x.shape
    lanes = tile_of(width, 1024)

    def body(x_ref, o_ref):
        total = jnp.zeros((8, lanes), jnp.float32)
        for c in range(width // lanes):
            def add(r, acc):
                here = pl.ds(pl.multiple_of(r * 16, 16), 16)
                value = x_ref[here, c * lanes:(c + 1) * lanes].astype(jnp.float32)
                value = value * value
                return acc + value[:8] + value[8:]

            total = lax.fori_loop(0, rows // 16, add, total)
        o_ref[0] = jnp.sum(total)

    return pl.pallas_call(
        body,
        in_specs=[pl.BlockSpec(memory_space=pltpu.VMEM)],
        out_specs=pl.BlockSpec(memory_space=pltpu.SMEM),
        out_shape=jax.ShapeDtypeStruct((1,), jnp.float32),
        compiler_params=pltpu.CompilerParams(vmem_limit_bytes=VMEM_LIMIT),
        cost_estimate=COST,
        name="square_sum",
    )(x)


def cut(x, side, after):
    rows, width = x.shape
    quarter = rows // 4

    def body(side_ref, after_ref, x_ref, outer_ref, inner_ref, sem):
        first = pl.ds(pl.multiple_of(side_ref[0] * (3 * quarter), 16), quarter)
        copies = [
            pltpu.make_async_copy(x_ref.at[first], outer_ref, sem.at[0]),
            pltpu.make_async_copy(x_ref.at[pl.ds(quarter, 2 * quarter)], inner_ref, sem.at[1]),
        ]
        for copy in copies:
            copy.start()
        for copy in copies:
            copy.wait()

    return pl.pallas_call(
        body,
        in_specs=[
            pl.BlockSpec(memory_space=pltpu.SMEM),
            pl.BlockSpec(memory_space=pltpu.SMEM),
            pl.BlockSpec(memory_space=pl.ANY),
        ],
        out_specs=[pl.BlockSpec(memory_space=pl.ANY)] * 2,
        out_shape=[
            jax.ShapeDtypeStruct((quarter, width), x.dtype),
            jax.ShapeDtypeStruct((2 * quarter, width), x.dtype),
        ],
        scratch_shapes=[pltpu.SemaphoreType.DMA((2,))],
        compiler_params=pltpu.CompilerParams(vmem_limit_bytes=VMEM_LIMIT),
        cost_estimate=COST,
        name="cut",
    )(side.reshape(1), after, x)


def columns(t, tile):
    return pl.ds(pl.multiple_of(t * tile, tile), tile)


def put_codes(o_ref, t, at, tile, value, inv_ref, b_ref):
    value = value * inv_ref[0] + b_ref[:, t * tile:(t + 1) * tile].astype(jnp.float32)
    o_ref[:, at * tile:(at + 1) * tile] = jnp.maximum(value, 0.0).astype(jnp.bfloat16)


def encode_first(x, inv, weight, bias, parts):
    rows, width = x.shape
    latents = weight.shape[1]
    tile = tile_of(latents // parts, TILE)
    count = latents // tile
    per = count // parts

    def body(inv_ref, b_ref, x_ref, w_ref, *refs):
        o_refs, held, sem = refs[:parts], refs[parts:parts + count], refs[parts + count]

        def copy(t):
            return pltpu.make_async_copy(w_ref.at[:, t * tile:(t + 1) * tile], held[t], sem.at[t])

        for t in range(count):
            copy(t).start()
        for t in range(count):
            copy(t).wait()
            value = jnp.dot(x_ref[...], held[t][...], preferred_element_type=jnp.float32)
            put_codes(o_refs[t // per], t, t % per, tile, value, inv_ref, b_ref)

    outs = pl.pallas_call(
        body,
        in_specs=[pl.BlockSpec(memory_space=pltpu.SMEM)]
        + [pl.BlockSpec(memory_space=pltpu.VMEM)] * 2 + [pl.BlockSpec(memory_space=pl.ANY)],
        out_specs=[pl.BlockSpec(memory_space=pltpu.VMEM)] * (parts + count),
        out_shape=[jax.ShapeDtypeStruct((rows, latents // parts), jnp.bfloat16)] * parts
        + [pltpu.VMEM((width, tile), weight.dtype)] * count,
        scratch_shapes=[pltpu.SemaphoreType.DMA((count,))],
        compiler_params=pltpu.CompilerParams(vmem_limit_bytes=VMEM_LIMIT),
        cost_estimate=COST,
        name="encode_first",
    )(inv.reshape(1), bias, x, weight)
    return outs[:parts], outs[parts:]


def call_with_held(body, held, specs, operands, out_specs, out_shape, scratch, also, name):
    n, m, k = len(held), len(specs), len(also)
    vmem = pl.BlockSpec(memory_space=pltpu.VMEM)

    def inner(*refs):
        body(refs[:n], *refs[n:n + m], *refs[n + m + k:n + m + k + len(out_specs)],
             *refs[n + m + k + len(out_specs) + n:])

    outs = pl.pallas_call(
        inner,
        in_specs=[vmem] * n + list(specs) + [pl.BlockSpec(memory_space=pl.ANY)] * k,
        out_specs=list(out_specs) + [vmem] * n,
        out_shape=list(out_shape) + [pltpu.VMEM(h.shape, h.dtype) for h in held],
        input_output_aliases={i: len(out_specs) + i for i in range(n)},
        scratch_shapes=scratch,
        compiler_params=pltpu.CompilerParams(vmem_limit_bytes=VMEM_LIMIT),
        cost_estimate=COST,
        name=name,
    )(*[pltpu.with_memory_space_constraint(h, pltpu.VMEM) for h in held], *operands, *also)
    return outs[:len(out_specs)], outs[len(out_specs):]


def encode(pieces, places, inv, held, count, bias, also):
    sizes = [piece.shape[0] for piece in pieces]
    rows = sum(sizes)
    width, tile = held[0].shape
    n = len(pieces)

    def body(held_refs, places_ref, inv_ref, b_ref, *refs):
        x_refs, (o_ref, lhs, sem) = refs[:n], refs[n:]
        copies = []
        for i in range(n):
            place = pl.ds(pl.multiple_of(places_ref[i], 16), sizes[i])
            copies.append(pltpu.make_async_copy(x_refs[i], lhs.at[place], sem.at[i]))
        for copy in copies:
            copy.start()
        for copy in copies:
            copy.wait()

        for t in range(count):
            value = jnp.dot(lhs[...], held_refs[t][...], preferred_element_type=jnp.float32)
            put_codes(o_ref, t, t, tile, value, inv_ref, b_ref)

    outs, held = call_with_held(
        body, held,
        [pl.BlockSpec(memory_space=pltpu.SMEM)] * 2 + [pl.BlockSpec(memory_space=pltpu.VMEM)]
        + [pl.BlockSpec(memory_space=pl.ANY)] * n,
        [places, inv.reshape(1), bias, *pieces],
        [pl.BlockSpec(memory_space=pltpu.VMEM)],
        [jax.ShapeDtypeStruct((rows, count * tile), jnp.bfloat16)],
        [pltpu.VMEM((rows, width), jnp.bfloat16), pltpu.SemaphoreType.DMA((n,))],
        also, "encode")
    return outs[0], held


def decode(codes, earlier, weights, info, outs, width, held, also, mode):
    parts = len(codes)
    rows, part = codes[0].shape
    latents = parts * part
    tile = tile_of(width, TILE)
    per = width // tile
    blocks = info.shape[0] - 1
    count = blocks * per
    slots = SLOTS if mode == "ring" else count

    def body(held_refs, info_ref, *refs):
        refs = list(refs)
        c_refs = [refs.pop(0) for _ in range(parts)]
        e_refs = [refs.pop(0) for _ in range(parts)]
        if mode != "held":
            s_ref, x_ref = refs.pop(0), refs.pop(0)
        o_refs = [refs.pop(0) for _ in outs]
        if mode == "held":
            s_tiles, x_tiles = held_refs[-2:]
        else:
            s_tiles, x_tiles, sem = refs
        later = info_ref[0] != 0

        def copy(source, target, i, t, slot):
            column = info_ref[1 + t // per] * width + lax.rem(t, per) * tile
            across = pl.ds(pl.multiple_of(column, tile), tile)
            return pltpu.make_async_copy(source.at[:, across], target.at[slot], sem.at[i, slot])

        def start(t, slot):
            t = jnp.int32(t)
            copy(s_ref, s_tiles, 0, t, slot).start()

            @pl.when(later)
            def _():
                copy(x_ref, x_tiles, 1, t, slot).start()

        def put(t, value):
            b = t // per
            for (block, many, spans, dtype), o_ref in zip(outs, o_refs):
                @pl.when((b >= block) & (b < block + many))
                def _():
                    here = jnp.clip(b - block, 0, many - 1)
                    at = 0
                    for row, height in spans:
                        o_ref[here, at:at + height, columns(lax.rem(t, per), tile)] = (
                            value[row:row + height].astype(dtype))
                        at += height

        def product(refs, tiles, slot):
            total = None
            for i, ref in enumerate(refs):
                one = jnp.dot(
                    ref[...], tiles[slot, i * part:(i + 1) * part], preferred_element_type=jnp.float32)
                total = one if total is None else total + one
            return total

        def step(t, slot):
            if mode != "held":
                copy(s_ref, s_tiles, 0, t, slot).wait()

            @pl.when(later)
            def _():
                if mode != "held":
                    copy(x_ref, x_tiles, 1, t, slot).wait()
                put(t, product(c_refs, s_tiles, slot) + product(e_refs, x_tiles, slot))

            @pl.when(jnp.logical_not(later))
            def _():
                put(t, product(c_refs, s_tiles, slot))

        if mode != "held":
            for t in range(min(slots, count)):
                start(t, t)

        def turn(t, carry):
            slot = lax.rem(t, slots)
            step(t, slot)
            if mode == "ring":
                @pl.when(t + slots < count)
                def _():
                    start(t + slots, slot)
            return carry

        lax.fori_loop(0, count, turn, 0)

    vmem = pl.BlockSpec(memory_space=pltpu.VMEM)
    out_specs = [vmem] * len(outs)
    out_shape = [
        jax.ShapeDtypeStruct((many, sum(height for _, height in spans), width), dtype)
        for _, many, spans, dtype in outs
    ]
    tiles = (slots, latents, tile)
    scratch = []
    if mode == "ring":
        scratch += [pltpu.VMEM(tiles, jnp.bfloat16)] * 2
    if mode == "keep":
        out_specs += [vmem] * 2
        out_shape += [pltpu.VMEM(tiles, jnp.bfloat16)] * 2
    if mode != "held":
        scratch += [pltpu.SemaphoreType.DMA((2, slots))]
    streamed = [] if mode == "held" else list(weights)
    results, held = call_with_held(
        body, held,
        [pl.BlockSpec(memory_space=pltpu.SMEM)] + [vmem] * (2 * parts)
        + [pl.BlockSpec(memory_space=pl.ANY)] * len(streamed),
        [info, *codes, *earlier, *streamed],
        out_specs, out_shape, scratch, also, "decode_" + mode)
    if mode == "keep":
        results, held = results[:-2], list(held) + list(results[-2:])
    return results, held


def shifted(value, axis, distance):
    n = lax.axis_size(axis)
    return lax.ppermute(value, axis, [(i, (i + distance) % n) for i in range(n)])


def swapped(value, axis, bit):
    n = lax.axis_size(axis)
    return lax.ppermute(value, axis, [(i, i ^ bit) for i in range(n)])


def sum_over(value, axis):
    total = value
    for distance in range(1, lax.axis_size(axis)):
        total = total + shifted(value, axis, distance)
    return total


def wide(value):
    return value.astype(jnp.float32)


def local(inputs, targets, enc_weight, encoder_layer_bias, dec_self, dec_cross, dec_bias):
    layer = lax.axis_index("layer")
    lat = lax.axis_index("latent")
    n_lat = lax.axis_size("latent")
    n_tok = lax.axis_size("token")
    x_own = inputs[0]
    rows, model = x_own.shape
    enc_w = pltpu.with_memory_space_constraint(enc_weight[0], pltpu.HBM)
    own_w = pltpu.with_memory_space_constraint(dec_self[0], pltpu.HBM)
    cross_w = pltpu.with_memory_space_constraint(dec_cross, pltpu.HBM)
    lat_dev = enc_w.shape[1]
    width = dec_bias.shape[1]
    quarter = rows // 4
    side = lat % 2

    square = sum_over(square_sum(x_own), "token")
    scale = jnp.sqrt(square / (rows * n_tok * model) + 1e-06)
    inv = 1.0 / scale
    outer, inner = cut(x_own, side.astype(jnp.int32), inv)
    foreign = []
    for distance in range(1, n_tok):
        mine = shifted(outer, "token", distance)
        theirs = swapped(mine, "latent", 1)
        foreign.append((n_tok - distance, mine, theirs, shifted(inner, "token", distance)))

    bias = lax.dynamic_slice_in_dim(
        encoder_layer_bias, lax.axis_index("token") * lat_dev, lat_dev, axis=1
    )

    group = n_lat // 4
    other, mine_bit = 1 - lat % 2, lat % 2
    far, near = 1 - (lat // 2) % 2, (lat // 2) % 2
    info_sent = jnp.stack(
        [layer] + [4 * i + 2 * b + other for b in (far, near) for i in range(group)]
    ).astype(jnp.int32)
    info_kept = jnp.stack(
        [layer] + [4 * i + 2 * b + mine_bit for b in (far, near) for i in range(group)]
    ).astype(jnp.int32)

    half = 2 * quarter
    both = 2 * group
    narrow = jnp.bfloat16

    def handed(codes):
        return codes, [lax.ppermute(part, "layer", [(0, 1)]) for part in codes]

    def finish(total):
        bit = 4
        while bit < n_lat:
            here = (lat // bit) % 2
            pairs = total.reshape(total.shape[0] // 2, 2, *total.shape[1:])
            away = lax.dynamic_index_in_dim(pairs, 1 - here, 1, keepdims=False)
            arrived = swapped(away.astype(narrow), "latent", bit)
            total = lax.dynamic_index_in_dim(pairs, here, 1, keepdims=False) + wide(arrived)
            bit *= 2
        return total[0]

    weights = (own_w, cross_w)
    codes, held = encode_first(x_own, inv, enc_w, bias, 2)
    codes, n_enc = handed(codes), len(held)
    inside = ((quarter, half),)
    outside = ((0, quarter), (3 * quarter, quarter))
    (sent_in, sent_out), held = decode(
        *codes, weights, info_sent,
        [(0, both, inside, narrow), (0, both, outside, jnp.float32)], width, held, [], "keep")
    there_in = swapped(sent_in, "latent", 1)
    (kept_in, kept_out), held = decode(
        *codes, weights, info_kept,
        [(0, both, inside, jnp.float32), (0, both, outside, jnp.float32)], width, held, [], "ring")
    across_in = (kept_in[:group] + wide(there_in[:group])).astype(narrow)
    total_in = kept_in[group:] + wide(there_in[group:]) + wide(swapped(across_in, "latent", 2))
    whole = ((0, half),)

    sent_back, kept_back = [], []
    for back, mine, theirs, _ in foreign:
        places = jnp.stack([side * quarter, (1 - side) * quarter]).astype(jnp.int32)
        codes, held = encode([mine, theirs], places, inv, held, n_enc, bias, [])
        codes = handed([codes])
        (sent,), held = decode(
            *codes, weights, info_sent, [(0, both, whole, narrow)], width, held, [across_in], "held")
        sent_back.append(shifted(sent, "token", back))
        (kept,), held = decode(
            *codes, weights, info_kept, [(0, both, whole, narrow)], width, held, [], "ring")
        kept_back.append(shifted(kept, "token", back))

    sent_out = (sent_out + sum(wide(part) for part in sent_back)).astype(narrow)
    there_out = swapped(sent_out, "latent", 1)
    returned = []
    for back, _, _, rows_in in foreign:
        codes, held = encode([rows_in], jnp.zeros((1,), jnp.int32), inv, held, n_enc, bias, [])
        codes = handed([codes])
        (far_sent, near_sent), held = decode(
            *codes, weights, info_sent,
            [(0, group, whole, narrow), (group, group, whole, narrow)], width, held, [], "held")
        far_in = swapped(far_sent, "latent", 1)
        near_in = swapped(near_sent, "latent", 1)
        (kept,), held = decode(
            *codes, weights, info_kept, [(0, both, whole, jnp.float32)], width, held,
            [sent_out, total_in], "ring")
        across = (kept[:group] + wide(far_in)).astype(narrow)
        part = finish(kept[group:] + wide(near_in) + wide(swapped(across, "latent", 2)))
        returned.append(shifted(part.astype(narrow), "token", back))

    kept_out = kept_out + sum(wide(part) for part in kept_back) + wide(there_out)
    across_out = swapped(kept_out[:group].astype(narrow), "latent", 2)
    total_out = finish(kept_out[group:] + wide(across_out))
    total_in = finish(total_in) + sum(wide(part) for part in returned)
    total = jnp.concatenate([total_out[:quarter], total_in, total_out[quarter:]])
    total = total + wide(dec_bias)
    recon = total.astype(jnp.bfloat16)[None]

    target = wide(targets[0])
    diff = total - target
    sums = jnp.stack([jnp.sum(diff * diff), jnp.sum(target * target)]).reshape(1, 2)
    sums = sum_over(sum_over(sums, "latent"), "token")
    ratio = sums[:, 0] / sums[:, 1]
    loss = sum_over(ratio, "layer") / 2.0
    return (recon, loss)


def solution(mesh):
    return jax.shard_map(
        local,
        mesh=mesh,
        in_specs=(
            P("layer", ("groups", "token"), None),
            P("layer", ("groups", "token"), "latent"),
            P("layer", None, ("latent", "token")),
            P("layer", "latent"),
            P("layer", ("latent", "token"), None),
            P(("latent", "token"), None),
            P("layer", "latent"),
        ),
        out_specs=(P("layer", ("groups", "token"), "latent"), P("groups")),
        check_vma=False,
    )
```

time: 417 us -> 243 us (0.58)
  waiting for transfers between devices: 264 us -> 60.3 us
  Pallas kernels: 0 us -> 68.1 us
  matrix products: 61.1 us -> 0 us
  starting transfers between devices: 2.2 us -> 41.9 us
  blocking collectives: 31.5 us -> 0 us
  local copies, waits for them, and re-layouts: 29 us -> 54.9 us
  between operations: 16.6 us -> 5.46 us
    reduce_scatter x1 -> x0, waiting for transfers between devices: 207 us -> none  [local(): lax.psum_scatter(result.reshape(rows * lax.axis_size(('latent', 'token'))...]
    pallas_call x0 -> x11, Pallas kernels: none -> 68.1 us  [the longest x8 55.2 us: call_with_held(): pl.pallas_call(inner, in_specs=[vmem] * n + list(specs) + [pl.BlockSpec(m...]
    dot_general x3 -> x0, matrix products: 61.1 us -> none  [the longest x1 21.3 us: local(): jnp.einsum('tm,mkp->ktp', earlier, cross_cols, preferred_element_type=jnp...]
    ppermute x1 -> x23, waiting for transfers between devices: 0.01 us -> 60.3 us  [the longest x8 48.9 us: swapped(): return lax.ppermute(value, axis, [(i, i ^ bit) for i in range(n)])]
    all_gather x1 -> x0, waiting for transfers between devices: 56.4 us -> none  [local(): lax.all_gather(x_local, 'token', axis=0, tiled=True).astype(jnp.float32)]
    unnamed x6 -> x84, local copies, waits for them, and re-layouts: 0.67 us -> 54 us
    ppermute x1 -> x23, starting transfers between devices: 2.12 us -> 41.9 us  [the longest x4 19 us: handed(): return (codes, [lax.ppermute(part, 'layer', [(0, 1)]) for part in codes])]
    psum x1 -> x0, blocking collectives: 31.5 us -> none  [local(): err_vec = lax.psum(slots * err_local, ('latent', 'token', 'layer'))]
  transfers between devices with their start and end apart: 3 -> 23, of which waited for: 2 -> 13; matrix products, arithmetic and copies ran while one was open for 12% -> 3% of each run, Pallas kernels for 0% -> 27%
where the time goes in v4:
time: 243 us; the launch traced here: 242 us
  Pallas kernels  68.1 us (28%)
  waiting for transfers between devices  60.3 us (25%)
  local copies, waits for them, and re-layouts  54.9 us (23%)
  starting transfers between devices  41.9 us (17%)
  other arithmetic  10.9 us (4%)
  between operations  5.46 us (2%)
    pallas_call x8, Pallas kernels, call_with_held(): pl.pallas_call(inner, in_specs=[vmem] * n + list(specs) + [pl.BlockSpec(m...  55.2 us
    unnamed x84, local copies, waits for them, and re-layouts  54 us
    ppermute x8, waiting for transfers between devices, swapped(): return lax.ppermute(value, axis, [(i, i ^ bit) for i in range(n)])  48.9 us
    ppermute x4, starting transfers between devices, handed(): return (codes, [lax.ppermute(part, 'layer', [(0, 1)]) for part in codes])  19 us
    ppermute x11, starting transfers between devices, shifted(): lax.ppermute(value, axis, [(i, (i + distance) % n) for i in range(n)])  12.9 us
    ppermute x11, waiting for transfers between devices, shifted(): lax.ppermute(value, axis, [(i, (i + distance) % n) for i in range(n)])  10.6 us
    pallas_call x1, Pallas kernels, encode_first(): pl.pallas_call(body, in_specs=[pl.BlockSpec(memory_space=pltpu.SMEM)] + [...  10.3 us
    ppermute x8, starting transfers between devices, swapped(): return lax.ppermute(value, axis, [(i, i ^ bit) for i in range(n)])  10 us
  transfers between devices with their start and end apart: 23, of which 13 were waited for; matrix products, arithmetic and copies ran while one was open for 3% of the time, Pallas kernels for 27%

profile of v4, /device:TPU:0, one launch (start us, length us, event | category | flops | bytes accessed | tf_op | source)
XLA Modules:
  0.0 241.6 jit_solution(3144337354060659546)
XLA Ops:
  0.7 1.9 copy-done.22
  2.5 1.6 square_sum.1
  4.2 3.0 %collective-permute-start = (f32[1]{0:T(128)}, f32[1]{0:T(128)}, u32[]{:S(2)}, u32[]{:S(2)}) collective-permute-start(f32[1]{0:T(128)} %square_sum.1), channel_id=1, source_target_pairs={{0,2},{2,0},{1,3},{3,1},{4,6},{6,4},{5,7},{7,5},{8,10},{10,8},{9,1... | collective-permute-start | bytes 20 | tf_op jit(solution)/shard_map/ppermute | solution.py:295
  7.2 1.8 collective-permute-done
  12.4 2.0 collective-permute-start.3
  14.4 10.3 %encode_first.1 = (bf16[384,1024]{1,0:T(8,128)(2,1)}, bf16[384,1024]{1,0:T(8,128)(2,1)}, bf16[4096,512]{1,0:T(8,128)(2,1)S(1)}, bf16[4096,512]{1,0:T(8,128)(2,1)...) custom-call(f32[1]{0:T(128)S(6)} %sqrt.3.inv_ref.after_ref.refs_7_, ...), custom_call_target="tpu_custom_call" | custom-call | tf_op jit(solution)/shard_map/encode_first/pallas_call | solution.py:111
  24.8 2.0 copy-done.6
  26.8 2.0 copy-done.10
  28.8 2.1 copy-done.14
  30.8 1.9 copy-done.18
  35.5 1.6 collective-permute-start.4
  39.4 2.2 copy-done.7
  41.6 2.2 copy-done.11
  43.8 2.2 copy-done.15
  46.0 2.2 copy-done.19
  48.2 9.0 %decode_keep.1 = (bf16[2,192,1024]{2,1,0:T(8,128)(2,1)}, f32[2,192,1024]{2,1,0:T(8,128)}, bf16[4,2048,512]{2,1,0:T(8,128)(2,1)S(1)}, bf16[4,2048,512]{2,1,0:T(8,...) custom-call(bf16[4096,512]{1,0:T(8,128)(2,1)S(1)} %copy-done.7, ...), custom_call_target="tpu_custom_call", output_to_operand_aliasing={{4}: (0, {}), {5}: (1, {}), {6}: (2, {}), {7}: (3, {})} | custom-call | tf_op jit(solution)/shard_map/decode_keep/pallas_call | solution.py:134
  57.2 3.3 %copy-done.2 = bf16[4,2048,512]{2,1,0:T(8,128)(2,1)} copy-done((bf16[4,2048,512]{2,1,0:T(8,128)(2,1)}, bf16[4,2048,512]{2,1,0:T(8,128)(2,1)S(1)}, u32[]{:S(2)}) %copy-start.2) | copy-done | bytes 8388632
  60.5 3.3 %copy-done.4 = bf16[4,2048,512]{2,1,0:T(8,128)(2,1)} copy-done((bf16[4,2048,512]{2,1,0:T(8,128)(2,1)}, bf16[4,2048,512]{2,1,0:T(8,128)(2,1)S(1)}, u32[]{:S(2)}) %copy-start.4) | copy-done | bytes 8388632
  63.8 2.0 copy-done.8
  65.8 2.0 copy-done.12
  67.8 2.1 copy-done.16
  69.9 1.9 copy-done.20
  73.7 3.4 %copy-done.3 = bf16[4,2048,512]{2,1,0:T(8,128)(2,1)S(1)} copy-done((bf16[4,2048,512]{2,1,0:T(8,128)(2,1)S(1)}, bf16[4,2048,512]{2,1,0:T(8,128)(2,1)}, u32[]{:S(2)}) %copy-start.3) | copy-done | bytes 8388632
  77.0 3.4 %copy-done.5 = bf16[4,2048,512]{2,1,0:T(8,128)(2,1)S(1)} copy-done((bf16[4,2048,512]{2,1,0:T(8,128)(2,1)S(1)}, bf16[4,2048,512]{2,1,0:T(8,128)(2,1)}, u32[]{:S(2)}) %copy-start.5) | copy-done | bytes 8388632
  80.4 2.2 copy-done.9
  82.6 2.2 copy-done.13
  84.8 2.2 copy-done.17
  87.0 2.2 copy-done.21
  89.2 9.4 %decode_ring.3 = (f32[2,192,1024]{2,1,0:T(8,128)}, f32[2,192,1024]{2,1,0:T(8,128)}, bf16[4096,512]{1,0:T(8,128)(2,1)S(1)}, bf16[4096,512]{1,0:T(8,128)(2,1)S(1)}...) custom-call(bf16[4096,512]{1,0:T(8,128)(2,1)S(1)} %copy-done.9, ...), custom_call_target="tpu_custom_call", output_to_operand_aliasing={{2}: (0, {}), {3}: (1, {}), {4}: (2, {}), {5}: (3, {}), {6}... | custom-call | tf_op jit(solution)/shard_map/decode_ring/pallas_call | solution.py:134
  98.6 6.5 %encode.2 = (bf16[192,2048]{1,0:T(8,128)(2,1)}, bf16[4096,512]{1,0:T(8,128)(2,1)S(1)}, bf16[4096,512]{1,0:T(8,128)(2,1)S(1)}, bf16[4096,512]{1,0:T(8,128)(2,1)S(...) custom-call(bf16[4096,512]{1,0:T(8,128)(2,1)S(1)} %get-tuple-element, ...), custom_call_target="tpu_custom_call", output_to_operand_aliasing={{1}: (0, {}), {2}: (1, {}), {3}: (2, {}), {4}: (3, {}), {5}... | custom-call | tf_op jit(solution)/shard_map/encode/pallas_call | solution.py:134
  105.1 10.0 %collective-permute-start.5 = (bf16[192,2048]{1,0:T(8,128)(2,1)}, bf16[192,2048]{1,0:T(8,128)(2,1)S(1)}, u32[]{:S(2)}, u32[]{:S(2)}) collective-permute-start(bf16[192,2048]{1,0:T(8,128)(2,1)} %get-tuple-element.89.refs_7_), channel_id=1, source_target_pairs={{0,1},{2,3},{4,5},{6,7},{8,9},{10,11},{12,13},{14,15},{16,17},{18,... | collective-permute-start | bytes 2359304 | tf_op jit(solution)/shard_map/ppermute | solution.py:358
  117.9 4.7 %decode_held.2 = (bf16[2,192,1024]{2,1,0:T(8,128)(2,1)}, bf16[4096,512]{1,0:T(8,128)(2,1)S(1)}, bf16[4096,512]{1,0:T(8,128)(2,1)S(1)}, bf16[4096,512]{1,0:T(8,12...) custom-call(bf16[4096,512]{1,0:T(8,128)(2,1)S(1)} %get-tuple-element, ...), custom_call_target="tpu_custom_call", output_to_operand_aliasing={{1}: (0, {}), {2}: (1, {}), {3}: (2, {}), {4}: (3, {}), {5}... | custom-call | tf_op jit(solution)/shard_map/decode_held/pallas_call | solution.py:134
  123.1 6.9 %decode_ring.4 = (bf16[2,192,1024]{2,1,0:T(8,128)(2,1)}, bf16[4096,512]{1,0:T(8,128)(2,1)S(1)}, bf16[4096,512]{1,0:T(8,128)(2,1)S(1)}, bf16[4096,512]{1,0:T(8,12...) custom-call(bf16[4096,512]{1,0:T(8,128)(2,1)S(1)} %get-tuple-element, ...), custom_call_target="tpu_custom_call", output_to_operand_aliasing={{1}: (0, {}), {2}: (1, {}), {3}: (2, {}), {4}: (3, {}), {5}... | custom-call | tf_op jit(solution)/shard_map/decode_ring/pallas_call | solution.py:134
  131.2 6.6 %encode.3 = (bf16[192,2048]{1,0:T(8,128)(2,1)}, bf16[4096,512]{1,0:T(8,128)(2,1)S(1)}, bf16[4096,512]{1,0:T(8,128)(2,1)S(1)}, bf16[4096,512]{1,0:T(8,128)(2,1)S(...) custom-call(bf16[4096,512]{1,0:T(8,128)(2,1)S(1)} %get-tuple-element, ...), custom_call_target="tpu_custom_call", output_to_operand_aliasing={{1}: (0, {}), {2}: (1, {}), {3}: (2, {}), {4}: (3, {}), {5}... | custom-call | tf_op jit(solution)/shard_map/encode/pallas_call | solution.py:134
  137.8 6.3 %collective-permute-start.13 = (bf16[192,2048]{1,0:T(8,128)(2,1)}, bf16[192,2048]{1,0:T(8,128)(2,1)S(1)}, u32[]{:S(2)}, u32[]{:S(2)}) collective-permute-start(bf16[192,2048]{1,0:T(8,128)(2,1)} %get-tuple-element.114.refs_7_), channel_id=1, source_target_pairs={{0,1},{2,3},{4,5},{6,7},{8,9},{10,11},{12,13},{14,15},{16,17},{18,... | collective-permute-start | bytes 2359304 | tf_op jit(solution)/shard_map/ppermute | solution.py:358
  144.1 2.7 %collective-permute-start.11 = (bf16[1,192,1024]{2,1,0:T(8,128)(2,1)S(1)}, bf16[1,192,1024]{2,1,0:T(8,128)(2,1)S(1)}, u32[]{:S(2)}, u32[]{:S(2)}) collective-permute-start(bf16[1,192,1024]{2,1,0:T(8,128)(2,1)S(1)} %copy-done.32), channel_id=1, source_target_pairs={{0,8},{4,12},{8,0},{12,4},{1,9},{5,13},{9,1},{13,5},{2,10},{6,14},... | collective-permute-start | bytes 1179656 | tf_op jit(solution)/shard_map/ppermute | solution.py:300
  149.9 4.8 %decode_held.3 = (bf16[1,192,1024]{2,1,0:T(8,128)(2,1)}, bf16[1,192,1024]{2,1,0:T(8,128)(2,1)}, bf16[4096,512]{1,0:T(8,128)(2,1)S(1)}, bf16[4096,512]{1,0:T(8,12...) custom-call(bf16[4096,512]{1,0:T(8,128)(2,1)S(1)} %get-tuple-element, ...), custom_call_target="tpu_custom_call", output_to_operand_aliasing={{2}: (0, {}), {3}: (1, {}), {4}: (2, {}), {5}: (3, {}), {6}... | custom-call | tf_op jit(solution)/shard_map/decode_held/pallas_call | solution.py:134
  154.8 1.6 collective-permute-start.15
  156.4 7.4 %collective-permute-done.11 = bf16[1,192,1024]{2,1,0:T(8,128)(2,1)S(1)} collective-permute-done((bf16[1,192,1024]{2,1,0:T(8,128)(2,1)S(1)}, bf16[1,192,1024]{2,1,0:T(8,128)(2,1)S(1)}, u32[]{:S(2)}, u32[]{:S(2)}) %collective-permute-start.11) | collective-permute-done | bytes 393248 | tf_op jit(solution)/shard_map/ppermute | solution.py:300
  164.8 7.3 %decode_ring.5 = (f32[2,192,1024]{2,1,0:T(8,128)}, bf16[4096,512]{1,0:T(8,128)(2,1)S(1)}, bf16[4096,512]{1,0:T(8,128)(2,1)S(1)}, bf16[4096,512]{1,0:T(8,128)(2,1...) custom-call(bf16[4096,512]{1,0:T(8,128)(2,1)S(1)} %get-tuple-element, ...), custom_call_target="tpu_custom_call", output_to_operand_aliasing={{1}: (0, {}), {2}: (1, {}), {3}: (2, {}), {4}: (3, {}), {5}... | custom-call | tf_op jit(solution)/shard_map/decode_ring/pallas_call | solution.py:134
  172.1 13.7 %collective-permute-done.15 = bf16[1,192,1024]{2,1,0:T(8,128)(2,1)S(1)} collective-permute-done((bf16[1,192,1024]{2,1,0:T(8,128)(2,1)}, bf16[1,192,1024]{2,1,0:T(8,128)(2,1)S(1)}, u32[]{:S(2)}, u32[]{:S(2)}) %collective-permute-start.15) | collective-permute-done | bytes 393248 | tf_op jit(solution)/shard_map/ppermute | solution.py:300
  187.6 3.0 %collective-permute-start.10 = (bf16[1,192,1024]{2,1,0:T(8,128)(2,1)S(1)}, bf16[1,192,1024]{2,1,0:T(8,128)(2,1)S(1)}, u32[]{:S(2)}, u32[]{:S(2)}) collective-permute-start(bf16[1,192,1024]{2,1,0:T(8,128)(2,1)S(1)} %slice.75), channel_id=1, source_target_pairs={{0,8},{4,12},{8,0},{12,4},{1,9},{5,13},{9,1},{13,5},{2,10},{6,14},... | collective-permute-start | bytes 1179656 | tf_op jit(solution)/shard_map/ppermute | solution.py:300
  190.5 4.3 %collective-permute-done.14 = bf16[1,192,1024]{2,1,0:T(8,128)(2,1)S(1)} collective-permute-done((bf16[1,192,1024]{2,1,0:T(8,128)(2,1)}, bf16[1,192,1024]{2,1,0:T(8,128)(2,1)S(1)}, u32[]{:S(2)}, u32[]{:S(2)}) %collective-permute-start.14) | collective-permute-done | bytes 393248 | tf_op jit(solution)/shard_map/ppermute | solution.py:300
  194.9 19.6 %collective-permute-done.16 = bf16[1,192,1024]{2,1,0:T(8,128)(2,1)S(1)} collective-permute-done((bf16[1,192,1024]{2,1,0:T(8,128)(2,1)S(1)}, bf16[1,192,1024]{2,1,0:T(8,128)(2,1)S(1)}, u32[]{:S(2)}, u32[]{:S(2)}) %collective-permute-start.16) | collective-permute-done | bytes 393248 | tf_op jit(solution)/shard_map/ppermute | solution.py:300
  216.1 3.9 %collective-permute-done.10 = bf16[1,192,1024]{2,1,0:T(8,128)(2,1)S(1)} collective-permute-done((bf16[1,192,1024]{2,1,0:T(8,128)(2,1)S(1)}, bf16[1,192,1024]{2,1,0:T(8,128)(2,1)S(1)}, u32[]{:S(2)}, u32[]{:S(2)}) %collective-permute-start.10) | collective-permute-done | bytes 393248 | tf_op jit(solution)/shard_map/ppermute | solution.py:300
  220.3 2.2 collective-permute-done.17
  228.6 2.2 collective-permute-done.19
  233.9 2.7 %collective-permute-done.21 = f32[1,2]{1,0:T(1,128)S(1)} collective-permute-done((f32[1,2]{1,0:T(1,128)S(1)}, f32[1,2]{1,0:T(1,128)S(1)}, u32[]{:S(2)}, u32[]{:S(2)}) %collective-permute-start.21) | collective-permute-done | bytes 40 | tf_op jit(solution)/shard_map/ppermute | solution.py:295
  (114 shorter events, 32.2 us)
Async XLA Ops:
  0.6 13.8 %copy-start = (bf16[1,4096]{1,0:T(2,128)(2,1)S(1)}, bf16[1,4096]{1,0:T(2,128)(2,1)}, u32[]{:S(2)}) copy-start(bf16[1,4096]{1,0:T(2,128)(2,1)} %param.10) | copy-start | bytes 24580
  2.5 7.7 %copy-start.23 = (bf16[1,384,4096]{2,1,0:T(8,128)(2,1)S(1)}, bf16[1,384,4096]{2,1,0:T(8,128)(2,1)}, u32[]{:S(2)}) copy-start(bf16[1,384,4096]{2,1,0:T(8,128)(2,1)} %param.7) | copy-start | bytes 9437188
  4.2 4.8 %collective-permute-start = (f32[1]{0:T(128)}, f32[1]{0:T(128)}, u32[]{:S(2)}, u32[]{:S(2)}) collective-permute-start(f32[1]{0:T(128)} %square_sum.1), channel_id=1, source_target_pairs={{0,2},{2,0},{1,3},{3,1},{4,6},{6,4},{5,7},{7,5},{8,10},{10,8},{9,1... | collective-permute-start | bytes 20 | tf_op jit(solution)/shard_map/ppermute | solution.py:295
  12.4 23.1 %collective-permute-start.3 = (bf16[96,4096]{1,0:T(8,128)(2,1)}, bf16[96,4096]{1,0:T(8,128)(2,1)}, u32[]{:S(2)}, u32[]{:S(2)}) collective-permute-start(bf16[96,4096]{1,0:T(8,128)(2,1)} %get-tuple-element.82), channel_id=1, source_target_pairs={{0,2},{2,0},{1,3},{3,1},{4,6},{6,4},{5,7},{7,5},{8,10},{10,8},{9,1... | collective-permute-start | bytes 2359304 | tf_op jit(solution)/shard_map/ppermute | solution.py:295
  14.4 10.4 %copy-start.24 = (bf16[1,2048]{1,0:T(2,128)(2,1)}, bf16[1,2048]{1,0:T(2,128)(2,1)S(1)}, u32[]{:S(2)}) copy-start(bf16[1,2048]{1,0:T(2,128)(2,1)S(1)} %constant_dynamic-slice_fusion.b_ref.refs_8_) | copy-start | bytes 12292
  32.8 5.5 %collective-permute-start.1 = (bf16[384,1024]{1,0:T(8,128)(2,1)}, bf16[384,1024]{1,0:T(8,128)(2,1)S(1)}, u32[]{:S(2)}, u32[]{:S(2)}) collective-permute-start(bf16[384,1024]{1,0:T(8,128)(2,1)} %get-tuple-element.67.refs_5_.refs_7_), channel_id=1, source_target_pairs={{0,1},{2,3},{4,5},{6,7},{8,9},{10,11},{12,13},{14,15},{16,17},{18,... | collective-permute-start | bytes 2359304 | tf_op jit(solution)/shard_map/ppermute | solution.py:358
  34.1 4.2 %collective-permute-start.2 = (bf16[384,1024]{1,0:T(8,128)(2,1)}, bf16[384,1024]{1,0:T(8,128)(2,1)S(1)}, u32[]{:S(2)}, u32[]{:S(2)}) collective-permute-start(bf16[384,1024]{1,0:T(8,128)(2,1)} %get-tuple-element.68.refs_6_.refs_8_), channel_id=1, source_target_pairs={{0,1},{2,3},{4,5},{6,7},{8,9},{10,11},{12,13},{14,15},{16,17},{18,... | collective-permute-start | bytes 2359304 | tf_op jit(solution)/shard_map/ppermute | solution.py:358
  35.5 63.1 %collective-permute-start.4 = (bf16[96,4096]{1,0:T(8,128)(2,1)}, bf16[96,4096]{1,0:T(8,128)(2,1)}, u32[]{:S(2)}, u32[]{:S(2)}) collective-permute-start(bf16[96,4096]{1,0:T(8,128)(2,1)} %collective-permute-done.3.refs_9_), channel_id=1, source_target_pairs={{0,4},{4,0},{8,12},{12,8},{1,5},{5,1},{9,13},{13,9},{2,6},{6,2},{1... | collective-permute-start | bytes 2359304 | tf_op jit(solution)/shard_map/ppermute | solution.py:300
  37.1 92.9 %collective-permute-start.12 = (bf16[192,4096]{1,0:T(8,128)(2,1)}, bf16[192,4096]{1,0:T(8,128)(2,1)S(1)}, u32[]{:S(2)}, u32[]{:S(2)}) collective-permute-start(bf16[192,4096]{1,0:T(8,128)(2,1)} %copy-done.25), channel_id=1, source_target_pairs={{0,2},{2,0},{1,3},{3,1},{4,6},{6,4},{5,7},{7,5},{8,10},{10,8},{9,1... | collective-permute-start | bytes 4718600 | tf_op jit(solution)/shard_map/ppermute | solution.py:295
  39.4 2.2 copy-start.7
  41.6 2.2 copy-start.11
  43.8 2.2 copy-start.15
  46.0 2.2 copy-start.19
  57.2 3.3 %copy-start.2 = (bf16[4,2048,512]{2,1,0:T(8,128)(2,1)}, bf16[4,2048,512]{2,1,0:T(8,128)(2,1)S(1)}, u32[]{:S(2)}) copy-start(bf16[4,2048,512]{2,1,0:T(8,128)(2,1)S(1)} %get-tuple-element.73.refs_4_) | copy-start | bytes 25165828
  60.5 3.3 %copy-start.4 = (bf16[4,2048,512]{2,1,0:T(8,128)(2,1)}, bf16[4,2048,512]{2,1,0:T(8,128)(2,1)S(1)}, u32[]{:S(2)}) copy-start(bf16[4,2048,512]{2,1,0:T(8,128)(2,1)S(1)} %get-tuple-element.74.refs_5_) | copy-start | bytes 25165828
  71.8 43.3 %collective-permute-start.6 = (bf16[2,192,1024]{2,1,0:T(8,128)(2,1)}, bf16[2,192,1024]{2,1,0:T(8,128)(2,1)S(1)}, u32[]{:S(2)}, u32[]{:S(2)}) collective-permute-start(bf16[2,192,1024]{2,1,0:T(8,128)(2,1)} %get-tuple-element.91), channel_id=1, source_target_pairs={{0,4},{4,0},{8,12},{12,8},{1,5},{5,1},{9,13},{13,9},{2,6},{6,2},{1... | collective-permute-start | bytes 2359304 | tf_op jit(solution)/shard_map/ppermute | solution.py:300
  73.7 3.4 %copy-start.3 = (bf16[4,2048,512]{2,1,0:T(8,128)(2,1)S(1)}, bf16[4,2048,512]{2,1,0:T(8,128)(2,1)}, u32[]{:S(2)}) copy-start(bf16[4,2048,512]{2,1,0:T(8,128)(2,1)} %copy-done.2) | copy-start | bytes 25165828
  77.0 3.4 %copy-start.5 = (bf16[4,2048,512]{2,1,0:T(8,128)(2,1)S(1)}, bf16[4,2048,512]{2,1,0:T(8,128)(2,1)}, u32[]{:S(2)}) copy-start(bf16[4,2048,512]{2,1,0:T(8,128)(2,1)} %copy-done.4) | copy-start | bytes 25165828
  80.4 2.2 copy-start.9
  82.6 2.2 copy-start.13
  98.6 16.6 %copy-start.35 = (f32[2,192,1024]{2,1,0:T(8,128)S(1)}, f32[2,192,1024]{2,1,0:T(8,128)}, u32[]{:S(2)}) copy-start(f32[2,192,1024]{2,1,0:T(8,128)} %get-tuple-element.90) | copy-start | bytes 4718596
  105.1 11.9 %collective-permute-start.5 = (bf16[192,2048]{1,0:T(8,128)(2,1)}, bf16[192,2048]{1,0:T(8,128)(2,1)S(1)}, u32[]{:S(2)}, u32[]{:S(2)}) collective-permute-start(bf16[192,2048]{1,0:T(8,128)(2,1)} %get-tuple-element.89.refs_7_), channel_id=1, source_target_pairs={{0,1},{2,3},{4,5},{6,7},{8,9},{10,11},{12,13},{14,15},{16,17},{18,... | collective-permute-start | bytes 2359304 | tf_op jit(solution)/shard_map/ppermute | solution.py:358
  115.1 7.5 %copy-start.38 = (bf16[2,192,1024]{2,1,0:T(8,128)(2,1)}, bf16[2,192,1024]{2,1,0:T(8,128)(2,1)S(1)}, u32[]{:S(2)}) copy-start(bf16[2,192,1024]{2,1,0:T(8,128)(2,1)S(1)} %collective-permute-done.6) | copy-start | bytes 2359300
  122.6 25.6 %collective-permute-start.8 = (bf16[2,192,1024]{2,1,0:T(8,128)(2,1)}, bf16[2,192,1024]{2,1,0:T(8,128)(2,1)S(1)}, u32[]{:S(2)}, u32[]{:S(2)}) collective-permute-start(bf16[2,192,1024]{2,1,0:T(8,128)(2,1)} %get-tuple-element.100), channel_id=1, source_target_pairs={{0,2},{2,0},{1,3},{3,1},{4,6},{6,4},{5,7},{7,5},{8,10},{10,8},{9,1... | collective-permute-start | bytes 2359304 | tf_op jit(solution)/shard_map/ppermute | solution.py:295
  131.2 12.9 %copy-start.32 = (bf16[1,192,1024]{2,1,0:T(8,128)(2,1)S(1)}, bf16[1,192,1024]{2,1,0:T(8,128)(2,1)}, u32[]{:S(2)}) copy-start(bf16[1,192,1024]{2,1,0:T(8,128)(2,1)} %add_convert_fusion.3.refs_9_) | copy-start | bytes 1179652
  131.2 17.1 %copy-start.34 = (f32[2,192,1024]{2,1,0:T(8,128)S(1)}, f32[2,192,1024]{2,1,0:T(8,128)}, u32[]{:S(2)}) copy-start(f32[2,192,1024]{2,1,0:T(8,128)} %get-tuple-element.99) | copy-start | bytes 4718596
  137.8 11.3 %collective-permute-start.13 = (bf16[192,2048]{1,0:T(8,128)(2,1)}, bf16[192,2048]{1,0:T(8,128)(2,1)S(1)}, u32[]{:S(2)}, u32[]{:S(2)}) collective-permute-start(bf16[192,2048]{1,0:T(8,128)(2,1)} %get-tuple-element.114.refs_7_), channel_id=1, source_target_pairs={{0,1},{2,3},{4,5},{6,7},{8,9},{10,11},{12,13},{14,15},{16,17},{18,... | collective-permute-start | bytes 2359304 | tf_op jit(solution)/shard_map/ppermute | solution.py:358
  144.1 19.7 %collective-permute-start.11 = (bf16[1,192,1024]{2,1,0:T(8,128)(2,1)S(1)}, bf16[1,192,1024]{2,1,0:T(8,128)(2,1)S(1)}, u32[]{:S(2)}, u32[]{:S(2)}) collective-permute-start(bf16[1,192,1024]{2,1,0:T(8,128)(2,1)S(1)} %copy-done.32), channel_id=1, source_target_pairs={{0,8},{4,12},{8,0},{12,4},{1,9},{5,13},{9,1},{13,5},{2,10},{6,14},... | collective-permute-start | bytes 1179656 | tf_op jit(solution)/shard_map/ppermute | solution.py:300
  146.8 40.4 %collective-permute-start.7 = (bf16[2,192,1024]{2,1,0:T(8,128)(2,1)}, bf16[2,192,1024]{2,1,0:T(8,128)(2,1)S(1)}, u32[]{:S(2)}, u32[]{:S(2)}) collective-permute-start(bf16[2,192,1024]{2,1,0:T(8,128)(2,1)} %get-tuple-element.98), channel_id=1, source_target_pairs={{0,2},{2,0},{1,3},{3,1},{4,6},{6,4},{5,7},{7,5},{8,10},{10,8},{9,1... | collective-permute-start | bytes 2359304 | tf_op jit(solution)/shard_map/ppermute | solution.py:295
  148.5 6.3 %copy-start.27 = (bf16[2,192,1024]{2,1,0:T(8,128)(2,1)}, bf16[2,192,1024]{2,1,0:T(8,128)(2,1)S(1)}, u32[]{:S(2)}) copy-start(bf16[2,192,1024]{2,1,0:T(8,128)(2,1)S(1)} %add_convert_fusion.refs_11_) | copy-start | bytes 2359300
  148.5 38.6 %collective-permute-start.9 = (bf16[2,192,1024]{2,1,0:T(8,128)(2,1)S(1)}, bf16[2,192,1024]{2,1,0:T(8,128)(2,1)S(1)}, u32[]{:S(2)}, u32[]{:S(2)}) collective-permute-start(bf16[2,192,1024]{2,1,0:T(8,128)(2,1)S(1)} %add_convert_fusion.refs_11_), channel_id=1, source_target_pairs={{0,4},{4,0},{8,12},{12,8},{1,5},{5,1},{9,13},{13,9},{2,6},{6,2},{1... | collective-permute-start | bytes 2359304 | tf_op jit(solution)/shard_map/ppermute | solution.py:300
  149.9 13.9 %copy-start.39 = (bf16[2,192,1024]{2,1,0:T(8,128)(2,1)S(1)}, bf16[2,192,1024]{2,1,0:T(8,128)(2,1)}, u32[]{:S(2)}) copy-start(bf16[2,192,1024]{2,1,0:T(8,128)(2,1)} %copy-done.38) | copy-start | bytes 2359300
  154.8 31.0 %collective-permute-start.15 = (bf16[1,192,1024]{2,1,0:T(8,128)(2,1)}, bf16[1,192,1024]{2,1,0:T(8,128)(2,1)S(1)}, u32[]{:S(2)}, u32[]{:S(2)}) collective-permute-start(bf16[1,192,1024]{2,1,0:T(8,128)(2,1)} %get-tuple-element.123), channel_id=1, source_target_pairs={{0,4},{4,0},{8,12},{12,8},{1,5},{5,1},{9,13},{13,9},{2,6},{6,2},{1... | collective-permute-start | bytes 1179656 | tf_op jit(solution)/shard_map/ppermute | solution.py:300
  164.8 30.0 %collective-permute-start.14 = (bf16[1,192,1024]{2,1,0:T(8,128)(2,1)}, bf16[1,192,1024]{2,1,0:T(8,128)(2,1)S(1)}, u32[]{:S(2)}, u32[]{:S(2)}) collective-permute-start(bf16[1,192,1024]{2,1,0:T(8,128)(2,1)} %get-tuple-element.122), channel_id=1, source_target_pairs={{0,4},{4,0},{8,12},{12,8},{1,5},{5,1},{9,13},{13,9},{2,6},{6,2},{1... | collective-permute-start | bytes 1179656 | tf_op jit(solution)/shard_map/ppermute | solution.py:300
  164.8 22.3 %copy-start.37 = (f32[2,192,1024]{2,1,0:T(8,128)S(1)}, f32[2,192,1024]{2,1,0:T(8,128)}, u32[]{:S(2)}) copy-start(f32[2,192,1024]{2,1,0:T(8,128)} %get-tuple-element.75) | copy-start | bytes 4718596
  172.1 18.4 %copy-start.41 = (bf16[1,1024]{1,0:T(2,128)(2,1)S(1)}, bf16[1,1024]{1,0:T(2,128)(2,1)}, u32[]{:S(2)}) copy-start(bf16[1,1024]{1,0:T(2,128)(2,1)} %param.13) | copy-start | bytes 6148
  172.1 42.3 %copy-start.36 = (f32[2,192,1024]{2,1,0:T(8,128)S(1)}, f32[2,192,1024]{2,1,0:T(8,128)}, u32[]{:S(2)}) copy-start(f32[2,192,1024]{2,1,0:T(8,128)} %get-tuple-element.121) | copy-start | bytes 4718596
  187.0 27.4 %collective-permute-start.16 = (bf16[1,192,1024]{2,1,0:T(8,128)(2,1)S(1)}, bf16[1,192,1024]{2,1,0:T(8,128)(2,1)S(1)}, u32[]{:S(2)}, u32[]{:S(2)}) collective-permute-start(bf16[1,192,1024]{2,1,0:T(8,128)(2,1)S(1)} %add_convert_fusion.2), channel_id=1, source_target_pairs={{0,8},{4,12},{8,0},{12,4},{1,9},{5,13},{9,1},{13,5},{2,10},{6,14},... | collective-permute-start | bytes 1179656 | tf_op jit(solution)/shard_map/ppermute | solution.py:300
  187.5 35.0 %copy-start.26 = (f32[1,192,1024]{2,1,0:T(8,128)S(1)}, f32[1,192,1024]{2,1,0:T(8,128)}, u32[]{:S(2)}) copy-start(f32[1,192,1024]{2,1,0:T(8,128)} %convert_add_fusion.1.refs_12_) | copy-start | bytes 2359300
  187.6 35.0 %copy-start.40 = (bf16[1,384,1024]{2,1,0:T(8,128)(2,1)S(1)}, bf16[1,384,1024]{2,1,0:T(8,128)(2,1)}, u32[]{:S(2)}) copy-start(bf16[1,384,1024]{2,1,0:T(8,128)(2,1)} %param.8) | copy-start | bytes 2359300
  187.6 32.4 %collective-permute-start.10 = (bf16[1,192,1024]{2,1,0:T(8,128)(2,1)S(1)}, bf16[1,192,1024]{2,1,0:T(8,128)(2,1)S(1)}, u32[]{:S(2)}, u32[]{:S(2)}) collective-permute-start(bf16[1,192,1024]{2,1,0:T(8,128)(2,1)S(1)} %slice.75), channel_id=1, source_target_pairs={{0,8},{4,12},{8,0},{12,4},{1,9},{5,13},{9,1},{13,5},{2,10},{6,14},... | collective-permute-start | bytes 1179656 | tf_op jit(solution)/shard_map/ppermute | solution.py:300
  214.6 7.8 %collective-permute-start.17 = (bf16[192,1024]{1,0:T(8,128)(2,1)S(1)}, bf16[192,1024]{1,0:T(8,128)(2,1)S(1)}, u32[]{:S(2)}, u32[]{:S(2)}) collective-permute-start(bf16[192,1024]{1,0:T(8,128)(2,1)S(1)} %fusion.4), channel_id=1, source_target_pairs={{0,2},{2,0},{1,3},{3,1},{4,6},{6,4},{5,7},{7,5},{8,10},{10,8},{9,1... | collective-permute-start | bytes 1179656 | tf_op jit(solution)/shard_map/ppermute | solution.py:295
  220.0 20.5 %copy-start.1 = (bf16[1,4096]{1,0:T(2,128)(2,1)S(1)}, bf16[1,4096]{1,0:T(2,128)(2,1)}, u32[]{:S(2)}) copy-start(bf16[1,4096]{1,0:T(2,128)(2,1)} %param.10) | copy-start | bytes 24580
  225.1 3.5 %collective-permute-start.20 = (f32[1,2]{1,0:T(1,128)S(1)}, f32[1,2]{1,0:T(1,128)S(1)}, u32[]{:S(2)}, u32[]{:S(2)}) collective-permute-start(f32[1,2]{1,0:T(1,128)S(1)} %maximum_bitcast_fusion), channel_id=1, source_target_pairs={{0,12},{4,0},{8,4},{12,8},{1,13},{5,1},{9,5},{13,9},{2,14},{6,2},{... | collective-permute-start | bytes 32 | tf_op jit(solution)/shard_map/ppermute | solution.py:295
  226.4 4.4 %collective-permute-start.19 = (f32[1,2]{1,0:T(1,128)S(1)}, f32[1,2]{1,0:T(1,128)S(1)}, u32[]{:S(2)}, u32[]{:S(2)}) collective-permute-start(f32[1,2]{1,0:T(1,128)S(1)} %maximum_bitcast_fusion), channel_id=1, source_target_pairs={{0,8},{4,12},{8,0},{12,4},{1,9},{5,13},{9,1},{13,5},{2,10},{6,14},... | collective-permute-start | bytes 32 | tf_op jit(solution)/shard_map/ppermute | solution.py:295
  226.4 5.3 %collective-permute-start.18 = (f32[1,2]{1,0:T(1,128)S(1)}, f32[1,2]{1,0:T(1,128)S(1)}, u32[]{:S(2)}, u32[]{:S(2)}) collective-permute-start(f32[1,2]{1,0:T(1,128)S(1)} %maximum_bitcast_fusion), channel_id=1, source_target_pairs={{0,4},{4,8},{8,12},{12,0},{1,5},{5,9},{9,13},{13,1},{2,6},{6,10},{... | collective-permute-start | bytes 32 | tf_op jit(solution)/shard_map/ppermute | solution.py:295
  233.1 3.5 %collective-permute-start.21 = (f32[1,2]{1,0:T(1,128)S(1)}, f32[1,2]{1,0:T(1,128)S(1)}, u32[]{:S(2)}, u32[]{:S(2)}) collective-permute-start(f32[1,2]{1,0:T(1,128)S(1)} %add_add_fusion), channel_id=1, source_target_pairs={{0,2},{2,0},{1,3},{3,1},{4,6},{6,4},{5,7},{7,5},{8,10},{10,8},{9,1... | collective-permute-start | bytes 32 | tf_op jit(solution)/shard_map/ppermute | solution.py:295
  238.5 1.3 collective-permute-start.22
  (17 other events, 28.4 us)

commit v5 on v3

--- a/solution.py
+++ b/solution.py
@@ -5,7 +5,7 @@
 from jax.experimental.pallas import tpu as pltpu
 from jax.sharding import PartitionSpec as P
 
-VMEM_LIMIT = 48 * 1024 * 1024
+VMEM_LIMIT = 40 * 1024 * 1024
 SLOTS = 3
 TILE = 512
 COST = pl.CostEstimate(flops=0, bytes_accessed=0, transcendentals=0)
@@ -72,6 +72,23 @@
     )(side.reshape(1), x)
 
 
+def gate(values, after):
+    n = len(values)
+
+    def body(after_ref, *refs):
+        pass
+
+    return pl.pallas_call(
+        body,
+        in_specs=[pl.BlockSpec(memory_space=pltpu.SMEM)] + [pl.BlockSpec(memory_space=pl.ANY)] * n,
+        out_specs=[pl.BlockSpec(memory_space=pl.ANY)] * n,
+        out_shape=[jax.ShapeDtypeStruct(value.shape, value.dtype) for value in values],
+        input_output_aliases={1 + i: i for i in range(n)},
+        cost_estimate=COST,
+        name="gate",
+    )(after, *values)
+
+
 def ring_loop(count, start, step):
     for t in range(min(SLOTS, count)):
         start(t, t)
@@ -89,16 +106,17 @@
     lax.fori_loop(0, count, turn, 0)
 
 
-def encode(pieces, places, inv, weight, bias, parts, after):
+def encode(pieces, places, inv, weight, bias, parts, also):
     rows, width = sum(piece[2] for piece in pieces), pieces[0][0].shape[1]
     latents = weight.shape[1]
-    tile = tile_of(latents // parts, TILE)
-    per = latents // parts // tile
-    n = len(pieces)
+    part = latents // parts
+    tile = tile_of(part, TILE)
+    n, m = len(pieces), len(also)
 
     def body(places_ref, inv_ref, b_ref, *refs):
-        x_refs, w_ref, o_refs = refs[:n], refs[n], refs[n + 2:n + 2 + parts]
-        lhs, ring, lhs_sem, ring_sem = refs[n + 2 + parts:]
+        x_refs, w_ref = refs[:n], refs[n]
+        o_refs = refs[n + 1 + m:n + 1 + m + parts]
+        lhs, ring, lhs_sem, ring_sem = refs[n + 1 + m + parts:]
 
         def lhs_copy(i):
             _, first, count = pieces[i]
@@ -122,13 +140,14 @@
                     lhs_copy(i).wait()
 
             tile_copy(t, slot).wait()
-            pre = jnp.dot(lhs[...], ring[slot], preferred_element_type=jnp.float32)
-            pre = pre * inv_ref[0] + b_ref[:, columns(t)].astype(jnp.float32)
-            value = jnp.maximum(pre, 0.0).astype(jnp.bfloat16)
-            for p in range(parts):
-                @pl.when(lax.div(t, per) == p)
+            value = jnp.dot(lhs[...], ring[slot], preferred_element_type=jnp.float32)
+            value = value * inv_ref[0] + b_ref[:, columns(t)].astype(jnp.float32)
+            value = jnp.maximum(value, 0.0).astype(jnp.bfloat16)
+            per = part // tile
+            for i, o_ref in enumerate(o_refs):
+                @pl.when(lax.div(t, per) == i)
                 def _():
-                    o_refs[p][:, columns(lax.rem(t, per))] = value
+                    o_ref[:, columns(lax.rem(t, per))] = value
 
         ring_loop(latents // tile, lambda t, slot: tile_copy(t, slot).start(), step)
 
@@ -138,9 +157,9 @@
             pl.BlockSpec(memory_space=pltpu.SMEM),
             pl.BlockSpec(memory_space=pltpu.SMEM),
             pl.BlockSpec(memory_space=pltpu.VMEM),
-        ] + [pl.BlockSpec(memory_space=pl.ANY)] * (n + 2),
+        ] + [pl.BlockSpec(memory_space=pl.ANY)] * (n + 1 + m),
         out_specs=[pl.BlockSpec(memory_space=pltpu.VMEM)] * parts,
-        out_shape=[jax.ShapeDtypeStruct((rows, latents // parts), jnp.bfloat16)] * parts,
+        out_shape=[jax.ShapeDtypeStruct((rows, part), jnp.bfloat16)] * parts,
         scratch_shapes=[
             pltpu.VMEM((rows, width), jnp.bfloat16),
             pltpu.VMEM((SLOTS, width, tile), jnp.bfloat16),
@@ -150,26 +169,27 @@
         compiler_params=pltpu.CompilerParams(vmem_limit_bytes=VMEM_LIMIT),
         cost_estimate=COST,
         name="encode",
-    )(places, inv.reshape(1), bias, *[piece[0] for piece in pieces], weight, after)
-
-
-def decode(codes, earlier, own_w, cross_w, info, outs, width, after):
+    )(places, inv, bias, *[piece[0] for piece in pieces], weight, *also)
+
+
+def decode(codes, earlier, own_w, cross_w, info, outs, width, also):
     parts = len(codes)
     rows, part = codes[0].shape
     latents = parts * part
     tile = tile_of(width, TILE)
     per = width // tile
     blocks = info.shape[0] - 1
+    m = len(also)
 
     def body(info_ref, *refs):
-        c_refs, e_refs, s_ref, x_ref = refs[:parts], refs[parts:2 * parts], refs[2 * parts], refs[2 * parts + 1]
-        o_refs = refs[2 * parts + 3:2 * parts + 3 + len(outs)]
-        lhs, ring, lhs_sem, ring_sem = refs[2 * parts + 3 + len(outs):]
+        code_refs, (s_ref, x_ref), refs = refs[:2 * parts], refs[2 * parts:2 * parts + 2], refs[2 * parts + 2:]
+        o_refs = refs[m:m + len(outs)]
+        lhs, ring, lhs_sem, ring_sem = refs[m + len(outs):]
         later = info_ref[0] != 0
 
         def lhs_copy(i):
-            source = c_refs[i] if i < parts else e_refs[i - parts]
-            return pltpu.make_async_copy(source, lhs.at[:, pl.ds(i * part, part)], lhs_sem.at[i])
+            return pltpu.make_async_copy(
+                code_refs[i], lhs.at[:, pl.ds(i * part, part)], lhs_sem.at[i])
 
         def tile_copy(source, i, t, slot):
             column = info_ref[1 + lax.div(t, per)] * width + lax.rem(t, per) * tile
@@ -196,11 +216,14 @@
         def put(t, value):
             b = lax.div(t, per)
             across = pl.ds(pl.multiple_of(lax.rem(t, per) * tile, tile), tile)
-            for (block, count, row, height, dtype), o_ref in zip(outs, o_refs):
-                @pl.when((b >= block) & (b < block + count))
+            for (block, many, spans, dtype), o_ref in zip(outs, o_refs):
+                @pl.when((b >= block) & (b < block + many))
                 def _():
-                    here = jnp.clip(b - block, 0, count - 1)
-                    o_ref[here, :, across] = value[row:row + height].astype(dtype)
+                    here = jnp.clip(b - block, 0, many - 1)
+                    at = 0
+                    for row, height in spans:
+                        o_ref[here, at:at + height, across] = value[row:row + height].astype(dtype)
+                        at += height
 
         def step(t, slot):
             @pl.when(t == 0)
@@ -230,11 +253,11 @@
     return pl.pallas_call(
         body,
         in_specs=[pl.BlockSpec(memory_space=pltpu.SMEM)]
-        + [pl.BlockSpec(memory_space=pl.ANY)] * (2 * parts + 3),
+        + [pl.BlockSpec(memory_space=pl.ANY)] * (2 * parts + 2 + m),
         out_specs=[pl.BlockSpec(memory_space=pltpu.VMEM)] * len(outs),
         out_shape=[
-            jax.ShapeDtypeStruct((count, height, width), dtype)
-            for _, count, _, height, dtype in outs
+            jax.ShapeDtypeStruct((many, sum(height for _, height in spans), width), dtype)
+            for _, many, spans, dtype in outs
         ],
         scratch_shapes=[
             pltpu.VMEM((rows, 2 * latents), jnp.bfloat16),
@@ -245,7 +268,7 @@
         compiler_params=pltpu.CompilerParams(vmem_limit_bytes=VMEM_LIMIT),
         cost_estimate=COST,
         name="decode",
-    )(info, *codes, *earlier, own_w, cross_w, after)
+    )(info, *codes, *earlier, own_w, cross_w, *also)
 
 
 def shifted(value, axis, distance):
@@ -265,6 +288,10 @@
     return total
 
 
+def in_hbm(value):
+    return pltpu.with_memory_space_constraint(value, pltpu.HBM)
+
+
 def wide(value):
     return value.astype(jnp.float32)
 
@@ -274,10 +301,11 @@
     lat = lax.axis_index("latent")
     n_lat = lax.axis_size("latent")
     n_tok = lax.axis_size("token")
-    x_own = inputs[0]
+    x_own = in_hbm(inputs[0])
     rows, model = x_own.shape
-    enc_w = enc_weight[0]
-    own_w = dec_self[0]
+    enc_w = in_hbm(enc_weight[0])
+    own_w = in_hbm(dec_self[0])
+    cross_w = in_hbm(dec_cross)
     lat_dev = enc_w.shape[1]
     width = dec_bias.shape[1]
     quarter = rows // 4
@@ -287,6 +315,7 @@
     square = sum_over(square, "token")
     scale = jnp.sqrt(square / (rows * n_tok * model) + 1e-06)
     inv = 1.0 / scale
+    outer, inner = gate([outer, inner], inv)
     foreign = []
     for distance in range(1, n_tok):
         mine = shifted(outer, "token", distance)
@@ -310,15 +339,15 @@
     half = 2 * quarter
     both = 2 * group
     narrow = jnp.bfloat16
-    origin = jnp.int32(0)
-
-    def codes_of(pieces, places, parts, after):
-        codes = encode(
-            pieces, jnp.stack(places).astype(jnp.int32), inv, enc_w, bias, parts, after)
-        return codes, [lax.ppermute(part, "layer", [(0, 1)]) for part in codes]
-
-    def products(codes, info, outs, after):
-        return decode(*codes, own_w, dec_cross, info, outs, width, after)
+
+    def earlier_of(codes):
+        return [lax.ppermute(part, "layer", [(0, 1)]) for part in codes]
+
+    def places(*rows):
+        return jnp.stack([jnp.int32(row) for row in rows])
+
+    def products(codes, earlier, info, outs, also):
+        return decode(codes, earlier, own_w, cross_w, info, outs, width, also)
 
     def finish(total):
         bit = 4
@@ -331,46 +360,54 @@
             bit *= 2
         return total[0]
 
-    codes = codes_of([(x_own, quarter, half), (x_own, 0, quarter), (x_own, 3 * quarter, quarter)],
-                     [origin, origin + half, origin + half + quarter], 2, x_own)
+    codes = encode([(x_own, 0, rows)], places(0), inv, enc_w, bias, 2, [])
+    earlier = earlier_of(codes)
+    inside = ((quarter, half),)
+    outside = ((0, quarter), (3 * quarter, quarter))
     sent_in, sent_out = products(
-        codes, info_sent, [(0, both, 0, half, narrow), (0, both, half, half, jnp.float32)], codes[0][0])
+        codes, earlier, info_sent, [(0, both, inside, narrow), (0, both, outside, jnp.float32)], [])
     there_in = swapped(sent_in, "latent", 1)
     kept_in, kept_out = products(
-        codes, info_kept, [(0, both, 0, half, jnp.float32), (0, both, half, half, jnp.float32)], sent_in)
-    after = kept_in
+        codes, earlier, info_kept,
+        [(0, both, inside, jnp.float32), (0, both, outside, jnp.float32)], [sent_in])
     across_in = (kept_in[:group] + wide(there_in[:group])).astype(narrow)
     total_in = kept_in[group:] + wide(there_in[group:]) + wide(swapped(across_in, "latent", 2))
 
-    sent_back, kept_back = [], []
-    for back, mine, theirs, _ in foreign:
-        codes = codes_of([(mine, 0, quarter), (theirs, 0, quarter)],
-                         [side * quarter, (1 - side) * quarter], 1, after)
-        sent, = products(codes, info_sent, [(0, both, 0, half, narrow)], across_in)
+    inside, outside = ((0, half),), ((half, half),)
+    after = across_in
+    sent_back, kept_back, parts = [], [], []
+    for back, mine, theirs, inner_rows in foreign:
+        codes = encode(
+            [(inner_rows, 0, half), (mine, 0, quarter), (theirs, 0, quarter)],
+            places(0, half + side * quarter, half + (1 - side) * quarter),
+            inv, enc_w, bias, 1, [after])
+        earlier = earlier_of(codes)
+        far_sent, near_sent, sent = products(
+            codes, earlier, info_sent,
+            [(0, group, inside, narrow), (group, group, inside, narrow), (0, both, outside, narrow)],
+            [])
+        far_in = swapped(far_sent, "latent", 1)
         sent_back.append(shifted(sent, "token", back))
-        kept, = products(codes, info_kept, [(0, both, 0, half, narrow)], sent)
-        kept_back.append(shifted(kept, "token", back))
+        near_in = swapped(near_sent, "latent", 1)
+        kept, kept_outer = products(
+            codes, earlier, info_kept,
+            [(0, both, inside, jnp.float32), (0, both, outside, narrow)], [sent, total_in])
+        kept_back.append(shifted(kept_outer, "token", back))
         after = kept
-
-    sent_out = (sent_out + sum(wide(part) for part in sent_back)).astype(narrow)
-    there_out = swapped(sent_out, "latent", 1)
+        parts.append((back, kept, far_in, near_in))
+
     returned = []
-    for back, _, _, rows_in in foreign:
-        codes = codes_of([(rows_in, 0, half)], [origin], 1, after)
-        far_sent, near_sent = products(
-            codes, info_sent, [(0, group, 0, half, narrow), (group, group, 0, half, narrow)], codes[0][0])
-        far_in = swapped(far_sent, "latent", 1)
-        near_in = swapped(near_sent, "latent", 1)
-        after = far_sent if returned else sent_out
-        kept, = products(codes, info_kept, [(0, both, 0, half, jnp.float32)], after)
+    for back, kept, far_in, near_in in parts:
         across = (kept[:group] + wide(far_in)).astype(narrow)
         part = finish(kept[group:] + wide(near_in) + wide(swapped(across, "latent", 2)))
         returned.append(shifted(part.astype(narrow), "token", back))
-        after = kept
-
-    kept_out = kept_out + sum(wide(part) for part in kept_back) + wide(there_out)
-    across_out = swapped(kept_out[:group].astype(narrow), "latent", 2)
-    total_out = finish(kept_out[group:] + wide(across_out))
+
+    sent_out = (sent_out + sum(wide(part) for part in sent_back)).astype(narrow)
+    far_out = swapped(sent_out[:group], "latent", 1)
+    near_out = swapped(sent_out[group:], "latent", 1)
+    kept_out = kept_out + sum(wide(part) for part in kept_back)
+    across_out = swapped((kept_out[:group] + wide(far_out)).astype(narrow), "latent", 2)
+    total_out = finish(kept_out[group:] + wide(near_out) + wide(across_out))
     total_in = finish(total_in) + sum(wide(part) for part in returned)
     total = jnp.concatenate([total_out[:quarter], total_in, total_out[quarter:]])
     total = total + wide(dec_bias)

time: 210 us -> 187 us (0.89)
  Pallas kernels: 66.8 us -> 54.5 us
  starting transfers between devices: 42.6 us -> 35.4 us
  waiting for transfers between devices: 83 us -> 77.3 us
    ppermute x4 -> x3, starting transfers between devices: 20 us -> 4.07 us  [earlier_of(): return [lax.ppermute(part, 'layer', [(0, 1)]) for part in codes]]
    ppermute x8 -> x9, waiting for transfers between devices: 59.8 us -> 47.5 us  [swapped(): return lax.ppermute(value, axis, [(i, i ^ bit) for i in range(n)])]
    pallas_call x6 -> x4, Pallas kernels: 36.9 us -> 27.2 us  [decode(): pl.pallas_call(body, in_specs=[pl.BlockSpec(memory_space=pltpu.SMEM)] + [...]
    ppermute x11, waiting for transfers between devices: 21.9 us -> 29.8 us  [shifted(): lax.ppermute(value, axis, [(i, (i + distance) % n) for i in range(n)])]
    ppermute x8 -> x9, starting transfers between devices: 7.96 us -> 15.6 us  [swapped(): return lax.ppermute(value, axis, [(i, i ^ bit) for i in range(n)])]
    pallas_call x3 -> x2, Pallas kernels: 27.6 us -> 24.1 us  [encode(): pl.pallas_call(body, in_specs=[pl.BlockSpec(memory_space=pltpu.SMEM), pl....]
  transfers between devices with their start and end apart: 23 -> 23, of which waited for: 12 -> 14; matrix products, arithmetic and copies ran while one was open for 2% -> 2% of each run, Pallas kernels for 31% -> 15%
where the time goes in v5:
time: 187 us; the launch traced here: 186 us
  waiting for transfers between devices  77.3 us (41%)
  Pallas kernels  54.5 us (29%)
  starting transfers between devices  35.4 us (19%)
  other arithmetic  8.64 us (5%)
  between operations  5.4 us (3%)
  local copies, waits for them, and re-layouts  4.96 us (3%)
    ppermute x9, waiting for transfers between devices, swapped(): return lax.ppermute(value, axis, [(i, i ^ bit) for i in range(n)])  47.5 us
    ppermute x11, waiting for transfers between devices, shifted(): lax.ppermute(value, axis, [(i, (i + distance) % n) for i in range(n)])  29.8 us
    pallas_call x4, Pallas kernels, decode(): pl.pallas_call(body, in_specs=[pl.BlockSpec(memory_space=pltpu.SMEM)] + [...  27.2 us
    pallas_call x2, Pallas kernels, encode(): pl.pallas_call(body, in_specs=[pl.BlockSpec(memory_space=pltpu.SMEM), pl....  24.1 us
    ppermute x11, starting transfers between devices, shifted(): lax.ppermute(value, axis, [(i, (i + distance) % n) for i in range(n)])  15.7 us
    ppermute x9, starting transfers between devices, swapped(): return lax.ppermute(value, axis, [(i, i ^ bit) for i in range(n)])  15.6 us
    unnamed x16, local copies, waits for them, and re-layouts  4.1 us
    ppermute x3, starting transfers between devices, earlier_of(): return [lax.ppermute(part, 'layer', [(0, 1)]) for part in codes]  4.07 us
  transfers between devices with their start and end apart: 23, of which 14 were waited for; matrix products, arithmetic and copies ran while one was open for 2% of the time, Pallas kernels for 15%

profile of v5, /device:TPU:0, one launch (start us, length us, event | category | flops | bytes accessed | tf_op | source)
XLA Modules:
  0.0 186.2 jit_solution(9180850742016664044)
XLA Ops:
  0.7 3.2 %prepare.1 = (bf16[96,4096]{1,0:T(8,128)(2,1)S(1)}, bf16[192,4096]{1,0:T(8,128)(2,1)S(1)}, f32[1]{0:T(128)}) custom-call(s32[1]{0:T(128)} %bitcast.3.side_ref, bf16[384,4096]{1,0:T(8,128)(2,1)} %bitcast.38), custom_call_target="tpu_custom_call" | custom-call | tf_op jit(solution)/shard_map/prepare/pallas_call | solution.py:55
  3.9 1.1 copy-done.4
  5.0 0.9 copy-done.5
  5.9 2.9 %collective-permute-start = (f32[1]{0:T(128)}, f32[1]{0:T(128)}, u32[]{:S(2)}, u32[]{:S(2)}) collective-permute-start(f32[1]{0:T(128)} %get-tuple-element.18), channel_id=1, source_target_pairs={{0,2},{2,0},{1,3},{3,1},{4,6},{6,4},{5,7},{7,5},{8,10},{10,8},{9,1... | collective-permute-start | bytes 20 | tf_op jit(solution)/shard_map/ppermute | solution.py:276
  8.8 1.7 collective-permute-done
  11.9 11.8 %encode.2 = (bf16[384,1024]{1,0:T(8,128)(2,1)S(1)}, bf16[384,1024]{1,0:T(8,128)(2,1)S(1)}) custom-call(s32[1]{0:T(128)} %constant.61.clone.1.places_ref, f32[1]{0:T(128)S(6)} %sqrt.3.inv_ref.after_ref, bf16[1,2048]{1,0:T(2,128)(2,1)S(1)} %constant_dynamic-slice_fusion.b_ref, bf16[384,4096]{1,0:T(8,128)(2,1)} %bitcast.39, bf16[4096,2048]{1,0:T(8,128)(2,1)} %bitcast.36), custom_call_target="tpu_custom_call" | custom-call | tf_op jit(solution)/shard_map/encode/pallas_call | solution.py:154
  23.7 1.3 collective-permute-start.1
  25.0 1.3 collective-permute-start.2
  26.4 2.1 %collective-permute-start.4 = (bf16[96,4096]{1,0:T(8,128)(2,1)}, bf16[96,4096]{1,0:T(8,128)(2,1)}, u32[]{:S(2)}, u32[]{:S(2)}) collective-permute-start(bf16[96,4096]{1,0:T(8,128)(2,1)} %get-tuple-element.26), channel_id=1, source_target_pairs={{0,2},{2,0},{1,3},{3,1},{4,6},{6,4},{5,7},{7,5},{8,10},{10,8},{9,1... | collective-permute-start | bytes 2359304 | tf_op jit(solution)/shard_map/ppermute | solution.py:276
  28.7 7.4 %decode.4 = (bf16[2,192,1024]{2,1,0:T(8,128)(2,1)}, f32[2,192,1024]{2,1,0:T(8,128)S(1)}) custom-call(s32[3]{0:T(128)S(1)} %pad_add_fusion.1.info_ref, bf16[384,1024]{1,0:T(8,128)(2,1)S(1)} %get-tuple-element.19.refs_0_, bf16[384,1024]{1,0:T(8,128)(2,1)S(1)} %get-tuple-element.20.refs_1_, bf16[384,1024]{1,0:T(8,128)(2,1)S(1)} %collective-permute-done.1.refs_2_, ...), custom_call_target="tpu_custom_call" | custom-call | tf_op jit(solution)/shard_map/decode/pallas_call | solution.py:253
  36.1 1.1 copy-done.2
  37.2 2.2 %collective-permute-start.6 = (bf16[2,192,1024]{2,1,0:T(8,128)(2,1)}, bf16[2,192,1024]{2,1,0:T(8,128)(2,1)}, u32[]{:S(2)}, u32[]{:S(2)}) collective-permute-start(bf16[2,192,1024]{2,1,0:T(8,128)(2,1)} %get-tuple-element.21.refs_6_), channel_id=1, source_target_pairs={{0,4},{4,0},{8,12},{12,8},{1,5},{5,1},{9,13},{13,9},{2,6},{6,2},{1... | collective-permute-start | bytes 2359304 | tf_op jit(solution)/shard_map/ppermute | solution.py:281
  39.4 7.8 %collective-permute-done.4.refs_1_ = bf16[96,4096]{1,0:T(8,128)(2,1)} collective-permute-done((bf16[96,4096]{1,0:T(8,128)(2,1)}, bf16[96,4096]{1,0:T(8,128)(2,1)}, u32[]{:S(2)}, u32[]{:S(2)}) %collective-permute-start.4) | collective-permute-done | bytes 786464 | tf_op jit(solution)/shard_map/ppermute | solution.py:276
  47.3 2.3 %collective-permute-start.5 = (bf16[96,4096]{1,0:T(8,128)(2,1)}, bf16[96,4096]{1,0:T(8,128)(2,1)}, u32[]{:S(2)}, u32[]{:S(2)}) collective-permute-start(bf16[96,4096]{1,0:T(8,128)(2,1)} %collective-permute-done.4.refs_1_), channel_id=1, source_target_pairs={{0,4},{4,0},{8,12},{12,8},{1,5},{5,1},{9,13},{13,9},{2,6},{6,2},{1... | collective-permute-start | bytes 2359304 | tf_op jit(solution)/shard_map/ppermute | solution.py:281
  49.7 6.6 %decode.5 = (f32[2,192,1024]{2,1,0:T(8,128)S(1)}, f32[2,192,1024]{2,1,0:T(8,128)S(1)}) custom-call(s32[3]{0:T(128)S(1)} %pad_add_fusion.info_ref, bf16[384,1024]{1,0:T(8,128)(2,1)S(1)} %get-tuple-element.19.refs_0_, bf16[384,1024]{1,0:T(8,128)(2,1)S(1)} %get-tuple-element.20.refs_1_, bf16[384,1024]{1,0:T(8,128)(2,1)S(1)} %collective-permute-done.1.refs_2_, ...), custom_call_target="tpu_custom_call" | custom-call | tf_op jit(solution)/shard_map/decode/pallas_call | solution.py:253
  56.3 1.1 add_convert_fusion.3.refs_4_
  57.4 14.2 %collective-permute-done.5.refs_2_ = bf16[96,4096]{1,0:T(8,128)(2,1)} collective-permute-done((bf16[96,4096]{1,0:T(8,128)(2,1)}, bf16[96,4096]{1,0:T(8,128)(2,1)}, u32[]{:S(2)}, u32[]{:S(2)}) %collective-permute-start.5) | collective-permute-done | bytes 786464 | tf_op jit(solution)/shard_map/ppermute | solution.py:281
  71.6 7.1 %collective-permute-done.3.refs_0_ = bf16[192,4096]{1,0:T(8,128)(2,1)} collective-permute-done((bf16[192,4096]{1,0:T(8,128)(2,1)}, bf16[192,4096]{1,0:T(8,128)(2,1)}, u32[]{:S(2)}, u32[]{:S(2)}) %collective-permute-start.3) | collective-permute-done | bytes 1572896 | tf_op jit(solution)/shard_map/ppermute | solution.py:276
  78.7 12.3 %encode.3.refs_0_ = bf16[384,2048]{1,0:T(8,128)(2,1)S(1)} custom-call(s32[3]{0:T(128)S(1)} %pad_add_fusion.2.places_ref, f32[1]{0:T(128)S(6)} %sqrt.3.inv_ref.after_ref, bf16[1,2048]{1,0:T(2,128)(2,1)S(1)} %constant_dynamic-slice_fusion.b_ref, bf16[192,4096]{1,0:T(8,128)(2,1)} %collective-permute-done.3.refs_0_, ...), custom_call_target="tpu_custom_call" | custom-call | tf_op jit(solution)/shard_map/encode/pallas_call | solution.py:154
  90.9 1.4 collective-permute-start.7
  92.3 2.9 %collective-permute-start.8 = (bf16[1,192,1024]{2,1,0:T(8,128)(2,1)S(1)}, bf16[1,192,1024]{2,1,0:T(8,128)(2,1)S(1)}, u32[]{:S(2)}, u32[]{:S(2)}) collective-permute-start(bf16[1,192,1024]{2,1,0:T(8,128)(2,1)S(1)} %add_convert_fusion.3.refs_4_), channel_id=1, source_target_pairs={{0,8},{4,12},{8,0},{12,4},{1,9},{5,13},{9,1},{13,5},{2,10},{6,14},... | collective-permute-start | bytes 1179656 | tf_op jit(solution)/shard_map/ppermute | solution.py:281
  95.2 6.5 %decode.6 = (bf16[1,192,1024]{2,1,0:T(8,128)(2,1)S(1)}, bf16[1,192,1024]{2,1,0:T(8,128)(2,1)S(1)}, bf16[2,192,1024]{2,1,0:T(8,128)(2,1)S(1)}) custom-call(s32[3]{0:T(128)S(1)} %pad_add_fusion.1.info_ref, bf16[384,2048]{1,0:T(8,128)(2,1)S(1)} %encode.3.refs_0_, bf16[384,2048]{1,0:T(8,128)(2,1)S(1)} %collective-permute-done.7.refs_1_, ...), custom_call_target="tpu_custom_call" | custom-call | tf_op jit(solution)/shard_map/decode/pallas_call | solution.py:253
  101.8 1.8 collective-permute-start.10
  103.6 1.8 collective-permute-start.15
  105.4 5.2 %collective-permute-done.8 = bf16[1,192,1024]{2,1,0:T(8,128)(2,1)S(1)} collective-permute-done((bf16[1,192,1024]{2,1,0:T(8,128)(2,1)S(1)}, bf16[1,192,1024]{2,1,0:T(8,128)(2,1)S(1)}, u32[]{:S(2)}, u32[]{:S(2)}) %collective-permute-start.8) | collective-permute-done | bytes 393248 | tf_op jit(solution)/shard_map/ppermute | solution.py:281
  110.5 1.2 convert_add_fusion.1.refs_5_
  111.7 0.6 collective-permute-start.14
  112.3 6.7 %decode.7 = (f32[2,192,1024]{2,1,0:T(8,128)S(1)}, bf16[2,192,1024]{2,1,0:T(8,128)(2,1)S(1)}) custom-call(s32[3]{0:T(128)S(1)} %pad_add_fusion.info_ref, bf16[384,2048]{1,0:T(8,128)(2,1)S(1)} %encode.3.refs_0_, bf16[384,2048]{1,0:T(8,128)(2,1)S(1)} %collective-permute-done.7.refs_1_, bf16[2048,4096]{1,0:T(8,128)(2,1)} %bitcast.35, ...), custom_call_target="tpu_custom_call" | custom-call | tf_op jit(solution)/shard_map/decode/pallas_call | solution.py:253
  119.1 1.6 collective-permute-start.9
  120.8 3.5 %collective-permute-start.16 = (bf16[1,192,1024]{2,1,0:T(8,128)(2,1)S(1)}, bf16[1,192,1024]{2,1,0:T(8,128)(2,1)S(1)}, u32[]{:S(2)}, u32[]{:S(2)}) collective-permute-start(bf16[1,192,1024]{2,1,0:T(8,128)(2,1)S(1)} %add_convert_fusion.2), channel_id=1, source_target_pairs={{0,8},{4,12},{8,0},{12,4},{1,9},{5,13},{9,1},{13,5},{2,10},{6,14},... | collective-permute-start | bytes 1179656 | tf_op jit(solution)/shard_map/ppermute | solution.py:281
  124.7 2.9 %collective-permute-done.14 = bf16[1,192,1024]{2,1,0:T(8,128)(2,1)S(1)} collective-permute-done((bf16[1,192,1024]{2,1,0:T(8,128)(2,1)S(1)}, bf16[1,192,1024]{2,1,0:T(8,128)(2,1)S(1)}, u32[]{:S(2)}, u32[]{:S(2)}) %collective-permute-start.14) | collective-permute-done | bytes 393248 | tf_op jit(solution)/shard_map/ppermute | solution.py:281
  127.6 14.6 %collective-permute-done.16 = bf16[1,192,1024]{2,1,0:T(8,128)(2,1)S(1)} collective-permute-done((bf16[1,192,1024]{2,1,0:T(8,128)(2,1)S(1)}, bf16[1,192,1024]{2,1,0:T(8,128)(2,1)S(1)}, u32[]{:S(2)}, u32[]{:S(2)}) %collective-permute-start.16) | collective-permute-done | bytes 393248 | tf_op jit(solution)/shard_map/ppermute | solution.py:281
  143.4 2.2 %collective-permute-start.13 = (bf16[1,192,1024]{2,1,0:T(8,128)(2,1)S(1)}, bf16[1,192,1024]{2,1,0:T(8,128)(2,1)S(1)}, u32[]{:S(2)}, u32[]{:S(2)}) collective-permute-start(bf16[1,192,1024]{2,1,0:T(8,128)(2,1)S(1)} %fusion.4), channel_id=1, source_target_pairs={{0,8},{4,12},{8,0},{12,4},{1,9},{5,13},{9,1},{13,5},{2,10},{6,14},... | collective-permute-start | bytes 1179656 | tf_op jit(solution)/shard_map/ppermute | solution.py:281
  145.6 8.3 %collective-permute-done.17 = bf16[192,1024]{1,0:T(8,128)(2,1)S(1)} collective-permute-done((bf16[192,1024]{1,0:T(8,128)(2,1)S(1)}, bf16[192,1024]{1,0:T(8,128)(2,1)S(1)}, u32[]{:S(2)}, u32[]{:S(2)}) %collective-permute-start.17) | collective-permute-done | bytes 393248 | tf_op jit(solution)/shard_map/ppermute | solution.py:276
  153.9 6.7 %collective-permute-done.11 = bf16[1,192,1024]{2,1,0:T(8,128)(2,1)S(1)} collective-permute-done((bf16[1,192,1024]{2,1,0:T(8,128)(2,1)S(1)}, bf16[1,192,1024]{2,1,0:T(8,128)(2,1)S(1)}, u32[]{:S(2)}, u32[]{:S(2)}) %collective-permute-start.11) | collective-permute-done | bytes 393248 | tf_op jit(solution)/shard_map/ppermute | solution.py:281
  160.6 3.9 %collective-permute-done.13 = bf16[1,192,1024]{2,1,0:T(8,128)(2,1)S(1)} collective-permute-done((bf16[1,192,1024]{2,1,0:T(8,128)(2,1)S(1)}, bf16[1,192,1024]{2,1,0:T(8,128)(2,1)S(1)}, u32[]{:S(2)}, u32[]{:S(2)}) %collective-permute-start.13) | collective-permute-done | bytes 393248 | tf_op jit(solution)/shard_map/ppermute | solution.py:281
  164.9 0.9 copy-done.6
  165.8 1.2 fusion.1
  167.0 1.4 maximum_bitcast_fusion
  168.4 0.9 collective-permute-start.18
  169.4 3.4 %collective-permute-start.19 = (f32[1,2]{1,0:T(1,128)S(1)}, f32[1,2]{1,0:T(1,128)S(1)}, u32[]{:S(2)}, u32[]{:S(2)}) collective-permute-start(f32[1,2]{1,0:T(1,128)S(1)} %maximum_bitcast_fusion), channel_id=1, source_target_pairs={{0,8},{4,12},{8,0},{12,4},{1,9},{5,13},{9,1},{13,5},{2,10},{6,14},... | collective-permute-start | bytes 32 | tf_op jit(solution)/shard_map/ppermute | solution.py:276
  172.7 1.0 fusion.3
  174.3 2.0 %collective-permute-done.20 = f32[1,2]{1,0:T(1,128)S(1)} collective-permute-done((f32[1,2]{1,0:T(1,128)S(1)}, f32[1,2]{1,0:T(1,128)S(1)}, u32[]{:S(2)}, u32[]{:S(2)}) %collective-permute-start.20) | collective-permute-done | bytes 40 | tf_op jit(solution)/shard_map/ppermute | solution.py:276
  176.3 1.4 add_add_fusion
  177.7 1.5 collective-permute-start.21
  179.2 2.1 %collective-permute-done.21 = f32[1,2]{1,0:T(1,128)S(1)} collective-permute-done((f32[1,2]{1,0:T(1,128)S(1)}, f32[1,2]{1,0:T(1,128)S(1)}, u32[]{:S(2)}, u32[]{:S(2)}) %collective-permute-start.21) | collective-permute-done | bytes 40 | tf_op jit(solution)/shard_map/ppermute | solution.py:276
  181.2 0.6 fusion.8
  183.2 0.9 collective-permute-start.22
  (44 shorter events, 3.2 us)
Async XLA Ops:
  0.6 8.2 %copy-start = (bf16[1,4096]{1,0:T(2,128)(2,1)S(1)}, bf16[1,4096]{1,0:T(2,128)(2,1)}, u32[]{:S(2)}) copy-start(bf16[1,4096]{1,0:T(2,128)(2,1)} %param.10) | copy-start | bytes 24580
  3.8 1.2 copy-start.4
  5.0 0.9 copy-start.5
  5.9 4.7 %collective-permute-start = (f32[1]{0:T(128)}, f32[1]{0:T(128)}, u32[]{:S(2)}, u32[]{:S(2)}) collective-permute-start(f32[1]{0:T(128)} %get-tuple-element.18), channel_id=1, source_target_pairs={{0,2},{2,0},{1,3},{3,1},{4,6},{6,4},{5,7},{7,5},{8,10},{10,8},{9,1... | collective-permute-start | bytes 20 | tf_op jit(solution)/shard_map/ppermute | solution.py:276
  23.7 5.0 %collective-permute-start.1 = (bf16[384,1024]{1,0:T(8,128)(2,1)S(1)}, bf16[384,1024]{1,0:T(8,128)(2,1)S(1)}, u32[]{:S(2)}, u32[]{:S(2)}) collective-permute-start(bf16[384,1024]{1,0:T(8,128)(2,1)S(1)} %get-tuple-element.19.refs_0_), channel_id=1, source_target_pairs={{0,1},{2,3},{4,5},{6,7},{8,9},{10,11},{12,13},{14,15},{16,17},{18,... | collective-permute-start | bytes 2359304 | tf_op jit(solution)/shard_map/ppermute | solution.py:344
  25.0 3.6 %collective-permute-start.2 = (bf16[384,1024]{1,0:T(8,128)(2,1)S(1)}, bf16[384,1024]{1,0:T(8,128)(2,1)S(1)}, u32[]{:S(2)}, u32[]{:S(2)}) collective-permute-start(bf16[384,1024]{1,0:T(8,128)(2,1)S(1)} %get-tuple-element.20.refs_1_), channel_id=1, source_target_pairs={{0,1},{2,3},{4,5},{6,7},{8,9},{10,11},{12,13},{14,15},{16,17},{18,... | collective-permute-start | bytes 2359304 | tf_op jit(solution)/shard_map/ppermute | solution.py:344
  26.4 20.9 %collective-permute-start.4 = (bf16[96,4096]{1,0:T(8,128)(2,1)}, bf16[96,4096]{1,0:T(8,128)(2,1)}, u32[]{:S(2)}, u32[]{:S(2)}) collective-permute-start(bf16[96,4096]{1,0:T(8,128)(2,1)} %get-tuple-element.26), channel_id=1, source_target_pairs={{0,2},{2,0},{1,3},{3,1},{4,6},{6,4},{5,7},{7,5},{8,10},{10,8},{9,1... | collective-permute-start | bytes 2359304 | tf_op jit(solution)/shard_map/ppermute | solution.py:276
  28.5 50.2 %collective-permute-start.3 = (bf16[192,4096]{1,0:T(8,128)(2,1)}, bf16[192,4096]{1,0:T(8,128)(2,1)}, u32[]{:S(2)}, u32[]{:S(2)}) collective-permute-start(bf16[192,4096]{1,0:T(8,128)(2,1)} %get-tuple-element.25), channel_id=1, source_target_pairs={{0,2},{2,0},{1,3},{3,1},{4,6},{6,4},{5,7},{7,5},{8,10},{10,8},{9,1... | collective-permute-start | bytes 4718600 | tf_op jit(solution)/shard_map/ppermute | solution.py:276
  36.1 1.1 copy-start.2
  37.2 19.1 %collective-permute-start.6 = (bf16[2,192,1024]{2,1,0:T(8,128)(2,1)}, bf16[2,192,1024]{2,1,0:T(8,128)(2,1)}, u32[]{:S(2)}, u32[]{:S(2)}) collective-permute-start(bf16[2,192,1024]{2,1,0:T(8,128)(2,1)} %get-tuple-element.21.refs_6_), channel_id=1, source_target_pairs={{0,4},{4,0},{8,12},{12,8},{1,5},{5,1},{9,13},{13,9},{2,6},{6,2},{1... | collective-permute-start | bytes 2359304 | tf_op jit(solution)/shard_map/ppermute | solution.py:281
  47.3 24.3 %collective-permute-start.5 = (bf16[96,4096]{1,0:T(8,128)(2,1)}, bf16[96,4096]{1,0:T(8,128)(2,1)}, u32[]{:S(2)}, u32[]{:S(2)}) collective-permute-start(bf16[96,4096]{1,0:T(8,128)(2,1)} %collective-permute-done.4.refs_1_), channel_id=1, source_target_pairs={{0,4},{4,0},{8,12},{12,8},{1,5},{5,1},{9,13},{13,9},{2,6},{6,2},{1... | collective-permute-start | bytes 2359304 | tf_op jit(solution)/shard_map/ppermute | solution.py:281
  90.9 4.3 %collective-permute-start.7 = (bf16[384,2048]{1,0:T(8,128)(2,1)S(1)}, bf16[384,2048]{1,0:T(8,128)(2,1)S(1)}, u32[]{:S(2)}, u32[]{:S(2)}) collective-permute-start(bf16[384,2048]{1,0:T(8,128)(2,1)S(1)} %encode.3.refs_0_), channel_id=1, source_target_pairs={{0,1},{2,3},{4,5},{6,7},{8,9},{10,11},{12,13},{14,15},{16,17},{18,... | collective-permute-start | bytes 4718600 | tf_op jit(solution)/shard_map/ppermute | solution.py:344
  92.3 18.2 %collective-permute-start.8 = (bf16[1,192,1024]{2,1,0:T(8,128)(2,1)S(1)}, bf16[1,192,1024]{2,1,0:T(8,128)(2,1)S(1)}, u32[]{:S(2)}, u32[]{:S(2)}) collective-permute-start(bf16[1,192,1024]{2,1,0:T(8,128)(2,1)S(1)} %add_convert_fusion.3.refs_4_), channel_id=1, source_target_pairs={{0,8},{4,12},{8,0},{12,4},{1,9},{5,13},{9,1},{13,5},{2,10},{6,14},... | collective-permute-start | bytes 1179656 | tf_op jit(solution)/shard_map/ppermute | solution.py:281
  101.8 22.5 %collective-permute-start.10 = (bf16[2,192,1024]{2,1,0:T(8,128)(2,1)S(1)}, bf16[2,192,1024]{2,1,0:T(8,128)(2,1)S(1)}, u32[]{:S(2)}, u32[]{:S(2)}) collective-permute-start(bf16[2,192,1024]{2,1,0:T(8,128)(2,1)S(1)} %get-tuple-element.28.refs_4_), channel_id=1, source_target_pairs={{0,2},{2,0},{1,3},{3,1},{4,6},{6,4},{5,7},{7,5},{8,10},{10,8},{9,1... | collective-permute-start | bytes 2359304 | tf_op jit(solution)/shard_map/ppermute | solution.py:276
  103.6 17.0 %collective-permute-start.15 = (bf16[1,192,1024]{2,1,0:T(8,128)(2,1)S(1)}, bf16[1,192,1024]{2,1,0:T(8,128)(2,1)S(1)}, u32[]{:S(2)}, u32[]{:S(2)}) collective-permute-start(bf16[1,192,1024]{2,1,0:T(8,128)(2,1)S(1)} %get-tuple-element.33), channel_id=1, source_target_pairs={{0,4},{4,0},{8,12},{12,8},{1,5},{5,1},{9,13},{13,9},{2,6},{6,2},{1... | collective-permute-start | bytes 1179656 | tf_op jit(solution)/shard_map/ppermute | solution.py:281
  111.7 15.9 %collective-permute-start.14 = (bf16[1,192,1024]{2,1,0:T(8,128)(2,1)S(1)}, bf16[1,192,1024]{2,1,0:T(8,128)(2,1)S(1)}, u32[]{:S(2)}, u32[]{:S(2)}) collective-permute-start(bf16[1,192,1024]{2,1,0:T(8,128)(2,1)S(1)} %get-tuple-element.32), channel_id=1, source_target_pairs={{0,4},{4,0},{8,12},{12,8},{1,5},{5,1},{9,13},{13,9},{2,6},{6,2},{1... | collective-permute-start | bytes 1179656 | tf_op jit(solution)/shard_map/ppermute | solution.py:281
  119.1 5.2 %copy-start.3 = (f32[2,192,1024]{2,1,0:T(8,128)S(1)}, f32[2,192,1024]{2,1,0:T(8,128)}, u32[]{:S(2)}) copy-start(f32[2,192,1024]{2,1,0:T(8,128)} %copy-done.2) | copy-start | bytes 4718596
  119.1 23.9 %collective-permute-start.9 = (bf16[2,192,1024]{2,1,0:T(8,128)(2,1)S(1)}, bf16[2,192,1024]{2,1,0:T(8,128)(2,1)S(1)}, u32[]{:S(2)}, u32[]{:S(2)}) collective-permute-start(bf16[2,192,1024]{2,1,0:T(8,128)(2,1)S(1)} %get-tuple-element.29), channel_id=1, source_target_pairs={{0,2},{2,0},{1,3},{3,1},{4,6},{6,4},{5,7},{7,5},{8,10},{10,8},{9,1... | collective-permute-start | bytes 2359304 | tf_op jit(solution)/shard_map/ppermute | solution.py:276
  120.8 21.5 %collective-permute-start.16 = (bf16[1,192,1024]{2,1,0:T(8,128)(2,1)S(1)}, bf16[1,192,1024]{2,1,0:T(8,128)(2,1)S(1)}, u32[]{:S(2)}, u32[]{:S(2)}) collective-permute-start(bf16[1,192,1024]{2,1,0:T(8,128)(2,1)S(1)} %add_convert_fusion.2), channel_id=1, source_target_pairs={{0,8},{4,12},{8,0},{12,4},{1,9},{5,13},{9,1},{13,5},{2,10},{6,14},... | collective-permute-start | bytes 1179656 | tf_op jit(solution)/shard_map/ppermute | solution.py:281
  124.6 18.6 %collective-permute-start.12 = (bf16[1,192,1024]{2,1,0:T(8,128)(2,1)S(1)}, bf16[1,192,1024]{2,1,0:T(8,128)(2,1)S(1)}, u32[]{:S(2)}, u32[]{:S(2)}) collective-permute-start(bf16[1,192,1024]{2,1,0:T(8,128)(2,1)S(1)} %get-tuple-element.41), channel_id=1, source_target_pairs={{0,4},{4,0},{8,12},{12,8},{1,5},{5,1},{9,13},{13,9},{2,6},{6,2},{1... | collective-permute-start | bytes 1179656 | tf_op jit(solution)/shard_map/ppermute | solution.py:281
  142.4 11.4 %collective-permute-start.17 = (bf16[192,1024]{1,0:T(8,128)(2,1)S(1)}, bf16[192,1024]{1,0:T(8,128)(2,1)S(1)}, u32[]{:S(2)}, u32[]{:S(2)}) collective-permute-start(bf16[192,1024]{1,0:T(8,128)(2,1)S(1)} %fusion.6), channel_id=1, source_target_pairs={{0,2},{2,0},{1,3},{3,1},{4,6},{6,4},{5,7},{7,5},{8,10},{10,8},{9,1... | collective-permute-start | bytes 1179656 | tf_op jit(solution)/shard_map/ppermute | solution.py:276
  143.0 17.6 %collective-permute-start.11 = (bf16[1,192,1024]{2,1,0:T(8,128)(2,1)S(1)}, bf16[1,192,1024]{2,1,0:T(8,128)(2,1)S(1)}, u32[]{:S(2)}, u32[]{:S(2)}) collective-permute-start(bf16[1,192,1024]{2,1,0:T(8,128)(2,1)S(1)} %get-tuple-element.40), channel_id=1, source_target_pairs={{0,4},{4,0},{8,12},{12,8},{1,5},{5,1},{9,13},{13,9},{2,6},{6,2},{1... | collective-permute-start | bytes 1179656 | tf_op jit(solution)/shard_map/ppermute | solution.py:281
  143.2 2.3 %copy-start.7 = (bf16[1,1024]{1,0:T(2,128)(2,1)S(1)}, bf16[1,1024]{1,0:T(2,128)(2,1)}, u32[]{:S(2)}) copy-start(bf16[1,1024]{1,0:T(2,128)(2,1)} %param.13) | copy-start | bytes 6148
  143.4 21.2 %collective-permute-start.13 = (bf16[1,192,1024]{2,1,0:T(8,128)(2,1)S(1)}, bf16[1,192,1024]{2,1,0:T(8,128)(2,1)S(1)}, u32[]{:S(2)}, u32[]{:S(2)}) collective-permute-start(bf16[1,192,1024]{2,1,0:T(8,128)(2,1)S(1)} %fusion.4), channel_id=1, source_target_pairs={{0,8},{4,12},{8,0},{12,4},{1,9},{5,13},{9,1},{13,5},{2,10},{6,14},... | collective-permute-start | bytes 1179656 | tf_op jit(solution)/shard_map/ppermute | solution.py:281
  164.7 1.1 copy-start.6
  165.8 19.2 %copy-start.1 = (bf16[1,4096]{1,0:T(2,128)(2,1)S(1)}, bf16[1,4096]{1,0:T(2,128)(2,1)}, u32[]{:S(2)}) copy-start(bf16[1,4096]{1,0:T(2,128)(2,1)} %param.10) | copy-start | bytes 24580
  168.4 5.4 %collective-permute-start.18 = (f32[1,2]{1,0:T(1,128)S(1)}, f32[1,2]{1,0:T(1,128)S(1)}, u32[]{:S(2)}, u32[]{:S(2)}) collective-permute-start(f32[1,2]{1,0:T(1,128)S(1)} %maximum_bitcast_fusion), channel_id=1, source_target_pairs={{0,4},{4,8},{8,12},{12,0},{1,5},{5,9},{9,13},{13,1},{2,6},{6,10},{... | collective-permute-start | bytes 32 | tf_op jit(solution)/shard_map/ppermute | solution.py:276
  169.4 4.9 %collective-permute-start.19 = (f32[1,2]{1,0:T(1,128)S(1)}, f32[1,2]{1,0:T(1,128)S(1)}, u32[]{:S(2)}, u32[]{:S(2)}) collective-permute-start(f32[1,2]{1,0:T(1,128)S(1)} %maximum_bitcast_fusion), channel_id=1, source_target_pairs={{0,8},{4,12},{8,0},{12,4},{1,9},{5,13},{9,1},{13,5},{2,10},{6,14},... | collective-permute-start | bytes 32 | tf_op jit(solution)/shard_map/ppermute | solution.py:276
  172.7 3.5 %collective-permute-start.20 = (f32[1,2]{1,0:T(1,128)S(1)}, f32[1,2]{1,0:T(1,128)S(1)}, u32[]{:S(2)}, u32[]{:S(2)}) collective-permute-start(f32[1,2]{1,0:T(1,128)S(1)} %maximum_bitcast_fusion), channel_id=1, source_target_pairs={{0,12},{4,0},{8,4},{12,8},{1,13},{5,1},{9,5},{13,9},{2,14},{6,2},{... | collective-permute-start | bytes 32 | tf_op jit(solution)/shard_map/ppermute | solution.py:276
  177.7 3.5 %collective-permute-start.21 = (f32[1,2]{1,0:T(1,128)S(1)}, f32[1,2]{1,0:T(1,128)S(1)}, u32[]{:S(2)}, u32[]{:S(2)}) collective-permute-start(f32[1,2]{1,0:T(1,128)S(1)} %add_add_fusion), channel_id=1, source_target_pairs={{0,2},{2,0},{1,3},{3,1},{4,6},{6,4},{5,7},{7,5},{8,10},{10,8},{9,1... | collective-permute-start | bytes 32 | tf_op jit(solution)/shard_map/ppermute | solution.py:276
  183.2 1.2 collective-permute-start.22

commit v6 on v5

--- a/solution.py
+++ b/solution.py
@@ -6,8 +6,8 @@
 from jax.sharding import PartitionSpec as P
 
 VMEM_LIMIT = 40 * 1024 * 1024
-SLOTS = 3
-TILE = 512
+SLOTS = 6
+TILE = 256
 COST = pl.CostEstimate(flops=0, bytes_accessed=0, transcendentals=0)
 
 
@@ -18,36 +18,38 @@
     return tile
 
 
-def prepare(x, side):
+def prepare(x, side, edge):
     rows, width = x.shape
-    quarter = rows // 4
+    middle = rows - 2 * edge
     lanes = tile_of(width, 1024)
+    loads = 4
+    piece = rows // loads
 
     def body(side_ref, x_ref, outer_ref, inner_ref, o_ref, held, sem, out_sem):
         def load(i):
-            place = pl.ds(i * quarter, quarter)
+            place = pl.ds(i * piece, piece)
             return pltpu.make_async_copy(x_ref.at[place], held.at[place], sem.at[i])
 
-        first = pl.ds(pl.multiple_of(side_ref[0] * (3 * quarter), 16), quarter)
+        first = pl.ds(pl.multiple_of(side_ref[0] * (rows - edge), 16), edge)
         cuts = [
             pltpu.make_async_copy(x_ref.at[first], outer_ref, out_sem.at[0]),
-            pltpu.make_async_copy(x_ref.at[pl.ds(quarter, 2 * quarter)], inner_ref, out_sem.at[1]),
+            pltpu.make_async_copy(x_ref.at[pl.ds(edge, middle)], inner_ref, out_sem.at[1]),
         ]
-        for i in range(4):
+        for i in range(loads):
             load(i).start()
         for copy in cuts:
             copy.start()
         total = jnp.zeros((8, lanes), jnp.float32)
-        for i in range(4):
+        for i in range(loads):
             load(i).wait()
             for c in range(width // lanes):
                 def add(r, acc):
-                    here = pl.ds(pl.multiple_of(i * quarter + r * 16, 16), 16)
+                    here = pl.ds(pl.multiple_of(i * piece + r * 16, 16), 16)
                     value = held[here, c * lanes:(c + 1) * lanes].astype(jnp.float32)
                     value = value * value
                     return acc + value[:8] + value[8:]
 
-                total = lax.fori_loop(0, quarter // 16, add, total)
+                total = lax.fori_loop(0, piece // 16, add, total, unroll=2)
         o_ref[0] = jnp.sum(total)
         for copy in cuts:
             copy.wait()
@@ -57,13 +59,13 @@
         in_specs=[pl.BlockSpec(memory_space=pltpu.SMEM), pl.BlockSpec(memory_space=pl.ANY)],
         out_specs=[pl.BlockSpec(memory_space=pl.ANY)] * 2 + [pl.BlockSpec(memory_space=pltpu.SMEM)],
         out_shape=[
-            jax.ShapeDtypeStruct((quarter, width), x.dtype),
-            jax.ShapeDtypeStruct((2 * quarter, width), x.dtype),
+            pltpu.HBM((edge, width), x.dtype),
+            pltpu.HBM((middle, width), x.dtype),
             jax.ShapeDtypeStruct((1,), jnp.float32),
         ],
         scratch_shapes=[
             pltpu.VMEM((rows, width), x.dtype),
-            pltpu.SemaphoreType.DMA((4,)),
+            pltpu.SemaphoreType.DMA((loads,)),
             pltpu.SemaphoreType.DMA((2,)),
         ],
         compiler_params=pltpu.CompilerParams(vmem_limit_bytes=VMEM_LIMIT),
@@ -82,11 +84,11 @@
         body,
         in_specs=[pl.BlockSpec(memory_space=pltpu.SMEM)] + [pl.BlockSpec(memory_space=pl.ANY)] * n,
         out_specs=[pl.BlockSpec(memory_space=pl.ANY)] * n,
-        out_shape=[jax.ShapeDtypeStruct(value.shape, value.dtype) for value in values],
+        out_shape=[pltpu.HBM(value.shape, value.dtype) for value in values],
         input_output_aliases={1 + i: i for i in range(n)},
         cost_estimate=COST,
         name="gate",
-    )(after, *values)
+    )(after, *[in_hbm(value) for value in values])
 
 
 def ring_loop(count, start, step):
@@ -271,6 +273,53 @@
     )(info, *codes, *earlier, own_w, cross_w, *also)
 
 
+def finale(outer_terms, inner_terms, bias, target, layer):
+    rows, width = target.shape
+    half, quarter = rows // 2, rows // 4
+    n, m = len(outer_terms), len(inner_terms)
+
+    def body(layer_ref, b_ref, t_ref, *refs):
+        terms = {0: refs[:n], 1: refs[n:n + m]}
+        r_ref, s_ref = refs[n + m:]
+        bias = b_ref[...].astype(jnp.float32)
+        spans = [(0, 0, 0, quarter), (1, 0, quarter, half), (0, quarter, 3 * quarter, quarter)]
+
+        def block(which, start, target_start):
+            def run(r, sums):
+                here = pl.ds(pl.multiple_of(start + r * 16, 16), 16)
+                there = pl.ds(pl.multiple_of(target_start + r * 16, 16), 16)
+                total = sum(term[here, :].astype(jnp.float32) for term in terms[which]) + bias
+                goal = t_ref[there, :].astype(jnp.float32)
+                r_ref[there, :] = total.astype(r_ref.dtype)
+                diff = total - goal
+                diff, goal = diff * diff, goal * goal
+                return sums[0] + diff[:8] + diff[8:], sums[1] + goal[:8] + goal[8:]
+
+            return run
+
+        zero = jnp.zeros((8, width), jnp.float32)
+        sums = (zero, zero)
+        for which, start, target_start, count in spans:
+            sums = lax.fori_loop(0, count // 16, block(which, start, target_start), sums)
+        lane = lax.broadcasted_iota(jnp.int32, (8, 128), 1)
+        value = jnp.where(lane == layer_ref[0], jnp.sum(sums[0]), 0.0)
+        s_ref[...] = jnp.where(lane == layer_ref[0] + 2, jnp.sum(sums[1]), value)
+
+    vmem = pl.BlockSpec(memory_space=pltpu.VMEM)
+    return pl.pallas_call(
+        body,
+        in_specs=[pl.BlockSpec(memory_space=pltpu.SMEM)] + [vmem] * (2 + n + m),
+        out_specs=[vmem] * 2,
+        out_shape=[
+            jax.ShapeDtypeStruct((rows, width), jnp.bfloat16),
+            jax.ShapeDtypeStruct((8, 128), jnp.float32),
+        ],
+        compiler_params=pltpu.CompilerParams(vmem_limit_bytes=VMEM_LIMIT),
+        cost_estimate=COST,
+        name="finale",
+    )(layer.astype(jnp.int32).reshape(1), bias, target, *outer_terms, *inner_terms)
+
+
 def shifted(value, axis, distance):
     n = lax.axis_size(axis)
     return lax.ppermute(value, axis, [(i, (i + distance) % n) for i in range(n)])
@@ -311,7 +360,8 @@
     quarter = rows // 4
     side = lat % 2
 
-    outer, inner, square = prepare(x_own, side.astype(jnp.int32))
+    edge = rows * 7 // 24 // 16 * 16
+    outer, inner, square = prepare(x_own, side.astype(jnp.int32), edge)
     square = sum_over(square, "token")
     scale = jnp.sqrt(square / (rows * n_tok * model) + 1e-06)
     inv = 1.0 / scale
@@ -329,12 +379,11 @@
     group = n_lat // 4
     other, mine_bit = 1 - lat % 2, lat % 2
     far, near = 1 - (lat // 2) % 2, (lat // 2) % 2
-    info_sent = jnp.stack(
-        [layer] + [4 * i + 2 * b + other for b in (far, near) for i in range(group)]
-    ).astype(jnp.int32)
-    info_kept = jnp.stack(
-        [layer] + [4 * i + 2 * b + mine_bit for b in (far, near) for i in range(group)]
-    ).astype(jnp.int32)
+
+    def info(low, highs):
+        blocks = [4 * i + 2 * high + low for high in highs for i in range(group)]
+        return jnp.stack([layer] + blocks).astype(jnp.int32)
+
 
     half = 2 * quarter
     both = 2 * group
@@ -364,62 +413,67 @@
     earlier = earlier_of(codes)
     inside = ((quarter, half),)
     outside = ((0, quarter), (3 * quarter, quarter))
-    sent_in, sent_out = products(
-        codes, earlier, info_sent, [(0, both, inside, narrow), (0, both, outside, jnp.float32)], [])
-    there_in = swapped(sent_in, "latent", 1)
-    kept_in, kept_out = products(
-        codes, earlier, info_kept,
-        [(0, both, inside, jnp.float32), (0, both, outside, jnp.float32)], [sent_in])
-    across_in = (kept_in[:group] + wide(there_in[:group])).astype(narrow)
-    total_in = kept_in[group:] + wide(there_in[group:]) + wide(swapped(across_in, "latent", 2))
-
-    inside, outside = ((0, half),), ((half, half),)
+    spans = [(0, group, inside), (group, group, inside), (0, group, outside), (group, group, outside)]
+    far_sent, near_sent, far_out_sent, near_out_sent = products(
+        codes, earlier, info(other, (far, near)),
+        [span + (dtype,) for span, dtype in zip(spans, (narrow, narrow, jnp.float32, jnp.float32))], [])
+    far_in = swapped(far_sent, "latent", 1)
+    near_in = swapped(near_sent, "latent", 1)
+    far_kept, near_kept, far_out_kept, near_out_kept = products(
+        codes, earlier, info(mine_bit, (far, near)), [span + (jnp.float32,) for span in spans], [far_sent])
+    across_in = (far_kept + wide(far_in)).astype(narrow)
+    total_in = near_kept + wide(near_in) + wide(swapped(across_in, "latent", 2))
+
     after = across_in
-    sent_back, kept_back, parts = [], [], []
+    returned = []
+    far_out_back, far_out_kept_back, near_out_back, near_out_kept_back = [], [], [], []
+
     for back, mine, theirs, inner_rows in foreign:
         codes = encode(
-            [(inner_rows, 0, half), (mine, 0, quarter), (theirs, 0, quarter)],
-            places(0, half + side * quarter, half + (1 - side) * quarter),
+            [(mine, 0, edge), (theirs, 0, edge), (inner_rows, 0, rows - 2 * edge)],
+            places(side * (rows - edge), (1 - side) * (rows - edge), edge),
             inv, enc_w, bias, 1, [after])
         earlier = earlier_of(codes)
-        far_sent, near_sent, sent = products(
-            codes, earlier, info_sent,
-            [(0, group, inside, narrow), (group, group, inside, narrow), (0, both, outside, narrow)],
-            [])
+
+        def quarter_of(low, high, spans, dtype, also):
+            *insides, outer = products(
+                codes, earlier, info(low, (high,)),
+                [(0, group, span, dtype) for span in spans] + [(0, group, outside, narrow)], also)
+            return insides, shifted(outer, "token", back)
+
+        (far_sent,), far_back = quarter_of(other, far, [inside], narrow, [])
         far_in = swapped(far_sent, "latent", 1)
-        sent_back.append(shifted(sent, "token", back))
-        near_in = swapped(near_sent, "latent", 1)
-        kept, kept_outer = products(
-            codes, earlier, info_kept,
-            [(0, both, inside, jnp.float32), (0, both, outside, narrow)], [sent, total_in])
-        kept_back.append(shifted(kept_outer, "token", back))
-        after = kept
-        parts.append((back, kept, far_in, near_in))
-
-    returned = []
-    for back, kept, far_in, near_in in parts:
-        across = (kept[:group] + wide(far_in)).astype(narrow)
-        part = finish(kept[group:] + wide(near_in) + wide(swapped(across, "latent", 2)))
+        (far_kept,), far_kept_back = quarter_of(mine_bit, far, [inside], jnp.float32, [far_sent, total_in])
+        across = (far_kept + wide(far_in)).astype(narrow)
+        halves = [((quarter, quarter),), ((2 * quarter, quarter),)]
+        near_sent, near_back = quarter_of(other, near, halves, narrow, [across])
+        near_in = jnp.concatenate([swapped(part, "latent", 1) for part in near_sent], axis=1)
+        (near_kept,), near_kept_back = quarter_of(mine_bit, near, [inside], jnp.float32, near_sent)
+        part = finish(near_kept + wide(near_in) + wide(swapped(across, "latent", 2)))
         returned.append(shifted(part.astype(narrow), "token", back))
-
-    sent_out = (sent_out + sum(wide(part) for part in sent_back)).astype(narrow)
-    far_out = swapped(sent_out[:group], "latent", 1)
-    near_out = swapped(sent_out[group:], "latent", 1)
-    kept_out = kept_out + sum(wide(part) for part in kept_back)
-    across_out = swapped((kept_out[:group] + wide(far_out)).astype(narrow), "latent", 2)
-    total_out = finish(kept_out[group:] + wide(near_out) + wide(across_out))
-    total_in = finish(total_in) + sum(wide(part) for part in returned)
-    total = jnp.concatenate([total_out[:quarter], total_in, total_out[quarter:]])
-    total = total + wide(dec_bias)
-    recon = total.astype(jnp.bfloat16)[None]
-
-    target = wide(targets[0])
-    diff = total - target
-    sums = jnp.stack([jnp.sum(diff * diff), jnp.sum(target * target)]).reshape(1, 2)
-    sums = sum_over(sum_over(sums, "latent"), "token")
-    ratio = sums[:, 0] / sums[:, 1]
-    loss = sum_over(ratio, "layer") / 2.0
-    return (recon, loss)
+        far_out_back.append(far_back)
+        far_out_kept_back.append(far_kept_back)
+        near_out_back.append(near_back)
+        near_out_kept_back.append(near_kept_back)
+        after = near_kept
+
+    def joined(own, back):
+        return own + sum(wide(part) for part in back)
+
+    far_out = swapped(joined(far_out_sent, far_out_back).astype(narrow), "latent", 1)
+    near_out = swapped(joined(near_out_sent, near_out_back).astype(narrow), "latent", 1)
+    across_out = (joined(far_out_kept, far_out_kept_back) + wide(far_out)).astype(narrow)
+    across_out = swapped(across_out, "latent", 2)
+    if group == 1:
+        outer_terms = [near_out_kept, *near_out_kept_back, near_out, across_out]
+        outer_terms = [term[0] for term in outer_terms]
+    else:
+        outer_terms = [finish(joined(near_out_kept, near_out_kept_back) + wide(near_out) + wide(across_out))]
+    recon, sums = finale(outer_terms, [finish(total_in), *returned], dec_bias, targets[0], layer)
+
+    sums = sum_over(sum_over(sums, ("token", "layer")), "latent")
+    loss = (sums[:1, 0] / sums[:1, 2] + sums[:1, 1] / sums[:1, 3]) / 2.0
+    return (recon[None], loss)
 
 
 def solution(mesh):

time: 187 us -> 238 us (1.27)
  Pallas kernels: 54.5 us -> 130 us
  waiting for transfers between devices: 77.3 us -> 56.4 us
  other arithmetic: 8.64 us -> 2.25 us
  starting transfers between devices: 35.4 us -> 39.4 us
    pallas_call x1, Pallas kernels: 3.18 us -> 69.2 us  [prepare(): pl.pallas_call(body, in_specs=[pl.BlockSpec(memory_space=pltpu.SMEM), pl....]
    ppermute x9 -> x11, waiting for transfers between devices: 47.5 us -> 34.4 us  [swapped(): return lax.ppermute(value, axis, [(i, i ^ bit) for i in range(n)])]
    ppermute x11 -> x14, waiting for transfers between devices: 29.8 us -> 21.9 us  [shifted(): lax.ppermute(value, axis, [(i, (i + distance) % n) for i in range(n)])]
    pallas_call x4 -> x6, Pallas kernels: 27.2 us -> 32.3 us  [decode(): pl.pallas_call(body, in_specs=[pl.BlockSpec(memory_space=pltpu.SMEM)] + [...]
    ppermute x11 -> x14, starting transfers between devices: 15.7 us -> 18.7 us  [shifted(): lax.ppermute(value, axis, [(i, (i + distance) % n) for i in range(n)])]
    pallas_call x2, Pallas kernels: 24.1 us -> 27 us  [encode(): pl.pallas_call(body, in_specs=[pl.BlockSpec(memory_space=pltpu.SMEM), pl....]
    ppermute x9 -> x11, starting transfers between devices: 15.6 us -> 16.6 us  [swapped(): return lax.ppermute(value, axis, [(i, i ^ bit) for i in range(n)])]
  transfers between devices with their start and end apart: 23 -> 28, of which waited for: 14 -> 17; matrix products, arithmetic and copies ran while one was open for 2% -> 1% of each run, Pallas kernels for 15% -> 19%
where the time goes in v6:
time: 238 us; the launch traced here: 237 us
  Pallas kernels  130 us (55%)
  waiting for transfers between devices  56.4 us (24%)
  starting transfers between devices  39.4 us (17%)
  between operations  5.97 us (3%)
  local copies, waits for them, and re-layouts  3.23 us (1%)
    pallas_call x1, Pallas kernels, prepare(): pl.pallas_call(body, in_specs=[pl.BlockSpec(memory_space=pltpu.SMEM), pl....  69.2 us
    ppermute x11, waiting for transfers between devices, swapped(): return lax.ppermute(value, axis, [(i, i ^ bit) for i in range(n)])  34.4 us
    pallas_call x6, Pallas kernels, decode(): pl.pallas_call(body, in_specs=[pl.BlockSpec(memory_space=pltpu.SMEM)] + [...  32.3 us
    pallas_call x2, Pallas kernels, encode(): pl.pallas_call(body, in_specs=[pl.BlockSpec(memory_space=pltpu.SMEM), pl....  27 us
    ppermute x14, waiting for transfers between devices, shifted(): lax.ppermute(value, axis, [(i, (i + distance) % n) for i in range(n)])  21.9 us
    ppermute x14, starting transfers between devices, shifted(): lax.ppermute(value, axis, [(i, (i + distance) % n) for i in range(n)])  18.7 us
    ppermute x11, starting transfers between devices, swapped(): return lax.ppermute(value, axis, [(i, i ^ bit) for i in range(n)])  16.6 us
  transfers between devices with their start and end apart: 28, of which 17 were waited for; matrix products, arithmetic and copies ran while one was open for 1% of the time, Pallas kernels for 19%

profile of v6, /device:TPU:0, one launch (start us, length us, event | category | flops | bytes accessed | tf_op | source)
XLA Modules:
  0.0 237.4 jit_solution(18418680860212988753)
XLA Ops:
  0.7 69.2 %prepare.1 = (bf16[112,4096]{1,0:T(8,128)(2,1)}, bf16[160,4096]{1,0:T(8,128)(2,1)}, f32[1]{0:T(128)}) custom-call(s32[1]{0:T(128)} %bitcast.4.side_ref, bf16[384,4096]{1,0:T(8,128)(2,1)} %bitcast.35), custom_call_target="tpu_custom_call" | custom-call | tf_op jit(solution)/shard_map/prepare/pallas_call | solution.py:57
  69.8 3.0 %collective-permute-start = (f32[1]{0:T(128)}, f32[1]{0:T(128)}, u32[]{:S(2)}, u32[]{:S(2)}) collective-permute-start(f32[1]{0:T(128)} %get-tuple-element.28), channel_id=1, source_target_pairs={{0,2},{2,0},{1,3},{3,1},{4,6},{6,4},{5,7},{7,5},{8,10},{10,8},{9,1... | collective-permute-start | bytes 20 | tf_op jit(solution)/shard_map/ppermute | solution.py:325
  72.9 1.6 collective-permute-done
  75.8 2.1 collective-permute-start.3
  77.9 13.3 %encode.2 = (bf16[384,1024]{1,0:T(8,128)(2,1)S(1)}, bf16[384,1024]{1,0:T(8,128)(2,1)S(1)}) custom-call(s32[1]{0:T(128)} %constant.61.clone.1.places_ref, f32[1]{0:T(128)S(6)} %sqrt.3.inv_ref.after_ref, bf16[1,2048]{1,0:T(2,128)(2,1)S(1)} %constant_dynamic-slice_fusion.b_ref, bf16[384,4096]{1,0:T(8,128)(2,1)} %bitcast.36, bf16[4096,2048]{1,0:T(8,128)(2,1)} %bitcast.33), custom_call_target="tpu_custom_call" | custom-call | tf_op jit(solution)/shard_map/encode/pallas_call | solution.py:156
  91.2 1.3 collective-permute-start.1
  92.5 1.3 collective-permute-start.2
  94.0 5.5 %collective-permute-done.3.refs_0_ = bf16[112,4096]{1,0:T(8,128)(2,1)} collective-permute-done((bf16[112,4096]{1,0:T(8,128)(2,1)}, bf16[112,4096]{1,0:T(8,128)(2,1)}, u32[]{:S(2)}, u32[]{:S(2)}) %collective-permute-start.3) | collective-permute-done | bytes 917536 | tf_op jit(solution)/shard_map/ppermute | solution.py:325
  99.5 2.1 collective-permute-start.4
  101.7 7.1 %decode.6 = (bf16[1,192,1024]{2,1,0:T(8,128)(2,1)S(1)}, bf16[1,192,1024]{2,1,0:T(8,128)(2,1)S(1)}, f32[1,192,1024]{2,1,0:T(8,128)S(1)}, f32[1,192,1024]{2,1,0:T(8,128)S(1)}) custom-call(s32[3]{0:T(128)S(1)} %get-tuple-element.59.info_ref, bf16[384,1024]{1,0:T(8,128)(2,1)S(1)} %get-tuple-element.29.refs_0_, bf16[384,1024]{1,0:T(8,128)(2,1)S(1)} %get-tuple-element.30.refs_1_, ...), custom_call_target="tpu_custom_call" | custom-call | tf_op jit(solution)/shard_map/decode/pallas_call | solution.py:255
  109.6 0.9 copy-done.5
  111.4 7.1 %decode.7 = (f32[1,192,1024]{2,1,0:T(8,128)S(1)}, f32[1,192,1024]{2,1,0:T(8,128)S(1)}, f32[1,192,1024]{2,1,0:T(8,128)S(1)}, f32[1,192,1024]{2,1,0:T(8,128)S(1)}) custom-call(s32[3]{0:T(128)S(1)} %get-tuple-element.58.info_ref, bf16[384,1024]{1,0:T(8,128)(2,1)S(1)} %get-tuple-element.29.refs_0_, bf16[384,1024]{1,0:T(8,128)(2,1)S(1)} %get-tuple-element.30.refs_1_, ...), custom_call_target="tpu_custom_call" | custom-call | tf_op jit(solution)/shard_map/decode/pallas_call | solution.py:255
  118.4 8.3 %collective-permute-done.6 = bf16[1,192,1024]{2,1,0:T(8,128)(2,1)} collective-permute-done((bf16[1,192,1024]{2,1,0:T(8,128)(2,1)S(1)}, bf16[1,192,1024]{2,1,0:T(8,128)(2,1)}, u32[]{:S(2)}, u32[]{:S(2)}) %collective-permute-start.6) | collective-permute-done | bytes 393248 | tf_op jit(solution)/shard_map/ppermute | solution.py:330
  126.7 1.1 add_convert_fusion.5.refs_4_
  127.9 13.7 %encode.3.refs_0_ = bf16[384,2048]{1,0:T(8,128)(2,1)S(1)} custom-call(s32[3]{0:T(128)S(1)} %pad_add_fusion.3.places_ref, f32[1]{0:T(128)S(6)} %sqrt.3.inv_ref.after_ref, bf16[1,2048]{1,0:T(2,128)(2,1)S(1)} %constant_dynamic-slice_fusion.b_ref, bf16[112,4096]{1,0:T(8,128)(2,1)} %collective-permute-done.3.refs_0_, ...), custom_call_target="tpu_custom_call" | custom-call | tf_op jit(solution)/shard_map/encode/pallas_call | solution.py:156
  141.6 1.4 collective-permute-start.7
  143.0 1.6 collective-permute-start.8
  144.6 2.6 %collective-permute-start.9 = (bf16[1,192,1024]{2,1,0:T(8,128)(2,1)S(1)}, bf16[1,192,1024]{2,1,0:T(8,128)(2,1)S(1)}, u32[]{:S(2)}, u32[]{:S(2)}) collective-permute-start(bf16[1,192,1024]{2,1,0:T(8,128)(2,1)S(1)} %add_convert_fusion.5.refs_4_), channel_id=1, source_target_pairs={{0,8},{4,12},{8,0},{12,4},{1,9},{5,13},{9,1},{13,5},{2,10},{6,14},... | collective-permute-start | bytes 1179656 | tf_op jit(solution)/shard_map/ppermute | solution.py:330
  147.4 4.5 %decode.8 = (bf16[1,192,1024]{2,1,0:T(8,128)(2,1)S(1)}, bf16[1,192,1024]{2,1,0:T(8,128)(2,1)S(1)}) custom-call(s32[2]{0:T(128)S(1)} %get-tuple-element.61.info_ref, bf16[384,2048]{1,0:T(8,128)(2,1)S(1)} %encode.3.refs_0_, bf16[384,2048]{1,0:T(8,128)(2,1)S(1)} %collective-permute-done.7.refs_1_, bf16[2048,4096]{1,0:T(8,128)(2,1)} %bitcast.29, ...), custom_call_target="tpu_custom_call" | custom-call | tf_op jit(solution)/shard_map/decode/pallas_call | solution.py:255
  152.5 1.5 collective-permute-start.15
  154.0 6.3 %collective-permute-done.8 = bf16[1,192,1024]{2,1,0:T(8,128)(2,1)S(1)} collective-permute-done((bf16[1,192,1024]{2,1,0:T(8,128)(2,1)S(1)}, bf16[1,192,1024]{2,1,0:T(8,128)(2,1)S(1)}, u32[]{:S(2)}, u32[]{:S(2)}) %collective-permute-start.8) | collective-permute-done | bytes 393248 | tf_op jit(solution)/shard_map/ppermute | solution.py:330
  160.5 4.5 %decode.9 = (f32[1,192,1024]{2,1,0:T(8,128)S(1)}, bf16[1,192,1024]{2,1,0:T(8,128)(2,1)S(1)}) custom-call(s32[2]{0:T(128)S(1)} %pad_add_fusion.5.info_ref, bf16[384,2048]{1,0:T(8,128)(2,1)S(1)} %encode.3.refs_0_, bf16[384,2048]{1,0:T(8,128)(2,1)S(1)} %collective-permute-done.7.refs_1_, bf16[2048,4096]{1,0:T(8,128)(2,1)} %bitcast.30, ...), custom_call_target="tpu_custom_call" | custom-call | tf_op jit(solution)/shard_map/decode/pallas_call | solution.py:255
  165.1 1.6 collective-permute-start.14
  166.9 3.2 %collective-permute-start.20 = (bf16[1,192,1024]{2,1,0:T(8,128)(2,1)S(1)}, bf16[1,192,1024]{2,1,0:T(8,128)(2,1)S(1)}, u32[]{:S(2)}, u32[]{:S(2)}) collective-permute-start(bf16[1,192,1024]{2,1,0:T(8,128)(2,1)S(1)} %add_convert_fusion.4.refs_4_), channel_id=1, source_target_pairs={{0,8},{4,12},{8,0},{12,4},{1,9},{5,13},{9,1},{13,5},{2,10},{6,14},... | collective-permute-start | bytes 1179656 | tf_op jit(solution)/shard_map/ppermute | solution.py:330
  170.2 4.5 %decode.10 = (bf16[1,96,1024]{2,1,0:T(8,128)(2,1)S(1)}, bf16[1,96,1024]{2,1,0:T(8,128)(2,1)S(1)}, bf16[1,192,1024]{2,1,0:T(8,128)(2,1)S(1)}) custom-call(s32[2]{0:T(128)S(1)} %pad_add_fusion.4.info_ref, bf16[384,2048]{1,0:T(8,128)(2,1)S(1)} %encode.3.refs_0_, bf16[384,2048]{1,0:T(8,128)(2,1)S(1)} %collective-permute-done.7.refs_1_, ...), custom_call_target="tpu_custom_call" | custom-call | tf_op jit(solution)/shard_map/decode/pallas_call | solution.py:255
  174.7 1.0 collective-permute-start.18
  175.7 1.1 collective-permute-start.19
  176.9 1.0 collective-permute-start.16
  177.9 4.7 %decode.11 = (f32[1,192,1024]{2,1,0:T(8,128)S(1)}, bf16[1,192,1024]{2,1,0:T(8,128)(2,1)S(1)}) custom-call(s32[2]{0:T(128)S(1)} %get-tuple-element.60.info_ref, bf16[384,2048]{1,0:T(8,128)(2,1)S(1)} %encode.3.refs_0_, bf16[384,2048]{1,0:T(8,128)(2,1)S(1)} %collective-permute-done.7.refs_1_, bf16[2048,4096]{1,0:T(8,128)(2,1)} %bitcast.32, ...), custom_call_target="tpu_custom_call" | custom-call | tf_op jit(solution)/shard_map/decode/pallas_call | solution.py:255
  182.6 6.3 %collective-permute-done.18 = bf16[1,96,1024]{2,1,0:T(8,128)(2,1)S(1)} collective-permute-done((bf16[1,96,1024]{2,1,0:T(8,128)(2,1)S(1)}, bf16[1,96,1024]{2,1,0:T(8,128)(2,1)S(1)}, u32[]{:S(2)}, u32[]{:S(2)}) %collective-permute-start.18) | collective-permute-done | bytes 196640 | tf_op jit(solution)/shard_map/ppermute | solution.py:330
  188.9 1.2 collective-permute-start.12
  190.1 3.1 %collective-permute-done.19 = bf16[1,96,1024]{2,1,0:T(8,128)(2,1)S(1)} collective-permute-done((bf16[1,96,1024]{2,1,0:T(8,128)(2,1)S(1)}, bf16[1,96,1024]{2,1,0:T(8,128)(2,1)S(1)}, u32[]{:S(2)}, u32[]{:S(2)}) %collective-permute-start.19) | collective-permute-done | bytes 196640 | tf_op jit(solution)/shard_map/ppermute | solution.py:330
  193.2 1.2 collective-permute-start.11
  194.5 0.9 collective-permute-start.21
  195.4 5.4 %collective-permute-done.16 = bf16[1,192,1024]{2,1,0:T(8,128)(2,1)S(1)} collective-permute-done((bf16[1,192,1024]{2,1,0:T(8,128)(2,1)S(1)}, bf16[1,192,1024]{2,1,0:T(8,128)(2,1)S(1)}, u32[]{:S(2)}, u32[]{:S(2)}) %collective-permute-start.16) | collective-permute-done | bytes 393248 | tf_op jit(solution)/shard_map/ppermute | solution.py:330
  201.1 0.9 collective-permute-start.17
  202.0 2.5 %collective-permute-start.13 = (bf16[1,192,1024]{2,1,0:T(8,128)(2,1)S(1)}, bf16[1,192,1024]{2,1,0:T(8,128)(2,1)S(1)}, u32[]{:S(2)}, u32[]{:S(2)}) collective-permute-start(bf16[1,192,1024]{2,1,0:T(8,128)(2,1)S(1)} %add_convert_fusion.3), channel_id=1, source_target_pairs={{0,4},{4,0},{8,12},{12,8},{1,5},{5,1},{9,13},{13,9},{2,6},{6,2},{1... | collective-permute-start | bytes 1179656 | tf_op jit(solution)/shard_map/ppermute | solution.py:330
  204.6 4.8 %collective-permute-done.11 = bf16[1,192,1024]{2,1,0:T(8,128)(2,1)S(1)} collective-permute-done((bf16[1,192,1024]{2,1,0:T(8,128)(2,1)S(1)}, bf16[1,192,1024]{2,1,0:T(8,128)(2,1)S(1)}, u32[]{:S(2)}, u32[]{:S(2)}) %collective-permute-start.11) | collective-permute-done | bytes 393248 | tf_op jit(solution)/shard_map/ppermute | solution.py:325
  209.4 6.2 %collective-permute-done.21.refs_5_ = bf16[192,1024]{1,0:T(8,128)(2,1)S(1)} collective-permute-done((bf16[192,1024]{1,0:T(8,128)(2,1)S(1)}, bf16[192,1024]{1,0:T(8,128)(2,1)S(1)}, u32[]{:S(2)}, u32[]{:S(2)}) %collective-permute-start.21) | collective-permute-done | bytes 393248 | tf_op jit(solution)/shard_map/ppermute | solution.py:325
  215.6 4.4 %collective-permute-done.17 = bf16[1,192,1024]{2,1,0:T(8,128)(2,1)S(1)} collective-permute-done((bf16[1,192,1024]{2,1,0:T(8,128)(2,1)S(1)}, bf16[1,192,1024]{2,1,0:T(8,128)(2,1)S(1)}, u32[]{:S(2)}, u32[]{:S(2)}) %collective-permute-start.17) | collective-permute-done | bytes 393248 | tf_op jit(solution)/shard_map/ppermute | solution.py:330
  220.3 1.6 finale.1
  221.9 1.9 collective-permute-start.23
  223.9 1.4 collective-permute-start.24
  225.6 1.1 collective-permute-done.24
  226.7 2.7 %collective-permute-start.26 = (f32[8,128]{1,0:T(8,128)S(1)}, f32[8,128]{1,0:T(8,128)S(1)}, u32[]{:S(2)}, u32[]{:S(2)}) collective-permute-start(f32[8,128]{1,0:T(8,128)S(1)} %add_add_fusion.1), channel_id=1, source_target_pairs={{0,8},{4,12},{8,0},{12,4},{1,9},{5,13},{9,1},{13,5},{2,10},{6,14},... | collective-permute-start | bytes 12296 | tf_op jit(solution)/shard_map/ppermute | solution.py:325
  229.4 1.1 collective-permute-start.27
  230.5 1.6 collective-permute-done.25
  232.1 0.9 collective-permute-done.27
  (55 shorter events, 5.0 us)
Async XLA Ops:
  0.6 77.3 %copy-start = (bf16[1,4096]{1,0:T(2,128)(2,1)S(1)}, bf16[1,4096]{1,0:T(2,128)(2,1)}, u32[]{:S(2)}) copy-start(bf16[1,4096]{1,0:T(2,128)(2,1)} %param.10) | copy-start | bytes 24580
  69.8 4.6 %collective-permute-start = (f32[1]{0:T(128)}, f32[1]{0:T(128)}, u32[]{:S(2)}, u32[]{:S(2)}) collective-permute-start(f32[1]{0:T(128)} %get-tuple-element.28), channel_id=1, source_target_pairs={{0,2},{2,0},{1,3},{3,1},{4,6},{6,4},{5,7},{7,5},{8,10},{10,8},{9,1... | collective-permute-start | bytes 20 | tf_op jit(solution)/shard_map/ppermute | solution.py:325
  75.8 23.7 %collective-permute-start.3 = (bf16[112,4096]{1,0:T(8,128)(2,1)}, bf16[112,4096]{1,0:T(8,128)(2,1)}, u32[]{:S(2)}, u32[]{:S(2)}) collective-permute-start(bf16[112,4096]{1,0:T(8,128)(2,1)} %get-tuple-element.35), channel_id=1, source_target_pairs={{0,2},{2,0},{1,3},{3,1},{4,6},{6,4},{5,7},{7,5},{8,10},{10,8},{9,1... | collective-permute-start | bytes 2752520 | tf_op jit(solution)/shard_map/ppermute | solution.py:325
  91.2 10.5 %collective-permute-start.1 = (bf16[384,1024]{1,0:T(8,128)(2,1)S(1)}, bf16[384,1024]{1,0:T(8,128)(2,1)S(1)}, u32[]{:S(2)}, u32[]{:S(2)}) collective-permute-start(bf16[384,1024]{1,0:T(8,128)(2,1)S(1)} %get-tuple-element.29.refs_0_), channel_id=1, source_target_pairs={{0,1},{2,3},{4,5},{6,7},{8,9},{10,11},{12,13},{14,15},{16,17},{18,... | collective-permute-start | bytes 2359304 | tf_op jit(solution)/shard_map/ppermute | solution.py:393
  92.5 9.1 %collective-permute-start.2 = (bf16[384,1024]{1,0:T(8,128)(2,1)S(1)}, bf16[384,1024]{1,0:T(8,128)(2,1)S(1)}, u32[]{:S(2)}, u32[]{:S(2)}) collective-permute-start(bf16[384,1024]{1,0:T(8,128)(2,1)S(1)} %get-tuple-element.30.refs_1_), channel_id=1, source_target_pairs={{0,1},{2,3},{4,5},{6,7},{8,9},{10,11},{12,13},{14,15},{16,17},{18,... | collective-permute-start | bytes 2359304 | tf_op jit(solution)/shard_map/ppermute | solution.py:393
  93.9 34.0 %collective-permute-start.5 = (bf16[160,4096]{1,0:T(8,128)(2,1)}, bf16[160,4096]{1,0:T(8,128)(2,1)}, u32[]{:S(2)}, u32[]{:S(2)}) collective-permute-start(bf16[160,4096]{1,0:T(8,128)(2,1)} %get-tuple-element.36), channel_id=1, source_target_pairs={{0,2},{2,0},{1,3},{3,1},{4,6},{6,4},{5,7},{7,5},{8,10},{10,8},{9,1... | collective-permute-start | bytes 3932168 | tf_op jit(solution)/shard_map/ppermute | solution.py:325
  99.5 28.4 %collective-permute-start.4 = (bf16[112,4096]{1,0:T(8,128)(2,1)}, bf16[112,4096]{1,0:T(8,128)(2,1)}, u32[]{:S(2)}, u32[]{:S(2)}) collective-permute-start(bf16[112,4096]{1,0:T(8,128)(2,1)} %collective-permute-done.3.refs_0_), channel_id=1, source_target_pairs={{0,4},{4,0},{8,12},{12,8},{1,5},{5,1},{9,13},{13,9},{2,6},{6,2},{1... | collective-permute-start | bytes 2752520 | tf_op jit(solution)/shard_map/ppermute | solution.py:330
  108.7 0.9 copy-start.3
  109.6 0.9 copy-start.5
  110.5 0.8 copy-start.8
  111.3 15.5 %collective-permute-start.6 = (bf16[1,192,1024]{2,1,0:T(8,128)(2,1)S(1)}, bf16[1,192,1024]{2,1,0:T(8,128)(2,1)}, u32[]{:S(2)}, u32[]{:S(2)}) collective-permute-start(bf16[1,192,1024]{2,1,0:T(8,128)(2,1)S(1)} %get-tuple-element.31.refs_6_), channel_id=1, source_target_pairs={{0,4},{4,0},{8,12},{12,8},{1,5},{5,1},{9,13},{13,9},{2,6},{6,2},{1... | collective-permute-start | bytes 1179656 | tf_op jit(solution)/shard_map/ppermute | solution.py:330
  127.8 15.2 %copy-start.9 = (bf16[1,192,1024]{2,1,0:T(8,128)(2,1)S(1)}, bf16[1,192,1024]{2,1,0:T(8,128)(2,1)}, u32[]{:S(2)}) copy-start(bf16[1,192,1024]{2,1,0:T(8,128)(2,1)} %copy-done.8) | copy-start | bytes 1179652
  141.6 5.8 %collective-permute-start.7 = (bf16[384,2048]{1,0:T(8,128)(2,1)S(1)}, bf16[384,2048]{1,0:T(8,128)(2,1)S(1)}, u32[]{:S(2)}, u32[]{:S(2)}) collective-permute-start(bf16[384,2048]{1,0:T(8,128)(2,1)S(1)} %encode.3.refs_0_), channel_id=1, source_target_pairs={{0,1},{2,3},{4,5},{6,7},{8,9},{10,11},{12,13},{14,15},{16,17},{18,... | collective-permute-start | bytes 4718600 | tf_op jit(solution)/shard_map/ppermute | solution.py:393
  143.0 17.2 %collective-permute-start.8 = (bf16[1,192,1024]{2,1,0:T(8,128)(2,1)S(1)}, bf16[1,192,1024]{2,1,0:T(8,128)(2,1)S(1)}, u32[]{:S(2)}, u32[]{:S(2)}) collective-permute-start(bf16[1,192,1024]{2,1,0:T(8,128)(2,1)S(1)} %copy-done.9), channel_id=1, source_target_pairs={{0,4},{4,0},{8,12},{12,8},{1,5},{5,1},{9,13},{13,9},{2,6},{6,2},{1... | collective-permute-start | bytes 1179656 | tf_op jit(solution)/shard_map/ppermute | solution.py:330
  144.6 15.7 %collective-permute-start.9 = (bf16[1,192,1024]{2,1,0:T(8,128)(2,1)S(1)}, bf16[1,192,1024]{2,1,0:T(8,128)(2,1)S(1)}, u32[]{:S(2)}, u32[]{:S(2)}) collective-permute-start(bf16[1,192,1024]{2,1,0:T(8,128)(2,1)S(1)} %add_convert_fusion.5.refs_4_), channel_id=1, source_target_pairs={{0,8},{4,12},{8,0},{12,4},{1,9},{5,13},{9,1},{13,5},{2,10},{6,14},... | collective-permute-start | bytes 1179656 | tf_op jit(solution)/shard_map/ppermute | solution.py:330
  151.9 14.9 %collective-permute-start.10 = (bf16[1,192,1024]{2,1,0:T(8,128)(2,1)S(1)}, bf16[1,192,1024]{2,1,0:T(8,128)(2,1)S(1)}, u32[]{:S(2)}, u32[]{:S(2)}) collective-permute-start(bf16[1,192,1024]{2,1,0:T(8,128)(2,1)S(1)} %get-tuple-element.38.refs_4_), channel_id=1, source_target_pairs={{0,4},{4,0},{8,12},{12,8},{1,5},{5,1},{9,13},{13,9},{2,6},{6,2},{1... | collective-permute-start | bytes 1179656 | tf_op jit(solution)/shard_map/ppermute | solution.py:330
  152.5 24.3 %collective-permute-start.15 = (bf16[1,192,1024]{2,1,0:T(8,128)(2,1)S(1)}, bf16[1,192,1024]{2,1,0:T(8,128)(2,1)S(1)}, u32[]{:S(2)}, u32[]{:S(2)}) collective-permute-start(bf16[1,192,1024]{2,1,0:T(8,128)(2,1)S(1)} %get-tuple-element.50), channel_id=1, source_target_pairs={{0,2},{2,0},{1,3},{3,1},{4,6},{6,4},{5,7},{7,5},{8,10},{10,8},{9,1... | collective-permute-start | bytes 1179656 | tf_op jit(solution)/shard_map/ppermute | solution.py:325
  165.1 30.4 %collective-permute-start.14 = (bf16[1,192,1024]{2,1,0:T(8,128)(2,1)S(1)}, bf16[1,192,1024]{2,1,0:T(8,128)(2,1)S(1)}, u32[]{:S(2)}, u32[]{:S(2)}) collective-permute-start(bf16[1,192,1024]{2,1,0:T(8,128)(2,1)S(1)} %get-tuple-element.48), channel_id=1, source_target_pairs={{0,2},{2,0},{1,3},{3,1},{4,6},{6,4},{5,7},{7,5},{8,10},{10,8},{9,1... | collective-permute-start | bytes 1179656 | tf_op jit(solution)/shard_map/ppermute | solution.py:325
  166.9 9.8 %copy-start.6 = (f32[1,192,1024]{2,1,0:T(8,128)S(1)}, f32[1,192,1024]{2,1,0:T(8,128)}, u32[]{:S(2)}) copy-start(f32[1,192,1024]{2,1,0:T(8,128)} %copy-done.5) | copy-start | bytes 2359300
  166.9 27.4 %collective-permute-start.20 = (bf16[1,192,1024]{2,1,0:T(8,128)(2,1)S(1)}, bf16[1,192,1024]{2,1,0:T(8,128)(2,1)S(1)}, u32[]{:S(2)}, u32[]{:S(2)}) collective-permute-start(bf16[1,192,1024]{2,1,0:T(8,128)(2,1)S(1)} %add_convert_fusion.4.refs_4_), channel_id=1, source_target_pairs={{0,8},{4,12},{8,0},{12,4},{1,9},{5,13},{9,1},{13,5},{2,10},{6,14},... | collective-permute-start | bytes 1179656 | tf_op jit(solution)/shard_map/ppermute | solution.py:330
  174.7 14.3 %collective-permute-start.18 = (bf16[1,96,1024]{2,1,0:T(8,128)(2,1)S(1)}, bf16[1,96,1024]{2,1,0:T(8,128)(2,1)S(1)}, u32[]{:S(2)}, u32[]{:S(2)}) collective-permute-start(bf16[1,96,1024]{2,1,0:T(8,128)(2,1)S(1)} %get-tuple-element.42.refs_4_), channel_id=1, source_target_pairs={{0,4},{4,0},{8,12},{12,8},{1,5},{5,1},{9,13},{13,9},{2,6},{6,2},{1... | collective-permute-start | bytes 589832 | tf_op jit(solution)/shard_map/ppermute | solution.py:330
  175.7 17.5 %collective-permute-start.19 = (bf16[1,96,1024]{2,1,0:T(8,128)(2,1)S(1)}, bf16[1,96,1024]{2,1,0:T(8,128)(2,1)S(1)}, u32[]{:S(2)}, u32[]{:S(2)}) collective-permute-start(bf16[1,96,1024]{2,1,0:T(8,128)(2,1)S(1)} %get-tuple-element.43.refs_5_), channel_id=1, source_target_pairs={{0,4},{4,0},{8,12},{12,8},{1,5},{5,1},{9,13},{13,9},{2,6},{6,2},{1... | collective-permute-start | bytes 589832 | tf_op jit(solution)/shard_map/ppermute | solution.py:330
  176.9 24.0 %collective-permute-start.16 = (bf16[1,192,1024]{2,1,0:T(8,128)(2,1)S(1)}, bf16[1,192,1024]{2,1,0:T(8,128)(2,1)S(1)}, u32[]{:S(2)}, u32[]{:S(2)}) collective-permute-start(bf16[1,192,1024]{2,1,0:T(8,128)(2,1)S(1)} %add_convert_fusion.2), channel_id=1, source_target_pairs={{0,4},{4,0},{8,12},{12,8},{1,5},{5,1},{9,13},{13,9},{2,6},{6,2},{1... | collective-permute-start | bytes 1179656 | tf_op jit(solution)/shard_map/ppermute | solution.py:330
  188.9 13.0 %collective-permute-start.12 = (bf16[1,192,1024]{2,1,0:T(8,128)(2,1)S(1)}, bf16[1,192,1024]{2,1,0:T(8,128)(2,1)S(1)}, u32[]{:S(2)}, u32[]{:S(2)}) collective-permute-start(bf16[1,192,1024]{2,1,0:T(8,128)(2,1)S(1)} %get-tuple-element.46), channel_id=1, source_target_pairs={{0,2},{2,0},{1,3},{3,1},{4,6},{6,4},{5,7},{7,5},{8,10},{10,8},{9,1... | collective-permute-start | bytes 1179656 | tf_op jit(solution)/shard_map/ppermute | solution.py:325
  193.2 16.3 %collective-permute-start.11 = (bf16[1,192,1024]{2,1,0:T(8,128)(2,1)S(1)}, bf16[1,192,1024]{2,1,0:T(8,128)(2,1)S(1)}, u32[]{:S(2)}, u32[]{:S(2)}) collective-permute-start(bf16[1,192,1024]{2,1,0:T(8,128)(2,1)S(1)} %get-tuple-element.44), channel_id=1, source_target_pairs={{0,2},{2,0},{1,3},{3,1},{4,6},{6,4},{5,7},{7,5},{8,10},{10,8},{9,1... | collective-permute-start | bytes 1179656 | tf_op jit(solution)/shard_map/ppermute | solution.py:325
  194.3 7.6 %copy-start.4 = (f32[1,192,1024]{2,1,0:T(8,128)S(1)}, f32[1,192,1024]{2,1,0:T(8,128)}, u32[]{:S(2)}) copy-start(f32[1,192,1024]{2,1,0:T(8,128)} %copy-done.3) | copy-start | bytes 2359300
  194.5 21.1 %collective-permute-start.21 = (bf16[192,1024]{1,0:T(8,128)(2,1)S(1)}, bf16[192,1024]{1,0:T(8,128)(2,1)S(1)}, u32[]{:S(2)}, u32[]{:S(2)}) collective-permute-start(bf16[192,1024]{1,0:T(8,128)(2,1)S(1)} %fusion), channel_id=1, source_target_pairs={{0,2},{2,0},{1,3},{3,1},{4,6},{6,4},{5,7},{7,5},{8,10},{10,8},{9,1... | collective-permute-start | bytes 1179656 | tf_op jit(solution)/shard_map/ppermute | solution.py:325
  200.9 19.4 %copy-start.2 = (bf16[1,384,1024]{2,1,0:T(8,128)(2,1)S(1)}, bf16[1,384,1024]{2,1,0:T(8,128)(2,1)}, u32[]{:S(2)}) copy-start(bf16[1,384,1024]{2,1,0:T(8,128)(2,1)} %param.8) | copy-start | bytes 2359300
  200.9 19.4 %copy-start.7 = (bf16[1,1024]{1,0:T(2,128)(2,1)S(1)}, bf16[1,1024]{1,0:T(2,128)(2,1)}, u32[]{:S(2)}) copy-start(bf16[1,1024]{1,0:T(2,128)(2,1)} %b_ref.1) | copy-start | bytes 6148
  201.1 18.9 %collective-permute-start.17 = (bf16[1,192,1024]{2,1,0:T(8,128)(2,1)S(1)}, bf16[1,192,1024]{2,1,0:T(8,128)(2,1)S(1)}, u32[]{:S(2)}, u32[]{:S(2)}) collective-permute-start(bf16[1,192,1024]{2,1,0:T(8,128)(2,1)S(1)} %add_convert_fusion.1), channel_id=1, source_target_pairs={{0,8},{4,12},{8,0},{12,4},{1,9},{5,13},{9,1},{13,5},{2,10},{6,14},... | collective-permute-start | bytes 1179656 | tf_op jit(solution)/shard_map/ppermute | solution.py:330
  202.0 18.2 %collective-permute-start.13 = (bf16[1,192,1024]{2,1,0:T(8,128)(2,1)S(1)}, bf16[1,192,1024]{2,1,0:T(8,128)(2,1)S(1)}, u32[]{:S(2)}, u32[]{:S(2)}) collective-permute-start(bf16[1,192,1024]{2,1,0:T(8,128)(2,1)S(1)} %add_convert_fusion.3), channel_id=1, source_target_pairs={{0,4},{4,0},{8,12},{12,8},{1,5},{5,1},{9,13},{13,9},{2,6},{6,2},{1... | collective-permute-start | bytes 1179656 | tf_op jit(solution)/shard_map/ppermute | solution.py:330
  220.3 16.0 %copy-start.1 = (bf16[1,4096]{1,0:T(2,128)(2,1)S(1)}, bf16[1,4096]{1,0:T(2,128)(2,1)}, u32[]{:S(2)}) copy-start(bf16[1,4096]{1,0:T(2,128)(2,1)} %param.10) | copy-start | bytes 24580
  221.9 3.4 %collective-permute-start.22 = (f32[8,128]{1,0:T(8,128)S(1)}, f32[8,128]{1,0:T(8,128)S(1)}, u32[]{:S(2)}, u32[]{:S(2)}) collective-permute-start(f32[8,128]{1,0:T(8,128)S(1)} %get-tuple-element.53), channel_id=1, source_target_pairs={{0,1},{1,2},{2,3},{3,0},{4,5},{5,6},{6,7},{7,4},{8,9},{9,10},{10,1... | collective-permute-start | bytes 12296 | tf_op jit(solution)/shard_map/ppermute | solution.py:325
  221.9 3.6 %collective-permute-start.23 = (f32[8,128]{1,0:T(8,128)S(1)}, f32[8,128]{1,0:T(8,128)S(1)}, u32[]{:S(2)}, u32[]{:S(2)}) collective-permute-start(f32[8,128]{1,0:T(8,128)S(1)} %get-tuple-element.53), channel_id=1, source_target_pairs={{0,2},{1,3},{2,0},{3,1},{4,6},{5,7},{6,4},{7,5},{8,10},{9,11},{10,... | collective-permute-start | bytes 12296 | tf_op jit(solution)/shard_map/ppermute | solution.py:325
  223.9 2.8 %collective-permute-start.24 = (f32[8,128]{1,0:T(8,128)S(1)}, f32[8,128]{1,0:T(8,128)S(1)}, u32[]{:S(2)}, u32[]{:S(2)}) collective-permute-start(f32[8,128]{1,0:T(8,128)S(1)} %get-tuple-element.53), channel_id=1, source_target_pairs={{0,3},{1,0},{2,1},{3,2},{4,7},{5,4},{6,5},{7,6},{8,11},{9,8},{10,9... | collective-permute-start | bytes 12296 | tf_op jit(solution)/shard_map/ppermute | solution.py:325
  226.7 5.4 %collective-permute-start.25 = (f32[8,128]{1,0:T(8,128)S(1)}, f32[8,128]{1,0:T(8,128)S(1)}, u32[]{:S(2)}, u32[]{:S(2)}) collective-permute-start(f32[8,128]{1,0:T(8,128)S(1)} %add_add_fusion.1), channel_id=1, source_target_pairs={{0,4},{4,8},{8,12},{12,0},{1,5},{5,9},{9,13},{13,1},{2,6},{6,10},{... | collective-permute-start | bytes 12296 | tf_op jit(solution)/shard_map/ppermute | solution.py:325
  226.7 5.4 %collective-permute-start.26 = (f32[8,128]{1,0:T(8,128)S(1)}, f32[8,128]{1,0:T(8,128)S(1)}, u32[]{:S(2)}, u32[]{:S(2)}) collective-permute-start(f32[8,128]{1,0:T(8,128)S(1)} %add_add_fusion.1), channel_id=1, source_target_pairs={{0,8},{4,12},{8,0},{12,4},{1,9},{5,13},{9,1},{13,5},{2,10},{6,14},... | collective-permute-start | bytes 12296 | tf_op jit(solution)/shard_map/ppermute | solution.py:325
  229.4 3.6 %collective-permute-start.27 = (f32[8,128]{1,0:T(8,128)S(1)}, f32[8,128]{1,0:T(8,128)S(1)}, u32[]{:S(2)}, u32[]{:S(2)}) collective-permute-start(f32[8,128]{1,0:T(8,128)S(1)} %add_add_fusion.1), channel_id=1, source_target_pairs={{0,12},{4,0},{8,4},{12,8},{1,13},{5,1},{9,5},{13,9},{2,14},{6,2},{... | collective-permute-start | bytes 12296 | tf_op jit(solution)/shard_map/ppermute | solution.py:325

commit v7 on v6

--- a/solution.py
+++ b/solution.py
@@ -5,9 +5,9 @@
 from jax.experimental.pallas import tpu as pltpu
 from jax.sharding import PartitionSpec as P
 
-VMEM_LIMIT = 40 * 1024 * 1024
-SLOTS = 6
-TILE = 256
+VMEM_LIMIT = 28 * 1024 * 1024
+ENCODE_TILE, ENCODE_SLOTS = 512, 3
+DECODE_TILE, DECODE_SLOTS = 256, 6
 COST = pl.CostEstimate(flops=0, bytes_accessed=0, transcendentals=0)
 
 
@@ -32,13 +32,11 @@
 
         first = pl.ds(pl.multiple_of(side_ref[0] * (rows - edge), 16), edge)
         cuts = [
-            pltpu.make_async_copy(x_ref.at[first], outer_ref, out_sem.at[0]),
-            pltpu.make_async_copy(x_ref.at[pl.ds(edge, middle)], inner_ref, out_sem.at[1]),
+            pltpu.make_async_copy(held.at[first], outer_ref, out_sem.at[0]),
+            pltpu.make_async_copy(held.at[pl.ds(edge, middle)], inner_ref, out_sem.at[1]),
         ]
         for i in range(loads):
             load(i).start()
-        for copy in cuts:
-            copy.start()
         total = jnp.zeros((8, lanes), jnp.float32)
         for i in range(loads):
             load(i).wait()
@@ -50,6 +48,8 @@
                     return acc + value[:8] + value[8:]
 
                 total = lax.fori_loop(0, piece // 16, add, total, unroll=2)
+        for copy in cuts:
+            copy.start()
         o_ref[0] = jnp.sum(total)
         for copy in cuts:
             copy.wait()
@@ -91,17 +91,17 @@
     )(after, *[in_hbm(value) for value in values])
 
 
-def ring_loop(count, start, step):
-    for t in range(min(SLOTS, count)):
+def ring_loop(count, slots, start, step):
+    for t in range(min(slots, count)):
         start(t, t)
 
     def turn(t, carry):
-        slot = lax.rem(t, SLOTS)
+        slot = lax.rem(t, slots)
         step(t, slot)
 
-        @pl.when(t + SLOTS < count)
+        @pl.when(t + slots < count)
         def _():
-            start(t + SLOTS, slot)
+            start(t + slots, slot)
 
         return carry
 
@@ -112,7 +112,7 @@
     rows, width = sum(piece[2] for piece in pieces), pieces[0][0].shape[1]
     latents = weight.shape[1]
     part = latents // parts
-    tile = tile_of(part, TILE)
+    tile = tile_of(part, ENCODE_TILE)
     n, m = len(pieces), len(also)
 
     def body(places_ref, inv_ref, b_ref, *refs):
@@ -151,7 +151,7 @@
                 def _():
                     o_ref[:, columns(lax.rem(t, per))] = value
 
-        ring_loop(latents // tile, lambda t, slot: tile_copy(t, slot).start(), step)
+        ring_loop(latents // tile, ENCODE_SLOTS, lambda t, slot: tile_copy(t, slot).start(), step)
 
     return pl.pallas_call(
         body,
@@ -164,9 +164,9 @@
         out_shape=[jax.ShapeDtypeStruct((rows, part), jnp.bfloat16)] * parts,
         scratch_shapes=[
             pltpu.VMEM((rows, width), jnp.bfloat16),
-            pltpu.VMEM((SLOTS, width, tile), jnp.bfloat16),
+            pltpu.VMEM((ENCODE_SLOTS, width, tile), jnp.bfloat16),
             pltpu.SemaphoreType.DMA((n,)),
-            pltpu.SemaphoreType.DMA((SLOTS,)),
+            pltpu.SemaphoreType.DMA((ENCODE_SLOTS,)),
         ],
         compiler_params=pltpu.CompilerParams(vmem_limit_bytes=VMEM_LIMIT),
         cost_estimate=COST,
@@ -178,7 +178,7 @@
     parts = len(codes)
     rows, part = codes[0].shape
     latents = parts * part
-    tile = tile_of(width, TILE)
+    tile = tile_of(width, DECODE_TILE)
     per = width // tile
     blocks = info.shape[0] - 1
     m = len(also)
@@ -250,7 +250,7 @@
                 put(t, jnp.dot(
                     lhs[:, :latents], ring[slot, :latents], preferred_element_type=jnp.float32))
 
-        ring_loop(blocks * per, start, step)
+        ring_loop(blocks * per, DECODE_SLOTS, start, step)
 
     return pl.pallas_call(
         body,
@@ -263,9 +263,9 @@
         ],
         scratch_shapes=[
             pltpu.VMEM((rows, 2 * latents), jnp.bfloat16),
-            pltpu.VMEM((SLOTS, 2 * latents, tile), jnp.bfloat16),
+            pltpu.VMEM((DECODE_SLOTS, 2 * latents, tile), jnp.bfloat16),
             pltpu.SemaphoreType.DMA((2 * parts,)),
-            pltpu.SemaphoreType.DMA((SLOTS, 2)),
+            pltpu.SemaphoreType.DMA((DECODE_SLOTS, 2)),
         ],
         compiler_params=pltpu.CompilerParams(vmem_limit_bytes=VMEM_LIMIT),
         cost_estimate=COST,
@@ -428,6 +428,9 @@
     returned = []
     far_out_back, far_out_kept_back, near_out_back, near_out_kept_back = [], [], [], []
 
+    def joined(own, back):
+        return own + sum(wide(part) for part in back)
+
     for back, mine, theirs, inner_rows in foreign:
         codes = encode(
             [(mine, 0, edge), (theirs, 0, edge), (inner_rows, 0, rows - 2 * edge)],
@@ -444,23 +447,23 @@
         (far_sent,), far_back = quarter_of(other, far, [inside], narrow, [])
         far_in = swapped(far_sent, "latent", 1)
         (far_kept,), far_kept_back = quarter_of(mine_bit, far, [inside], jnp.float32, [far_sent, total_in])
-        across = (far_kept + wide(far_in)).astype(narrow)
+        far_out_back.append(far_back)
+        ready = [(far_kept + wide(far_in)).astype(narrow)]
+        across = swapped(ready[0], "latent", 2)
+        if len(far_out_back) == n_tok - 1:
+            ready.append(joined(far_out_sent, far_out_back).astype(narrow))
+            far_out = swapped(ready[1], "latent", 1)
         halves = [((quarter, quarter),), ((2 * quarter, quarter),)]
-        near_sent, near_back = quarter_of(other, near, halves, narrow, [across])
+        near_sent, near_back = quarter_of(other, near, halves, narrow, ready)
         near_in = jnp.concatenate([swapped(part, "latent", 1) for part in near_sent], axis=1)
         (near_kept,), near_kept_back = quarter_of(mine_bit, near, [inside], jnp.float32, near_sent)
-        part = finish(near_kept + wide(near_in) + wide(swapped(across, "latent", 2)))
+        part = finish(near_kept + wide(near_in) + wide(across))
         returned.append(shifted(part.astype(narrow), "token", back))
-        far_out_back.append(far_back)
         far_out_kept_back.append(far_kept_back)
         near_out_back.append(near_back)
         near_out_kept_back.append(near_kept_back)
         after = near_kept
 
-    def joined(own, back):
-        return own + sum(wide(part) for part in back)
-
-    far_out = swapped(joined(far_out_sent, far_out_back).astype(narrow), "latent", 1)
     near_out = swapped(joined(near_out_sent, near_out_back).astype(narrow), "latent", 1)
     across_out = (joined(far_out_kept, far_out_kept_back) + wide(far_out)).astype(narrow)
     across_out = swapped(across_out, "latent", 2)

time: 238 us -> 171 us (0.72)
  Pallas kernels: 130 us -> 62.1 us
    pallas_call x1, Pallas kernels: 69.2 us -> 3.98 us  [prepare(): pl.pallas_call(body, in_specs=[pl.BlockSpec(memory_space=pltpu.SMEM), pl....]
    pallas_call x2, Pallas kernels: 27 us -> 24.1 us  [encode(): pl.pallas_call(body, in_specs=[pl.BlockSpec(memory_space=pltpu.SMEM), pl....]
  transfers between devices with their start and end apart: 28 -> 28, of which waited for: 17 -> 18; matrix products, arithmetic and copies ran while one was open for 1% -> 1% of each run, Pallas kernels for 19% -> 26%
where the time goes in v7:
time: 171 us
  Pallas kernels  62.1 us (36%)
  waiting for transfers between devices  58.5 us (34%)
  starting transfers between devices  39.1 us (23%)
  between operations  5.96 us (3%)
  local copies, waits for them, and re-layouts  3.23 us (2%)
  other arithmetic  2.29 us (1%)
    ppermute x11, waiting for transfers between devices, swapped(): return lax.ppermute(value, axis, [(i, i ^ bit) for i in range(n)])  35.2 us
    pallas_call x6, Pallas kernels, decode(): pl.pallas_call(body, in_specs=[pl.BlockSpec(memory_space=pltpu.SMEM)] + [...  32.3 us
    pallas_call x2, Pallas kernels, encode(): pl.pallas_call(body, in_specs=[pl.BlockSpec(memory_space=pltpu.SMEM), pl....  24.1 us
    ppermute x14, waiting for transfers between devices, shifted(): lax.ppermute(value, axis, [(i, (i + distance) % n) for i in range(n)])  23.3 us
    ppermute x14, starting transfers between devices, shifted(): lax.ppermute(value, axis, [(i, (i + distance) % n) for i in range(n)])  18.5 us
    ppermute x11, starting transfers between devices, swapped(): return lax.ppermute(value, axis, [(i, i ^ bit) for i in range(n)])  16.5 us
    ppermute x3, starting transfers between devices, earlier_of(): return [lax.ppermute(part, 'layer', [(0, 1)]) for part in codes]  4.07 us
    pallas_call x1, Pallas kernels, prepare(): pl.pallas_call(body, in_specs=[pl.BlockSpec(memory_space=pltpu.SMEM), pl....  3.98 us
  transfers between devices with their start and end apart: 28, of which 18 were waited for; matrix products, arithmetic and copies ran while one was open for 1% of the time, Pallas kernels for 26%

profile of v7, /device:TPU:0, one launch (start us, length us, event | category | flops | bytes accessed | tf_op | source)
XLA Modules:
  0.0 171.2 jit_solution(11620544708476642321)
XLA Ops:
  0.7 4.0 %prepare.1 = (bf16[112,4096]{1,0:T(8,128)(2,1)}, bf16[160,4096]{1,0:T(8,128)(2,1)}, f32[1]{0:T(128)}) custom-call(s32[1]{0:T(128)} %bitcast.4.side_ref, bf16[384,4096]{1,0:T(8,128)(2,1)} %bitcast.35), custom_call_target="tpu_custom_call" | custom-call | tf_op jit(solution)/shard_map/prepare/pallas_call | solution.py:57
  4.6 3.0 %collective-permute-start = (f32[1]{0:T(128)}, f32[1]{0:T(128)}, u32[]{:S(2)}, u32[]{:S(2)}) collective-permute-start(f32[1]{0:T(128)} %get-tuple-element.28), channel_id=1, source_target_pairs={{0,2},{2,0},{1,3},{3,1},{4,6},{6,4},{5,7},{7,5},{8,10},{10,8},{9,1... | collective-permute-start | bytes 20 | tf_op jit(solution)/shard_map/ppermute | solution.py:325
  7.7 1.6 collective-permute-done
  10.6 2.1 %collective-permute-start.3 = (bf16[112,4096]{1,0:T(8,128)(2,1)}, bf16[112,4096]{1,0:T(8,128)(2,1)}, u32[]{:S(2)}, u32[]{:S(2)}) collective-permute-start(bf16[112,4096]{1,0:T(8,128)(2,1)} %get-tuple-element.35), channel_id=1, source_target_pairs={{0,2},{2,0},{1,3},{3,1},{4,6},{6,4},{5,7},{7,5},{8,10},{10,8},{9,1... | collective-permute-start | bytes 2752520 | tf_op jit(solution)/shard_map/ppermute | solution.py:325
  12.7 11.8 %encode.2 = (bf16[384,1024]{1,0:T(8,128)(2,1)S(1)}, bf16[384,1024]{1,0:T(8,128)(2,1)S(1)}) custom-call(s32[1]{0:T(128)} %constant.61.clone.1.places_ref, f32[1]{0:T(128)S(6)} %sqrt.3.inv_ref.after_ref, bf16[1,2048]{1,0:T(2,128)(2,1)S(1)} %constant_dynamic-slice_fusion.b_ref, bf16[384,4096]{1,0:T(8,128)(2,1)} %bitcast.36, bf16[4096,2048]{1,0:T(8,128)(2,1)} %bitcast.33), custom_call_target="tpu_custom_call" | custom-call | tf_op jit(solution)/shard_map/encode/pallas_call | solution.py:156
  24.5 1.3 collective-permute-start.1
  25.9 1.3 collective-permute-start.2
  27.3 7.0 %collective-permute-done.3.refs_0_ = bf16[112,4096]{1,0:T(8,128)(2,1)} collective-permute-done((bf16[112,4096]{1,0:T(8,128)(2,1)}, bf16[112,4096]{1,0:T(8,128)(2,1)}, u32[]{:S(2)}, u32[]{:S(2)}) %collective-permute-start.3) | collective-permute-done | bytes 917536 | tf_op jit(solution)/shard_map/ppermute | solution.py:325
  34.3 2.1 %collective-permute-start.4 = (bf16[112,4096]{1,0:T(8,128)(2,1)}, bf16[112,4096]{1,0:T(8,128)(2,1)}, u32[]{:S(2)}, u32[]{:S(2)}) collective-permute-start(bf16[112,4096]{1,0:T(8,128)(2,1)} %collective-permute-done.3.refs_0_), channel_id=1, source_target_pairs={{0,4},{4,0},{8,12},{12,8},{1,5},{5,1},{9,13},{13,9},{2,6},{6,2},{1... | collective-permute-start | bytes 2752520 | tf_op jit(solution)/shard_map/ppermute | solution.py:330
  36.5 7.1 %decode.6 = (bf16[1,192,1024]{2,1,0:T(8,128)(2,1)S(1)}, bf16[1,192,1024]{2,1,0:T(8,128)(2,1)S(1)}, f32[1,192,1024]{2,1,0:T(8,128)S(1)}, f32[1,192,1024]{2,1,0:T(8,128)S(1)}) custom-call(s32[3]{0:T(128)S(1)} %get-tuple-element.59.info_ref, bf16[384,1024]{1,0:T(8,128)(2,1)S(1)} %get-tuple-element.29.refs_0_, bf16[384,1024]{1,0:T(8,128)(2,1)S(1)} %get-tuple-element.30.refs_1_, ...), custom_call_target="tpu_custom_call" | custom-call | tf_op jit(solution)/shard_map/decode/pallas_call | solution.py:255
  43.5 0.9 copy-done.3
  44.4 0.9 copy-done.5
  45.3 0.7 copy-done.8
  46.1 7.1 %decode.7 = (f32[1,192,1024]{2,1,0:T(8,128)S(1)}, f32[1,192,1024]{2,1,0:T(8,128)S(1)}, f32[1,192,1024]{2,1,0:T(8,128)S(1)}, f32[1,192,1024]{2,1,0:T(8,128)S(1)}) custom-call(s32[3]{0:T(128)S(1)} %get-tuple-element.58.info_ref, bf16[384,1024]{1,0:T(8,128)(2,1)S(1)} %get-tuple-element.29.refs_0_, bf16[384,1024]{1,0:T(8,128)(2,1)S(1)} %get-tuple-element.30.refs_1_, ...), custom_call_target="tpu_custom_call" | custom-call | tf_op jit(solution)/shard_map/decode/pallas_call | solution.py:255
  53.2 8.3 %collective-permute-done.6 = bf16[1,192,1024]{2,1,0:T(8,128)(2,1)} collective-permute-done((bf16[1,192,1024]{2,1,0:T(8,128)(2,1)S(1)}, bf16[1,192,1024]{2,1,0:T(8,128)(2,1)}, u32[]{:S(2)}, u32[]{:S(2)}) %collective-permute-start.6) | collective-permute-done | bytes 393248 | tf_op jit(solution)/shard_map/ppermute | solution.py:330
  61.5 1.1 add_convert_fusion.5.refs_4_
  62.7 12.3 %encode.3.refs_0_ = bf16[384,2048]{1,0:T(8,128)(2,1)S(1)} custom-call(s32[3]{0:T(128)S(1)} %pad_add_fusion.3.places_ref, f32[1]{0:T(128)S(6)} %sqrt.3.inv_ref.after_ref, bf16[1,2048]{1,0:T(2,128)(2,1)S(1)} %constant_dynamic-slice_fusion.b_ref, bf16[112,4096]{1,0:T(8,128)(2,1)} %collective-permute-done.3.refs_0_, ...), custom_call_target="tpu_custom_call" | custom-call | tf_op jit(solution)/shard_map/encode/pallas_call | solution.py:156
  75.0 1.4 collective-permute-start.7
  76.4 1.6 collective-permute-start.8
  78.0 2.6 %collective-permute-start.9 = (bf16[1,192,1024]{2,1,0:T(8,128)(2,1)S(1)}, bf16[1,192,1024]{2,1,0:T(8,128)(2,1)S(1)}, u32[]{:S(2)}, u32[]{:S(2)}) collective-permute-start(bf16[1,192,1024]{2,1,0:T(8,128)(2,1)S(1)} %add_convert_fusion.5.refs_4_), channel_id=1, source_target_pairs={{0,8},{4,12},{8,0},{12,4},{1,9},{5,13},{9,1},{13,5},{2,10},{6,14},... | collective-permute-start | bytes 1179656 | tf_op jit(solution)/shard_map/ppermute | solution.py:330
  80.7 4.5 %decode.8 = (bf16[1,192,1024]{2,1,0:T(8,128)(2,1)S(1)}, bf16[1,192,1024]{2,1,0:T(8,128)(2,1)S(1)}) custom-call(s32[2]{0:T(128)S(1)} %get-tuple-element.61.info_ref, bf16[384,2048]{1,0:T(8,128)(2,1)S(1)} %encode.3.refs_0_, bf16[384,2048]{1,0:T(8,128)(2,1)S(1)} %collective-permute-done.7.refs_1_, bf16[2048,4096]{1,0:T(8,128)(2,1)} %bitcast.29, ...), custom_call_target="tpu_custom_call" | custom-call | tf_op jit(solution)/shard_map/decode/pallas_call | solution.py:255
  85.8 1.5 collective-permute-start.11
  87.3 6.3 %collective-permute-done.8 = bf16[1,192,1024]{2,1,0:T(8,128)(2,1)S(1)} collective-permute-done((bf16[1,192,1024]{2,1,0:T(8,128)(2,1)S(1)}, bf16[1,192,1024]{2,1,0:T(8,128)(2,1)S(1)}, u32[]{:S(2)}, u32[]{:S(2)}) %collective-permute-start.8) | collective-permute-done | bytes 393248 | tf_op jit(solution)/shard_map/ppermute | solution.py:330
  93.9 4.5 %decode.9 = (f32[1,192,1024]{2,1,0:T(8,128)S(1)}, bf16[1,192,1024]{2,1,0:T(8,128)(2,1)S(1)}) custom-call(s32[2]{0:T(128)S(1)} %pad_add_fusion.5.info_ref, bf16[384,2048]{1,0:T(8,128)(2,1)S(1)} %encode.3.refs_0_, bf16[384,2048]{1,0:T(8,128)(2,1)S(1)} %collective-permute-done.7.refs_1_, bf16[2048,4096]{1,0:T(8,128)(2,1)} %bitcast.30, ...), custom_call_target="tpu_custom_call" | custom-call | tf_op jit(solution)/shard_map/decode/pallas_call | solution.py:255
  98.4 1.8 %collective-permute-done.10 = bf16[1,192,1024]{2,1,0:T(8,128)(2,1)S(1)} collective-permute-done((bf16[1,192,1024]{2,1,0:T(8,128)(2,1)S(1)}, bf16[1,192,1024]{2,1,0:T(8,128)(2,1)S(1)}, u32[]{:S(2)}, u32[]{:S(2)}) %collective-permute-start.10) | collective-permute-done | bytes 393248 | tf_op jit(solution)/shard_map/ppermute | solution.py:330
  100.3 2.7 %collective-permute-start.20 = (bf16[1,192,1024]{2,1,0:T(8,128)(2,1)S(1)}, bf16[1,192,1024]{2,1,0:T(8,128)(2,1)S(1)}, u32[]{:S(2)}, u32[]{:S(2)}) collective-permute-start(bf16[1,192,1024]{2,1,0:T(8,128)(2,1)S(1)} %add_convert_fusion.4.refs_4_), channel_id=1, source_target_pairs={{0,8},{4,12},{8,0},{12,4},{1,9},{5,13},{9,1},{13,5},{2,10},{6,14},... | collective-permute-start | bytes 1179656 | tf_op jit(solution)/shard_map/ppermute | solution.py:330
  103.1 4.5 %decode.10 = (bf16[1,96,1024]{2,1,0:T(8,128)(2,1)S(1)}, bf16[1,96,1024]{2,1,0:T(8,128)(2,1)S(1)}, bf16[1,192,1024]{2,1,0:T(8,128)(2,1)S(1)}) custom-call(s32[2]{0:T(128)S(1)} %pad_add_fusion.4.info_ref, bf16[384,2048]{1,0:T(8,128)(2,1)S(1)} %encode.3.refs_0_, bf16[384,2048]{1,0:T(8,128)(2,1)S(1)} %collective-permute-done.7.refs_1_, ...), custom_call_target="tpu_custom_call" | custom-call | tf_op jit(solution)/shard_map/decode/pallas_call | solution.py:255
  107.6 1.6 collective-permute-start.18
  109.7 1.5 collective-permute-start.15
  111.2 1.5 collective-permute-start.16
  112.7 4.7 %decode.11 = (f32[1,192,1024]{2,1,0:T(8,128)S(1)}, bf16[1,192,1024]{2,1,0:T(8,128)(2,1)S(1)}) custom-call(s32[2]{0:T(128)S(1)} %get-tuple-element.60.info_ref, bf16[384,2048]{1,0:T(8,128)(2,1)S(1)} %encode.3.refs_0_, bf16[384,2048]{1,0:T(8,128)(2,1)S(1)} %collective-permute-done.7.refs_1_, bf16[2048,4096]{1,0:T(8,128)(2,1)} %bitcast.32, ...), custom_call_target="tpu_custom_call" | custom-call | tf_op jit(solution)/shard_map/decode/pallas_call | solution.py:255
  117.4 4.7 %collective-permute-done.18 = bf16[1,96,1024]{2,1,0:T(8,128)(2,1)S(1)} collective-permute-done((bf16[1,96,1024]{2,1,0:T(8,128)(2,1)S(1)}, bf16[1,96,1024]{2,1,0:T(8,128)(2,1)S(1)}, u32[]{:S(2)}, u32[]{:S(2)}) %collective-permute-start.18) | collective-permute-done | bytes 196640 | tf_op jit(solution)/shard_map/ppermute | solution.py:330
  122.1 1.5 collective-permute-start.13
  123.6 2.7 %collective-permute-done.19 = bf16[1,96,1024]{2,1,0:T(8,128)(2,1)S(1)} collective-permute-done((bf16[1,96,1024]{2,1,0:T(8,128)(2,1)S(1)}, bf16[1,96,1024]{2,1,0:T(8,128)(2,1)S(1)}, u32[]{:S(2)}, u32[]{:S(2)}) %collective-permute-start.19) | collective-permute-done | bytes 196640 | tf_op jit(solution)/shard_map/ppermute | solution.py:330
  126.3 1.5 collective-permute-start.12
  128.6 5.8 %collective-permute-done.16 = bf16[1,192,1024]{2,1,0:T(8,128)(2,1)S(1)} collective-permute-done((bf16[1,192,1024]{2,1,0:T(8,128)(2,1)S(1)}, bf16[1,192,1024]{2,1,0:T(8,128)(2,1)S(1)}, u32[]{:S(2)}, u32[]{:S(2)}) %collective-permute-start.16) | collective-permute-done | bytes 393248 | tf_op jit(solution)/shard_map/ppermute | solution.py:330
  134.6 0.9 collective-permute-start.17
  135.5 2.5 %collective-permute-start.14 = (bf16[1,192,1024]{2,1,0:T(8,128)(2,1)S(1)}, bf16[1,192,1024]{2,1,0:T(8,128)(2,1)S(1)}, u32[]{:S(2)}, u32[]{:S(2)}) collective-permute-start(bf16[1,192,1024]{2,1,0:T(8,128)(2,1)S(1)} %add_convert_fusion.2), channel_id=1, source_target_pairs={{0,4},{4,0},{8,12},{12,8},{1,5},{5,1},{9,13},{13,9},{2,6},{6,2},{1... | collective-permute-start | bytes 1179656 | tf_op jit(solution)/shard_map/ppermute | solution.py:330
  138.1 4.5 %collective-permute-done.12 = bf16[1,192,1024]{2,1,0:T(8,128)(2,1)S(1)} collective-permute-done((bf16[1,192,1024]{2,1,0:T(8,128)(2,1)S(1)}, bf16[1,192,1024]{2,1,0:T(8,128)(2,1)S(1)}, u32[]{:S(2)}, u32[]{:S(2)}) %collective-permute-start.12) | collective-permute-done | bytes 393248 | tf_op jit(solution)/shard_map/ppermute | solution.py:325
  142.6 6.8 %collective-permute-done.21.refs_5_ = bf16[192,1024]{1,0:T(8,128)(2,1)S(1)} collective-permute-done((bf16[192,1024]{1,0:T(8,128)(2,1)S(1)}, bf16[192,1024]{1,0:T(8,128)(2,1)S(1)}, u32[]{:S(2)}, u32[]{:S(2)}) %collective-permute-start.21) | collective-permute-done | bytes 393248 | tf_op jit(solution)/shard_map/ppermute | solution.py:325
  149.3 5.2 %collective-permute-done.17 = bf16[1,192,1024]{2,1,0:T(8,128)(2,1)S(1)} collective-permute-done((bf16[1,192,1024]{2,1,0:T(8,128)(2,1)S(1)}, bf16[1,192,1024]{2,1,0:T(8,128)(2,1)S(1)}, u32[]{:S(2)}, u32[]{:S(2)}) %collective-permute-start.17) | collective-permute-done | bytes 393248 | tf_op jit(solution)/shard_map/ppermute | solution.py:330
  154.9 1.6 finale.1
  156.5 1.5 collective-permute-start.23
  158.0 1.4 collective-permute-start.24
  160.8 2.1 %collective-permute-start.26 = (f32[8,128]{1,0:T(8,128)S(1)}, f32[8,128]{1,0:T(8,128)S(1)}, u32[]{:S(2)}, u32[]{:S(2)}) collective-permute-start(f32[8,128]{1,0:T(8,128)S(1)} %add_add_fusion.1), channel_id=1, source_target_pairs={{0,8},{4,12},{8,0},{12,4},{1,9},{5,13},{9,1},{13,5},{2,10},{6,14},... | collective-permute-start | bytes 12296 | tf_op jit(solution)/shard_map/ppermute | solution.py:325
  162.9 1.8 %collective-permute-start.27 = (f32[8,128]{1,0:T(8,128)S(1)}, f32[8,128]{1,0:T(8,128)S(1)}, u32[]{:S(2)}, u32[]{:S(2)}) collective-permute-start(f32[8,128]{1,0:T(8,128)S(1)} %add_add_fusion.1), channel_id=1, source_target_pairs={{0,12},{4,0},{8,4},{12,8},{1,13},{5,1},{9,5},{13,9},{2,14},{6,2},{... | collective-permute-start | bytes 12296 | tf_op jit(solution)/shard_map/ppermute | solution.py:325
  164.6 1.6 collective-permute-done.25
  166.8 0.7 fusion.1
  (55 shorter events, 5.4 us)
Async XLA Ops:
  0.6 12.1 %copy-start = (bf16[1,4096]{1,0:T(2,128)(2,1)S(1)}, bf16[1,4096]{1,0:T(2,128)(2,1)}, u32[]{:S(2)}) copy-start(bf16[1,4096]{1,0:T(2,128)(2,1)} %param.10) | copy-start | bytes 24580
  4.6 4.6 %collective-permute-start = (f32[1]{0:T(128)}, f32[1]{0:T(128)}, u32[]{:S(2)}, u32[]{:S(2)}) collective-permute-start(f32[1]{0:T(128)} %get-tuple-element.28), channel_id=1, source_target_pairs={{0,2},{2,0},{1,3},{3,1},{4,6},{6,4},{5,7},{7,5},{8,10},{10,8},{9,1... | collective-permute-start | bytes 20 | tf_op jit(solution)/shard_map/ppermute | solution.py:325
  10.6 23.7 %collective-permute-start.3 = (bf16[112,4096]{1,0:T(8,128)(2,1)}, bf16[112,4096]{1,0:T(8,128)(2,1)}, u32[]{:S(2)}, u32[]{:S(2)}) collective-permute-start(bf16[112,4096]{1,0:T(8,128)(2,1)} %get-tuple-element.35), channel_id=1, source_target_pairs={{0,2},{2,0},{1,3},{3,1},{4,6},{6,4},{5,7},{7,5},{8,10},{10,8},{9,1... | collective-permute-start | bytes 2752520 | tf_op jit(solution)/shard_map/ppermute | solution.py:325
  24.5 11.9 %collective-permute-start.1 = (bf16[384,1024]{1,0:T(8,128)(2,1)S(1)}, bf16[384,1024]{1,0:T(8,128)(2,1)S(1)}, u32[]{:S(2)}, u32[]{:S(2)}) collective-permute-start(bf16[384,1024]{1,0:T(8,128)(2,1)S(1)} %get-tuple-element.29.refs_0_), channel_id=1, source_target_pairs={{0,1},{2,3},{4,5},{6,7},{8,9},{10,11},{12,13},{14,15},{16,17},{18,... | collective-permute-start | bytes 2359304 | tf_op jit(solution)/shard_map/ppermute | solution.py:393
  25.9 10.6 %collective-permute-start.2 = (bf16[384,1024]{1,0:T(8,128)(2,1)S(1)}, bf16[384,1024]{1,0:T(8,128)(2,1)S(1)}, u32[]{:S(2)}, u32[]{:S(2)}) collective-permute-start(bf16[384,1024]{1,0:T(8,128)(2,1)S(1)} %get-tuple-element.30.refs_1_), channel_id=1, source_target_pairs={{0,1},{2,3},{4,5},{6,7},{8,9},{10,11},{12,13},{14,15},{16,17},{18,... | collective-permute-start | bytes 2359304 | tf_op jit(solution)/shard_map/ppermute | solution.py:393
  27.2 35.5 %collective-permute-start.5 = (bf16[160,4096]{1,0:T(8,128)(2,1)}, bf16[160,4096]{1,0:T(8,128)(2,1)}, u32[]{:S(2)}, u32[]{:S(2)}) collective-permute-start(bf16[160,4096]{1,0:T(8,128)(2,1)} %get-tuple-element.36), channel_id=1, source_target_pairs={{0,2},{2,0},{1,3},{3,1},{4,6},{6,4},{5,7},{7,5},{8,10},{10,8},{9,1... | collective-permute-start | bytes 3932168 | tf_op jit(solution)/shard_map/ppermute | solution.py:325
  34.3 28.4 %collective-permute-start.4 = (bf16[112,4096]{1,0:T(8,128)(2,1)}, bf16[112,4096]{1,0:T(8,128)(2,1)}, u32[]{:S(2)}, u32[]{:S(2)}) collective-permute-start(bf16[112,4096]{1,0:T(8,128)(2,1)} %collective-permute-done.3.refs_0_), channel_id=1, source_target_pairs={{0,4},{4,0},{8,12},{12,8},{1,5},{5,1},{9,13},{13,9},{2,6},{6,2},{1... | collective-permute-start | bytes 2752520 | tf_op jit(solution)/shard_map/ppermute | solution.py:330
  43.5 0.9 copy-start.3
  44.4 0.9 copy-start.5
  45.3 0.8 copy-start.8
  46.1 15.5 %collective-permute-start.6 = (bf16[1,192,1024]{2,1,0:T(8,128)(2,1)S(1)}, bf16[1,192,1024]{2,1,0:T(8,128)(2,1)}, u32[]{:S(2)}, u32[]{:S(2)}) collective-permute-start(bf16[1,192,1024]{2,1,0:T(8,128)(2,1)S(1)} %get-tuple-element.31.refs_6_), channel_id=1, source_target_pairs={{0,4},{4,0},{8,12},{12,8},{1,5},{5,1},{9,13},{13,9},{2,6},{6,2},{1... | collective-permute-start | bytes 1179656 | tf_op jit(solution)/shard_map/ppermute | solution.py:330
  62.6 13.7 %copy-start.9 = (bf16[1,192,1024]{2,1,0:T(8,128)(2,1)S(1)}, bf16[1,192,1024]{2,1,0:T(8,128)(2,1)}, u32[]{:S(2)}) copy-start(bf16[1,192,1024]{2,1,0:T(8,128)(2,1)} %copy-done.8) | copy-start | bytes 1179652
  75.0 5.8 %collective-permute-start.7 = (bf16[384,2048]{1,0:T(8,128)(2,1)S(1)}, bf16[384,2048]{1,0:T(8,128)(2,1)S(1)}, u32[]{:S(2)}, u32[]{:S(2)}) collective-permute-start(bf16[384,2048]{1,0:T(8,128)(2,1)S(1)} %encode.3.refs_0_), channel_id=1, source_target_pairs={{0,1},{2,3},{4,5},{6,7},{8,9},{10,11},{12,13},{14,15},{16,17},{18,... | collective-permute-start | bytes 4718600 | tf_op jit(solution)/shard_map/ppermute | solution.py:393
  76.4 17.2 %collective-permute-start.8 = (bf16[1,192,1024]{2,1,0:T(8,128)(2,1)S(1)}, bf16[1,192,1024]{2,1,0:T(8,128)(2,1)S(1)}, u32[]{:S(2)}, u32[]{:S(2)}) collective-permute-start(bf16[1,192,1024]{2,1,0:T(8,128)(2,1)S(1)} %copy-done.9), channel_id=1, source_target_pairs={{0,4},{4,0},{8,12},{12,8},{1,5},{5,1},{9,13},{13,9},{2,6},{6,2},{1... | collective-permute-start | bytes 1179656 | tf_op jit(solution)/shard_map/ppermute | solution.py:330
  78.0 15.7 %collective-permute-start.9 = (bf16[1,192,1024]{2,1,0:T(8,128)(2,1)S(1)}, bf16[1,192,1024]{2,1,0:T(8,128)(2,1)S(1)}, u32[]{:S(2)}, u32[]{:S(2)}) collective-permute-start(bf16[1,192,1024]{2,1,0:T(8,128)(2,1)S(1)} %add_convert_fusion.5.refs_4_), channel_id=1, source_target_pairs={{0,8},{4,12},{8,0},{12,4},{1,9},{5,13},{9,1},{13,5},{2,10},{6,14},... | collective-permute-start | bytes 1179656 | tf_op jit(solution)/shard_map/ppermute | solution.py:330
  85.2 14.9 %collective-permute-start.10 = (bf16[1,192,1024]{2,1,0:T(8,128)(2,1)S(1)}, bf16[1,192,1024]{2,1,0:T(8,128)(2,1)S(1)}, u32[]{:S(2)}, u32[]{:S(2)}) collective-permute-start(bf16[1,192,1024]{2,1,0:T(8,128)(2,1)S(1)} %get-tuple-element.38.refs_4_), channel_id=1, source_target_pairs={{0,4},{4,0},{8,12},{12,8},{1,5},{5,1},{9,13},{13,9},{2,6},{6,2},{1... | collective-permute-start | bytes 1179656 | tf_op jit(solution)/shard_map/ppermute | solution.py:330
  85.8 17.2 %collective-permute-start.11 = (bf16[1,192,1024]{2,1,0:T(8,128)(2,1)S(1)}, bf16[1,192,1024]{2,1,0:T(8,128)(2,1)S(1)}, u32[]{:S(2)}, u32[]{:S(2)}) collective-permute-start(bf16[1,192,1024]{2,1,0:T(8,128)(2,1)S(1)} %get-tuple-element.43), channel_id=1, source_target_pairs={{0,2},{2,0},{1,3},{3,1},{4,6},{6,4},{5,7},{7,5},{8,10},{10,8},{9,1... | collective-permute-start | bytes 1179656 | tf_op jit(solution)/shard_map/ppermute | solution.py:325
  98.4 4.6 %copy-start.6 = (f32[1,192,1024]{2,1,0:T(8,128)S(1)}, f32[1,192,1024]{2,1,0:T(8,128)}, u32[]{:S(2)}) copy-start(f32[1,192,1024]{2,1,0:T(8,128)} %copy-done.5) | copy-start | bytes 2359300
  100.3 27.5 %collective-permute-start.20 = (bf16[1,192,1024]{2,1,0:T(8,128)(2,1)S(1)}, bf16[1,192,1024]{2,1,0:T(8,128)(2,1)S(1)}, u32[]{:S(2)}, u32[]{:S(2)}) collective-permute-start(bf16[1,192,1024]{2,1,0:T(8,128)(2,1)S(1)} %add_convert_fusion.4.refs_4_), channel_id=1, source_target_pairs={{0,8},{4,12},{8,0},{12,4},{1,9},{5,13},{9,1},{13,5},{2,10},{6,14},... | collective-permute-start | bytes 1179656 | tf_op jit(solution)/shard_map/ppermute | solution.py:330
  107.6 14.5 %collective-permute-start.18 = (bf16[1,96,1024]{2,1,0:T(8,128)(2,1)S(1)}, bf16[1,96,1024]{2,1,0:T(8,128)(2,1)S(1)}, u32[]{:S(2)}, u32[]{:S(2)}) collective-permute-start(bf16[1,96,1024]{2,1,0:T(8,128)(2,1)S(1)} %get-tuple-element.44.refs_4_), channel_id=1, source_target_pairs={{0,4},{4,0},{8,12},{12,8},{1,5},{5,1},{9,13},{13,9},{2,6},{6,2},{1... | collective-permute-start | bytes 589832 | tf_op jit(solution)/shard_map/ppermute | solution.py:330
  109.2 17.1 %collective-permute-start.19 = (bf16[1,96,1024]{2,1,0:T(8,128)(2,1)S(1)}, bf16[1,96,1024]{2,1,0:T(8,128)(2,1)S(1)}, u32[]{:S(2)}, u32[]{:S(2)}) collective-permute-start(bf16[1,96,1024]{2,1,0:T(8,128)(2,1)S(1)} %get-tuple-element.45.refs_5_), channel_id=1, source_target_pairs={{0,4},{4,0},{8,12},{12,8},{1,5},{5,1},{9,13},{13,9},{2,6},{6,2},{1... | collective-permute-start | bytes 589832 | tf_op jit(solution)/shard_map/ppermute | solution.py:330
  109.7 18.9 %collective-permute-start.15 = (bf16[1,192,1024]{2,1,0:T(8,128)(2,1)S(1)}, bf16[1,192,1024]{2,1,0:T(8,128)(2,1)S(1)}, u32[]{:S(2)}, u32[]{:S(2)}) collective-permute-start(bf16[1,192,1024]{2,1,0:T(8,128)(2,1)S(1)} %get-tuple-element.50), channel_id=1, source_target_pairs={{0,2},{2,0},{1,3},{3,1},{4,6},{6,4},{5,7},{7,5},{8,10},{10,8},{9,1... | collective-permute-start | bytes 1179656 | tf_op jit(solution)/shard_map/ppermute | solution.py:325
  111.2 23.2 %collective-permute-start.16 = (bf16[1,192,1024]{2,1,0:T(8,128)(2,1)S(1)}, bf16[1,192,1024]{2,1,0:T(8,128)(2,1)S(1)}, u32[]{:S(2)}, u32[]{:S(2)}) collective-permute-start(bf16[1,192,1024]{2,1,0:T(8,128)(2,1)S(1)} %add_convert_fusion.3.refs_5_), channel_id=1, source_target_pairs={{0,4},{4,0},{8,12},{12,8},{1,5},{5,1},{9,13},{13,9},{2,6},{6,2},{1... | collective-permute-start | bytes 1179656 | tf_op jit(solution)/shard_map/ppermute | solution.py:330
  122.1 13.3 %collective-permute-start.13 = (bf16[1,192,1024]{2,1,0:T(8,128)(2,1)S(1)}, bf16[1,192,1024]{2,1,0:T(8,128)(2,1)S(1)}, u32[]{:S(2)}, u32[]{:S(2)}) collective-permute-start(bf16[1,192,1024]{2,1,0:T(8,128)(2,1)S(1)} %get-tuple-element.48), channel_id=1, source_target_pairs={{0,2},{2,0},{1,3},{3,1},{4,6},{6,4},{5,7},{7,5},{8,10},{10,8},{9,1... | collective-permute-start | bytes 1179656 | tf_op jit(solution)/shard_map/ppermute | solution.py:325
  126.3 16.3 %collective-permute-start.12 = (bf16[1,192,1024]{2,1,0:T(8,128)(2,1)S(1)}, bf16[1,192,1024]{2,1,0:T(8,128)(2,1)S(1)}, u32[]{:S(2)}, u32[]{:S(2)}) collective-permute-start(bf16[1,192,1024]{2,1,0:T(8,128)(2,1)S(1)} %get-tuple-element.46), channel_id=1, source_target_pairs={{0,2},{2,0},{1,3},{3,1},{4,6},{6,4},{5,7},{7,5},{8,10},{10,8},{9,1... | collective-permute-start | bytes 1179656 | tf_op jit(solution)/shard_map/ppermute | solution.py:325
  127.8 7.6 %copy-start.4 = (f32[1,192,1024]{2,1,0:T(8,128)S(1)}, f32[1,192,1024]{2,1,0:T(8,128)}, u32[]{:S(2)}) copy-start(f32[1,192,1024]{2,1,0:T(8,128)} %copy-done.3) | copy-start | bytes 2359300
  128.0 21.3 %collective-permute-start.21 = (bf16[192,1024]{1,0:T(8,128)(2,1)S(1)}, bf16[192,1024]{1,0:T(8,128)(2,1)S(1)}, u32[]{:S(2)}, u32[]{:S(2)}) collective-permute-start(bf16[192,1024]{1,0:T(8,128)(2,1)S(1)} %fusion), channel_id=1, source_target_pairs={{0,2},{2,0},{1,3},{3,1},{4,6},{6,4},{5,7},{7,5},{8,10},{10,8},{9,1... | collective-permute-start | bytes 1179656 | tf_op jit(solution)/shard_map/ppermute | solution.py:325
  134.4 20.5 %copy-start.2 = (bf16[1,384,1024]{2,1,0:T(8,128)(2,1)S(1)}, bf16[1,384,1024]{2,1,0:T(8,128)(2,1)}, u32[]{:S(2)}) copy-start(bf16[1,384,1024]{2,1,0:T(8,128)(2,1)} %param.8) | copy-start | bytes 2359300
  134.4 20.5 %copy-start.7 = (bf16[1,1024]{1,0:T(2,128)(2,1)S(1)}, bf16[1,1024]{1,0:T(2,128)(2,1)}, u32[]{:S(2)}) copy-start(bf16[1,1024]{1,0:T(2,128)(2,1)} %b_ref.1) | copy-start | bytes 6148
  134.6 20.0 %collective-permute-start.17 = (bf16[1,192,1024]{2,1,0:T(8,128)(2,1)S(1)}, bf16[1,192,1024]{2,1,0:T(8,128)(2,1)S(1)}, u32[]{:S(2)}, u32[]{:S(2)}) collective-permute-start(bf16[1,192,1024]{2,1,0:T(8,128)(2,1)S(1)} %add_convert_fusion.1), channel_id=1, source_target_pairs={{0,8},{4,12},{8,0},{12,4},{1,9},{5,13},{9,1},{13,5},{2,10},{6,14},... | collective-permute-start | bytes 1179656 | tf_op jit(solution)/shard_map/ppermute | solution.py:330
  135.5 19.3 %collective-permute-start.14 = (bf16[1,192,1024]{2,1,0:T(8,128)(2,1)S(1)}, bf16[1,192,1024]{2,1,0:T(8,128)(2,1)S(1)}, u32[]{:S(2)}, u32[]{:S(2)}) collective-permute-start(bf16[1,192,1024]{2,1,0:T(8,128)(2,1)S(1)} %add_convert_fusion.2), channel_id=1, source_target_pairs={{0,4},{4,0},{8,12},{12,8},{1,5},{5,1},{9,13},{13,9},{2,6},{6,2},{1... | collective-permute-start | bytes 1179656 | tf_op jit(solution)/shard_map/ppermute | solution.py:330
  154.9 15.2 %copy-start.1 = (bf16[1,4096]{1,0:T(2,128)(2,1)S(1)}, bf16[1,4096]{1,0:T(2,128)(2,1)}, u32[]{:S(2)}) copy-start(bf16[1,4096]{1,0:T(2,128)(2,1)} %param.10) | copy-start | bytes 24580
  156.5 3.0 %collective-permute-start.22 = (f32[8,128]{1,0:T(8,128)S(1)}, f32[8,128]{1,0:T(8,128)S(1)}, u32[]{:S(2)}, u32[]{:S(2)}) collective-permute-start(f32[8,128]{1,0:T(8,128)S(1)} %get-tuple-element.53), channel_id=1, source_target_pairs={{0,1},{1,2},{2,3},{3,0},{4,5},{5,6},{6,7},{7,4},{8,9},{9,10},{10,1... | collective-permute-start | bytes 12296 | tf_op jit(solution)/shard_map/ppermute | solution.py:325
  156.5 3.6 %collective-permute-start.23 = (f32[8,128]{1,0:T(8,128)S(1)}, f32[8,128]{1,0:T(8,128)S(1)}, u32[]{:S(2)}, u32[]{:S(2)}) collective-permute-start(f32[8,128]{1,0:T(8,128)S(1)} %get-tuple-element.53), channel_id=1, source_target_pairs={{0,2},{1,3},{2,0},{3,1},{4,6},{5,7},{6,4},{7,5},{8,10},{9,11},{10,... | collective-permute-start | bytes 12296 | tf_op jit(solution)/shard_map/ppermute | solution.py:325
  158.0 2.8 %collective-permute-start.24 = (f32[8,128]{1,0:T(8,128)S(1)}, f32[8,128]{1,0:T(8,128)S(1)}, u32[]{:S(2)}, u32[]{:S(2)}) collective-permute-start(f32[8,128]{1,0:T(8,128)S(1)} %get-tuple-element.53), channel_id=1, source_target_pairs={{0,3},{1,0},{2,1},{3,2},{4,7},{5,4},{6,5},{7,6},{8,11},{9,8},{10,9... | collective-permute-start | bytes 12296 | tf_op jit(solution)/shard_map/ppermute | solution.py:325
  160.8 5.4 %collective-permute-start.25 = (f32[8,128]{1,0:T(8,128)S(1)}, f32[8,128]{1,0:T(8,128)S(1)}, u32[]{:S(2)}, u32[]{:S(2)}) collective-permute-start(f32[8,128]{1,0:T(8,128)S(1)} %add_add_fusion.1), channel_id=1, source_target_pairs={{0,4},{4,8},{8,12},{12,0},{1,5},{5,9},{9,13},{13,1},{2,6},{6,10},{... | collective-permute-start | bytes 12296 | tf_op jit(solution)/shard_map/ppermute | solution.py:325
  160.8 5.4 %collective-permute-start.26 = (f32[8,128]{1,0:T(8,128)S(1)}, f32[8,128]{1,0:T(8,128)S(1)}, u32[]{:S(2)}, u32[]{:S(2)}) collective-permute-start(f32[8,128]{1,0:T(8,128)S(1)} %add_add_fusion.1), channel_id=1, source_target_pairs={{0,8},{4,12},{8,0},{12,4},{1,9},{5,13},{9,1},{13,5},{2,10},{6,14},... | collective-permute-start | bytes 12296 | tf_op jit(solution)/shard_map/ppermute | solution.py:325
  162.9 3.9 %collective-permute-start.27 = (f32[8,128]{1,0:T(8,128)S(1)}, f32[8,128]{1,0:T(8,128)S(1)}, u32[]{:S(2)}, u32[]{:S(2)}) collective-permute-start(f32[8,128]{1,0:T(8,128)S(1)} %add_add_fusion.1), channel_id=1, source_target_pairs={{0,12},{4,0},{8,4},{12,8},{1,13},{5,1},{9,5},{13,9},{2,14},{6,2},{... | collective-permute-start | bytes 12296 | tf_op jit(solution)/shard_map/ppermute | solution.py:325

commit v8 on v7

--- a/solution.py
+++ b/solution.py
@@ -18,23 +18,17 @@
     return tile
 
 
-def prepare(x, side, edge):
+def square_sum(x):
     rows, width = x.shape
-    middle = rows - 2 * edge
     lanes = tile_of(width, 1024)
     loads = 4
     piece = rows // loads
 
-    def body(side_ref, x_ref, outer_ref, inner_ref, o_ref, held, sem, out_sem):
+    def body(x_ref, o_ref, held, sem):
         def load(i):
             place = pl.ds(i * piece, piece)
             return pltpu.make_async_copy(x_ref.at[place], held.at[place], sem.at[i])
 
-        first = pl.ds(pl.multiple_of(side_ref[0] * (rows - edge), 16), edge)
-        cuts = [
-            pltpu.make_async_copy(held.at[first], outer_ref, out_sem.at[0]),
-            pltpu.make_async_copy(held.at[pl.ds(edge, middle)], inner_ref, out_sem.at[1]),
-        ]
         for i in range(loads):
             load(i).start()
         total = jnp.zeros((8, lanes), jnp.float32)
@@ -48,30 +42,61 @@
                     return acc + value[:8] + value[8:]
 
                 total = lax.fori_loop(0, piece // 16, add, total, unroll=2)
-        for copy in cuts:
-            copy.start()
         o_ref[0] = jnp.sum(total)
-        for copy in cuts:
-            copy.wait()
 
     return pl.pallas_call(
         body,
-        in_specs=[pl.BlockSpec(memory_space=pltpu.SMEM), pl.BlockSpec(memory_space=pl.ANY)],
-        out_specs=[pl.BlockSpec(memory_space=pl.ANY)] * 2 + [pl.BlockSpec(memory_space=pltpu.SMEM)],
-        out_shape=[
-            pltpu.HBM((edge, width), x.dtype),
-            pltpu.HBM((middle, width), x.dtype),
-            jax.ShapeDtypeStruct((1,), jnp.float32),
+        in_specs=[pl.BlockSpec(memory_space=pl.ANY)],
+        out_specs=pl.BlockSpec(memory_space=pltpu.SMEM),
+        out_shape=jax.ShapeDtypeStruct((1,), jnp.float32),
+        scratch_shapes=[pltpu.VMEM((rows, width), x.dtype), pltpu.SemaphoreType.DMA((loads,))],
+        compiler_params=pltpu.CompilerParams(vmem_limit_bytes=VMEM_LIMIT),
+        cost_estimate=COST,
+        name="square_sum",
+    )(x)
+
+
+def cut(x, side, edge, after):
+    rows, width = x.shape
+    middle = rows - 2 * edge
+
+    def body(side_ref, after_ref, x_ref, outer_ref, inner_ref, first, second, sem, out_sem):
+        start = pl.multiple_of(side_ref[0] * (rows - edge), 16)
+        loads = [
+            pltpu.make_async_copy(x_ref.at[pl.ds(start, edge)], first, sem.at[0]),
+            pltpu.make_async_copy(x_ref.at[pl.ds(edge, middle)], second, sem.at[1]),
+        ]
+        stores = [
+            pltpu.make_async_copy(first, outer_ref, out_sem.at[0]),
+            pltpu.make_async_copy(second, inner_ref, out_sem.at[1]),
+        ]
+        for load in loads:
+            load.start()
+        for load, store in zip(loads, stores):
+            load.wait()
+            store.start()
+        for store in stores:
+            store.wait()
+
+    return pl.pallas_call(
+        body,
+        in_specs=[
+            pl.BlockSpec(memory_space=pltpu.SMEM),
+            pl.BlockSpec(memory_space=pltpu.SMEM),
+            pl.BlockSpec(memory_space=pl.ANY),
         ],
+        out_specs=[pl.BlockSpec(memory_space=pl.ANY)] * 2,
+        out_shape=[pltpu.HBM((edge, width), x.dtype), pltpu.HBM((middle, width), x.dtype)],
         scratch_shapes=[
-            pltpu.VMEM((rows, width), x.dtype),
-            pltpu.SemaphoreType.DMA((loads,)),
+            pltpu.VMEM((edge, width), x.dtype),
+            pltpu.VMEM((middle, width), x.dtype),
+            pltpu.SemaphoreType.DMA((2,)),
             pltpu.SemaphoreType.DMA((2,)),
         ],
         compiler_params=pltpu.CompilerParams(vmem_limit_bytes=VMEM_LIMIT),
         cost_estimate=COST,
-        name="prepare",
-    )(side.reshape(1), x)
+        name="cut",
+    )(side.reshape(1), after, x)
 
 
 def gate(values, after):
@@ -258,7 +283,8 @@
         + [pl.BlockSpec(memory_space=pl.ANY)] * (2 * parts + 2 + m),
         out_specs=[pl.BlockSpec(memory_space=pltpu.VMEM)] * len(outs),
         out_shape=[
-            jax.ShapeDtypeStruct((many, sum(height for _, height in spans), width), dtype)
+            (pltpu.HBM if dtype == jnp.float32 else jax.ShapeDtypeStruct)(
+                (many, sum(height for _, height in spans), width), dtype)
             for _, many, spans, dtype in outs
         ],
         scratch_shapes=[
@@ -275,14 +301,15 @@
 
 def finale(outer_terms, inner_terms, bias, target, layer):
     rows, width = target.shape
-    half, quarter = rows // 2, rows // 4
+    half = inner_terms[0].shape[0]
+    quarter = (rows - half) // 2
     n, m = len(outer_terms), len(inner_terms)
 
     def body(layer_ref, b_ref, t_ref, *refs):
         terms = {0: refs[:n], 1: refs[n:n + m]}
         r_ref, s_ref = refs[n + m:]
         bias = b_ref[...].astype(jnp.float32)
-        spans = [(0, 0, 0, quarter), (1, 0, quarter, half), (0, quarter, 3 * quarter, quarter)]
+        spans = [(0, 0, 0, quarter), (1, 0, quarter, half), (0, quarter, quarter + half, quarter)]
 
         def block(which, start, target_start):
             def run(r, sums):
@@ -357,11 +384,11 @@
     cross_w = in_hbm(dec_cross)
     lat_dev = enc_w.shape[1]
     width = dec_bias.shape[1]
-    quarter = rows // 4
     side = lat % 2
 
     edge = rows * 7 // 24 // 16 * 16
-    outer, inner, square = prepare(x_own, side.astype(jnp.int32), edge)
+    square = square_sum(x_own)
+    outer, inner = cut(x_own, side.astype(jnp.int32), edge, square)
     square = sum_over(square, "token")
     scale = jnp.sqrt(square / (rows * n_tok * model) + 1e-06)
     inv = 1.0 / scale
@@ -384,9 +411,8 @@
         blocks = [4 * i + 2 * high + low for high in highs for i in range(group)]
         return jnp.stack([layer] + blocks).astype(jnp.int32)
 
-
-    half = 2 * quarter
-    both = 2 * group
+    middle = rows * 7 // 12 // 16 * 16
+    first = (rows - middle) // 2
     narrow = jnp.bfloat16
 
     def earlier_of(codes):
@@ -411,22 +437,24 @@
 
     codes = encode([(x_own, 0, rows)], places(0), inv, enc_w, bias, 2, [])
     earlier = earlier_of(codes)
-    inside = ((quarter, half),)
-    outside = ((0, quarter), (3 * quarter, quarter))
+    inside = ((first, middle),)
+    outside = ((0, first), (rows - first, first))
     spans = [(0, group, inside), (group, group, inside), (0, group, outside), (group, group, outside)]
     far_sent, near_sent, far_out_sent, near_out_sent = products(
         codes, earlier, info(other, (far, near)),
         [span + (dtype,) for span, dtype in zip(spans, (narrow, narrow, jnp.float32, jnp.float32))], [])
     far_in = swapped(far_sent, "latent", 1)
     near_in = swapped(near_sent, "latent", 1)
-    far_kept, near_kept, far_out_kept, near_out_kept = products(
-        codes, earlier, info(mine_bit, (far, near)), [span + (jnp.float32,) for span in spans], [far_sent])
+    (far_kept, far_out_kept) = products(
+        codes, earlier, info(mine_bit, (far,)),
+        [(0, group, inside, jnp.float32), (0, group, outside, jnp.float32)], [far_sent])
     across_in = (far_kept + wide(far_in)).astype(narrow)
-    total_in = near_kept + wide(near_in) + wide(swapped(across_in, "latent", 2))
+    across_in_there = swapped(across_in, "latent", 2)
+    own = codes, earlier
 
     after = across_in
     returned = []
-    far_out_back, far_out_kept_back, near_out_back, near_out_kept_back = [], [], [], []
+    far_out_back, near_out_back, near_out_kept_back = [], [], []
 
     def joined(own, back):
         return own + sum(wide(part) for part in back)
@@ -444,7 +472,14 @@
                 [(0, group, span, dtype) for span in spans] + [(0, group, outside, narrow)], also)
             return insides, shifted(outer, "token", back)
 
-        (far_sent,), far_back = quarter_of(other, far, [inside], narrow, [])
+        before = []
+        if not returned:
+            near_own, near_out_kept = products(
+                *own, info(mine_bit, (near,)),
+                [(0, group, inside, jnp.float32), (0, group, outside, jnp.float32)], codes)
+            total_in = near_own + wide(near_in) + wide(across_in_there)
+            before = [near_own]
+        (far_sent,), far_back = quarter_of(other, far, [inside], narrow, before)
         far_in = swapped(far_sent, "latent", 1)
         (far_kept,), far_kept_back = quarter_of(mine_bit, far, [inside], jnp.float32, [far_sent, total_in])
         far_out_back.append(far_back)
@@ -453,20 +488,23 @@
         if len(far_out_back) == n_tok - 1:
             ready.append(joined(far_out_sent, far_out_back).astype(narrow))
             far_out = swapped(ready[1], "latent", 1)
-        halves = [((quarter, quarter),), ((2 * quarter, quarter),)]
+        halves = [((first + i * (middle // 2), middle // 2),) for i in range(2)]
         near_sent, near_back = quarter_of(other, near, halves, narrow, ready)
-        near_in = jnp.concatenate([swapped(part, "latent", 1) for part in near_sent], axis=1)
-        (near_kept,), near_kept_back = quarter_of(mine_bit, near, [inside], jnp.float32, near_sent)
+        near_in = jnp.concatenate([swapped(rows_in, "latent", 1) for rows_in in near_sent], axis=1)
+        far_out_kept = far_out_kept + wide(far_kept_back)
+        pins = list(near_sent)
+        if len(far_out_back) == n_tok - 1:
+            far_out_kept = (far_out_kept + wide(far_out)).astype(narrow)
+            pins.append(far_out_kept)
+        (near_kept,), near_kept_back = quarter_of(mine_bit, near, [inside], jnp.float32, pins)
         part = finish(near_kept + wide(near_in) + wide(across))
         returned.append(shifted(part.astype(narrow), "token", back))
-        far_out_kept_back.append(far_kept_back)
         near_out_back.append(near_back)
         near_out_kept_back.append(near_kept_back)
         after = near_kept
 
     near_out = swapped(joined(near_out_sent, near_out_back).astype(narrow), "latent", 1)
-    across_out = (joined(far_out_kept, far_out_kept_back) + wide(far_out)).astype(narrow)
-    across_out = swapped(across_out, "latent", 2)
+    across_out = swapped(far_out_kept, "latent", 2)
     if group == 1:
         outer_terms = [near_out_kept, *near_out_kept_back, near_out, across_out]
         outer_terms = [term[0] for term in outer_terms]

time: 171 us -> 180 us (1.053)
  Pallas kernels: 62.1 us -> 71.5 us
  starting transfers between devices: 39.1 us -> 34.9 us
  waiting for transfers between devices: 58.5 us -> 54.3 us
  other arithmetic: 2.29 us -> 5.89 us
  local copies, waits for them, and re-layouts: 3.23 us -> 6.43 us
    pallas_call x6 -> x7, Pallas kernels: 32.3 us -> 39.7 us  [decode(): pl.pallas_call(body, in_specs=[pl.BlockSpec(memory_space=pltpu.SMEM)] + [...]
    ppermute x14, waiting for transfers between devices: 23.3 us -> 16.7 us  [shifted(): lax.ppermute(value, axis, [(i, (i + distance) % n) for i in range(n)])]
    unnamed x20 -> x36, local copies, waits for them, and re-layouts: 2.57 us -> 5.77 us
    ppermute x11, starting transfers between devices: 16.5 us -> 13.7 us  [swapped(): return lax.ppermute(value, axis, [(i, i ^ bit) for i in range(n)])]
    ppermute x11, waiting for transfers between devices: 35.2 us -> 37.5 us  [swapped(): return lax.ppermute(value, axis, [(i, i ^ bit) for i in range(n)])]
    pallas_call x1 -> x2, Pallas kernels: 3.98 us -> 6.09 us  [the longest x1 3.37 us: cut(): pl.pallas_call(body, in_specs=[pl.BlockSpec(memory_space=pltpu.SMEM), pl....]
  transfers between devices with their start and end apart: 28 -> 28, of which waited for: 18 -> 15; matrix products, arithmetic and copies ran while one was open for 1% -> 3% of each run, Pallas kernels for 26% -> 31%
where the time goes in v8:
time: 180 us; the launch traced here: 179 us
  Pallas kernels  71.5 us (40%)
  waiting for transfers between devices  54.3 us (30%)
  starting transfers between devices  34.9 us (19%)
  local copies, waits for them, and re-layouts  6.43 us (4%)
  between operations  5.99 us (3%)
  other arithmetic  5.89 us (3%)
    pallas_call x7, Pallas kernels, decode(): pl.pallas_call(body, in_specs=[pl.BlockSpec(memory_space=pltpu.SMEM)] + [...  39.7 us
    ppermute x11, waiting for transfers between devices, swapped(): return lax.ppermute(value, axis, [(i, i ^ bit) for i in range(n)])  37.5 us
    pallas_call x2, Pallas kernels, encode(): pl.pallas_call(body, in_specs=[pl.BlockSpec(memory_space=pltpu.SMEM), pl....  24.1 us
    ppermute x14, starting transfers between devices, shifted(): lax.ppermute(value, axis, [(i, (i + distance) % n) for i in range(n)])  17.2 us
    ppermute x14, waiting for transfers between devices, shifted(): lax.ppermute(value, axis, [(i, (i + distance) % n) for i in range(n)])  16.7 us
    ppermute x11, starting transfers between devices, swapped(): return lax.ppermute(value, axis, [(i, i ^ bit) for i in range(n)])  13.7 us
    unnamed x36, local copies, waits for them, and re-layouts  5.77 us
    ppermute x3, starting transfers between devices, earlier_of(): return [lax.ppermute(part, 'layer', [(0, 1)]) for part in codes]  4.07 us
  transfers between devices with their start and end apart: 28, of which 15 were waited for; matrix products, arithmetic and copies ran while one was open for 3% of the time, Pallas kernels for 31%

profile of v8, /device:TPU:0, one launch (start us, length us, event | category | flops | bytes accessed | tf_op | source)
XLA Modules:
  0.0 179.0 jit_solution(13628065744473996496)
XLA Ops:
  0.6 2.7 %square_sum.1.after_ref = f32[1]{0:T(128)} custom-call(bf16[384,4096]{1,0:T(8,128)(2,1)} %bitcast.36), custom_call_target="tpu_custom_call" | custom-call | tf_op jit(solution)/shard_map/square_sum/pallas_call | solution.py:47
  3.4 3.0 %collective-permute-start = (f32[1]{0:T(128)}, f32[1]{0:T(128)}, u32[]{:S(2)}, u32[]{:S(2)}) collective-permute-start(f32[1]{0:T(128)} %square_sum.1.after_ref), channel_id=1, source_target_pairs={{0,2},{2,0},{1,3},{3,1},{4,6},{6,4},{5,7},{7,5},{8,10},{10,8},{9,1... | collective-permute-start | bytes 20 | tf_op jit(solution)/shard_map/ppermute | solution.py:352
  6.4 3.4 %cut.1 = (bf16[112,4096]{1,0:T(8,128)(2,1)}, bf16[160,4096]{1,0:T(8,128)(2,1)}) custom-call(s32[1]{0:T(128)} %bitcast.8.side_ref, f32[1]{0:T(128)} %square_sum.1.after_ref, bf16[384,4096]{1,0:T(8,128)(2,1)} %bitcast.37), custom_call_target="tpu_custom_call" | custom-call | tf_op jit(solution)/shard_map/cut/pallas_call | solution.py:81
  11.6 11.8 %encode.2 = (bf16[384,1024]{1,0:T(8,128)(2,1)S(1)}, bf16[384,1024]{1,0:T(8,128)(2,1)S(1)}) custom-call(s32[1]{0:T(128)} %constant.61.clone.1.places_ref, f32[1]{0:T(128)S(6)} %sqrt.3.inv_ref.after_ref, bf16[1,2048]{1,0:T(2,128)(2,1)S(1)} %constant_dynamic-slice_fusion.b_ref, bf16[384,4096]{1,0:T(8,128)(2,1)} %bitcast.38, bf16[4096,2048]{1,0:T(8,128)(2,1)} %bitcast.34), custom_call_target="tpu_custom_call" | custom-call | tf_op jit(solution)/shard_map/encode/pallas_call | solution.py:181
  23.4 1.3 collective-permute-start.1
  24.7 1.3 collective-permute-start.2
  26.1 1.7 collective-permute-start.5
  27.8 7.0 %collective-permute-done.3.refs_0_ = bf16[112,4096]{1,0:T(8,128)(2,1)} collective-permute-done((bf16[112,4096]{1,0:T(8,128)(2,1)}, bf16[112,4096]{1,0:T(8,128)(2,1)}, u32[]{:S(2)}, u32[]{:S(2)}) %collective-permute-start.3) | collective-permute-done | bytes 917536 | tf_op jit(solution)/shard_map/ppermute | solution.py:352
  34.7 1.6 collective-permute-start.4
  36.4 8.5 %decode.7 = (bf16[1,224,1024]{2,1,0:T(8,128)(2,1)}, bf16[1,224,1024]{2,1,0:T(8,128)(2,1)}, f32[1,160,1024]{2,1,0:T(8,128)}, f32[1,160,1024]{2,1,0:T(8,128)}) custom-call(s32[3]{0:T(128)S(1)} %pad_add_fusion.3.info_ref, bf16[384,1024]{1,0:T(8,128)(2,1)S(1)} %get-tuple-element.27.refs_0_, bf16[384,1024]{1,0:T(8,128)(2,1)S(1)} %get-tuple-element.28.refs_1_, ...), custom_call_target="tpu_custom_call" | custom-call | tf_op jit(solution)/shard_map/decode/pallas_call | solution.py:280
  45.6 5.7 %decode.8 = (f32[1,224,1024]{2,1,0:T(8,128)}, f32[1,160,1024]{2,1,0:T(8,128)}) custom-call(s32[2]{0:T(128)S(1)} %pad_add_fusion.2.info_ref, bf16[384,1024]{1,0:T(8,128)(2,1)S(1)} %get-tuple-element.27.refs_0_, bf16[384,1024]{1,0:T(8,128)(2,1)S(1)} %get-tuple-element.28.refs_1_, bf16[384,1024]{1,0:T(8,128)(2,1)S(1)} %collective-permute-done.1.refs_2_, ...), custom_call_target="tpu_custom_call" | custom-call | tf_op jit(solution)/shard_map/decode/pallas_call | solution.py:280
  51.3 13.0 %collective-permute-done.6 = bf16[1,224,1024]{2,1,0:T(8,128)(2,1)} collective-permute-done((bf16[1,224,1024]{2,1,0:T(8,128)(2,1)}, bf16[1,224,1024]{2,1,0:T(8,128)(2,1)}, u32[]{:S(2)}, u32[]{:S(2)}) %collective-permute-start.6) | collective-permute-done | bytes 458784 | tf_op jit(solution)/shard_map/ppermute | solution.py:357
  64.3 2.2 %add_convert_fusion.2.refs_4_ = bf16[1,224,1024]{2,1,0:T(8,128)(2,1)} fusion(f32[1,224,1024]{2,1,0:T(8,128)} %get-tuple-element.34, bf16[1,224,1024]{2,1,0:T(8,128)(2,1)} %collective-permute-done.6), kind=kLoop, calls=%fused_computation.3 | loop fusion | flops 688128 | bytes 1835008 | tf_op jit(solution)/shard_map/convert_element_type | solution.py:451
  66.5 12.3 %encode.3.refs_6_.refs_0_ = bf16[384,2048]{1,0:T(8,128)(2,1)S(1)} custom-call(s32[3]{0:T(128)S(1)} %pad_add_fusion.1.places_ref, f32[1]{0:T(128)S(6)} %sqrt.3.inv_ref.after_ref, bf16[1,2048]{1,0:T(2,128)(2,1)S(1)} %constant_dynamic-slice_fusion.b_ref, bf16[112,4096]{1,0:T(8,128)(2,1)} %collective-permute-done.3.refs_0_, ...), custom_call_target="tpu_custom_call" | custom-call | tf_op jit(solution)/shard_map/encode/pallas_call | solution.py:181
  78.8 1.4 collective-permute-start.7
  80.2 1.6 collective-permute-start.8
  81.9 2.6 %collective-permute-start.9 = (bf16[1,224,1024]{2,1,0:T(8,128)(2,1)}, bf16[1,224,1024]{2,1,0:T(8,128)(2,1)}, u32[]{:S(2)}, u32[]{:S(2)}) collective-permute-start(bf16[1,224,1024]{2,1,0:T(8,128)(2,1)} %add_convert_fusion.2.refs_4_), channel_id=1, source_target_pairs={{0,8},{4,12},{8,0},{12,4},{1,9},{5,13},{9,1},{13,5},{2,10},{6,14},... | collective-permute-start | bytes 1376264 | tf_op jit(solution)/shard_map/ppermute | solution.py:357
  84.6 1.1 copy-done.3
  85.7 1.1 copy-done.5
  86.8 1.1 copy-done.7
  88.0 1.1 copy-done.9
  89.1 5.6 %decode.9 = (f32[1,224,1024]{2,1,0:T(8,128)}, f32[1,160,1024]{2,1,0:T(8,128)}) custom-call(s32[2]{0:T(128)S(1)} %get-tuple-element.56.info_ref, bf16[384,1024]{1,0:T(8,128)(2,1)S(1)} %copy-done.3, bf16[384,1024]{1,0:T(8,128)(2,1)S(1)} %copy-done.5, bf16[384,1024]{1,0:T(8,128)(2,1)S(1)} %copy-done.7, bf16[384,1024]{1,0:T(8,128)(2,1)S(1)} %copy-done.9, ...), custom_call_target="tpu_custom_call" | custom-call | tf_op jit(solution)/shard_map/decode/pallas_call | solution.py:280
  94.8 1.2 copy-done.10
  95.9 4.4 %decode.10 = (bf16[1,224,1024]{2,1,0:T(8,128)(2,1)S(1)}, bf16[1,160,1024]{2,1,0:T(8,128)(2,1)S(1)}) custom-call(s32[2]{0:T(128)S(1)} %get-tuple-element.57.info_ref, bf16[384,2048]{1,0:T(8,128)(2,1)S(1)} %encode.3.refs_6_.refs_0_, bf16[384,2048]{1,0:T(8,128)(2,1)S(1)} %collective-permute-done.7.refs_1_, bf16[2048,4096]{1,0:T(8,128)(2,1)} %bitcast.30, ...), custom_call_target="tpu_custom_call" | custom-call | tf_op jit(solution)/shard_map/decode/pallas_call | solution.py:280
  101.4 1.4 convert_add_fusion.refs_5_
  102.8 5.4 %decode.11 = (f32[1,224,1024]{2,1,0:T(8,128)}, bf16[1,160,1024]{2,1,0:T(8,128)(2,1)S(1)}) custom-call(s32[2]{0:T(128)S(1)} %pad_add_fusion.2.info_ref, bf16[384,2048]{1,0:T(8,128)(2,1)S(1)} %encode.3.refs_6_.refs_0_, bf16[384,2048]{1,0:T(8,128)(2,1)S(1)} %collective-permute-done.7.refs_1_, bf16[2048,4096]{1,0:T(8,128)(2,1)} %bitcast.31, ...), custom_call_target="tpu_custom_call" | custom-call | tf_op jit(solution)/shard_map/decode/pallas_call | solution.py:280
  108.2 1.6 collective-permute-start.12
  109.9 1.6 collective-permute-start.13
  111.5 1.3 collective-permute-done.10
  113.5 4.6 %decode.12 = (bf16[1,112,1024]{2,1,0:T(8,128)(2,1)S(1)}, bf16[1,112,1024]{2,1,0:T(8,128)(2,1)S(1)}, bf16[1,160,1024]{2,1,0:T(8,128)(2,1)S(1)}) custom-call(s32[2]{0:T(128)S(1)} %pad_add_fusion.4.info_ref, bf16[384,2048]{1,0:T(8,128)(2,1)S(1)} %encode.3.refs_6_.refs_0_, bf16[384,2048]{1,0:T(8,128)(2,1)S(1)} %collective-permute-done.7.refs_1_, ...), custom_call_target="tpu_custom_call" | custom-call | tf_op jit(solution)/shard_map/decode/pallas_call | solution.py:280
  118.1 0.9 collective-permute-start.18
  119.0 1.2 collective-permute-start.19
  120.2 1.8 collective-permute-start.15
  122.0 3.0 %collective-permute-done.13 = bf16[1,160,1024]{2,1,0:T(8,128)(2,1)S(1)} collective-permute-done((bf16[1,160,1024]{2,1,0:T(8,128)(2,1)S(1)}, bf16[1,160,1024]{2,1,0:T(8,128)(2,1)S(1)}, u32[]{:S(2)}, u32[]{:S(2)}) %collective-permute-start.13) | collective-permute-done | bytes 327712 | tf_op jit(solution)/shard_map/ppermute | solution.py:357
  125.1 2.7 %collective-permute-start.17 = (bf16[1,160,1024]{2,1,0:T(8,128)(2,1)S(1)}, bf16[1,160,1024]{2,1,0:T(8,128)(2,1)S(1)}, u32[]{:S(2)}, u32[]{:S(2)}) collective-permute-start(bf16[1,160,1024]{2,1,0:T(8,128)(2,1)S(1)} %add_convert_fusion.4.refs_6_), channel_id=1, source_target_pairs={{0,8},{4,12},{8,0},{12,4},{1,9},{5,13},{9,1},{13,5},{2,10},{6,14},... | collective-permute-start | bytes 983048 | tf_op jit(solution)/shard_map/ppermute | solution.py:357
  127.9 5.4 %decode.13 = (f32[1,224,1024]{2,1,0:T(8,128)}, bf16[1,160,1024]{2,1,0:T(8,128)(2,1)S(1)}) custom-call(s32[2]{0:T(128)S(1)} %get-tuple-element.56.info_ref, bf16[384,2048]{1,0:T(8,128)(2,1)S(1)} %encode.3.refs_6_.refs_0_, bf16[384,2048]{1,0:T(8,128)(2,1)S(1)} %collective-permute-done.7.refs_1_, bf16[2048,4096]{1,0:T(8,128)(2,1)} %bitcast.33, ...), custom_call_target="tpu_custom_call" | custom-call | tf_op jit(solution)/shard_map/decode/pallas_call | solution.py:280
  133.3 1.1 collective-permute-done.18
  134.9 9.7 %collective-permute-done.19 = bf16[1,112,1024]{2,1,0:T(8,128)(2,1)S(1)} collective-permute-done((bf16[1,112,1024]{2,1,0:T(8,128)(2,1)S(1)}, bf16[1,112,1024]{2,1,0:T(8,128)(2,1)S(1)}, u32[]{:S(2)}, u32[]{:S(2)}) %collective-permute-start.19) | collective-permute-done | bytes 229408 | tf_op jit(solution)/shard_map/ppermute | solution.py:357
  144.7 1.5 fusion
  146.2 1.1 collective-permute-start.21
  147.4 2.3 %collective-permute-done.17 = bf16[1,160,1024]{2,1,0:T(8,128)(2,1)S(1)} collective-permute-done((bf16[1,160,1024]{2,1,0:T(8,128)(2,1)S(1)}, bf16[1,160,1024]{2,1,0:T(8,128)(2,1)S(1)}, u32[]{:S(2)}, u32[]{:S(2)}) %collective-permute-start.17) | collective-permute-done | bytes 327712 | tf_op jit(solution)/shard_map/ppermute | solution.py:357
  149.7 7.0 %collective-permute-done.16 = bf16[1,160,1024]{2,1,0:T(8,128)(2,1)S(1)} collective-permute-done((bf16[1,160,1024]{2,1,0:T(8,128)(2,1)S(1)}, bf16[1,160,1024]{2,1,0:T(8,128)(2,1)S(1)}, u32[]{:S(2)}, u32[]{:S(2)}) %collective-permute-start.16) | collective-permute-done | bytes 327712 | tf_op jit(solution)/shard_map/ppermute | solution.py:357
  156.7 2.0 %collective-permute-done.21.refs_5_ = bf16[224,1024]{1,0:T(8,128)(2,1)S(1)} collective-permute-done((bf16[224,1024]{1,0:T(8,128)(2,1)S(1)}, bf16[224,1024]{1,0:T(8,128)(2,1)S(1)}, u32[]{:S(2)}, u32[]{:S(2)}) %collective-permute-start.21) | collective-permute-done | bytes 458784 | tf_op jit(solution)/shard_map/ppermute | solution.py:352
  158.7 1.6 finale.1
  160.4 0.9 collective-permute-start.23
  161.7 2.3 %collective-permute-done.23 = f32[8,128]{1,0:T(8,128)S(1)} collective-permute-done((f32[8,128]{1,0:T(8,128)S(1)}, f32[8,128]{1,0:T(8,128)S(1)}, u32[]{:S(2)}, u32[]{:S(2)}) %collective-permute-start.23) | collective-permute-done | bytes 4128 | tf_op jit(solution)/shard_map/ppermute | solution.py:352
  164.3 4.8 %collective-permute-start.27 = (f32[8,128]{1,0:T(8,128)S(1)}, f32[8,128]{1,0:T(8,128)S(1)}, u32[]{:S(2)}, u32[]{:S(2)}) collective-permute-start(f32[8,128]{1,0:T(8,128)S(1)} %add_add_fusion.1), channel_id=1, source_target_pairs={{0,12},{4,0},{8,4},{12,8},{1,13},{5,1},{9,5},{13,9},{2,14},{6,2},{... | collective-permute-start | bytes 12296 | tf_op jit(solution)/shard_map/ppermute | solution.py:352
  170.5 3.2 %collective-permute-done.26 = f32[8,128]{1,0:T(8,128)S(1)} collective-permute-done((f32[8,128]{1,0:T(8,128)S(1)}, f32[8,128]{1,0:T(8,128)S(1)}, u32[]{:S(2)}, u32[]{:S(2)}) %collective-permute-start.26) | collective-permute-done | bytes 4128 | tf_op jit(solution)/shard_map/ppermute | solution.py:352
  (73 shorter events, 7.6 us)
Async XLA Ops:
  0.6 10.9 %copy-start = (bf16[1,4096]{1,0:T(2,128)(2,1)S(1)}, bf16[1,4096]{1,0:T(2,128)(2,1)}, u32[]{:S(2)}) copy-start(bf16[1,4096]{1,0:T(2,128)(2,1)} %param.10) | copy-start | bytes 24580
  3.4 6.4 %collective-permute-start = (f32[1]{0:T(128)}, f32[1]{0:T(128)}, u32[]{:S(2)}, u32[]{:S(2)}) collective-permute-start(f32[1]{0:T(128)} %square_sum.1.after_ref), channel_id=1, source_target_pairs={{0,2},{2,0},{1,3},{3,1},{4,6},{6,4},{5,7},{7,5},{8,10},{10,8},{9,1... | collective-permute-start | bytes 20 | tf_op jit(solution)/shard_map/ppermute | solution.py:352
  11.1 23.7 %collective-permute-start.3 = (bf16[112,4096]{1,0:T(8,128)(2,1)}, bf16[112,4096]{1,0:T(8,128)(2,1)}, u32[]{:S(2)}, u32[]{:S(2)}) collective-permute-start(bf16[112,4096]{1,0:T(8,128)(2,1)} %get-tuple-element.31), channel_id=1, source_target_pairs={{0,2},{2,0},{1,3},{3,1},{4,6},{6,4},{5,7},{7,5},{8,10},{10,8},{9,1... | collective-permute-start | bytes 2752520 | tf_op jit(solution)/shard_map/ppermute | solution.py:352
  23.4 22.2 %copy-start.2 = (bf16[384,1024]{1,0:T(8,128)(2,1)}, bf16[384,1024]{1,0:T(8,128)(2,1)S(1)}, u32[]{:S(2)}) copy-start(bf16[384,1024]{1,0:T(8,128)(2,1)S(1)} %get-tuple-element.27.refs_0_) | copy-start | bytes 2359300
  23.4 22.2 %copy-start.4 = (bf16[384,1024]{1,0:T(8,128)(2,1)}, bf16[384,1024]{1,0:T(8,128)(2,1)S(1)}, u32[]{:S(2)}) copy-start(bf16[384,1024]{1,0:T(8,128)(2,1)S(1)} %get-tuple-element.28.refs_1_) | copy-start | bytes 2359300
  23.4 13.0 %collective-permute-start.1 = (bf16[384,1024]{1,0:T(8,128)(2,1)S(1)}, bf16[384,1024]{1,0:T(8,128)(2,1)S(1)}, u32[]{:S(2)}, u32[]{:S(2)}) collective-permute-start(bf16[384,1024]{1,0:T(8,128)(2,1)S(1)} %get-tuple-element.27.refs_0_), channel_id=1, source_target_pairs={{0,1},{2,3},{4,5},{6,7},{8,9},{10,11},{12,13},{14,15},{16,17},{18,... | collective-permute-start | bytes 2359304 | tf_op jit(solution)/shard_map/ppermute | solution.py:419
  24.7 11.7 %collective-permute-start.2 = (bf16[384,1024]{1,0:T(8,128)(2,1)S(1)}, bf16[384,1024]{1,0:T(8,128)(2,1)S(1)}, u32[]{:S(2)}, u32[]{:S(2)}) collective-permute-start(bf16[384,1024]{1,0:T(8,128)(2,1)S(1)} %get-tuple-element.28.refs_1_), channel_id=1, source_target_pairs={{0,1},{2,3},{4,5},{6,7},{8,9},{10,11},{12,13},{14,15},{16,17},{18,... | collective-permute-start | bytes 2359304 | tf_op jit(solution)/shard_map/ppermute | solution.py:419
  26.1 40.4 %collective-permute-start.5 = (bf16[160,4096]{1,0:T(8,128)(2,1)}, bf16[160,4096]{1,0:T(8,128)(2,1)}, u32[]{:S(2)}, u32[]{:S(2)}) collective-permute-start(bf16[160,4096]{1,0:T(8,128)(2,1)} %get-tuple-element.32), channel_id=1, source_target_pairs={{0,2},{2,0},{1,3},{3,1},{4,6},{6,4},{5,7},{7,5},{8,10},{10,8},{9,1... | collective-permute-start | bytes 3932168 | tf_op jit(solution)/shard_map/ppermute | solution.py:352
  34.7 31.8 %collective-permute-start.4 = (bf16[112,4096]{1,0:T(8,128)(2,1)}, bf16[112,4096]{1,0:T(8,128)(2,1)}, u32[]{:S(2)}, u32[]{:S(2)}) collective-permute-start(bf16[112,4096]{1,0:T(8,128)(2,1)} %collective-permute-done.3.refs_0_), channel_id=1, source_target_pairs={{0,4},{4,0},{8,12},{12,8},{1,5},{5,1},{9,13},{13,9},{2,6},{6,2},{1... | collective-permute-start | bytes 2752520 | tf_op jit(solution)/shard_map/ppermute | solution.py:357
  36.4 9.2 %copy-start.6 = (bf16[384,1024]{1,0:T(8,128)(2,1)}, bf16[384,1024]{1,0:T(8,128)(2,1)S(1)}, u32[]{:S(2)}) copy-start(bf16[384,1024]{1,0:T(8,128)(2,1)S(1)} %collective-permute-done.1.refs_2_) | copy-start | bytes 2359300
  36.4 9.2 %copy-start.8 = (bf16[384,1024]{1,0:T(8,128)(2,1)}, bf16[384,1024]{1,0:T(8,128)(2,1)S(1)}, u32[]{:S(2)}) copy-start(bf16[384,1024]{1,0:T(8,128)(2,1)S(1)} %collective-permute-done.2.refs_3_) | copy-start | bytes 2359300
  44.9 19.4 %collective-permute-start.6 = (bf16[1,224,1024]{2,1,0:T(8,128)(2,1)}, bf16[1,224,1024]{2,1,0:T(8,128)(2,1)}, u32[]{:S(2)}, u32[]{:S(2)}) collective-permute-start(bf16[1,224,1024]{2,1,0:T(8,128)(2,1)} %get-tuple-element.33.refs_6_), channel_id=1, source_target_pairs={{0,4},{4,0},{8,12},{12,8},{1,5},{5,1},{9,13},{13,9},{2,6},{6,2},{1... | collective-permute-start | bytes 1376264 | tf_op jit(solution)/shard_map/ppermute | solution.py:357
  78.8 15.9 %collective-permute-start.7 = (bf16[384,2048]{1,0:T(8,128)(2,1)S(1)}, bf16[384,2048]{1,0:T(8,128)(2,1)S(1)}, u32[]{:S(2)}, u32[]{:S(2)}) collective-permute-start(bf16[384,2048]{1,0:T(8,128)(2,1)S(1)} %encode.3.refs_6_.refs_0_), channel_id=1, source_target_pairs={{0,1},{2,3},{4,5},{6,7},{8,9},{10,11},{12,13},{14,15},{16,17},{18,... | collective-permute-start | bytes 4718600 | tf_op jit(solution)/shard_map/ppermute | solution.py:419
  80.2 21.2 %collective-permute-start.8 = (bf16[1,224,1024]{2,1,0:T(8,128)(2,1)}, bf16[1,224,1024]{2,1,0:T(8,128)(2,1)}, u32[]{:S(2)}, u32[]{:S(2)}) collective-permute-start(bf16[1,224,1024]{2,1,0:T(8,128)(2,1)} %get-tuple-element.38), channel_id=1, source_target_pairs={{0,4},{4,0},{8,12},{12,8},{1,5},{5,1},{9,13},{13,9},{2,6},{6,2},{1... | collective-permute-start | bytes 1376264 | tf_op jit(solution)/shard_map/ppermute | solution.py:357
  81.9 19.5 %collective-permute-start.9 = (bf16[1,224,1024]{2,1,0:T(8,128)(2,1)}, bf16[1,224,1024]{2,1,0:T(8,128)(2,1)}, u32[]{:S(2)}, u32[]{:S(2)}) collective-permute-start(bf16[1,224,1024]{2,1,0:T(8,128)(2,1)} %add_convert_fusion.2.refs_4_), channel_id=1, source_target_pairs={{0,8},{4,12},{8,0},{12,4},{1,9},{5,13},{9,1},{13,5},{2,10},{6,14},... | collective-permute-start | bytes 1376264 | tf_op jit(solution)/shard_map/ppermute | solution.py:357
  84.5 1.1 copy-start.3
  85.7 1.1 copy-start.5
  86.8 1.1 copy-start.7
  88.0 1.1 copy-start.9
  94.7 1.2 copy-start.10
  100.4 9.4 %collective-permute-start.11 = (bf16[1,160,1024]{2,1,0:T(8,128)(2,1)S(1)}, bf16[1,160,1024]{2,1,0:T(8,128)(2,1)S(1)}, u32[]{:S(2)}, u32[]{:S(2)}) collective-permute-start(bf16[1,160,1024]{2,1,0:T(8,128)(2,1)S(1)} %get-tuple-element.41), channel_id=1, source_target_pairs={{0,2},{2,0},{1,3},{3,1},{4,6},{6,4},{5,7},{7,5},{8,10},{10,8},{9,1... | collective-permute-start | bytes 983048 | tf_op jit(solution)/shard_map/ppermute | solution.py:352
  101.0 11.9 %collective-permute-start.10 = (bf16[1,224,1024]{2,1,0:T(8,128)(2,1)S(1)}, bf16[1,224,1024]{2,1,0:T(8,128)(2,1)S(1)}, u32[]{:S(2)}, u32[]{:S(2)}) collective-permute-start(bf16[1,224,1024]{2,1,0:T(8,128)(2,1)S(1)} %get-tuple-element.37.refs_4_), channel_id=1, source_target_pairs={{0,4},{4,0},{8,12},{12,8},{1,5},{5,1},{9,13},{13,9},{2,6},{6,2},{1... | collective-permute-start | bytes 1376264 | tf_op jit(solution)/shard_map/ppermute | solution.py:357
  102.8 7.0 %copy-start.17 = (f32[1,160,1024]{2,1,0:T(8,128)S(1)}, f32[1,160,1024]{2,1,0:T(8,128)}, u32[]{:S(2)}) copy-start(f32[1,160,1024]{2,1,0:T(8,128)} %get-tuple-element.40) | copy-start | bytes 1966084
  108.2 4.7 %copy-start.14 = (f32[1,224,1024]{2,1,0:T(8,128)S(1)}, f32[1,224,1024]{2,1,0:T(8,128)}, u32[]{:S(2)}) copy-start(f32[1,224,1024]{2,1,0:T(8,128)} %get-tuple-element.39) | copy-start | bytes 2752516
  108.2 12.0 %collective-permute-start.12 = (bf16[1,160,1024]{2,1,0:T(8,128)(2,1)S(1)}, bf16[1,160,1024]{2,1,0:T(8,128)(2,1)S(1)}, u32[]{:S(2)}, u32[]{:S(2)}) collective-permute-start(bf16[1,160,1024]{2,1,0:T(8,128)(2,1)S(1)} %get-tuple-element.45), channel_id=1, source_target_pairs={{0,2},{2,0},{1,3},{3,1},{4,6},{6,4},{5,7},{7,5},{8,10},{10,8},{9,1... | collective-permute-start | bytes 983048 | tf_op jit(solution)/shard_map/ppermute | solution.py:352
  109.9 15.1 %collective-permute-start.13 = (bf16[1,160,1024]{2,1,0:T(8,128)(2,1)S(1)}, bf16[1,160,1024]{2,1,0:T(8,128)(2,1)S(1)}, u32[]{:S(2)}, u32[]{:S(2)}) collective-permute-start(bf16[1,160,1024]{2,1,0:T(8,128)(2,1)S(1)} %add_convert_fusion.5.refs_5_), channel_id=1, source_target_pairs={{0,4},{4,0},{8,12},{12,8},{1,5},{5,1},{9,13},{13,9},{2,6},{6,2},{1... | collective-permute-start | bytes 983048 | tf_op jit(solution)/shard_map/ppermute | solution.py:357
  113.0 31.6 %collective-permute-start.20 = (bf16[1,224,1024]{2,1,0:T(8,128)(2,1)S(1)}, bf16[1,224,1024]{2,1,0:T(8,128)(2,1)S(1)}, u32[]{:S(2)}, u32[]{:S(2)}) collective-permute-start(bf16[1,224,1024]{2,1,0:T(8,128)(2,1)S(1)} %add_convert_fusion.1.refs_4_), channel_id=1, source_target_pairs={{0,8},{4,12},{8,0},{12,4},{1,9},{5,13},{9,1},{13,5},{2,10},{6,14},... | collective-permute-start | bytes 1376264 | tf_op jit(solution)/shard_map/ppermute | solution.py:357
  113.5 11.5 %copy-start.15 = (f32[1,160,1024]{2,1,0:T(8,128)S(1)}, f32[1,160,1024]{2,1,0:T(8,128)}, u32[]{:S(2)}) copy-start(f32[1,160,1024]{2,1,0:T(8,128)} %get-tuple-element.44) | copy-start | bytes 1966084
  118.1 16.3 %collective-permute-start.18 = (bf16[1,112,1024]{2,1,0:T(8,128)(2,1)S(1)}, bf16[1,112,1024]{2,1,0:T(8,128)(2,1)S(1)}, u32[]{:S(2)}, u32[]{:S(2)}) collective-permute-start(bf16[1,112,1024]{2,1,0:T(8,128)(2,1)S(1)} %get-tuple-element.42.refs_4_), channel_id=1, source_target_pairs={{0,4},{4,0},{8,12},{12,8},{1,5},{5,1},{9,13},{13,9},{2,6},{6,2},{1... | collective-permute-start | bytes 688136 | tf_op jit(solution)/shard_map/ppermute | solution.py:357
  119.0 25.6 %collective-permute-start.19 = (bf16[1,112,1024]{2,1,0:T(8,128)(2,1)S(1)}, bf16[1,112,1024]{2,1,0:T(8,128)(2,1)S(1)}, u32[]{:S(2)}, u32[]{:S(2)}) collective-permute-start(bf16[1,112,1024]{2,1,0:T(8,128)(2,1)S(1)} %get-tuple-element.43.refs_5_), channel_id=1, source_target_pairs={{0,4},{4,0},{8,12},{12,8},{1,5},{5,1},{9,13},{13,9},{2,6},{6,2},{1... | collective-permute-start | bytes 688136 | tf_op jit(solution)/shard_map/ppermute | solution.py:357
  120.2 27.0 %collective-permute-start.15 = (bf16[1,160,1024]{2,1,0:T(8,128)(2,1)S(1)}, bf16[1,160,1024]{2,1,0:T(8,128)(2,1)S(1)}, u32[]{:S(2)}, u32[]{:S(2)}) collective-permute-start(bf16[1,160,1024]{2,1,0:T(8,128)(2,1)S(1)} %get-tuple-element.48), channel_id=1, source_target_pairs={{0,2},{2,0},{1,3},{3,1},{4,6},{6,4},{5,7},{7,5},{8,10},{10,8},{9,1... | collective-permute-start | bytes 983048 | tf_op jit(solution)/shard_map/ppermute | solution.py:352
  125.1 24.6 %collective-permute-start.17 = (bf16[1,160,1024]{2,1,0:T(8,128)(2,1)S(1)}, bf16[1,160,1024]{2,1,0:T(8,128)(2,1)S(1)}, u32[]{:S(2)}, u32[]{:S(2)}) collective-permute-start(bf16[1,160,1024]{2,1,0:T(8,128)(2,1)S(1)} %add_convert_fusion.4.refs_6_), channel_id=1, source_target_pairs={{0,8},{4,12},{8,0},{12,4},{1,9},{5,13},{9,1},{13,5},{2,10},{6,14},... | collective-permute-start | bytes 983048 | tf_op jit(solution)/shard_map/ppermute | solution.py:357
  133.3 14.0 %copy-start.16 = (f32[1,160,1024]{2,1,0:T(8,128)S(1)}, f32[1,160,1024]{2,1,0:T(8,128)}, u32[]{:S(2)}) copy-start(f32[1,160,1024]{2,1,0:T(8,128)} %get-tuple-element.47) | copy-start | bytes 1966084
  134.4 15.3 %collective-permute-start.14 = (bf16[1,160,1024]{2,1,0:T(8,128)(2,1)S(1)}, bf16[1,160,1024]{2,1,0:T(8,128)(2,1)S(1)}, u32[]{:S(2)}, u32[]{:S(2)}) collective-permute-start(bf16[1,160,1024]{2,1,0:T(8,128)(2,1)S(1)} %get-tuple-element.46), channel_id=1, source_target_pairs={{0,2},{2,0},{1,3},{3,1},{4,6},{6,4},{5,7},{7,5},{8,10},{10,8},{9,1... | collective-permute-start | bytes 983048 | tf_op jit(solution)/shard_map/ppermute | solution.py:352
  144.6 14.1 %copy-start.11 = (bf16[1,384,1024]{2,1,0:T(8,128)(2,1)S(1)}, bf16[1,384,1024]{2,1,0:T(8,128)(2,1)}, u32[]{:S(2)}) copy-start(bf16[1,384,1024]{2,1,0:T(8,128)(2,1)} %param.8) | copy-start | bytes 2359300
  144.6 14.1 %copy-start.12 = (f32[1,160,1024]{2,1,0:T(8,128)S(1)}, f32[1,160,1024]{2,1,0:T(8,128)}, u32[]{:S(2)}) copy-start(f32[1,160,1024]{2,1,0:T(8,128)} %get-tuple-element.35) | copy-start | bytes 1966084
  144.6 14.1 %copy-start.13 = (bf16[1,1024]{1,0:T(2,128)(2,1)S(1)}, bf16[1,1024]{1,0:T(2,128)(2,1)}, u32[]{:S(2)}) copy-start(bf16[1,1024]{1,0:T(2,128)(2,1)} %b_ref.1) | copy-start | bytes 6148
  146.2 12.6 %collective-permute-start.21 = (bf16[224,1024]{1,0:T(8,128)(2,1)S(1)}, bf16[224,1024]{1,0:T(8,128)(2,1)S(1)}, u32[]{:S(2)}, u32[]{:S(2)}) collective-permute-start(bf16[224,1024]{1,0:T(8,128)(2,1)S(1)} %fusion), channel_id=1, source_target_pairs={{0,2},{2,0},{1,3},{3,1},{4,6},{6,4},{5,7},{7,5},{8,10},{10,8},{9,1... | collective-permute-start | bytes 1376264 | tf_op jit(solution)/shard_map/ppermute | solution.py:352
  147.3 9.4 %collective-permute-start.16 = (bf16[1,160,1024]{2,1,0:T(8,128)(2,1)S(1)}, bf16[1,160,1024]{2,1,0:T(8,128)(2,1)S(1)}, u32[]{:S(2)}, u32[]{:S(2)}) collective-permute-start(bf16[1,160,1024]{2,1,0:T(8,128)(2,1)S(1)} %add_convert_fusion.3), channel_id=1, source_target_pairs={{0,4},{4,0},{8,12},{12,8},{1,5},{5,1},{9,13},{13,9},{2,6},{6,2},{1... | collective-permute-start | bytes 983048 | tf_op jit(solution)/shard_map/ppermute | solution.py:357
  158.7 19.1 %copy-start.1 = (bf16[1,4096]{1,0:T(2,128)(2,1)S(1)}, bf16[1,4096]{1,0:T(2,128)(2,1)}, u32[]{:S(2)}) copy-start(bf16[1,4096]{1,0:T(2,128)(2,1)} %param.10) | copy-start | bytes 24580
  160.4 1.3 collective-permute-start.24
  160.4 3.6 %collective-permute-start.23 = (f32[8,128]{1,0:T(8,128)S(1)}, f32[8,128]{1,0:T(8,128)S(1)}, u32[]{:S(2)}, u32[]{:S(2)}) collective-permute-start(f32[8,128]{1,0:T(8,128)S(1)} %get-tuple-element.51), channel_id=1, source_target_pairs={{0,2},{1,3},{2,0},{3,1},{4,6},{5,7},{6,4},{7,5},{8,10},{9,11},{10,... | collective-permute-start | bytes 12296 | tf_op jit(solution)/shard_map/ppermute | solution.py:352
  161.3 3.0 %collective-permute-start.22 = (f32[8,128]{1,0:T(8,128)S(1)}, f32[8,128]{1,0:T(8,128)S(1)}, u32[]{:S(2)}, u32[]{:S(2)}) collective-permute-start(f32[8,128]{1,0:T(8,128)S(1)} %get-tuple-element.51), channel_id=1, source_target_pairs={{0,1},{1,2},{2,3},{3,0},{4,5},{5,6},{6,7},{7,4},{8,9},{9,10},{10,1... | collective-permute-start | bytes 12296 | tf_op jit(solution)/shard_map/ppermute | solution.py:352
  164.3 6.2 %collective-permute-start.27 = (f32[8,128]{1,0:T(8,128)S(1)}, f32[8,128]{1,0:T(8,128)S(1)}, u32[]{:S(2)}, u32[]{:S(2)}) collective-permute-start(f32[8,128]{1,0:T(8,128)S(1)} %add_add_fusion.1), channel_id=1, source_target_pairs={{0,12},{4,0},{8,4},{12,8},{1,13},{5,1},{9,5},{13,9},{2,14},{6,2},{... | collective-permute-start | bytes 12296 | tf_op jit(solution)/shard_map/ppermute | solution.py:352
  169.2 4.5 %collective-permute-start.26 = (f32[8,128]{1,0:T(8,128)S(1)}, f32[8,128]{1,0:T(8,128)S(1)}, u32[]{:S(2)}, u32[]{:S(2)}) collective-permute-start(f32[8,128]{1,0:T(8,128)S(1)} %add_add_fusion.1), channel_id=1, source_target_pairs={{0,8},{4,12},{8,0},{12,4},{1,9},{5,13},{9,1},{13,5},{2,10},{6,14},... | collective-permute-start | bytes 12296 | tf_op jit(solution)/shard_map/ppermute | solution.py:352
  169.2 5.4 %collective-permute-start.25 = (f32[8,128]{1,0:T(8,128)S(1)}, f32[8,128]{1,0:T(8,128)S(1)}, u32[]{:S(2)}, u32[]{:S(2)}) collective-permute-start(f32[8,128]{1,0:T(8,128)S(1)} %add_add_fusion.1), channel_id=1, source_target_pairs={{0,4},{4,8},{8,12},{12,0},{1,5},{5,9},{9,13},{13,1},{2,6},{6,10},{... | collective-permute-start | bytes 12296 | tf_op jit(solution)/shard_map/ppermute | solution.py:352

commit v9 on v8

--- a/solution.py
+++ b/solution.py
@@ -283,8 +283,7 @@
         + [pl.BlockSpec(memory_space=pl.ANY)] * (2 * parts + 2 + m),
         out_specs=[pl.BlockSpec(memory_space=pltpu.VMEM)] * len(outs),
         out_shape=[
-            (pltpu.HBM if dtype == jnp.float32 else jax.ShapeDtypeStruct)(
-                (many, sum(height for _, height in spans), width), dtype)
+            jax.ShapeDtypeStruct((many, sum(height for _, height in spans), width), dtype)
             for _, many, spans, dtype in outs
         ],
         scratch_shapes=[
@@ -328,9 +327,9 @@
         sums = (zero, zero)
         for which, start, target_start, count in spans:
             sums = lax.fori_loop(0, count // 16, block(which, start, target_start), sums)
-        lane = lax.broadcasted_iota(jnp.int32, (8, 128), 1)
-        value = jnp.where(lane == layer_ref[0], jnp.sum(sums[0]), 0.0)
-        s_ref[...] = jnp.where(lane == layer_ref[0] + 2, jnp.sum(sums[1]), value)
+        row = lax.broadcasted_iota(jnp.int32, (8, 128), 0)
+        value = jnp.where(row == layer_ref[0], jnp.sum(sums[0]), 0.0)
+        s_ref[...] = jnp.where(row == layer_ref[0] + 2, jnp.sum(sums[1]), value)
 
     vmem = pl.BlockSpec(memory_space=pltpu.VMEM)
     return pl.pallas_call(
@@ -345,6 +344,25 @@
         cost_estimate=COST,
         name="finale",
     )(layer.astype(jnp.int32).reshape(1), bias, target, *outer_terms, *inner_terms)
+
+
+def mean_ratio(terms):
+    n = len(terms)
+
+    def body(*refs):
+        total = sum(ref[...] for ref in refs[:n])
+        ratio = total[0:2] / total[2:4]
+        refs[n][...] = (ratio[0:1, 0:1] + ratio[1:2, 0:1]) / 2.0
+
+    vmem = pl.BlockSpec(memory_space=pltpu.VMEM)
+    return pl.pallas_call(
+        body,
+        in_specs=[vmem] * n,
+        out_specs=vmem,
+        out_shape=jax.ShapeDtypeStruct((1, 1), jnp.float32),
+        cost_estimate=COST,
+        name="mean_ratio",
+    )(*terms).reshape(1)
 
 
 def shifted(value, axis, distance):
@@ -445,12 +463,10 @@
         [span + (dtype,) for span, dtype in zip(spans, (narrow, narrow, jnp.float32, jnp.float32))], [])
     far_in = swapped(far_sent, "latent", 1)
     near_in = swapped(near_sent, "latent", 1)
-    (far_kept, far_out_kept) = products(
-        codes, earlier, info(mine_bit, (far,)),
-        [(0, group, inside, jnp.float32), (0, group, outside, jnp.float32)], [far_sent])
+    far_kept, near_kept, far_out_kept, near_out_kept = products(
+        codes, earlier, info(mine_bit, (far, near)), [span + (jnp.float32,) for span in spans], [far_sent])
     across_in = (far_kept + wide(far_in)).astype(narrow)
-    across_in_there = swapped(across_in, "latent", 2)
-    own = codes, earlier
+    total_in = near_kept + wide(near_in) + wide(swapped(across_in, "latent", 2))
 
     after = across_in
     returned = []
@@ -472,14 +488,7 @@
                 [(0, group, span, dtype) for span in spans] + [(0, group, outside, narrow)], also)
             return insides, shifted(outer, "token", back)
 
-        before = []
-        if not returned:
-            near_own, near_out_kept = products(
-                *own, info(mine_bit, (near,)),
-                [(0, group, inside, jnp.float32), (0, group, outside, jnp.float32)], codes)
-            total_in = near_own + wide(near_in) + wide(across_in_there)
-            before = [near_own]
-        (far_sent,), far_back = quarter_of(other, far, [inside], narrow, before)
+        (far_sent,), far_back = quarter_of(other, far, [inside], narrow, [])
         far_in = swapped(far_sent, "latent", 1)
         (far_kept,), far_kept_back = quarter_of(mine_bit, far, [inside], jnp.float32, [far_sent, total_in])
         far_out_back.append(far_back)
@@ -512,8 +521,8 @@
         outer_terms = [finish(joined(near_out_kept, near_out_kept_back) + wide(near_out) + wide(across_out))]
     recon, sums = finale(outer_terms, [finish(total_in), *returned], dec_bias, targets[0], layer)
 
-    sums = sum_over(sum_over(sums, ("token", "layer")), "latent")
-    loss = (sums[:1, 0] / sums[:1, 2] + sums[:1, 1] / sums[:1, 3]) / 2.0
+    sums = sum_over(sums, ("token", "layer"))
+    loss = mean_ratio([sums] + [shifted(sums, "latent", d) for d in range(1, n_lat)])
     return (recon[None], loss)
 
 

time: 180 us -> 166 us (0.922)
  Pallas kernels: 71.5 us -> 66.2 us
  waiting for transfers between devices: 54.3 us -> 58.5 us
  between operations: 5.99 us -> 2.32 us
  other arithmetic: 5.89 us -> 2.43 us
  local copies, waits for them, and re-layouts: 6.43 us -> 3.14 us
  starting transfers between devices: 34.9 us -> 32.9 us
    pallas_call x7 -> x6, Pallas kernels: 39.7 us -> 33.1 us  [decode(): pl.pallas_call(body, in_specs=[pl.BlockSpec(memory_space=pltpu.SMEM)] + [...]
    ppermute x11, waiting for transfers between devices: 37.5 us -> 43.4 us  [swapped(): return lax.ppermute(value, axis, [(i, i ^ bit) for i in range(n)])]
    ppermute x14, starting transfers between devices: 17.2 us -> 13.5 us  [shifted(): lax.ppermute(value, axis, [(i, (i + distance) % n) for i in range(n)])]
    unnamed x36 -> x28, local copies, waits for them, and re-layouts: 5.77 us -> 3.14 us
  transfers between devices with their start and end apart: 28 -> 28, of which waited for: 15 -> 17; matrix products, arithmetic and copies ran while one was open for 3% -> 1% of each run, Pallas kernels for 31% -> 29%
where the time goes in v9:
time: 166 us
  Pallas kernels  66.2 us (40%)
  waiting for transfers between devices  58.5 us (35%)
  starting transfers between devices  32.9 us (20%)
  local copies, waits for them, and re-layouts  3.14 us (2%)
  other arithmetic  2.43 us (1%)
  between operations  2.32 us (1%)
    ppermute x11, waiting for transfers between devices, swapped(): return lax.ppermute(value, axis, [(i, i ^ bit) for i in range(n)])  43.4 us
    pallas_call x6, Pallas kernels, decode(): pl.pallas_call(body, in_specs=[pl.BlockSpec(memory_space=pltpu.SMEM)] + [...  33.1 us
    pallas_call x2, Pallas kernels, encode(): pl.pallas_call(body, in_specs=[pl.BlockSpec(memory_space=pltpu.SMEM), pl....  24.1 us
    ppermute x11, starting transfers between devices, swapped(): return lax.ppermute(value, axis, [(i, i ^ bit) for i in range(n)])  15.3 us
    ppermute x14, waiting for transfers between devices, shifted(): lax.ppermute(value, axis, [(i, (i + distance) % n) for i in range(n)])  15.1 us
    ppermute x14, starting transfers between devices, shifted(): lax.ppermute(value, axis, [(i, (i + distance) % n) for i in range(n)])  13.5 us
    ppermute x3, starting transfers between devices, earlier_of(): return [lax.ppermute(part, 'layer', [(0, 1)]) for part in codes]  4.07 us
    pallas_call x1, Pallas kernels, cut(): pl.pallas_call(body, in_specs=[pl.BlockSpec(memory_space=pltpu.SMEM), pl....  3.37 us
  transfers between devices with their start and end apart: 28, of which 17 were waited for; matrix products, arithmetic and copies ran while one was open for 1% of the time, Pallas kernels for 29%

profile of v9, /device:TPU:0, one launch (start us, length us, event | category | flops | bytes accessed | tf_op | source)
XLA Modules:
  0.0 165.5 jit_solution(14225330554252983366)
XLA Ops:
  0.6 2.7 %square_sum.1.after_ref = f32[1]{0:T(128)} custom-call(bf16[384,4096]{1,0:T(8,128)(2,1)} %bitcast.35), custom_call_target="tpu_custom_call" | custom-call | tf_op jit(solution)/shard_map/square_sum/pallas_call | solution.py:47
  3.4 3.0 %collective-permute-start = (f32[1]{0:T(128)}, f32[1]{0:T(128)}, u32[]{:S(2)}, u32[]{:S(2)}) collective-permute-start(f32[1]{0:T(128)} %square_sum.1.after_ref), channel_id=1, source_target_pairs={{0,2},{2,0},{1,3},{3,1},{4,6},{6,4},{5,7},{7,5},{8,10},{10,8},{9,1... | collective-permute-start | bytes 20 | tf_op jit(solution)/shard_map/ppermute | solution.py:370
  6.4 3.4 %cut.1 = (bf16[112,4096]{1,0:T(8,128)(2,1)}, bf16[160,4096]{1,0:T(8,128)(2,1)}) custom-call(s32[1]{0:T(128)} %bitcast.12.side_ref, f32[1]{0:T(128)} %square_sum.1.after_ref, bf16[384,4096]{1,0:T(8,128)(2,1)} %bitcast.36), custom_call_target="tpu_custom_call" | custom-call | tf_op jit(solution)/shard_map/cut/pallas_call | solution.py:81
  11.5 11.8 %encode.2 = (bf16[384,1024]{1,0:T(8,128)(2,1)S(1)}, bf16[384,1024]{1,0:T(8,128)(2,1)S(1)}) custom-call(s32[1]{0:T(128)} %constant.58.clone.1.places_ref, f32[1]{0:T(128)S(6)} %sqrt.3.inv_ref.after_ref, bf16[1,2048]{1,0:T(2,128)(2,1)S(1)} %constant_dynamic-slice_fusion.b_ref, bf16[384,4096]{1,0:T(8,128)(2,1)} %bitcast.37, bf16[4096,2048]{1,0:T(8,128)(2,1)} %bitcast.33), custom_call_target="tpu_custom_call" | custom-call | tf_op jit(solution)/shard_map/encode/pallas_call | solution.py:181
  23.3 1.3 collective-permute-start.1
  24.6 1.3 collective-permute-start.2
  26.0 1.8 %collective-permute-start.5 = (bf16[160,4096]{1,0:T(8,128)(2,1)}, bf16[160,4096]{1,0:T(8,128)(2,1)}, u32[]{:S(2)}, u32[]{:S(2)}) collective-permute-start(bf16[160,4096]{1,0:T(8,128)(2,1)} %get-tuple-element.34), channel_id=1, source_target_pairs={{0,2},{2,0},{1,3},{3,1},{4,6},{6,4},{5,7},{7,5},{8,10},{10,8},{9,1... | collective-permute-start | bytes 3932168 | tf_op jit(solution)/shard_map/ppermute | solution.py:370
  27.8 7.0 %collective-permute-done.3.refs_0_ = bf16[112,4096]{1,0:T(8,128)(2,1)} collective-permute-done((bf16[112,4096]{1,0:T(8,128)(2,1)}, bf16[112,4096]{1,0:T(8,128)(2,1)}, u32[]{:S(2)}, u32[]{:S(2)}) %collective-permute-start.3) | collective-permute-done | bytes 917536 | tf_op jit(solution)/shard_map/ppermute | solution.py:370
  34.8 1.6 collective-permute-start.4
  36.5 7.9 %decode.6 = (bf16[1,224,1024]{2,1,0:T(8,128)(2,1)}, bf16[1,224,1024]{2,1,0:T(8,128)(2,1)S(1)}, f32[1,160,1024]{2,1,0:T(8,128)S(1)}, f32[1,160,1024]{2,1,0:T(8,128)S(1)}) custom-call(s32[3]{0:T(128)S(1)} %get-tuple-element.53.info_ref, bf16[384,1024]{1,0:T(8,128)(2,1)S(1)} %get-tuple-element.27.refs_0_, bf16[384,1024]{1,0:T(8,128)(2,1)S(1)} %get-tuple-element.28.refs_1_, ...), custom_call_target="tpu_custom_call" | custom-call | tf_op jit(solution)/shard_map/decode/pallas_call | solution.py:280
  44.3 0.9 copy-done.3
  45.2 0.8 copy-done.5
  46.1 0.8 copy-done.8
  47.3 7.1 %decode.7 = (f32[1,224,1024]{2,1,0:T(8,128)S(1)}, f32[1,224,1024]{2,1,0:T(8,128)S(1)}, f32[1,160,1024]{2,1,0:T(8,128)S(1)}, f32[1,160,1024]{2,1,0:T(8,128)S(1)}) custom-call(s32[3]{0:T(128)S(1)} %get-tuple-element.52.info_ref, bf16[384,1024]{1,0:T(8,128)(2,1)S(1)} %get-tuple-element.27.refs_0_, bf16[384,1024]{1,0:T(8,128)(2,1)S(1)} %get-tuple-element.28.refs_1_, ...), custom_call_target="tpu_custom_call" | custom-call | tf_op jit(solution)/shard_map/decode/pallas_call | solution.py:280
  54.4 10.0 %collective-permute-done.6 = bf16[1,224,1024]{2,1,0:T(8,128)(2,1)} collective-permute-done((bf16[1,224,1024]{2,1,0:T(8,128)(2,1)}, bf16[1,224,1024]{2,1,0:T(8,128)(2,1)}, u32[]{:S(2)}, u32[]{:S(2)}) %collective-permute-start.6) | collective-permute-done | bytes 458784 | tf_op jit(solution)/shard_map/ppermute | solution.py:375
  64.4 1.1 add_convert_fusion.2.refs_4_
  65.6 12.3 %encode.3.refs_0_ = bf16[384,2048]{1,0:T(8,128)(2,1)S(1)} custom-call(s32[3]{0:T(128)S(1)} %pad_add_fusion.3.places_ref, f32[1]{0:T(128)S(6)} %sqrt.3.inv_ref.after_ref, bf16[1,2048]{1,0:T(2,128)(2,1)S(1)} %constant_dynamic-slice_fusion.b_ref, bf16[112,4096]{1,0:T(8,128)(2,1)} %collective-permute-done.3.refs_0_, ...), custom_call_target="tpu_custom_call" | custom-call | tf_op jit(solution)/shard_map/encode/pallas_call | solution.py:181
  77.9 1.4 collective-permute-start.7
  79.3 1.6 collective-permute-start.8
  80.9 2.6 %collective-permute-start.9 = (bf16[1,224,1024]{2,1,0:T(8,128)(2,1)S(1)}, bf16[1,224,1024]{2,1,0:T(8,128)(2,1)S(1)}, u32[]{:S(2)}, u32[]{:S(2)}) collective-permute-start(bf16[1,224,1024]{2,1,0:T(8,128)(2,1)S(1)} %add_convert_fusion.2.refs_4_), channel_id=1, source_target_pairs={{0,8},{4,12},{8,0},{12,4},{1,9},{5,13},{9,1},{13,5},{2,10},{6,14},... | collective-permute-start | bytes 1376264 | tf_op jit(solution)/shard_map/ppermute | solution.py:375
  83.6 4.5 %decode.8 = (bf16[1,224,1024]{2,1,0:T(8,128)(2,1)S(1)}, bf16[1,160,1024]{2,1,0:T(8,128)(2,1)S(1)}) custom-call(s32[2]{0:T(128)S(1)} %pad_add_fusion.6.info_ref, bf16[384,2048]{1,0:T(8,128)(2,1)S(1)} %encode.3.refs_0_, bf16[384,2048]{1,0:T(8,128)(2,1)S(1)} %collective-permute-done.7.refs_1_, bf16[2048,4096]{1,0:T(8,128)(2,1)} %bitcast.29, ...), custom_call_target="tpu_custom_call" | custom-call | tf_op jit(solution)/shard_map/decode/pallas_call | solution.py:280
  88.1 0.6 collective-permute-start.11
  89.2 10.9 %collective-permute-done.8 = bf16[1,224,1024]{2,1,0:T(8,128)(2,1)S(1)} collective-permute-done((bf16[1,224,1024]{2,1,0:T(8,128)(2,1)S(1)}, bf16[1,224,1024]{2,1,0:T(8,128)(2,1)S(1)}, u32[]{:S(2)}, u32[]{:S(2)}) %collective-permute-start.8) | collective-permute-done | bytes 458784 | tf_op jit(solution)/shard_map/ppermute | solution.py:375
  100.1 1.6 collective-permute-done.9
  102.0 4.5 %decode.9 = (f32[1,224,1024]{2,1,0:T(8,128)S(1)}, bf16[1,160,1024]{2,1,0:T(8,128)(2,1)S(1)}) custom-call(s32[2]{0:T(128)S(1)} %pad_add_fusion.5.info_ref, bf16[384,2048]{1,0:T(8,128)(2,1)S(1)} %encode.3.refs_0_, bf16[384,2048]{1,0:T(8,128)(2,1)S(1)} %collective-permute-done.7.refs_1_, bf16[2048,4096]{1,0:T(8,128)(2,1)} %bitcast.30, ...), custom_call_target="tpu_custom_call" | custom-call | tf_op jit(solution)/shard_map/decode/pallas_call | solution.py:280
  106.8 3.6 %collective-permute-start.13 = (bf16[1,160,1024]{2,1,0:T(8,128)(2,1)S(1)}, bf16[1,160,1024]{2,1,0:T(8,128)(2,1)S(1)}, u32[]{:S(2)}, u32[]{:S(2)}) collective-permute-start(bf16[1,160,1024]{2,1,0:T(8,128)(2,1)S(1)} %add_convert_fusion.5.refs_5_), channel_id=1, source_target_pairs={{0,4},{4,0},{8,12},{12,8},{1,5},{5,1},{9,13},{13,9},{2,6},{6,2},{1... | collective-permute-start | bytes 983048 | tf_op jit(solution)/shard_map/ppermute | solution.py:375
  110.4 3.7 %collective-permute-done.10 = bf16[1,224,1024]{2,1,0:T(8,128)(2,1)S(1)} collective-permute-done((bf16[1,224,1024]{2,1,0:T(8,128)(2,1)S(1)}, bf16[1,224,1024]{2,1,0:T(8,128)(2,1)S(1)}, u32[]{:S(2)}, u32[]{:S(2)}) %collective-permute-start.10) | collective-permute-done | bytes 458784 | tf_op jit(solution)/shard_map/ppermute | solution.py:375
  114.5 4.7 %decode.10 = (bf16[1,112,1024]{2,1,0:T(8,128)(2,1)S(1)}, bf16[1,112,1024]{2,1,0:T(8,128)(2,1)S(1)}, bf16[1,160,1024]{2,1,0:T(8,128)(2,1)S(1)}) custom-call(s32[2]{0:T(128)S(1)} %pad_add_fusion.4.info_ref, bf16[384,2048]{1,0:T(8,128)(2,1)S(1)} %encode.3.refs_0_, bf16[384,2048]{1,0:T(8,128)(2,1)S(1)} %collective-permute-done.7.refs_1_, ...), custom_call_target="tpu_custom_call" | custom-call | tf_op jit(solution)/shard_map/decode/pallas_call | solution.py:280
  119.2 2.0 %collective-permute-start.19 = (bf16[1,112,1024]{2,1,0:T(8,128)(2,1)S(1)}, bf16[1,112,1024]{2,1,0:T(8,128)(2,1)S(1)}, u32[]{:S(2)}, u32[]{:S(2)}) collective-permute-start(bf16[1,112,1024]{2,1,0:T(8,128)(2,1)S(1)} %get-tuple-element.43.refs_5_), channel_id=1, source_target_pairs={{0,4},{4,0},{8,12},{12,8},{1,5},{5,1},{9,13},{13,9},{2,6},{6,2},{1... | collective-permute-start | bytes 688136 | tf_op jit(solution)/shard_map/ppermute | solution.py:375
  121.5 2.8 %collective-permute-start.17 = (bf16[1,160,1024]{2,1,0:T(8,128)(2,1)S(1)}, bf16[1,160,1024]{2,1,0:T(8,128)(2,1)S(1)}, u32[]{:S(2)}, u32[]{:S(2)}) collective-permute-start(bf16[1,160,1024]{2,1,0:T(8,128)(2,1)S(1)} %add_convert_fusion.4.refs_6_), channel_id=1, source_target_pairs={{0,8},{4,12},{8,0},{12,4},{1,9},{5,13},{9,1},{13,5},{2,10},{6,14},... | collective-permute-start | bytes 983048 | tf_op jit(solution)/shard_map/ppermute | solution.py:375
  124.4 4.5 %decode.11 = (f32[1,224,1024]{2,1,0:T(8,128)S(1)}, bf16[1,160,1024]{2,1,0:T(8,128)(2,1)S(1)}) custom-call(s32[2]{0:T(128)S(1)} %pad_add_fusion.2.info_ref, bf16[384,2048]{1,0:T(8,128)(2,1)S(1)} %encode.3.refs_0_, bf16[384,2048]{1,0:T(8,128)(2,1)S(1)} %collective-permute-done.7.refs_1_, bf16[2048,4096]{1,0:T(8,128)(2,1)} %bitcast.32, ...), custom_call_target="tpu_custom_call" | custom-call | tf_op jit(solution)/shard_map/decode/pallas_call | solution.py:280
  128.9 6.1 %collective-permute-done.18 = bf16[1,112,1024]{2,1,0:T(8,128)(2,1)S(1)} collective-permute-done((bf16[1,112,1024]{2,1,0:T(8,128)(2,1)S(1)}, bf16[1,112,1024]{2,1,0:T(8,128)(2,1)S(1)}, u32[]{:S(2)}, u32[]{:S(2)}) %collective-permute-start.18) | collective-permute-done | bytes 229408 | tf_op jit(solution)/shard_map/ppermute | solution.py:375
  135.0 5.1 %collective-permute-done.19 = bf16[1,112,1024]{2,1,0:T(8,128)(2,1)S(1)} collective-permute-done((bf16[1,112,1024]{2,1,0:T(8,128)(2,1)S(1)}, bf16[1,112,1024]{2,1,0:T(8,128)(2,1)S(1)}, u32[]{:S(2)}, u32[]{:S(2)}) %collective-permute-start.19) | collective-permute-done | bytes 229408 | tf_op jit(solution)/shard_map/ppermute | solution.py:375
  140.3 1.6 collective-permute-start.21
  142.1 2.0 %collective-permute-done.14 = bf16[1,160,1024]{2,1,0:T(8,128)(2,1)S(1)} collective-permute-done((bf16[1,160,1024]{2,1,0:T(8,128)(2,1)S(1)}, bf16[1,160,1024]{2,1,0:T(8,128)(2,1)S(1)}, u32[]{:S(2)}, u32[]{:S(2)}) %collective-permute-start.14) | collective-permute-done | bytes 327712 | tf_op jit(solution)/shard_map/ppermute | solution.py:370
  144.0 0.8 collective-permute-done.17
  144.8 5.1 %collective-permute-done.16 = bf16[1,160,1024]{2,1,0:T(8,128)(2,1)S(1)} collective-permute-done((bf16[1,160,1024]{2,1,0:T(8,128)(2,1)S(1)}, bf16[1,160,1024]{2,1,0:T(8,128)(2,1)S(1)}, u32[]{:S(2)}, u32[]{:S(2)}) %collective-permute-start.16) | collective-permute-done | bytes 327712 | tf_op jit(solution)/shard_map/ppermute | solution.py:375
  149.9 2.0 %collective-permute-done.21.refs_5_ = bf16[224,1024]{1,0:T(8,128)(2,1)S(1)} collective-permute-done((bf16[224,1024]{1,0:T(8,128)(2,1)S(1)}, bf16[224,1024]{1,0:T(8,128)(2,1)S(1)}, u32[]{:S(2)}, u32[]{:S(2)}) %collective-permute-start.21) | collective-permute-done | bytes 458784 | tf_op jit(solution)/shard_map/ppermute | solution.py:370
  151.9 1.6 finale.1
  153.5 1.8 %collective-permute-start.24 = (f32[8,128]{1,0:T(8,128)S(1)}, f32[8,128]{1,0:T(8,128)S(1)}, u32[]{:S(2)}, u32[]{:S(2)}) collective-permute-start(f32[8,128]{1,0:T(8,128)S(1)} %get-tuple-element.51), channel_id=1, source_target_pairs={{0,3},{1,0},{2,1},{3,2},{4,7},{5,4},{6,5},{7,6},{8,11},{9,8},{10,9... | collective-permute-start | bytes 12296 | tf_op jit(solution)/shard_map/ppermute | solution.py:370
  155.3 1.3 collective-permute-done.22
  156.6 0.6 collective-permute-done.23
  157.2 1.4 collective-permute-start.25
  158.6 1.5 collective-permute-start.26
  160.0 1.2 collective-permute-start.27
  161.3 1.3 collective-permute-done.25.refs_1_
  163.7 0.6 copy-done.13
  164.3 1.2 mean_ratio.1
  (64 shorter events, 4.3 us)
Async XLA Ops:
  0.6 10.8 %copy-start = (bf16[1,4096]{1,0:T(2,128)(2,1)S(1)}, bf16[1,4096]{1,0:T(2,128)(2,1)}, u32[]{:S(2)}) copy-start(bf16[1,4096]{1,0:T(2,128)(2,1)} %param.10) | copy-start | bytes 24580
  3.4 6.4 %collective-permute-start = (f32[1]{0:T(128)}, f32[1]{0:T(128)}, u32[]{:S(2)}, u32[]{:S(2)}) collective-permute-start(f32[1]{0:T(128)} %square_sum.1.after_ref), channel_id=1, source_target_pairs={{0,2},{2,0},{1,3},{3,1},{4,6},{6,4},{5,7},{7,5},{8,10},{10,8},{9,1... | collective-permute-start | bytes 20 | tf_op jit(solution)/shard_map/ppermute | solution.py:370
  11.2 23.7 %collective-permute-start.3 = (bf16[112,4096]{1,0:T(8,128)(2,1)}, bf16[112,4096]{1,0:T(8,128)(2,1)}, u32[]{:S(2)}, u32[]{:S(2)}) collective-permute-start(bf16[112,4096]{1,0:T(8,128)(2,1)} %get-tuple-element.33), channel_id=1, source_target_pairs={{0,2},{2,0},{1,3},{3,1},{4,6},{6,4},{5,7},{7,5},{8,10},{10,8},{9,1... | collective-permute-start | bytes 2752520 | tf_op jit(solution)/shard_map/ppermute | solution.py:370
  23.3 13.2 %collective-permute-start.1 = (bf16[384,1024]{1,0:T(8,128)(2,1)S(1)}, bf16[384,1024]{1,0:T(8,128)(2,1)S(1)}, u32[]{:S(2)}, u32[]{:S(2)}) collective-permute-start(bf16[384,1024]{1,0:T(8,128)(2,1)S(1)} %get-tuple-element.27.refs_0_), channel_id=1, source_target_pairs={{0,1},{2,3},{4,5},{6,7},{8,9},{10,11},{12,13},{14,15},{16,17},{18,... | collective-permute-start | bytes 2359304 | tf_op jit(solution)/shard_map/ppermute | solution.py:437
  24.6 11.8 %collective-permute-start.2 = (bf16[384,1024]{1,0:T(8,128)(2,1)S(1)}, bf16[384,1024]{1,0:T(8,128)(2,1)S(1)}, u32[]{:S(2)}, u32[]{:S(2)}) collective-permute-start(bf16[384,1024]{1,0:T(8,128)(2,1)S(1)} %get-tuple-element.28.refs_1_), channel_id=1, source_target_pairs={{0,1},{2,3},{4,5},{6,7},{8,9},{10,11},{12,13},{14,15},{16,17},{18,... | collective-permute-start | bytes 2359304 | tf_op jit(solution)/shard_map/ppermute | solution.py:437
  26.0 39.6 %collective-permute-start.5 = (bf16[160,4096]{1,0:T(8,128)(2,1)}, bf16[160,4096]{1,0:T(8,128)(2,1)}, u32[]{:S(2)}, u32[]{:S(2)}) collective-permute-start(bf16[160,4096]{1,0:T(8,128)(2,1)} %get-tuple-element.34), channel_id=1, source_target_pairs={{0,2},{2,0},{1,3},{3,1},{4,6},{6,4},{5,7},{7,5},{8,10},{10,8},{9,1... | collective-permute-start | bytes 3932168 | tf_op jit(solution)/shard_map/ppermute | solution.py:370
  34.8 30.7 %collective-permute-start.4 = (bf16[112,4096]{1,0:T(8,128)(2,1)}, bf16[112,4096]{1,0:T(8,128)(2,1)}, u32[]{:S(2)}, u32[]{:S(2)}) collective-permute-start(bf16[112,4096]{1,0:T(8,128)(2,1)} %collective-permute-done.3.refs_0_), channel_id=1, source_target_pairs={{0,4},{4,0},{8,12},{12,8},{1,5},{5,1},{9,13},{13,9},{2,6},{6,2},{1... | collective-permute-start | bytes 2752520 | tf_op jit(solution)/shard_map/ppermute | solution.py:375
  44.3 0.9 copy-start.3
  45.2 0.8 copy-start.5
  46.1 0.8 copy-start.8
  46.8 17.6 %collective-permute-start.6 = (bf16[1,224,1024]{2,1,0:T(8,128)(2,1)}, bf16[1,224,1024]{2,1,0:T(8,128)(2,1)}, u32[]{:S(2)}, u32[]{:S(2)}) collective-permute-start(bf16[1,224,1024]{2,1,0:T(8,128)(2,1)} %get-tuple-element.29.refs_6_), channel_id=1, source_target_pairs={{0,4},{4,0},{8,12},{12,8},{1,5},{5,1},{9,13},{13,9},{2,6},{6,2},{1... | collective-permute-start | bytes 1376264 | tf_op jit(solution)/shard_map/ppermute | solution.py:375
  65.5 13.7 %copy-start.9 = (bf16[1,224,1024]{2,1,0:T(8,128)(2,1)S(1)}, bf16[1,224,1024]{2,1,0:T(8,128)(2,1)}, u32[]{:S(2)}) copy-start(bf16[1,224,1024]{2,1,0:T(8,128)(2,1)} %copy-done.8) | copy-start | bytes 1376260
  77.9 5.7 %collective-permute-start.7 = (bf16[384,2048]{1,0:T(8,128)(2,1)S(1)}, bf16[384,2048]{1,0:T(8,128)(2,1)S(1)}, u32[]{:S(2)}, u32[]{:S(2)}) collective-permute-start(bf16[384,2048]{1,0:T(8,128)(2,1)S(1)} %encode.3.refs_0_), channel_id=1, source_target_pairs={{0,1},{2,3},{4,5},{6,7},{8,9},{10,11},{12,13},{14,15},{16,17},{18,... | collective-permute-start | bytes 4718600 | tf_op jit(solution)/shard_map/ppermute | solution.py:437
  79.3 20.8 %collective-permute-start.8 = (bf16[1,224,1024]{2,1,0:T(8,128)(2,1)S(1)}, bf16[1,224,1024]{2,1,0:T(8,128)(2,1)S(1)}, u32[]{:S(2)}, u32[]{:S(2)}) collective-permute-start(bf16[1,224,1024]{2,1,0:T(8,128)(2,1)S(1)} %copy-done.9), channel_id=1, source_target_pairs={{0,4},{4,0},{8,12},{12,8},{1,5},{5,1},{9,13},{13,9},{2,6},{6,2},{1... | collective-permute-start | bytes 1376264 | tf_op jit(solution)/shard_map/ppermute | solution.py:375
  80.9 20.8 %collective-permute-start.9 = (bf16[1,224,1024]{2,1,0:T(8,128)(2,1)S(1)}, bf16[1,224,1024]{2,1,0:T(8,128)(2,1)S(1)}, u32[]{:S(2)}, u32[]{:S(2)}) collective-permute-start(bf16[1,224,1024]{2,1,0:T(8,128)(2,1)S(1)} %add_convert_fusion.2.refs_4_), channel_id=1, source_target_pairs={{0,8},{4,12},{8,0},{12,4},{1,9},{5,13},{9,1},{13,5},{2,10},{6,14},... | collective-permute-start | bytes 1376264 | tf_op jit(solution)/shard_map/ppermute | solution.py:375
  88.1 18.7 %collective-permute-start.11 = (bf16[1,160,1024]{2,1,0:T(8,128)(2,1)S(1)}, bf16[1,160,1024]{2,1,0:T(8,128)(2,1)S(1)}, u32[]{:S(2)}, u32[]{:S(2)}) collective-permute-start(bf16[1,160,1024]{2,1,0:T(8,128)(2,1)S(1)} %get-tuple-element.41), channel_id=1, source_target_pairs={{0,2},{2,0},{1,3},{3,1},{4,6},{6,4},{5,7},{7,5},{8,10},{10,8},{9,1... | collective-permute-start | bytes 983048 | tf_op jit(solution)/shard_map/ppermute | solution.py:370
  88.8 25.3 %collective-permute-start.10 = (bf16[1,224,1024]{2,1,0:T(8,128)(2,1)S(1)}, bf16[1,224,1024]{2,1,0:T(8,128)(2,1)S(1)}, u32[]{:S(2)}, u32[]{:S(2)}) collective-permute-start(bf16[1,224,1024]{2,1,0:T(8,128)(2,1)S(1)} %get-tuple-element.36.refs_4_), channel_id=1, source_target_pairs={{0,4},{4,0},{8,12},{12,8},{1,5},{5,1},{9,13},{13,9},{2,6},{6,2},{1... | collective-permute-start | bytes 1376264 | tf_op jit(solution)/shard_map/ppermute | solution.py:375
  101.9 4.8 %copy-start.6 = (f32[1,160,1024]{2,1,0:T(8,128)S(1)}, f32[1,160,1024]{2,1,0:T(8,128)}, u32[]{:S(2)}) copy-start(f32[1,160,1024]{2,1,0:T(8,128)} %copy-done.5) | copy-start | bytes 1966084
  106.5 14.8 %collective-permute-start.12 = (bf16[1,160,1024]{2,1,0:T(8,128)(2,1)S(1)}, bf16[1,160,1024]{2,1,0:T(8,128)(2,1)S(1)}, u32[]{:S(2)}, u32[]{:S(2)}) collective-permute-start(bf16[1,160,1024]{2,1,0:T(8,128)(2,1)S(1)} %get-tuple-element.45), channel_id=1, source_target_pairs={{0,2},{2,0},{1,3},{3,1},{4,6},{6,4},{5,7},{7,5},{8,10},{10,8},{9,1... | collective-permute-start | bytes 983048 | tf_op jit(solution)/shard_map/ppermute | solution.py:370
  106.8 14.5 %collective-permute-start.13 = (bf16[1,160,1024]{2,1,0:T(8,128)(2,1)S(1)}, bf16[1,160,1024]{2,1,0:T(8,128)(2,1)S(1)}, u32[]{:S(2)}, u32[]{:S(2)}) collective-permute-start(bf16[1,160,1024]{2,1,0:T(8,128)(2,1)S(1)} %add_convert_fusion.5.refs_5_), channel_id=1, source_target_pairs={{0,4},{4,0},{8,12},{12,8},{1,5},{5,1},{9,13},{13,9},{2,6},{6,2},{1... | collective-permute-start | bytes 983048 | tf_op jit(solution)/shard_map/ppermute | solution.py:375
  114.2 25.8 %collective-permute-start.20 = (bf16[1,224,1024]{2,1,0:T(8,128)(2,1)S(1)}, bf16[1,224,1024]{2,1,0:T(8,128)(2,1)S(1)}, u32[]{:S(2)}, u32[]{:S(2)}) collective-permute-start(bf16[1,224,1024]{2,1,0:T(8,128)(2,1)S(1)} %add_convert_fusion.1.refs_4_), channel_id=1, source_target_pairs={{0,8},{4,12},{8,0},{12,4},{1,9},{5,13},{9,1},{13,5},{2,10},{6,14},... | collective-permute-start | bytes 1376264 | tf_op jit(solution)/shard_map/ppermute | solution.py:375
  119.1 15.8 %collective-permute-start.18 = (bf16[1,112,1024]{2,1,0:T(8,128)(2,1)S(1)}, bf16[1,112,1024]{2,1,0:T(8,128)(2,1)S(1)}, u32[]{:S(2)}, u32[]{:S(2)}) collective-permute-start(bf16[1,112,1024]{2,1,0:T(8,128)(2,1)S(1)} %get-tuple-element.42.refs_4_), channel_id=1, source_target_pairs={{0,4},{4,0},{8,12},{12,8},{1,5},{5,1},{9,13},{13,9},{2,6},{6,2},{1... | collective-permute-start | bytes 688136 | tf_op jit(solution)/shard_map/ppermute | solution.py:375
  119.2 20.8 %collective-permute-start.19 = (bf16[1,112,1024]{2,1,0:T(8,128)(2,1)S(1)}, bf16[1,112,1024]{2,1,0:T(8,128)(2,1)S(1)}, u32[]{:S(2)}, u32[]{:S(2)}) collective-permute-start(bf16[1,112,1024]{2,1,0:T(8,128)(2,1)S(1)} %get-tuple-element.43.refs_5_), channel_id=1, source_target_pairs={{0,4},{4,0},{8,12},{12,8},{1,5},{5,1},{9,13},{13,9},{2,6},{6,2},{1... | collective-permute-start | bytes 688136 | tf_op jit(solution)/shard_map/ppermute | solution.py:375
  121.2 20.7 %collective-permute-start.15 = (bf16[1,160,1024]{2,1,0:T(8,128)(2,1)S(1)}, bf16[1,160,1024]{2,1,0:T(8,128)(2,1)S(1)}, u32[]{:S(2)}, u32[]{:S(2)}) collective-permute-start(bf16[1,160,1024]{2,1,0:T(8,128)(2,1)S(1)} %get-tuple-element.48), channel_id=1, source_target_pairs={{0,2},{2,0},{1,3},{3,1},{4,6},{6,4},{5,7},{7,5},{8,10},{10,8},{9,1... | collective-permute-start | bytes 983048 | tf_op jit(solution)/shard_map/ppermute | solution.py:370
  121.5 23.3 %collective-permute-start.17 = (bf16[1,160,1024]{2,1,0:T(8,128)(2,1)S(1)}, bf16[1,160,1024]{2,1,0:T(8,128)(2,1)S(1)}, u32[]{:S(2)}, u32[]{:S(2)}) collective-permute-start(bf16[1,160,1024]{2,1,0:T(8,128)(2,1)S(1)} %add_convert_fusion.4.refs_6_), channel_id=1, source_target_pairs={{0,8},{4,12},{8,0},{12,4},{1,9},{5,13},{9,1},{13,5},{2,10},{6,14},... | collective-permute-start | bytes 983048 | tf_op jit(solution)/shard_map/ppermute | solution.py:375
  128.9 13.0 %copy-start.4 = (f32[1,160,1024]{2,1,0:T(8,128)S(1)}, f32[1,160,1024]{2,1,0:T(8,128)}, u32[]{:S(2)}) copy-start(f32[1,160,1024]{2,1,0:T(8,128)} %copy-done.3) | copy-start | bytes 1966084
  135.0 9.0 %collective-permute-start.14 = (bf16[1,160,1024]{2,1,0:T(8,128)(2,1)S(1)}, bf16[1,160,1024]{2,1,0:T(8,128)(2,1)S(1)}, u32[]{:S(2)}, u32[]{:S(2)}) collective-permute-start(bf16[1,160,1024]{2,1,0:T(8,128)(2,1)S(1)} %get-tuple-element.46), channel_id=1, source_target_pairs={{0,2},{2,0},{1,3},{3,1},{4,6},{6,4},{5,7},{7,5},{8,10},{10,8},{9,1... | collective-permute-start | bytes 983048 | tf_op jit(solution)/shard_map/ppermute | solution.py:370
  140.1 11.8 %copy-start.2 = (bf16[1,384,1024]{2,1,0:T(8,128)(2,1)S(1)}, bf16[1,384,1024]{2,1,0:T(8,128)(2,1)}, u32[]{:S(2)}) copy-start(bf16[1,384,1024]{2,1,0:T(8,128)(2,1)} %param.8) | copy-start | bytes 2359300
  140.1 11.8 %copy-start.7 = (bf16[1,1024]{1,0:T(2,128)(2,1)S(1)}, bf16[1,1024]{1,0:T(2,128)(2,1)}, u32[]{:S(2)}) copy-start(bf16[1,1024]{1,0:T(2,128)(2,1)} %b_ref.1) | copy-start | bytes 6148
  140.3 11.6 %collective-permute-start.21 = (bf16[224,1024]{1,0:T(8,128)(2,1)S(1)}, bf16[224,1024]{1,0:T(8,128)(2,1)S(1)}, u32[]{:S(2)}, u32[]{:S(2)}) collective-permute-start(bf16[224,1024]{1,0:T(8,128)(2,1)S(1)} %fusion), channel_id=1, source_target_pairs={{0,2},{2,0},{1,3},{3,1},{4,6},{6,4},{5,7},{7,5},{8,10},{10,8},{9,1... | collective-permute-start | bytes 1376264 | tf_op jit(solution)/shard_map/ppermute | solution.py:370
  142.0 7.9 %collective-permute-start.16 = (bf16[1,160,1024]{2,1,0:T(8,128)(2,1)S(1)}, bf16[1,160,1024]{2,1,0:T(8,128)(2,1)S(1)}, u32[]{:S(2)}, u32[]{:S(2)}) collective-permute-start(bf16[1,160,1024]{2,1,0:T(8,128)(2,1)S(1)} %add_convert_fusion.3), channel_id=1, source_target_pairs={{0,4},{4,0},{8,12},{12,8},{1,5},{5,1},{9,13},{13,9},{2,6},{6,2},{1... | collective-permute-start | bytes 983048 | tf_op jit(solution)/shard_map/ppermute | solution.py:375
  151.9 13.6 %copy-start.1 = (bf16[1,4096]{1,0:T(2,128)(2,1)S(1)}, bf16[1,4096]{1,0:T(2,128)(2,1)}, u32[]{:S(2)}) copy-start(bf16[1,4096]{1,0:T(2,128)(2,1)} %param.10) | copy-start | bytes 24580
  153.5 3.0 %collective-permute-start.22 = (f32[8,128]{1,0:T(8,128)S(1)}, f32[8,128]{1,0:T(8,128)S(1)}, u32[]{:S(2)}, u32[]{:S(2)}) collective-permute-start(f32[8,128]{1,0:T(8,128)S(1)} %get-tuple-element.51), channel_id=1, source_target_pairs={{0,1},{1,2},{2,3},{3,0},{4,5},{5,6},{6,7},{7,4},{8,9},{9,10},{10,1... | collective-permute-start | bytes 12296 | tf_op jit(solution)/shard_map/ppermute | solution.py:370
  153.5 3.6 %collective-permute-start.23 = (f32[8,128]{1,0:T(8,128)S(1)}, f32[8,128]{1,0:T(8,128)S(1)}, u32[]{:S(2)}, u32[]{:S(2)}) collective-permute-start(f32[8,128]{1,0:T(8,128)S(1)} %get-tuple-element.51), channel_id=1, source_target_pairs={{0,2},{1,3},{2,0},{3,1},{4,6},{5,7},{6,4},{7,5},{8,10},{9,11},{10,... | collective-permute-start | bytes 12296 | tf_op jit(solution)/shard_map/ppermute | solution.py:370
  153.5 3.6 %collective-permute-start.24 = (f32[8,128]{1,0:T(8,128)S(1)}, f32[8,128]{1,0:T(8,128)S(1)}, u32[]{:S(2)}, u32[]{:S(2)}) collective-permute-start(f32[8,128]{1,0:T(8,128)S(1)} %get-tuple-element.51), channel_id=1, source_target_pairs={{0,3},{1,0},{2,1},{3,2},{4,7},{5,4},{6,5},{7,6},{8,11},{9,8},{10,9... | collective-permute-start | bytes 12296 | tf_op jit(solution)/shard_map/ppermute | solution.py:370
  157.2 6.5 %copy-start.10 = (f32[8,128]{1,0:T(8,128)}, f32[8,128]{1,0:T(8,128)S(1)}, u32[]{:S(2)}) copy-start(f32[8,128]{1,0:T(8,128)S(1)} %add_add_fusion.refs_0_) | copy-start | bytes 12292
  157.2 5.5 %collective-permute-start.25 = (f32[8,128]{1,0:T(8,128)S(1)}, f32[8,128]{1,0:T(8,128)S(1)}, u32[]{:S(2)}, u32[]{:S(2)}) collective-permute-start(f32[8,128]{1,0:T(8,128)S(1)} %add_add_fusion.refs_0_), channel_id=1, source_target_pairs={{0,4},{4,8},{8,12},{12,0},{1,5},{5,9},{9,13},{13,1},{2,6},{6,10},{... | collective-permute-start | bytes 12296 | tf_op jit(solution)/shard_map/ppermute | solution.py:370
  158.6 4.5 %collective-permute-start.26 = (f32[8,128]{1,0:T(8,128)S(1)}, f32[8,128]{1,0:T(8,128)S(1)}, u32[]{:S(2)}, u32[]{:S(2)}) collective-permute-start(f32[8,128]{1,0:T(8,128)S(1)} %add_add_fusion.refs_0_), channel_id=1, source_target_pairs={{0,8},{4,12},{8,0},{12,4},{1,9},{5,13},{9,1},{13,5},{2,10},{6,14},... | collective-permute-start | bytes 12296 | tf_op jit(solution)/shard_map/ppermute | solution.py:370
  160.0 3.6 %collective-permute-start.27 = (f32[8,128]{1,0:T(8,128)S(1)}, f32[8,128]{1,0:T(8,128)S(1)}, u32[]{:S(2)}, u32[]{:S(2)}) collective-permute-start(f32[8,128]{1,0:T(8,128)S(1)} %add_add_fusion.refs_0_), channel_id=1, source_target_pairs={{0,12},{4,0},{8,4},{12,8},{1,13},{5,1},{9,5},{13,9},{2,14},{6,2},{... | collective-permute-start | bytes 12296 | tf_op jit(solution)/shard_map/ppermute | solution.py:370
  162.6 1.0 copy-start.11
  163.1 0.6 copy-start.12
  163.7 0.6 copy-start.13

commit v10 on v9

--- a/solution.py
+++ b/solution.py
@@ -458,17 +458,16 @@
     inside = ((first, middle),)
     outside = ((0, first), (rows - first, first))
     spans = [(0, group, inside), (group, group, inside), (0, group, outside), (group, group, outside)]
-    far_sent, near_sent, far_out_sent, near_out_sent = products(
+    sent_in, far_out_sent, near_out_sent = products(
         codes, earlier, info(other, (far, near)),
-        [span + (dtype,) for span, dtype in zip(spans, (narrow, narrow, jnp.float32, jnp.float32))], [])
-    far_in = swapped(far_sent, "latent", 1)
-    near_in = swapped(near_sent, "latent", 1)
+        [(0, 2 * group, inside, narrow)] + [span + (jnp.float32,) for span in spans[2:]], [])
+    there_in = swapped(sent_in, "latent", 1)
     far_kept, near_kept, far_out_kept, near_out_kept = products(
-        codes, earlier, info(mine_bit, (far, near)), [span + (jnp.float32,) for span in spans], [far_sent])
-    across_in = (far_kept + wide(far_in)).astype(narrow)
-    total_in = near_kept + wide(near_in) + wide(swapped(across_in, "latent", 2))
-
-    after = across_in
+        codes, earlier, info(mine_bit, (far, near)), [span + (jnp.float32,) for span in spans], [sent_in])
+    across_in = (far_kept + wide(there_in[:group])).astype(narrow)
+    total_in = near_kept + wide(there_in[group:]) + wide(swapped(across_in, "latent", 2))
+
+    after, before = near_kept, [across_in]
     returned = []
     far_out_back, near_out_back, near_out_kept_back = [], [], []
 
@@ -479,7 +478,7 @@
         codes = encode(
             [(mine, 0, edge), (theirs, 0, edge), (inner_rows, 0, rows - 2 * edge)],
             places(side * (rows - edge), (1 - side) * (rows - edge), edge),
-            inv, enc_w, bias, 1, [after])
+            inv, enc_w, bias, min(2, lat_dev // 256), [after])
         earlier = earlier_of(codes)
 
         def quarter_of(low, high, spans, dtype, also):
@@ -488,7 +487,7 @@
                 [(0, group, span, dtype) for span in spans] + [(0, group, outside, narrow)], also)
             return insides, shifted(outer, "token", back)
 
-        (far_sent,), far_back = quarter_of(other, far, [inside], narrow, [])
+        (far_sent,), far_back = quarter_of(other, far, [inside], narrow, before)
         far_in = swapped(far_sent, "latent", 1)
         (far_kept,), far_kept_back = quarter_of(mine_bit, far, [inside], jnp.float32, [far_sent, total_in])
         far_out_back.append(far_back)
@@ -510,7 +509,7 @@
         returned.append(shifted(part.astype(narrow), "token", back))
         near_out_back.append(near_back)
         near_out_kept_back.append(near_kept_back)
-        after = near_kept
+        after, before = near_kept, []
 
     near_out = swapped(joined(near_out_sent, near_out_back).astype(narrow), "latent", 1)
     across_out = swapped(far_out_kept, "latent", 2)

time: 166 us -> 171 us (1.030)
  waiting for transfers between devices: 58.5 us -> 61.7 us
  starting transfers between devices: 32.9 us -> 34.8 us
    ppermute x14, waiting for transfers between devices: 15.1 us -> 22.6 us  [shifted(): lax.ppermute(value, axis, [(i, (i + distance) % n) for i in range(n)])]
    ppermute x11 -> x10, waiting for transfers between devices: 43.4 us -> 39.1 us  [swapped(): return lax.ppermute(value, axis, [(i, i ^ bit) for i in range(n)])]
    ppermute x14, starting transfers between devices: 13.5 us -> 16.9 us  [shifted(): lax.ppermute(value, axis, [(i, (i + distance) % n) for i in range(n)])]
    ppermute x11 -> x10, starting transfers between devices: 15.3 us -> 12.5 us  [swapped(): return lax.ppermute(value, axis, [(i, i ^ bit) for i in range(n)])]
    ppermute x3 -> x4, starting transfers between devices: 4.07 us -> 5.36 us  [earlier_of(): return [lax.ppermute(part, 'layer', [(0, 1)]) for part in codes]]
  transfers between devices with their start and end apart: 28 -> 28, of which waited for: 17 -> 14; matrix products, arithmetic and copies ran while one was open for 1% -> 2% of each run, Pallas kernels for 29% -> 36%
where the time goes in v10:
time: 171 us
  Pallas kernels  66.3 us (39%)
  waiting for transfers between devices  61.7 us (36%)
  starting transfers between devices  34.8 us (20%)
  other arithmetic  3.44 us (2%)
  local copies, waits for them, and re-layouts  2.3 us (1%)
  between operations  2.2 us (1%)
    ppermute x10, waiting for transfers between devices, swapped(): return lax.ppermute(value, axis, [(i, i ^ bit) for i in range(n)])  39.1 us
    pallas_call x6, Pallas kernels, decode(): pl.pallas_call(body, in_specs=[pl.BlockSpec(memory_space=pltpu.SMEM)] + [...  33.2 us
    pallas_call x2, Pallas kernels, encode(): pl.pallas_call(body, in_specs=[pl.BlockSpec(memory_space=pltpu.SMEM), pl....  24.1 us
    ppermute x14, waiting for transfers between devices, shifted(): lax.ppermute(value, axis, [(i, (i + distance) % n) for i in range(n)])  22.6 us
    ppermute x14, starting transfers between devices, shifted(): lax.ppermute(value, axis, [(i, (i + distance) % n) for i in range(n)])  16.9 us
    ppermute x10, starting transfers between devices, swapped(): return lax.ppermute(value, axis, [(i, i ^ bit) for i in range(n)])  12.5 us
    ppermute x4, starting transfers between devices, earlier_of(): return [lax.ppermute(part, 'layer', [(0, 1)]) for part in codes]  5.36 us
  transfers between devices with their start and end apart: 28, of which 14 were waited for; matrix products, arithmetic and copies ran while one was open for 2% of the time, Pallas kernels for 36%

profile of v10, /device:TPU:0, one launch (start us, length us, event | category | flops | bytes accessed | tf_op | source)
XLA Modules:
  0.0 170.6 jit_solution(11595691977952898004)
XLA Ops:
  0.6 2.7 %square_sum.1.after_ref = f32[1]{0:T(128)} custom-call(bf16[384,4096]{1,0:T(8,128)(2,1)} %bitcast.35), custom_call_target="tpu_custom_call" | custom-call | tf_op jit(solution)/shard_map/square_sum/pallas_call | solution.py:47
  3.4 3.0 %collective-permute-start = (f32[1]{0:T(128)}, f32[1]{0:T(128)}, u32[]{:S(2)}, u32[]{:S(2)}) collective-permute-start(f32[1]{0:T(128)} %square_sum.1.after_ref), channel_id=1, source_target_pairs={{0,2},{2,0},{1,3},{3,1},{4,6},{6,4},{5,7},{7,5},{8,10},{10,8},{9,1... | collective-permute-start | bytes 20 | tf_op jit(solution)/shard_map/ppermute | solution.py:370
  6.4 3.4 %cut.1 = (bf16[112,4096]{1,0:T(8,128)(2,1)}, bf16[160,4096]{1,0:T(8,128)(2,1)}) custom-call(s32[1]{0:T(128)} %bitcast.12.side_ref, f32[1]{0:T(128)} %square_sum.1.after_ref, bf16[384,4096]{1,0:T(8,128)(2,1)} %bitcast.36), custom_call_target="tpu_custom_call" | custom-call | tf_op jit(solution)/shard_map/cut/pallas_call | solution.py:81
  11.5 11.8 %encode.2 = (bf16[384,1024]{1,0:T(8,128)(2,1)S(1)}, bf16[384,1024]{1,0:T(8,128)(2,1)S(1)}) custom-call(s32[1]{0:T(128)} %constant.58.clone.1.places_ref, f32[1]{0:T(128)S(6)} %sqrt.3.inv_ref.after_ref, bf16[1,2048]{1,0:T(2,128)(2,1)S(1)} %constant_dynamic-slice_fusion.b_ref, bf16[384,4096]{1,0:T(8,128)(2,1)} %bitcast.37, bf16[4096,2048]{1,0:T(8,128)(2,1)} %bitcast.33), custom_call_target="tpu_custom_call" | custom-call | tf_op jit(solution)/shard_map/encode/pallas_call | solution.py:181
  23.3 1.3 collective-permute-start.1
  24.7 1.3 collective-permute-start.2
  26.0 1.7 collective-permute-start.5
  27.7 7.0 %collective-permute-done.3.refs_0_ = bf16[112,4096]{1,0:T(8,128)(2,1)} collective-permute-done((bf16[112,4096]{1,0:T(8,128)(2,1)}, bf16[112,4096]{1,0:T(8,128)(2,1)}, u32[]{:S(2)}, u32[]{:S(2)}) %collective-permute-start.3) | collective-permute-done | bytes 917536 | tf_op jit(solution)/shard_map/ppermute | solution.py:370
  34.7 1.6 collective-permute-start.4
  36.3 8.0 %decode.6 = (bf16[2,224,1024]{2,1,0:T(8,128)(2,1)}, f32[1,160,1024]{2,1,0:T(8,128)S(1)}, f32[1,160,1024]{2,1,0:T(8,128)S(1)}) custom-call(s32[3]{0:T(128)S(1)} %get-tuple-element.55.info_ref, bf16[384,1024]{1,0:T(8,128)(2,1)S(1)} %get-tuple-element.28.refs_0_, bf16[384,1024]{1,0:T(8,128)(2,1)S(1)} %get-tuple-element.29.refs_1_, ...), custom_call_target="tpu_custom_call" | custom-call | tf_op jit(solution)/shard_map/decode/pallas_call | solution.py:280
  44.4 0.8 copy-done.3
  45.2 0.8 copy-done.5
  46.5 7.1 %decode.7 = (f32[1,224,1024]{2,1,0:T(8,128)S(1)}, f32[1,224,1024]{2,1,0:T(8,128)S(1)}, f32[1,160,1024]{2,1,0:T(8,128)S(1)}, f32[1,160,1024]{2,1,0:T(8,128)S(1)}) custom-call(s32[3]{0:T(128)S(1)} %get-tuple-element.54.info_ref, bf16[384,1024]{1,0:T(8,128)(2,1)S(1)} %get-tuple-element.28.refs_0_, bf16[384,1024]{1,0:T(8,128)(2,1)S(1)} %get-tuple-element.29.refs_1_, ...), custom_call_target="tpu_custom_call" | custom-call | tf_op jit(solution)/shard_map/decode/pallas_call | solution.py:280
  53.6 7.7 %collective-permute-done.5.refs_2_ = bf16[160,4096]{1,0:T(8,128)(2,1)} collective-permute-done((bf16[160,4096]{1,0:T(8,128)(2,1)}, bf16[160,4096]{1,0:T(8,128)(2,1)}, u32[]{:S(2)}, u32[]{:S(2)}) %collective-permute-start.5) | collective-permute-done | bytes 1310752 | tf_op jit(solution)/shard_map/ppermute | solution.py:370
  61.3 12.3 %encode.3 = (bf16[384,1024]{1,0:T(8,128)(2,1)S(1)}, bf16[384,1024]{1,0:T(8,128)(2,1)S(1)}) custom-call(s32[3]{0:T(128)S(1)} %pad_add_fusion.3.places_ref, f32[1]{0:T(128)S(6)} %sqrt.3.inv_ref.after_ref, bf16[1,2048]{1,0:T(2,128)(2,1)S(1)} %constant_dynamic-slice_fusion.b_ref, bf16[112,4096]{1,0:T(8,128)(2,1)} %collective-permute-done.3.refs_0_, ...), custom_call_target="tpu_custom_call" | custom-call | tf_op jit(solution)/shard_map/encode/pallas_call | solution.py:181
  73.6 1.3 collective-permute-start.6
  75.0 1.3 collective-permute-start.7
  76.3 1.1 add_convert_fusion.2.refs_6_
  77.5 2.7 %collective-permute-start.9 = (bf16[1,224,1024]{2,1,0:T(8,128)(2,1)S(1)}, bf16[1,224,1024]{2,1,0:T(8,128)(2,1)S(1)}, u32[]{:S(2)}, u32[]{:S(2)}) collective-permute-start(bf16[1,224,1024]{2,1,0:T(8,128)(2,1)S(1)} %add_convert_fusion.2.refs_6_), channel_id=1, source_target_pairs={{0,8},{4,12},{8,0},{12,4},{1,9},{5,13},{9,1},{13,5},{2,10},{6,14},... | collective-permute-start | bytes 1376264 | tf_op jit(solution)/shard_map/ppermute | solution.py:375
  80.2 4.5 %decode.8 = (bf16[1,224,1024]{2,1,0:T(8,128)(2,1)S(1)}, bf16[1,160,1024]{2,1,0:T(8,128)(2,1)S(1)}) custom-call(s32[2]{0:T(128)S(1)} %pad_add_fusion.6.info_ref, bf16[384,1024]{1,0:T(8,128)(2,1)S(1)} %get-tuple-element.37.refs_0_, bf16[384,1024]{1,0:T(8,128)(2,1)S(1)} %get-tuple-element.38.refs_1_, bf16[384,1024]{1,0:T(8,128)(2,1)S(1)} %collective-permute-done.6.refs_2_, ...), custom_call_target="tpu_custom_call" | custom-call | tf_op jit(solution)/shard_map/decode/pallas_call | solution.py:280
  84.7 0.6 collective-permute-start.11
  85.4 1.6 collective-permute-start.10
  87.0 12.4 %collective-permute-done.9 = bf16[1,224,1024]{2,1,0:T(8,128)(2,1)S(1)} collective-permute-done((bf16[1,224,1024]{2,1,0:T(8,128)(2,1)S(1)}, bf16[1,224,1024]{2,1,0:T(8,128)(2,1)S(1)}, u32[]{:S(2)}, u32[]{:S(2)}) %collective-permute-start.9) | collective-permute-done | bytes 458784 | tf_op jit(solution)/shard_map/ppermute | solution.py:375
  99.3 1.2 convert_add_fusion.refs_7_
  100.6 4.5 %decode.9 = (f32[1,224,1024]{2,1,0:T(8,128)S(1)}, bf16[1,160,1024]{2,1,0:T(8,128)(2,1)S(1)}) custom-call(s32[2]{0:T(128)S(1)} %pad_add_fusion.5.info_ref, bf16[384,1024]{1,0:T(8,128)(2,1)S(1)} %get-tuple-element.37.refs_0_, bf16[384,1024]{1,0:T(8,128)(2,1)S(1)} %get-tuple-element.38.refs_1_, bf16[384,1024]{1,0:T(8,128)(2,1)S(1)} %collective-permute-done.6.refs_2_, ...), custom_call_target="tpu_custom_call" | custom-call | tf_op jit(solution)/shard_map/decode/pallas_call | solution.py:280
  105.1 0.5 collective-permute-start.12
  105.7 0.7 collective-permute-start.13
  106.7 3.4 %collective-permute-start.20 = (bf16[1,224,1024]{2,1,0:T(8,128)(2,1)S(1)}, bf16[1,224,1024]{2,1,0:T(8,128)(2,1)S(1)}, u32[]{:S(2)}, u32[]{:S(2)}) collective-permute-start(bf16[1,224,1024]{2,1,0:T(8,128)(2,1)S(1)} %add_convert_fusion.1.refs_6_), channel_id=1, source_target_pairs={{0,8},{4,12},{8,0},{12,4},{1,9},{5,13},{9,1},{13,5},{2,10},{6,14},... | collective-permute-start | bytes 1376264 | tf_op jit(solution)/shard_map/ppermute | solution.py:375
  110.3 4.7 %decode.10 = (bf16[1,112,1024]{2,1,0:T(8,128)(2,1)S(1)}, bf16[1,112,1024]{2,1,0:T(8,128)(2,1)S(1)}, bf16[1,160,1024]{2,1,0:T(8,128)(2,1)S(1)}) custom-call(s32[2]{0:T(128)S(1)} %pad_add_fusion.4.info_ref, bf16[384,1024]{1,0:T(8,128)(2,1)S(1)} %get-tuple-element.37.refs_0_, bf16[384,1024]{1,0:T(8,128)(2,1)S(1)} %get-tuple-element.38.refs_1_, ...), custom_call_target="tpu_custom_call" | custom-call | tf_op jit(solution)/shard_map/decode/pallas_call | solution.py:280
  114.9 1.5 collective-permute-start.15
  116.5 2.0 %collective-permute-start.18 = (bf16[1,112,1024]{2,1,0:T(8,128)(2,1)S(1)}, bf16[1,112,1024]{2,1,0:T(8,128)(2,1)S(1)}, u32[]{:S(2)}, u32[]{:S(2)}) collective-permute-start(bf16[1,112,1024]{2,1,0:T(8,128)(2,1)S(1)} %get-tuple-element.44.refs_6_), channel_id=1, source_target_pairs={{0,4},{4,0},{8,12},{12,8},{1,5},{5,1},{9,13},{13,9},{2,6},{6,2},{1... | collective-permute-start | bytes 688136 | tf_op jit(solution)/shard_map/ppermute | solution.py:375
  118.5 4.2 %collective-permute-done.13 = bf16[1,160,1024]{2,1,0:T(8,128)(2,1)S(1)} collective-permute-done((bf16[1,160,1024]{2,1,0:T(8,128)(2,1)S(1)}, bf16[1,160,1024]{2,1,0:T(8,128)(2,1)S(1)}, u32[]{:S(2)}, u32[]{:S(2)}) %collective-permute-start.13) | collective-permute-done | bytes 327712 | tf_op jit(solution)/shard_map/ppermute | solution.py:375
  122.9 4.5 %decode.11 = (f32[1,224,1024]{2,1,0:T(8,128)S(1)}, bf16[1,160,1024]{2,1,0:T(8,128)(2,1)S(1)}) custom-call(s32[2]{0:T(128)S(1)} %pad_add_fusion.2.info_ref, bf16[384,1024]{1,0:T(8,128)(2,1)S(1)} %get-tuple-element.37.refs_0_, bf16[384,1024]{1,0:T(8,128)(2,1)S(1)} %get-tuple-element.38.refs_1_, bf16[384,1024]{1,0:T(8,128)(2,1)S(1)} %collective-permute-done.6.refs_2_, ...), custom_call_target="tpu_custom_call" | custom-call | tf_op jit(solution)/shard_map/decode/pallas_call | solution.py:280
  127.4 1.1 collective-permute-done.19
  128.5 1.5 collective-permute-start.14
  130.0 12.1 %collective-permute-done.18 = bf16[1,112,1024]{2,1,0:T(8,128)(2,1)S(1)} collective-permute-done((bf16[1,112,1024]{2,1,0:T(8,128)(2,1)S(1)}, bf16[1,112,1024]{2,1,0:T(8,128)(2,1)S(1)}, u32[]{:S(2)}, u32[]{:S(2)}) %collective-permute-start.18) | collective-permute-done | bytes 229408 | tf_op jit(solution)/shard_map/ppermute | solution.py:375
  142.4 1.6 collective-permute-start.21
  144.1 9.1 %collective-permute-done.16 = bf16[1,160,1024]{2,1,0:T(8,128)(2,1)S(1)} collective-permute-done((bf16[1,160,1024]{2,1,0:T(8,128)(2,1)S(1)}, bf16[1,160,1024]{2,1,0:T(8,128)(2,1)S(1)}, u32[]{:S(2)}, u32[]{:S(2)}) %collective-permute-start.16) | collective-permute-done | bytes 327712 | tf_op jit(solution)/shard_map/ppermute | solution.py:375
  153.2 1.5 collective-permute-done.21.refs_5_
  154.8 1.6 finale.1
  156.4 1.4 collective-permute-start.23
  158.1 1.9 %collective-permute-done.23 = f32[8,128]{1,0:T(8,128)S(1)} collective-permute-done((f32[8,128]{1,0:T(8,128)S(1)}, f32[8,128]{1,0:T(8,128)S(1)}, u32[]{:S(2)}, u32[]{:S(2)}) %collective-permute-start.23) | collective-permute-done | bytes 4128 | tf_op jit(solution)/shard_map/ppermute | solution.py:370
  160.0 0.9 collective-permute-done.22
  160.9 4.3 %collective-permute-start.26 = (f32[8,128]{1,0:T(8,128)S(1)}, f32[8,128]{1,0:T(8,128)S(1)}, u32[]{:S(2)}, u32[]{:S(2)}) collective-permute-start(f32[8,128]{1,0:T(8,128)S(1)} %add_add_fusion.refs_0_), channel_id=1, source_target_pairs={{0,8},{4,12},{8,0},{12,4},{1,9},{5,13},{9,1},{13,5},{2,10},{6,14},... | collective-permute-start | bytes 12296 | tf_op jit(solution)/shard_map/ppermute | solution.py:370
  165.2 1.1 collective-permute-done.25.refs_1_
  166.8 2.0 %collective-permute-done.27.refs_3_ = f32[8,128]{1,0:T(8,128)S(1)} collective-permute-done((f32[8,128]{1,0:T(8,128)S(1)}, f32[8,128]{1,0:T(8,128)S(1)}, u32[]{:S(2)}, u32[]{:S(2)}) %collective-permute-start.27) | collective-permute-done | bytes 4128 | tf_op jit(solution)/shard_map/ppermute | solution.py:370
  168.8 0.6 copy-done.11
  169.4 1.2 mean_ratio.1
  (60 shorter events, 3.1 us)
Async XLA Ops:
  0.6 10.9 %copy-start = (bf16[1,4096]{1,0:T(2,128)(2,1)S(1)}, bf16[1,4096]{1,0:T(2,128)(2,1)}, u32[]{:S(2)}) copy-start(bf16[1,4096]{1,0:T(2,128)(2,1)} %param.10) | copy-start | bytes 24580
  3.4 6.4 %collective-permute-start = (f32[1]{0:T(128)}, f32[1]{0:T(128)}, u32[]{:S(2)}, u32[]{:S(2)}) collective-permute-start(f32[1]{0:T(128)} %square_sum.1.after_ref), channel_id=1, source_target_pairs={{0,2},{2,0},{1,3},{3,1},{4,6},{6,4},{5,7},{7,5},{8,10},{10,8},{9,1... | collective-permute-start | bytes 20 | tf_op jit(solution)/shard_map/ppermute | solution.py:370
  11.0 23.7 %collective-permute-start.3 = (bf16[112,4096]{1,0:T(8,128)(2,1)}, bf16[112,4096]{1,0:T(8,128)(2,1)}, u32[]{:S(2)}, u32[]{:S(2)}) collective-permute-start(bf16[112,4096]{1,0:T(8,128)(2,1)} %get-tuple-element.34), channel_id=1, source_target_pairs={{0,2},{2,0},{1,3},{3,1},{4,6},{6,4},{5,7},{7,5},{8,10},{10,8},{9,1... | collective-permute-start | bytes 2752520 | tf_op jit(solution)/shard_map/ppermute | solution.py:370
  23.3 13.0 %collective-permute-start.1 = (bf16[384,1024]{1,0:T(8,128)(2,1)S(1)}, bf16[384,1024]{1,0:T(8,128)(2,1)S(1)}, u32[]{:S(2)}, u32[]{:S(2)}) collective-permute-start(bf16[384,1024]{1,0:T(8,128)(2,1)S(1)} %get-tuple-element.28.refs_0_), channel_id=1, source_target_pairs={{0,1},{2,3},{4,5},{6,7},{8,9},{10,11},{12,13},{14,15},{16,17},{18,... | collective-permute-start | bytes 2359304 | tf_op jit(solution)/shard_map/ppermute | solution.py:437
  24.7 11.7 %collective-permute-start.2 = (bf16[384,1024]{1,0:T(8,128)(2,1)S(1)}, bf16[384,1024]{1,0:T(8,128)(2,1)S(1)}, u32[]{:S(2)}, u32[]{:S(2)}) collective-permute-start(bf16[384,1024]{1,0:T(8,128)(2,1)S(1)} %get-tuple-element.29.refs_1_), channel_id=1, source_target_pairs={{0,1},{2,3},{4,5},{6,7},{8,9},{10,11},{12,13},{14,15},{16,17},{18,... | collective-permute-start | bytes 2359304 | tf_op jit(solution)/shard_map/ppermute | solution.py:437
  26.0 35.3 %collective-permute-start.5 = (bf16[160,4096]{1,0:T(8,128)(2,1)}, bf16[160,4096]{1,0:T(8,128)(2,1)}, u32[]{:S(2)}, u32[]{:S(2)}) collective-permute-start(bf16[160,4096]{1,0:T(8,128)(2,1)} %get-tuple-element.35), channel_id=1, source_target_pairs={{0,2},{2,0},{1,3},{3,1},{4,6},{6,4},{5,7},{7,5},{8,10},{10,8},{9,1... | collective-permute-start | bytes 3932168 | tf_op jit(solution)/shard_map/ppermute | solution.py:370
  34.7 26.6 %collective-permute-start.4 = (bf16[112,4096]{1,0:T(8,128)(2,1)}, bf16[112,4096]{1,0:T(8,128)(2,1)}, u32[]{:S(2)}, u32[]{:S(2)}) collective-permute-start(bf16[112,4096]{1,0:T(8,128)(2,1)} %collective-permute-done.3.refs_0_), channel_id=1, source_target_pairs={{0,4},{4,0},{8,12},{12,8},{1,5},{5,1},{9,13},{13,9},{2,6},{6,2},{1... | collective-permute-start | bytes 2752520 | tf_op jit(solution)/shard_map/ppermute | solution.py:375
  44.3 0.8 copy-start.3
  45.2 0.8 copy-start.5
  46.0 30.3 %collective-permute-start.8 = (bf16[2,224,1024]{2,1,0:T(8,128)(2,1)}, bf16[2,224,1024]{2,1,0:T(8,128)(2,1)}, u32[]{:S(2)}, u32[]{:S(2)}) collective-permute-start(bf16[2,224,1024]{2,1,0:T(8,128)(2,1)} %get-tuple-element.30.refs_6_), channel_id=1, source_target_pairs={{0,4},{4,0},{8,12},{12,8},{1,5},{5,1},{9,13},{13,9},{2,6},{6,2},{1... | collective-permute-start | bytes 2752520 | tf_op jit(solution)/shard_map/ppermute | solution.py:375
  73.6 6.6 %collective-permute-start.6 = (bf16[384,1024]{1,0:T(8,128)(2,1)S(1)}, bf16[384,1024]{1,0:T(8,128)(2,1)S(1)}, u32[]{:S(2)}, u32[]{:S(2)}) collective-permute-start(bf16[384,1024]{1,0:T(8,128)(2,1)S(1)} %get-tuple-element.37.refs_0_), channel_id=1, source_target_pairs={{0,1},{2,3},{4,5},{6,7},{8,9},{10,11},{12,13},{14,15},{16,17},{18,... | collective-permute-start | bytes 2359304 | tf_op jit(solution)/shard_map/ppermute | solution.py:437
  75.0 5.2 %collective-permute-start.7 = (bf16[384,1024]{1,0:T(8,128)(2,1)S(1)}, bf16[384,1024]{1,0:T(8,128)(2,1)S(1)}, u32[]{:S(2)}, u32[]{:S(2)}) collective-permute-start(bf16[384,1024]{1,0:T(8,128)(2,1)S(1)} %get-tuple-element.38.refs_1_), channel_id=1, source_target_pairs={{0,1},{2,3},{4,5},{6,7},{8,9},{10,11},{12,13},{14,15},{16,17},{18,... | collective-permute-start | bytes 2359304 | tf_op jit(solution)/shard_map/ppermute | solution.py:437
  77.5 21.9 %collective-permute-start.9 = (bf16[1,224,1024]{2,1,0:T(8,128)(2,1)S(1)}, bf16[1,224,1024]{2,1,0:T(8,128)(2,1)S(1)}, u32[]{:S(2)}, u32[]{:S(2)}) collective-permute-start(bf16[1,224,1024]{2,1,0:T(8,128)(2,1)S(1)} %add_convert_fusion.2.refs_6_), channel_id=1, source_target_pairs={{0,8},{4,12},{8,0},{12,4},{1,9},{5,13},{9,1},{13,5},{2,10},{6,14},... | collective-permute-start | bytes 1376264 | tf_op jit(solution)/shard_map/ppermute | solution.py:375
  84.7 20.9 %collective-permute-start.11 = (bf16[1,160,1024]{2,1,0:T(8,128)(2,1)S(1)}, bf16[1,160,1024]{2,1,0:T(8,128)(2,1)S(1)}, u32[]{:S(2)}, u32[]{:S(2)}) collective-permute-start(bf16[1,160,1024]{2,1,0:T(8,128)(2,1)S(1)} %get-tuple-element.43), channel_id=1, source_target_pairs={{0,2},{2,0},{1,3},{3,1},{4,6},{6,4},{5,7},{7,5},{8,10},{10,8},{9,1... | collective-permute-start | bytes 983048 | tf_op jit(solution)/shard_map/ppermute | solution.py:370
  85.4 21.2 %collective-permute-start.10 = (bf16[1,224,1024]{2,1,0:T(8,128)(2,1)S(1)}, bf16[1,224,1024]{2,1,0:T(8,128)(2,1)S(1)}, u32[]{:S(2)}, u32[]{:S(2)}) collective-permute-start(bf16[1,224,1024]{2,1,0:T(8,128)(2,1)S(1)} %get-tuple-element.40.refs_6_), channel_id=1, source_target_pairs={{0,4},{4,0},{8,12},{12,8},{1,5},{5,1},{9,13},{13,9},{2,6},{6,2},{1... | collective-permute-start | bytes 1376264 | tf_op jit(solution)/shard_map/ppermute | solution.py:375
  100.6 5.1 %copy-start.6 = (f32[1,160,1024]{2,1,0:T(8,128)S(1)}, f32[1,160,1024]{2,1,0:T(8,128)}, u32[]{:S(2)}) copy-start(f32[1,160,1024]{2,1,0:T(8,128)} %copy-done.5) | copy-start | bytes 1966084
  105.1 11.4 %collective-permute-start.12 = (bf16[1,160,1024]{2,1,0:T(8,128)(2,1)S(1)}, bf16[1,160,1024]{2,1,0:T(8,128)(2,1)S(1)}, u32[]{:S(2)}, u32[]{:S(2)}) collective-permute-start(bf16[1,160,1024]{2,1,0:T(8,128)(2,1)S(1)} %get-tuple-element.47), channel_id=1, source_target_pairs={{0,2},{2,0},{1,3},{3,1},{4,6},{6,4},{5,7},{7,5},{8,10},{10,8},{9,1... | collective-permute-start | bytes 983048 | tf_op jit(solution)/shard_map/ppermute | solution.py:370
  105.7 17.0 %collective-permute-start.13 = (bf16[1,160,1024]{2,1,0:T(8,128)(2,1)S(1)}, bf16[1,160,1024]{2,1,0:T(8,128)(2,1)S(1)}, u32[]{:S(2)}, u32[]{:S(2)}) collective-permute-start(bf16[1,160,1024]{2,1,0:T(8,128)(2,1)S(1)} %add_convert_fusion.5.refs_7_), channel_id=1, source_target_pairs={{0,4},{4,0},{8,12},{12,8},{1,5},{5,1},{9,13},{13,9},{2,6},{6,2},{1... | collective-permute-start | bytes 983048 | tf_op jit(solution)/shard_map/ppermute | solution.py:375
  106.7 35.4 %collective-permute-start.20 = (bf16[1,224,1024]{2,1,0:T(8,128)(2,1)S(1)}, bf16[1,224,1024]{2,1,0:T(8,128)(2,1)S(1)}, u32[]{:S(2)}, u32[]{:S(2)}) collective-permute-start(bf16[1,224,1024]{2,1,0:T(8,128)(2,1)S(1)} %add_convert_fusion.1.refs_6_), channel_id=1, source_target_pairs={{0,8},{4,12},{8,0},{12,4},{1,9},{5,13},{9,1},{13,5},{2,10},{6,14},... | collective-permute-start | bytes 1376264 | tf_op jit(solution)/shard_map/ppermute | solution.py:375
  114.9 29.0 %collective-permute-start.15 = (bf16[1,160,1024]{2,1,0:T(8,128)(2,1)S(1)}, bf16[1,160,1024]{2,1,0:T(8,128)(2,1)S(1)}, u32[]{:S(2)}, u32[]{:S(2)}) collective-permute-start(bf16[1,160,1024]{2,1,0:T(8,128)(2,1)S(1)} %get-tuple-element.50), channel_id=1, source_target_pairs={{0,2},{2,0},{1,3},{3,1},{4,6},{6,4},{5,7},{7,5},{8,10},{10,8},{9,1... | collective-permute-start | bytes 983048 | tf_op jit(solution)/shard_map/ppermute | solution.py:370
  116.5 12.0 %collective-permute-start.19 = (bf16[1,112,1024]{2,1,0:T(8,128)(2,1)S(1)}, bf16[1,112,1024]{2,1,0:T(8,128)(2,1)S(1)}, u32[]{:S(2)}, u32[]{:S(2)}) collective-permute-start(bf16[1,112,1024]{2,1,0:T(8,128)(2,1)S(1)} %get-tuple-element.45.refs_7_), channel_id=1, source_target_pairs={{0,4},{4,0},{8,12},{12,8},{1,5},{5,1},{9,13},{13,9},{2,6},{6,2},{1... | collective-permute-start | bytes 688136 | tf_op jit(solution)/shard_map/ppermute | solution.py:375
  116.5 25.6 %collective-permute-start.18 = (bf16[1,112,1024]{2,1,0:T(8,128)(2,1)S(1)}, bf16[1,112,1024]{2,1,0:T(8,128)(2,1)S(1)}, u32[]{:S(2)}, u32[]{:S(2)}) collective-permute-start(bf16[1,112,1024]{2,1,0:T(8,128)(2,1)S(1)} %get-tuple-element.44.refs_6_), channel_id=1, source_target_pairs={{0,4},{4,0},{8,12},{12,8},{1,5},{5,1},{9,13},{13,9},{2,6},{6,2},{1... | collective-permute-start | bytes 688136 | tf_op jit(solution)/shard_map/ppermute | solution.py:375
  122.8 21.1 %copy-start.4 = (f32[1,160,1024]{2,1,0:T(8,128)S(1)}, f32[1,160,1024]{2,1,0:T(8,128)}, u32[]{:S(2)}) copy-start(f32[1,160,1024]{2,1,0:T(8,128)} %copy-done.3) | copy-start | bytes 1966084
  122.8 21.3 %collective-permute-start.17 = (bf16[1,160,1024]{2,1,0:T(8,128)(2,1)S(1)}, bf16[1,160,1024]{2,1,0:T(8,128)(2,1)S(1)}, u32[]{:S(2)}, u32[]{:S(2)}) collective-permute-start(bf16[1,160,1024]{2,1,0:T(8,128)(2,1)S(1)} %add_convert_fusion.4.refs_8_), channel_id=1, source_target_pairs={{0,8},{4,12},{8,0},{12,4},{1,9},{5,13},{9,1},{13,5},{2,10},{6,14},... | collective-permute-start | bytes 983048 | tf_op jit(solution)/shard_map/ppermute | solution.py:375
  127.4 27.3 %copy-start.2 = (bf16[1,384,1024]{2,1,0:T(8,128)(2,1)S(1)}, bf16[1,384,1024]{2,1,0:T(8,128)(2,1)}, u32[]{:S(2)}) copy-start(bf16[1,384,1024]{2,1,0:T(8,128)(2,1)} %param.8) | copy-start | bytes 2359300
  127.4 27.3 %copy-start.7 = (bf16[1,1024]{1,0:T(2,128)(2,1)S(1)}, bf16[1,1024]{1,0:T(2,128)(2,1)}, u32[]{:S(2)}) copy-start(bf16[1,1024]{1,0:T(2,128)(2,1)} %b_ref.1) | copy-start | bytes 6148
  128.5 15.6 %collective-permute-start.14 = (bf16[1,160,1024]{2,1,0:T(8,128)(2,1)S(1)}, bf16[1,160,1024]{2,1,0:T(8,128)(2,1)S(1)}, u32[]{:S(2)}, u32[]{:S(2)}) collective-permute-start(bf16[1,160,1024]{2,1,0:T(8,128)(2,1)S(1)} %get-tuple-element.48), channel_id=1, source_target_pairs={{0,2},{2,0},{1,3},{3,1},{4,6},{6,4},{5,7},{7,5},{8,10},{10,8},{9,1... | collective-permute-start | bytes 983048 | tf_op jit(solution)/shard_map/ppermute | solution.py:370
  142.1 28.5 %copy-start.1 = (bf16[1,4096]{1,0:T(2,128)(2,1)S(1)}, bf16[1,4096]{1,0:T(2,128)(2,1)}, u32[]{:S(2)}) copy-start(bf16[1,4096]{1,0:T(2,128)(2,1)} %param.10) | copy-start | bytes 24580
  142.4 12.4 %collective-permute-start.21 = (bf16[224,1024]{1,0:T(8,128)(2,1)S(1)}, bf16[224,1024]{1,0:T(8,128)(2,1)S(1)}, u32[]{:S(2)}, u32[]{:S(2)}) collective-permute-start(bf16[224,1024]{1,0:T(8,128)(2,1)S(1)} %fusion), channel_id=1, source_target_pairs={{0,2},{2,0},{1,3},{3,1},{4,6},{6,4},{5,7},{7,5},{8,10},{10,8},{9,1... | collective-permute-start | bytes 1376264 | tf_op jit(solution)/shard_map/ppermute | solution.py:370
  144.0 9.2 %collective-permute-start.16 = (bf16[1,160,1024]{2,1,0:T(8,128)(2,1)S(1)}, bf16[1,160,1024]{2,1,0:T(8,128)(2,1)S(1)}, u32[]{:S(2)}, u32[]{:S(2)}) collective-permute-start(bf16[1,160,1024]{2,1,0:T(8,128)(2,1)S(1)} %add_convert_fusion.3), channel_id=1, source_target_pairs={{0,4},{4,0},{8,12},{12,8},{1,5},{5,1},{9,13},{13,9},{2,6},{6,2},{1... | collective-permute-start | bytes 983048 | tf_op jit(solution)/shard_map/ppermute | solution.py:375
  156.4 1.7 collective-permute-start.24
  156.4 3.6 %collective-permute-start.23 = (f32[8,128]{1,0:T(8,128)S(1)}, f32[8,128]{1,0:T(8,128)S(1)}, u32[]{:S(2)}, u32[]{:S(2)}) collective-permute-start(f32[8,128]{1,0:T(8,128)S(1)} %get-tuple-element.53), channel_id=1, source_target_pairs={{0,2},{1,3},{2,0},{3,1},{4,6},{5,7},{6,4},{7,5},{8,10},{9,11},{10,... | collective-permute-start | bytes 12296 | tf_op jit(solution)/shard_map/ppermute | solution.py:370
  157.8 3.0 %collective-permute-start.22 = (f32[8,128]{1,0:T(8,128)S(1)}, f32[8,128]{1,0:T(8,128)S(1)}, u32[]{:S(2)}, u32[]{:S(2)}) collective-permute-start(f32[8,128]{1,0:T(8,128)S(1)} %get-tuple-element.53), channel_id=1, source_target_pairs={{0,1},{1,2},{2,3},{3,0},{4,5},{5,6},{6,7},{7,4},{8,9},{9,10},{10,1... | collective-permute-start | bytes 12296 | tf_op jit(solution)/shard_map/ppermute | solution.py:370
  160.9 7.9 %copy-start.8 = (f32[8,128]{1,0:T(8,128)}, f32[8,128]{1,0:T(8,128)S(1)}, u32[]{:S(2)}) copy-start(f32[8,128]{1,0:T(8,128)S(1)} %add_add_fusion.refs_0_) | copy-start | bytes 12292
  160.9 5.4 %collective-permute-start.25 = (f32[8,128]{1,0:T(8,128)S(1)}, f32[8,128]{1,0:T(8,128)S(1)}, u32[]{:S(2)}, u32[]{:S(2)}) collective-permute-start(f32[8,128]{1,0:T(8,128)S(1)} %add_add_fusion.refs_0_), channel_id=1, source_target_pairs={{0,4},{4,8},{8,12},{12,0},{1,5},{5,9},{9,13},{13,1},{2,6},{6,10},{... | collective-permute-start | bytes 12296 | tf_op jit(solution)/shard_map/ppermute | solution.py:370
  160.9 5.9 %collective-permute-start.26 = (f32[8,128]{1,0:T(8,128)S(1)}, f32[8,128]{1,0:T(8,128)S(1)}, u32[]{:S(2)}, u32[]{:S(2)}) collective-permute-start(f32[8,128]{1,0:T(8,128)S(1)} %add_add_fusion.refs_0_), channel_id=1, source_target_pairs={{0,8},{4,12},{8,0},{12,4},{1,9},{5,13},{9,1},{13,5},{2,10},{6,14},... | collective-permute-start | bytes 12296 | tf_op jit(solution)/shard_map/ppermute | solution.py:370
  165.2 3.6 %collective-permute-start.27 = (f32[8,128]{1,0:T(8,128)S(1)}, f32[8,128]{1,0:T(8,128)S(1)}, u32[]{:S(2)}, u32[]{:S(2)}) collective-permute-start(f32[8,128]{1,0:T(8,128)S(1)} %add_add_fusion.refs_0_), channel_id=1, source_target_pairs={{0,12},{4,0},{8,4},{12,8},{1,13},{5,1},{9,5},{13,9},{2,14},{6,2},{... | collective-permute-start | bytes 12296 | tf_op jit(solution)/shard_map/ppermute | solution.py:370
  166.3 2.5 %copy-start.9 = (f32[8,128]{1,0:T(8,128)}, f32[8,128]{1,0:T(8,128)S(1)}, u32[]{:S(2)}) copy-start(f32[8,128]{1,0:T(8,128)S(1)} %collective-permute-done.25.refs_1_) | copy-start | bytes 12292
  166.7 2.0 %copy-start.10 = (f32[8,128]{1,0:T(8,128)}, f32[8,128]{1,0:T(8,128)S(1)}, u32[]{:S(2)}) copy-start(f32[8,128]{1,0:T(8,128)S(1)} %collective-permute-done.26.refs_2_) | copy-start | bytes 12292
  168.8 0.6 copy-start.11

commit v11 on v9

--- a/solution.py
+++ b/solution.py
@@ -47,9 +47,9 @@
     return pl.pallas_call(
         body,
         in_specs=[pl.BlockSpec(memory_space=pl.ANY)],
-        out_specs=pl.BlockSpec(memory_space=pltpu.SMEM),
-        out_shape=jax.ShapeDtypeStruct((1,), jnp.float32),
-        scratch_shapes=[pltpu.VMEM((rows, width), x.dtype), pltpu.SemaphoreType.DMA((loads,))],
+        out_specs=[pl.BlockSpec(memory_space=pltpu.SMEM), pl.BlockSpec(memory_space=pltpu.VMEM)],
+        out_shape=[jax.ShapeDtypeStruct((1,), jnp.float32), pltpu.VMEM((rows, width), x.dtype)],
+        scratch_shapes=[pltpu.SemaphoreType.DMA((loads,))],
         compiler_params=pltpu.CompilerParams(vmem_limit_bytes=VMEM_LIMIT),
         cost_estimate=COST,
         name="square_sum",
@@ -60,60 +60,31 @@
     rows, width = x.shape
     middle = rows - 2 * edge
 
-    def body(side_ref, after_ref, x_ref, outer_ref, inner_ref, first, second, sem, out_sem):
+    def body(side_ref, after_ref, x_ref, outer_ref, inner_ref, sem):
         start = pl.multiple_of(side_ref[0] * (rows - edge), 16)
-        loads = [
-            pltpu.make_async_copy(x_ref.at[pl.ds(start, edge)], first, sem.at[0]),
-            pltpu.make_async_copy(x_ref.at[pl.ds(edge, middle)], second, sem.at[1]),
+        copies = [
+            pltpu.make_async_copy(x_ref.at[pl.ds(start, edge)], outer_ref, sem.at[0]),
+            pltpu.make_async_copy(x_ref.at[pl.ds(edge, middle)], inner_ref, sem.at[1]),
         ]
-        stores = [
-            pltpu.make_async_copy(first, outer_ref, out_sem.at[0]),
-            pltpu.make_async_copy(second, inner_ref, out_sem.at[1]),
-        ]
-        for load in loads:
-            load.start()
-        for load, store in zip(loads, stores):
-            load.wait()
-            store.start()
-        for store in stores:
-            store.wait()
+        for copy in copies:
+            copy.start()
+        for copy in copies:
+            copy.wait()
 
     return pl.pallas_call(
         body,
         in_specs=[
             pl.BlockSpec(memory_space=pltpu.SMEM),
             pl.BlockSpec(memory_space=pltpu.SMEM),
-            pl.BlockSpec(memory_space=pl.ANY),
+            pl.BlockSpec(memory_space=pltpu.VMEM),
         ],
         out_specs=[pl.BlockSpec(memory_space=pl.ANY)] * 2,
         out_shape=[pltpu.HBM((edge, width), x.dtype), pltpu.HBM((middle, width), x.dtype)],
-        scratch_shapes=[
-            pltpu.VMEM((edge, width), x.dtype),
-            pltpu.VMEM((middle, width), x.dtype),
-            pltpu.SemaphoreType.DMA((2,)),
-            pltpu.SemaphoreType.DMA((2,)),
-        ],
+        scratch_shapes=[pltpu.SemaphoreType.DMA((2,))],
         compiler_params=pltpu.CompilerParams(vmem_limit_bytes=VMEM_LIMIT),
         cost_estimate=COST,
         name="cut",
-    )(side.reshape(1), after, x)
-
-
-def gate(values, after):
-    n = len(values)
-
-    def body(after_ref, *refs):
-        pass
-
-    return pl.pallas_call(
-        body,
-        in_specs=[pl.BlockSpec(memory_space=pltpu.SMEM)] + [pl.BlockSpec(memory_space=pl.ANY)] * n,
-        out_specs=[pl.BlockSpec(memory_space=pl.ANY)] * n,
-        out_shape=[pltpu.HBM(value.shape, value.dtype) for value in values],
-        input_output_aliases={1 + i: i for i in range(n)},
-        cost_estimate=COST,
-        name="gate",
-    )(after, *[in_hbm(value) for value in values])
+    )(side.reshape(1), after, pltpu.with_memory_space_constraint(x, pltpu.VMEM))
 
 
 def ring_loop(count, slots, start, step):
@@ -298,17 +269,17 @@
     )(info, *codes, *earlier, own_w, cross_w, *also)
 
 
-def finale(outer_terms, inner_terms, bias, target, layer):
+def finale(outer_terms, inner_terms, first, bias, target, layer):
     rows, width = target.shape
-    half = inner_terms[0].shape[0]
-    quarter = (rows - half) // 2
+    middle = inner_terms[0].shape[0]
+    last = first + middle
     n, m = len(outer_terms), len(inner_terms)
 
     def body(layer_ref, b_ref, t_ref, *refs):
         terms = {0: refs[:n], 1: refs[n:n + m]}
         r_ref, s_ref = refs[n + m:]
         bias = b_ref[...].astype(jnp.float32)
-        spans = [(0, 0, 0, quarter), (1, 0, quarter, half), (0, quarter, quarter + half, quarter)]
+        spans = [(0, 0, 0, first), (1, 0, first, middle), (0, first, last, rows - last)]
 
         def block(which, start, target_start):
             def run(r, sums):
@@ -405,12 +376,11 @@
     side = lat % 2
 
     edge = rows * 7 // 24 // 16 * 16
-    square = square_sum(x_own)
-    outer, inner = cut(x_own, side.astype(jnp.int32), edge, square)
+    square, x_held = square_sum(x_own)
     square = sum_over(square, "token")
     scale = jnp.sqrt(square / (rows * n_tok * model) + 1e-06)
     inv = 1.0 / scale
-    outer, inner = gate([outer, inner], inv)
+    outer, inner = cut(x_held, side.astype(jnp.int32), edge, inv)
     foreign = []
     for distance in range(1, n_tok):
         mine = shifted(outer, "token", distance)
@@ -429,8 +399,9 @@
         blocks = [4 * i + 2 * high + low for high in highs for i in range(group)]
         return jnp.stack([layer] + blocks).astype(jnp.int32)
 
-    middle = rows * 7 // 12 // 16 * 16
-    first = (rows - middle) // 2
+    middle = rows * 13 // 24 // 16 * 16
+    first = (rows - middle) // 2 // 16 * 16
+    last = first + middle
     narrow = jnp.bfloat16
 
     def earlier_of(codes):
@@ -453,10 +424,10 @@
             bit *= 2
         return total[0]
 
-    codes = encode([(x_own, 0, rows)], places(0), inv, enc_w, bias, 2, [])
+    codes = encode([(x_held, 0, rows)], places(0), inv, enc_w, bias, 2, [])
     earlier = earlier_of(codes)
     inside = ((first, middle),)
-    outside = ((0, first), (rows - first, first))
+    outside = ((0, first), (last, rows - last))
     spans = [(0, group, inside), (group, group, inside), (0, group, outside), (group, group, outside)]
     far_sent, near_sent, far_out_sent, near_out_sent = products(
         codes, earlier, info(other, (far, near)),
@@ -497,7 +468,8 @@
         if len(far_out_back) == n_tok - 1:
             ready.append(joined(far_out_sent, far_out_back).astype(narrow))
             far_out = swapped(ready[1], "latent", 1)
-        halves = [((first + i * (middle // 2), middle // 2),) for i in range(2)]
+        cut_at = (middle // 2 + 15) // 16 * 16
+        halves = [((first, cut_at),), ((first + cut_at, middle - cut_at),)]
         near_sent, near_back = quarter_of(other, near, halves, narrow, ready)
         near_in = jnp.concatenate([swapped(rows_in, "latent", 1) for rows_in in near_sent], axis=1)
         far_out_kept = far_out_kept + wide(far_kept_back)
@@ -519,7 +491,7 @@
         outer_terms = [term[0] for term in outer_terms]
     else:
         outer_terms = [finish(joined(near_out_kept, near_out_kept_back) + wide(near_out) + wide(across_out))]
-    recon, sums = finale(outer_terms, [finish(total_in), *returned], dec_bias, targets[0], layer)
+    recon, sums = finale(outer_terms, [finish(total_in), *returned], first, dec_bias, targets[0], layer)
 
     sums = sum_over(sums, ("token", "layer"))
     loss = mean_ratio([sums] + [shifted(sums, "latent", d) for d in range(1, n_lat)])

time: 166 us -> 162 us (0.976)
  Pallas kernels: 66.2 us -> 61.7 us
    ppermute x11, waiting for transfers between devices: 43.4 us -> 33.4 us  [swapped(): return lax.ppermute(value, axis, [(i, i ^ bit) for i in range(n)])]
    ppermute x14, waiting for transfers between devices: 15.1 us -> 24.6 us  [shifted(): lax.ppermute(value, axis, [(i, (i + distance) % n) for i in range(n)])]
    pallas_call x2, Pallas kernels: 24.1 us -> 21.7 us  [encode(): pl.pallas_call(body, in_specs=[pl.BlockSpec(memory_space=pltpu.SMEM), pl....]
    ppermute x14, starting transfers between devices: 13.5 us -> 15.7 us  [shifted(): lax.ppermute(value, axis, [(i, (i + distance) % n) for i in range(n)])]
    pallas_call x1, Pallas kernels: 3.37 us -> 1.39 us  [cut(): pl.pallas_call(body, in_specs=[pl.BlockSpec(memory_space=pltpu.SMEM), pl....]
  transfers between devices with their start and end apart: 28 -> 28, of which waited for: 17 -> 16; matrix products, arithmetic and copies ran while one was open for 1% -> 1% of each run, Pallas kernels for 29% -> 27%
where the time goes in v11:
time: 162 us
  Pallas kernels  61.7 us (38%)
  waiting for transfers between devices  58.1 us (36%)
  starting transfers between devices  34.1 us (21%)
  local copies, waits for them, and re-layouts  3.2 us (2%)
  other arithmetic  2.38 us (1%)
  between operations  2.28 us (1%)
    ppermute x11, waiting for transfers between devices, swapped(): return lax.ppermute(value, axis, [(i, i ^ bit) for i in range(n)])  33.4 us
    pallas_call x6, Pallas kernels, decode(): pl.pallas_call(body, in_specs=[pl.BlockSpec(memory_space=pltpu.SMEM)] + [...  33 us
    ppermute x14, waiting for transfers between devices, shifted(): lax.ppermute(value, axis, [(i, (i + distance) % n) for i in range(n)])  24.6 us
    pallas_call x2, Pallas kernels, encode(): pl.pallas_call(body, in_specs=[pl.BlockSpec(memory_space=pltpu.SMEM), pl....  21.7 us
    ppermute x14, starting transfers between devices, shifted(): lax.ppermute(value, axis, [(i, (i + distance) % n) for i in range(n)])  15.7 us
    ppermute x11, starting transfers between devices, swapped(): return lax.ppermute(value, axis, [(i, i ^ bit) for i in range(n)])  14.3 us
    ppermute x3, starting transfers between devices, earlier_of(): return [lax.ppermute(part, 'layer', [(0, 1)]) for part in codes]  4.07 us
  transfers between devices with their start and end apart: 28, of which 16 were waited for; matrix products, arithmetic and copies ran while one was open for 1% of the time, Pallas kernels for 27%

profile of v11, /device:TPU:0, one launch (start us, length us, event | category | flops | bytes accessed | tf_op | source)
XLA Modules:
  0.0 161.7 jit_solution(13896450333661937532)
XLA Ops:
  0.6 2.7 %square_sum.1 = (f32[1]{0:T(128)}, bf16[384,4096]{1,0:T(8,128)(2,1)S(1)}) custom-call(bf16[384,4096]{1,0:T(8,128)(2,1)} %bitcast.35), custom_call_target="tpu_custom_call" | custom-call | tf_op jit(solution)/shard_map/square_sum/pallas_call | solution.py:47
  3.4 3.0 %collective-permute-start = (f32[1]{0:T(128)}, f32[1]{0:T(128)}, u32[]{:S(2)}, u32[]{:S(2)}) collective-permute-start(f32[1]{0:T(128)} %get-tuple-element.27), channel_id=1, source_target_pairs={{0,2},{2,0},{1,3},{3,1},{4,6},{6,4},{5,7},{7,5},{8,10},{10,8},{9,1... | collective-permute-start | bytes 20 | tf_op jit(solution)/shard_map/ppermute | solution.py:341
  6.4 1.6 collective-permute-done
  9.3 1.4 cut.1
  10.7 2.1 %collective-permute-start.3 = (bf16[112,4096]{1,0:T(8,128)(2,1)}, bf16[112,4096]{1,0:T(8,128)(2,1)}, u32[]{:S(2)}, u32[]{:S(2)}) collective-permute-start(bf16[112,4096]{1,0:T(8,128)(2,1)} %get-tuple-element.33), channel_id=1, source_target_pairs={{0,2},{2,0},{1,3},{3,1},{4,6},{6,4},{5,7},{7,5},{8,10},{10,8},{9,1... | collective-permute-start | bytes 2752520 | tf_op jit(solution)/shard_map/ppermute | solution.py:341
  12.8 11.0 %encode.2 = (bf16[384,1024]{1,0:T(8,128)(2,1)}, bf16[384,1024]{1,0:T(8,128)(2,1)}) custom-call(s32[1]{0:T(128)} %constant.58.clone.1.places_ref, f32[1]{0:T(128)S(6)} %sqrt.3.inv_ref.after_ref, bf16[1,2048]{1,0:T(2,128)(2,1)S(1)} %constant_dynamic-slice_fusion.b_ref, bf16[384,4096]{1,0:T(8,128)(2,1)S(1)} %get-tuple-element.28.refs_0_.x_ref, ...), custom_call_target="tpu_custom_call" | custom-call | tf_op jit(solution)/shard_map/encode/pallas_call | solution.py:152
  23.8 1.3 collective-permute-start.1
  25.1 1.3 collective-permute-start.2
  26.6 7.8 %collective-permute-done.3.refs_0_ = bf16[112,4096]{1,0:T(8,128)(2,1)} collective-permute-done((bf16[112,4096]{1,0:T(8,128)(2,1)}, bf16[112,4096]{1,0:T(8,128)(2,1)}, u32[]{:S(2)}, u32[]{:S(2)}) %collective-permute-start.3) | collective-permute-done | bytes 917536 | tf_op jit(solution)/shard_map/ppermute | solution.py:341
  34.4 2.1 %collective-permute-start.4 = (bf16[112,4096]{1,0:T(8,128)(2,1)}, bf16[112,4096]{1,0:T(8,128)(2,1)}, u32[]{:S(2)}, u32[]{:S(2)}) collective-permute-start(bf16[112,4096]{1,0:T(8,128)(2,1)} %collective-permute-done.3.refs_0_), channel_id=1, source_target_pairs={{0,4},{4,0},{8,12},{12,8},{1,5},{5,1},{9,13},{13,9},{2,6},{6,2},{1... | collective-permute-start | bytes 2752520 | tf_op jit(solution)/shard_map/ppermute | solution.py:346
  36.6 7.4 %decode.6 = (bf16[1,208,1024]{2,1,0:T(8,128)(2,1)S(1)}, bf16[1,208,1024]{2,1,0:T(8,128)(2,1)S(1)}, f32[1,176,1024]{2,1,0:T(8,128)S(1)}, f32[1,176,1024]{2,1,0:T(8,128)S(1)}) custom-call(s32[3]{0:T(128)S(1)} %get-tuple-element.53.info_ref, bf16[384,1024]{1,0:T(8,128)(2,1)} %get-tuple-element.29.refs_0_, bf16[384,1024]{1,0:T(8,128)(2,1)} %get-tuple-element.30.refs_1_, ...), custom_call_target="tpu_custom_call" | custom-call | tf_op jit(solution)/shard_map/decode/pallas_call | solution.py:251
  44.0 0.9 copy-done.3
  44.8 0.9 copy-done.5
  45.8 0.8 copy-done.8
  46.6 7.4 %decode.7 = (f32[1,208,1024]{2,1,0:T(8,128)S(1)}, f32[1,208,1024]{2,1,0:T(8,128)S(1)}, f32[1,176,1024]{2,1,0:T(8,128)S(1)}, f32[1,176,1024]{2,1,0:T(8,128)S(1)}) custom-call(s32[3]{0:T(128)S(1)} %get-tuple-element.52.info_ref, bf16[384,1024]{1,0:T(8,128)(2,1)} %get-tuple-element.29.refs_0_, bf16[384,1024]{1,0:T(8,128)(2,1)} %get-tuple-element.30.refs_1_, ...), custom_call_target="tpu_custom_call" | custom-call | tf_op jit(solution)/shard_map/decode/pallas_call | solution.py:251
  54.0 8.3 %collective-permute-done.6 = bf16[1,208,1024]{2,1,0:T(8,128)(2,1)} collective-permute-done((bf16[1,208,1024]{2,1,0:T(8,128)(2,1)S(1)}, bf16[1,208,1024]{2,1,0:T(8,128)(2,1)}, u32[]{:S(2)}, u32[]{:S(2)}) %collective-permute-start.6) | collective-permute-done | bytes 426016 | tf_op jit(solution)/shard_map/ppermute | solution.py:346
  62.3 1.1 add_convert_fusion.2.refs_4_
  63.5 10.7 %encode.3.refs_0_ = bf16[384,2048]{1,0:T(8,128)(2,1)S(1)} custom-call(s32[3]{0:T(128)S(1)} %pad_add_fusion.3.places_ref, f32[1]{0:T(128)S(6)} %sqrt.3.inv_ref.after_ref, bf16[1,2048]{1,0:T(2,128)(2,1)S(1)} %constant_dynamic-slice_fusion.b_ref, bf16[112,4096]{1,0:T(8,128)(2,1)} %collective-permute-done.3.refs_0_, ...), custom_call_target="tpu_custom_call" | custom-call | tf_op jit(solution)/shard_map/encode/pallas_call | solution.py:152
  74.2 1.4 collective-permute-start.7
  75.6 1.6 collective-permute-start.8
  77.2 2.6 %collective-permute-start.9 = (bf16[1,208,1024]{2,1,0:T(8,128)(2,1)S(1)}, bf16[1,208,1024]{2,1,0:T(8,128)(2,1)S(1)}, u32[]{:S(2)}, u32[]{:S(2)}) collective-permute-start(bf16[1,208,1024]{2,1,0:T(8,128)(2,1)S(1)} %add_convert_fusion.2.refs_4_), channel_id=1, source_target_pairs={{0,8},{4,12},{8,0},{12,4},{1,9},{5,13},{9,1},{13,5},{2,10},{6,14},... | collective-permute-start | bytes 1277960 | tf_op jit(solution)/shard_map/ppermute | solution.py:346
  79.9 4.5 %decode.8 = (bf16[1,208,1024]{2,1,0:T(8,128)(2,1)S(1)}, bf16[1,176,1024]{2,1,0:T(8,128)(2,1)S(1)}) custom-call(s32[2]{0:T(128)S(1)} %pad_add_fusion.6.info_ref, bf16[384,2048]{1,0:T(8,128)(2,1)S(1)} %encode.3.refs_0_, bf16[384,2048]{1,0:T(8,128)(2,1)S(1)} %collective-permute-done.7.refs_1_, bf16[2048,4096]{1,0:T(8,128)(2,1)} %bitcast.29, ...), custom_call_target="tpu_custom_call" | custom-call | tf_op jit(solution)/shard_map/decode/pallas_call | solution.py:251
  84.4 1.6 collective-permute-start.11
  86.5 7.3 %collective-permute-done.8 = bf16[1,208,1024]{2,1,0:T(8,128)(2,1)S(1)} collective-permute-done((bf16[1,208,1024]{2,1,0:T(8,128)(2,1)S(1)}, bf16[1,208,1024]{2,1,0:T(8,128)(2,1)S(1)}, u32[]{:S(2)}, u32[]{:S(2)}) %collective-permute-start.8) | collective-permute-done | bytes 426016 | tf_op jit(solution)/shard_map/ppermute | solution.py:346
  94.0 4.5 %decode.9 = (f32[1,208,1024]{2,1,0:T(8,128)S(1)}, bf16[1,176,1024]{2,1,0:T(8,128)(2,1)S(1)}) custom-call(s32[2]{0:T(128)S(1)} %pad_add_fusion.5.info_ref, bf16[384,2048]{1,0:T(8,128)(2,1)S(1)} %encode.3.refs_0_, bf16[384,2048]{1,0:T(8,128)(2,1)S(1)} %collective-permute-done.7.refs_1_, bf16[2048,4096]{1,0:T(8,128)(2,1)} %bitcast.30, ...), custom_call_target="tpu_custom_call" | custom-call | tf_op jit(solution)/shard_map/decode/pallas_call | solution.py:251
  98.5 1.8 %collective-permute-start.12 = (bf16[1,176,1024]{2,1,0:T(8,128)(2,1)S(1)}, bf16[1,176,1024]{2,1,0:T(8,128)(2,1)S(1)}, u32[]{:S(2)}, u32[]{:S(2)}) collective-permute-start(bf16[1,176,1024]{2,1,0:T(8,128)(2,1)S(1)} %get-tuple-element.45), channel_id=1, source_target_pairs={{0,2},{2,0},{1,3},{3,1},{4,6},{6,4},{5,7},{7,5},{8,10},{10,8},{9,1... | collective-permute-start | bytes 1081352 | tf_op jit(solution)/shard_map/ppermute | solution.py:341
  100.4 3.6 %collective-permute-start.13 = (bf16[1,176,1024]{2,1,0:T(8,128)(2,1)S(1)}, bf16[1,176,1024]{2,1,0:T(8,128)(2,1)S(1)}, u32[]{:S(2)}, u32[]{:S(2)}) collective-permute-start(bf16[1,176,1024]{2,1,0:T(8,128)(2,1)S(1)} %add_convert_fusion.5.refs_5_), channel_id=1, source_target_pairs={{0,4},{4,0},{8,12},{12,8},{1,5},{5,1},{9,13},{13,9},{2,6},{6,2},{1... | collective-permute-start | bytes 1081352 | tf_op jit(solution)/shard_map/ppermute | solution.py:346
  104.1 1.7 %collective-permute-start.20 = (bf16[1,208,1024]{2,1,0:T(8,128)(2,1)S(1)}, bf16[1,208,1024]{2,1,0:T(8,128)(2,1)S(1)}, u32[]{:S(2)}, u32[]{:S(2)}) collective-permute-start(bf16[1,208,1024]{2,1,0:T(8,128)(2,1)S(1)} %add_convert_fusion.1.refs_4_), channel_id=1, source_target_pairs={{0,8},{4,12},{8,0},{12,4},{1,9},{5,13},{9,1},{13,5},{2,10},{6,14},... | collective-permute-start | bytes 1277960 | tf_op jit(solution)/shard_map/ppermute | solution.py:346
  106.0 4.5 %decode.10 = (bf16[1,112,1024]{2,1,0:T(8,128)(2,1)S(1)}, bf16[1,96,1024]{2,1,0:T(8,128)(2,1)S(1)}, bf16[1,176,1024]{2,1,0:T(8,128)(2,1)S(1)}) custom-call(s32[2]{0:T(128)S(1)} %pad_add_fusion.4.info_ref, bf16[384,2048]{1,0:T(8,128)(2,1)S(1)} %encode.3.refs_0_, bf16[384,2048]{1,0:T(8,128)(2,1)S(1)} %collective-permute-done.7.refs_1_, ...), custom_call_target="tpu_custom_call" | custom-call | tf_op jit(solution)/shard_map/decode/pallas_call | solution.py:251
  110.8 1.8 %collective-permute-start.18 = (bf16[1,112,1024]{2,1,0:T(8,128)(2,1)S(1)}, bf16[1,112,1024]{2,1,0:T(8,128)(2,1)S(1)}, u32[]{:S(2)}, u32[]{:S(2)}) collective-permute-start(bf16[1,112,1024]{2,1,0:T(8,128)(2,1)S(1)} %get-tuple-element.42.refs_4_), channel_id=1, source_target_pairs={{0,4},{4,0},{8,12},{12,8},{1,5},{5,1},{9,13},{13,9},{2,6},{6,2},{1... | collective-permute-start | bytes 688136 | tf_op jit(solution)/shard_map/ppermute | solution.py:346
  112.6 3.4 %collective-permute-start.15 = (bf16[1,176,1024]{2,1,0:T(8,128)(2,1)S(1)}, bf16[1,176,1024]{2,1,0:T(8,128)(2,1)S(1)}, u32[]{:S(2)}, u32[]{:S(2)}) collective-permute-start(bf16[1,176,1024]{2,1,0:T(8,128)(2,1)S(1)} %get-tuple-element.48), channel_id=1, source_target_pairs={{0,2},{2,0},{1,3},{3,1},{4,6},{6,4},{5,7},{7,5},{8,10},{10,8},{9,1... | collective-permute-start | bytes 1081352 | tf_op jit(solution)/shard_map/ppermute | solution.py:341
  116.0 4.6 %collective-permute-done.13 = bf16[1,176,1024]{2,1,0:T(8,128)(2,1)S(1)} collective-permute-done((bf16[1,176,1024]{2,1,0:T(8,128)(2,1)S(1)}, bf16[1,176,1024]{2,1,0:T(8,128)(2,1)S(1)}, u32[]{:S(2)}, u32[]{:S(2)}) %collective-permute-start.13) | collective-permute-done | bytes 360480 | tf_op jit(solution)/shard_map/ppermute | solution.py:346
  120.8 4.7 %decode.11 = (f32[1,208,1024]{2,1,0:T(8,128)S(1)}, bf16[1,176,1024]{2,1,0:T(8,128)(2,1)S(1)}) custom-call(s32[2]{0:T(128)S(1)} %pad_add_fusion.2.info_ref, bf16[384,2048]{1,0:T(8,128)(2,1)S(1)} %encode.3.refs_0_, bf16[384,2048]{1,0:T(8,128)(2,1)S(1)} %collective-permute-done.7.refs_1_, bf16[2048,4096]{1,0:T(8,128)(2,1)} %bitcast.32, ...), custom_call_target="tpu_custom_call" | custom-call | tf_op jit(solution)/shard_map/decode/pallas_call | solution.py:251
  125.5 4.5 %collective-permute-done.19 = bf16[1,96,1024]{2,1,0:T(8,128)(2,1)S(1)} collective-permute-done((bf16[1,96,1024]{2,1,0:T(8,128)(2,1)S(1)}, bf16[1,96,1024]{2,1,0:T(8,128)(2,1)S(1)}, u32[]{:S(2)}, u32[]{:S(2)}) %collective-permute-start.19) | collective-permute-done | bytes 196640 | tf_op jit(solution)/shard_map/ppermute | solution.py:346
  130.1 4.4 %collective-permute-done.18 = bf16[1,112,1024]{2,1,0:T(8,128)(2,1)S(1)} collective-permute-done((bf16[1,112,1024]{2,1,0:T(8,128)(2,1)S(1)}, bf16[1,112,1024]{2,1,0:T(8,128)(2,1)S(1)}, u32[]{:S(2)}, u32[]{:S(2)}) %collective-permute-start.18) | collective-permute-done | bytes 229408 | tf_op jit(solution)/shard_map/ppermute | solution.py:346
  134.9 2.1 %collective-permute-done.17 = bf16[1,176,1024]{2,1,0:T(8,128)(2,1)S(1)} collective-permute-done((bf16[1,176,1024]{2,1,0:T(8,128)(2,1)S(1)}, bf16[1,176,1024]{2,1,0:T(8,128)(2,1)S(1)}, u32[]{:S(2)}, u32[]{:S(2)}) %collective-permute-start.17) | collective-permute-done | bytes 360480 | tf_op jit(solution)/shard_map/ppermute | solution.py:346
  137.0 3.4 %collective-permute-done.14 = bf16[1,176,1024]{2,1,0:T(8,128)(2,1)S(1)} collective-permute-done((bf16[1,176,1024]{2,1,0:T(8,128)(2,1)S(1)}, bf16[1,176,1024]{2,1,0:T(8,128)(2,1)S(1)}, u32[]{:S(2)}, u32[]{:S(2)}) %collective-permute-start.14) | collective-permute-done | bytes 360480 | tf_op jit(solution)/shard_map/ppermute | solution.py:341
  140.4 2.3 %collective-permute-done.16 = bf16[1,176,1024]{2,1,0:T(8,128)(2,1)S(1)} collective-permute-done((bf16[1,176,1024]{2,1,0:T(8,128)(2,1)S(1)}, bf16[1,176,1024]{2,1,0:T(8,128)(2,1)S(1)}, u32[]{:S(2)}, u32[]{:S(2)}) %collective-permute-start.16) | collective-permute-done | bytes 360480 | tf_op jit(solution)/shard_map/ppermute | solution.py:346
  142.7 4.0 %collective-permute-done.21.refs_5_ = bf16[208,1024]{1,0:T(8,128)(2,1)S(1)} collective-permute-done((bf16[208,1024]{1,0:T(8,128)(2,1)S(1)}, bf16[208,1024]{1,0:T(8,128)(2,1)S(1)}, u32[]{:S(2)}, u32[]{:S(2)}) %collective-permute-start.21) | collective-permute-done | bytes 426016 | tf_op jit(solution)/shard_map/ppermute | solution.py:341
  146.6 1.6 %finale.1 = (bf16[384,1024]{1,0:T(8,128)(2,1)}, f32[8,128]{1,0:T(8,128)S(1)}) custom-call(s32[1]{0:T(128)} %bitcast.layer_ref, bf16[1,1024]{1,0:T(2,128)(2,1)S(1)} %copy-done.7, bf16[384,1024]{1,0:T(8,128)(2,1)S(1)} %bitcast.22, f32[176,1024]{1,0:T(8,128)S(1)} %bitcast.23, bf16[176,1024]{1,0:T(8,128)(2,1)S(1)} %bitcast.25, bf16[176,1024]{1,0:T(8,128)(2,1)S(1)} %bitcast.26, ...), custom_call_target="tpu_custom_call" | custom-call | tf_op jit(solution)/shard_map/finale/pallas_call | solution.py:306
  148.8 0.8 collective-permute-done.24
  149.6 2.3 %collective-permute-done.23 = f32[8,128]{1,0:T(8,128)S(1)} collective-permute-done((f32[8,128]{1,0:T(8,128)S(1)}, f32[8,128]{1,0:T(8,128)S(1)}, u32[]{:S(2)}, u32[]{:S(2)}) %collective-permute-start.23) | collective-permute-done | bytes 4128 | tf_op jit(solution)/shard_map/ppermute | solution.py:341
  151.9 2.6 %collective-permute-start.27 = (f32[8,128]{1,0:T(8,128)S(1)}, f32[8,128]{1,0:T(8,128)S(1)}, u32[]{:S(2)}, u32[]{:S(2)}) collective-permute-start(f32[8,128]{1,0:T(8,128)S(1)} %add_add_fusion.refs_0_), channel_id=1, source_target_pairs={{0,12},{4,0},{8,4},{12,8},{1,13},{5,1},{9,5},{13,9},{2,14},{6,2},{... | collective-permute-start | bytes 12296 | tf_op jit(solution)/shard_map/ppermute | solution.py:341
  154.5 0.6 collective-permute-start.25
  155.1 0.7 collective-permute-done.27.refs_3_
  155.8 3.2 %collective-permute-done.26.refs_2_ = f32[8,128]{1,0:T(8,128)S(1)} collective-permute-done((f32[8,128]{1,0:T(8,128)S(1)}, f32[8,128]{1,0:T(8,128)S(1)}, u32[]{:S(2)}, u32[]{:S(2)}) %collective-permute-start.26) | collective-permute-done | bytes 4128 | tf_op jit(solution)/shard_map/ppermute | solution.py:341
  159.0 0.9 collective-permute-done.25.refs_1_
  160.5 1.2 mean_ratio.1
  (63 shorter events, 3.5 us)
Async XLA Ops:
  0.6 12.2 %copy-start = (bf16[1,4096]{1,0:T(2,128)(2,1)S(1)}, bf16[1,4096]{1,0:T(2,128)(2,1)}, u32[]{:S(2)}) copy-start(bf16[1,4096]{1,0:T(2,128)(2,1)} %param.10) | copy-start | bytes 24580
  3.4 4.6 %collective-permute-start = (f32[1]{0:T(128)}, f32[1]{0:T(128)}, u32[]{:S(2)}, u32[]{:S(2)}) collective-permute-start(f32[1]{0:T(128)} %get-tuple-element.27), channel_id=1, source_target_pairs={{0,2},{2,0},{1,3},{3,1},{4,6},{6,4},{5,7},{7,5},{8,10},{10,8},{9,1... | collective-permute-start | bytes 20 | tf_op jit(solution)/shard_map/ppermute | solution.py:341
  10.7 23.7 %collective-permute-start.3 = (bf16[112,4096]{1,0:T(8,128)(2,1)}, bf16[112,4096]{1,0:T(8,128)(2,1)}, u32[]{:S(2)}, u32[]{:S(2)}) collective-permute-start(bf16[112,4096]{1,0:T(8,128)(2,1)} %get-tuple-element.33), channel_id=1, source_target_pairs={{0,2},{2,0},{1,3},{3,1},{4,6},{6,4},{5,7},{7,5},{8,10},{10,8},{9,1... | collective-permute-start | bytes 2752520 | tf_op jit(solution)/shard_map/ppermute | solution.py:341
  23.8 12.8 %collective-permute-start.1 = (bf16[384,1024]{1,0:T(8,128)(2,1)}, bf16[384,1024]{1,0:T(8,128)(2,1)S(1)}, u32[]{:S(2)}, u32[]{:S(2)}) collective-permute-start(bf16[384,1024]{1,0:T(8,128)(2,1)} %get-tuple-element.29.refs_0_), channel_id=1, source_target_pairs={{0,1},{2,3},{4,5},{6,7},{8,9},{10,11},{12,13},{14,15},{16,17},{18,... | collective-permute-start | bytes 2359304 | tf_op jit(solution)/shard_map/ppermute | solution.py:408
  25.1 11.4 %collective-permute-start.2 = (bf16[384,1024]{1,0:T(8,128)(2,1)}, bf16[384,1024]{1,0:T(8,128)(2,1)S(1)}, u32[]{:S(2)}, u32[]{:S(2)}) collective-permute-start(bf16[384,1024]{1,0:T(8,128)(2,1)} %get-tuple-element.30.refs_1_), channel_id=1, source_target_pairs={{0,1},{2,3},{4,5},{6,7},{8,9},{10,11},{12,13},{14,15},{16,17},{18,... | collective-permute-start | bytes 2359304 | tf_op jit(solution)/shard_map/ppermute | solution.py:408
  26.5 37.0 %collective-permute-start.5 = (bf16[160,4096]{1,0:T(8,128)(2,1)}, bf16[160,4096]{1,0:T(8,128)(2,1)S(1)}, u32[]{:S(2)}, u32[]{:S(2)}) collective-permute-start(bf16[160,4096]{1,0:T(8,128)(2,1)} %get-tuple-element.34), channel_id=1, source_target_pairs={{0,2},{2,0},{1,3},{3,1},{4,6},{6,4},{5,7},{7,5},{8,10},{10,8},{9,1... | collective-permute-start | bytes 3932168 | tf_op jit(solution)/shard_map/ppermute | solution.py:341
  34.4 29.1 %collective-permute-start.4 = (bf16[112,4096]{1,0:T(8,128)(2,1)}, bf16[112,4096]{1,0:T(8,128)(2,1)}, u32[]{:S(2)}, u32[]{:S(2)}) collective-permute-start(bf16[112,4096]{1,0:T(8,128)(2,1)} %collective-permute-done.3.refs_0_), channel_id=1, source_target_pairs={{0,4},{4,0},{8,12},{12,8},{1,5},{5,1},{9,13},{13,9},{2,6},{6,2},{1... | collective-permute-start | bytes 2752520 | tf_op jit(solution)/shard_map/ppermute | solution.py:346
  44.0 0.9 copy-start.3
  44.8 0.9 copy-start.5
  45.8 0.8 copy-start.8
  46.5 15.8 %collective-permute-start.6 = (bf16[1,208,1024]{2,1,0:T(8,128)(2,1)S(1)}, bf16[1,208,1024]{2,1,0:T(8,128)(2,1)}, u32[]{:S(2)}, u32[]{:S(2)}) collective-permute-start(bf16[1,208,1024]{2,1,0:T(8,128)(2,1)S(1)} %get-tuple-element.31.refs_6_), channel_id=1, source_target_pairs={{0,4},{4,0},{8,12},{12,8},{1,5},{5,1},{9,13},{13,9},{2,6},{6,2},{1... | collective-permute-start | bytes 1277960 | tf_op jit(solution)/shard_map/ppermute | solution.py:346
  63.5 12.2 %copy-start.9 = (bf16[1,208,1024]{2,1,0:T(8,128)(2,1)S(1)}, bf16[1,208,1024]{2,1,0:T(8,128)(2,1)}, u32[]{:S(2)}) copy-start(bf16[1,208,1024]{2,1,0:T(8,128)(2,1)} %copy-done.8) | copy-start | bytes 1277956
  74.2 5.7 %collective-permute-start.7 = (bf16[384,2048]{1,0:T(8,128)(2,1)S(1)}, bf16[384,2048]{1,0:T(8,128)(2,1)S(1)}, u32[]{:S(2)}, u32[]{:S(2)}) collective-permute-start(bf16[384,2048]{1,0:T(8,128)(2,1)S(1)} %encode.3.refs_0_), channel_id=1, source_target_pairs={{0,1},{2,3},{4,5},{6,7},{8,9},{10,11},{12,13},{14,15},{16,17},{18,... | collective-permute-start | bytes 4718600 | tf_op jit(solution)/shard_map/ppermute | solution.py:408
  75.6 18.1 %collective-permute-start.8 = (bf16[1,208,1024]{2,1,0:T(8,128)(2,1)S(1)}, bf16[1,208,1024]{2,1,0:T(8,128)(2,1)S(1)}, u32[]{:S(2)}, u32[]{:S(2)}) collective-permute-start(bf16[1,208,1024]{2,1,0:T(8,128)(2,1)S(1)} %copy-done.9), channel_id=1, source_target_pairs={{0,4},{4,0},{8,12},{12,8},{1,5},{5,1},{9,13},{13,9},{2,6},{6,2},{1... | collective-permute-start | bytes 1277960 | tf_op jit(solution)/shard_map/ppermute | solution.py:346
  77.2 16.5 %collective-permute-start.9 = (bf16[1,208,1024]{2,1,0:T(8,128)(2,1)S(1)}, bf16[1,208,1024]{2,1,0:T(8,128)(2,1)S(1)}, u32[]{:S(2)}, u32[]{:S(2)}) collective-permute-start(bf16[1,208,1024]{2,1,0:T(8,128)(2,1)S(1)} %add_convert_fusion.2.refs_4_), channel_id=1, source_target_pairs={{0,8},{4,12},{8,0},{12,4},{1,9},{5,13},{9,1},{13,5},{2,10},{6,14},... | collective-permute-start | bytes 1277960 | tf_op jit(solution)/shard_map/ppermute | solution.py:346
  84.4 15.9 %collective-permute-start.11 = (bf16[1,176,1024]{2,1,0:T(8,128)(2,1)S(1)}, bf16[1,176,1024]{2,1,0:T(8,128)(2,1)S(1)}, u32[]{:S(2)}, u32[]{:S(2)}) collective-permute-start(bf16[1,176,1024]{2,1,0:T(8,128)(2,1)S(1)} %get-tuple-element.41), channel_id=1, source_target_pairs={{0,2},{2,0},{1,3},{3,1},{4,6},{6,4},{5,7},{7,5},{8,10},{10,8},{9,1... | collective-permute-start | bytes 1081352 | tf_op jit(solution)/shard_map/ppermute | solution.py:341
  86.1 18.0 %collective-permute-start.10 = (bf16[1,208,1024]{2,1,0:T(8,128)(2,1)S(1)}, bf16[1,208,1024]{2,1,0:T(8,128)(2,1)S(1)}, u32[]{:S(2)}, u32[]{:S(2)}) collective-permute-start(bf16[1,208,1024]{2,1,0:T(8,128)(2,1)S(1)} %get-tuple-element.36.refs_4_), channel_id=1, source_target_pairs={{0,4},{4,0},{8,12},{12,8},{1,5},{5,1},{9,13},{13,9},{2,6},{6,2},{1... | collective-permute-start | bytes 1277960 | tf_op jit(solution)/shard_map/ppermute | solution.py:346
  94.0 6.3 %copy-start.6 = (f32[1,176,1024]{2,1,0:T(8,128)S(1)}, f32[1,176,1024]{2,1,0:T(8,128)}, u32[]{:S(2)}) copy-start(f32[1,176,1024]{2,1,0:T(8,128)} %copy-done.5) | copy-start | bytes 2162692
  98.5 14.1 %collective-permute-start.12 = (bf16[1,176,1024]{2,1,0:T(8,128)(2,1)S(1)}, bf16[1,176,1024]{2,1,0:T(8,128)(2,1)S(1)}, u32[]{:S(2)}, u32[]{:S(2)}) collective-permute-start(bf16[1,176,1024]{2,1,0:T(8,128)(2,1)S(1)} %get-tuple-element.45), channel_id=1, source_target_pairs={{0,2},{2,0},{1,3},{3,1},{4,6},{6,4},{5,7},{7,5},{8,10},{10,8},{9,1... | collective-permute-start | bytes 1081352 | tf_op jit(solution)/shard_map/ppermute | solution.py:341
  100.4 20.1 %collective-permute-start.13 = (bf16[1,176,1024]{2,1,0:T(8,128)(2,1)S(1)}, bf16[1,176,1024]{2,1,0:T(8,128)(2,1)S(1)}, u32[]{:S(2)}, u32[]{:S(2)}) collective-permute-start(bf16[1,176,1024]{2,1,0:T(8,128)(2,1)S(1)} %add_convert_fusion.5.refs_5_), channel_id=1, source_target_pairs={{0,4},{4,0},{8,12},{12,8},{1,5},{5,1},{9,13},{13,9},{2,6},{6,2},{1... | collective-permute-start | bytes 1081352 | tf_op jit(solution)/shard_map/ppermute | solution.py:346
  104.1 30.3 %collective-permute-start.20 = (bf16[1,208,1024]{2,1,0:T(8,128)(2,1)S(1)}, bf16[1,208,1024]{2,1,0:T(8,128)(2,1)S(1)}, u32[]{:S(2)}, u32[]{:S(2)}) collective-permute-start(bf16[1,208,1024]{2,1,0:T(8,128)(2,1)S(1)} %add_convert_fusion.1.refs_4_), channel_id=1, source_target_pairs={{0,8},{4,12},{8,0},{12,4},{1,9},{5,13},{9,1},{13,5},{2,10},{6,14},... | collective-permute-start | bytes 1277960 | tf_op jit(solution)/shard_map/ppermute | solution.py:346
  110.5 19.5 %collective-permute-start.19 = (bf16[1,96,1024]{2,1,0:T(8,128)(2,1)S(1)}, bf16[1,96,1024]{2,1,0:T(8,128)(2,1)S(1)}, u32[]{:S(2)}, u32[]{:S(2)}) collective-permute-start(bf16[1,96,1024]{2,1,0:T(8,128)(2,1)S(1)} %get-tuple-element.43.refs_5_), channel_id=1, source_target_pairs={{0,4},{4,0},{8,12},{12,8},{1,5},{5,1},{9,13},{13,9},{2,6},{6,2},{1... | collective-permute-start | bytes 589832 | tf_op jit(solution)/shard_map/ppermute | solution.py:346
  110.8 23.6 %collective-permute-start.18 = (bf16[1,112,1024]{2,1,0:T(8,128)(2,1)S(1)}, bf16[1,112,1024]{2,1,0:T(8,128)(2,1)S(1)}, u32[]{:S(2)}, u32[]{:S(2)}) collective-permute-start(bf16[1,112,1024]{2,1,0:T(8,128)(2,1)S(1)} %get-tuple-element.42.refs_4_), channel_id=1, source_target_pairs={{0,4},{4,0},{8,12},{12,8},{1,5},{5,1},{9,13},{13,9},{2,6},{6,2},{1... | collective-permute-start | bytes 688136 | tf_op jit(solution)/shard_map/ppermute | solution.py:346
  112.6 22.1 %collective-permute-start.15 = (bf16[1,176,1024]{2,1,0:T(8,128)(2,1)S(1)}, bf16[1,176,1024]{2,1,0:T(8,128)(2,1)S(1)}, u32[]{:S(2)}, u32[]{:S(2)}) collective-permute-start(bf16[1,176,1024]{2,1,0:T(8,128)(2,1)S(1)} %get-tuple-element.48), channel_id=1, source_target_pairs={{0,2},{2,0},{1,3},{3,1},{4,6},{6,4},{5,7},{7,5},{8,10},{10,8},{9,1... | collective-permute-start | bytes 1081352 | tf_op jit(solution)/shard_map/ppermute | solution.py:341
  120.7 14.0 %copy-start.4 = (f32[1,176,1024]{2,1,0:T(8,128)S(1)}, f32[1,176,1024]{2,1,0:T(8,128)}, u32[]{:S(2)}) copy-start(f32[1,176,1024]{2,1,0:T(8,128)} %copy-done.3) | copy-start | bytes 2162692
  120.7 16.3 %collective-permute-start.17 = (bf16[1,176,1024]{2,1,0:T(8,128)(2,1)S(1)}, bf16[1,176,1024]{2,1,0:T(8,128)(2,1)S(1)}, u32[]{:S(2)}, u32[]{:S(2)}) collective-permute-start(bf16[1,176,1024]{2,1,0:T(8,128)(2,1)S(1)} %add_convert_fusion.4.refs_6_), channel_id=1, source_target_pairs={{0,8},{4,12},{8,0},{12,4},{1,9},{5,13},{9,1},{13,5},{2,10},{6,14},... | collective-permute-start | bytes 1081352 | tf_op jit(solution)/shard_map/ppermute | solution.py:346
  125.5 21.1 %copy-start.2 = (bf16[1,384,1024]{2,1,0:T(8,128)(2,1)S(1)}, bf16[1,384,1024]{2,1,0:T(8,128)(2,1)}, u32[]{:S(2)}) copy-start(bf16[1,384,1024]{2,1,0:T(8,128)(2,1)} %param.8) | copy-start | bytes 2359300
  125.5 21.1 %copy-start.7 = (bf16[1,1024]{1,0:T(2,128)(2,1)S(1)}, bf16[1,1024]{1,0:T(2,128)(2,1)}, u32[]{:S(2)}) copy-start(bf16[1,1024]{1,0:T(2,128)(2,1)} %b_ref.1) | copy-start | bytes 6148
  130.1 10.3 %collective-permute-start.14 = (bf16[1,176,1024]{2,1,0:T(8,128)(2,1)S(1)}, bf16[1,176,1024]{2,1,0:T(8,128)(2,1)S(1)}, u32[]{:S(2)}, u32[]{:S(2)}) collective-permute-start(bf16[1,176,1024]{2,1,0:T(8,128)(2,1)S(1)} %get-tuple-element.46), channel_id=1, source_target_pairs={{0,2},{2,0},{1,3},{3,1},{4,6},{6,4},{5,7},{7,5},{8,10},{10,8},{9,1... | collective-permute-start | bytes 1081352 | tf_op jit(solution)/shard_map/ppermute | solution.py:341
  134.4 27.3 %copy-start.1 = (bf16[1,4096]{1,0:T(2,128)(2,1)S(1)}, bf16[1,4096]{1,0:T(2,128)(2,1)}, u32[]{:S(2)}) copy-start(bf16[1,4096]{1,0:T(2,128)(2,1)} %param.10) | copy-start | bytes 24580
  134.6 12.0 %collective-permute-start.21 = (bf16[208,1024]{1,0:T(8,128)(2,1)S(1)}, bf16[208,1024]{1,0:T(8,128)(2,1)S(1)}, u32[]{:S(2)}, u32[]{:S(2)}) collective-permute-start(bf16[208,1024]{1,0:T(8,128)(2,1)S(1)} %fusion), channel_id=1, source_target_pairs={{0,2},{2,0},{1,3},{3,1},{4,6},{6,4},{5,7},{7,5},{8,10},{10,8},{9,1... | collective-permute-start | bytes 1277960 | tf_op jit(solution)/shard_map/ppermute | solution.py:341
  134.8 7.8 %collective-permute-start.16 = (bf16[1,176,1024]{2,1,0:T(8,128)(2,1)S(1)}, bf16[1,176,1024]{2,1,0:T(8,128)(2,1)S(1)}, u32[]{:S(2)}, u32[]{:S(2)}) collective-permute-start(bf16[1,176,1024]{2,1,0:T(8,128)(2,1)S(1)} %add_convert_fusion.3), channel_id=1, source_target_pairs={{0,4},{4,0},{8,12},{12,8},{1,5},{5,1},{9,13},{13,9},{2,6},{6,2},{1... | collective-permute-start | bytes 1081352 | tf_op jit(solution)/shard_map/ppermute | solution.py:346
  148.2 1.3 collective-permute-start.24
  148.3 3.6 %collective-permute-start.23 = (f32[8,128]{1,0:T(8,128)S(1)}, f32[8,128]{1,0:T(8,128)S(1)}, u32[]{:S(2)}, u32[]{:S(2)}) collective-permute-start(f32[8,128]{1,0:T(8,128)S(1)} %get-tuple-element.51), channel_id=1, source_target_pairs={{0,2},{1,3},{2,0},{3,1},{4,6},{5,7},{6,4},{7,5},{8,10},{9,11},{10,... | collective-permute-start | bytes 12296 | tf_op jit(solution)/shard_map/ppermute | solution.py:341
  148.3 3.5 %collective-permute-start.22 = (f32[8,128]{1,0:T(8,128)S(1)}, f32[8,128]{1,0:T(8,128)S(1)}, u32[]{:S(2)}, u32[]{:S(2)}) collective-permute-start(f32[8,128]{1,0:T(8,128)S(1)} %get-tuple-element.51), channel_id=1, source_target_pairs={{0,1},{1,2},{2,3},{3,0},{4,5},{5,6},{6,7},{7,4},{8,9},{9,10},{10,1... | collective-permute-start | bytes 12296 | tf_op jit(solution)/shard_map/ppermute | solution.py:341
  151.9 8.0 %copy-start.10 = (f32[8,128]{1,0:T(8,128)}, f32[8,128]{1,0:T(8,128)S(1)}, u32[]{:S(2)}) copy-start(f32[8,128]{1,0:T(8,128)S(1)} %add_add_fusion.refs_0_) | copy-start | bytes 12292
  151.9 3.9 %collective-permute-start.27 = (f32[8,128]{1,0:T(8,128)S(1)}, f32[8,128]{1,0:T(8,128)S(1)}, u32[]{:S(2)}, u32[]{:S(2)}) collective-permute-start(f32[8,128]{1,0:T(8,128)S(1)} %add_add_fusion.refs_0_), channel_id=1, source_target_pairs={{0,12},{4,0},{8,4},{12,8},{1,13},{5,1},{9,5},{13,9},{2,14},{6,2},{... | collective-permute-start | bytes 12296 | tf_op jit(solution)/shard_map/ppermute | solution.py:341
  154.4 4.5 %collective-permute-start.26 = (f32[8,128]{1,0:T(8,128)S(1)}, f32[8,128]{1,0:T(8,128)S(1)}, u32[]{:S(2)}, u32[]{:S(2)}) collective-permute-start(f32[8,128]{1,0:T(8,128)S(1)} %add_add_fusion.refs_0_), channel_id=1, source_target_pairs={{0,8},{4,12},{8,0},{12,4},{1,9},{5,13},{9,1},{13,5},{2,10},{6,14},... | collective-permute-start | bytes 12296 | tf_op jit(solution)/shard_map/ppermute | solution.py:341
  154.5 5.4 %collective-permute-start.25 = (f32[8,128]{1,0:T(8,128)S(1)}, f32[8,128]{1,0:T(8,128)S(1)}, u32[]{:S(2)}, u32[]{:S(2)}) collective-permute-start(f32[8,128]{1,0:T(8,128)S(1)} %add_add_fusion.refs_0_), channel_id=1, source_target_pairs={{0,4},{4,8},{8,12},{12,0},{1,5},{5,9},{9,13},{13,1},{2,6},{6,10},{... | collective-permute-start | bytes 12296 | tf_op jit(solution)/shard_map/ppermute | solution.py:341
  155.8 4.1 %copy-start.11 = (f32[8,128]{1,0:T(8,128)}, f32[8,128]{1,0:T(8,128)S(1)}, u32[]{:S(2)}) copy-start(f32[8,128]{1,0:T(8,128)S(1)} %collective-permute-done.27.refs_3_) | copy-start | bytes 12292
  159.0 0.9 copy-start.12
  159.9 0.6 copy-start.13

commit v12 on v11

--- a/solution.py
+++ b/solution.py
@@ -380,7 +380,7 @@
     square = sum_over(square, "token")
     scale = jnp.sqrt(square / (rows * n_tok * model) + 1e-06)
     inv = 1.0 / scale
-    outer, inner = cut(x_held, side.astype(jnp.int32), edge, inv)
+    outer, inner = cut(x_held, side.astype(jnp.int32), edge, square)
     foreign = []
     for distance in range(1, n_tok):
         mine = shifted(outer, "token", distance)
@@ -450,7 +450,7 @@
         codes = encode(
             [(mine, 0, edge), (theirs, 0, edge), (inner_rows, 0, rows - 2 * edge)],
             places(side * (rows - edge), (1 - side) * (rows - edge), edge),
-            inv, enc_w, bias, 1, [after])
+            inv, enc_w, bias, min(2, lat_dev // 256), [after])
         earlier = earlier_of(codes)
 
         def quarter_of(low, high, spans, dtype, also):

time: 162 us -> 163 us (level)
  starting transfers between devices: 34.1 us -> 40.9 us
  waiting for transfers between devices: 58.1 us -> 52.6 us
    ppermute x14, waiting for transfers between devices: 24.6 us -> 18.6 us  [shifted(): lax.ppermute(value, axis, [(i, (i + distance) % n) for i in range(n)])]
    ppermute x14, starting transfers between devices: 15.7 us -> 19.9 us  [shifted(): lax.ppermute(value, axis, [(i, (i + distance) % n) for i in range(n)])]
    ppermute x3 -> x4, starting transfers between devices: 4.07 us -> 5.36 us  [earlier_of(): return [lax.ppermute(part, 'layer', [(0, 1)]) for part in codes]]
  transfers between devices with their start and end apart: 28 -> 29, of which waited for: 16 -> 18; matrix products, arithmetic and copies ran while one was open for 1% -> 1% of each run, Pallas kernels for 27% -> 27%
where the time goes in v12:
time: 163 us
  Pallas kernels  61.6 us (38%)
  waiting for transfers between devices  52.6 us (32%)
  starting transfers between devices  40.9 us (25%)
  local copies, waits for them, and re-layouts  3.18 us (2%)
  other arithmetic  2.38 us (1%)
  between operations  2.33 us (1%)
    ppermute x11, waiting for transfers between devices, swapped(): return lax.ppermute(value, axis, [(i, i ^ bit) for i in range(n)])  33.9 us
    pallas_call x6, Pallas kernels, decode(): pl.pallas_call(body, in_specs=[pl.BlockSpec(memory_space=pltpu.SMEM)] + [...  32.9 us
    pallas_call x2, Pallas kernels, encode(): pl.pallas_call(body, in_specs=[pl.BlockSpec(memory_space=pltpu.SMEM), pl....  21.7 us
    ppermute x14, starting transfers between devices, shifted(): lax.ppermute(value, axis, [(i, (i + distance) % n) for i in range(n)])  19.9 us
    ppermute x14, waiting for transfers between devices, shifted(): lax.ppermute(value, axis, [(i, (i + distance) % n) for i in range(n)])  18.6 us
    ppermute x11, starting transfers between devices, swapped(): return lax.ppermute(value, axis, [(i, i ^ bit) for i in range(n)])  15.7 us
    ppermute x4, starting transfers between devices, earlier_of(): return [lax.ppermute(part, 'layer', [(0, 1)]) for part in codes]  5.36 us
  transfers between devices with their start and end apart: 29, of which 18 were waited for; matrix products, arithmetic and copies ran while one was open for 1% of the time, Pallas kernels for 27%

profile of v12, /device:TPU:0, one launch (start us, length us, event | category | flops | bytes accessed | tf_op | source)
XLA Modules:
  0.0 163.0 jit_solution(2068756057144481006)
XLA Ops:
  0.6 2.7 %square_sum.1 = (f32[1]{0:T(128)}, bf16[384,4096]{1,0:T(8,128)(2,1)S(1)}) custom-call(bf16[384,4096]{1,0:T(8,128)(2,1)} %bitcast.35), custom_call_target="tpu_custom_call" | custom-call | tf_op jit(solution)/shard_map/square_sum/pallas_call | solution.py:47
  3.4 3.0 %collective-permute-start = (f32[1]{0:T(128)}, f32[1]{0:T(128)}, u32[]{:S(2)}, u32[]{:S(2)}) collective-permute-start(f32[1]{0:T(128)} %get-tuple-element.29), channel_id=1, source_target_pairs={{0,2},{2,0},{1,3},{3,1},{4,6},{6,4},{5,7},{7,5},{8,10},{10,8},{9,1... | collective-permute-start | bytes 20 | tf_op jit(solution)/shard_map/ppermute | solution.py:341
  6.4 1.6 collective-permute-done
  9.3 1.4 cut.1
  10.7 2.1 %collective-permute-start.3 = (bf16[112,4096]{1,0:T(8,128)(2,1)}, bf16[112,4096]{1,0:T(8,128)(2,1)}, u32[]{:S(2)}, u32[]{:S(2)}) collective-permute-start(bf16[112,4096]{1,0:T(8,128)(2,1)} %get-tuple-element.35), channel_id=1, source_target_pairs={{0,2},{2,0},{1,3},{3,1},{4,6},{6,4},{5,7},{7,5},{8,10},{10,8},{9,1... | collective-permute-start | bytes 2752520 | tf_op jit(solution)/shard_map/ppermute | solution.py:341
  12.9 11.0 %encode.2 = (bf16[384,1024]{1,0:T(8,128)(2,1)}, bf16[384,1024]{1,0:T(8,128)(2,1)}) custom-call(s32[1]{0:T(128)} %constant.58.clone.1.places_ref, f32[1]{0:T(128)S(6)} %sqrt.3.inv_ref, bf16[1,2048]{1,0:T(2,128)(2,1)S(1)} %constant_dynamic-slice_fusion.b_ref, bf16[384,4096]{1,0:T(8,128)(2,1)S(1)} %get-tuple-element.30.refs_0_.x_ref, bf16[4096,2048]{1,0:T(8,128)(2,1)} %bitcast.33), custom_call_target="tpu_custom_call" | custom-call | tf_op jit(solution)/shard_map/encode/pallas_call | solution.py:152
  23.8 1.3 collective-permute-start.1
  25.2 1.3 collective-permute-start.2
  26.6 7.8 %collective-permute-done.3.refs_0_ = bf16[112,4096]{1,0:T(8,128)(2,1)} collective-permute-done((bf16[112,4096]{1,0:T(8,128)(2,1)}, bf16[112,4096]{1,0:T(8,128)(2,1)}, u32[]{:S(2)}, u32[]{:S(2)}) %collective-permute-start.3) | collective-permute-done | bytes 917536 | tf_op jit(solution)/shard_map/ppermute | solution.py:341
  34.4 2.1 %collective-permute-start.4 = (bf16[112,4096]{1,0:T(8,128)(2,1)}, bf16[112,4096]{1,0:T(8,128)(2,1)}, u32[]{:S(2)}, u32[]{:S(2)}) collective-permute-start(bf16[112,4096]{1,0:T(8,128)(2,1)} %collective-permute-done.3.refs_0_), channel_id=1, source_target_pairs={{0,4},{4,0},{8,12},{12,8},{1,5},{5,1},{9,13},{13,9},{2,6},{6,2},{1... | collective-permute-start | bytes 2752520 | tf_op jit(solution)/shard_map/ppermute | solution.py:346
  36.6 7.4 %decode.6 = (bf16[1,208,1024]{2,1,0:T(8,128)(2,1)S(1)}, bf16[1,208,1024]{2,1,0:T(8,128)(2,1)S(1)}, f32[1,176,1024]{2,1,0:T(8,128)S(1)}, f32[1,176,1024]{2,1,0:T(8,128)S(1)}) custom-call(s32[3]{0:T(128)S(1)} %get-tuple-element.57.info_ref, bf16[384,1024]{1,0:T(8,128)(2,1)} %get-tuple-element.31.refs_0_, bf16[384,1024]{1,0:T(8,128)(2,1)} %get-tuple-element.32.refs_1_, ...), custom_call_target="tpu_custom_call" | custom-call | tf_op jit(solution)/shard_map/decode/pallas_call | solution.py:251
  44.0 0.9 copy-done.3
  44.9 0.9 copy-done.5
  45.8 0.8 copy-done.8
  46.6 7.4 %decode.7 = (f32[1,208,1024]{2,1,0:T(8,128)S(1)}, f32[1,208,1024]{2,1,0:T(8,128)S(1)}, f32[1,176,1024]{2,1,0:T(8,128)S(1)}, f32[1,176,1024]{2,1,0:T(8,128)S(1)}) custom-call(s32[3]{0:T(128)S(1)} %get-tuple-element.56.info_ref, bf16[384,1024]{1,0:T(8,128)(2,1)} %get-tuple-element.31.refs_0_, bf16[384,1024]{1,0:T(8,128)(2,1)} %get-tuple-element.32.refs_1_, ...), custom_call_target="tpu_custom_call" | custom-call | tf_op jit(solution)/shard_map/decode/pallas_call | solution.py:251
  54.0 8.4 %collective-permute-done.6 = bf16[1,208,1024]{2,1,0:T(8,128)(2,1)} collective-permute-done((bf16[1,208,1024]{2,1,0:T(8,128)(2,1)S(1)}, bf16[1,208,1024]{2,1,0:T(8,128)(2,1)}, u32[]{:S(2)}, u32[]{:S(2)}) %collective-permute-start.6) | collective-permute-done | bytes 426016 | tf_op jit(solution)/shard_map/ppermute | solution.py:346
  62.4 1.1 add_convert_fusion.2.refs_4_
  63.5 10.8 %encode.3 = (bf16[384,1024]{1,0:T(8,128)(2,1)S(1)}, bf16[384,1024]{1,0:T(8,128)(2,1)S(1)}) custom-call(s32[3]{0:T(128)S(1)} %pad_add_fusion.3.places_ref, f32[1]{0:T(128)S(6)} %sqrt.3.inv_ref, bf16[1,2048]{1,0:T(2,128)(2,1)S(1)} %constant_dynamic-slice_fusion.b_ref, bf16[112,4096]{1,0:T(8,128)(2,1)} %collective-permute-done.3.refs_0_, ...), custom_call_target="tpu_custom_call" | custom-call | tf_op jit(solution)/shard_map/encode/pallas_call | solution.py:152
  74.3 1.3 collective-permute-start.7
  75.6 1.3 collective-permute-start.8
  77.0 1.6 collective-permute-start.9
  78.6 2.6 %collective-permute-start.10 = (bf16[1,208,1024]{2,1,0:T(8,128)(2,1)S(1)}, bf16[1,208,1024]{2,1,0:T(8,128)(2,1)S(1)}, u32[]{:S(2)}, u32[]{:S(2)}) collective-permute-start(bf16[1,208,1024]{2,1,0:T(8,128)(2,1)S(1)} %add_convert_fusion.2.refs_4_), channel_id=1, source_target_pairs={{0,8},{4,12},{8,0},{12,4},{1,9},{5,13},{9,1},{13,5},{2,10},{6,14},... | collective-permute-start | bytes 1277960 | tf_op jit(solution)/shard_map/ppermute | solution.py:346
  81.3 4.5 %decode.8 = (bf16[1,208,1024]{2,1,0:T(8,128)(2,1)S(1)}, bf16[1,176,1024]{2,1,0:T(8,128)(2,1)S(1)}) custom-call(s32[2]{0:T(128)S(1)} %pad_add_fusion.6.info_ref, bf16[384,1024]{1,0:T(8,128)(2,1)S(1)} %get-tuple-element.38.refs_0_, bf16[384,1024]{1,0:T(8,128)(2,1)S(1)} %get-tuple-element.39.refs_1_, bf16[384,1024]{1,0:T(8,128)(2,1)S(1)} %collective-permute-done.7.refs_2_, ...), custom_call_target="tpu_custom_call" | custom-call | tf_op jit(solution)/shard_map/decode/pallas_call | solution.py:251
  85.8 1.6 collective-permute-start.12
  87.8 7.4 %collective-permute-done.9 = bf16[1,208,1024]{2,1,0:T(8,128)(2,1)S(1)} collective-permute-done((bf16[1,208,1024]{2,1,0:T(8,128)(2,1)S(1)}, bf16[1,208,1024]{2,1,0:T(8,128)(2,1)S(1)}, u32[]{:S(2)}, u32[]{:S(2)}) %collective-permute-start.9) | collective-permute-done | bytes 426016 | tf_op jit(solution)/shard_map/ppermute | solution.py:346
  95.8 4.5 %decode.9 = (f32[1,208,1024]{2,1,0:T(8,128)S(1)}, bf16[1,176,1024]{2,1,0:T(8,128)(2,1)S(1)}) custom-call(s32[2]{0:T(128)S(1)} %pad_add_fusion.5.info_ref, bf16[384,1024]{1,0:T(8,128)(2,1)S(1)} %get-tuple-element.38.refs_0_, bf16[384,1024]{1,0:T(8,128)(2,1)S(1)} %get-tuple-element.39.refs_1_, bf16[384,1024]{1,0:T(8,128)(2,1)S(1)} %collective-permute-done.7.refs_2_, ...), custom_call_target="tpu_custom_call" | custom-call | tf_op jit(solution)/shard_map/decode/pallas_call | solution.py:251
  100.3 2.4 %collective-permute-start.13 = (bf16[1,176,1024]{2,1,0:T(8,128)(2,1)S(1)}, bf16[1,176,1024]{2,1,0:T(8,128)(2,1)S(1)}, u32[]{:S(2)}, u32[]{:S(2)}) collective-permute-start(bf16[1,176,1024]{2,1,0:T(8,128)(2,1)S(1)} %get-tuple-element.49), channel_id=1, source_target_pairs={{0,2},{2,0},{1,3},{3,1},{4,6},{6,4},{5,7},{7,5},{8,10},{10,8},{9,1... | collective-permute-start | bytes 1081352 | tf_op jit(solution)/shard_map/ppermute | solution.py:341
  102.8 3.6 %collective-permute-start.14 = (bf16[1,176,1024]{2,1,0:T(8,128)(2,1)S(1)}, bf16[1,176,1024]{2,1,0:T(8,128)(2,1)S(1)}, u32[]{:S(2)}, u32[]{:S(2)}) collective-permute-start(bf16[1,176,1024]{2,1,0:T(8,128)(2,1)S(1)} %add_convert_fusion.5.refs_7_), channel_id=1, source_target_pairs={{0,4},{4,0},{8,12},{12,8},{1,5},{5,1},{9,13},{13,9},{2,6},{6,2},{1... | collective-permute-start | bytes 1081352 | tf_op jit(solution)/shard_map/ppermute | solution.py:346
  106.4 2.2 %collective-permute-done.11 = bf16[1,208,1024]{2,1,0:T(8,128)(2,1)S(1)} collective-permute-done((bf16[1,208,1024]{2,1,0:T(8,128)(2,1)S(1)}, bf16[1,208,1024]{2,1,0:T(8,128)(2,1)S(1)}, u32[]{:S(2)}, u32[]{:S(2)}) %collective-permute-start.11) | collective-permute-done | bytes 426016 | tf_op jit(solution)/shard_map/ppermute | solution.py:346
  108.9 4.7 %decode.10 = (bf16[1,112,1024]{2,1,0:T(8,128)(2,1)S(1)}, bf16[1,96,1024]{2,1,0:T(8,128)(2,1)S(1)}, bf16[1,176,1024]{2,1,0:T(8,128)(2,1)S(1)}) custom-call(s32[2]{0:T(128)S(1)} %pad_add_fusion.4.info_ref, bf16[384,1024]{1,0:T(8,128)(2,1)S(1)} %get-tuple-element.38.refs_0_, bf16[384,1024]{1,0:T(8,128)(2,1)S(1)} %get-tuple-element.39.refs_1_, ...), custom_call_target="tpu_custom_call" | custom-call | tf_op jit(solution)/shard_map/decode/pallas_call | solution.py:251
  113.7 2.0 %collective-permute-start.19 = (bf16[1,112,1024]{2,1,0:T(8,128)(2,1)S(1)}, bf16[1,112,1024]{2,1,0:T(8,128)(2,1)S(1)}, u32[]{:S(2)}, u32[]{:S(2)}) collective-permute-start(bf16[1,112,1024]{2,1,0:T(8,128)(2,1)S(1)} %get-tuple-element.46.refs_6_), channel_id=1, source_target_pairs={{0,4},{4,0},{8,12},{12,8},{1,5},{5,1},{9,13},{13,9},{2,6},{6,2},{1... | collective-permute-start | bytes 688136 | tf_op jit(solution)/shard_map/ppermute | solution.py:346
  115.7 2.5 %collective-permute-start.16 = (bf16[1,176,1024]{2,1,0:T(8,128)(2,1)S(1)}, bf16[1,176,1024]{2,1,0:T(8,128)(2,1)S(1)}, u32[]{:S(2)}, u32[]{:S(2)}) collective-permute-start(bf16[1,176,1024]{2,1,0:T(8,128)(2,1)S(1)} %get-tuple-element.52), channel_id=1, source_target_pairs={{0,2},{2,0},{1,3},{3,1},{4,6},{6,4},{5,7},{7,5},{8,10},{10,8},{9,1... | collective-permute-start | bytes 1081352 | tf_op jit(solution)/shard_map/ppermute | solution.py:341
  118.2 2.4 %collective-permute-done.14 = bf16[1,176,1024]{2,1,0:T(8,128)(2,1)S(1)} collective-permute-done((bf16[1,176,1024]{2,1,0:T(8,128)(2,1)S(1)}, bf16[1,176,1024]{2,1,0:T(8,128)(2,1)S(1)}, u32[]{:S(2)}, u32[]{:S(2)}) %collective-permute-start.14) | collective-permute-done | bytes 360480 | tf_op jit(solution)/shard_map/ppermute | solution.py:346
  120.8 3.1 %collective-permute-start.18 = (bf16[1,176,1024]{2,1,0:T(8,128)(2,1)S(1)}, bf16[1,176,1024]{2,1,0:T(8,128)(2,1)S(1)}, u32[]{:S(2)}, u32[]{:S(2)}) collective-permute-start(bf16[1,176,1024]{2,1,0:T(8,128)(2,1)S(1)} %add_convert_fusion.4.refs_8_), channel_id=1, source_target_pairs={{0,8},{4,12},{8,0},{12,4},{1,9},{5,13},{9,1},{13,5},{2,10},{6,14},... | collective-permute-start | bytes 1081352 | tf_op jit(solution)/shard_map/ppermute | solution.py:346
  123.8 4.5 %decode.11 = (f32[1,208,1024]{2,1,0:T(8,128)S(1)}, bf16[1,176,1024]{2,1,0:T(8,128)(2,1)S(1)}) custom-call(s32[2]{0:T(128)S(1)} %pad_add_fusion.2.info_ref, bf16[384,1024]{1,0:T(8,128)(2,1)S(1)} %get-tuple-element.38.refs_0_, bf16[384,1024]{1,0:T(8,128)(2,1)S(1)} %get-tuple-element.39.refs_1_, bf16[384,1024]{1,0:T(8,128)(2,1)S(1)} %collective-permute-done.7.refs_2_, ...), custom_call_target="tpu_custom_call" | custom-call | tf_op jit(solution)/shard_map/decode/pallas_call | solution.py:251
  128.6 1.3 collective-permute-start.15
  130.0 5.1 %collective-permute-done.19 = bf16[1,112,1024]{2,1,0:T(8,128)(2,1)S(1)} collective-permute-done((bf16[1,112,1024]{2,1,0:T(8,128)(2,1)S(1)}, bf16[1,112,1024]{2,1,0:T(8,128)(2,1)S(1)}, u32[]{:S(2)}, u32[]{:S(2)}) %collective-permute-start.19) | collective-permute-done | bytes 229408 | tf_op jit(solution)/shard_map/ppermute | solution.py:346
  135.6 3.4 %collective-permute-done.18 = bf16[1,176,1024]{2,1,0:T(8,128)(2,1)S(1)} collective-permute-done((bf16[1,176,1024]{2,1,0:T(8,128)(2,1)S(1)}, bf16[1,176,1024]{2,1,0:T(8,128)(2,1)S(1)}, u32[]{:S(2)}, u32[]{:S(2)}) %collective-permute-start.18) | collective-permute-done | bytes 360480 | tf_op jit(solution)/shard_map/ppermute | solution.py:346
  139.1 4.5 %collective-permute-done.17 = bf16[1,176,1024]{2,1,0:T(8,128)(2,1)S(1)} collective-permute-done((bf16[1,176,1024]{2,1,0:T(8,128)(2,1)S(1)}, bf16[1,176,1024]{2,1,0:T(8,128)(2,1)S(1)}, u32[]{:S(2)}, u32[]{:S(2)}) %collective-permute-start.17) | collective-permute-done | bytes 360480 | tf_op jit(solution)/shard_map/ppermute | solution.py:346
  143.6 1.6 collective-permute-done.22.refs_5_
  145.2 1.6 %finale.1 = (bf16[384,1024]{1,0:T(8,128)(2,1)}, f32[8,128]{1,0:T(8,128)S(1)}) custom-call(s32[1]{0:T(128)} %bitcast.layer_ref, bf16[1,1024]{1,0:T(2,128)(2,1)S(1)} %copy-done.7, bf16[384,1024]{1,0:T(8,128)(2,1)S(1)} %bitcast.22, f32[176,1024]{1,0:T(8,128)S(1)} %bitcast.23, bf16[176,1024]{1,0:T(8,128)(2,1)S(1)} %bitcast.25, bf16[176,1024]{1,0:T(8,128)(2,1)S(1)} %bitcast.26, ...), custom_call_target="tpu_custom_call" | custom-call | tf_op jit(solution)/shard_map/finale/pallas_call | solution.py:306
  146.8 1.1 collective-permute-start.24
  148.2 2.3 %collective-permute-done.24 = f32[8,128]{1,0:T(8,128)S(1)} collective-permute-done((f32[8,128]{1,0:T(8,128)S(1)}, f32[8,128]{1,0:T(8,128)S(1)}, u32[]{:S(2)}, u32[]{:S(2)}) %collective-permute-start.24) | collective-permute-done | bytes 4128 | tf_op jit(solution)/shard_map/ppermute | solution.py:341
  151.0 4.8 %collective-permute-start.28 = (f32[8,128]{1,0:T(8,128)S(1)}, f32[8,128]{1,0:T(8,128)S(1)}, u32[]{:S(2)}, u32[]{:S(2)}) collective-permute-start(f32[8,128]{1,0:T(8,128)S(1)} %add_add_fusion.refs_0_), channel_id=1, source_target_pairs={{0,12},{4,0},{8,4},{12,8},{1,13},{5,1},{9,5},{13,9},{2,14},{6,2},{... | collective-permute-start | bytes 12296 | tf_op jit(solution)/shard_map/ppermute | solution.py:341
  156.4 0.7 collective-permute-done.28.refs_3_
  157.1 3.2 %collective-permute-done.27.refs_2_ = f32[8,128]{1,0:T(8,128)S(1)} collective-permute-done((f32[8,128]{1,0:T(8,128)S(1)}, f32[8,128]{1,0:T(8,128)S(1)}, u32[]{:S(2)}, u32[]{:S(2)}) %collective-permute-start.27) | collective-permute-done | bytes 4128 | tf_op jit(solution)/shard_map/ppermute | solution.py:341
  160.3 0.9 collective-permute-done.26.refs_1_
  161.8 1.2 mean_ratio.1
  (65 shorter events, 4.9 us)
Async XLA Ops:
  0.6 12.2 %copy-start = (bf16[1,4096]{1,0:T(2,128)(2,1)S(1)}, bf16[1,4096]{1,0:T(2,128)(2,1)}, u32[]{:S(2)}) copy-start(bf16[1,4096]{1,0:T(2,128)(2,1)} %param.10) | copy-start | bytes 24580
  3.4 4.6 %collective-permute-start = (f32[1]{0:T(128)}, f32[1]{0:T(128)}, u32[]{:S(2)}, u32[]{:S(2)}) collective-permute-start(f32[1]{0:T(128)} %get-tuple-element.29), channel_id=1, source_target_pairs={{0,2},{2,0},{1,3},{3,1},{4,6},{6,4},{5,7},{7,5},{8,10},{10,8},{9,1... | collective-permute-start | bytes 20 | tf_op jit(solution)/shard_map/ppermute | solution.py:341
  10.7 23.7 %collective-permute-start.3 = (bf16[112,4096]{1,0:T(8,128)(2,1)}, bf16[112,4096]{1,0:T(8,128)(2,1)}, u32[]{:S(2)}, u32[]{:S(2)}) collective-permute-start(bf16[112,4096]{1,0:T(8,128)(2,1)} %get-tuple-element.35), channel_id=1, source_target_pairs={{0,2},{2,0},{1,3},{3,1},{4,6},{6,4},{5,7},{7,5},{8,10},{10,8},{9,1... | collective-permute-start | bytes 2752520 | tf_op jit(solution)/shard_map/ppermute | solution.py:341
  23.8 12.7 %collective-permute-start.1 = (bf16[384,1024]{1,0:T(8,128)(2,1)}, bf16[384,1024]{1,0:T(8,128)(2,1)S(1)}, u32[]{:S(2)}, u32[]{:S(2)}) collective-permute-start(bf16[384,1024]{1,0:T(8,128)(2,1)} %get-tuple-element.31.refs_0_), channel_id=1, source_target_pairs={{0,1},{2,3},{4,5},{6,7},{8,9},{10,11},{12,13},{14,15},{16,17},{18,... | collective-permute-start | bytes 2359304 | tf_op jit(solution)/shard_map/ppermute | solution.py:408
  25.2 11.4 %collective-permute-start.2 = (bf16[384,1024]{1,0:T(8,128)(2,1)}, bf16[384,1024]{1,0:T(8,128)(2,1)S(1)}, u32[]{:S(2)}, u32[]{:S(2)}) collective-permute-start(bf16[384,1024]{1,0:T(8,128)(2,1)} %get-tuple-element.32.refs_1_), channel_id=1, source_target_pairs={{0,1},{2,3},{4,5},{6,7},{8,9},{10,11},{12,13},{14,15},{16,17},{18,... | collective-permute-start | bytes 2359304 | tf_op jit(solution)/shard_map/ppermute | solution.py:408
  26.5 37.0 %collective-permute-start.5 = (bf16[160,4096]{1,0:T(8,128)(2,1)}, bf16[160,4096]{1,0:T(8,128)(2,1)S(1)}, u32[]{:S(2)}, u32[]{:S(2)}) collective-permute-start(bf16[160,4096]{1,0:T(8,128)(2,1)} %get-tuple-element.36), channel_id=1, source_target_pairs={{0,2},{2,0},{1,3},{3,1},{4,6},{6,4},{5,7},{7,5},{8,10},{10,8},{9,1... | collective-permute-start | bytes 3932168 | tf_op jit(solution)/shard_map/ppermute | solution.py:341
  34.4 29.1 %collective-permute-start.4 = (bf16[112,4096]{1,0:T(8,128)(2,1)}, bf16[112,4096]{1,0:T(8,128)(2,1)}, u32[]{:S(2)}, u32[]{:S(2)}) collective-permute-start(bf16[112,4096]{1,0:T(8,128)(2,1)} %collective-permute-done.3.refs_0_), channel_id=1, source_target_pairs={{0,4},{4,0},{8,12},{12,8},{1,5},{5,1},{9,13},{13,9},{2,6},{6,2},{1... | collective-permute-start | bytes 2752520 | tf_op jit(solution)/shard_map/ppermute | solution.py:346
  44.0 0.9 copy-start.3
  44.9 0.9 copy-start.5
  45.8 0.8 copy-start.8
  46.5 15.8 %collective-permute-start.6 = (bf16[1,208,1024]{2,1,0:T(8,128)(2,1)S(1)}, bf16[1,208,1024]{2,1,0:T(8,128)(2,1)}, u32[]{:S(2)}, u32[]{:S(2)}) collective-permute-start(bf16[1,208,1024]{2,1,0:T(8,128)(2,1)S(1)} %get-tuple-element.33.refs_6_), channel_id=1, source_target_pairs={{0,4},{4,0},{8,12},{12,8},{1,5},{5,1},{9,13},{13,9},{2,6},{6,2},{1... | collective-permute-start | bytes 1277960 | tf_op jit(solution)/shard_map/ppermute | solution.py:346
  63.5 13.5 %copy-start.9 = (bf16[1,208,1024]{2,1,0:T(8,128)(2,1)S(1)}, bf16[1,208,1024]{2,1,0:T(8,128)(2,1)}, u32[]{:S(2)}) copy-start(bf16[1,208,1024]{2,1,0:T(8,128)(2,1)} %copy-done.8) | copy-start | bytes 1277956
  74.3 7.0 %collective-permute-start.7 = (bf16[384,1024]{1,0:T(8,128)(2,1)S(1)}, bf16[384,1024]{1,0:T(8,128)(2,1)S(1)}, u32[]{:S(2)}, u32[]{:S(2)}) collective-permute-start(bf16[384,1024]{1,0:T(8,128)(2,1)S(1)} %get-tuple-element.38.refs_0_), channel_id=1, source_target_pairs={{0,1},{2,3},{4,5},{6,7},{8,9},{10,11},{12,13},{14,15},{16,17},{18,... | collective-permute-start | bytes 2359304 | tf_op jit(solution)/shard_map/ppermute | solution.py:408
  75.6 5.6 %collective-permute-start.8 = (bf16[384,1024]{1,0:T(8,128)(2,1)S(1)}, bf16[384,1024]{1,0:T(8,128)(2,1)S(1)}, u32[]{:S(2)}, u32[]{:S(2)}) collective-permute-start(bf16[384,1024]{1,0:T(8,128)(2,1)S(1)} %get-tuple-element.39.refs_1_), channel_id=1, source_target_pairs={{0,1},{2,3},{4,5},{6,7},{8,9},{10,11},{12,13},{14,15},{16,17},{18,... | collective-permute-start | bytes 2359304 | tf_op jit(solution)/shard_map/ppermute | solution.py:408
  77.0 18.3 %collective-permute-start.9 = (bf16[1,208,1024]{2,1,0:T(8,128)(2,1)S(1)}, bf16[1,208,1024]{2,1,0:T(8,128)(2,1)S(1)}, u32[]{:S(2)}, u32[]{:S(2)}) collective-permute-start(bf16[1,208,1024]{2,1,0:T(8,128)(2,1)S(1)} %copy-done.9), channel_id=1, source_target_pairs={{0,4},{4,0},{8,12},{12,8},{1,5},{5,1},{9,13},{13,9},{2,6},{6,2},{1... | collective-permute-start | bytes 1277960 | tf_op jit(solution)/shard_map/ppermute | solution.py:346
  78.6 17.0 %collective-permute-start.10 = (bf16[1,208,1024]{2,1,0:T(8,128)(2,1)S(1)}, bf16[1,208,1024]{2,1,0:T(8,128)(2,1)S(1)}, u32[]{:S(2)}, u32[]{:S(2)}) collective-permute-start(bf16[1,208,1024]{2,1,0:T(8,128)(2,1)S(1)} %add_convert_fusion.2.refs_4_), channel_id=1, source_target_pairs={{0,8},{4,12},{8,0},{12,4},{1,9},{5,13},{9,1},{13,5},{2,10},{6,14},... | collective-permute-start | bytes 1277960 | tf_op jit(solution)/shard_map/ppermute | solution.py:346
  85.8 16.9 %collective-permute-start.12 = (bf16[1,176,1024]{2,1,0:T(8,128)(2,1)S(1)}, bf16[1,176,1024]{2,1,0:T(8,128)(2,1)S(1)}, u32[]{:S(2)}, u32[]{:S(2)}) collective-permute-start(bf16[1,176,1024]{2,1,0:T(8,128)(2,1)S(1)} %get-tuple-element.45), channel_id=1, source_target_pairs={{0,2},{2,0},{1,3},{3,1},{4,6},{6,4},{5,7},{7,5},{8,10},{10,8},{9,1... | collective-permute-start | bytes 1081352 | tf_op jit(solution)/shard_map/ppermute | solution.py:341
  87.4 21.2 %collective-permute-start.11 = (bf16[1,208,1024]{2,1,0:T(8,128)(2,1)S(1)}, bf16[1,208,1024]{2,1,0:T(8,128)(2,1)S(1)}, u32[]{:S(2)}, u32[]{:S(2)}) collective-permute-start(bf16[1,208,1024]{2,1,0:T(8,128)(2,1)S(1)} %get-tuple-element.40.refs_6_), channel_id=1, source_target_pairs={{0,4},{4,0},{8,12},{12,8},{1,5},{5,1},{9,13},{13,9},{2,6},{6,2},{1... | collective-permute-start | bytes 1277960 | tf_op jit(solution)/shard_map/ppermute | solution.py:346
  95.8 6.9 %copy-start.6 = (f32[1,176,1024]{2,1,0:T(8,128)S(1)}, f32[1,176,1024]{2,1,0:T(8,128)}, u32[]{:S(2)}) copy-start(f32[1,176,1024]{2,1,0:T(8,128)} %copy-done.5) | copy-start | bytes 2162692
  100.3 15.4 %collective-permute-start.13 = (bf16[1,176,1024]{2,1,0:T(8,128)(2,1)S(1)}, bf16[1,176,1024]{2,1,0:T(8,128)(2,1)S(1)}, u32[]{:S(2)}, u32[]{:S(2)}) collective-permute-start(bf16[1,176,1024]{2,1,0:T(8,128)(2,1)S(1)} %get-tuple-element.49), channel_id=1, source_target_pairs={{0,2},{2,0},{1,3},{3,1},{4,6},{6,4},{5,7},{7,5},{8,10},{10,8},{9,1... | collective-permute-start | bytes 1081352 | tf_op jit(solution)/shard_map/ppermute | solution.py:341
  102.8 17.8 %collective-permute-start.14 = (bf16[1,176,1024]{2,1,0:T(8,128)(2,1)S(1)}, bf16[1,176,1024]{2,1,0:T(8,128)(2,1)S(1)}, u32[]{:S(2)}, u32[]{:S(2)}) collective-permute-start(bf16[1,176,1024]{2,1,0:T(8,128)(2,1)S(1)} %add_convert_fusion.5.refs_7_), channel_id=1, source_target_pairs={{0,4},{4,0},{8,12},{12,8},{1,5},{5,1},{9,13},{13,9},{2,6},{6,2},{1... | collective-permute-start | bytes 1081352 | tf_op jit(solution)/shard_map/ppermute | solution.py:346
  108.7 26.4 %collective-permute-start.21 = (bf16[1,208,1024]{2,1,0:T(8,128)(2,1)S(1)}, bf16[1,208,1024]{2,1,0:T(8,128)(2,1)S(1)}, u32[]{:S(2)}, u32[]{:S(2)}) collective-permute-start(bf16[1,208,1024]{2,1,0:T(8,128)(2,1)S(1)} %add_convert_fusion.1.refs_6_), channel_id=1, source_target_pairs={{0,8},{4,12},{8,0},{12,4},{1,9},{5,13},{9,1},{13,5},{2,10},{6,14},... | collective-permute-start | bytes 1277960 | tf_op jit(solution)/shard_map/ppermute | solution.py:346
  113.6 15.0 %collective-permute-start.20 = (bf16[1,96,1024]{2,1,0:T(8,128)(2,1)S(1)}, bf16[1,96,1024]{2,1,0:T(8,128)(2,1)S(1)}, u32[]{:S(2)}, u32[]{:S(2)}) collective-permute-start(bf16[1,96,1024]{2,1,0:T(8,128)(2,1)S(1)} %get-tuple-element.47.refs_7_), channel_id=1, source_target_pairs={{0,4},{4,0},{8,12},{12,8},{1,5},{5,1},{9,13},{13,9},{2,6},{6,2},{1... | collective-permute-start | bytes 589832 | tf_op jit(solution)/shard_map/ppermute | solution.py:346
  113.7 21.4 %collective-permute-start.19 = (bf16[1,112,1024]{2,1,0:T(8,128)(2,1)S(1)}, bf16[1,112,1024]{2,1,0:T(8,128)(2,1)S(1)}, u32[]{:S(2)}, u32[]{:S(2)}) collective-permute-start(bf16[1,112,1024]{2,1,0:T(8,128)(2,1)S(1)} %get-tuple-element.46.refs_6_), channel_id=1, source_target_pairs={{0,4},{4,0},{8,12},{12,8},{1,5},{5,1},{9,13},{13,9},{2,6},{6,2},{1... | collective-permute-start | bytes 688136 | tf_op jit(solution)/shard_map/ppermute | solution.py:346
  115.7 19.6 %collective-permute-start.16 = (bf16[1,176,1024]{2,1,0:T(8,128)(2,1)S(1)}, bf16[1,176,1024]{2,1,0:T(8,128)(2,1)S(1)}, u32[]{:S(2)}, u32[]{:S(2)}) collective-permute-start(bf16[1,176,1024]{2,1,0:T(8,128)(2,1)S(1)} %get-tuple-element.52), channel_id=1, source_target_pairs={{0,2},{2,0},{1,3},{3,1},{4,6},{6,4},{5,7},{7,5},{8,10},{10,8},{9,1... | collective-permute-start | bytes 1081352 | tf_op jit(solution)/shard_map/ppermute | solution.py:341
  120.8 14.6 %copy-start.4 = (f32[1,176,1024]{2,1,0:T(8,128)S(1)}, f32[1,176,1024]{2,1,0:T(8,128)}, u32[]{:S(2)}) copy-start(f32[1,176,1024]{2,1,0:T(8,128)} %copy-done.3) | copy-start | bytes 2162692
  120.8 18.2 %collective-permute-start.18 = (bf16[1,176,1024]{2,1,0:T(8,128)(2,1)S(1)}, bf16[1,176,1024]{2,1,0:T(8,128)(2,1)S(1)}, u32[]{:S(2)}, u32[]{:S(2)}) collective-permute-start(bf16[1,176,1024]{2,1,0:T(8,128)(2,1)S(1)} %add_convert_fusion.4.refs_8_), channel_id=1, source_target_pairs={{0,8},{4,12},{8,0},{12,4},{1,9},{5,13},{9,1},{13,5},{2,10},{6,14},... | collective-permute-start | bytes 1081352 | tf_op jit(solution)/shard_map/ppermute | solution.py:346
  128.3 16.9 %copy-start.2 = (bf16[1,384,1024]{2,1,0:T(8,128)(2,1)S(1)}, bf16[1,384,1024]{2,1,0:T(8,128)(2,1)}, u32[]{:S(2)}) copy-start(bf16[1,384,1024]{2,1,0:T(8,128)(2,1)} %param.8) | copy-start | bytes 2359300
  128.3 16.9 %copy-start.7 = (bf16[1,1024]{1,0:T(2,128)(2,1)S(1)}, bf16[1,1024]{1,0:T(2,128)(2,1)}, u32[]{:S(2)}) copy-start(bf16[1,1024]{1,0:T(2,128)(2,1)} %b_ref.1) | copy-start | bytes 6148
  128.6 10.5 %collective-permute-start.15 = (bf16[1,176,1024]{2,1,0:T(8,128)(2,1)S(1)}, bf16[1,176,1024]{2,1,0:T(8,128)(2,1)S(1)}, u32[]{:S(2)}, u32[]{:S(2)}) collective-permute-start(bf16[1,176,1024]{2,1,0:T(8,128)(2,1)S(1)} %get-tuple-element.50), channel_id=1, source_target_pairs={{0,2},{2,0},{1,3},{3,1},{4,6},{6,4},{5,7},{7,5},{8,10},{10,8},{9,1... | collective-permute-start | bytes 1081352 | tf_op jit(solution)/shard_map/ppermute | solution.py:341
  135.1 27.9 %copy-start.1 = (bf16[1,4096]{1,0:T(2,128)(2,1)S(1)}, bf16[1,4096]{1,0:T(2,128)(2,1)}, u32[]{:S(2)}) copy-start(bf16[1,4096]{1,0:T(2,128)(2,1)} %param.10) | copy-start | bytes 24580
  135.3 9.9 %collective-permute-start.22 = (bf16[208,1024]{1,0:T(8,128)(2,1)S(1)}, bf16[208,1024]{1,0:T(8,128)(2,1)S(1)}, u32[]{:S(2)}, u32[]{:S(2)}) collective-permute-start(bf16[208,1024]{1,0:T(8,128)(2,1)S(1)} %fusion), channel_id=1, source_target_pairs={{0,2},{2,0},{1,3},{3,1},{4,6},{6,4},{5,7},{7,5},{8,10},{10,8},{9,1... | collective-permute-start | bytes 1277960 | tf_op jit(solution)/shard_map/ppermute | solution.py:341
  135.4 8.2 %collective-permute-start.17 = (bf16[1,176,1024]{2,1,0:T(8,128)(2,1)S(1)}, bf16[1,176,1024]{2,1,0:T(8,128)(2,1)S(1)}, u32[]{:S(2)}, u32[]{:S(2)}) collective-permute-start(bf16[1,176,1024]{2,1,0:T(8,128)(2,1)S(1)} %add_convert_fusion.3), channel_id=1, source_target_pairs={{0,4},{4,0},{8,12},{12,8},{1,5},{5,1},{9,13},{13,9},{2,6},{6,2},{1... | collective-permute-start | bytes 1081352 | tf_op jit(solution)/shard_map/ppermute | solution.py:346
  146.8 1.3 collective-permute-start.25
  146.8 3.6 %collective-permute-start.24 = (f32[8,128]{1,0:T(8,128)S(1)}, f32[8,128]{1,0:T(8,128)S(1)}, u32[]{:S(2)}, u32[]{:S(2)}) collective-permute-start(f32[8,128]{1,0:T(8,128)S(1)} %get-tuple-element.55), channel_id=1, source_target_pairs={{0,2},{1,3},{2,0},{3,1},{4,6},{5,7},{6,4},{7,5},{8,10},{9,11},{10,... | collective-permute-start | bytes 12296 | tf_op jit(solution)/shard_map/ppermute | solution.py:341
  147.9 3.0 %collective-permute-start.23 = (f32[8,128]{1,0:T(8,128)S(1)}, f32[8,128]{1,0:T(8,128)S(1)}, u32[]{:S(2)}, u32[]{:S(2)}) collective-permute-start(f32[8,128]{1,0:T(8,128)S(1)} %get-tuple-element.55), channel_id=1, source_target_pairs={{0,1},{1,2},{2,3},{3,0},{4,5},{5,6},{6,7},{7,4},{8,9},{9,10},{10,1... | collective-permute-start | bytes 12296 | tf_op jit(solution)/shard_map/ppermute | solution.py:341
  151.0 10.2 %copy-start.10 = (f32[8,128]{1,0:T(8,128)}, f32[8,128]{1,0:T(8,128)S(1)}, u32[]{:S(2)}) copy-start(f32[8,128]{1,0:T(8,128)S(1)} %add_add_fusion.refs_0_) | copy-start | bytes 12292
  151.0 6.1 %collective-permute-start.28 = (f32[8,128]{1,0:T(8,128)S(1)}, f32[8,128]{1,0:T(8,128)S(1)}, u32[]{:S(2)}, u32[]{:S(2)}) collective-permute-start(f32[8,128]{1,0:T(8,128)S(1)} %add_add_fusion.refs_0_), channel_id=1, source_target_pairs={{0,12},{4,0},{8,4},{12,8},{1,13},{5,1},{9,5},{13,9},{2,14},{6,2},{... | collective-permute-start | bytes 12296 | tf_op jit(solution)/shard_map/ppermute | solution.py:341
  155.8 4.5 %collective-permute-start.27 = (f32[8,128]{1,0:T(8,128)S(1)}, f32[8,128]{1,0:T(8,128)S(1)}, u32[]{:S(2)}, u32[]{:S(2)}) collective-permute-start(f32[8,128]{1,0:T(8,128)S(1)} %add_add_fusion.refs_0_), channel_id=1, source_target_pairs={{0,8},{4,12},{8,0},{12,4},{1,9},{5,13},{9,1},{13,5},{2,10},{6,14},... | collective-permute-start | bytes 12296 | tf_op jit(solution)/shard_map/ppermute | solution.py:341
  155.8 5.4 %collective-permute-start.26 = (f32[8,128]{1,0:T(8,128)S(1)}, f32[8,128]{1,0:T(8,128)S(1)}, u32[]{:S(2)}, u32[]{:S(2)}) collective-permute-start(f32[8,128]{1,0:T(8,128)S(1)} %add_add_fusion.refs_0_), channel_id=1, source_target_pairs={{0,4},{4,8},{8,12},{12,0},{1,5},{5,9},{9,13},{13,1},{2,6},{6,10},{... | collective-permute-start | bytes 12296 | tf_op jit(solution)/shard_map/ppermute | solution.py:341
  157.1 4.1 %copy-start.11 = (f32[8,128]{1,0:T(8,128)}, f32[8,128]{1,0:T(8,128)S(1)}, u32[]{:S(2)}) copy-start(f32[8,128]{1,0:T(8,128)S(1)} %collective-permute-done.28.refs_3_) | copy-start | bytes 12292
  160.3 0.9 copy-start.12
  161.2 0.6 copy-start.13

commit v13 on v11

--- a/solution.py
+++ b/solution.py
@@ -18,13 +18,16 @@
     return tile
 
 
-def square_sum(x):
+def square_sum(x, side, edge):
     rows, width = x.shape
     lanes = tile_of(width, 1024)
     loads = 4
     piece = rows // loads
 
-    def body(x_ref, o_ref, held, sem):
+    def body(side_ref, x_ref, o_ref, held, outer_ref, sem, out_sem):
+        start = pl.multiple_of(side_ref[0] * (rows - edge), 16)
+        store = pltpu.make_async_copy(held.at[pl.ds(start, edge)], outer_ref, out_sem)
+
         def load(i):
             place = pl.ds(i * piece, piece)
             return pltpu.make_async_copy(x_ref.at[place], held.at[place], sem.at[i])
@@ -42,49 +45,49 @@
                     return acc + value[:8] + value[8:]
 
                 total = lax.fori_loop(0, piece // 16, add, total, unroll=2)
+        store.start()
         o_ref[0] = jnp.sum(total)
-
-    return pl.pallas_call(
-        body,
-        in_specs=[pl.BlockSpec(memory_space=pl.ANY)],
-        out_specs=[pl.BlockSpec(memory_space=pltpu.SMEM), pl.BlockSpec(memory_space=pltpu.VMEM)],
-        out_shape=[jax.ShapeDtypeStruct((1,), jnp.float32), pltpu.VMEM((rows, width), x.dtype)],
-        scratch_shapes=[pltpu.SemaphoreType.DMA((loads,))],
+        store.wait()
+
+    return pl.pallas_call(
+        body,
+        in_specs=[pl.BlockSpec(memory_space=pltpu.SMEM), pl.BlockSpec(memory_space=pl.ANY)],
+        out_specs=[
+            pl.BlockSpec(memory_space=pltpu.SMEM),
+            pl.BlockSpec(memory_space=pltpu.VMEM),
+            pl.BlockSpec(memory_space=pl.ANY),
+        ],
+        out_shape=[
+            jax.ShapeDtypeStruct((1,), jnp.float32),
+            pltpu.VMEM((rows, width), x.dtype),
+            pltpu.HBM((edge, width), x.dtype),
+        ],
+        scratch_shapes=[pltpu.SemaphoreType.DMA((loads,)), pltpu.SemaphoreType.DMA],
         compiler_params=pltpu.CompilerParams(vmem_limit_bytes=VMEM_LIMIT),
         cost_estimate=COST,
         name="square_sum",
-    )(x)
-
-
-def cut(x, side, edge, after):
+    )(side.reshape(1), x)
+
+
+def cut(x, edge, after):
     rows, width = x.shape
     middle = rows - 2 * edge
 
-    def body(side_ref, after_ref, x_ref, outer_ref, inner_ref, sem):
-        start = pl.multiple_of(side_ref[0] * (rows - edge), 16)
-        copies = [
-            pltpu.make_async_copy(x_ref.at[pl.ds(start, edge)], outer_ref, sem.at[0]),
-            pltpu.make_async_copy(x_ref.at[pl.ds(edge, middle)], inner_ref, sem.at[1]),
-        ]
-        for copy in copies:
-            copy.start()
-        for copy in copies:
-            copy.wait()
-
-    return pl.pallas_call(
-        body,
-        in_specs=[
-            pl.BlockSpec(memory_space=pltpu.SMEM),
-            pl.BlockSpec(memory_space=pltpu.SMEM),
-            pl.BlockSpec(memory_space=pltpu.VMEM),
-        ],
-        out_specs=[pl.BlockSpec(memory_space=pl.ANY)] * 2,
-        out_shape=[pltpu.HBM((edge, width), x.dtype), pltpu.HBM((middle, width), x.dtype)],
-        scratch_shapes=[pltpu.SemaphoreType.DMA((2,))],
+    def body(x_ref, after_ref, inner_ref, sem):
+        copy = pltpu.make_async_copy(x_ref.at[pl.ds(edge, middle)], inner_ref, sem)
+        copy.start()
+        copy.wait()
+
+    return pl.pallas_call(
+        body,
+        in_specs=[pl.BlockSpec(memory_space=pltpu.VMEM), pl.BlockSpec(memory_space=pl.ANY)],
+        out_specs=pl.BlockSpec(memory_space=pl.ANY),
+        out_shape=pltpu.HBM((middle, width), x.dtype),
+        scratch_shapes=[pltpu.SemaphoreType.DMA],
         compiler_params=pltpu.CompilerParams(vmem_limit_bytes=VMEM_LIMIT),
         cost_estimate=COST,
         name="cut",
-    )(side.reshape(1), after, pltpu.with_memory_space_constraint(x, pltpu.VMEM))
+    )(pltpu.with_memory_space_constraint(x, pltpu.VMEM), after)
 
 
 def ring_loop(count, slots, start, step):
@@ -110,6 +113,8 @@
     part = latents // parts
     tile = tile_of(part, ENCODE_TILE)
     n, m = len(pieces), len(also)
+    raw = inv is None
+    inv = jnp.ones((1,), jnp.float32) if raw else inv
 
     def body(places_ref, inv_ref, b_ref, *refs):
         x_refs, w_ref = refs[:n], refs[n]
@@ -139,8 +144,9 @@
 
             tile_copy(t, slot).wait()
             value = jnp.dot(lhs[...], ring[slot], preferred_element_type=jnp.float32)
-            value = value * inv_ref[0] + b_ref[:, columns(t)].astype(jnp.float32)
-            value = jnp.maximum(value, 0.0).astype(jnp.bfloat16)
+            if not raw:
+                value = value * inv_ref[0] + b_ref[:, columns(t)].astype(jnp.float32)
+                value = jnp.maximum(value, 0.0).astype(jnp.bfloat16)
             per = part // tile
             for i, o_ref in enumerate(o_refs):
                 @pl.when(lax.div(t, per) == i)
@@ -157,7 +163,7 @@
             pl.BlockSpec(memory_space=pltpu.VMEM),
         ] + [pl.BlockSpec(memory_space=pl.ANY)] * (n + 1 + m),
         out_specs=[pl.BlockSpec(memory_space=pltpu.VMEM)] * parts,
-        out_shape=[jax.ShapeDtypeStruct((rows, part), jnp.bfloat16)] * parts,
+        out_shape=[jax.ShapeDtypeStruct((rows, part), jnp.float32 if raw else jnp.bfloat16)] * parts,
         scratch_shapes=[
             pltpu.VMEM((rows, width), jnp.bfloat16),
             pltpu.VMEM((ENCODE_SLOTS, width, tile), jnp.bfloat16),
@@ -168,6 +174,35 @@
         cost_estimate=COST,
         name="encode",
     )(places, inv, bias, *[piece[0] for piece in pieces], weight, *also)
+
+
+def activate(products, inv, bias):
+    n = len(products)
+    rows, part = products[0].shape
+
+    def body(inv_ref, b_ref, *refs):
+        for i in range(n):
+            p_ref, o_ref = refs[i], refs[n + i]
+            bias = b_ref[:, i * part:(i + 1) * part].astype(jnp.float32)
+
+            def block(r, carry):
+                here = pl.ds(pl.multiple_of(r * 16, 16), 16)
+                value = p_ref[here, :] * inv_ref[0] + bias
+                o_ref[here, :] = jnp.maximum(value, 0.0).astype(o_ref.dtype)
+                return carry
+
+            lax.fori_loop(0, rows // 16, block, 0, unroll=2)
+
+    vmem = pl.BlockSpec(memory_space=pltpu.VMEM)
+    return pl.pallas_call(
+        body,
+        in_specs=[pl.BlockSpec(memory_space=pltpu.SMEM)] + [vmem] * (1 + n),
+        out_specs=[vmem] * n,
+        out_shape=[jax.ShapeDtypeStruct((rows, part), jnp.bfloat16)] * n,
+        compiler_params=pltpu.CompilerParams(vmem_limit_bytes=VMEM_LIMIT),
+        cost_estimate=COST,
+        name="activate",
+    )(inv, bias, *products)
 
 
 def decode(codes, earlier, own_w, cross_w, info, outs, width, also):
@@ -376,17 +411,10 @@
     side = lat % 2
 
     edge = rows * 7 // 24 // 16 * 16
-    square, x_held = square_sum(x_own)
+    square, x_held, outer = square_sum(x_own, side.astype(jnp.int32), edge)
     square = sum_over(square, "token")
     scale = jnp.sqrt(square / (rows * n_tok * model) + 1e-06)
     inv = 1.0 / scale
-    outer, inner = cut(x_held, side.astype(jnp.int32), edge, inv)
-    foreign = []
-    for distance in range(1, n_tok):
-        mine = shifted(outer, "token", distance)
-        theirs = swapped(mine, "latent", 1)
-        foreign.append((n_tok - distance, mine, theirs, shifted(inner, "token", distance)))
-
     bias = lax.dynamic_slice_in_dim(
         encoder_layer_bias, lax.axis_index("token") * lat_dev, lat_dev, axis=1
     )
@@ -424,7 +452,13 @@
             bit *= 2
         return total[0]
 
-    codes = encode([(x_held, 0, rows)], places(0), inv, enc_w, bias, 2, [])
+    codes = activate(encode([(x_held, 0, rows)], places(0), None, enc_w, bias, 2, []), inv, bias)
+    inner = cut(x_held, edge, codes[0])
+    foreign = []
+    for distance in range(1, n_tok):
+        mine = shifted(outer, "token", distance)
+        theirs = swapped(mine, "latent", 1)
+        foreign.append((n_tok - distance, mine, theirs, shifted(inner, "token", distance)))
     earlier = earlier_of(codes)
     inside = ((first, middle),)
     outside = ((0, first), (last, rows - last))

time: 162 us -> 175 us (1.080)
  starting transfers between devices: 34.1 us -> 41.7 us
  waiting for transfers between devices: 58.1 us -> 61.4 us
  Pallas kernels: 61.7 us -> 64.6 us
    ppermute x3, starting transfers between devices: 4.07 us -> 8.56 us  [earlier_of(): return [lax.ppermute(part, 'layer', [(0, 1)]) for part in codes]]
    ppermute x11, waiting for transfers between devices: 33.4 us -> 36.1 us  [swapped(): return lax.ppermute(value, axis, [(i, i ^ bit) for i in range(n)])]
    ppermute x14, starting transfers between devices: 15.7 us -> 18 us  [shifted(): lax.ppermute(value, axis, [(i, (i + distance) % n) for i in range(n)])]
    pallas_call x2 -> x3, Pallas kernels: 4.11 us -> 6.33 us  [the longest x1 3.56 us: square_sum(): pl.pallas_call(body, in_specs=[pl.BlockSpec(memory_space=pltpu.SMEM), pl....]
    pallas_call x6, Pallas kernels: 33 us -> 35 us  [decode(): pl.pallas_call(body, in_specs=[pl.BlockSpec(memory_space=pltpu.SMEM)] + [...]
  transfers between devices with their start and end apart: 28 -> 28, of which waited for: 16 -> 15; matrix products, arithmetic and copies ran while one was open for 1% -> 1% of each run, Pallas kernels for 27% -> 27%
where the time goes in v13:
time: 175 us
  Pallas kernels  64.6 us (37%)
  waiting for transfers between devices  61.4 us (35%)
  starting transfers between devices  41.7 us (24%)
  other arithmetic  2.34 us (1%)
  local copies, waits for them, and re-layouts  2.29 us (1%)
  between operations  2.15 us (1%)
    ppermute x11, waiting for transfers between devices, swapped(): return lax.ppermute(value, axis, [(i, i ^ bit) for i in range(n)])  36.1 us
    pallas_call x6, Pallas kernels, decode(): pl.pallas_call(body, in_specs=[pl.BlockSpec(memory_space=pltpu.SMEM)] + [...  35 us
    ppermute x14, waiting for transfers between devices, shifted(): lax.ppermute(value, axis, [(i, (i + distance) % n) for i in range(n)])  25.3 us
    pallas_call x2, Pallas kernels, encode(): pl.pallas_call(body, in_specs=[pl.BlockSpec(memory_space=pltpu.SMEM), pl....  20.4 us
    ppermute x14, starting transfers between devices, shifted(): lax.ppermute(value, axis, [(i, (i + distance) % n) for i in range(n)])  18 us
    ppermute x11, starting transfers between devices, swapped(): return lax.ppermute(value, axis, [(i, i ^ bit) for i in range(n)])  15.2 us
    ppermute x3, starting transfers between devices, earlier_of(): return [lax.ppermute(part, 'layer', [(0, 1)]) for part in codes]  8.56 us
    pallas_call x1, Pallas kernels, square_sum(): pl.pallas_call(body, in_specs=[pl.BlockSpec(memory_space=pltpu.SMEM), pl....  3.56 us
  transfers between devices with their start and end apart: 28, of which 15 were waited for; matrix products, arithmetic and copies ran while one was open for 1% of the time, Pallas kernels for 27%

profile of v13, /device:TPU:0, one launch (start us, length us, event | category | flops | bytes accessed | tf_op | source)
XLA Modules:
  0.0 174.6 jit_solution(778934633212109814)
XLA Ops:
  0.7 3.6 %square_sum.1 = (f32[1]{0:T(128)}, bf16[384,4096]{1,0:T(8,128)(2,1)S(1)}, bf16[112,4096]{1,0:T(8,128)(2,1)}) custom-call(s32[1]{0:T(128)} %bitcast.4.side_ref, bf16[384,4096]{1,0:T(8,128)(2,1)} %bitcast.35), custom_call_target="tpu_custom_call" | custom-call | tf_op jit(solution)/shard_map/square_sum/pallas_call | solution.py:52
  4.2 3.0 %collective-permute-start.3 = (bf16[112,4096]{1,0:T(8,128)(2,1)}, bf16[112,4096]{1,0:T(8,128)(2,1)}, u32[]{:S(2)}, u32[]{:S(2)}) collective-permute-start(bf16[112,4096]{1,0:T(8,128)(2,1)} %get-tuple-element.36), channel_id=1, source_target_pairs={{0,2},{2,0},{1,3},{3,1},{4,6},{6,4},{5,7},{7,5},{8,10},{10,8},{9,1... | collective-permute-start | bytes 2752520 | tf_op jit(solution)/shard_map/ppermute | solution.py:376
  7.3 9.8 %encode.2 = (f32[384,1024]{1,0:T(8,128)S(1)}, f32[384,1024]{1,0:T(8,128)S(1)}) custom-call(s32[1]{0:T(128)} %constant.62.clone.1.places_ref, f32[1]{0:T(128)} %constant.63.clone.1.inv_ref, bf16[1,2048]{1,0:T(2,128)(2,1)S(1)} %constant_dynamic-slice_fusion.b_ref, bf16[384,4096]{1,0:T(8,128)(2,1)S(1)} %get-tuple-element.29.refs_0_.x_ref, ...), custom_call_target="tpu_custom_call" | custom-call | tf_op jit(solution)/shard_map/encode/pallas_call | solution.py:158
  17.2 10.8 %collective-permute-done = f32[1]{0:T(128)} collective-permute-done((f32[1]{0:T(128)}, f32[1]{0:T(128)}, u32[]{:S(2)}, u32[]{:S(2)}) %collective-permute-start) | collective-permute-done | bytes 36 | tf_op jit(solution)/shard_map/ppermute | solution.py:376
  29.2 1.7 activate.1
  30.9 2.2 %collective-permute-start.2 = (bf16[384,1024]{1,0:T(8,128)(2,1)}, bf16[384,1024]{1,0:T(8,128)(2,1)}, u32[]{:S(2)}, u32[]{:S(2)}) collective-permute-start(bf16[384,1024]{1,0:T(8,128)(2,1)} %get-tuple-element.33.refs_1_), channel_id=1, source_target_pairs={{0,1},{2,3},{4,5},{6,7},{8,9},{10,11},{12,13},{14,15},{16,17},{18,... | collective-permute-start | bytes 2359304 | tf_op jit(solution)/shard_map/ppermute | solution.py:436
  33.1 2.2 %collective-permute-start.1 = (bf16[384,1024]{1,0:T(8,128)(2,1)}, bf16[384,1024]{1,0:T(8,128)(2,1)}, u32[]{:S(2)}, u32[]{:S(2)}) collective-permute-start(bf16[384,1024]{1,0:T(8,128)(2,1)} %get-tuple-element.32.refs_0_.after_ref), channel_id=1, source_target_pairs={{0,1},{2,3},{4,5},{6,7},{8,9},{10,11},{12,13},{14,15},{16,17},{18,... | collective-permute-start | bytes 2359304 | tf_op jit(solution)/shard_map/ppermute | solution.py:436
  35.2 1.1 cut.1
  36.3 1.8 %collective-permute-start.5 = (bf16[160,4096]{1,0:T(8,128)(2,1)}, bf16[160,4096]{1,0:T(8,128)(2,1)S(1)}, u32[]{:S(2)}, u32[]{:S(2)}) collective-permute-start(bf16[160,4096]{1,0:T(8,128)(2,1)} %cut.1), channel_id=1, source_target_pairs={{0,2},{2,0},{1,3},{3,1},{4,6},{6,4},{5,7},{7,5},{8,10},{10,8},{9,1... | collective-permute-start | bytes 3932168 | tf_op jit(solution)/shard_map/ppermute | solution.py:376
  38.1 1.6 collective-permute-start.4
  39.8 8.4 %decode.6 = (bf16[1,208,1024]{2,1,0:T(8,128)(2,1)S(1)}, bf16[1,208,1024]{2,1,0:T(8,128)(2,1)S(1)}, f32[1,176,1024]{2,1,0:T(8,128)S(1)}, f32[1,176,1024]{2,1,0:T(8,128)S(1)}) custom-call(s32[3]{0:T(128)S(1)} %get-tuple-element.55.info_ref, bf16[384,1024]{1,0:T(8,128)(2,1)} %get-tuple-element.32.refs_0_.after_ref, ...), custom_call_target="tpu_custom_call" | custom-call | tf_op jit(solution)/shard_map/decode/pallas_call | solution.py:286
  48.2 0.9 copy-done.3
  50.4 8.4 %decode.7 = (f32[1,208,1024]{2,1,0:T(8,128)S(1)}, f32[1,208,1024]{2,1,0:T(8,128)S(1)}, f32[1,176,1024]{2,1,0:T(8,128)S(1)}, f32[1,176,1024]{2,1,0:T(8,128)S(1)}) custom-call(s32[3]{0:T(128)S(1)} %get-tuple-element.54.info_ref, bf16[384,1024]{1,0:T(8,128)(2,1)} %get-tuple-element.32.refs_0_.after_ref, bf16[384,1024]{1,0:T(8,128)(2,1)} %get-tuple-element.33.refs_1_, ...), custom_call_target="tpu_custom_call" | custom-call | tf_op jit(solution)/shard_map/decode/pallas_call | solution.py:286
  58.8 7.9 %collective-permute-done.6 = bf16[1,208,1024]{2,1,0:T(8,128)(2,1)} collective-permute-done((bf16[1,208,1024]{2,1,0:T(8,128)(2,1)S(1)}, bf16[1,208,1024]{2,1,0:T(8,128)(2,1)}, u32[]{:S(2)}, u32[]{:S(2)}) %collective-permute-start.6) | collective-permute-done | bytes 426016 | tf_op jit(solution)/shard_map/ppermute | solution.py:381
  66.7 1.1 add_convert_fusion.2.refs_4_
  67.8 10.5 %encode.3.refs_0_ = bf16[384,2048]{1,0:T(8,128)(2,1)S(1)} custom-call(s32[3]{0:T(128)S(1)} %pad_add_fusion.3.places_ref, f32[1]{0:T(128)S(6)} %sqrt.3.inv_ref, bf16[1,2048]{1,0:T(2,128)(2,1)S(1)} %constant_dynamic-slice_fusion.b_ref, bf16[112,4096]{1,0:T(8,128)(2,1)} %collective-permute-done.3.refs_0_, bf16[112,4096]{1,0:T(8,128)(2,1)S(1)} %collective-permute-done.4.refs_1_, ...), custom_call_target="tpu_custom_call" | custom-call | tf_op jit(solution)/shard_map/encode/pallas_call | solution.py:158
  78.4 4.2 %collective-permute-start.7 = (bf16[384,2048]{1,0:T(8,128)(2,1)S(1)}, bf16[384,2048]{1,0:T(8,128)(2,1)S(1)}, u32[]{:S(2)}, u32[]{:S(2)}) collective-permute-start(bf16[384,2048]{1,0:T(8,128)(2,1)S(1)} %encode.3.refs_0_), channel_id=1, source_target_pairs={{0,1},{2,3},{4,5},{6,7},{8,9},{10,11},{12,13},{14,15},{16,17},{18,... | collective-permute-start | bytes 4718600 | tf_op jit(solution)/shard_map/ppermute | solution.py:436
  83.0 2.8 %collective-permute-start.9 = (bf16[1,208,1024]{2,1,0:T(8,128)(2,1)S(1)}, bf16[1,208,1024]{2,1,0:T(8,128)(2,1)S(1)}, u32[]{:S(2)}, u32[]{:S(2)}) collective-permute-start(bf16[1,208,1024]{2,1,0:T(8,128)(2,1)S(1)} %add_convert_fusion.2.refs_4_), channel_id=1, source_target_pairs={{0,8},{4,12},{8,0},{12,4},{1,9},{5,13},{9,1},{13,5},{2,10},{6,14},... | collective-permute-start | bytes 1277960 | tf_op jit(solution)/shard_map/ppermute | solution.py:381
  85.8 4.5 %decode.8 = (bf16[1,208,1024]{2,1,0:T(8,128)(2,1)S(1)}, bf16[1,176,1024]{2,1,0:T(8,128)(2,1)S(1)}) custom-call(s32[2]{0:T(128)S(1)} %pad_add_fusion.6.info_ref, bf16[384,2048]{1,0:T(8,128)(2,1)S(1)} %encode.3.refs_0_, bf16[384,2048]{1,0:T(8,128)(2,1)S(1)} %collective-permute-done.7.refs_1_, bf16[2048,4096]{1,0:T(8,128)(2,1)} %bitcast.29, ...), custom_call_target="tpu_custom_call" | custom-call | tf_op jit(solution)/shard_map/decode/pallas_call | solution.py:286
  90.3 1.6 collective-permute-start.11
  92.0 1.6 collective-permute-start.10
  93.5 10.5 %collective-permute-done.8 = bf16[1,208,1024]{2,1,0:T(8,128)(2,1)S(1)} collective-permute-done((bf16[1,208,1024]{2,1,0:T(8,128)(2,1)S(1)}, bf16[1,208,1024]{2,1,0:T(8,128)(2,1)S(1)}, u32[]{:S(2)}, u32[]{:S(2)}) %collective-permute-start.8) | collective-permute-done | bytes 426016 | tf_op jit(solution)/shard_map/ppermute | solution.py:381
  104.2 4.5 %decode.9 = (f32[1,208,1024]{2,1,0:T(8,128)S(1)}, bf16[1,176,1024]{2,1,0:T(8,128)(2,1)S(1)}) custom-call(s32[2]{0:T(128)S(1)} %pad_add_fusion.5.info_ref, bf16[384,2048]{1,0:T(8,128)(2,1)S(1)} %encode.3.refs_0_, bf16[384,2048]{1,0:T(8,128)(2,1)S(1)} %collective-permute-done.7.refs_1_, bf16[2048,4096]{1,0:T(8,128)(2,1)} %bitcast.30, ...), custom_call_target="tpu_custom_call" | custom-call | tf_op jit(solution)/shard_map/decode/pallas_call | solution.py:286
  108.7 1.6 collective-permute-start.12
  110.4 3.2 %collective-permute-start.13 = (bf16[1,176,1024]{2,1,0:T(8,128)(2,1)S(1)}, bf16[1,176,1024]{2,1,0:T(8,128)(2,1)S(1)}, u32[]{:S(2)}, u32[]{:S(2)}) collective-permute-start(bf16[1,176,1024]{2,1,0:T(8,128)(2,1)S(1)} %add_convert_fusion.5.refs_5_), channel_id=1, source_target_pairs={{0,4},{4,0},{8,12},{12,8},{1,5},{5,1},{9,13},{13,9},{2,6},{6,2},{1... | collective-permute-start | bytes 1081352 | tf_op jit(solution)/shard_map/ppermute | solution.py:381
  113.7 1.4 collective-permute-start.20
  115.3 4.5 %decode.10 = (bf16[1,112,1024]{2,1,0:T(8,128)(2,1)S(1)}, bf16[1,96,1024]{2,1,0:T(8,128)(2,1)S(1)}, bf16[1,176,1024]{2,1,0:T(8,128)(2,1)S(1)}) custom-call(s32[2]{0:T(128)S(1)} %pad_add_fusion.4.info_ref, bf16[384,2048]{1,0:T(8,128)(2,1)S(1)} %encode.3.refs_0_, bf16[384,2048]{1,0:T(8,128)(2,1)S(1)} %collective-permute-done.7.refs_1_, ...), custom_call_target="tpu_custom_call" | custom-call | tf_op jit(solution)/shard_map/decode/pallas_call | solution.py:286
  119.9 2.0 %collective-permute-start.18 = (bf16[1,112,1024]{2,1,0:T(8,128)(2,1)S(1)}, bf16[1,112,1024]{2,1,0:T(8,128)(2,1)S(1)}, u32[]{:S(2)}, u32[]{:S(2)}) collective-permute-start(bf16[1,112,1024]{2,1,0:T(8,128)(2,1)S(1)} %get-tuple-element.44.refs_4_), channel_id=1, source_target_pairs={{0,4},{4,0},{8,12},{12,8},{1,5},{5,1},{9,13},{13,9},{2,6},{6,2},{1... | collective-permute-start | bytes 688136 | tf_op jit(solution)/shard_map/ppermute | solution.py:381
  121.9 2.3 %collective-permute-start.15 = (bf16[1,176,1024]{2,1,0:T(8,128)(2,1)S(1)}, bf16[1,176,1024]{2,1,0:T(8,128)(2,1)S(1)}, u32[]{:S(2)}, u32[]{:S(2)}) collective-permute-start(bf16[1,176,1024]{2,1,0:T(8,128)(2,1)S(1)} %get-tuple-element.50), channel_id=1, source_target_pairs={{0,2},{2,0},{1,3},{3,1},{4,6},{6,4},{5,7},{7,5},{8,10},{10,8},{9,1... | collective-permute-start | bytes 1081352 | tf_op jit(solution)/shard_map/ppermute | solution.py:376
  124.1 5.1 %collective-permute-done.13 = bf16[1,176,1024]{2,1,0:T(8,128)(2,1)S(1)} collective-permute-done((bf16[1,176,1024]{2,1,0:T(8,128)(2,1)S(1)}, bf16[1,176,1024]{2,1,0:T(8,128)(2,1)S(1)}, u32[]{:S(2)}, u32[]{:S(2)}) %collective-permute-start.13) | collective-permute-done | bytes 360480 | tf_op jit(solution)/shard_map/ppermute | solution.py:381
  129.4 1.8 %collective-permute-start.17 = (bf16[1,176,1024]{2,1,0:T(8,128)(2,1)S(1)}, bf16[1,176,1024]{2,1,0:T(8,128)(2,1)S(1)}, u32[]{:S(2)}, u32[]{:S(2)}) collective-permute-start(bf16[1,176,1024]{2,1,0:T(8,128)(2,1)S(1)} %add_convert_fusion.4.refs_6_), channel_id=1, source_target_pairs={{0,8},{4,12},{8,0},{12,4},{1,9},{5,13},{9,1},{13,5},{2,10},{6,14},... | collective-permute-start | bytes 1081352 | tf_op jit(solution)/shard_map/ppermute | solution.py:381
  131.2 4.7 %decode.11 = (f32[1,208,1024]{2,1,0:T(8,128)S(1)}, bf16[1,176,1024]{2,1,0:T(8,128)(2,1)S(1)}) custom-call(s32[2]{0:T(128)S(1)} %pad_add_fusion.2.info_ref, bf16[384,2048]{1,0:T(8,128)(2,1)S(1)} %encode.3.refs_0_, bf16[384,2048]{1,0:T(8,128)(2,1)S(1)} %collective-permute-done.7.refs_1_, bf16[2048,4096]{1,0:T(8,128)(2,1)} %bitcast.32, ...), custom_call_target="tpu_custom_call" | custom-call | tf_op jit(solution)/shard_map/decode/pallas_call | solution.py:286
  135.9 6.7 %collective-permute-done.19 = bf16[1,96,1024]{2,1,0:T(8,128)(2,1)S(1)} collective-permute-done((bf16[1,96,1024]{2,1,0:T(8,128)(2,1)S(1)}, bf16[1,96,1024]{2,1,0:T(8,128)(2,1)S(1)}, u32[]{:S(2)}, u32[]{:S(2)}) %collective-permute-start.19) | collective-permute-done | bytes 196640 | tf_op jit(solution)/shard_map/ppermute | solution.py:381
  142.6 1.5 collective-permute-start.14
  144.1 1.1 collective-permute-done.18
  145.4 1.6 collective-permute-start.21
  147.2 2.2 %collective-permute-done.17 = bf16[1,176,1024]{2,1,0:T(8,128)(2,1)S(1)} collective-permute-done((bf16[1,176,1024]{2,1,0:T(8,128)(2,1)S(1)}, bf16[1,176,1024]{2,1,0:T(8,128)(2,1)S(1)}, u32[]{:S(2)}, u32[]{:S(2)}) %collective-permute-start.17) | collective-permute-done | bytes 360480 | tf_op jit(solution)/shard_map/ppermute | solution.py:381
  149.4 4.5 %collective-permute-done.14 = bf16[1,176,1024]{2,1,0:T(8,128)(2,1)S(1)} collective-permute-done((bf16[1,176,1024]{2,1,0:T(8,128)(2,1)S(1)}, bf16[1,176,1024]{2,1,0:T(8,128)(2,1)S(1)}, u32[]{:S(2)}, u32[]{:S(2)}) %collective-permute-start.14) | collective-permute-done | bytes 360480 | tf_op jit(solution)/shard_map/ppermute | solution.py:376
  153.9 2.6 %collective-permute-done.16 = bf16[1,176,1024]{2,1,0:T(8,128)(2,1)S(1)} collective-permute-done((bf16[1,176,1024]{2,1,0:T(8,128)(2,1)S(1)}, bf16[1,176,1024]{2,1,0:T(8,128)(2,1)S(1)}, u32[]{:S(2)}, u32[]{:S(2)}) %collective-permute-start.16) | collective-permute-done | bytes 360480 | tf_op jit(solution)/shard_map/ppermute | solution.py:381
  156.4 2.4 %collective-permute-done.21.refs_5_ = bf16[208,1024]{1,0:T(8,128)(2,1)S(1)} collective-permute-done((bf16[208,1024]{1,0:T(8,128)(2,1)S(1)}, bf16[208,1024]{1,0:T(8,128)(2,1)S(1)}, u32[]{:S(2)}, u32[]{:S(2)}) %collective-permute-start.21) | collective-permute-done | bytes 426016 | tf_op jit(solution)/shard_map/ppermute | solution.py:376
  158.9 1.6 finale.1
  160.5 1.5 collective-permute-start.23
  162.3 1.9 %collective-permute-done.23 = f32[8,128]{1,0:T(8,128)S(1)} collective-permute-done((f32[8,128]{1,0:T(8,128)S(1)}, f32[8,128]{1,0:T(8,128)S(1)}, u32[]{:S(2)}, u32[]{:S(2)}) %collective-permute-start.23) | collective-permute-done | bytes 4128 | tf_op jit(solution)/shard_map/ppermute | solution.py:376
  164.1 0.9 collective-permute-done.22
  165.1 2.2 %collective-permute-start.27 = (f32[8,128]{1,0:T(8,128)S(1)}, f32[8,128]{1,0:T(8,128)S(1)}, u32[]{:S(2)}, u32[]{:S(2)}) collective-permute-start(f32[8,128]{1,0:T(8,128)S(1)} %add_add_fusion.refs_0_), channel_id=1, source_target_pairs={{0,12},{4,0},{8,4},{12,8},{1,13},{5,1},{9,5},{13,9},{2,14},{6,2},{... | collective-permute-start | bytes 12296 | tf_op jit(solution)/shard_map/ppermute | solution.py:376
  168.7 3.1 %collective-permute-done.26.refs_2_ = f32[8,128]{1,0:T(8,128)S(1)} collective-permute-done((f32[8,128]{1,0:T(8,128)S(1)}, f32[8,128]{1,0:T(8,128)S(1)}, u32[]{:S(2)}, u32[]{:S(2)}) %collective-permute-start.26) | collective-permute-done | bytes 4128 | tf_op jit(solution)/shard_map/ppermute | solution.py:376
  171.8 0.9 collective-permute-done.25.refs_1_
  173.3 1.2 mean_ratio.1
  (60 shorter events, 5.4 us)
Async XLA Ops:
  0.6 6.7 %copy-start = (bf16[1,4096]{1,0:T(2,128)(2,1)S(1)}, bf16[1,4096]{1,0:T(2,128)(2,1)}, u32[]{:S(2)}) copy-start(bf16[1,4096]{1,0:T(2,128)(2,1)} %param.10) | copy-start | bytes 24580
  4.2 33.9 %collective-permute-start.3 = (bf16[112,4096]{1,0:T(8,128)(2,1)}, bf16[112,4096]{1,0:T(8,128)(2,1)}, u32[]{:S(2)}, u32[]{:S(2)}) collective-permute-start(bf16[112,4096]{1,0:T(8,128)(2,1)} %get-tuple-element.36), channel_id=1, source_target_pairs={{0,2},{2,0},{1,3},{3,1},{4,6},{6,4},{5,7},{7,5},{8,10},{10,8},{9,1... | collective-permute-start | bytes 2752520 | tf_op jit(solution)/shard_map/ppermute | solution.py:376
  7.2 20.7 %collective-permute-start = (f32[1]{0:T(128)}, f32[1]{0:T(128)}, u32[]{:S(2)}, u32[]{:S(2)}) collective-permute-start(f32[1]{0:T(128)} %get-tuple-element.28), channel_id=1, source_target_pairs={{0,2},{2,0},{1,3},{3,1},{4,6},{6,4},{5,7},{7,5},{8,10},{10,8},{9,1... | collective-permute-start | bytes 20 | tf_op jit(solution)/shard_map/ppermute | solution.py:376
  30.9 8.9 %collective-permute-start.2 = (bf16[384,1024]{1,0:T(8,128)(2,1)}, bf16[384,1024]{1,0:T(8,128)(2,1)}, u32[]{:S(2)}, u32[]{:S(2)}) collective-permute-start(bf16[384,1024]{1,0:T(8,128)(2,1)} %get-tuple-element.33.refs_1_), channel_id=1, source_target_pairs={{0,1},{2,3},{4,5},{6,7},{8,9},{10,11},{12,13},{14,15},{16,17},{18,... | collective-permute-start | bytes 2359304 | tf_op jit(solution)/shard_map/ppermute | solution.py:436
  33.1 6.7 %collective-permute-start.1 = (bf16[384,1024]{1,0:T(8,128)(2,1)}, bf16[384,1024]{1,0:T(8,128)(2,1)}, u32[]{:S(2)}, u32[]{:S(2)}) collective-permute-start(bf16[384,1024]{1,0:T(8,128)(2,1)} %get-tuple-element.32.refs_0_.after_ref), channel_id=1, source_target_pairs={{0,1},{2,3},{4,5},{6,7},{8,9},{10,11},{12,13},{14,15},{16,17},{18,... | collective-permute-start | bytes 2359304 | tf_op jit(solution)/shard_map/ppermute | solution.py:436
  36.3 31.5 %collective-permute-start.5 = (bf16[160,4096]{1,0:T(8,128)(2,1)}, bf16[160,4096]{1,0:T(8,128)(2,1)S(1)}, u32[]{:S(2)}, u32[]{:S(2)}) collective-permute-start(bf16[160,4096]{1,0:T(8,128)(2,1)} %cut.1), channel_id=1, source_target_pairs={{0,2},{2,0},{1,3},{3,1},{4,6},{6,4},{5,7},{7,5},{8,10},{10,8},{9,1... | collective-permute-start | bytes 3932168 | tf_op jit(solution)/shard_map/ppermute | solution.py:376
  38.1 29.7 %collective-permute-start.4 = (bf16[112,4096]{1,0:T(8,128)(2,1)}, bf16[112,4096]{1,0:T(8,128)(2,1)S(1)}, u32[]{:S(2)}, u32[]{:S(2)}) collective-permute-start(bf16[112,4096]{1,0:T(8,128)(2,1)} %collective-permute-done.3.refs_0_), channel_id=1, source_target_pairs={{0,4},{4,0},{8,12},{12,8},{1,5},{5,1},{9,13},{13,9},{2,6},{6,2},{1... | collective-permute-start | bytes 2752520 | tf_op jit(solution)/shard_map/ppermute | solution.py:381
  48.2 0.9 copy-start.3
  49.1 0.8 copy-start.6
  49.9 16.8 %collective-permute-start.6 = (bf16[1,208,1024]{2,1,0:T(8,128)(2,1)S(1)}, bf16[1,208,1024]{2,1,0:T(8,128)(2,1)}, u32[]{:S(2)}, u32[]{:S(2)}) collective-permute-start(bf16[1,208,1024]{2,1,0:T(8,128)(2,1)S(1)} %get-tuple-element.34.refs_6_), channel_id=1, source_target_pairs={{0,4},{4,0},{8,12},{12,8},{1,5},{5,1},{9,13},{13,9},{2,6},{6,2},{1... | collective-permute-start | bytes 1277960 | tf_op jit(solution)/shard_map/ppermute | solution.py:381
  67.8 14.8 %copy-start.7 = (bf16[1,208,1024]{2,1,0:T(8,128)(2,1)S(1)}, bf16[1,208,1024]{2,1,0:T(8,128)(2,1)}, u32[]{:S(2)}) copy-start(bf16[1,208,1024]{2,1,0:T(8,128)(2,1)} %copy-done.6) | copy-start | bytes 1277956
  78.4 7.4 %collective-permute-start.7 = (bf16[384,2048]{1,0:T(8,128)(2,1)S(1)}, bf16[384,2048]{1,0:T(8,128)(2,1)S(1)}, u32[]{:S(2)}, u32[]{:S(2)}) collective-permute-start(bf16[384,2048]{1,0:T(8,128)(2,1)S(1)} %encode.3.refs_0_), channel_id=1, source_target_pairs={{0,1},{2,3},{4,5},{6,7},{8,9},{10,11},{12,13},{14,15},{16,17},{18,... | collective-permute-start | bytes 4718600 | tf_op jit(solution)/shard_map/ppermute | solution.py:436
  82.6 21.4 %collective-permute-start.8 = (bf16[1,208,1024]{2,1,0:T(8,128)(2,1)S(1)}, bf16[1,208,1024]{2,1,0:T(8,128)(2,1)S(1)}, u32[]{:S(2)}, u32[]{:S(2)}) collective-permute-start(bf16[1,208,1024]{2,1,0:T(8,128)(2,1)S(1)} %copy-done.7), channel_id=1, source_target_pairs={{0,4},{4,0},{8,12},{12,8},{1,5},{5,1},{9,13},{13,9},{2,6},{6,2},{1... | collective-permute-start | bytes 1277960 | tf_op jit(solution)/shard_map/ppermute | solution.py:381
  83.0 21.0 %collective-permute-start.9 = (bf16[1,208,1024]{2,1,0:T(8,128)(2,1)S(1)}, bf16[1,208,1024]{2,1,0:T(8,128)(2,1)S(1)}, u32[]{:S(2)}, u32[]{:S(2)}) collective-permute-start(bf16[1,208,1024]{2,1,0:T(8,128)(2,1)S(1)} %add_convert_fusion.2.refs_4_), channel_id=1, source_target_pairs={{0,8},{4,12},{8,0},{12,4},{1,9},{5,13},{9,1},{13,5},{2,10},{6,14},... | collective-permute-start | bytes 1277960 | tf_op jit(solution)/shard_map/ppermute | solution.py:381
  90.3 20.0 %collective-permute-start.11 = (bf16[1,176,1024]{2,1,0:T(8,128)(2,1)S(1)}, bf16[1,176,1024]{2,1,0:T(8,128)(2,1)S(1)}, u32[]{:S(2)}, u32[]{:S(2)}) collective-permute-start(bf16[1,176,1024]{2,1,0:T(8,128)(2,1)S(1)} %get-tuple-element.43), channel_id=1, source_target_pairs={{0,2},{2,0},{1,3},{3,1},{4,6},{6,4},{5,7},{7,5},{8,10},{10,8},{9,1... | collective-permute-start | bytes 1081352 | tf_op jit(solution)/shard_map/ppermute | solution.py:376
  92.0 21.6 %collective-permute-start.10 = (bf16[1,208,1024]{2,1,0:T(8,128)(2,1)S(1)}, bf16[1,208,1024]{2,1,0:T(8,128)(2,1)S(1)}, u32[]{:S(2)}, u32[]{:S(2)}) collective-permute-start(bf16[1,208,1024]{2,1,0:T(8,128)(2,1)S(1)} %get-tuple-element.38.refs_4_), channel_id=1, source_target_pairs={{0,4},{4,0},{8,12},{12,8},{1,5},{5,1},{9,13},{13,9},{2,6},{6,2},{1... | collective-permute-start | bytes 1277960 | tf_op jit(solution)/shard_map/ppermute | solution.py:381
  104.2 6.2 %copy-start.4 = (f32[1,176,1024]{2,1,0:T(8,128)S(1)}, f32[1,176,1024]{2,1,0:T(8,128)}, u32[]{:S(2)}) copy-start(f32[1,176,1024]{2,1,0:T(8,128)} %copy-done.3) | copy-start | bytes 2162692
  108.7 13.1 %collective-permute-start.12 = (bf16[1,176,1024]{2,1,0:T(8,128)(2,1)S(1)}, bf16[1,176,1024]{2,1,0:T(8,128)(2,1)S(1)}, u32[]{:S(2)}, u32[]{:S(2)}) collective-permute-start(bf16[1,176,1024]{2,1,0:T(8,128)(2,1)S(1)} %get-tuple-element.47), channel_id=1, source_target_pairs={{0,2},{2,0},{1,3},{3,1},{4,6},{6,4},{5,7},{7,5},{8,10},{10,8},{9,1... | collective-permute-start | bytes 1081352 | tf_op jit(solution)/shard_map/ppermute | solution.py:376
  110.4 18.8 %collective-permute-start.13 = (bf16[1,176,1024]{2,1,0:T(8,128)(2,1)S(1)}, bf16[1,176,1024]{2,1,0:T(8,128)(2,1)S(1)}, u32[]{:S(2)}, u32[]{:S(2)}) collective-permute-start(bf16[1,176,1024]{2,1,0:T(8,128)(2,1)S(1)} %add_convert_fusion.5.refs_5_), channel_id=1, source_target_pairs={{0,4},{4,0},{8,12},{12,8},{1,5},{5,1},{9,13},{13,9},{2,6},{6,2},{1... | collective-permute-start | bytes 1081352 | tf_op jit(solution)/shard_map/ppermute | solution.py:381
  113.7 31.5 %collective-permute-start.20 = (bf16[1,208,1024]{2,1,0:T(8,128)(2,1)S(1)}, bf16[1,208,1024]{2,1,0:T(8,128)(2,1)S(1)}, u32[]{:S(2)}, u32[]{:S(2)}) collective-permute-start(bf16[1,208,1024]{2,1,0:T(8,128)(2,1)S(1)} %add_convert_fusion.1.refs_4_), channel_id=1, source_target_pairs={{0,8},{4,12},{8,0},{12,4},{1,9},{5,13},{9,1},{13,5},{2,10},{6,14},... | collective-permute-start | bytes 1277960 | tf_op jit(solution)/shard_map/ppermute | solution.py:381
  119.8 22.8 %collective-permute-start.19 = (bf16[1,96,1024]{2,1,0:T(8,128)(2,1)S(1)}, bf16[1,96,1024]{2,1,0:T(8,128)(2,1)S(1)}, u32[]{:S(2)}, u32[]{:S(2)}) collective-permute-start(bf16[1,96,1024]{2,1,0:T(8,128)(2,1)S(1)} %get-tuple-element.45.refs_5_), channel_id=1, source_target_pairs={{0,4},{4,0},{8,12},{12,8},{1,5},{5,1},{9,13},{13,9},{2,6},{6,2},{1... | collective-permute-start | bytes 589832 | tf_op jit(solution)/shard_map/ppermute | solution.py:381
  119.9 25.3 %collective-permute-start.18 = (bf16[1,112,1024]{2,1,0:T(8,128)(2,1)S(1)}, bf16[1,112,1024]{2,1,0:T(8,128)(2,1)S(1)}, u32[]{:S(2)}, u32[]{:S(2)}) collective-permute-start(bf16[1,112,1024]{2,1,0:T(8,128)(2,1)S(1)} %get-tuple-element.44.refs_4_), channel_id=1, source_target_pairs={{0,4},{4,0},{8,12},{12,8},{1,5},{5,1},{9,13},{13,9},{2,6},{6,2},{1... | collective-permute-start | bytes 688136 | tf_op jit(solution)/shard_map/ppermute | solution.py:381
  121.9 25.1 %collective-permute-start.15 = (bf16[1,176,1024]{2,1,0:T(8,128)(2,1)S(1)}, bf16[1,176,1024]{2,1,0:T(8,128)(2,1)S(1)}, u32[]{:S(2)}, u32[]{:S(2)}) collective-permute-start(bf16[1,176,1024]{2,1,0:T(8,128)(2,1)S(1)} %get-tuple-element.50), channel_id=1, source_target_pairs={{0,2},{2,0},{1,3},{3,1},{4,6},{6,4},{5,7},{7,5},{8,10},{10,8},{9,1... | collective-permute-start | bytes 1081352 | tf_op jit(solution)/shard_map/ppermute | solution.py:376
  129.4 20.0 %collective-permute-start.17 = (bf16[1,176,1024]{2,1,0:T(8,128)(2,1)S(1)}, bf16[1,176,1024]{2,1,0:T(8,128)(2,1)S(1)}, u32[]{:S(2)}, u32[]{:S(2)}) collective-permute-start(bf16[1,176,1024]{2,1,0:T(8,128)(2,1)S(1)} %add_convert_fusion.4.refs_6_), channel_id=1, source_target_pairs={{0,8},{4,12},{8,0},{12,4},{1,9},{5,13},{9,1},{13,5},{2,10},{6,14},... | collective-permute-start | bytes 1081352 | tf_op jit(solution)/shard_map/ppermute | solution.py:381
  142.6 11.3 %collective-permute-start.14 = (bf16[1,176,1024]{2,1,0:T(8,128)(2,1)S(1)}, bf16[1,176,1024]{2,1,0:T(8,128)(2,1)S(1)}, u32[]{:S(2)}, u32[]{:S(2)}) collective-permute-start(bf16[1,176,1024]{2,1,0:T(8,128)(2,1)S(1)} %get-tuple-element.48), channel_id=1, source_target_pairs={{0,2},{2,0},{1,3},{3,1},{4,6},{6,4},{5,7},{7,5},{8,10},{10,8},{9,1... | collective-permute-start | bytes 1081352 | tf_op jit(solution)/shard_map/ppermute | solution.py:376
  145.2 13.7 %copy-start.2 = (bf16[1,384,1024]{2,1,0:T(8,128)(2,1)S(1)}, bf16[1,384,1024]{2,1,0:T(8,128)(2,1)}, u32[]{:S(2)}) copy-start(bf16[1,384,1024]{2,1,0:T(8,128)(2,1)} %param.8) | copy-start | bytes 2359300
  145.2 13.7 %copy-start.5 = (bf16[1,1024]{1,0:T(2,128)(2,1)S(1)}, bf16[1,1024]{1,0:T(2,128)(2,1)}, u32[]{:S(2)}) copy-start(bf16[1,1024]{1,0:T(2,128)(2,1)} %b_ref.1) | copy-start | bytes 6148
  145.4 13.5 %collective-permute-start.21 = (bf16[208,1024]{1,0:T(8,128)(2,1)S(1)}, bf16[208,1024]{1,0:T(8,128)(2,1)S(1)}, u32[]{:S(2)}, u32[]{:S(2)}) collective-permute-start(bf16[208,1024]{1,0:T(8,128)(2,1)S(1)} %fusion), channel_id=1, source_target_pairs={{0,2},{2,0},{1,3},{3,1},{4,6},{6,4},{5,7},{7,5},{8,10},{10,8},{9,1... | collective-permute-start | bytes 1277960 | tf_op jit(solution)/shard_map/ppermute | solution.py:376
  147.1 9.4 %collective-permute-start.16 = (bf16[1,176,1024]{2,1,0:T(8,128)(2,1)S(1)}, bf16[1,176,1024]{2,1,0:T(8,128)(2,1)S(1)}, u32[]{:S(2)}, u32[]{:S(2)}) collective-permute-start(bf16[1,176,1024]{2,1,0:T(8,128)(2,1)S(1)} %add_convert_fusion.3), channel_id=1, source_target_pairs={{0,4},{4,0},{8,12},{12,8},{1,5},{5,1},{9,13},{13,9},{2,6},{6,2},{1... | collective-permute-start | bytes 1081352 | tf_op jit(solution)/shard_map/ppermute | solution.py:381
  158.9 15.7 %copy-start.1 = (bf16[1,4096]{1,0:T(2,128)(2,1)S(1)}, bf16[1,4096]{1,0:T(2,128)(2,1)}, u32[]{:S(2)}) copy-start(bf16[1,4096]{1,0:T(2,128)(2,1)} %param.10) | copy-start | bytes 24580
  160.5 1.7 collective-permute-start.24
  160.5 3.6 %collective-permute-start.23 = (f32[8,128]{1,0:T(8,128)S(1)}, f32[8,128]{1,0:T(8,128)S(1)}, u32[]{:S(2)}, u32[]{:S(2)}) collective-permute-start(f32[8,128]{1,0:T(8,128)S(1)} %get-tuple-element.53), channel_id=1, source_target_pairs={{0,2},{1,3},{2,0},{3,1},{4,6},{5,7},{6,4},{7,5},{8,10},{9,11},{10,... | collective-permute-start | bytes 12296 | tf_op jit(solution)/shard_map/ppermute | solution.py:376
  162.0 3.0 %collective-permute-start.22 = (f32[8,128]{1,0:T(8,128)S(1)}, f32[8,128]{1,0:T(8,128)S(1)}, u32[]{:S(2)}, u32[]{:S(2)}) collective-permute-start(f32[8,128]{1,0:T(8,128)S(1)} %get-tuple-element.53), channel_id=1, source_target_pairs={{0,1},{1,2},{2,3},{3,0},{4,5},{5,6},{6,7},{7,4},{8,9},{9,10},{10,1... | collective-permute-start | bytes 12296 | tf_op jit(solution)/shard_map/ppermute | solution.py:376
  165.1 7.6 %copy-start.8 = (f32[8,128]{1,0:T(8,128)}, f32[8,128]{1,0:T(8,128)S(1)}, u32[]{:S(2)}) copy-start(f32[8,128]{1,0:T(8,128)S(1)} %add_add_fusion.refs_0_) | copy-start | bytes 12292
  165.1 3.6 %collective-permute-start.27 = (f32[8,128]{1,0:T(8,128)S(1)}, f32[8,128]{1,0:T(8,128)S(1)}, u32[]{:S(2)}, u32[]{:S(2)}) collective-permute-start(f32[8,128]{1,0:T(8,128)S(1)} %add_add_fusion.refs_0_), channel_id=1, source_target_pairs={{0,12},{4,0},{8,4},{12,8},{1,13},{5,1},{9,5},{13,9},{2,14},{6,2},{... | collective-permute-start | bytes 12296 | tf_op jit(solution)/shard_map/ppermute | solution.py:376
  167.3 4.5 %collective-permute-start.26 = (f32[8,128]{1,0:T(8,128)S(1)}, f32[8,128]{1,0:T(8,128)S(1)}, u32[]{:S(2)}, u32[]{:S(2)}) collective-permute-start(f32[8,128]{1,0:T(8,128)S(1)} %add_add_fusion.refs_0_), channel_id=1, source_target_pairs={{0,8},{4,12},{8,0},{12,4},{1,9},{5,13},{9,1},{13,5},{2,10},{6,14},... | collective-permute-start | bytes 12296 | tf_op jit(solution)/shard_map/ppermute | solution.py:376
  167.3 5.4 %collective-permute-start.25 = (f32[8,128]{1,0:T(8,128)S(1)}, f32[8,128]{1,0:T(8,128)S(1)}, u32[]{:S(2)}, u32[]{:S(2)}) collective-permute-start(f32[8,128]{1,0:T(8,128)S(1)} %add_add_fusion.refs_0_), channel_id=1, source_target_pairs={{0,4},{4,8},{8,12},{12,0},{1,5},{5,9},{9,13},{13,1},{2,6},{6,10},{... | collective-permute-start | bytes 12296 | tf_op jit(solution)/shard_map/ppermute | solution.py:376
  168.7 4.0 %copy-start.9 = (f32[8,128]{1,0:T(8,128)}, f32[8,128]{1,0:T(8,128)S(1)}, u32[]{:S(2)}) copy-start(f32[8,128]{1,0:T(8,128)S(1)} %collective-permute-done.27.refs_3_) | copy-start | bytes 12292
  171.8 0.9 copy-start.10
  172.7 0.6 copy-start.11

commit v14 on v11

--- a/solution.py
+++ b/solution.py
@@ -56,35 +56,29 @@
     )(x)
 
 
-def cut(x, side, edge, after):
-    rows, width = x.shape
-    middle = rows - 2 * edge
-
-    def body(side_ref, after_ref, x_ref, outer_ref, inner_ref, sem):
-        start = pl.multiple_of(side_ref[0] * (rows - edge), 16)
-        copies = [
-            pltpu.make_async_copy(x_ref.at[pl.ds(start, edge)], outer_ref, sem.at[0]),
-            pltpu.make_async_copy(x_ref.at[pl.ds(edge, middle)], inner_ref, sem.at[1]),
-        ]
-        for copy in copies:
-            copy.start()
-        for copy in copies:
-            copy.wait()
+def cut(x, first, count, after):
+    width = x.shape[1]
+
+    def body(first_ref, x_ref, after_ref, o_ref, sem):
+        place = pl.ds(pl.multiple_of(first_ref[0], 16), count)
+        copy = pltpu.make_async_copy(x_ref.at[place], o_ref, sem)
+        copy.start()
+        copy.wait()
 
     return pl.pallas_call(
         body,
         in_specs=[
             pl.BlockSpec(memory_space=pltpu.SMEM),
-            pl.BlockSpec(memory_space=pltpu.SMEM),
             pl.BlockSpec(memory_space=pltpu.VMEM),
+            pl.BlockSpec(memory_space=pl.ANY),
         ],
-        out_specs=[pl.BlockSpec(memory_space=pl.ANY)] * 2,
-        out_shape=[pltpu.HBM((edge, width), x.dtype), pltpu.HBM((middle, width), x.dtype)],
-        scratch_shapes=[pltpu.SemaphoreType.DMA((2,))],
+        out_specs=pl.BlockSpec(memory_space=pl.ANY),
+        out_shape=pltpu.HBM((count, width), x.dtype),
+        scratch_shapes=[pltpu.SemaphoreType.DMA],
         compiler_params=pltpu.CompilerParams(vmem_limit_bytes=VMEM_LIMIT),
         cost_estimate=COST,
         name="cut",
-    )(side.reshape(1), after, pltpu.with_memory_space_constraint(x, pltpu.VMEM))
+    )(first.reshape(1), pltpu.with_memory_space_constraint(x, pltpu.VMEM), after)
 
 
 def ring_loop(count, slots, start, step):
@@ -375,18 +369,12 @@
     width = dec_bias.shape[1]
     side = lat % 2
 
-    edge = rows * 7 // 24 // 16 * 16
+    edge = rows // 4 // 16 * 16
     square, x_held = square_sum(x_own)
     square = sum_over(square, "token")
     scale = jnp.sqrt(square / (rows * n_tok * model) + 1e-06)
     inv = 1.0 / scale
-    outer, inner = cut(x_held, side.astype(jnp.int32), edge, inv)
-    foreign = []
-    for distance in range(1, n_tok):
-        mine = shifted(outer, "token", distance)
-        theirs = swapped(mine, "latent", 1)
-        foreign.append((n_tok - distance, mine, theirs, shifted(inner, "token", distance)))
-
+    outer = cut(x_held, (side * (rows - edge)).astype(jnp.int32), edge, square)
     bias = lax.dynamic_slice_in_dim(
         encoder_layer_bias, lax.axis_index("token") * lat_dev, lat_dev, axis=1
     )
@@ -425,6 +413,12 @@
         return total[0]
 
     codes = encode([(x_held, 0, rows)], places(0), inv, enc_w, bias, 2, [])
+    inner = cut(x_held, jnp.int32(edge), rows - 2 * edge, codes[0])
+    foreign = []
+    for distance in range(1, n_tok):
+        mine = shifted(outer, "token", distance)
+        theirs = swapped(mine, "latent", 1)
+        foreign.append((n_tok - distance, mine, theirs, shifted(inner, "token", distance)))
     earlier = earlier_of(codes)
     inside = ((first, middle),)
     outside = ((0, first), (last, rows - last))

time: 162 us -> 163 us (level)
  waiting for transfers between devices: 58.1 us -> 55.1 us
  starting transfers between devices: 34.1 us -> 36.8 us
    ppermute x14, starting transfers between devices: 15.7 us -> 18.5 us  [shifted(): lax.ppermute(value, axis, [(i, (i + distance) % n) for i in range(n)])]
    ppermute x14, waiting for transfers between devices: 24.6 us -> 22.8 us  [shifted(): lax.ppermute(value, axis, [(i, (i + distance) % n) for i in range(n)])]
  transfers between devices with their start and end apart: 28 -> 28, of which waited for: 16 -> 17; matrix products, arithmetic and copies ran while one was open for 1% -> 1% of each run, Pallas kernels for 27% -> 28%
where the time goes in v14:
time: 163 us
  Pallas kernels  63.1 us (39%)
  waiting for transfers between devices  55.1 us (34%)
  starting transfers between devices  36.8 us (23%)
  local copies, waits for them, and re-layouts  3.19 us (2%)
  other arithmetic  2.33 us (1%)
  between operations  2.33 us (1%)
    pallas_call x6, Pallas kernels, decode(): pl.pallas_call(body, in_specs=[pl.BlockSpec(memory_space=pltpu.SMEM)] + [...  33.8 us
    ppermute x11, waiting for transfers between devices, swapped(): return lax.ppermute(value, axis, [(i, i ^ bit) for i in range(n)])  32.3 us
    ppermute x14, waiting for transfers between devices, shifted(): lax.ppermute(value, axis, [(i, (i + distance) % n) for i in range(n)])  22.8 us
    pallas_call x2, Pallas kernels, encode(): pl.pallas_call(body, in_specs=[pl.BlockSpec(memory_space=pltpu.SMEM), pl....  21.6 us
    ppermute x14, starting transfers between devices, shifted(): lax.ppermute(value, axis, [(i, (i + distance) % n) for i in range(n)])  18.5 us
    ppermute x11, starting transfers between devices, swapped(): return lax.ppermute(value, axis, [(i, i ^ bit) for i in range(n)])  14.3 us
    ppermute x3, starting transfers between devices, earlier_of(): return [lax.ppermute(part, 'layer', [(0, 1)]) for part in codes]  4.06 us
  transfers between devices with their start and end apart: 28, of which 17 were waited for; matrix products, arithmetic and copies ran while one was open for 1% of the time, Pallas kernels for 28%

profile of v14, /device:TPU:0, one launch (start us, length us, event | category | flops | bytes accessed | tf_op | source)
XLA Modules:
  0.0 162.9 jit_solution(16972641053101057327)
XLA Ops:
  0.6 2.7 %square_sum.1 = (f32[1]{0:T(128)}, bf16[384,4096]{1,0:T(8,128)(2,1)S(1)}) custom-call(bf16[384,4096]{1,0:T(8,128)(2,1)} %bitcast.34), custom_call_target="tpu_custom_call" | custom-call | tf_op jit(solution)/shard_map/square_sum/pallas_call | solution.py:47
  3.4 3.0 %collective-permute-start = (f32[1]{0:T(128)}, f32[1]{0:T(128)}, u32[]{:S(2)}, u32[]{:S(2)}) collective-permute-start(f32[1]{0:T(128)} %get-tuple-element.25), channel_id=1, source_target_pairs={{0,2},{2,0},{1,3},{3,1},{4,6},{6,4},{5,7},{7,5},{8,10},{10,8},{9,1... | collective-permute-start | bytes 20 | tf_op jit(solution)/shard_map/ppermute | solution.py:335
  6.4 1.8 %collective-permute-done = f32[1]{0:T(128)} collective-permute-done((f32[1]{0:T(128)}, f32[1]{0:T(128)}, u32[]{:S(2)}, u32[]{:S(2)}) %collective-permute-start) | collective-permute-done | bytes 36 | tf_op jit(solution)/shard_map/ppermute | solution.py:335
  10.3 2.1 %collective-permute-start.3 = (bf16[96,4096]{1,0:T(8,128)(2,1)}, bf16[96,4096]{1,0:T(8,128)(2,1)}, u32[]{:S(2)}, u32[]{:S(2)}) collective-permute-start(bf16[96,4096]{1,0:T(8,128)(2,1)} %cut.2), channel_id=1, source_target_pairs={{0,2},{2,0},{1,3},{3,1},{4,6},{6,4},{5,7},{7,5},{8,10},{10,8},{9,1... | collective-permute-start | bytes 2359304 | tf_op jit(solution)/shard_map/ppermute | solution.py:335
  12.5 10.9 %encode.2 = (bf16[384,1024]{1,0:T(8,128)(2,1)}, bf16[384,1024]{1,0:T(8,128)(2,1)}) custom-call(s32[1]{0:T(128)} %constant.58.clone.1.places_ref, f32[1]{0:T(128)S(6)} %sqrt.3.inv_ref, bf16[1,2048]{1,0:T(2,128)(2,1)S(1)} %constant_dynamic-slice_fusion.b_ref, bf16[384,4096]{1,0:T(8,128)(2,1)S(1)} %get-tuple-element.26.refs_0_.x_ref, bf16[4096,2048]{1,0:T(8,128)(2,1)} %bitcast.32), custom_call_target="tpu_custom_call" | custom-call | tf_op jit(solution)/shard_map/encode/pallas_call | solution.py:146
  23.4 1.2 cut.3
  24.7 1.3 collective-permute-start.2
  26.1 1.3 collective-permute-start.1
  27.5 3.7 %collective-permute-done.3.refs_0_ = bf16[96,4096]{1,0:T(8,128)(2,1)} collective-permute-done((bf16[96,4096]{1,0:T(8,128)(2,1)}, bf16[96,4096]{1,0:T(8,128)(2,1)}, u32[]{:S(2)}, u32[]{:S(2)}) %collective-permute-start.3) | collective-permute-done | bytes 786464 | tf_op jit(solution)/shard_map/ppermute | solution.py:335
  31.2 2.1 %collective-permute-start.4 = (bf16[96,4096]{1,0:T(8,128)(2,1)}, bf16[96,4096]{1,0:T(8,128)(2,1)}, u32[]{:S(2)}, u32[]{:S(2)}) collective-permute-start(bf16[96,4096]{1,0:T(8,128)(2,1)} %collective-permute-done.3.refs_0_), channel_id=1, source_target_pairs={{0,4},{4,0},{8,12},{12,8},{1,5},{5,1},{9,13},{13,9},{2,6},{6,2},{1... | collective-permute-start | bytes 2359304 | tf_op jit(solution)/shard_map/ppermute | solution.py:340
  33.4 8.2 %decode.6 = (bf16[1,208,1024]{2,1,0:T(8,128)(2,1)}, bf16[1,208,1024]{2,1,0:T(8,128)(2,1)S(1)}, f32[1,176,1024]{2,1,0:T(8,128)S(1)}, f32[1,176,1024]{2,1,0:T(8,128)S(1)}) custom-call(s32[3]{0:T(128)S(1)} %get-tuple-element.49.info_ref, bf16[384,1024]{1,0:T(8,128)(2,1)} %get-tuple-element.27.refs_0_.after_ref, bf16[384,1024]{1,0:T(8,128)(2,1)} %get-tuple-element.28.refs_1_, ...), custom_call_target="tpu_custom_call" | custom-call | tf_op jit(solution)/shard_map/decode/pallas_call | solution.py:245
  42.4 0.9 copy-done.5
  44.2 7.4 %decode.7 = (f32[1,208,1024]{2,1,0:T(8,128)S(1)}, f32[1,208,1024]{2,1,0:T(8,128)S(1)}, f32[1,176,1024]{2,1,0:T(8,128)S(1)}, f32[1,176,1024]{2,1,0:T(8,128)S(1)}) custom-call(s32[3]{0:T(128)S(1)} %get-tuple-element.48.info_ref, bf16[384,1024]{1,0:T(8,128)(2,1)} %get-tuple-element.27.refs_0_.after_ref, bf16[384,1024]{1,0:T(8,128)(2,1)} %get-tuple-element.28.refs_1_, ...), custom_call_target="tpu_custom_call" | custom-call | tf_op jit(solution)/shard_map/decode/pallas_call | solution.py:245
  51.6 4.9 %collective-permute-done.6 = bf16[1,208,1024]{2,1,0:T(8,128)(2,1)} collective-permute-done((bf16[1,208,1024]{2,1,0:T(8,128)(2,1)}, bf16[1,208,1024]{2,1,0:T(8,128)(2,1)}, u32[]{:S(2)}, u32[]{:S(2)}) %collective-permute-start.6) | collective-permute-done | bytes 426016 | tf_op jit(solution)/shard_map/ppermute | solution.py:340
  56.6 1.1 add_convert_fusion.2.refs_4_
  57.7 4.9 %collective-permute-done.5.refs_2_ = bf16[192,4096]{1,0:T(8,128)(2,1)S(1)} collective-permute-done((bf16[192,4096]{1,0:T(8,128)(2,1)}, bf16[192,4096]{1,0:T(8,128)(2,1)S(1)}, u32[]{:S(2)}, u32[]{:S(2)}) %collective-permute-start.5) | collective-permute-done | bytes 1572896 | tf_op jit(solution)/shard_map/ppermute | solution.py:335
  62.6 10.6 %encode.3.refs_0_ = bf16[384,2048]{1,0:T(8,128)(2,1)S(1)} custom-call(s32[3]{0:T(128)S(1)} %pad_add_fusion.3.places_ref, f32[1]{0:T(128)S(6)} %sqrt.3.inv_ref, bf16[1,2048]{1,0:T(2,128)(2,1)S(1)} %constant_dynamic-slice_fusion.b_ref, bf16[96,4096]{1,0:T(8,128)(2,1)} %collective-permute-done.3.refs_0_, bf16[96,4096]{1,0:T(8,128)(2,1)} %collective-permute-done.4.refs_1_, ...), custom_call_target="tpu_custom_call" | custom-call | tf_op jit(solution)/shard_map/encode/pallas_call | solution.py:146
  73.2 1.4 collective-permute-start.7
  74.6 1.9 %collective-permute-start.8 = (bf16[1,208,1024]{2,1,0:T(8,128)(2,1)S(1)}, bf16[1,208,1024]{2,1,0:T(8,128)(2,1)S(1)}, u32[]{:S(2)}, u32[]{:S(2)}) collective-permute-start(bf16[1,208,1024]{2,1,0:T(8,128)(2,1)S(1)} %copy-done.9), channel_id=1, source_target_pairs={{0,4},{4,0},{8,12},{12,8},{1,5},{5,1},{9,13},{13,9},{2,6},{6,2},{1... | collective-permute-start | bytes 1277960 | tf_op jit(solution)/shard_map/ppermute | solution.py:340
  76.5 2.6 %collective-permute-start.9 = (bf16[1,208,1024]{2,1,0:T(8,128)(2,1)S(1)}, bf16[1,208,1024]{2,1,0:T(8,128)(2,1)S(1)}, u32[]{:S(2)}, u32[]{:S(2)}) collective-permute-start(bf16[1,208,1024]{2,1,0:T(8,128)(2,1)S(1)} %add_convert_fusion.2.refs_4_), channel_id=1, source_target_pairs={{0,8},{4,12},{8,0},{12,4},{1,9},{5,13},{9,1},{13,5},{2,10},{6,14},... | collective-permute-start | bytes 1277960 | tf_op jit(solution)/shard_map/ppermute | solution.py:340
  79.2 4.5 %decode.8 = (bf16[1,208,1024]{2,1,0:T(8,128)(2,1)S(1)}, bf16[1,176,1024]{2,1,0:T(8,128)(2,1)S(1)}) custom-call(s32[2]{0:T(128)S(1)} %pad_add_fusion.6.info_ref, bf16[384,2048]{1,0:T(8,128)(2,1)S(1)} %encode.3.refs_0_, bf16[384,2048]{1,0:T(8,128)(2,1)S(1)} %collective-permute-done.7.refs_1_, bf16[2048,4096]{1,0:T(8,128)(2,1)} %bitcast.28, ...), custom_call_target="tpu_custom_call" | custom-call | tf_op jit(solution)/shard_map/decode/pallas_call | solution.py:245
  83.7 1.6 collective-permute-start.11
  85.8 9.9 %collective-permute-done.8 = bf16[1,208,1024]{2,1,0:T(8,128)(2,1)S(1)} collective-permute-done((bf16[1,208,1024]{2,1,0:T(8,128)(2,1)S(1)}, bf16[1,208,1024]{2,1,0:T(8,128)(2,1)S(1)}, u32[]{:S(2)}, u32[]{:S(2)}) %collective-permute-start.8) | collective-permute-done | bytes 426016 | tf_op jit(solution)/shard_map/ppermute | solution.py:340
  96.2 4.5 %decode.9 = (f32[1,208,1024]{2,1,0:T(8,128)S(1)}, bf16[1,176,1024]{2,1,0:T(8,128)(2,1)S(1)}) custom-call(s32[2]{0:T(128)S(1)} %pad_add_fusion.5.info_ref, bf16[384,2048]{1,0:T(8,128)(2,1)S(1)} %encode.3.refs_0_, bf16[384,2048]{1,0:T(8,128)(2,1)S(1)} %collective-permute-done.7.refs_1_, bf16[2048,4096]{1,0:T(8,128)(2,1)} %bitcast.29, ...), custom_call_target="tpu_custom_call" | custom-call | tf_op jit(solution)/shard_map/decode/pallas_call | solution.py:245
  100.7 1.6 collective-permute-start.12
  102.4 3.6 %collective-permute-start.13 = (bf16[1,176,1024]{2,1,0:T(8,128)(2,1)S(1)}, bf16[1,176,1024]{2,1,0:T(8,128)(2,1)S(1)}, u32[]{:S(2)}, u32[]{:S(2)}) collective-permute-start(bf16[1,176,1024]{2,1,0:T(8,128)(2,1)S(1)} %add_convert_fusion.5.refs_5_), channel_id=1, source_target_pairs={{0,4},{4,0},{8,12},{12,8},{1,5},{5,1},{9,13},{13,9},{2,6},{6,2},{1... | collective-permute-start | bytes 1081352 | tf_op jit(solution)/shard_map/ppermute | solution.py:340
  106.3 4.5 %decode.10 = (bf16[1,112,1024]{2,1,0:T(8,128)(2,1)S(1)}, bf16[1,96,1024]{2,1,0:T(8,128)(2,1)S(1)}, bf16[1,176,1024]{2,1,0:T(8,128)(2,1)S(1)}) custom-call(s32[2]{0:T(128)S(1)} %pad_add_fusion.4.info_ref, bf16[384,2048]{1,0:T(8,128)(2,1)S(1)} %encode.3.refs_0_, bf16[384,2048]{1,0:T(8,128)(2,1)S(1)} %collective-permute-done.7.refs_1_, ...), custom_call_target="tpu_custom_call" | custom-call | tf_op jit(solution)/shard_map/decode/pallas_call | solution.py:245
  110.8 2.0 %collective-permute-start.19 = (bf16[1,96,1024]{2,1,0:T(8,128)(2,1)S(1)}, bf16[1,96,1024]{2,1,0:T(8,128)(2,1)S(1)}, u32[]{:S(2)}, u32[]{:S(2)}) collective-permute-start(bf16[1,96,1024]{2,1,0:T(8,128)(2,1)S(1)} %get-tuple-element.39.refs_5_), channel_id=1, source_target_pairs={{0,4},{4,0},{8,12},{12,8},{1,5},{5,1},{9,13},{13,9},{2,6},{6,2},{1... | collective-permute-start | bytes 589832 | tf_op jit(solution)/shard_map/ppermute | solution.py:340
  112.9 1.2 collective-permute-start.15
  114.1 7.6 %collective-permute-done.13 = bf16[1,176,1024]{2,1,0:T(8,128)(2,1)S(1)} collective-permute-done((bf16[1,176,1024]{2,1,0:T(8,128)(2,1)S(1)}, bf16[1,176,1024]{2,1,0:T(8,128)(2,1)S(1)}, u32[]{:S(2)}, u32[]{:S(2)}) %collective-permute-start.13) | collective-permute-done | bytes 360480 | tf_op jit(solution)/shard_map/ppermute | solution.py:340
  121.9 1.5 collective-permute-start.17
  123.3 4.7 %decode.11 = (f32[1,208,1024]{2,1,0:T(8,128)S(1)}, bf16[1,176,1024]{2,1,0:T(8,128)(2,1)S(1)}) custom-call(s32[2]{0:T(128)S(1)} %pad_add_fusion.2.info_ref, bf16[384,2048]{1,0:T(8,128)(2,1)S(1)} %encode.3.refs_0_, bf16[384,2048]{1,0:T(8,128)(2,1)S(1)} %collective-permute-done.7.refs_1_, bf16[2048,4096]{1,0:T(8,128)(2,1)} %bitcast.31, ...), custom_call_target="tpu_custom_call" | custom-call | tf_op jit(solution)/shard_map/decode/pallas_call | solution.py:245
  128.1 3.0 %collective-permute-done.19 = bf16[1,96,1024]{2,1,0:T(8,128)(2,1)S(1)} collective-permute-done((bf16[1,96,1024]{2,1,0:T(8,128)(2,1)S(1)}, bf16[1,96,1024]{2,1,0:T(8,128)(2,1)S(1)}, u32[]{:S(2)}, u32[]{:S(2)}) %collective-permute-start.19) | collective-permute-done | bytes 196640 | tf_op jit(solution)/shard_map/ppermute | solution.py:340
  131.1 2.7 %collective-permute-start.14 = (bf16[1,176,1024]{2,1,0:T(8,128)(2,1)S(1)}, bf16[1,176,1024]{2,1,0:T(8,128)(2,1)S(1)}, u32[]{:S(2)}, u32[]{:S(2)}) collective-permute-start(bf16[1,176,1024]{2,1,0:T(8,128)(2,1)S(1)} %get-tuple-element.42), channel_id=1, source_target_pairs={{0,2},{2,0},{1,3},{3,1},{4,6},{6,4},{5,7},{7,5},{8,10},{10,8},{9,1... | collective-permute-start | bytes 1081352 | tf_op jit(solution)/shard_map/ppermute | solution.py:335
  133.8 1.9 %collective-permute-done.18 = bf16[1,112,1024]{2,1,0:T(8,128)(2,1)S(1)} collective-permute-done((bf16[1,112,1024]{2,1,0:T(8,128)(2,1)S(1)}, bf16[1,112,1024]{2,1,0:T(8,128)(2,1)S(1)}, u32[]{:S(2)}, u32[]{:S(2)}) %collective-permute-start.18) | collective-permute-done | bytes 229408 | tf_op jit(solution)/shard_map/ppermute | solution.py:340
  135.9 2.0 %collective-permute-start.21 = (bf16[208,1024]{1,0:T(8,128)(2,1)S(1)}, bf16[208,1024]{1,0:T(8,128)(2,1)S(1)}, u32[]{:S(2)}, u32[]{:S(2)}) collective-permute-start(bf16[208,1024]{1,0:T(8,128)(2,1)S(1)} %fusion), channel_id=1, source_target_pairs={{0,2},{2,0},{1,3},{3,1},{4,6},{6,4},{5,7},{7,5},{8,10},{10,8},{9,1... | collective-permute-start | bytes 1277960 | tf_op jit(solution)/shard_map/ppermute | solution.py:335
  138.1 3.5 %collective-permute-done.14 = bf16[1,176,1024]{2,1,0:T(8,128)(2,1)S(1)} collective-permute-done((bf16[1,176,1024]{2,1,0:T(8,128)(2,1)S(1)}, bf16[1,176,1024]{2,1,0:T(8,128)(2,1)S(1)}, u32[]{:S(2)}, u32[]{:S(2)}) %collective-permute-start.14) | collective-permute-done | bytes 360480 | tf_op jit(solution)/shard_map/ppermute | solution.py:335
  141.6 4.6 %collective-permute-done.16 = bf16[1,176,1024]{2,1,0:T(8,128)(2,1)S(1)} collective-permute-done((bf16[1,176,1024]{2,1,0:T(8,128)(2,1)S(1)}, bf16[1,176,1024]{2,1,0:T(8,128)(2,1)S(1)}, u32[]{:S(2)}, u32[]{:S(2)}) %collective-permute-start.16) | collective-permute-done | bytes 360480 | tf_op jit(solution)/shard_map/ppermute | solution.py:340
  146.1 2.2 %collective-permute-done.21.refs_5_ = bf16[208,1024]{1,0:T(8,128)(2,1)S(1)} collective-permute-done((bf16[208,1024]{1,0:T(8,128)(2,1)S(1)}, bf16[208,1024]{1,0:T(8,128)(2,1)S(1)}, u32[]{:S(2)}, u32[]{:S(2)}) %collective-permute-start.21) | collective-permute-done | bytes 426016 | tf_op jit(solution)/shard_map/ppermute | solution.py:335
  148.3 1.6 finale.1
  150.0 2.0 %collective-permute-start.23 = (f32[8,128]{1,0:T(8,128)S(1)}, f32[8,128]{1,0:T(8,128)S(1)}, u32[]{:S(2)}, u32[]{:S(2)}) collective-permute-start(f32[8,128]{1,0:T(8,128)S(1)} %get-tuple-element.47), channel_id=1, source_target_pairs={{0,2},{1,3},{2,0},{3,1},{4,6},{5,7},{6,4},{7,5},{8,10},{9,11},{10,... | collective-permute-start | bytes 12296 | tf_op jit(solution)/shard_map/ppermute | solution.py:335
  152.2 1.4 collective-permute-done.23
  153.6 1.4 collective-permute-done.22
  155.5 1.5 collective-permute-start.25
  157.1 1.6 collective-permute-done.27.refs_3_
  158.6 1.0 collective-permute-done.26.refs_2_
  159.6 1.4 collective-permute-done.25.refs_1_
  161.7 1.2 mean_ratio.1
  (64 shorter events, 6.3 us)
Async XLA Ops:
  0.6 11.8 %copy-start = (bf16[1,4096]{1,0:T(2,128)(2,1)S(1)}, bf16[1,4096]{1,0:T(2,128)(2,1)}, u32[]{:S(2)}) copy-start(bf16[1,4096]{1,0:T(2,128)(2,1)} %param.10) | copy-start | bytes 24580
  3.4 4.8 %collective-permute-start = (f32[1]{0:T(128)}, f32[1]{0:T(128)}, u32[]{:S(2)}, u32[]{:S(2)}) collective-permute-start(f32[1]{0:T(128)} %get-tuple-element.25), channel_id=1, source_target_pairs={{0,2},{2,0},{1,3},{3,1},{4,6},{6,4},{5,7},{7,5},{8,10},{10,8},{9,1... | collective-permute-start | bytes 20 | tf_op jit(solution)/shard_map/ppermute | solution.py:335
  10.3 20.9 %collective-permute-start.3 = (bf16[96,4096]{1,0:T(8,128)(2,1)}, bf16[96,4096]{1,0:T(8,128)(2,1)}, u32[]{:S(2)}, u32[]{:S(2)}) collective-permute-start(bf16[96,4096]{1,0:T(8,128)(2,1)} %cut.2), channel_id=1, source_target_pairs={{0,2},{2,0},{1,3},{3,1},{4,6},{6,4},{5,7},{7,5},{8,10},{10,8},{9,1... | collective-permute-start | bytes 2359304 | tf_op jit(solution)/shard_map/ppermute | solution.py:335
  24.6 38.0 %collective-permute-start.5 = (bf16[192,4096]{1,0:T(8,128)(2,1)}, bf16[192,4096]{1,0:T(8,128)(2,1)S(1)}, u32[]{:S(2)}, u32[]{:S(2)}) collective-permute-start(bf16[192,4096]{1,0:T(8,128)(2,1)} %cut.3), channel_id=1, source_target_pairs={{0,2},{2,0},{1,3},{3,1},{4,6},{6,4},{5,7},{7,5},{8,10},{10,8},{9,1... | collective-permute-start | bytes 4718600 | tf_op jit(solution)/shard_map/ppermute | solution.py:335
  24.7 8.7 %collective-permute-start.2 = (bf16[384,1024]{1,0:T(8,128)(2,1)}, bf16[384,1024]{1,0:T(8,128)(2,1)S(1)}, u32[]{:S(2)}, u32[]{:S(2)}) collective-permute-start(bf16[384,1024]{1,0:T(8,128)(2,1)} %get-tuple-element.28.refs_1_), channel_id=1, source_target_pairs={{0,1},{2,3},{4,5},{6,7},{8,9},{10,11},{12,13},{14,15},{16,17},{18,... | collective-permute-start | bytes 2359304 | tf_op jit(solution)/shard_map/ppermute | solution.py:396
  26.1 7.3 %collective-permute-start.1 = (bf16[384,1024]{1,0:T(8,128)(2,1)}, bf16[384,1024]{1,0:T(8,128)(2,1)S(1)}, u32[]{:S(2)}, u32[]{:S(2)}) collective-permute-start(bf16[384,1024]{1,0:T(8,128)(2,1)} %get-tuple-element.27.refs_0_.after_ref), channel_id=1, source_target_pairs={{0,1},{2,3},{4,5},{6,7},{8,9},{10,11},{12,13},{14,15},{16,17},{18,... | collective-permute-start | bytes 2359304 | tf_op jit(solution)/shard_map/ppermute | solution.py:396
  31.2 26.5 %collective-permute-start.4 = (bf16[96,4096]{1,0:T(8,128)(2,1)}, bf16[96,4096]{1,0:T(8,128)(2,1)}, u32[]{:S(2)}, u32[]{:S(2)}) collective-permute-start(bf16[96,4096]{1,0:T(8,128)(2,1)} %collective-permute-done.3.refs_0_), channel_id=1, source_target_pairs={{0,4},{4,0},{8,12},{12,8},{1,5},{5,1},{9,13},{13,9},{2,6},{6,2},{1... | collective-permute-start | bytes 2359304 | tf_op jit(solution)/shard_map/ppermute | solution.py:340
  41.6 0.9 copy-start.3
  42.4 0.9 copy-start.5
  43.3 0.8 copy-start.8
  44.1 12.4 %collective-permute-start.6 = (bf16[1,208,1024]{2,1,0:T(8,128)(2,1)}, bf16[1,208,1024]{2,1,0:T(8,128)(2,1)}, u32[]{:S(2)}, u32[]{:S(2)}) collective-permute-start(bf16[1,208,1024]{2,1,0:T(8,128)(2,1)} %get-tuple-element.29.refs_6_), channel_id=1, source_target_pairs={{0,4},{4,0},{8,12},{12,8},{1,5},{5,1},{9,13},{13,9},{2,6},{6,2},{1... | collective-permute-start | bytes 1277960 | tf_op jit(solution)/shard_map/ppermute | solution.py:340
  57.7 17.0 %copy-start.9 = (bf16[1,208,1024]{2,1,0:T(8,128)(2,1)S(1)}, bf16[1,208,1024]{2,1,0:T(8,128)(2,1)}, u32[]{:S(2)}) copy-start(bf16[1,208,1024]{2,1,0:T(8,128)(2,1)} %copy-done.8) | copy-start | bytes 1277956
  73.2 6.0 %collective-permute-start.7 = (bf16[384,2048]{1,0:T(8,128)(2,1)S(1)}, bf16[384,2048]{1,0:T(8,128)(2,1)S(1)}, u32[]{:S(2)}, u32[]{:S(2)}) collective-permute-start(bf16[384,2048]{1,0:T(8,128)(2,1)S(1)} %encode.3.refs_0_), channel_id=1, source_target_pairs={{0,1},{2,3},{4,5},{6,7},{8,9},{10,11},{12,13},{14,15},{16,17},{18,... | collective-permute-start | bytes 4718600 | tf_op jit(solution)/shard_map/ppermute | solution.py:396
  74.6 21.0 %collective-permute-start.8 = (bf16[1,208,1024]{2,1,0:T(8,128)(2,1)S(1)}, bf16[1,208,1024]{2,1,0:T(8,128)(2,1)S(1)}, u32[]{:S(2)}, u32[]{:S(2)}) collective-permute-start(bf16[1,208,1024]{2,1,0:T(8,128)(2,1)S(1)} %copy-done.9), channel_id=1, source_target_pairs={{0,4},{4,0},{8,12},{12,8},{1,5},{5,1},{9,13},{13,9},{2,6},{6,2},{1... | collective-permute-start | bytes 1277960 | tf_op jit(solution)/shard_map/ppermute | solution.py:340
  76.5 19.4 %collective-permute-start.9 = (bf16[1,208,1024]{2,1,0:T(8,128)(2,1)S(1)}, bf16[1,208,1024]{2,1,0:T(8,128)(2,1)S(1)}, u32[]{:S(2)}, u32[]{:S(2)}) collective-permute-start(bf16[1,208,1024]{2,1,0:T(8,128)(2,1)S(1)} %add_convert_fusion.2.refs_4_), channel_id=1, source_target_pairs={{0,8},{4,12},{8,0},{12,4},{1,9},{5,13},{9,1},{13,5},{2,10},{6,14},... | collective-permute-start | bytes 1277960 | tf_op jit(solution)/shard_map/ppermute | solution.py:340
  83.7 18.5 %collective-permute-start.11 = (bf16[1,176,1024]{2,1,0:T(8,128)(2,1)S(1)}, bf16[1,176,1024]{2,1,0:T(8,128)(2,1)S(1)}, u32[]{:S(2)}, u32[]{:S(2)}) collective-permute-start(bf16[1,176,1024]{2,1,0:T(8,128)(2,1)S(1)} %get-tuple-element.37), channel_id=1, source_target_pairs={{0,2},{2,0},{1,3},{3,1},{4,6},{6,4},{5,7},{7,5},{8,10},{10,8},{9,1... | collective-permute-start | bytes 1081352 | tf_op jit(solution)/shard_map/ppermute | solution.py:335
  85.3 20.6 %collective-permute-start.10 = (bf16[1,208,1024]{2,1,0:T(8,128)(2,1)S(1)}, bf16[1,208,1024]{2,1,0:T(8,128)(2,1)S(1)}, u32[]{:S(2)}, u32[]{:S(2)}) collective-permute-start(bf16[1,208,1024]{2,1,0:T(8,128)(2,1)S(1)} %get-tuple-element.32.refs_4_), channel_id=1, source_target_pairs={{0,4},{4,0},{8,12},{12,8},{1,5},{5,1},{9,13},{13,9},{2,6},{6,2},{1... | collective-permute-start | bytes 1277960 | tf_op jit(solution)/shard_map/ppermute | solution.py:340
  96.2 6.1 %copy-start.6 = (f32[1,176,1024]{2,1,0:T(8,128)S(1)}, f32[1,176,1024]{2,1,0:T(8,128)}, u32[]{:S(2)}) copy-start(f32[1,176,1024]{2,1,0:T(8,128)} %copy-done.5) | copy-start | bytes 2162692
  100.7 12.2 %collective-permute-start.12 = (bf16[1,176,1024]{2,1,0:T(8,128)(2,1)S(1)}, bf16[1,176,1024]{2,1,0:T(8,128)(2,1)S(1)}, u32[]{:S(2)}, u32[]{:S(2)}) collective-permute-start(bf16[1,176,1024]{2,1,0:T(8,128)(2,1)S(1)} %get-tuple-element.41), channel_id=1, source_target_pairs={{0,2},{2,0},{1,3},{3,1},{4,6},{6,4},{5,7},{7,5},{8,10},{10,8},{9,1... | collective-permute-start | bytes 1081352 | tf_op jit(solution)/shard_map/ppermute | solution.py:335
  102.4 19.3 %collective-permute-start.13 = (bf16[1,176,1024]{2,1,0:T(8,128)(2,1)S(1)}, bf16[1,176,1024]{2,1,0:T(8,128)(2,1)S(1)}, u32[]{:S(2)}, u32[]{:S(2)}) collective-permute-start(bf16[1,176,1024]{2,1,0:T(8,128)(2,1)S(1)} %add_convert_fusion.5.refs_5_), channel_id=1, source_target_pairs={{0,4},{4,0},{8,12},{12,8},{1,5},{5,1},{9,13},{13,9},{2,6},{6,2},{1... | collective-permute-start | bytes 1081352 | tf_op jit(solution)/shard_map/ppermute | solution.py:340
  106.0 29.7 %collective-permute-start.20 = (bf16[1,208,1024]{2,1,0:T(8,128)(2,1)S(1)}, bf16[1,208,1024]{2,1,0:T(8,128)(2,1)S(1)}, u32[]{:S(2)}, u32[]{:S(2)}) collective-permute-start(bf16[1,208,1024]{2,1,0:T(8,128)(2,1)S(1)} %add_convert_fusion.1.refs_4_), channel_id=1, source_target_pairs={{0,8},{4,12},{8,0},{12,4},{1,9},{5,13},{9,1},{13,5},{2,10},{6,14},... | collective-permute-start | bytes 1277960 | tf_op jit(solution)/shard_map/ppermute | solution.py:340
  110.8 20.3 %collective-permute-start.19 = (bf16[1,96,1024]{2,1,0:T(8,128)(2,1)S(1)}, bf16[1,96,1024]{2,1,0:T(8,128)(2,1)S(1)}, u32[]{:S(2)}, u32[]{:S(2)}) collective-permute-start(bf16[1,96,1024]{2,1,0:T(8,128)(2,1)S(1)} %get-tuple-element.39.refs_5_), channel_id=1, source_target_pairs={{0,4},{4,0},{8,12},{12,8},{1,5},{5,1},{9,13},{13,9},{2,6},{6,2},{1... | collective-permute-start | bytes 589832 | tf_op jit(solution)/shard_map/ppermute | solution.py:340
  112.7 23.0 %collective-permute-start.18 = (bf16[1,112,1024]{2,1,0:T(8,128)(2,1)S(1)}, bf16[1,112,1024]{2,1,0:T(8,128)(2,1)S(1)}, u32[]{:S(2)}, u32[]{:S(2)}) collective-permute-start(bf16[1,112,1024]{2,1,0:T(8,128)(2,1)S(1)} %get-tuple-element.38.refs_4_), channel_id=1, source_target_pairs={{0,4},{4,0},{8,12},{12,8},{1,5},{5,1},{9,13},{13,9},{2,6},{6,2},{1... | collective-permute-start | bytes 688136 | tf_op jit(solution)/shard_map/ppermute | solution.py:340
  112.9 25.0 %collective-permute-start.15 = (bf16[1,176,1024]{2,1,0:T(8,128)(2,1)S(1)}, bf16[1,176,1024]{2,1,0:T(8,128)(2,1)S(1)}, u32[]{:S(2)}, u32[]{:S(2)}) collective-permute-start(bf16[1,176,1024]{2,1,0:T(8,128)(2,1)S(1)} %get-tuple-element.44), channel_id=1, source_target_pairs={{0,2},{2,0},{1,3},{3,1},{4,6},{6,4},{5,7},{7,5},{8,10},{10,8},{9,1... | collective-permute-start | bytes 1081352 | tf_op jit(solution)/shard_map/ppermute | solution.py:335
  121.8 16.1 %copy-start.4 = (f32[1,176,1024]{2,1,0:T(8,128)S(1)}, f32[1,176,1024]{2,1,0:T(8,128)}, u32[]{:S(2)}) copy-start(f32[1,176,1024]{2,1,0:T(8,128)} %copy-done.3) | copy-start | bytes 2162692
  121.9 16.2 %collective-permute-start.17 = (bf16[1,176,1024]{2,1,0:T(8,128)(2,1)S(1)}, bf16[1,176,1024]{2,1,0:T(8,128)(2,1)S(1)}, u32[]{:S(2)}, u32[]{:S(2)}) collective-permute-start(bf16[1,176,1024]{2,1,0:T(8,128)(2,1)S(1)} %add_convert_fusion.4.refs_6_), channel_id=1, source_target_pairs={{0,8},{4,12},{8,0},{12,4},{1,9},{5,13},{9,1},{13,5},{2,10},{6,14},... | collective-permute-start | bytes 1081352 | tf_op jit(solution)/shard_map/ppermute | solution.py:340
  128.0 20.3 %copy-start.2 = (bf16[1,384,1024]{2,1,0:T(8,128)(2,1)S(1)}, bf16[1,384,1024]{2,1,0:T(8,128)(2,1)}, u32[]{:S(2)}) copy-start(bf16[1,384,1024]{2,1,0:T(8,128)(2,1)} %param.8) | copy-start | bytes 2359300
  128.1 20.3 %copy-start.7 = (bf16[1,1024]{1,0:T(2,128)(2,1)S(1)}, bf16[1,1024]{1,0:T(2,128)(2,1)}, u32[]{:S(2)}) copy-start(bf16[1,1024]{1,0:T(2,128)(2,1)} %b_ref.1) | copy-start | bytes 6148
  131.1 10.4 %collective-permute-start.14 = (bf16[1,176,1024]{2,1,0:T(8,128)(2,1)S(1)}, bf16[1,176,1024]{2,1,0:T(8,128)(2,1)S(1)}, u32[]{:S(2)}, u32[]{:S(2)}) collective-permute-start(bf16[1,176,1024]{2,1,0:T(8,128)(2,1)S(1)} %get-tuple-element.42), channel_id=1, source_target_pairs={{0,2},{2,0},{1,3},{3,1},{4,6},{6,4},{5,7},{7,5},{8,10},{10,8},{9,1... | collective-permute-start | bytes 1081352 | tf_op jit(solution)/shard_map/ppermute | solution.py:335
  135.7 27.2 %copy-start.1 = (bf16[1,4096]{1,0:T(2,128)(2,1)S(1)}, bf16[1,4096]{1,0:T(2,128)(2,1)}, u32[]{:S(2)}) copy-start(bf16[1,4096]{1,0:T(2,128)(2,1)} %param.10) | copy-start | bytes 24580
  135.9 12.4 %collective-permute-start.21 = (bf16[208,1024]{1,0:T(8,128)(2,1)S(1)}, bf16[208,1024]{1,0:T(8,128)(2,1)S(1)}, u32[]{:S(2)}, u32[]{:S(2)}) collective-permute-start(bf16[208,1024]{1,0:T(8,128)(2,1)S(1)} %fusion), channel_id=1, source_target_pairs={{0,2},{2,0},{1,3},{3,1},{4,6},{6,4},{5,7},{7,5},{8,10},{10,8},{9,1... | collective-permute-start | bytes 1277960 | tf_op jit(solution)/shard_map/ppermute | solution.py:335
  138.0 8.1 %collective-permute-start.16 = (bf16[1,176,1024]{2,1,0:T(8,128)(2,1)S(1)}, bf16[1,176,1024]{2,1,0:T(8,128)(2,1)S(1)}, u32[]{:S(2)}, u32[]{:S(2)}) collective-permute-start(bf16[1,176,1024]{2,1,0:T(8,128)(2,1)S(1)} %add_convert_fusion.3), channel_id=1, source_target_pairs={{0,4},{4,0},{8,12},{12,8},{1,5},{5,1},{9,13},{13,9},{2,6},{6,2},{1... | collective-permute-start | bytes 1081352 | tf_op jit(solution)/shard_map/ppermute | solution.py:340
  150.0 2.3 %collective-permute-start.24 = (f32[8,128]{1,0:T(8,128)S(1)}, f32[8,128]{1,0:T(8,128)S(1)}, u32[]{:S(2)}, u32[]{:S(2)}) collective-permute-start(f32[8,128]{1,0:T(8,128)S(1)} %get-tuple-element.47), channel_id=1, source_target_pairs={{0,3},{1,0},{2,1},{3,2},{4,7},{5,4},{6,5},{7,6},{8,11},{9,8},{10,9... | collective-permute-start | bytes 12296 | tf_op jit(solution)/shard_map/ppermute | solution.py:335
  150.0 3.6 %collective-permute-start.23 = (f32[8,128]{1,0:T(8,128)S(1)}, f32[8,128]{1,0:T(8,128)S(1)}, u32[]{:S(2)}, u32[]{:S(2)}) collective-permute-start(f32[8,128]{1,0:T(8,128)S(1)} %get-tuple-element.47), channel_id=1, source_target_pairs={{0,2},{1,3},{2,0},{3,1},{4,6},{5,7},{6,4},{7,5},{8,10},{9,11},{10,... | collective-permute-start | bytes 12296 | tf_op jit(solution)/shard_map/ppermute | solution.py:335
  152.0 3.0 %collective-permute-start.22 = (f32[8,128]{1,0:T(8,128)S(1)}, f32[8,128]{1,0:T(8,128)S(1)}, u32[]{:S(2)}, u32[]{:S(2)}) collective-permute-start(f32[8,128]{1,0:T(8,128)S(1)} %get-tuple-element.47), channel_id=1, source_target_pairs={{0,1},{1,2},{2,3},{3,0},{4,5},{5,6},{6,7},{7,4},{8,9},{9,10},{10,1... | collective-permute-start | bytes 12296 | tf_op jit(solution)/shard_map/ppermute | solution.py:335
  155.0 6.0 %copy-start.10 = (f32[8,128]{1,0:T(8,128)}, f32[8,128]{1,0:T(8,128)S(1)}, u32[]{:S(2)}) copy-start(f32[8,128]{1,0:T(8,128)S(1)} %add_add_fusion.refs_0_) | copy-start | bytes 12292
  155.0 3.6 %collective-permute-start.27 = (f32[8,128]{1,0:T(8,128)S(1)}, f32[8,128]{1,0:T(8,128)S(1)}, u32[]{:S(2)}, u32[]{:S(2)}) collective-permute-start(f32[8,128]{1,0:T(8,128)S(1)} %add_add_fusion.refs_0_), channel_id=1, source_target_pairs={{0,12},{4,0},{8,4},{12,8},{1,13},{5,1},{9,5},{13,9},{2,14},{6,2},{... | collective-permute-start | bytes 12296 | tf_op jit(solution)/shard_map/ppermute | solution.py:335
  155.0 4.6 %collective-permute-start.26 = (f32[8,128]{1,0:T(8,128)S(1)}, f32[8,128]{1,0:T(8,128)S(1)}, u32[]{:S(2)}, u32[]{:S(2)}) collective-permute-start(f32[8,128]{1,0:T(8,128)S(1)} %add_add_fusion.refs_0_), channel_id=1, source_target_pairs={{0,8},{4,12},{8,0},{12,4},{1,9},{5,13},{9,1},{13,5},{2,10},{6,14},... | collective-permute-start | bytes 12296 | tf_op jit(solution)/shard_map/ppermute | solution.py:335
  155.5 5.5 %collective-permute-start.25 = (f32[8,128]{1,0:T(8,128)S(1)}, f32[8,128]{1,0:T(8,128)S(1)}, u32[]{:S(2)}, u32[]{:S(2)}) collective-permute-start(f32[8,128]{1,0:T(8,128)S(1)} %add_add_fusion.refs_0_), channel_id=1, source_target_pairs={{0,4},{4,8},{8,12},{12,0},{1,5},{5,9},{9,13},{13,1},{2,6},{6,10},{... | collective-permute-start | bytes 12296 | tf_op jit(solution)/shard_map/ppermute | solution.py:335
  158.6 2.4 %copy-start.11 = (f32[8,128]{1,0:T(8,128)}, f32[8,128]{1,0:T(8,128)S(1)}, u32[]{:S(2)}) copy-start(f32[8,128]{1,0:T(8,128)S(1)} %collective-permute-done.27.refs_3_) | copy-start | bytes 12292
  159.6 1.4 copy-start.12
  161.1 0.6 copy-start.13

commit v15 on v14

--- a/solution.py
+++ b/solution.py
@@ -309,6 +309,33 @@
         cost_estimate=COST,
         name="finale",
     )(layer.astype(jnp.int32).reshape(1), bias, target, *outer_terms, *inner_terms)
+
+
+def summed(terms, also):
+    n = len(terms)
+    shape = terms[0].shape
+
+    def body(*refs):
+        o_ref = refs[-1]
+
+        def block(r, carry):
+            here = pl.ds(pl.multiple_of(r * 16, 16), 16)
+            for g in range(shape[0]):
+                o_ref[g, here, :] = sum(ref[g, here, :].astype(jnp.float32) for ref in refs[:n])
+            return carry
+
+        lax.fori_loop(0, shape[1] // 16, block, 0)
+
+    vmem = pl.BlockSpec(memory_space=pltpu.VMEM)
+    return pl.pallas_call(
+        body,
+        in_specs=[vmem] * n + [pl.BlockSpec(memory_space=pl.ANY)] * len(also),
+        out_specs=vmem,
+        out_shape=jax.ShapeDtypeStruct(shape, jnp.float32),
+        compiler_params=pltpu.CompilerParams(vmem_limit_bytes=VMEM_LIMIT),
+        cost_estimate=COST,
+        name="summed",
+    )(*terms, *also)
 
 
 def mean_ratio(terms):
@@ -431,7 +458,8 @@
     far_kept, near_kept, far_out_kept, near_out_kept = products(
         codes, earlier, info(mine_bit, (far, near)), [span + (jnp.float32,) for span in spans], [far_sent])
     across_in = (far_kept + wide(far_in)).astype(narrow)
-    total_in = near_kept + wide(near_in) + wide(swapped(across_in, "latent", 2))
+    across_there = swapped(across_in, "latent", 2)
+    total_in = near_kept + wide(near_in)
 
     after = across_in
     returned = []
@@ -455,22 +483,25 @@
 
         (far_sent,), far_back = quarter_of(other, far, [inside], narrow, [])
         far_in = swapped(far_sent, "latent", 1)
-        (far_kept,), far_kept_back = quarter_of(mine_bit, far, [inside], jnp.float32, [far_sent, total_in])
+        halves = [inside]
+        near_sent, near_back = quarter_of(other, near, halves, narrow, [far_sent])
+        near_in = [swapped(rows_in, "latent", 1) for rows_in in near_sent]
+        near_in = jnp.concatenate(near_in, axis=1) if len(near_in) > 1 else near_in[0]
         far_out_back.append(far_back)
-        ready = [(far_kept + wide(far_in)).astype(narrow)]
-        across = swapped(ready[0], "latent", 2)
+        pins = list(near_sent)
+        if not returned:
+            total_in = summed([total_in, across_there], near_sent)
+            pins.append(total_in)
         if len(far_out_back) == n_tok - 1:
-            ready.append(joined(far_out_sent, far_out_back).astype(narrow))
-            far_out = swapped(ready[1], "latent", 1)
-        cut_at = (middle // 2 + 15) // 16 * 16
-        halves = [((first, cut_at),), ((first + cut_at, middle - cut_at),)]
-        near_sent, near_back = quarter_of(other, near, halves, narrow, ready)
-        near_in = jnp.concatenate([swapped(rows_in, "latent", 1) for rows_in in near_sent], axis=1)
+            pins.append(joined(far_out_sent, far_out_back).astype(narrow))
+            far_out = swapped(pins[-1], "latent", 1)
+        (far_kept,), far_kept_back = quarter_of(mine_bit, far, [inside], jnp.float32, pins)
+        pins = [(far_kept + wide(far_in)).astype(narrow)]
+        across = swapped(pins[0], "latent", 2)
         far_out_kept = far_out_kept + wide(far_kept_back)
-        pins = list(near_sent)
         if len(far_out_back) == n_tok - 1:
             far_out_kept = (far_out_kept + wide(far_out)).astype(narrow)
-            pins.append(far_out_kept)
+
         (near_kept,), near_kept_back = quarter_of(mine_bit, near, [inside], jnp.float32, pins)
         part = finish(near_kept + wide(near_in) + wide(across))
         returned.append(shifted(part.astype(narrow), "token", back))

time: 163 us -> 165 us (1.012)
  waiting for transfers between devices: 55.1 us -> 59.8 us
  starting transfers between devices: 36.8 us -> 34.4 us
    ppermute x11 -> x10, waiting for transfers between devices: 32.3 us -> 41.8 us  [swapped(): return lax.ppermute(value, axis, [(i, i ^ bit) for i in range(n)])]
    ppermute x14, waiting for transfers between devices: 22.8 us -> 18 us  [shifted(): lax.ppermute(value, axis, [(i, (i + distance) % n) for i in range(n)])]
    ppermute x14, starting transfers between devices: 18.5 us -> 15.8 us  [shifted(): lax.ppermute(value, axis, [(i, (i + distance) % n) for i in range(n)])]
    ppermute x11 -> x10, starting transfers between devices: 14.3 us -> 14.6 us  [swapped(): return lax.ppermute(value, axis, [(i, i ^ bit) for i in range(n)])]
  transfers between devices with their start and end apart: 28 -> 27, of which waited for: 17 -> 13; matrix products, arithmetic and copies ran while one was open for 1% -> 1% of each run, Pallas kernels for 28% -> 28%
where the time goes in v15:
time: 165 us
  Pallas kernels  63.2 us (38%)
  waiting for transfers between devices  59.8 us (36%)
  starting transfers between devices  34.4 us (21%)
  local copies, waits for them, and re-layouts  3.19 us (2%)
  between operations  2.35 us (1%)
  other arithmetic  2.2 us (1%)
    ppermute x10, waiting for transfers between devices, swapped(): return lax.ppermute(value, axis, [(i, i ^ bit) for i in range(n)])  41.8 us
    pallas_call x6, Pallas kernels, decode(): pl.pallas_call(body, in_specs=[pl.BlockSpec(memory_space=pltpu.SMEM)] + [...  33.8 us
    pallas_call x2, Pallas kernels, encode(): pl.pallas_call(body, in_specs=[pl.BlockSpec(memory_space=pltpu.SMEM), pl....  21.6 us
    ppermute x14, waiting for transfers between devices, shifted(): lax.ppermute(value, axis, [(i, (i + distance) % n) for i in range(n)])  18 us
    ppermute x14, starting transfers between devices, shifted(): lax.ppermute(value, axis, [(i, (i + distance) % n) for i in range(n)])  15.8 us
    ppermute x10, starting transfers between devices, swapped(): return lax.ppermute(value, axis, [(i, i ^ bit) for i in range(n)])  14.6 us
    ppermute x3, starting transfers between devices, earlier_of(): return [lax.ppermute(part, 'layer', [(0, 1)]) for part in codes]  4.06 us
  transfers between devices with their start and end apart: 27, of which 13 were waited for; matrix products, arithmetic and copies ran while one was open for 1% of the time, Pallas kernels for 28%

profile of v15, /device:TPU:0, one launch (start us, length us, event | category | flops | bytes accessed | tf_op | source)
XLA Modules:
  0.0 165.2 jit_solution(6174981264442612366)
XLA Ops:
  0.6 2.7 %square_sum.1 = (f32[1]{0:T(128)}, bf16[384,4096]{1,0:T(8,128)(2,1)S(1)}) custom-call(bf16[384,4096]{1,0:T(8,128)(2,1)} %bitcast.34), custom_call_target="tpu_custom_call" | custom-call | tf_op jit(solution)/shard_map/square_sum/pallas_call | solution.py:47
  3.4 3.0 %collective-permute-start = (f32[1]{0:T(128)}, f32[1]{0:T(128)}, u32[]{:S(2)}, u32[]{:S(2)}) collective-permute-start(f32[1]{0:T(128)} %get-tuple-element.24), channel_id=1, source_target_pairs={{0,2},{2,0},{1,3},{3,1},{4,6},{6,4},{5,7},{7,5},{8,10},{10,8},{9,1... | collective-permute-start | bytes 20 | tf_op jit(solution)/shard_map/ppermute | solution.py:362
  6.4 1.8 %collective-permute-done = f32[1]{0:T(128)} collective-permute-done((f32[1]{0:T(128)}, f32[1]{0:T(128)}, u32[]{:S(2)}, u32[]{:S(2)}) %collective-permute-start) | collective-permute-done | bytes 36 | tf_op jit(solution)/shard_map/ppermute | solution.py:362
  9.4 0.9 cut.2
  10.3 2.1 %collective-permute-start.3 = (bf16[96,4096]{1,0:T(8,128)(2,1)}, bf16[96,4096]{1,0:T(8,128)(2,1)}, u32[]{:S(2)}, u32[]{:S(2)}) collective-permute-start(bf16[96,4096]{1,0:T(8,128)(2,1)} %cut.2), channel_id=1, source_target_pairs={{0,2},{2,0},{1,3},{3,1},{4,6},{6,4},{5,7},{7,5},{8,10},{10,8},{9,1... | collective-permute-start | bytes 2359304 | tf_op jit(solution)/shard_map/ppermute | solution.py:362
  12.5 10.9 %encode.2 = (bf16[384,1024]{1,0:T(8,128)(2,1)}, bf16[384,1024]{1,0:T(8,128)(2,1)}) custom-call(s32[1]{0:T(128)} %constant.58.clone.1.places_ref, f32[1]{0:T(128)S(6)} %sqrt.3.inv_ref, bf16[1,2048]{1,0:T(2,128)(2,1)S(1)} %constant_dynamic-slice_fusion.b_ref, bf16[384,4096]{1,0:T(8,128)(2,1)S(1)} %get-tuple-element.25.refs_0_.x_ref, bf16[4096,2048]{1,0:T(8,128)(2,1)} %bitcast.32), custom_call_target="tpu_custom_call" | custom-call | tf_op jit(solution)/shard_map/encode/pallas_call | solution.py:146
  23.4 1.2 cut.3
  24.7 1.3 collective-permute-start.2
  26.1 1.3 collective-permute-start.1
  27.5 3.7 %collective-permute-done.3.refs_0_ = bf16[96,4096]{1,0:T(8,128)(2,1)} collective-permute-done((bf16[96,4096]{1,0:T(8,128)(2,1)}, bf16[96,4096]{1,0:T(8,128)(2,1)}, u32[]{:S(2)}, u32[]{:S(2)}) %collective-permute-start.3) | collective-permute-done | bytes 786464 | tf_op jit(solution)/shard_map/ppermute | solution.py:362
  31.2 2.1 %collective-permute-start.4 = (bf16[96,4096]{1,0:T(8,128)(2,1)}, bf16[96,4096]{1,0:T(8,128)(2,1)}, u32[]{:S(2)}, u32[]{:S(2)}) collective-permute-start(bf16[96,4096]{1,0:T(8,128)(2,1)} %collective-permute-done.3.refs_0_), channel_id=1, source_target_pairs={{0,4},{4,0},{8,12},{12,8},{1,5},{5,1},{9,13},{13,9},{2,6},{6,2},{1... | collective-permute-start | bytes 2359304 | tf_op jit(solution)/shard_map/ppermute | solution.py:367
  33.4 8.2 %decode.6 = (bf16[1,208,1024]{2,1,0:T(8,128)(2,1)}, bf16[1,208,1024]{2,1,0:T(8,128)(2,1)S(1)}, f32[1,176,1024]{2,1,0:T(8,128)S(1)}, f32[1,176,1024]{2,1,0:T(8,128)S(1)}) custom-call(s32[3]{0:T(128)S(1)} %get-tuple-element.47.info_ref, bf16[384,1024]{1,0:T(8,128)(2,1)} %get-tuple-element.26.refs_0_.after_ref, bf16[384,1024]{1,0:T(8,128)(2,1)} %get-tuple-element.27.refs_1_, ...), custom_call_target="tpu_custom_call" | custom-call | tf_op jit(solution)/shard_map/decode/pallas_call | solution.py:245
  41.6 0.9 copy-done.3
  42.4 0.9 copy-done.5
  43.3 0.8 copy-done.8
  44.2 7.4 %decode.7 = (f32[1,208,1024]{2,1,0:T(8,128)S(1)}, f32[1,208,1024]{2,1,0:T(8,128)S(1)}, f32[1,176,1024]{2,1,0:T(8,128)S(1)}, f32[1,176,1024]{2,1,0:T(8,128)S(1)}) custom-call(s32[3]{0:T(128)S(1)} %get-tuple-element.46.info_ref, bf16[384,1024]{1,0:T(8,128)(2,1)} %get-tuple-element.26.refs_0_.after_ref, bf16[384,1024]{1,0:T(8,128)(2,1)} %get-tuple-element.27.refs_1_, ...), custom_call_target="tpu_custom_call" | custom-call | tf_op jit(solution)/shard_map/decode/pallas_call | solution.py:245
  51.6 4.9 %collective-permute-done.6 = bf16[1,208,1024]{2,1,0:T(8,128)(2,1)} collective-permute-done((bf16[1,208,1024]{2,1,0:T(8,128)(2,1)}, bf16[1,208,1024]{2,1,0:T(8,128)(2,1)}, u32[]{:S(2)}, u32[]{:S(2)}) %collective-permute-start.6) | collective-permute-done | bytes 426016 | tf_op jit(solution)/shard_map/ppermute | solution.py:367
  56.6 1.1 add_convert_fusion.2.refs_4_
  57.7 4.9 %collective-permute-done.5.refs_2_ = bf16[192,4096]{1,0:T(8,128)(2,1)S(1)} collective-permute-done((bf16[192,4096]{1,0:T(8,128)(2,1)}, bf16[192,4096]{1,0:T(8,128)(2,1)S(1)}, u32[]{:S(2)}, u32[]{:S(2)}) %collective-permute-start.5) | collective-permute-done | bytes 1572896 | tf_op jit(solution)/shard_map/ppermute | solution.py:362
  62.6 10.6 %encode.3.refs_0_ = bf16[384,2048]{1,0:T(8,128)(2,1)S(1)} custom-call(s32[3]{0:T(128)S(1)} %pad_add_fusion.3.places_ref, f32[1]{0:T(128)S(6)} %sqrt.3.inv_ref, bf16[1,2048]{1,0:T(2,128)(2,1)S(1)} %constant_dynamic-slice_fusion.b_ref, bf16[96,4096]{1,0:T(8,128)(2,1)} %collective-permute-done.3.refs_0_, bf16[96,4096]{1,0:T(8,128)(2,1)} %collective-permute-done.4.refs_1_, ...), custom_call_target="tpu_custom_call" | custom-call | tf_op jit(solution)/shard_map/encode/pallas_call | solution.py:146
  73.2 1.4 collective-permute-start.7
  74.6 1.9 %collective-permute-start.8 = (bf16[1,208,1024]{2,1,0:T(8,128)(2,1)S(1)}, bf16[1,208,1024]{2,1,0:T(8,128)(2,1)S(1)}, u32[]{:S(2)}, u32[]{:S(2)}) collective-permute-start(bf16[1,208,1024]{2,1,0:T(8,128)(2,1)S(1)} %copy-done.9), channel_id=1, source_target_pairs={{0,4},{4,0},{8,12},{12,8},{1,5},{5,1},{9,13},{13,9},{2,6},{6,2},{1... | collective-permute-start | bytes 1277960 | tf_op jit(solution)/shard_map/ppermute | solution.py:367
  76.5 2.6 %collective-permute-start.9 = (bf16[1,208,1024]{2,1,0:T(8,128)(2,1)S(1)}, bf16[1,208,1024]{2,1,0:T(8,128)(2,1)S(1)}, u32[]{:S(2)}, u32[]{:S(2)}) collective-permute-start(bf16[1,208,1024]{2,1,0:T(8,128)(2,1)S(1)} %add_convert_fusion.2.refs_4_), channel_id=1, source_target_pairs={{0,8},{4,12},{8,0},{12,4},{1,9},{5,13},{9,1},{13,5},{2,10},{6,14},... | collective-permute-start | bytes 1277960 | tf_op jit(solution)/shard_map/ppermute | solution.py:367
  79.2 4.5 %decode.8 = (bf16[1,208,1024]{2,1,0:T(8,128)(2,1)S(1)}, bf16[1,176,1024]{2,1,0:T(8,128)(2,1)S(1)}) custom-call(s32[2]{0:T(128)S(1)} %get-tuple-element.49.info_ref, bf16[384,2048]{1,0:T(8,128)(2,1)S(1)} %encode.3.refs_0_, bf16[384,2048]{1,0:T(8,128)(2,1)S(1)} %collective-permute-done.7.refs_1_, bf16[2048,4096]{1,0:T(8,128)(2,1)} %bitcast.28, ...), custom_call_target="tpu_custom_call" | custom-call | tf_op jit(solution)/shard_map/decode/pallas_call | solution.py:245
  83.7 1.6 collective-permute-start.10
  85.8 9.9 %collective-permute-done.8 = bf16[1,208,1024]{2,1,0:T(8,128)(2,1)S(1)} collective-permute-done((bf16[1,208,1024]{2,1,0:T(8,128)(2,1)S(1)}, bf16[1,208,1024]{2,1,0:T(8,128)(2,1)S(1)}, u32[]{:S(2)}, u32[]{:S(2)}) %collective-permute-start.8) | collective-permute-done | bytes 426016 | tf_op jit(solution)/shard_map/ppermute | solution.py:367
  95.8 4.5 %decode.9 = (bf16[1,208,1024]{2,1,0:T(8,128)(2,1)S(1)}, bf16[1,176,1024]{2,1,0:T(8,128)(2,1)S(1)}) custom-call(s32[2]{0:T(128)S(1)} %get-tuple-element.48.info_ref, bf16[384,2048]{1,0:T(8,128)(2,1)S(1)} %encode.3.refs_0_, bf16[384,2048]{1,0:T(8,128)(2,1)S(1)} %collective-permute-done.7.refs_1_, bf16[2048,4096]{1,0:T(8,128)(2,1)} %bitcast.29, ...), custom_call_target="tpu_custom_call" | custom-call | tf_op jit(solution)/shard_map/decode/pallas_call | solution.py:245
  100.3 1.6 collective-permute-start.13
  102.2 4.5 %decode.10 = (f32[1,208,1024]{2,1,0:T(8,128)S(1)}, bf16[1,176,1024]{2,1,0:T(8,128)(2,1)S(1)}) custom-call(s32[2]{0:T(128)S(1)} %pad_add_fusion.4.info_ref, bf16[384,2048]{1,0:T(8,128)(2,1)S(1)} %encode.3.refs_0_, bf16[384,2048]{1,0:T(8,128)(2,1)S(1)} %collective-permute-done.7.refs_1_, bf16[2048,4096]{1,0:T(8,128)(2,1)} %bitcast.30, ...), custom_call_target="tpu_custom_call" | custom-call | tf_op jit(solution)/shard_map/decode/pallas_call | solution.py:245
  106.8 3.1 %collective-permute-start.19 = (bf16[1,208,1024]{2,1,0:T(8,128)(2,1)S(1)}, bf16[1,208,1024]{2,1,0:T(8,128)(2,1)S(1)}, u32[]{:S(2)}, u32[]{:S(2)}) collective-permute-start(bf16[1,208,1024]{2,1,0:T(8,128)(2,1)S(1)} %add_convert_fusion.1.refs_4_), channel_id=1, source_target_pairs={{0,8},{4,12},{8,0},{12,4},{1,9},{5,13},{9,1},{13,5},{2,10},{6,14},... | collective-permute-start | bytes 1277960 | tf_op jit(solution)/shard_map/ppermute | solution.py:367
  110.7 2.0 %collective-permute-start.14 = (bf16[1,176,1024]{2,1,0:T(8,128)(2,1)S(1)}, bf16[1,176,1024]{2,1,0:T(8,128)(2,1)S(1)}, u32[]{:S(2)}, u32[]{:S(2)}) collective-permute-start(bf16[1,176,1024]{2,1,0:T(8,128)(2,1)S(1)} %add_convert_fusion.4), channel_id=1, source_target_pairs={{0,4},{4,0},{8,12},{12,8},{1,5},{5,1},{9,13},{13,9},{2,6},{6,2},{1... | collective-permute-start | bytes 1081352 | tf_op jit(solution)/shard_map/ppermute | solution.py:367
  112.7 4.7 %decode.11 = (f32[1,208,1024]{2,1,0:T(8,128)S(1)}, bf16[1,176,1024]{2,1,0:T(8,128)(2,1)S(1)}) custom-call(s32[2]{0:T(128)S(1)} %pad_add_fusion.2.info_ref, bf16[384,2048]{1,0:T(8,128)(2,1)S(1)} %encode.3.refs_0_, bf16[384,2048]{1,0:T(8,128)(2,1)S(1)} %collective-permute-done.7.refs_1_, bf16[2048,4096]{1,0:T(8,128)(2,1)} %bitcast.31, ...), custom_call_target="tpu_custom_call" | custom-call | tf_op jit(solution)/shard_map/decode/pallas_call | solution.py:245
  117.4 1.5 collective-permute-start.12
  119.0 10.3 %collective-permute-done.19 = bf16[1,208,1024]{2,1,0:T(8,128)(2,1)S(1)} collective-permute-done((bf16[1,208,1024]{2,1,0:T(8,128)(2,1)S(1)}, bf16[1,208,1024]{2,1,0:T(8,128)(2,1)S(1)}, u32[]{:S(2)}, u32[]{:S(2)}) %collective-permute-start.19) | collective-permute-done | bytes 426016 | tf_op jit(solution)/shard_map/ppermute | solution.py:367
  129.5 0.7 collective-permute-start.20
  130.3 2.4 %collective-permute-start.17 = (bf16[1,176,1024]{2,1,0:T(8,128)(2,1)S(1)}, bf16[1,176,1024]{2,1,0:T(8,128)(2,1)S(1)}, u32[]{:S(2)}, u32[]{:S(2)}) collective-permute-start(bf16[1,176,1024]{2,1,0:T(8,128)(2,1)S(1)} %add_convert_fusion.3), channel_id=1, source_target_pairs={{0,8},{4,12},{8,0},{12,4},{1,9},{5,13},{9,1},{13,5},{2,10},{6,14},... | collective-permute-start | bytes 1081352 | tf_op jit(solution)/shard_map/ppermute | solution.py:367
  132.7 8.4 %collective-permute-done.14 = bf16[1,176,1024]{2,1,0:T(8,128)(2,1)S(1)} collective-permute-done((bf16[1,176,1024]{2,1,0:T(8,128)(2,1)S(1)}, bf16[1,176,1024]{2,1,0:T(8,128)(2,1)S(1)}, u32[]{:S(2)}, u32[]{:S(2)}) %collective-permute-start.14) | collective-permute-done | bytes 360480 | tf_op jit(solution)/shard_map/ppermute | solution.py:367
  141.1 8.3 %collective-permute-done.17 = bf16[1,176,1024]{2,1,0:T(8,128)(2,1)S(1)} collective-permute-done((bf16[1,176,1024]{2,1,0:T(8,128)(2,1)S(1)}, bf16[1,176,1024]{2,1,0:T(8,128)(2,1)S(1)}, u32[]{:S(2)}, u32[]{:S(2)}) %collective-permute-start.17) | collective-permute-done | bytes 360480 | tf_op jit(solution)/shard_map/ppermute | solution.py:367
  149.4 1.6 finale.1
  151.3 1.2 collective-permute-start.22
  152.7 2.2 %collective-permute-done.22 = f32[8,128]{1,0:T(8,128)S(1)} collective-permute-done((f32[8,128]{1,0:T(8,128)S(1)}, f32[8,128]{1,0:T(8,128)S(1)}, u32[]{:S(2)}, u32[]{:S(2)}) %collective-permute-start.22) | collective-permute-done | bytes 4128 | tf_op jit(solution)/shard_map/ppermute | solution.py:362
  154.9 0.6 collective-permute-done.21
  155.5 2.4 %collective-permute-start.26 = (f32[8,128]{1,0:T(8,128)S(1)}, f32[8,128]{1,0:T(8,128)S(1)}, u32[]{:S(2)}, u32[]{:S(2)}) collective-permute-start(f32[8,128]{1,0:T(8,128)S(1)} %add_add_fusion.refs_0_), channel_id=1, source_target_pairs={{0,12},{4,0},{8,4},{12,8},{1,13},{5,1},{9,5},{13,9},{2,14},{6,2},{... | collective-permute-start | bytes 12296 | tf_op jit(solution)/shard_map/ppermute | solution.py:362
  157.9 0.6 collective-permute-start.24
  158.6 0.7 collective-permute-done.26.refs_3_
  159.3 3.2 %collective-permute-done.25.refs_2_ = f32[8,128]{1,0:T(8,128)S(1)} collective-permute-done((f32[8,128]{1,0:T(8,128)S(1)}, f32[8,128]{1,0:T(8,128)S(1)}, u32[]{:S(2)}, u32[]{:S(2)}) %collective-permute-start.25) | collective-permute-done | bytes 4128 | tf_op jit(solution)/shard_map/ppermute | solution.py:362
  162.4 0.9 collective-permute-done.24.refs_1_
  163.9 1.2 mean_ratio.1
  (62 shorter events, 3.6 us)
Async XLA Ops:
  0.6 11.8 %copy-start = (bf16[1,4096]{1,0:T(2,128)(2,1)S(1)}, bf16[1,4096]{1,0:T(2,128)(2,1)}, u32[]{:S(2)}) copy-start(bf16[1,4096]{1,0:T(2,128)(2,1)} %param.10) | copy-start | bytes 24580
  3.4 4.8 %collective-permute-start = (f32[1]{0:T(128)}, f32[1]{0:T(128)}, u32[]{:S(2)}, u32[]{:S(2)}) collective-permute-start(f32[1]{0:T(128)} %get-tuple-element.24), channel_id=1, source_target_pairs={{0,2},{2,0},{1,3},{3,1},{4,6},{6,4},{5,7},{7,5},{8,10},{10,8},{9,1... | collective-permute-start | bytes 20 | tf_op jit(solution)/shard_map/ppermute | solution.py:362
  10.3 20.9 %collective-permute-start.3 = (bf16[96,4096]{1,0:T(8,128)(2,1)}, bf16[96,4096]{1,0:T(8,128)(2,1)}, u32[]{:S(2)}, u32[]{:S(2)}) collective-permute-start(bf16[96,4096]{1,0:T(8,128)(2,1)} %cut.2), channel_id=1, source_target_pairs={{0,2},{2,0},{1,3},{3,1},{4,6},{6,4},{5,7},{7,5},{8,10},{10,8},{9,1... | collective-permute-start | bytes 2359304 | tf_op jit(solution)/shard_map/ppermute | solution.py:362
  24.6 38.0 %collective-permute-start.5 = (bf16[192,4096]{1,0:T(8,128)(2,1)}, bf16[192,4096]{1,0:T(8,128)(2,1)S(1)}, u32[]{:S(2)}, u32[]{:S(2)}) collective-permute-start(bf16[192,4096]{1,0:T(8,128)(2,1)} %cut.3), channel_id=1, source_target_pairs={{0,2},{2,0},{1,3},{3,1},{4,6},{6,4},{5,7},{7,5},{8,10},{10,8},{9,1... | collective-permute-start | bytes 4718600 | tf_op jit(solution)/shard_map/ppermute | solution.py:362
  24.7 8.7 %collective-permute-start.2 = (bf16[384,1024]{1,0:T(8,128)(2,1)}, bf16[384,1024]{1,0:T(8,128)(2,1)S(1)}, u32[]{:S(2)}, u32[]{:S(2)}) collective-permute-start(bf16[384,1024]{1,0:T(8,128)(2,1)} %get-tuple-element.27.refs_1_), channel_id=1, source_target_pairs={{0,1},{2,3},{4,5},{6,7},{8,9},{10,11},{12,13},{14,15},{16,17},{18,... | collective-permute-start | bytes 2359304 | tf_op jit(solution)/shard_map/ppermute | solution.py:423
  26.1 7.3 %collective-permute-start.1 = (bf16[384,1024]{1,0:T(8,128)(2,1)}, bf16[384,1024]{1,0:T(8,128)(2,1)S(1)}, u32[]{:S(2)}, u32[]{:S(2)}) collective-permute-start(bf16[384,1024]{1,0:T(8,128)(2,1)} %get-tuple-element.26.refs_0_.after_ref), channel_id=1, source_target_pairs={{0,1},{2,3},{4,5},{6,7},{8,9},{10,11},{12,13},{14,15},{16,17},{18,... | collective-permute-start | bytes 2359304 | tf_op jit(solution)/shard_map/ppermute | solution.py:423
  31.2 26.5 %collective-permute-start.4 = (bf16[96,4096]{1,0:T(8,128)(2,1)}, bf16[96,4096]{1,0:T(8,128)(2,1)}, u32[]{:S(2)}, u32[]{:S(2)}) collective-permute-start(bf16[96,4096]{1,0:T(8,128)(2,1)} %collective-permute-done.3.refs_0_), channel_id=1, source_target_pairs={{0,4},{4,0},{8,12},{12,8},{1,5},{5,1},{9,13},{13,9},{2,6},{6,2},{1... | collective-permute-start | bytes 2359304 | tf_op jit(solution)/shard_map/ppermute | solution.py:367
  41.6 0.9 copy-start.3
  42.4 0.9 copy-start.5
  43.3 0.8 copy-start.8
  44.1 12.4 %collective-permute-start.6 = (bf16[1,208,1024]{2,1,0:T(8,128)(2,1)}, bf16[1,208,1024]{2,1,0:T(8,128)(2,1)}, u32[]{:S(2)}, u32[]{:S(2)}) collective-permute-start(bf16[1,208,1024]{2,1,0:T(8,128)(2,1)} %get-tuple-element.28.refs_6_), channel_id=1, source_target_pairs={{0,4},{4,0},{8,12},{12,8},{1,5},{5,1},{9,13},{13,9},{2,6},{6,2},{1... | collective-permute-start | bytes 1277960 | tf_op jit(solution)/shard_map/ppermute | solution.py:367
  57.7 17.0 %copy-start.9 = (bf16[1,208,1024]{2,1,0:T(8,128)(2,1)S(1)}, bf16[1,208,1024]{2,1,0:T(8,128)(2,1)}, u32[]{:S(2)}) copy-start(bf16[1,208,1024]{2,1,0:T(8,128)(2,1)} %copy-done.8) | copy-start | bytes 1277956
  73.2 6.0 %collective-permute-start.7 = (bf16[384,2048]{1,0:T(8,128)(2,1)S(1)}, bf16[384,2048]{1,0:T(8,128)(2,1)S(1)}, u32[]{:S(2)}, u32[]{:S(2)}) collective-permute-start(bf16[384,2048]{1,0:T(8,128)(2,1)S(1)} %encode.3.refs_0_), channel_id=1, source_target_pairs={{0,1},{2,3},{4,5},{6,7},{8,9},{10,11},{12,13},{14,15},{16,17},{18,... | collective-permute-start | bytes 4718600 | tf_op jit(solution)/shard_map/ppermute | solution.py:423
  74.6 21.0 %collective-permute-start.8 = (bf16[1,208,1024]{2,1,0:T(8,128)(2,1)S(1)}, bf16[1,208,1024]{2,1,0:T(8,128)(2,1)S(1)}, u32[]{:S(2)}, u32[]{:S(2)}) collective-permute-start(bf16[1,208,1024]{2,1,0:T(8,128)(2,1)S(1)} %copy-done.9), channel_id=1, source_target_pairs={{0,4},{4,0},{8,12},{12,8},{1,5},{5,1},{9,13},{13,9},{2,6},{6,2},{1... | collective-permute-start | bytes 1277960 | tf_op jit(solution)/shard_map/ppermute | solution.py:367
  76.5 25.4 %collective-permute-start.9 = (bf16[1,208,1024]{2,1,0:T(8,128)(2,1)S(1)}, bf16[1,208,1024]{2,1,0:T(8,128)(2,1)S(1)}, u32[]{:S(2)}, u32[]{:S(2)}) collective-permute-start(bf16[1,208,1024]{2,1,0:T(8,128)(2,1)S(1)} %add_convert_fusion.2.refs_4_), channel_id=1, source_target_pairs={{0,8},{4,12},{8,0},{12,4},{1,9},{5,13},{9,1},{13,5},{2,10},{6,14},... | collective-permute-start | bytes 1277960 | tf_op jit(solution)/shard_map/ppermute | solution.py:367
  83.7 18.3 %collective-permute-start.10 = (bf16[1,176,1024]{2,1,0:T(8,128)(2,1)S(1)}, bf16[1,176,1024]{2,1,0:T(8,128)(2,1)S(1)}, u32[]{:S(2)}, u32[]{:S(2)}) collective-permute-start(bf16[1,176,1024]{2,1,0:T(8,128)(2,1)S(1)} %get-tuple-element.36), channel_id=1, source_target_pairs={{0,2},{2,0},{1,3},{3,1},{4,6},{6,4},{5,7},{7,5},{8,10},{10,8},{9,1... | collective-permute-start | bytes 1081352 | tf_op jit(solution)/shard_map/ppermute | solution.py:362
  85.3 21.3 %collective-permute-start.11 = (bf16[1,208,1024]{2,1,0:T(8,128)(2,1)S(1)}, bf16[1,208,1024]{2,1,0:T(8,128)(2,1)S(1)}, u32[]{:S(2)}, u32[]{:S(2)}) collective-permute-start(bf16[1,208,1024]{2,1,0:T(8,128)(2,1)S(1)} %get-tuple-element.31.refs_4_), channel_id=1, source_target_pairs={{0,4},{4,0},{8,12},{12,8},{1,5},{5,1},{9,13},{13,9},{2,6},{6,2},{1... | collective-permute-start | bytes 1277960 | tf_op jit(solution)/shard_map/ppermute | solution.py:367
  95.8 6.2 %copy-start.6 = (f32[1,176,1024]{2,1,0:T(8,128)S(1)}, f32[1,176,1024]{2,1,0:T(8,128)}, u32[]{:S(2)}) copy-start(f32[1,176,1024]{2,1,0:T(8,128)} %copy-done.5) | copy-start | bytes 2162692
  100.3 10.2 %collective-permute-start.13 = (bf16[1,176,1024]{2,1,0:T(8,128)(2,1)S(1)}, bf16[1,176,1024]{2,1,0:T(8,128)(2,1)S(1)}, u32[]{:S(2)}, u32[]{:S(2)}) collective-permute-start(bf16[1,176,1024]{2,1,0:T(8,128)(2,1)S(1)} %get-tuple-element.40), channel_id=1, source_target_pairs={{0,2},{2,0},{1,3},{3,1},{4,6},{6,4},{5,7},{7,5},{8,10},{10,8},{9,1... | collective-permute-start | bytes 1081352 | tf_op jit(solution)/shard_map/ppermute | solution.py:362
  101.9 15.5 %collective-permute-start.18 = (bf16[1,208,1024]{2,1,0:T(8,128)(2,1)S(1)}, bf16[1,208,1024]{2,1,0:T(8,128)(2,1)S(1)}, u32[]{:S(2)}, u32[]{:S(2)}) collective-permute-start(bf16[1,208,1024]{2,1,0:T(8,128)(2,1)S(1)} %get-tuple-element.32.refs_2_.refs_4_), channel_id=1, source_target_pairs={{0,4},{4,0},{8,12},{12,8},{1,5},{5,1},{9,13},{13,9},{2,6},{6,2},{1... | collective-permute-start | bytes 1277960 | tf_op jit(solution)/shard_map/ppermute | solution.py:367
  102.1 8.4 %copy-start.4 = (f32[1,176,1024]{2,1,0:T(8,128)S(1)}, f32[1,176,1024]{2,1,0:T(8,128)}, u32[]{:S(2)}) copy-start(f32[1,176,1024]{2,1,0:T(8,128)} %copy-done.3) | copy-start | bytes 2162692
  106.8 22.5 %collective-permute-start.19 = (bf16[1,208,1024]{2,1,0:T(8,128)(2,1)S(1)}, bf16[1,208,1024]{2,1,0:T(8,128)(2,1)S(1)}, u32[]{:S(2)}, u32[]{:S(2)}) collective-permute-start(bf16[1,208,1024]{2,1,0:T(8,128)(2,1)S(1)} %add_convert_fusion.1.refs_4_), channel_id=1, source_target_pairs={{0,8},{4,12},{8,0},{12,4},{1,9},{5,13},{9,1},{13,5},{2,10},{6,14},... | collective-permute-start | bytes 1277960 | tf_op jit(solution)/shard_map/ppermute | solution.py:367
  110.0 20.2 %collective-permute-start.16 = (bf16[1,176,1024]{2,1,0:T(8,128)(2,1)S(1)}, bf16[1,176,1024]{2,1,0:T(8,128)(2,1)S(1)}, u32[]{:S(2)}, u32[]{:S(2)}) collective-permute-start(bf16[1,176,1024]{2,1,0:T(8,128)(2,1)S(1)} %add_convert_fusion.5.refs_6_), channel_id=1, source_target_pairs={{0,4},{4,0},{8,12},{12,8},{1,5},{5,1},{9,13},{13,9},{2,6},{6,2},{1... | collective-permute-start | bytes 1081352 | tf_op jit(solution)/shard_map/ppermute | solution.py:367
  110.0 20.2 %collective-permute-start.15 = (bf16[1,176,1024]{2,1,0:T(8,128)(2,1)S(1)}, bf16[1,176,1024]{2,1,0:T(8,128)(2,1)S(1)}, u32[]{:S(2)}, u32[]{:S(2)}) collective-permute-start(bf16[1,176,1024]{2,1,0:T(8,128)(2,1)S(1)} %get-tuple-element.42), channel_id=1, source_target_pairs={{0,2},{2,0},{1,3},{3,1},{4,6},{6,4},{5,7},{7,5},{8,10},{10,8},{9,1... | collective-permute-start | bytes 1081352 | tf_op jit(solution)/shard_map/ppermute | solution.py:362
  110.7 30.4 %collective-permute-start.14 = (bf16[1,176,1024]{2,1,0:T(8,128)(2,1)S(1)}, bf16[1,176,1024]{2,1,0:T(8,128)(2,1)S(1)}, u32[]{:S(2)}, u32[]{:S(2)}) collective-permute-start(bf16[1,176,1024]{2,1,0:T(8,128)(2,1)S(1)} %add_convert_fusion.4), channel_id=1, source_target_pairs={{0,4},{4,0},{8,12},{12,8},{1,5},{5,1},{9,13},{13,9},{2,6},{6,2},{1... | collective-permute-start | bytes 1081352 | tf_op jit(solution)/shard_map/ppermute | solution.py:367
  117.4 32.0 %copy-start.2 = (bf16[1,384,1024]{2,1,0:T(8,128)(2,1)S(1)}, bf16[1,384,1024]{2,1,0:T(8,128)(2,1)}, u32[]{:S(2)}) copy-start(bf16[1,384,1024]{2,1,0:T(8,128)(2,1)} %param.8) | copy-start | bytes 2359300
  117.4 32.0 %copy-start.7 = (bf16[1,1024]{1,0:T(2,128)(2,1)S(1)}, bf16[1,1024]{1,0:T(2,128)(2,1)}, u32[]{:S(2)}) copy-start(bf16[1,1024]{1,0:T(2,128)(2,1)} %b_ref.1) | copy-start | bytes 6148
  117.4 23.6 %collective-permute-start.12 = (bf16[1,176,1024]{2,1,0:T(8,128)(2,1)S(1)}, bf16[1,176,1024]{2,1,0:T(8,128)(2,1)S(1)}, u32[]{:S(2)}, u32[]{:S(2)}) collective-permute-start(bf16[1,176,1024]{2,1,0:T(8,128)(2,1)S(1)} %get-tuple-element.38), channel_id=1, source_target_pairs={{0,2},{2,0},{1,3},{3,1},{4,6},{6,4},{5,7},{7,5},{8,10},{10,8},{9,1... | collective-permute-start | bytes 1081352 | tf_op jit(solution)/shard_map/ppermute | solution.py:362
  129.3 35.9 %copy-start.1 = (bf16[1,4096]{1,0:T(2,128)(2,1)S(1)}, bf16[1,4096]{1,0:T(2,128)(2,1)}, u32[]{:S(2)}) copy-start(bf16[1,4096]{1,0:T(2,128)(2,1)} %param.10) | copy-start | bytes 24580
  129.5 19.9 %collective-permute-start.20 = (bf16[208,1024]{1,0:T(8,128)(2,1)S(1)}, bf16[208,1024]{1,0:T(8,128)(2,1)S(1)}, u32[]{:S(2)}, u32[]{:S(2)}) collective-permute-start(bf16[208,1024]{1,0:T(8,128)(2,1)S(1)} %fusion), channel_id=1, source_target_pairs={{0,2},{2,0},{1,3},{3,1},{4,6},{6,4},{5,7},{7,5},{8,10},{10,8},{9,1... | collective-permute-start | bytes 1277960 | tf_op jit(solution)/shard_map/ppermute | solution.py:362
  130.3 19.1 %collective-permute-start.17 = (bf16[1,176,1024]{2,1,0:T(8,128)(2,1)S(1)}, bf16[1,176,1024]{2,1,0:T(8,128)(2,1)S(1)}, u32[]{:S(2)}, u32[]{:S(2)}) collective-permute-start(bf16[1,176,1024]{2,1,0:T(8,128)(2,1)S(1)} %add_convert_fusion.3), channel_id=1, source_target_pairs={{0,8},{4,12},{8,0},{12,4},{1,9},{5,13},{9,1},{13,5},{2,10},{6,14},... | collective-permute-start | bytes 1081352 | tf_op jit(solution)/shard_map/ppermute | solution.py:367
  151.0 1.7 %collective-permute-start.23 = (f32[8,128]{1,0:T(8,128)S(1)}, f32[8,128]{1,0:T(8,128)S(1)}, u32[]{:S(2)}, u32[]{:S(2)}) collective-permute-start(f32[8,128]{1,0:T(8,128)S(1)} %get-tuple-element.45), channel_id=1, source_target_pairs={{0,3},{1,0},{2,1},{3,2},{4,7},{5,4},{6,5},{7,6},{8,11},{9,8},{10,9... | collective-permute-start | bytes 12296 | tf_op jit(solution)/shard_map/ppermute | solution.py:362
  151.3 3.6 %collective-permute-start.22 = (f32[8,128]{1,0:T(8,128)S(1)}, f32[8,128]{1,0:T(8,128)S(1)}, u32[]{:S(2)}, u32[]{:S(2)}) collective-permute-start(f32[8,128]{1,0:T(8,128)S(1)} %get-tuple-element.45), channel_id=1, source_target_pairs={{0,2},{1,3},{2,0},{3,1},{4,6},{5,7},{6,4},{7,5},{8,10},{9,11},{10,... | collective-permute-start | bytes 12296 | tf_op jit(solution)/shard_map/ppermute | solution.py:362
  152.5 3.0 %collective-permute-start.21 = (f32[8,128]{1,0:T(8,128)S(1)}, f32[8,128]{1,0:T(8,128)S(1)}, u32[]{:S(2)}, u32[]{:S(2)}) collective-permute-start(f32[8,128]{1,0:T(8,128)S(1)} %get-tuple-element.45), channel_id=1, source_target_pairs={{0,1},{1,2},{2,3},{3,0},{4,5},{5,6},{6,7},{7,4},{8,9},{9,10},{10,1... | collective-permute-start | bytes 12296 | tf_op jit(solution)/shard_map/ppermute | solution.py:362
  155.5 7.8 %copy-start.10 = (f32[8,128]{1,0:T(8,128)}, f32[8,128]{1,0:T(8,128)S(1)}, u32[]{:S(2)}) copy-start(f32[8,128]{1,0:T(8,128)S(1)} %add_add_fusion.refs_0_) | copy-start | bytes 12292
  155.5 3.7 %collective-permute-start.26 = (f32[8,128]{1,0:T(8,128)S(1)}, f32[8,128]{1,0:T(8,128)S(1)}, u32[]{:S(2)}, u32[]{:S(2)}) collective-permute-start(f32[8,128]{1,0:T(8,128)S(1)} %add_add_fusion.refs_0_), channel_id=1, source_target_pairs={{0,12},{4,0},{8,4},{12,8},{1,13},{5,1},{9,5},{13,9},{2,14},{6,2},{... | collective-permute-start | bytes 12296 | tf_op jit(solution)/shard_map/ppermute | solution.py:362
  157.9 4.5 %collective-permute-start.25 = (f32[8,128]{1,0:T(8,128)S(1)}, f32[8,128]{1,0:T(8,128)S(1)}, u32[]{:S(2)}, u32[]{:S(2)}) collective-permute-start(f32[8,128]{1,0:T(8,128)S(1)} %add_add_fusion.refs_0_), channel_id=1, source_target_pairs={{0,8},{4,12},{8,0},{12,4},{1,9},{5,13},{9,1},{13,5},{2,10},{6,14},... | collective-permute-start | bytes 12296 | tf_op jit(solution)/shard_map/ppermute | solution.py:362
  157.9 5.4 %collective-permute-start.24 = (f32[8,128]{1,0:T(8,128)S(1)}, f32[8,128]{1,0:T(8,128)S(1)}, u32[]{:S(2)}, u32[]{:S(2)}) collective-permute-start(f32[8,128]{1,0:T(8,128)S(1)} %add_add_fusion.refs_0_), channel_id=1, source_target_pairs={{0,4},{4,8},{8,12},{12,0},{1,5},{5,9},{9,13},{13,1},{2,6},{6,10},{... | collective-permute-start | bytes 12296 | tf_op jit(solution)/shard_map/ppermute | solution.py:362
  159.3 4.1 %copy-start.11 = (f32[8,128]{1,0:T(8,128)}, f32[8,128]{1,0:T(8,128)S(1)}, u32[]{:S(2)}) copy-start(f32[8,128]{1,0:T(8,128)S(1)} %collective-permute-done.26.refs_3_) | copy-start | bytes 12292
  162.4 0.9 copy-start.12
  163.3 0.6 copy-start.13

commit v16 on v15

--- a/solution.py
+++ b/solution.py
@@ -459,7 +459,7 @@
         codes, earlier, info(mine_bit, (far, near)), [span + (jnp.float32,) for span in spans], [far_sent])
     across_in = (far_kept + wide(far_in)).astype(narrow)
     across_there = swapped(across_in, "latent", 2)
-    total_in = near_kept + wide(near_in)
+    own_terms = [near_kept, near_in, across_there]
 
     after = across_in
     returned = []
@@ -490,7 +490,7 @@
         far_out_back.append(far_back)
         pins = list(near_sent)
         if not returned:
-            total_in = summed([total_in, across_there], near_sent)
+            total_in = summed(own_terms, near_sent)
             pins.append(total_in)
         if len(far_out_back) == n_tok - 1:
             pins.append(joined(far_out_sent, far_out_back).astype(narrow))

time: 165 us -> 164 us (level)
  starting transfers between devices: 34.4 us -> 31.6 us
    ppermute x10, starting transfers between devices: 14.6 us -> 12.7 us  [swapped(): return lax.ppermute(value, axis, [(i, i ^ bit) for i in range(n)])]
  transfers between devices with their start and end apart: 27 -> 27, of which waited for: 13 -> 16; matrix products, arithmetic and copies ran while one was open for 1% -> 1% of each run, Pallas kernels for 28% -> 28%
where the time goes in v16:
time: 164 us
  Pallas kernels  63.2 us (39%)
  waiting for transfers between devices  61.1 us (37%)
  starting transfers between devices  31.6 us (19%)
  local copies, waits for them, and re-layouts  3.19 us (2%)
  between operations  2.33 us (1%)
  other arithmetic  2.07 us (1%)
    ppermute x10, waiting for transfers between devices, swapped(): return lax.ppermute(value, axis, [(i, i ^ bit) for i in range(n)])  43.1 us
    pallas_call x6, Pallas kernels, decode(): pl.pallas_call(body, in_specs=[pl.BlockSpec(memory_space=pltpu.SMEM)] + [...  33.8 us
    pallas_call x2, Pallas kernels, encode(): pl.pallas_call(body, in_specs=[pl.BlockSpec(memory_space=pltpu.SMEM), pl....  21.6 us
    ppermute x14, waiting for transfers between devices, shifted(): lax.ppermute(value, axis, [(i, (i + distance) % n) for i in range(n)])  18 us
    ppermute x14, starting transfers between devices, shifted(): lax.ppermute(value, axis, [(i, (i + distance) % n) for i in range(n)])  14.8 us
    ppermute x10, starting transfers between devices, swapped(): return lax.ppermute(value, axis, [(i, i ^ bit) for i in range(n)])  12.7 us
    ppermute x3, starting transfers between devices, earlier_of(): return [lax.ppermute(part, 'layer', [(0, 1)]) for part in codes]  4.06 us
  transfers between devices with their start and end apart: 27, of which 16 were waited for; matrix products, arithmetic and copies ran while one was open for 1% of the time, Pallas kernels for 28%

profile of v16, /device:TPU:0, one launch (start us, length us, event | category | flops | bytes accessed | tf_op | source)
XLA Modules:
  0.0 163.6 jit_solution(15500917683405826723)
XLA Ops:
  0.6 2.7 %square_sum.1 = (f32[1]{0:T(128)}, bf16[384,4096]{1,0:T(8,128)(2,1)S(1)}) custom-call(bf16[384,4096]{1,0:T(8,128)(2,1)} %bitcast.34), custom_call_target="tpu_custom_call" | custom-call | tf_op jit(solution)/shard_map/square_sum/pallas_call | solution.py:47
  3.4 3.0 %collective-permute-start = (f32[1]{0:T(128)}, f32[1]{0:T(128)}, u32[]{:S(2)}, u32[]{:S(2)}) collective-permute-start(f32[1]{0:T(128)} %get-tuple-element.24), channel_id=1, source_target_pairs={{0,2},{2,0},{1,3},{3,1},{4,6},{6,4},{5,7},{7,5},{8,10},{10,8},{9,1... | collective-permute-start | bytes 20 | tf_op jit(solution)/shard_map/ppermute | solution.py:362
  6.4 1.8 %collective-permute-done = f32[1]{0:T(128)} collective-permute-done((f32[1]{0:T(128)}, f32[1]{0:T(128)}, u32[]{:S(2)}, u32[]{:S(2)}) %collective-permute-start) | collective-permute-done | bytes 36 | tf_op jit(solution)/shard_map/ppermute | solution.py:362
  9.4 0.9 cut.2
  10.3 2.1 %collective-permute-start.3 = (bf16[96,4096]{1,0:T(8,128)(2,1)}, bf16[96,4096]{1,0:T(8,128)(2,1)}, u32[]{:S(2)}, u32[]{:S(2)}) collective-permute-start(bf16[96,4096]{1,0:T(8,128)(2,1)} %cut.2), channel_id=1, source_target_pairs={{0,2},{2,0},{1,3},{3,1},{4,6},{6,4},{5,7},{7,5},{8,10},{10,8},{9,1... | collective-permute-start | bytes 2359304 | tf_op jit(solution)/shard_map/ppermute | solution.py:362
  12.5 10.9 %encode.2 = (bf16[384,1024]{1,0:T(8,128)(2,1)}, bf16[384,1024]{1,0:T(8,128)(2,1)}) custom-call(s32[1]{0:T(128)} %constant.58.clone.1.places_ref, f32[1]{0:T(128)S(6)} %sqrt.3.inv_ref, bf16[1,2048]{1,0:T(2,128)(2,1)S(1)} %constant_dynamic-slice_fusion.b_ref, bf16[384,4096]{1,0:T(8,128)(2,1)S(1)} %get-tuple-element.25.refs_0_.x_ref, bf16[4096,2048]{1,0:T(8,128)(2,1)} %bitcast.32), custom_call_target="tpu_custom_call" | custom-call | tf_op jit(solution)/shard_map/encode/pallas_call | solution.py:146
  23.4 1.2 cut.3
  24.7 1.3 collective-permute-start.2
  26.1 1.3 collective-permute-start.1
  27.5 3.7 %collective-permute-done.3.refs_0_ = bf16[96,4096]{1,0:T(8,128)(2,1)} collective-permute-done((bf16[96,4096]{1,0:T(8,128)(2,1)}, bf16[96,4096]{1,0:T(8,128)(2,1)}, u32[]{:S(2)}, u32[]{:S(2)}) %collective-permute-start.3) | collective-permute-done | bytes 786464 | tf_op jit(solution)/shard_map/ppermute | solution.py:362
  31.2 2.1 %collective-permute-start.4 = (bf16[96,4096]{1,0:T(8,128)(2,1)}, bf16[96,4096]{1,0:T(8,128)(2,1)}, u32[]{:S(2)}, u32[]{:S(2)}) collective-permute-start(bf16[96,4096]{1,0:T(8,128)(2,1)} %collective-permute-done.3.refs_0_), channel_id=1, source_target_pairs={{0,4},{4,0},{8,12},{12,8},{1,5},{5,1},{9,13},{13,9},{2,6},{6,2},{1... | collective-permute-start | bytes 2359304 | tf_op jit(solution)/shard_map/ppermute | solution.py:367
  33.4 8.2 %decode.6 = (bf16[1,208,1024]{2,1,0:T(8,128)(2,1)}, bf16[1,208,1024]{2,1,0:T(8,128)(2,1)S(1)}, f32[1,176,1024]{2,1,0:T(8,128)S(1)}, f32[1,176,1024]{2,1,0:T(8,128)S(1)}) custom-call(s32[3]{0:T(128)S(1)} %get-tuple-element.47.info_ref, bf16[384,1024]{1,0:T(8,128)(2,1)} %get-tuple-element.26.refs_0_.after_ref, bf16[384,1024]{1,0:T(8,128)(2,1)} %get-tuple-element.27.refs_1_, ...), custom_call_target="tpu_custom_call" | custom-call | tf_op jit(solution)/shard_map/decode/pallas_call | solution.py:245
  41.6 0.9 copy-done.3
  42.4 0.9 copy-done.5
  43.3 0.8 copy-done.8
  44.2 7.4 %decode.7 = (f32[1,208,1024]{2,1,0:T(8,128)S(1)}, f32[1,208,1024]{2,1,0:T(8,128)S(1)}, f32[1,176,1024]{2,1,0:T(8,128)S(1)}, f32[1,176,1024]{2,1,0:T(8,128)S(1)}) custom-call(s32[3]{0:T(128)S(1)} %get-tuple-element.46.info_ref, bf16[384,1024]{1,0:T(8,128)(2,1)} %get-tuple-element.26.refs_0_.after_ref, bf16[384,1024]{1,0:T(8,128)(2,1)} %get-tuple-element.27.refs_1_, ...), custom_call_target="tpu_custom_call" | custom-call | tf_op jit(solution)/shard_map/decode/pallas_call | solution.py:245
  51.6 4.9 %collective-permute-done.6 = bf16[1,208,1024]{2,1,0:T(8,128)(2,1)} collective-permute-done((bf16[1,208,1024]{2,1,0:T(8,128)(2,1)}, bf16[1,208,1024]{2,1,0:T(8,128)(2,1)}, u32[]{:S(2)}, u32[]{:S(2)}) %collective-permute-start.6) | collective-permute-done | bytes 426016 | tf_op jit(solution)/shard_map/ppermute | solution.py:367
  56.6 1.1 add_convert_fusion.2.refs_4_
  57.7 4.9 %collective-permute-done.5.refs_2_ = bf16[192,4096]{1,0:T(8,128)(2,1)S(1)} collective-permute-done((bf16[192,4096]{1,0:T(8,128)(2,1)}, bf16[192,4096]{1,0:T(8,128)(2,1)S(1)}, u32[]{:S(2)}, u32[]{:S(2)}) %collective-permute-start.5) | collective-permute-done | bytes 1572896 | tf_op jit(solution)/shard_map/ppermute | solution.py:362
  62.6 10.6 %encode.3.refs_0_ = bf16[384,2048]{1,0:T(8,128)(2,1)S(1)} custom-call(s32[3]{0:T(128)S(1)} %pad_add_fusion.3.places_ref, f32[1]{0:T(128)S(6)} %sqrt.3.inv_ref, bf16[1,2048]{1,0:T(2,128)(2,1)S(1)} %constant_dynamic-slice_fusion.b_ref, bf16[96,4096]{1,0:T(8,128)(2,1)} %collective-permute-done.3.refs_0_, bf16[96,4096]{1,0:T(8,128)(2,1)} %collective-permute-done.4.refs_1_, ...), custom_call_target="tpu_custom_call" | custom-call | tf_op jit(solution)/shard_map/encode/pallas_call | solution.py:146
  73.2 1.4 collective-permute-start.7
  74.6 1.9 %collective-permute-start.8 = (bf16[1,208,1024]{2,1,0:T(8,128)(2,1)S(1)}, bf16[1,208,1024]{2,1,0:T(8,128)(2,1)S(1)}, u32[]{:S(2)}, u32[]{:S(2)}) collective-permute-start(bf16[1,208,1024]{2,1,0:T(8,128)(2,1)S(1)} %copy-done.9), channel_id=1, source_target_pairs={{0,4},{4,0},{8,12},{12,8},{1,5},{5,1},{9,13},{13,9},{2,6},{6,2},{1... | collective-permute-start | bytes 1277960 | tf_op jit(solution)/shard_map/ppermute | solution.py:367
  76.5 2.6 %collective-permute-start.9 = (bf16[1,208,1024]{2,1,0:T(8,128)(2,1)S(1)}, bf16[1,208,1024]{2,1,0:T(8,128)(2,1)S(1)}, u32[]{:S(2)}, u32[]{:S(2)}) collective-permute-start(bf16[1,208,1024]{2,1,0:T(8,128)(2,1)S(1)} %add_convert_fusion.2.refs_4_), channel_id=1, source_target_pairs={{0,8},{4,12},{8,0},{12,4},{1,9},{5,13},{9,1},{13,5},{2,10},{6,14},... | collective-permute-start | bytes 1277960 | tf_op jit(solution)/shard_map/ppermute | solution.py:367
  79.2 4.5 %decode.8 = (bf16[1,208,1024]{2,1,0:T(8,128)(2,1)S(1)}, bf16[1,176,1024]{2,1,0:T(8,128)(2,1)S(1)}) custom-call(s32[2]{0:T(128)S(1)} %get-tuple-element.49.info_ref, bf16[384,2048]{1,0:T(8,128)(2,1)S(1)} %encode.3.refs_0_, bf16[384,2048]{1,0:T(8,128)(2,1)S(1)} %collective-permute-done.7.refs_1_, bf16[2048,4096]{1,0:T(8,128)(2,1)} %bitcast.28, ...), custom_call_target="tpu_custom_call" | custom-call | tf_op jit(solution)/shard_map/decode/pallas_call | solution.py:245
  83.7 1.6 collective-permute-start.10
  85.8 4.5 %decode.9 = (bf16[1,208,1024]{2,1,0:T(8,128)(2,1)S(1)}, bf16[1,176,1024]{2,1,0:T(8,128)(2,1)S(1)}) custom-call(s32[2]{0:T(128)S(1)} %get-tuple-element.48.info_ref, bf16[384,2048]{1,0:T(8,128)(2,1)S(1)} %encode.3.refs_0_, bf16[384,2048]{1,0:T(8,128)(2,1)S(1)} %collective-permute-done.7.refs_1_, bf16[2048,4096]{1,0:T(8,128)(2,1)} %bitcast.29, ...), custom_call_target="tpu_custom_call" | custom-call | tf_op jit(solution)/shard_map/decode/pallas_call | solution.py:245
  90.9 4.7 %collective-permute-done.8.refs_1_ = bf16[1,208,1024]{2,1,0:T(8,128)(2,1)S(1)} collective-permute-done((bf16[1,208,1024]{2,1,0:T(8,128)(2,1)S(1)}, bf16[1,208,1024]{2,1,0:T(8,128)(2,1)S(1)}, u32[]{:S(2)}, u32[]{:S(2)}) %collective-permute-start.8) | collective-permute-done | bytes 426016 | tf_op jit(solution)/shard_map/ppermute | solution.py:367
  96.3 4.5 %decode.10 = (f32[1,208,1024]{2,1,0:T(8,128)S(1)}, bf16[1,176,1024]{2,1,0:T(8,128)(2,1)S(1)}) custom-call(s32[2]{0:T(128)S(1)} %pad_add_fusion.4.info_ref, bf16[384,2048]{1,0:T(8,128)(2,1)S(1)} %encode.3.refs_0_, bf16[384,2048]{1,0:T(8,128)(2,1)S(1)} %collective-permute-done.7.refs_1_, bf16[2048,4096]{1,0:T(8,128)(2,1)} %bitcast.30, ...), custom_call_target="tpu_custom_call" | custom-call | tf_op jit(solution)/shard_map/decode/pallas_call | solution.py:245
  100.8 4.3 %collective-permute-done.11 = bf16[1,208,1024]{2,1,0:T(8,128)(2,1)S(1)} collective-permute-done((bf16[1,208,1024]{2,1,0:T(8,128)(2,1)S(1)}, bf16[1,208,1024]{2,1,0:T(8,128)(2,1)S(1)}, u32[]{:S(2)}, u32[]{:S(2)}) %collective-permute-start.11) | collective-permute-done | bytes 426016 | tf_op jit(solution)/shard_map/ppermute | solution.py:367
  105.2 3.6 %collective-permute-start.19 = (bf16[1,208,1024]{2,1,0:T(8,128)(2,1)S(1)}, bf16[1,208,1024]{2,1,0:T(8,128)(2,1)S(1)}, u32[]{:S(2)}, u32[]{:S(2)}) collective-permute-start(bf16[1,208,1024]{2,1,0:T(8,128)(2,1)S(1)} %add_convert_fusion.1.refs_4_), channel_id=1, source_target_pairs={{0,8},{4,12},{8,0},{12,4},{1,9},{5,13},{9,1},{13,5},{2,10},{6,14},... | collective-permute-start | bytes 1277960 | tf_op jit(solution)/shard_map/ppermute | solution.py:367
  108.8 1.6 collective-permute-start.15
  110.5 2.0 %collective-permute-start.14 = (bf16[1,176,1024]{2,1,0:T(8,128)(2,1)S(1)}, bf16[1,176,1024]{2,1,0:T(8,128)(2,1)S(1)}, u32[]{:S(2)}, u32[]{:S(2)}) collective-permute-start(bf16[1,176,1024]{2,1,0:T(8,128)(2,1)S(1)} %add_convert_fusion.4), channel_id=1, source_target_pairs={{0,4},{4,0},{8,12},{12,8},{1,5},{5,1},{9,13},{13,9},{2,6},{6,2},{1... | collective-permute-start | bytes 1081352 | tf_op jit(solution)/shard_map/ppermute | solution.py:367
  112.5 4.7 %decode.11 = (f32[1,208,1024]{2,1,0:T(8,128)S(1)}, bf16[1,176,1024]{2,1,0:T(8,128)(2,1)S(1)}) custom-call(s32[2]{0:T(128)S(1)} %pad_add_fusion.2.info_ref, bf16[384,2048]{1,0:T(8,128)(2,1)S(1)} %encode.3.refs_0_, bf16[384,2048]{1,0:T(8,128)(2,1)S(1)} %collective-permute-done.7.refs_1_, bf16[2048,4096]{1,0:T(8,128)(2,1)} %bitcast.31, ...), custom_call_target="tpu_custom_call" | custom-call | tf_op jit(solution)/shard_map/decode/pallas_call | solution.py:245
  117.2 5.8 %collective-permute-done.18 = bf16[1,208,1024]{2,1,0:T(8,128)(2,1)S(1)} collective-permute-done((bf16[1,208,1024]{2,1,0:T(8,128)(2,1)S(1)}, bf16[1,208,1024]{2,1,0:T(8,128)(2,1)S(1)}, u32[]{:S(2)}, u32[]{:S(2)}) %collective-permute-start.18) | collective-permute-done | bytes 426016 | tf_op jit(solution)/shard_map/ppermute | solution.py:367
  123.1 1.5 collective-permute-start.12
  125.3 9.3 %collective-permute-done.16 = bf16[1,176,1024]{2,1,0:T(8,128)(2,1)S(1)} collective-permute-done((bf16[1,176,1024]{2,1,0:T(8,128)(2,1)S(1)}, bf16[1,176,1024]{2,1,0:T(8,128)(2,1)S(1)}, u32[]{:S(2)}, u32[]{:S(2)}) %collective-permute-start.16) | collective-permute-done | bytes 360480 | tf_op jit(solution)/shard_map/ppermute | solution.py:367
  134.9 5.9 %collective-permute-done.14 = bf16[1,176,1024]{2,1,0:T(8,128)(2,1)S(1)} collective-permute-done((bf16[1,176,1024]{2,1,0:T(8,128)(2,1)S(1)}, bf16[1,176,1024]{2,1,0:T(8,128)(2,1)S(1)}, u32[]{:S(2)}, u32[]{:S(2)}) %collective-permute-start.14) | collective-permute-done | bytes 360480 | tf_op jit(solution)/shard_map/ppermute | solution.py:367
  140.8 7.9 %collective-permute-done.17 = bf16[1,176,1024]{2,1,0:T(8,128)(2,1)S(1)} collective-permute-done((bf16[1,176,1024]{2,1,0:T(8,128)(2,1)S(1)}, bf16[1,176,1024]{2,1,0:T(8,128)(2,1)S(1)}, u32[]{:S(2)}, u32[]{:S(2)}) %collective-permute-start.17) | collective-permute-done | bytes 360480 | tf_op jit(solution)/shard_map/ppermute | solution.py:367
  148.6 1.6 finale.1
  150.3 1.5 collective-permute-start.22
  152.0 1.9 %collective-permute-done.22 = f32[8,128]{1,0:T(8,128)S(1)} collective-permute-done((f32[8,128]{1,0:T(8,128)S(1)}, f32[8,128]{1,0:T(8,128)S(1)}, u32[]{:S(2)}, u32[]{:S(2)}) %collective-permute-start.22) | collective-permute-done | bytes 4128 | tf_op jit(solution)/shard_map/ppermute | solution.py:362
  153.9 0.9 collective-permute-done.21
  154.8 1.5 collective-permute-start.26
  156.3 0.6 collective-permute-start.24
  156.9 1.5 collective-permute-done.26.refs_3_
  158.4 2.4 %collective-permute-done.25.refs_2_ = f32[8,128]{1,0:T(8,128)S(1)} collective-permute-done((f32[8,128]{1,0:T(8,128)S(1)}, f32[8,128]{1,0:T(8,128)S(1)}, u32[]{:S(2)}, u32[]{:S(2)}) %collective-permute-start.25) | collective-permute-done | bytes 4128 | tf_op jit(solution)/shard_map/ppermute | solution.py:362
  160.8 0.9 collective-permute-done.24.refs_1_
  162.3 1.2 mean_ratio.1
  (61 shorter events, 4.2 us)
Async XLA Ops:
  0.6 11.8 %copy-start = (bf16[1,4096]{1,0:T(2,128)(2,1)S(1)}, bf16[1,4096]{1,0:T(2,128)(2,1)}, u32[]{:S(2)}) copy-start(bf16[1,4096]{1,0:T(2,128)(2,1)} %param.10) | copy-start | bytes 24580
  3.4 4.8 %collective-permute-start = (f32[1]{0:T(128)}, f32[1]{0:T(128)}, u32[]{:S(2)}, u32[]{:S(2)}) collective-permute-start(f32[1]{0:T(128)} %get-tuple-element.24), channel_id=1, source_target_pairs={{0,2},{2,0},{1,3},{3,1},{4,6},{6,4},{5,7},{7,5},{8,10},{10,8},{9,1... | collective-permute-start | bytes 20 | tf_op jit(solution)/shard_map/ppermute | solution.py:362
  10.3 20.9 %collective-permute-start.3 = (bf16[96,4096]{1,0:T(8,128)(2,1)}, bf16[96,4096]{1,0:T(8,128)(2,1)}, u32[]{:S(2)}, u32[]{:S(2)}) collective-permute-start(bf16[96,4096]{1,0:T(8,128)(2,1)} %cut.2), channel_id=1, source_target_pairs={{0,2},{2,0},{1,3},{3,1},{4,6},{6,4},{5,7},{7,5},{8,10},{10,8},{9,1... | collective-permute-start | bytes 2359304 | tf_op jit(solution)/shard_map/ppermute | solution.py:362
  24.6 38.0 %collective-permute-start.5 = (bf16[192,4096]{1,0:T(8,128)(2,1)}, bf16[192,4096]{1,0:T(8,128)(2,1)S(1)}, u32[]{:S(2)}, u32[]{:S(2)}) collective-permute-start(bf16[192,4096]{1,0:T(8,128)(2,1)} %cut.3), channel_id=1, source_target_pairs={{0,2},{2,0},{1,3},{3,1},{4,6},{6,4},{5,7},{7,5},{8,10},{10,8},{9,1... | collective-permute-start | bytes 4718600 | tf_op jit(solution)/shard_map/ppermute | solution.py:362
  24.7 8.7 %collective-permute-start.2 = (bf16[384,1024]{1,0:T(8,128)(2,1)}, bf16[384,1024]{1,0:T(8,128)(2,1)S(1)}, u32[]{:S(2)}, u32[]{:S(2)}) collective-permute-start(bf16[384,1024]{1,0:T(8,128)(2,1)} %get-tuple-element.27.refs_1_), channel_id=1, source_target_pairs={{0,1},{2,3},{4,5},{6,7},{8,9},{10,11},{12,13},{14,15},{16,17},{18,... | collective-permute-start | bytes 2359304 | tf_op jit(solution)/shard_map/ppermute | solution.py:423
  26.1 7.3 %collective-permute-start.1 = (bf16[384,1024]{1,0:T(8,128)(2,1)}, bf16[384,1024]{1,0:T(8,128)(2,1)S(1)}, u32[]{:S(2)}, u32[]{:S(2)}) collective-permute-start(bf16[384,1024]{1,0:T(8,128)(2,1)} %get-tuple-element.26.refs_0_.after_ref), channel_id=1, source_target_pairs={{0,1},{2,3},{4,5},{6,7},{8,9},{10,11},{12,13},{14,15},{16,17},{18,... | collective-permute-start | bytes 2359304 | tf_op jit(solution)/shard_map/ppermute | solution.py:423
  31.2 26.5 %collective-permute-start.4 = (bf16[96,4096]{1,0:T(8,128)(2,1)}, bf16[96,4096]{1,0:T(8,128)(2,1)}, u32[]{:S(2)}, u32[]{:S(2)}) collective-permute-start(bf16[96,4096]{1,0:T(8,128)(2,1)} %collective-permute-done.3.refs_0_), channel_id=1, source_target_pairs={{0,4},{4,0},{8,12},{12,8},{1,5},{5,1},{9,13},{13,9},{2,6},{6,2},{1... | collective-permute-start | bytes 2359304 | tf_op jit(solution)/shard_map/ppermute | solution.py:367
  41.6 0.9 copy-start.3
  42.4 0.9 copy-start.5
  43.3 0.8 copy-start.8
  44.1 12.4 %collective-permute-start.6 = (bf16[1,208,1024]{2,1,0:T(8,128)(2,1)}, bf16[1,208,1024]{2,1,0:T(8,128)(2,1)}, u32[]{:S(2)}, u32[]{:S(2)}) collective-permute-start(bf16[1,208,1024]{2,1,0:T(8,128)(2,1)} %get-tuple-element.28.refs_6_), channel_id=1, source_target_pairs={{0,4},{4,0},{8,12},{12,8},{1,5},{5,1},{9,13},{13,9},{2,6},{6,2},{1... | collective-permute-start | bytes 1277960 | tf_op jit(solution)/shard_map/ppermute | solution.py:367
  57.7 17.0 %copy-start.9 = (bf16[1,208,1024]{2,1,0:T(8,128)(2,1)S(1)}, bf16[1,208,1024]{2,1,0:T(8,128)(2,1)}, u32[]{:S(2)}) copy-start(bf16[1,208,1024]{2,1,0:T(8,128)(2,1)} %copy-done.8) | copy-start | bytes 1277956
  73.2 6.0 %collective-permute-start.7 = (bf16[384,2048]{1,0:T(8,128)(2,1)S(1)}, bf16[384,2048]{1,0:T(8,128)(2,1)S(1)}, u32[]{:S(2)}, u32[]{:S(2)}) collective-permute-start(bf16[384,2048]{1,0:T(8,128)(2,1)S(1)} %encode.3.refs_0_), channel_id=1, source_target_pairs={{0,1},{2,3},{4,5},{6,7},{8,9},{10,11},{12,13},{14,15},{16,17},{18,... | collective-permute-start | bytes 4718600 | tf_op jit(solution)/shard_map/ppermute | solution.py:423
  74.6 21.0 %collective-permute-start.8 = (bf16[1,208,1024]{2,1,0:T(8,128)(2,1)S(1)}, bf16[1,208,1024]{2,1,0:T(8,128)(2,1)S(1)}, u32[]{:S(2)}, u32[]{:S(2)}) collective-permute-start(bf16[1,208,1024]{2,1,0:T(8,128)(2,1)S(1)} %copy-done.9), channel_id=1, source_target_pairs={{0,4},{4,0},{8,12},{12,8},{1,5},{5,1},{9,13},{13,9},{2,6},{6,2},{1... | collective-permute-start | bytes 1277960 | tf_op jit(solution)/shard_map/ppermute | solution.py:367
  76.5 19.4 %collective-permute-start.9 = (bf16[1,208,1024]{2,1,0:T(8,128)(2,1)S(1)}, bf16[1,208,1024]{2,1,0:T(8,128)(2,1)S(1)}, u32[]{:S(2)}, u32[]{:S(2)}) collective-permute-start(bf16[1,208,1024]{2,1,0:T(8,128)(2,1)S(1)} %add_convert_fusion.2.refs_4_), channel_id=1, source_target_pairs={{0,8},{4,12},{8,0},{12,4},{1,9},{5,13},{9,1},{13,5},{2,10},{6,14},... | collective-permute-start | bytes 1277960 | tf_op jit(solution)/shard_map/ppermute | solution.py:367
  83.7 12.4 %collective-permute-start.10 = (bf16[1,176,1024]{2,1,0:T(8,128)(2,1)S(1)}, bf16[1,176,1024]{2,1,0:T(8,128)(2,1)S(1)}, u32[]{:S(2)}, u32[]{:S(2)}) collective-permute-start(bf16[1,176,1024]{2,1,0:T(8,128)(2,1)S(1)} %get-tuple-element.36), channel_id=1, source_target_pairs={{0,2},{2,0},{1,3},{3,1},{4,6},{6,4},{5,7},{7,5},{8,10},{10,8},{9,1... | collective-permute-start | bytes 1081352 | tf_op jit(solution)/shard_map/ppermute | solution.py:362
  85.3 19.8 %collective-permute-start.11 = (bf16[1,208,1024]{2,1,0:T(8,128)(2,1)S(1)}, bf16[1,208,1024]{2,1,0:T(8,128)(2,1)S(1)}, u32[]{:S(2)}, u32[]{:S(2)}) collective-permute-start(bf16[1,208,1024]{2,1,0:T(8,128)(2,1)S(1)} %get-tuple-element.31.refs_4_), channel_id=1, source_target_pairs={{0,4},{4,0},{8,12},{12,8},{1,5},{5,1},{9,13},{13,9},{2,6},{6,2},{1... | collective-permute-start | bytes 1277960 | tf_op jit(solution)/shard_map/ppermute | solution.py:367
  90.3 5.9 %copy-start.6 = (f32[1,176,1024]{2,1,0:T(8,128)S(1)}, f32[1,176,1024]{2,1,0:T(8,128)}, u32[]{:S(2)}) copy-start(f32[1,176,1024]{2,1,0:T(8,128)} %copy-done.5) | copy-start | bytes 2162692
  90.3 20.1 %collective-permute-start.13 = (bf16[1,176,1024]{2,1,0:T(8,128)(2,1)S(1)}, bf16[1,176,1024]{2,1,0:T(8,128)(2,1)S(1)}, u32[]{:S(2)}, u32[]{:S(2)}) collective-permute-start(bf16[1,176,1024]{2,1,0:T(8,128)(2,1)S(1)} %get-tuple-element.40), channel_id=1, source_target_pairs={{0,2},{2,0},{1,3},{3,1},{4,6},{6,4},{5,7},{7,5},{8,10},{10,8},{9,1... | collective-permute-start | bytes 1081352 | tf_op jit(solution)/shard_map/ppermute | solution.py:362
  95.7 27.4 %collective-permute-start.18 = (bf16[1,208,1024]{2,1,0:T(8,128)(2,1)S(1)}, bf16[1,208,1024]{2,1,0:T(8,128)(2,1)S(1)}, u32[]{:S(2)}, u32[]{:S(2)}) collective-permute-start(bf16[1,208,1024]{2,1,0:T(8,128)(2,1)S(1)} %get-tuple-element.32.refs_3_.refs_4_), channel_id=1, source_target_pairs={{0,4},{4,0},{8,12},{12,8},{1,5},{5,1},{9,13},{13,9},{2,6},{6,2},{1... | collective-permute-start | bytes 1277960 | tf_op jit(solution)/shard_map/ppermute | solution.py:367
  96.3 14.1 %copy-start.4 = (f32[1,176,1024]{2,1,0:T(8,128)S(1)}, f32[1,176,1024]{2,1,0:T(8,128)}, u32[]{:S(2)}) copy-start(f32[1,176,1024]{2,1,0:T(8,128)} %copy-done.3) | copy-start | bytes 2162692
  105.2 19.4 %collective-permute-start.19 = (bf16[1,208,1024]{2,1,0:T(8,128)(2,1)S(1)}, bf16[1,208,1024]{2,1,0:T(8,128)(2,1)S(1)}, u32[]{:S(2)}, u32[]{:S(2)}) collective-permute-start(bf16[1,208,1024]{2,1,0:T(8,128)(2,1)S(1)} %add_convert_fusion.1.refs_4_), channel_id=1, source_target_pairs={{0,8},{4,12},{8,0},{12,4},{1,9},{5,13},{9,1},{13,5},{2,10},{6,14},... | collective-permute-start | bytes 1277960 | tf_op jit(solution)/shard_map/ppermute | solution.py:367
  108.8 25.8 %collective-permute-start.16 = (bf16[1,176,1024]{2,1,0:T(8,128)(2,1)S(1)}, bf16[1,176,1024]{2,1,0:T(8,128)(2,1)S(1)}, u32[]{:S(2)}, u32[]{:S(2)}) collective-permute-start(bf16[1,176,1024]{2,1,0:T(8,128)(2,1)S(1)} %add_convert_fusion.5.refs_6_), channel_id=1, source_target_pairs={{0,4},{4,0},{8,12},{12,8},{1,5},{5,1},{9,13},{13,9},{2,6},{6,2},{1... | collective-permute-start | bytes 1081352 | tf_op jit(solution)/shard_map/ppermute | solution.py:367
  108.8 25.8 %collective-permute-start.15 = (bf16[1,176,1024]{2,1,0:T(8,128)(2,1)S(1)}, bf16[1,176,1024]{2,1,0:T(8,128)(2,1)S(1)}, u32[]{:S(2)}, u32[]{:S(2)}) collective-permute-start(bf16[1,176,1024]{2,1,0:T(8,128)(2,1)S(1)} %get-tuple-element.42), channel_id=1, source_target_pairs={{0,2},{2,0},{1,3},{3,1},{4,6},{6,4},{5,7},{7,5},{8,10},{10,8},{9,1... | collective-permute-start | bytes 1081352 | tf_op jit(solution)/shard_map/ppermute | solution.py:362
  110.5 30.2 %collective-permute-start.14 = (bf16[1,176,1024]{2,1,0:T(8,128)(2,1)S(1)}, bf16[1,176,1024]{2,1,0:T(8,128)(2,1)S(1)}, u32[]{:S(2)}, u32[]{:S(2)}) collective-permute-start(bf16[1,176,1024]{2,1,0:T(8,128)(2,1)S(1)} %add_convert_fusion.4), channel_id=1, source_target_pairs={{0,4},{4,0},{8,12},{12,8},{1,5},{5,1},{9,13},{13,9},{2,6},{6,2},{1... | collective-permute-start | bytes 1081352 | tf_op jit(solution)/shard_map/ppermute | solution.py:367
  117.2 31.4 %copy-start.2 = (bf16[1,384,1024]{2,1,0:T(8,128)(2,1)S(1)}, bf16[1,384,1024]{2,1,0:T(8,128)(2,1)}, u32[]{:S(2)}) copy-start(bf16[1,384,1024]{2,1,0:T(8,128)(2,1)} %param.8) | copy-start | bytes 2359300
  117.2 31.4 %copy-start.7 = (bf16[1,1024]{1,0:T(2,128)(2,1)S(1)}, bf16[1,1024]{1,0:T(2,128)(2,1)}, u32[]{:S(2)}) copy-start(bf16[1,1024]{1,0:T(2,128)(2,1)} %b_ref.1) | copy-start | bytes 6148
  123.1 17.7 %collective-permute-start.12 = (bf16[1,176,1024]{2,1,0:T(8,128)(2,1)S(1)}, bf16[1,176,1024]{2,1,0:T(8,128)(2,1)S(1)}, u32[]{:S(2)}, u32[]{:S(2)}) collective-permute-start(bf16[1,176,1024]{2,1,0:T(8,128)(2,1)S(1)} %get-tuple-element.38), channel_id=1, source_target_pairs={{0,2},{2,0},{1,3},{3,1},{4,6},{6,4},{5,7},{7,5},{8,10},{10,8},{9,1... | collective-permute-start | bytes 1081352 | tf_op jit(solution)/shard_map/ppermute | solution.py:362
  124.6 39.0 %copy-start.1 = (bf16[1,4096]{1,0:T(2,128)(2,1)S(1)}, bf16[1,4096]{1,0:T(2,128)(2,1)}, u32[]{:S(2)}) copy-start(bf16[1,4096]{1,0:T(2,128)(2,1)} %param.10) | copy-start | bytes 24580
  124.7 23.9 %collective-permute-start.20 = (bf16[208,1024]{1,0:T(8,128)(2,1)S(1)}, bf16[208,1024]{1,0:T(8,128)(2,1)S(1)}, u32[]{:S(2)}, u32[]{:S(2)}) collective-permute-start(bf16[208,1024]{1,0:T(8,128)(2,1)S(1)} %fusion), channel_id=1, source_target_pairs={{0,2},{2,0},{1,3},{3,1},{4,6},{6,4},{5,7},{7,5},{8,10},{10,8},{9,1... | collective-permute-start | bytes 1277960 | tf_op jit(solution)/shard_map/ppermute | solution.py:362
  134.8 13.8 %collective-permute-start.17 = (bf16[1,176,1024]{2,1,0:T(8,128)(2,1)S(1)}, bf16[1,176,1024]{2,1,0:T(8,128)(2,1)S(1)}, u32[]{:S(2)}, u32[]{:S(2)}) collective-permute-start(bf16[1,176,1024]{2,1,0:T(8,128)(2,1)S(1)} %add_convert_fusion.3), channel_id=1, source_target_pairs={{0,8},{4,12},{8,0},{12,4},{1,9},{5,13},{9,1},{13,5},{2,10},{6,14},... | collective-permute-start | bytes 1081352 | tf_op jit(solution)/shard_map/ppermute | solution.py:367
  150.3 1.7 %collective-permute-start.23 = (f32[8,128]{1,0:T(8,128)S(1)}, f32[8,128]{1,0:T(8,128)S(1)}, u32[]{:S(2)}, u32[]{:S(2)}) collective-permute-start(f32[8,128]{1,0:T(8,128)S(1)} %get-tuple-element.45), channel_id=1, source_target_pairs={{0,3},{1,0},{2,1},{3,2},{4,7},{5,4},{6,5},{7,6},{8,11},{9,8},{10,9... | collective-permute-start | bytes 12296 | tf_op jit(solution)/shard_map/ppermute | solution.py:362
  150.3 3.6 %collective-permute-start.22 = (f32[8,128]{1,0:T(8,128)S(1)}, f32[8,128]{1,0:T(8,128)S(1)}, u32[]{:S(2)}, u32[]{:S(2)}) collective-permute-start(f32[8,128]{1,0:T(8,128)S(1)} %get-tuple-element.45), channel_id=1, source_target_pairs={{0,2},{1,3},{2,0},{3,1},{4,6},{5,7},{6,4},{7,5},{8,10},{9,11},{10,... | collective-permute-start | bytes 12296 | tf_op jit(solution)/shard_map/ppermute | solution.py:362
  151.8 3.0 %collective-permute-start.21 = (f32[8,128]{1,0:T(8,128)S(1)}, f32[8,128]{1,0:T(8,128)S(1)}, u32[]{:S(2)}, u32[]{:S(2)}) collective-permute-start(f32[8,128]{1,0:T(8,128)S(1)} %get-tuple-element.45), channel_id=1, source_target_pairs={{0,1},{1,2},{2,3},{3,0},{4,5},{5,6},{6,7},{7,4},{8,9},{9,10},{10,1... | collective-permute-start | bytes 12296 | tf_op jit(solution)/shard_map/ppermute | solution.py:362
  154.8 6.9 %copy-start.10 = (f32[8,128]{1,0:T(8,128)}, f32[8,128]{1,0:T(8,128)S(1)}, u32[]{:S(2)}) copy-start(f32[8,128]{1,0:T(8,128)S(1)} %add_add_fusion.refs_0_) | copy-start | bytes 12292
  154.8 3.6 %collective-permute-start.26 = (f32[8,128]{1,0:T(8,128)S(1)}, f32[8,128]{1,0:T(8,128)S(1)}, u32[]{:S(2)}, u32[]{:S(2)}) collective-permute-start(f32[8,128]{1,0:T(8,128)S(1)} %add_add_fusion.refs_0_), channel_id=1, source_target_pairs={{0,12},{4,0},{8,4},{12,8},{1,13},{5,1},{9,5},{13,9},{2,14},{6,2},{... | collective-permute-start | bytes 12296 | tf_op jit(solution)/shard_map/ppermute | solution.py:362
  156.3 4.5 %collective-permute-start.25 = (f32[8,128]{1,0:T(8,128)S(1)}, f32[8,128]{1,0:T(8,128)S(1)}, u32[]{:S(2)}, u32[]{:S(2)}) collective-permute-start(f32[8,128]{1,0:T(8,128)S(1)} %add_add_fusion.refs_0_), channel_id=1, source_target_pairs={{0,8},{4,12},{8,0},{12,4},{1,9},{5,13},{9,1},{13,5},{2,10},{6,14},... | collective-permute-start | bytes 12296 | tf_op jit(solution)/shard_map/ppermute | solution.py:362
  156.3 5.4 %collective-permute-start.24 = (f32[8,128]{1,0:T(8,128)S(1)}, f32[8,128]{1,0:T(8,128)S(1)}, u32[]{:S(2)}, u32[]{:S(2)}) collective-permute-start(f32[8,128]{1,0:T(8,128)S(1)} %add_add_fusion.refs_0_), channel_id=1, source_target_pairs={{0,4},{4,8},{8,12},{12,0},{1,5},{5,9},{9,13},{13,1},{2,6},{6,10},{... | collective-permute-start | bytes 12296 | tf_op jit(solution)/shard_map/ppermute | solution.py:362
  158.4 3.3 %copy-start.11 = (f32[8,128]{1,0:T(8,128)}, f32[8,128]{1,0:T(8,128)S(1)}, u32[]{:S(2)}) copy-start(f32[8,128]{1,0:T(8,128)S(1)} %collective-permute-done.26.refs_3_) | copy-start | bytes 12292
  160.8 0.9 copy-start.12
  161.7 0.6 copy-start.13

commit v17 on v16

--- a/solution.py
+++ b/solution.py
@@ -414,7 +414,7 @@
         blocks = [4 * i + 2 * high + low for high in highs for i in range(group)]
         return jnp.stack([layer] + blocks).astype(jnp.int32)
 
-    middle = rows * 13 // 24 // 16 * 16
+    middle = rows * 11 // 24 // 16 * 16
     first = (rows - middle) // 2 // 16 * 16
     last = first + middle
     narrow = jnp.bfloat16

time: 164 us -> 175 us (1.067)
  starting transfers between devices: 31.6 us -> 41.2 us
  waiting for transfers between devices: 61.1 us -> 63.5 us
    ppermute x10, waiting for transfers between devices: 43.1 us -> 37.8 us  [swapped(): return lax.ppermute(value, axis, [(i, i ^ bit) for i in range(n)])]
    ppermute x14, starting transfers between devices: 14.8 us -> 19.9 us  [shifted(): lax.ppermute(value, axis, [(i, (i + distance) % n) for i in range(n)])]
    ppermute x14, waiting for transfers between devices: 18 us -> 22.8 us  [shifted(): lax.ppermute(value, axis, [(i, (i + distance) % n) for i in range(n)])]
    ppermute x10, starting transfers between devices: 12.7 us -> 17.3 us  [swapped(): return lax.ppermute(value, axis, [(i, i ^ bit) for i in range(n)])]
    ppermute x3, waiting for transfers between devices: 0.01 us -> 2.85 us  [earlier_of(): return [lax.ppermute(part, 'layer', [(0, 1)]) for part in codes]]
  transfers between devices with their start and end apart: 27 -> 27, of which waited for: 16 -> 14; matrix products, arithmetic and copies ran while one was open for 1% -> 1% of each run, Pallas kernels for 28% -> 23%
where the time goes in v17:
time: 175 us
  waiting for transfers between devices  63.5 us (36%)
  Pallas kernels  62.5 us (36%)
  starting transfers between devices  41.2 us (24%)
  local copies, waits for them, and re-layouts  3.2 us (2%)
  between operations  2.25 us (1%)
  other arithmetic  2.05 us (1%)
    ppermute x10, waiting for transfers between devices, swapped(): return lax.ppermute(value, axis, [(i, i ^ bit) for i in range(n)])  37.8 us
    pallas_call x6, Pallas kernels, decode(): pl.pallas_call(body, in_specs=[pl.BlockSpec(memory_space=pltpu.SMEM)] + [...  33 us
    ppermute x14, waiting for transfers between devices, shifted(): lax.ppermute(value, axis, [(i, (i + distance) % n) for i in range(n)])  22.8 us
    pallas_call x2, Pallas kernels, encode(): pl.pallas_call(body, in_specs=[pl.BlockSpec(memory_space=pltpu.SMEM), pl....  21.6 us
    ppermute x14, starting transfers between devices, shifted(): lax.ppermute(value, axis, [(i, (i + distance) % n) for i in range(n)])  19.9 us
    ppermute x10, starting transfers between devices, swapped(): return lax.ppermute(value, axis, [(i, i ^ bit) for i in range(n)])  17.3 us
    ppermute x3, starting transfers between devices, earlier_of(): return [lax.ppermute(part, 'layer', [(0, 1)]) for part in codes]  4.06 us
  transfers between devices with their start and end apart: 27, of which 14 were waited for; matrix products, arithmetic and copies ran while one was open for 1% of the time, Pallas kernels for 23%

profile of v17, /device:TPU:0, one launch (start us, length us, event | category | flops | bytes accessed | tf_op | source)
XLA Modules:
  0.0 174.6 jit_solution(4504030945669925809)
XLA Ops:
  0.6 2.7 %square_sum.1 = (f32[1]{0:T(128)}, bf16[384,4096]{1,0:T(8,128)(2,1)S(1)}) custom-call(bf16[384,4096]{1,0:T(8,128)(2,1)} %bitcast.34), custom_call_target="tpu_custom_call" | custom-call | tf_op jit(solution)/shard_map/square_sum/pallas_call | solution.py:47
  3.4 3.0 %collective-permute-start = (f32[1]{0:T(128)}, f32[1]{0:T(128)}, u32[]{:S(2)}, u32[]{:S(2)}) collective-permute-start(f32[1]{0:T(128)} %get-tuple-element.24), channel_id=1, source_target_pairs={{0,2},{2,0},{1,3},{3,1},{4,6},{6,4},{5,7},{7,5},{8,10},{10,8},{9,1... | collective-permute-start | bytes 20 | tf_op jit(solution)/shard_map/ppermute | solution.py:362
  6.4 1.7 collective-permute-done
  9.5 0.9 cut.2
  10.4 2.1 %collective-permute-start.3 = (bf16[96,4096]{1,0:T(8,128)(2,1)}, bf16[96,4096]{1,0:T(8,128)(2,1)}, u32[]{:S(2)}, u32[]{:S(2)}) collective-permute-start(bf16[96,4096]{1,0:T(8,128)(2,1)} %cut.2), channel_id=1, source_target_pairs={{0,2},{2,0},{1,3},{3,1},{4,6},{6,4},{5,7},{7,5},{8,10},{10,8},{9,1... | collective-permute-start | bytes 2359304 | tf_op jit(solution)/shard_map/ppermute | solution.py:362
  12.5 10.9 %encode.2 = (bf16[384,1024]{1,0:T(8,128)(2,1)}, bf16[384,1024]{1,0:T(8,128)(2,1)}) custom-call(s32[1]{0:T(128)} %constant.58.clone.1.places_ref, f32[1]{0:T(128)S(6)} %sqrt.3.inv_ref, bf16[1,2048]{1,0:T(2,128)(2,1)S(1)} %constant_dynamic-slice_fusion.b_ref, bf16[384,4096]{1,0:T(8,128)(2,1)S(1)} %get-tuple-element.25.refs_0_.x_ref, bf16[4096,2048]{1,0:T(8,128)(2,1)} %bitcast.32), custom_call_target="tpu_custom_call" | custom-call | tf_op jit(solution)/shard_map/encode/pallas_call | solution.py:146
  23.4 1.2 cut.3
  24.7 1.3 collective-permute-start.2
  26.1 1.3 collective-permute-start.1
  27.4 3.9 %collective-permute-done.3.refs_0_ = bf16[96,4096]{1,0:T(8,128)(2,1)} collective-permute-done((bf16[96,4096]{1,0:T(8,128)(2,1)}, bf16[96,4096]{1,0:T(8,128)(2,1)}, u32[]{:S(2)}, u32[]{:S(2)}) %collective-permute-start.3) | collective-permute-done | bytes 786464 | tf_op jit(solution)/shard_map/ppermute | solution.py:362
  31.3 2.1 %collective-permute-start.4 = (bf16[96,4096]{1,0:T(8,128)(2,1)}, bf16[96,4096]{1,0:T(8,128)(2,1)}, u32[]{:S(2)}, u32[]{:S(2)}) collective-permute-start(bf16[96,4096]{1,0:T(8,128)(2,1)} %collective-permute-done.3.refs_0_), channel_id=1, source_target_pairs={{0,4},{4,0},{8,12},{12,8},{1,5},{5,1},{9,13},{13,9},{2,6},{6,2},{1... | collective-permute-start | bytes 2359304 | tf_op jit(solution)/shard_map/ppermute | solution.py:367
  33.5 7.4 %decode.6 = (bf16[1,176,1024]{2,1,0:T(8,128)(2,1)S(1)}, bf16[1,176,1024]{2,1,0:T(8,128)(2,1)S(1)}, f32[1,208,1024]{2,1,0:T(8,128)S(1)}, f32[1,208,1024]{2,1,0:T(8,128)S(1)}) custom-call(s32[3]{0:T(128)S(1)} %get-tuple-element.47.info_ref, bf16[384,1024]{1,0:T(8,128)(2,1)} %get-tuple-element.26.refs_0_.after_ref, ...), custom_call_target="tpu_custom_call" | custom-call | tf_op jit(solution)/shard_map/decode/pallas_call | solution.py:245
  40.9 0.9 copy-done.2
  41.8 0.9 copy-done.4
  42.7 0.7 copy-done.8
  43.5 7.4 %decode.7 = (f32[1,176,1024]{2,1,0:T(8,128)S(1)}, f32[1,176,1024]{2,1,0:T(8,128)S(1)}, f32[1,208,1024]{2,1,0:T(8,128)S(1)}, f32[1,208,1024]{2,1,0:T(8,128)S(1)}) custom-call(s32[3]{0:T(128)S(1)} %get-tuple-element.46.info_ref, bf16[384,1024]{1,0:T(8,128)(2,1)} %get-tuple-element.26.refs_0_.after_ref, bf16[384,1024]{1,0:T(8,128)(2,1)} %get-tuple-element.27.refs_1_, ...), custom_call_target="tpu_custom_call" | custom-call | tf_op jit(solution)/shard_map/decode/pallas_call | solution.py:245
  50.9 3.5 %collective-permute-done.6 = bf16[1,176,1024]{2,1,0:T(8,128)(2,1)} collective-permute-done((bf16[1,176,1024]{2,1,0:T(8,128)(2,1)S(1)}, bf16[1,176,1024]{2,1,0:T(8,128)(2,1)}, u32[]{:S(2)}, u32[]{:S(2)}) %collective-permute-start.6) | collective-permute-done | bytes 360480 | tf_op jit(solution)/shard_map/ppermute | solution.py:367
  54.4 1.1 add_convert_fusion.5.refs_4_
  55.5 7.1 %collective-permute-done.5.refs_2_ = bf16[192,4096]{1,0:T(8,128)(2,1)S(1)} collective-permute-done((bf16[192,4096]{1,0:T(8,128)(2,1)}, bf16[192,4096]{1,0:T(8,128)(2,1)S(1)}, u32[]{:S(2)}, u32[]{:S(2)}) %collective-permute-start.5) | collective-permute-done | bytes 1572896 | tf_op jit(solution)/shard_map/ppermute | solution.py:362
  62.6 10.6 %encode.3.refs_0_ = bf16[384,2048]{1,0:T(8,128)(2,1)S(1)} custom-call(s32[3]{0:T(128)S(1)} %pad_add_fusion.3.places_ref, f32[1]{0:T(128)S(6)} %sqrt.3.inv_ref, bf16[1,2048]{1,0:T(2,128)(2,1)S(1)} %constant_dynamic-slice_fusion.b_ref, bf16[96,4096]{1,0:T(8,128)(2,1)} %collective-permute-done.3.refs_0_, bf16[96,4096]{1,0:T(8,128)(2,1)} %collective-permute-done.4.refs_1_, ...), custom_call_target="tpu_custom_call" | custom-call | tf_op jit(solution)/shard_map/encode/pallas_call | solution.py:146
  73.3 1.4 collective-permute-start.7
  74.8 2.8 %collective-permute-done.7.refs_1_ = bf16[384,2048]{1,0:T(8,128)(2,1)S(1)} collective-permute-done((bf16[384,2048]{1,0:T(8,128)(2,1)S(1)}, bf16[384,2048]{1,0:T(8,128)(2,1)S(1)}, u32[]{:S(2)}, u32[]{:S(2)}) %collective-permute-start.7) | collective-permute-done | bytes 1572896 | tf_op jit(solution)/shard_map/ppermute | solution.py:423
  77.6 4.5 %decode.8 = (bf16[1,176,1024]{2,1,0:T(8,128)(2,1)S(1)}, bf16[1,208,1024]{2,1,0:T(8,128)(2,1)S(1)}) custom-call(s32[2]{0:T(128)S(1)} %get-tuple-element.49.info_ref, bf16[384,2048]{1,0:T(8,128)(2,1)S(1)} %encode.3.refs_0_, bf16[384,2048]{1,0:T(8,128)(2,1)S(1)} %collective-permute-done.7.refs_1_, bf16[2048,4096]{1,0:T(8,128)(2,1)} %bitcast.28, ...), custom_call_target="tpu_custom_call" | custom-call | tf_op jit(solution)/shard_map/decode/pallas_call | solution.py:245
  82.1 1.8 %collective-permute-start.10 = (bf16[1,208,1024]{2,1,0:T(8,128)(2,1)S(1)}, bf16[1,208,1024]{2,1,0:T(8,128)(2,1)S(1)}, u32[]{:S(2)}, u32[]{:S(2)}) collective-permute-start(bf16[1,208,1024]{2,1,0:T(8,128)(2,1)S(1)} %get-tuple-element.36), channel_id=1, source_target_pairs={{0,2},{2,0},{1,3},{3,1},{4,6},{6,4},{5,7},{7,5},{8,10},{10,8},{9,1... | collective-permute-start | bytes 1277960 | tf_op jit(solution)/shard_map/ppermute | solution.py:362
  83.9 1.6 collective-permute-start.8
  85.5 2.6 %collective-permute-start.9 = (bf16[1,176,1024]{2,1,0:T(8,128)(2,1)S(1)}, bf16[1,176,1024]{2,1,0:T(8,128)(2,1)S(1)}, u32[]{:S(2)}, u32[]{:S(2)}) collective-permute-start(bf16[1,176,1024]{2,1,0:T(8,128)(2,1)S(1)} %add_convert_fusion.5.refs_4_), channel_id=1, source_target_pairs={{0,8},{4,12},{8,0},{12,4},{1,9},{5,13},{9,1},{13,5},{2,10},{6,14},... | collective-permute-start | bytes 1081352 | tf_op jit(solution)/shard_map/ppermute | solution.py:367
  88.7 4.5 %decode.9 = (bf16[1,176,1024]{2,1,0:T(8,128)(2,1)S(1)}, bf16[1,208,1024]{2,1,0:T(8,128)(2,1)S(1)}) custom-call(s32[2]{0:T(128)S(1)} %get-tuple-element.48.info_ref, bf16[384,2048]{1,0:T(8,128)(2,1)S(1)} %encode.3.refs_0_, bf16[384,2048]{1,0:T(8,128)(2,1)S(1)} %collective-permute-done.7.refs_1_, bf16[2048,4096]{1,0:T(8,128)(2,1)} %bitcast.29, ...), custom_call_target="tpu_custom_call" | custom-call | tf_op jit(solution)/shard_map/decode/pallas_call | solution.py:245
  93.2 1.6 collective-permute-start.18
  94.9 6.4 %collective-permute-done.8.refs_1_ = bf16[1,176,1024]{2,1,0:T(8,128)(2,1)S(1)} collective-permute-done((bf16[1,176,1024]{2,1,0:T(8,128)(2,1)S(1)}, bf16[1,176,1024]{2,1,0:T(8,128)(2,1)S(1)}, u32[]{:S(2)}, u32[]{:S(2)}) %collective-permute-start.8) | collective-permute-done | bytes 360480 | tf_op jit(solution)/shard_map/ppermute | solution.py:367
  101.7 3.0 %collective-permute-start.16 = (bf16[1,208,1024]{2,1,0:T(8,128)(2,1)S(1)}, bf16[1,208,1024]{2,1,0:T(8,128)(2,1)S(1)}, u32[]{:S(2)}, u32[]{:S(2)}) collective-permute-start(bf16[1,208,1024]{2,1,0:T(8,128)(2,1)S(1)} %add_convert_fusion.2.refs_6_), channel_id=1, source_target_pairs={{0,4},{4,0},{8,12},{12,8},{1,5},{5,1},{9,13},{13,9},{2,6},{6,2},{1... | collective-permute-start | bytes 1277960 | tf_op jit(solution)/shard_map/ppermute | solution.py:367
  104.7 4.5 %decode.10 = (f32[1,176,1024]{2,1,0:T(8,128)S(1)}, bf16[1,208,1024]{2,1,0:T(8,128)(2,1)S(1)}) custom-call(s32[2]{0:T(128)S(1)} %pad_add_fusion.4.info_ref, bf16[384,2048]{1,0:T(8,128)(2,1)S(1)} %encode.3.refs_0_, bf16[384,2048]{1,0:T(8,128)(2,1)S(1)} %collective-permute-done.7.refs_1_, bf16[2048,4096]{1,0:T(8,128)(2,1)} %bitcast.30, ...), custom_call_target="tpu_custom_call" | custom-call | tf_op jit(solution)/shard_map/decode/pallas_call | solution.py:245
  109.9 2.6 %collective-permute-start.19 = (bf16[1,176,1024]{2,1,0:T(8,128)(2,1)S(1)}, bf16[1,176,1024]{2,1,0:T(8,128)(2,1)S(1)}, u32[]{:S(2)}, u32[]{:S(2)}) collective-permute-start(bf16[1,176,1024]{2,1,0:T(8,128)(2,1)S(1)} %add_convert_fusion.4.refs_4_), channel_id=1, source_target_pairs={{0,8},{4,12},{8,0},{12,4},{1,9},{5,13},{9,1},{13,5},{2,10},{6,14},... | collective-permute-start | bytes 1081352 | tf_op jit(solution)/shard_map/ppermute | solution.py:367
  112.6 1.3 collective-permute-start.14
  113.9 4.7 %decode.11 = (f32[1,176,1024]{2,1,0:T(8,128)S(1)}, bf16[1,208,1024]{2,1,0:T(8,128)(2,1)S(1)}) custom-call(s32[2]{0:T(128)S(1)} %pad_add_fusion.2.info_ref, bf16[384,2048]{1,0:T(8,128)(2,1)S(1)} %encode.3.refs_0_, bf16[384,2048]{1,0:T(8,128)(2,1)S(1)} %collective-permute-done.7.refs_1_, bf16[2048,4096]{1,0:T(8,128)(2,1)} %bitcast.31, ...), custom_call_target="tpu_custom_call" | custom-call | tf_op jit(solution)/shard_map/decode/pallas_call | solution.py:245
  118.6 15.4 %collective-permute-done.16 = bf16[1,208,1024]{2,1,0:T(8,128)(2,1)S(1)} collective-permute-done((bf16[1,208,1024]{2,1,0:T(8,128)(2,1)S(1)}, bf16[1,208,1024]{2,1,0:T(8,128)(2,1)S(1)}, u32[]{:S(2)}, u32[]{:S(2)}) %collective-permute-start.16) | collective-permute-done | bytes 426016 | tf_op jit(solution)/shard_map/ppermute | solution.py:367
  134.3 2.1 %collective-permute-start.17 = (bf16[1,208,1024]{2,1,0:T(8,128)(2,1)S(1)}, bf16[1,208,1024]{2,1,0:T(8,128)(2,1)S(1)}, u32[]{:S(2)}, u32[]{:S(2)}) collective-permute-start(bf16[1,208,1024]{2,1,0:T(8,128)(2,1)S(1)} %add_convert_fusion), channel_id=1, source_target_pairs={{0,8},{4,12},{8,0},{12,4},{1,9},{5,13},{9,1},{13,5},{2,10},{6,14},... | collective-permute-start | bytes 1277960 | tf_op jit(solution)/shard_map/ppermute | solution.py:367
  136.6 1.6 collective-permute-start.20
  138.1 12.6 %collective-permute-done.14 = bf16[1,208,1024]{2,1,0:T(8,128)(2,1)S(1)} collective-permute-done((bf16[1,208,1024]{2,1,0:T(8,128)(2,1)S(1)}, bf16[1,208,1024]{2,1,0:T(8,128)(2,1)S(1)}, u32[]{:S(2)}, u32[]{:S(2)}) %collective-permute-start.14) | collective-permute-done | bytes 426016 | tf_op jit(solution)/shard_map/ppermute | solution.py:367
  150.7 1.8 %collective-permute-done.20.refs_5_ = bf16[176,1024]{1,0:T(8,128)(2,1)S(1)} collective-permute-done((bf16[176,1024]{1,0:T(8,128)(2,1)S(1)}, bf16[176,1024]{1,0:T(8,128)(2,1)S(1)}, u32[]{:S(2)}, u32[]{:S(2)}) %collective-permute-start.20) | collective-permute-done | bytes 360480 | tf_op jit(solution)/shard_map/ppermute | solution.py:362
  152.6 1.7 finale.1
  154.2 5.8 %collective-permute-start.23 = (f32[8,128]{1,0:T(8,128)S(1)}, f32[8,128]{1,0:T(8,128)S(1)}, u32[]{:S(2)}, u32[]{:S(2)}) collective-permute-start(f32[8,128]{1,0:T(8,128)S(1)} %get-tuple-element.45), channel_id=1, source_target_pairs={{0,3},{1,0},{2,1},{3,2},{4,7},{5,4},{6,5},{7,6},{8,11},{9,8},{10,9... | collective-permute-start | bytes 12296 | tf_op jit(solution)/shard_map/ppermute | solution.py:362
  160.3 1.1 collective-permute-done.23
  161.4 2.3 %collective-permute-done.22 = f32[8,128]{1,0:T(8,128)S(1)} collective-permute-done((f32[8,128]{1,0:T(8,128)S(1)}, f32[8,128]{1,0:T(8,128)S(1)}, u32[]{:S(2)}, u32[]{:S(2)}) %collective-permute-start.22) | collective-permute-done | bytes 4128 | tf_op jit(solution)/shard_map/ppermute | solution.py:362
  163.7 3.7 %collective-permute-start.26 = (f32[8,128]{1,0:T(8,128)S(1)}, f32[8,128]{1,0:T(8,128)S(1)}, u32[]{:S(2)}, u32[]{:S(2)}) collective-permute-start(f32[8,128]{1,0:T(8,128)S(1)} %add_add_fusion.refs_0_), channel_id=1, source_target_pairs={{0,12},{4,0},{8,4},{12,8},{1,13},{5,1},{9,5},{13,9},{2,14},{6,2},{... | collective-permute-start | bytes 12296 | tf_op jit(solution)/shard_map/ppermute | solution.py:362
  168.0 0.7 collective-permute-done.26.refs_3_
  168.7 3.2 %collective-permute-done.25.refs_2_ = f32[8,128]{1,0:T(8,128)S(1)} collective-permute-done((f32[8,128]{1,0:T(8,128)S(1)}, f32[8,128]{1,0:T(8,128)S(1)}, u32[]{:S(2)}, u32[]{:S(2)}) %collective-permute-start.25) | collective-permute-done | bytes 4128 | tf_op jit(solution)/shard_map/ppermute | solution.py:362
  171.9 0.9 collective-permute-done.24.refs_1_
  173.4 1.2 mean_ratio.1
  (61 shorter events, 4.2 us)
Async XLA Ops:
  0.6 5.8 %copy-start = (bf16[1,4096]{1,0:T(2,128)(2,1)S(1)}, bf16[1,4096]{1,0:T(2,128)(2,1)}, u32[]{:S(2)}) copy-start(bf16[1,4096]{1,0:T(2,128)(2,1)} %param.10) | copy-start | bytes 24580
  3.4 4.8 %collective-permute-start = (f32[1]{0:T(128)}, f32[1]{0:T(128)}, u32[]{:S(2)}, u32[]{:S(2)}) collective-permute-start(f32[1]{0:T(128)} %get-tuple-element.24), channel_id=1, source_target_pairs={{0,2},{2,0},{1,3},{3,1},{4,6},{6,4},{5,7},{7,5},{8,10},{10,8},{9,1... | collective-permute-start | bytes 20 | tf_op jit(solution)/shard_map/ppermute | solution.py:362
  10.4 20.9 %collective-permute-start.3 = (bf16[96,4096]{1,0:T(8,128)(2,1)}, bf16[96,4096]{1,0:T(8,128)(2,1)}, u32[]{:S(2)}, u32[]{:S(2)}) collective-permute-start(bf16[96,4096]{1,0:T(8,128)(2,1)} %cut.2), channel_id=1, source_target_pairs={{0,2},{2,0},{1,3},{3,1},{4,6},{6,4},{5,7},{7,5},{8,10},{10,8},{9,1... | collective-permute-start | bytes 2359304 | tf_op jit(solution)/shard_map/ppermute | solution.py:362
  24.6 38.0 %collective-permute-start.5 = (bf16[192,4096]{1,0:T(8,128)(2,1)}, bf16[192,4096]{1,0:T(8,128)(2,1)S(1)}, u32[]{:S(2)}, u32[]{:S(2)}) collective-permute-start(bf16[192,4096]{1,0:T(8,128)(2,1)} %cut.3), channel_id=1, source_target_pairs={{0,2},{2,0},{1,3},{3,1},{4,6},{6,4},{5,7},{7,5},{8,10},{10,8},{9,1... | collective-permute-start | bytes 4718600 | tf_op jit(solution)/shard_map/ppermute | solution.py:362
  24.7 8.7 %collective-permute-start.2 = (bf16[384,1024]{1,0:T(8,128)(2,1)}, bf16[384,1024]{1,0:T(8,128)(2,1)S(1)}, u32[]{:S(2)}, u32[]{:S(2)}) collective-permute-start(bf16[384,1024]{1,0:T(8,128)(2,1)} %get-tuple-element.27.refs_1_), channel_id=1, source_target_pairs={{0,1},{2,3},{4,5},{6,7},{8,9},{10,11},{12,13},{14,15},{16,17},{18,... | collective-permute-start | bytes 2359304 | tf_op jit(solution)/shard_map/ppermute | solution.py:423
  26.1 7.4 %collective-permute-start.1 = (bf16[384,1024]{1,0:T(8,128)(2,1)}, bf16[384,1024]{1,0:T(8,128)(2,1)S(1)}, u32[]{:S(2)}, u32[]{:S(2)}) collective-permute-start(bf16[384,1024]{1,0:T(8,128)(2,1)} %get-tuple-element.26.refs_0_.after_ref), channel_id=1, source_target_pairs={{0,1},{2,3},{4,5},{6,7},{8,9},{10,11},{12,13},{14,15},{16,17},{18,... | collective-permute-start | bytes 2359304 | tf_op jit(solution)/shard_map/ppermute | solution.py:423
  31.3 24.2 %collective-permute-start.4 = (bf16[96,4096]{1,0:T(8,128)(2,1)}, bf16[96,4096]{1,0:T(8,128)(2,1)}, u32[]{:S(2)}, u32[]{:S(2)}) collective-permute-start(bf16[96,4096]{1,0:T(8,128)(2,1)} %collective-permute-done.3.refs_0_), channel_id=1, source_target_pairs={{0,4},{4,0},{8,12},{12,8},{1,5},{5,1},{9,13},{13,9},{2,6},{6,2},{1... | collective-permute-start | bytes 2359304 | tf_op jit(solution)/shard_map/ppermute | solution.py:367
  40.9 0.9 copy-start.2
  41.8 0.9 copy-start.4
  42.7 0.7 copy-start.8
  43.4 11.0 %collective-permute-start.6 = (bf16[1,176,1024]{2,1,0:T(8,128)(2,1)S(1)}, bf16[1,176,1024]{2,1,0:T(8,128)(2,1)}, u32[]{:S(2)}, u32[]{:S(2)}) collective-permute-start(bf16[1,176,1024]{2,1,0:T(8,128)(2,1)S(1)} %get-tuple-element.28.refs_6_), channel_id=1, source_target_pairs={{0,4},{4,0},{8,12},{12,8},{1,5},{5,1},{9,13},{13,9},{2,6},{6,2},{1... | collective-permute-start | bytes 1081352 | tf_op jit(solution)/shard_map/ppermute | solution.py:367
  73.3 4.3 %collective-permute-start.7 = (bf16[384,2048]{1,0:T(8,128)(2,1)S(1)}, bf16[384,2048]{1,0:T(8,128)(2,1)S(1)}, u32[]{:S(2)}, u32[]{:S(2)}) collective-permute-start(bf16[384,2048]{1,0:T(8,128)(2,1)S(1)} %encode.3.refs_0_), channel_id=1, source_target_pairs={{0,1},{2,3},{4,5},{6,7},{8,9},{10,11},{12,13},{14,15},{16,17},{18,... | collective-permute-start | bytes 4718600 | tf_op jit(solution)/shard_map/ppermute | solution.py:423
  77.6 6.3 %copy-start.9 = (bf16[1,176,1024]{2,1,0:T(8,128)(2,1)S(1)}, bf16[1,176,1024]{2,1,0:T(8,128)(2,1)}, u32[]{:S(2)}) copy-start(bf16[1,176,1024]{2,1,0:T(8,128)(2,1)} %copy-done.8) | copy-start | bytes 1081348
  82.1 19.5 %collective-permute-start.10 = (bf16[1,208,1024]{2,1,0:T(8,128)(2,1)S(1)}, bf16[1,208,1024]{2,1,0:T(8,128)(2,1)S(1)}, u32[]{:S(2)}, u32[]{:S(2)}) collective-permute-start(bf16[1,208,1024]{2,1,0:T(8,128)(2,1)S(1)} %get-tuple-element.36), channel_id=1, source_target_pairs={{0,2},{2,0},{1,3},{3,1},{4,6},{6,4},{5,7},{7,5},{8,10},{10,8},{9,1... | collective-permute-start | bytes 1277960 | tf_op jit(solution)/shard_map/ppermute | solution.py:362
  83.9 17.3 %collective-permute-start.8 = (bf16[1,176,1024]{2,1,0:T(8,128)(2,1)S(1)}, bf16[1,176,1024]{2,1,0:T(8,128)(2,1)S(1)}, u32[]{:S(2)}, u32[]{:S(2)}) collective-permute-start(bf16[1,176,1024]{2,1,0:T(8,128)(2,1)S(1)} %copy-done.9), channel_id=1, source_target_pairs={{0,4},{4,0},{8,12},{12,8},{1,5},{5,1},{9,13},{13,9},{2,6},{6,2},{1... | collective-permute-start | bytes 1081352 | tf_op jit(solution)/shard_map/ppermute | solution.py:367
  85.5 15.9 %collective-permute-start.9 = (bf16[1,176,1024]{2,1,0:T(8,128)(2,1)S(1)}, bf16[1,176,1024]{2,1,0:T(8,128)(2,1)S(1)}, u32[]{:S(2)}, u32[]{:S(2)}) collective-permute-start(bf16[1,176,1024]{2,1,0:T(8,128)(2,1)S(1)} %add_convert_fusion.5.refs_4_), channel_id=1, source_target_pairs={{0,8},{4,12},{8,0},{12,4},{1,9},{5,13},{9,1},{13,5},{2,10},{6,14},... | collective-permute-start | bytes 1081352 | tf_op jit(solution)/shard_map/ppermute | solution.py:367
  88.2 21.6 %collective-permute-start.11 = (bf16[1,176,1024]{2,1,0:T(8,128)(2,1)S(1)}, bf16[1,176,1024]{2,1,0:T(8,128)(2,1)S(1)}, u32[]{:S(2)}, u32[]{:S(2)}) collective-permute-start(bf16[1,176,1024]{2,1,0:T(8,128)(2,1)S(1)} %get-tuple-element.31.refs_4_), channel_id=1, source_target_pairs={{0,4},{4,0},{8,12},{12,8},{1,5},{5,1},{9,13},{13,9},{2,6},{6,2},{1... | collective-permute-start | bytes 1081352 | tf_op jit(solution)/shard_map/ppermute | solution.py:367
  88.7 12.9 %copy-start.5 = (f32[1,208,1024]{2,1,0:T(8,128)S(1)}, f32[1,208,1024]{2,1,0:T(8,128)}, u32[]{:S(2)}) copy-start(f32[1,208,1024]{2,1,0:T(8,128)} %copy-done.4) | copy-start | bytes 2555908
  93.2 43.2 %collective-permute-start.18 = (bf16[1,176,1024]{2,1,0:T(8,128)(2,1)S(1)}, bf16[1,176,1024]{2,1,0:T(8,128)(2,1)S(1)}, u32[]{:S(2)}, u32[]{:S(2)}) collective-permute-start(bf16[1,176,1024]{2,1,0:T(8,128)(2,1)S(1)} %get-tuple-element.32.refs_3_.refs_4_), channel_id=1, source_target_pairs={{0,4},{4,0},{8,12},{12,8},{1,5},{5,1},{9,13},{13,9},{2,6},{6,2},{1... | collective-permute-start | bytes 1081352 | tf_op jit(solution)/shard_map/ppermute | solution.py:367
  101.3 11.2 %collective-permute-start.13 = (bf16[1,208,1024]{2,1,0:T(8,128)(2,1)S(1)}, bf16[1,208,1024]{2,1,0:T(8,128)(2,1)S(1)}, u32[]{:S(2)}, u32[]{:S(2)}) collective-permute-start(bf16[1,208,1024]{2,1,0:T(8,128)(2,1)S(1)} %get-tuple-element.40), channel_id=1, source_target_pairs={{0,2},{2,0},{1,3},{3,1},{4,6},{6,4},{5,7},{7,5},{8,10},{10,8},{9,1... | collective-permute-start | bytes 1277960 | tf_op jit(solution)/shard_map/ppermute | solution.py:362
  101.7 10.8 %copy-start.3 = (f32[1,208,1024]{2,1,0:T(8,128)S(1)}, f32[1,208,1024]{2,1,0:T(8,128)}, u32[]{:S(2)}) copy-start(f32[1,208,1024]{2,1,0:T(8,128)} %copy-done.2) | copy-start | bytes 2555908
  101.7 32.2 %collective-permute-start.16 = (bf16[1,208,1024]{2,1,0:T(8,128)(2,1)S(1)}, bf16[1,208,1024]{2,1,0:T(8,128)(2,1)S(1)}, u32[]{:S(2)}, u32[]{:S(2)}) collective-permute-start(bf16[1,208,1024]{2,1,0:T(8,128)(2,1)S(1)} %add_convert_fusion.2.refs_6_), channel_id=1, source_target_pairs={{0,4},{4,0},{8,12},{12,8},{1,5},{5,1},{9,13},{13,9},{2,6},{6,2},{1... | collective-permute-start | bytes 1277960 | tf_op jit(solution)/shard_map/ppermute | solution.py:367
  109.2 24.9 %collective-permute-start.15 = (bf16[1,208,1024]{2,1,0:T(8,128)(2,1)S(1)}, bf16[1,208,1024]{2,1,0:T(8,128)(2,1)S(1)}, u32[]{:S(2)}, u32[]{:S(2)}) collective-permute-start(bf16[1,208,1024]{2,1,0:T(8,128)(2,1)S(1)} %get-tuple-element.42), channel_id=1, source_target_pairs={{0,2},{2,0},{1,3},{3,1},{4,6},{6,4},{5,7},{7,5},{8,10},{10,8},{9,1... | collective-permute-start | bytes 1277960 | tf_op jit(solution)/shard_map/ppermute | solution.py:362
  109.9 26.5 %collective-permute-start.19 = (bf16[1,176,1024]{2,1,0:T(8,128)(2,1)S(1)}, bf16[1,176,1024]{2,1,0:T(8,128)(2,1)S(1)}, u32[]{:S(2)}, u32[]{:S(2)}) collective-permute-start(bf16[1,176,1024]{2,1,0:T(8,128)(2,1)S(1)} %add_convert_fusion.4.refs_4_), channel_id=1, source_target_pairs={{0,8},{4,12},{8,0},{12,4},{1,9},{5,13},{9,1},{13,5},{2,10},{6,14},... | collective-permute-start | bytes 1081352 | tf_op jit(solution)/shard_map/ppermute | solution.py:367
  112.6 38.1 %collective-permute-start.14 = (bf16[1,208,1024]{2,1,0:T(8,128)(2,1)S(1)}, bf16[1,208,1024]{2,1,0:T(8,128)(2,1)S(1)}, u32[]{:S(2)}, u32[]{:S(2)}) collective-permute-start(bf16[1,208,1024]{2,1,0:T(8,128)(2,1)S(1)} %add_convert_fusion.1), channel_id=1, source_target_pairs={{0,4},{4,0},{8,12},{12,8},{1,5},{5,1},{9,13},{13,9},{2,6},{6,2},{1... | collective-permute-start | bytes 1277960 | tf_op jit(solution)/shard_map/ppermute | solution.py:367
  118.6 34.0 %copy-start.6 = (bf16[1,384,1024]{2,1,0:T(8,128)(2,1)S(1)}, bf16[1,384,1024]{2,1,0:T(8,128)(2,1)}, u32[]{:S(2)}) copy-start(bf16[1,384,1024]{2,1,0:T(8,128)(2,1)} %param.8) | copy-start | bytes 2359300
  118.6 34.0 %copy-start.7 = (bf16[1,1024]{1,0:T(2,128)(2,1)S(1)}, bf16[1,1024]{1,0:T(2,128)(2,1)}, u32[]{:S(2)}) copy-start(bf16[1,1024]{1,0:T(2,128)(2,1)} %b_ref.1) | copy-start | bytes 6148
  133.9 16.8 %collective-permute-start.12 = (bf16[1,208,1024]{2,1,0:T(8,128)(2,1)S(1)}, bf16[1,208,1024]{2,1,0:T(8,128)(2,1)S(1)}, u32[]{:S(2)}, u32[]{:S(2)}) collective-permute-start(bf16[1,208,1024]{2,1,0:T(8,128)(2,1)S(1)} %get-tuple-element.38), channel_id=1, source_target_pairs={{0,2},{2,0},{1,3},{3,1},{4,6},{6,4},{5,7},{7,5},{8,10},{10,8},{9,1... | collective-permute-start | bytes 1277960 | tf_op jit(solution)/shard_map/ppermute | solution.py:362
  134.1 40.5 %copy-start.1 = (bf16[1,4096]{1,0:T(2,128)(2,1)S(1)}, bf16[1,4096]{1,0:T(2,128)(2,1)}, u32[]{:S(2)}) copy-start(bf16[1,4096]{1,0:T(2,128)(2,1)} %param.10) | copy-start | bytes 24580
  134.3 18.2 %collective-permute-start.17 = (bf16[1,208,1024]{2,1,0:T(8,128)(2,1)S(1)}, bf16[1,208,1024]{2,1,0:T(8,128)(2,1)S(1)}, u32[]{:S(2)}, u32[]{:S(2)}) collective-permute-start(bf16[1,208,1024]{2,1,0:T(8,128)(2,1)S(1)} %add_convert_fusion), channel_id=1, source_target_pairs={{0,8},{4,12},{8,0},{12,4},{1,9},{5,13},{9,1},{13,5},{2,10},{6,14},... | collective-permute-start | bytes 1277960 | tf_op jit(solution)/shard_map/ppermute | solution.py:367
  136.6 16.0 %collective-permute-start.20 = (bf16[176,1024]{1,0:T(8,128)(2,1)S(1)}, bf16[176,1024]{1,0:T(8,128)(2,1)S(1)}, u32[]{:S(2)}, u32[]{:S(2)}) collective-permute-start(bf16[176,1024]{1,0:T(8,128)(2,1)S(1)} %fusion), channel_id=1, source_target_pairs={{0,2},{2,0},{1,3},{3,1},{4,6},{6,4},{5,7},{7,5},{8,10},{10,8},{9,1... | collective-permute-start | bytes 1081352 | tf_op jit(solution)/shard_map/ppermute | solution.py:362
  154.2 7.2 %collective-permute-start.23 = (f32[8,128]{1,0:T(8,128)S(1)}, f32[8,128]{1,0:T(8,128)S(1)}, u32[]{:S(2)}, u32[]{:S(2)}) collective-permute-start(f32[8,128]{1,0:T(8,128)S(1)} %get-tuple-element.45), channel_id=1, source_target_pairs={{0,3},{1,0},{2,1},{3,2},{4,7},{5,4},{6,5},{7,6},{8,11},{9,8},{10,9... | collective-permute-start | bytes 12296 | tf_op jit(solution)/shard_map/ppermute | solution.py:362
  160.1 3.6 %collective-permute-start.22 = (f32[8,128]{1,0:T(8,128)S(1)}, f32[8,128]{1,0:T(8,128)S(1)}, u32[]{:S(2)}, u32[]{:S(2)}) collective-permute-start(f32[8,128]{1,0:T(8,128)S(1)} %get-tuple-element.45), channel_id=1, source_target_pairs={{0,2},{1,3},{2,0},{3,1},{4,6},{5,7},{6,4},{7,5},{8,10},{9,11},{10,... | collective-permute-start | bytes 12296 | tf_op jit(solution)/shard_map/ppermute | solution.py:362
  160.3 3.4 %collective-permute-start.21 = (f32[8,128]{1,0:T(8,128)S(1)}, f32[8,128]{1,0:T(8,128)S(1)}, u32[]{:S(2)}, u32[]{:S(2)}) collective-permute-start(f32[8,128]{1,0:T(8,128)S(1)} %get-tuple-element.45), channel_id=1, source_target_pairs={{0,1},{1,2},{2,3},{3,0},{4,5},{5,6},{6,7},{7,4},{8,9},{9,10},{10,1... | collective-permute-start | bytes 12296 | tf_op jit(solution)/shard_map/ppermute | solution.py:362
  163.7 9.1 %copy-start.10 = (f32[8,128]{1,0:T(8,128)}, f32[8,128]{1,0:T(8,128)S(1)}, u32[]{:S(2)}) copy-start(f32[8,128]{1,0:T(8,128)S(1)} %add_add_fusion.refs_0_) | copy-start | bytes 12292
  163.7 5.0 %collective-permute-start.26 = (f32[8,128]{1,0:T(8,128)S(1)}, f32[8,128]{1,0:T(8,128)S(1)}, u32[]{:S(2)}, u32[]{:S(2)}) collective-permute-start(f32[8,128]{1,0:T(8,128)S(1)} %add_add_fusion.refs_0_), channel_id=1, source_target_pairs={{0,12},{4,0},{8,4},{12,8},{1,13},{5,1},{9,5},{13,9},{2,14},{6,2},{... | collective-permute-start | bytes 12296 | tf_op jit(solution)/shard_map/ppermute | solution.py:362
  167.4 4.5 %collective-permute-start.25 = (f32[8,128]{1,0:T(8,128)S(1)}, f32[8,128]{1,0:T(8,128)S(1)}, u32[]{:S(2)}, u32[]{:S(2)}) collective-permute-start(f32[8,128]{1,0:T(8,128)S(1)} %add_add_fusion.refs_0_), channel_id=1, source_target_pairs={{0,8},{4,12},{8,0},{12,4},{1,9},{5,13},{9,1},{13,5},{2,10},{6,14},... | collective-permute-start | bytes 12296 | tf_op jit(solution)/shard_map/ppermute | solution.py:362
  167.4 5.4 %collective-permute-start.24 = (f32[8,128]{1,0:T(8,128)S(1)}, f32[8,128]{1,0:T(8,128)S(1)}, u32[]{:S(2)}, u32[]{:S(2)}) collective-permute-start(f32[8,128]{1,0:T(8,128)S(1)} %add_add_fusion.refs_0_), channel_id=1, source_target_pairs={{0,4},{4,8},{8,12},{12,0},{1,5},{5,9},{9,13},{13,1},{2,6},{6,10},{... | collective-permute-start | bytes 12296 | tf_op jit(solution)/shard_map/ppermute | solution.py:362
  168.7 4.1 %copy-start.11 = (f32[8,128]{1,0:T(8,128)}, f32[8,128]{1,0:T(8,128)S(1)}, u32[]{:S(2)}) copy-start(f32[8,128]{1,0:T(8,128)S(1)} %collective-permute-done.26.refs_3_) | copy-start | bytes 12292
  171.9 0.9 copy-start.12
  172.8 0.6 copy-start.13
